TPU v7x, 32 devices: a whole 2x2x4 slice. The times are simulated.
32 devices in a mesh: group: 2 (over y), sec: 16 (over z, x, core), op: 1.
Axes of the slice: x: 2, y: 2, z: 4, core: 2. Of those that a mesh axis runs over, the one named last changes fastest.
Arguments:
- psi: bfloat16 [32, 16, 256, 256], P(('group', 'sec')), parts along dimension 0, may hold values from -6 to 6
- left_env: bfloat16 [16, 16, 256, 256], P(('group', 'op'), 'sec'), parts along dimension 0, may hold values from -0.375 to 0.375
- right_env: bfloat16 [16, 16, 256, 256], P(('group', 'op'), 'sec'), parts along dimension 0, may hold values from -0.125 to 0.125
- source_map: int32 [16, 16], P(('group', 'op')), parts along dimension 0, may hold values from 0 to 15
Outputs:
- hpsi: bfloat16 [32, 16, 256, 256], P('group', 'sec', 'op'), parts along dimension 0
There are 2 independent parts, one for each index of `group`. A program takes and returns all parts, laid end to end along the dimension named above; each array names one. Nothing has to cross between parts.
Inputs may be any that keep to these rules, and one draw needn't show every extreme that they name: source_map[k, q] is the right sector of psi that term k carries into output right sector q.
All inputs are finite; a program needn't handle non-finite values.
Results may differ from a plain program's by a relative error of at most 0.0049.
Values may be sent and summed in bfloat16 or wider, within the bound.
No kernel may reach another device: no remote copies, remote signals or barrier semaphores. Data moves between devices by JAX's collectives and lax.ppermute only.
A program may use at most 128 MiB of HBM per device.

v0:
```python
import jax
import jax.numpy as jnp
from jax import lax
from jax.sharding import PartitionSpec as P


def sum_terms(partial_out):
    return lax.psum_scatter(partial_out, "op", scatter_dimension=2, tiled=True)


def on_device(psi, left_env, right_env, source_map):
    chosen = jnp.take(psi, source_map, axis=1)
    mid = jnp.einsum(
        "kaij,akqjm->kaqim", left_env, chosen, preferred_element_type=jnp.float32
    ).astype(jnp.bfloat16)
    local_sums = jnp.einsum(
        "kaqim,kqnm->aqin",
        mid,
        lax.all_gather(right_env, "sec", axis=1, tiled=True),
        preferred_element_type=jnp.float32,
    )
    partial_out = lax.all_to_all(local_sums, "sec", split_axis=1, concat_axis=0, tiled=True)
    summed = sum_terms(partial_out).astype(jnp.bfloat16)
    return summed


def solution(mesh):
    placed = (
        P(("group", "sec"), None, None, None),
        P(("group", "op"), "sec", None, None),
        P(("group", "op"), "sec", None, None),
        P(("group", "op"), None),
    )
    return jax.shard_map(
        on_device,
        mesh=mesh,
        in_specs=placed,
        out_specs=P("group", "sec", "op", None),
        check_vma=False,
    )
```

profile of v0, /device:TPU:0, one launch (start us, length us, event | category | flops | bytes accessed | tf_op | source)
XLA Modules:
  0.0 214.1 jit_solution(11870207428966189934)
XLA Ops:
  6.5 0.0 copy-start
  6.5 0.0 all-gather.2.cloned.1.call-start
  6.5 0.7 all-gather.2.cloned.1.call-update
  7.3 0.7 compare_select_fusion
  8.0 0.1 reshape.40
  8.0 0.1 copy-done
  8.1 8.3 %gather_fusion = bf16[128,256,256]{2,1,0:T(8,128)(2,1)} fusion(bf16[16,256,256]{2,1,0:T(8,128)(2,1)S(1)} %bitcast.34, s32[1024]{0:T(1024)S(1)} %pad_clamp_fusion), kind=kCustom, calls=%fused_computation | custom fusion | bytes 33554944 | tf_op jit(solution)/shard_map/jit(_take)/gather | solution.py:12
  16.4 0.0 copy-start.1
  16.5 0.0 copy-start.2
  16.5 21.8 %copy.9 = bf16[8,16,256,256]{2,3,1,0:T(8,128)(2,1)} copy(bf16[8,16,256,256]{3,2,1,0:T(8,128)(2,1)} %bitcast.35) | data formatting | bytes 33554432 | tf_op jit(solution)/shard_map/jit(_take)/gather | solution.py:12
  38.3 0.0 copy-done.1
  38.3 100.8 %all-gather.2.cloned.1.call-done = bf16[8,16,256,256]{3,2,0,1:T(8,128)(2,1)} async-done(((bf16[8,1,256,256]{3,2,0,1:T(8,128)(2,1)}), bf16[8,16,256,256]{3,2,0,1:T(8,128)(2,1)}) %all-gather.2.cloned.1.call-update) | async-done | bytes 16777232 | tf_op jit(solution)/shard_map/all_gather | solution.py:19
  139.1 0.0 copy-done.2
  139.1 15.9 %fusion.13 = bf16[1,16,256,256]{3,2,0,1:T(8,128)(2,1)} fusion(bf16[8,16,256,256]{3,2,0,1:T(8,128)(2,1)} %all-gather.2.cloned.1.call-done, bf16[8,16,256,256]{2,3,1,0:T(8,128)(2,1)} %copy.9, pred[8,16]{1,0:T(8,128)(4,1)S(1)} %compare_and_fusion, bf16[8,1,256,256]{3,2,1,0:T(8,128)(2,1)S(1)} %copy-done.2), kind=kOutput, calls=%fused_computation.9 | convolution fusion | flops 8606711808 | bytes 36700288 | tf_op jit(solution)/shard_map/kaqim,kqnm->aqin/dot_general | solution.py:16
  155.0 50.9 %all_to_all.4 = bf16[1,16,256,256]{3,2,0,1:T(8,128)(2,1)S(1)} all-to-all(bf16[1,16,256,256]{3,2,0,1:T(8,128)(2,1)} %fusion.13), channel_id=1, replica_groups=mesh['group'=2,'sec'=16,'op'=1] {'sec'}, dimensions={1} | all-to-all | bytes 4194304 | tf_op jit(solution)/shard_map/all_to_all | solution.py:22
  206.0 1.3 copy.22
  (2 shorter events, 0.0 us)
Async XLA Ops:
  6.5 1.6 copy-start
  6.5 132.6 %all-gather.2.cloned.1.call-start = ((), (), s32[]{:S(2)}) async-start(), calls=%async_computation.1 | async-start | bytes 17825792 | tf_op jit(solution)/shard_map/all_gather | solution.py:19
  16.4 21.8 %copy-start.1 = (s32[8,16]{1,0:T(8,128)S(1)}, s32[8,16]{1,0:T(8,128)}, u32[]{:S(2)}) copy-start(s32[8,16]{1,0:T(8,128)} %param.7) | copy-start | bytes 1540
  16.5 122.7 %copy-start.2 = (bf16[8,1,256,256]{3,2,1,0:T(8,128)(2,1)S(1)}, bf16[8,1,256,256]{3,2,1,0:T(8,128)(2,1)}, u32[]{:S(2)}) copy-start(bf16[8,1,256,256]{3,2,1,0:T(8,128)(2,1)} %param.5) | copy-start | bytes 3145732
Sparse Core Ops, SparseCore 0:
  9.5 129.5 all-gather.1
where the time goes:
time: 215 us; the launch traced here: 214 us
  waiting for transfers between devices  102 us (47%)
  blocking collectives  50.9 us (24%)
  local copies, waits for them, and re-layouts  31.7 us (15%)
  matrix products  15.9 us (7%)
  between operations  13.4 us (6%)
    all_gather x1, waiting for transfers between devices, on_device(): lax.all_gather(right_env, 'sec', axis=1, tiled=True)  101 us
    all_to_all x1, blocking collectives, on_device(): lax.all_to_all(local_sums, 'sec', split_axis=1, concat_axis=0, tiled=True)  50.9 us
    gather x2, local copies, waits for them, and re-layouts, on_device(): chosen = jnp.take(psi, source_map, axis=1)  30.2 us
    dot_general x1, matrix products, on_device(): jnp.einsum('kaqim,kqnm->aqin', mid, lax.all_gather(right_env, 'sec', axis...  15.9 us
  transfers between devices with their start and end apart: 1, of which 1 were waited for; matrix products, arithmetic and copies ran while one was open for 14% of the time, Pallas kernels for 0%

commit v1 on v0

v1 whole, which is shorter than its diff:
```python
import functools

import jax
import jax.numpy as jnp
from jax import lax
from jax.experimental import pallas as pl
from jax.experimental.pallas import tpu as pltpu
from jax.sharding import PartitionSpec as P

HBM = pl.BlockSpec(memory_space=pl.ANY)
SMEM = pl.BlockSpec(memory_space=pltpu.SMEM)
VMEM = pl.BlockSpec(memory_space=pltpu.VMEM)


def slot_kernel(count, choices, meta, source, *refs):
    lefts, psis = refs[:count], refs[count : 2 * count]
    rights = refs[2 * count : 2 * count + choices]
    out, left_buf, psi_buf, right_buf, left_sem, psi_sem, right_sem = refs[2 * count + choices :]
    terms = right_buf.shape[0]
    q = meta[0]

    def copies(k, i):
        return (
            pltpu.make_async_copy(lefts[i].at[k, 0], left_buf.at[i, k], left_sem.at[i, k]),
            pltpu.make_async_copy(psis[i].at[0, source[k, q]], psi_buf.at[i, k], psi_sem.at[i, k]),
        )

    def right_copy(k, choice):
        return pltpu.make_async_copy(rights[choice].at[k, 0], right_buf.at[k], right_sem.at[k])

    for k in range(terms):
        if choices == 1:
            right_copy(k, 0).start()
        else:
            for choice in range(choices):
                pl.when(meta[1] == choice)(lambda k=k, choice=choice: right_copy(k, choice).start())
        for copy in copies(k, 0):
            copy.start()
    for i in range(1, count):
        for k in range(terms):
            for copy in copies(k, i):
                copy.start()
    for i in range(count):
        total = None
        for k in range(terms):
            for copy in copies(k, i):
                copy.wait()
            if i == 0:
                right_copy(k, 0).wait()
            mid = jnp.dot(left_buf[i, k], psi_buf[i, k], preferred_element_type=jnp.float32).astype(jnp.bfloat16)
            term = lax.dot_general(mid, right_buf[k], (((1,), (1,)), ((), ())), preferred_element_type=jnp.float32)
            total = term if total is None else total + term
        out[i] = total.astype(out.dtype)


def slot(q, choice, source_map, lefts, psis, rights, dtype):
    terms, _, rows, columns = lefts[0].shape
    count = len(lefts)
    meta = jnp.stack([q, choice]).astype(jnp.int32)
    block = rows * columns
    return pl.pallas_call(
        functools.partial(slot_kernel, count, len(rights)),
        out_shape=jax.ShapeDtypeStruct((count, rows, columns), dtype),
        in_specs=[SMEM, SMEM] + [HBM] * (2 * count + len(rights)),
        out_specs=VMEM,
        scratch_shapes=[
            pltpu.VMEM((count, terms, rows, columns), jnp.bfloat16),
            pltpu.VMEM((count, terms, rows, columns), jnp.bfloat16),
            pltpu.VMEM((terms, rows, columns), jnp.bfloat16),
            pltpu.SemaphoreType.DMA((count, terms)),
            pltpu.SemaphoreType.DMA((count, terms)),
            pltpu.SemaphoreType.DMA((terms,)),
        ],
        compiler_params=pltpu.CompilerParams(vmem_limit_bytes=24 << 20),
        cost_estimate=pl.CostEstimate(
            flops=4 * count * terms * block * rows,
            bytes_accessed=2 * block * terms * (2 * count + 1) + 2 * block * count,
            transcendentals=0,
        ),
    )(meta, source_map, *lefts, *psis, *rights)


def place_kernel(width, meta, *refs):
    pieces, out, sem = refs[:-2], refs[-2], refs[-1]
    me = meta[0]

    def copy(j):
        return pltpu.make_async_copy(pieces[j // width].at[j % width], out.at[me ^ j], sem.at[j])

    for j in range(len(pieces) * width):
        copy(j).start()
    for j in range(len(pieces) * width):
        copy(j).wait()


def place(me, pieces):
    width, rows, columns = pieces[0].shape
    sectors = width * len(pieces)
    return pl.pallas_call(
        functools.partial(place_kernel, width),
        out_shape=jax.ShapeDtypeStruct((sectors, rows, columns), pieces[0].dtype),
        in_specs=[SMEM] + [HBM] * len(pieces),
        out_specs=HBM,
        scratch_shapes=[pltpu.SemaphoreType.DMA((sectors,))],
    )(me[None].astype(jnp.int32), *pieces)


def exchange(array, bits, members):
    return lax.ppermute(array, "sec", [(s, s ^ bits) for s in members])


def on_device(ops, psi, left_env, right_env, source_map):
    me = lax.axis_index("sec")
    row = me // 4
    outer = (row == 0) | (row == 3)
    dtype = jnp.bfloat16 if ops == 1 else jnp.float32
    every = range(16)
    inner_to_outer = range(4, 12)

    near = exchange(right_env, 4, every)
    middle = exchange(right_env, 12, inner_to_outer)
    far_in = exchange(near, 12, inner_to_outer)
    second = exchange(middle, 4, inner_to_outer)
    third = exchange(far_in, 4, inner_to_outer)

    left, sectors = [left_env], [psi]
    left.append(exchange(left_env, 1, every))
    sectors.append(exchange(psi, 1, every))
    left.append(exchange(left_env, 2, every))
    sectors.append(exchange(psi, 2, every))
    left.append(exchange(left[2], 1, every))
    sectors.append(exchange(sectors[2], 1, every))

    rights = ((right_env,), (near,), (second, far_in), (third, middle))
    choice = jnp.where(outer, 0, 1)
    pieces = []
    for step in range(4):
        for half in (slice(0, 2), slice(2, 4)):
            piece = slot(me ^ (4 * step), choice, source_map, left[half], sectors[half], rights[step], dtype)
            if step > 0:
                piece = exchange(piece, 4 * step, every)
            pieces.append(piece)
    out = place(me, pieces)[:, None]
    if ops > 1:
        out = lax.psum_scatter(out, "op", scatter_dimension=2, tiled=True).astype(jnp.bfloat16)
    return out


def solution(mesh):
    placed = (
        P(("group", "sec"), None, None, None),
        P(("group", "op"), "sec", None, None),
        P(("group", "op"), "sec", None, None),
        P(("group", "op"), None),
    )
    return jax.shard_map(
        functools.partial(on_device, mesh.shape["op"]),
        mesh=mesh,
        in_specs=placed,
        out_specs=P("group", "sec", "op", None),
        check_vma=False,
    )
```

time: 215 us -> 257 us (1.20)
  Pallas kernels: 0 us -> 137 us
  blocking collectives: 50.9 us -> 0 us
  starting transfers between devices: 0.01 us -> 23.1 us
  local copies, waits for them, and re-layouts: 31.7 us -> 9.03 us
  matrix products: 15.9 us -> 0 us
  waiting for transfers between devices: 102 us -> 86.2 us
  between operations: 13.4 us -> 0.42 us
    pallas_call x0 -> x9, Pallas kernels: none -> 137 us  [the longest x8 72.5 us: slot(): pl.pallas_call(functools.partial(slot_kernel, count, len(rights)), out_sh...]
    all_gather x1 -> x0, waiting for transfers between devices: 101 us -> none  [on_device(): lax.all_gather(right_env, 'sec', axis=1, tiled=True)]
    ppermute x0 -> x17, waiting for transfers between devices: none -> 86.2 us  [exchange(): return lax.ppermute(array, 'sec', [(s, s ^ bits) for s in members])]
    all_to_all x1 -> x0, blocking collectives: 50.9 us -> none  [on_device(): lax.all_to_all(local_sums, 'sec', split_axis=1, concat_axis=0, tiled=True)]
    gather x2 -> x0, local copies, waits for them, and re-layouts: 30.2 us -> none  [on_device(): chosen = jnp.take(psi, source_map, axis=1)]
    ppermute x0 -> x17, starting transfers between devices: none -> 23.1 us  [exchange(): return lax.ppermute(array, 'sec', [(s, s ^ bits) for s in members])]
    dot_general x1 -> x0, matrix products: 15.9 us -> none  [on_device(): jnp.einsum('kaqim,kqnm->aqin', mid, lax.all_gather(right_env, 'sec', axis...]
    unnamed x7 -> x38, local copies, waits for them, and re-layouts: 1.41 us -> 9.03 us
  transfers between devices with their start and end apart: 1 -> 17, of which waited for: 1 -> 4; matrix products, arithmetic and copies ran while one was open for 14% -> 0% of each run, Pallas kernels for 0% -> 28%
where the time goes in v1:
time: 257 us; the launch traced here: 256 us
  Pallas kernels  137 us (53%)
  waiting for transfers between devices  86.2 us (34%)
  starting transfers between devices  23.1 us (9%)
  local copies, waits for them, and re-layouts  9.03 us (4%)
    ppermute x17, waiting for transfers between devices, exchange(): return lax.ppermute(array, 'sec', [(s, s ^ bits) for s in members])  86.2 us
    pallas_call x8, Pallas kernels, slot(): pl.pallas_call(functools.partial(slot_kernel, count, len(rights)), out_sh...  72.5 us
    pallas_call x1, Pallas kernels, place(): pl.pallas_call(functools.partial(place_kernel, width), out_shape=jax.Shap...  64.8 us
    ppermute x17, starting transfers between devices, exchange(): return lax.ppermute(array, 'sec', [(s, s ^ bits) for s in members])  23.1 us
    unnamed x38, local copies, waits for them, and re-layouts  9.03 us
  transfers between devices with their start and end apart: 17, of which 4 were waited for; matrix products, arithmetic and copies ran while one was open for 0% of the time, Pallas kernels for 28%

profile of v1, /device:TPU:0, one launch (start us, length us, event | category | flops | bytes accessed | tf_op | source)
XLA Modules:
  0.0 256.3 jit_solution(8853819539747158503)
XLA Ops:
  0.0 2.9 %collective-permute-start.4 = (bf16[1,16,256,256]{3,2,1,0:T(8,128)(2,1)}, bf16[1,16,256,256]{3,2,1,0:T(8,128)(2,1)S(1)}, u32[]{:S(2)}, u32[]{:S(2)}) collective-permute-start(bf16[1,16,256,256]{3,2,1,0:T(8,128)(2,1)} %refs_2_.7), channel_id=1, source_target_pairs={{0,2},{1,3},{2,0},{3,1},{4,6},{5,7},{6,4},{7,5},{8,10},{9,11},{10,... | collective-permute-start | bytes 6291464 | tf_op jit(solution)/shard_map/ppermute | solution.py:109
  2.9 1.6 collective-permute-start.6
  4.5 0.5 collective-permute-start.2
  5.1 1.6 collective-permute-start.9
  6.7 21.1 %collective-permute-done.6.refs_4_ = bf16[8,1,256,256]{3,2,1,0:T(8,128)(2,1)S(1)} collective-permute-done((bf16[8,1,256,256]{3,2,1,0:T(8,128)(2,1)}, bf16[8,1,256,256]{3,2,1,0:T(8,128)(2,1)S(1)}, u32[]{:S(2)}, u32[]{:S(2)}) %collective-permute-start.6) | collective-permute-done | bytes 1048608 | tf_op jit(solution)/shard_map/ppermute | solution.py:109
  27.8 1.6 collective-permute-start.11
  29.4 1.0 copy-done.8
  30.4 40.8 %collective-permute-done.2.refs_0_ = bf16[8,1,256,256]{3,2,1,0:T(8,128)(2,1)S(1)} collective-permute-done((bf16[8,1,256,256]{3,2,1,0:T(8,128)(2,1)}, bf16[8,1,256,256]{3,2,1,0:T(8,128)(2,1)S(1)}, u32[]{:S(2)}, u32[]{:S(2)}) %collective-permute-start.2) | collective-permute-done | bytes 1048608 | tf_op jit(solution)/shard_map/ppermute | solution.py:109
  71.3 0.5 collective-permute-start.5
  71.8 1.3 collective-permute-start.10
  73.1 1.3 collective-permute-start.14
  74.4 1.2 collective-permute-done.refs_1_
  75.5 1.0 copy-done.4
  76.5 0.1 collective-permute-start.3
  76.6 0.1 pad_add_fusion.2.meta
  76.7 0.1 pad_add_fusion.3.meta
  76.8 0.1 pad_add_fusion.1.meta
  76.9 23.1 %collective-permute-done.10.refs_4_ = bf16[8,1,256,256]{3,2,1,0:T(8,128)(2,1)} collective-permute-done((bf16[8,1,256,256]{3,2,1,0:T(8,128)(2,1)}, bf16[8,1,256,256]{3,2,1,0:T(8,128)(2,1)}, u32[]{:S(2)}, u32[]{:S(2)}) %collective-permute-start.10) | collective-permute-done | bytes 1048608 | tf_op jit(solution)/shard_map/ppermute | solution.py:109
  100.0 1.6 copy-done
  101.6 1.2 copy-done.2
  102.8 1.2 copy-done.5
  104.0 0.7 copy-done.12
  104.7 9.0 %shard_map.50 = bf16[2,256,256]{2,1,0:T(8,128)(2,1)S(1)} custom-call(s32[2]{0:T(128)S(1)} %pad_add_fusion.2.meta, s32[8,16]{1,0:T(8,128)S(1)} %copy-done.12, bf16[8,1,256,256]{3,2,1,0:T(8,128)(2,1)S(1)} %copy-done.2, bf16[8,1,256,256]{3,2,1,0:T(8,128)(2,1)S(1)} %copy-done.5, bf16[1,16,256,256]{3,2,1,0:T(8,128)(2,1)S(1)} %copy-done, ...), custom_call_target="tpu_custom_call" | custom-call | flops 1073741824 | bytes 5505024 | tf_op jit(solution)/shard_map/pallas_call | solution.py:61
  113.8 2.0 collective-permute-start.12
  115.8 10.4 %shard_map.48 = bf16[2,256,256]{2,1,0:T(8,128)(2,1)S(1)} custom-call(s32[2]{0:T(128)S(1)} %pad_add_fusion.1.meta, s32[8,16]{1,0:T(8,128)S(1)} %copy-done.12, bf16[8,1,256,256]{3,2,1,0:T(8,128)(2,1)S(1)} %copy-done.2, bf16[8,1,256,256]{3,2,1,0:T(8,128)(2,1)S(1)} %copy-done.5, bf16[1,16,256,256]{3,2,1,0:T(8,128)(2,1)S(1)} %copy-done, ...), custom_call_target="tpu_custom_call" | custom-call | flops 1073741824 | bytes 5505024 | tf_op jit(solution)/shard_map/pallas_call | solution.py:61
  126.2 2.5 collective-permute-start.7
  128.7 9.0 %shard_map.52 = bf16[2,256,256]{2,1,0:T(8,128)(2,1)S(1)} custom-call(s32[2]{0:T(128)S(1)} %pad_add_fusion.3.meta, s32[8,16]{1,0:T(8,128)S(1)} %copy-done.12, bf16[8,1,256,256]{3,2,1,0:T(8,128)(2,1)S(1)} %copy-done.2, bf16[8,1,256,256]{3,2,1,0:T(8,128)(2,1)S(1)} %copy-done.5, bf16[1,16,256,256]{3,2,1,0:T(8,128)(2,1)S(1)} %copy-done, ...), custom_call_target="tpu_custom_call" | custom-call | flops 1073741824 | bytes 5505024 | tf_op jit(solution)/shard_map/pallas_call | solution.py:61
  137.8 3.3 %collective-permute-start.15 = (bf16[2,256,256]{2,1,0:T(8,128)(2,1)S(1)}, bf16[2,256,256]{2,1,0:T(8,128)(2,1)S(1)}, u32[]{:S(2)}, u32[]{:S(2)}) collective-permute-start(bf16[2,256,256]{2,1,0:T(8,128)(2,1)S(1)} %shard_map.52), channel_id=1, source_target_pairs={{0,12},{1,13},{2,14},{3,15},{4,8},{5,9},{6,10},{7,11},{8,4},{9,5},... | collective-permute-start | bytes 786440 | tf_op jit(solution)/shard_map/ppermute | solution.py:109
  141.1 7.7 %shard_map.51 = bf16[2,256,256]{2,1,0:T(8,128)(2,1)S(1)} custom-call(s32[2]{0:T(128)S(1)} %pad_add_fusion.2.meta, s32[8,16]{1,0:T(8,128)S(1)} %copy-done.12, bf16[8,1,256,256]{3,2,1,0:T(8,128)(2,1)S(1)} %collective-permute-done.2.refs_0_, bf16[8,1,256,256]{3,2,1,0:T(8,128)(2,1)} %collective-permute-done.3.refs_1_, ...), custom_call_target="tpu_custom_call" | custom-call | flops 1073741824 | bytes 5505024 | tf_op jit(solution)/shard_map/pallas_call | solution.py:61
  148.8 0.1 collective-permute-start.13
  148.9 7.7 %shard_map.53 = bf16[2,256,256]{2,1,0:T(8,128)(2,1)S(1)} custom-call(s32[2]{0:T(128)S(1)} %pad_add_fusion.3.meta, s32[8,16]{1,0:T(8,128)S(1)} %copy-done.12, bf16[8,1,256,256]{3,2,1,0:T(8,128)(2,1)S(1)} %collective-permute-done.2.refs_0_, bf16[8,1,256,256]{3,2,1,0:T(8,128)(2,1)} %collective-permute-done.3.refs_1_, ...), custom_call_target="tpu_custom_call" | custom-call | flops 1073741824 | bytes 5505024 | tf_op jit(solution)/shard_map/pallas_call | solution.py:61
  156.6 0.0 copy-start.1
  156.6 0.0 copy-start.3
  156.6 0.0 copy-start.6
  156.6 0.0 copy-start.7
  156.6 0.0 copy-start.13
  156.6 1.1 collective-permute-start.16
  157.7 9.2 %shard_map.49 = bf16[2,256,256]{2,1,0:T(8,128)(2,1)S(1)} custom-call(s32[2]{0:T(128)S(1)} %pad_add_fusion.1.meta, s32[8,16]{1,0:T(8,128)S(1)} %copy-done.12, bf16[8,1,256,256]{3,2,1,0:T(8,128)(2,1)S(1)} %collective-permute-done.2.refs_0_, bf16[8,1,256,256]{3,2,1,0:T(8,128)(2,1)} %collective-permute-done.3.refs_1_, ...), custom_call_target="tpu_custom_call" | custom-call | flops 1073741824 | bytes 5505024 | tf_op jit(solution)/shard_map/pallas_call | solution.py:61
  166.9 2.6 collective-permute-start.8
  169.5 0.1 pad_add_fusion.meta
  169.6 10.4 %shard_map.46.refs_0_ = bf16[2,256,256]{2,1,0:T(8,128)(2,1)S(1)} custom-call(s32[2]{0:T(128)S(1)} %pad_add_fusion.meta, s32[8,16]{1,0:T(8,128)S(1)} %copy-done.13, bf16[8,1,256,256]{3,2,1,0:T(8,128)(2,1)S(1)} %copy-done.3, bf16[8,1,256,256]{3,2,1,0:T(8,128)(2,1)S(1)} %copy-done.6, bf16[1,16,256,256]{3,2,1,0:T(8,128)(2,1)S(1)} %copy-done.1, ...), custom_call_target="tpu_custom_call" | custom-call | flops 1073741824 | bytes 5505024 | tf_op jit(solution)/shard_map/pallas_call | solution.py:61
  180.0 9.0 %shard_map.47.refs_1_ = bf16[2,256,256]{2,1,0:T(8,128)(2,1)S(1)} custom-call(s32[2]{0:T(128)S(1)} %pad_add_fusion.meta, s32[8,16]{1,0:T(8,128)S(1)} %copy-done.13, bf16[8,1,256,256]{3,2,1,0:T(8,128)(2,1)S(1)} %collective-permute-done.2.refs_0_, bf16[8,1,256,256]{3,2,1,0:T(8,128)(2,1)} %collective-permute-done.3.refs_1_, ...), custom_call_target="tpu_custom_call" | custom-call | flops 1073741824 | bytes 5505024 | tf_op jit(solution)/shard_map/pallas_call | solution.py:61
  189.1 0.7 copy-done.11
  189.8 0.7 copy-done.15
  190.4 0.1 copy-done.16
  190.6 0.1 copy-done.17
  190.7 0.7 copy-done.18
  191.4 64.8 %shard_map.54 = bf16[16,256,256]{2,1,0:T(8,128)(2,1)} custom-call(s32[1]{0:T(128)} %bitcast.meta, bf16[2,256,256]{2,1,0:T(8,128)(2,1)} %copy-done.10, bf16[2,256,256]{2,1,0:T(8,128)(2,1)} %copy-done.11, bf16[2,256,256]{2,1,0:T(8,128)(2,1)} %copy-done.15, bf16[2,256,256]{2,1,0:T(8,128)(2,1)} %collective-permute-done.8.refs_3_, ...), custom_call_target="tpu_custom_call" | custom-call | tf_op jit(solution)/shard_map/pallas_call | solution.py:99
  (37 shorter events, 0.1 us)
Async XLA Ops:
  0.0 71.3 %collective-permute-start.4 = (bf16[1,16,256,256]{3,2,1,0:T(8,128)(2,1)}, bf16[1,16,256,256]{3,2,1,0:T(8,128)(2,1)S(1)}, u32[]{:S(2)}, u32[]{:S(2)}) collective-permute-start(bf16[1,16,256,256]{3,2,1,0:T(8,128)(2,1)} %refs_2_.7), channel_id=1, source_target_pairs={{0,2},{1,3},{2,0},{3,1},{4,6},{5,7},{6,4},{7,5},{8,10},{9,11},{10,... | collective-permute-start | bytes 6291464 | tf_op jit(solution)/shard_map/ppermute | solution.py:109
  2.9 24.8 %collective-permute-start.6 = (bf16[8,1,256,256]{3,2,1,0:T(8,128)(2,1)}, bf16[8,1,256,256]{3,2,1,0:T(8,128)(2,1)S(1)}, u32[]{:S(2)}, u32[]{:S(2)}) collective-permute-start(bf16[8,1,256,256]{3,2,1,0:T(8,128)(2,1)} %refs_4_.3), channel_id=1, source_target_pairs={{0,4},{1,5},{2,6},{3,7},{4,0},{5,1},{6,2},{7,3},{8,12},{9,13},{10,... | collective-permute-start | bytes 3145736 | tf_op jit(solution)/shard_map/ppermute | solution.py:109
  4.5 66.7 %collective-permute-start.2 = (bf16[8,1,256,256]{3,2,1,0:T(8,128)(2,1)}, bf16[8,1,256,256]{3,2,1,0:T(8,128)(2,1)S(1)}, u32[]{:S(2)}, u32[]{:S(2)}) collective-permute-start(bf16[8,1,256,256]{3,2,1,0:T(8,128)(2,1)} %refs_0_.7), channel_id=1, source_target_pairs={{0,2},{1,3},{2,0},{3,1},{4,6},{5,7},{6,4},{7,5},{8,10},{9,11},{10,... | collective-permute-start | bytes 3145736 | tf_op jit(solution)/shard_map/ppermute | solution.py:109
  5.1 66.7 %collective-permute-start.9 = (bf16[8,1,256,256]{3,2,1,0:T(8,128)(2,1)}, bf16[8,1,256,256]{3,2,1,0:T(8,128)(2,1)}, u32[]{:S(2)}, u32[]{:S(2)}) collective-permute-start(bf16[8,1,256,256]{3,2,1,0:T(8,128)(2,1)} %refs_4_.3), channel_id=1, source_target_pairs={{4,8},{5,9},{6,10},{7,11},{8,4},{9,5},{10,6},{11,7},{20,24},{21,25... | collective-permute-start | bytes 3145736 | tf_op jit(solution)/shard_map/ppermute | solution.py:109
  6.7 93.3 %collective-permute-start.1 = (bf16[1,16,256,256]{3,2,1,0:T(8,128)(2,1)}, bf16[1,16,256,256]{3,2,1,0:T(8,128)(2,1)}, u32[]{:S(2)}, u32[]{:S(2)}) collective-permute-start(bf16[1,16,256,256]{3,2,1,0:T(8,128)(2,1)} %refs_2_.7), channel_id=1, source_target_pairs={{0,1},{1,0},{2,3},{3,2},{4,5},{5,4},{6,7},{7,6},{8,9},{9,8},{10,11... | collective-permute-start | bytes 6291464 | tf_op jit(solution)/shard_map/ppermute | solution.py:109
  27.8 45.3 %collective-permute-start.11 = (bf16[8,1,256,256]{3,2,1,0:T(8,128)(2,1)S(1)}, bf16[8,1,256,256]{3,2,1,0:T(8,128)(2,1)}, u32[]{:S(2)}, u32[]{:S(2)}) collective-permute-start(bf16[8,1,256,256]{3,2,1,0:T(8,128)(2,1)S(1)} %collective-permute-done.6.refs_4_), channel_id=1, source_target_pairs={{4,8},{5,9},{6,10},{7,11},{8,4},{9,5},{10,6},{11,7},{20,24},{21,25... | collective-permute-start | bytes 3145736 | tf_op jit(solution)/shard_map/ppermute | solution.py:109
  29.4 1.0 copy-start.8
  71.2 4.3 %collective-permute-start = (bf16[8,1,256,256]{3,2,1,0:T(8,128)(2,1)}, bf16[8,1,256,256]{3,2,1,0:T(8,128)(2,1)S(1)}, u32[]{:S(2)}, u32[]{:S(2)}) collective-permute-start(bf16[8,1,256,256]{3,2,1,0:T(8,128)(2,1)} %refs_0_.7), channel_id=1, source_target_pairs={{0,1},{1,0},{2,3},{3,2},{4,5},{5,4},{6,7},{7,6},{8,9},{9,8},{10,11... | collective-permute-start | bytes 3145736 | tf_op jit(solution)/shard_map/ppermute | solution.py:109
  71.3 69.8 %collective-permute-start.5 = (bf16[1,16,256,256]{3,2,1,0:T(8,128)(2,1)S(1)}, bf16[1,16,256,256]{3,2,1,0:T(8,128)(2,1)}, u32[]{:S(2)}, u32[]{:S(2)}) collective-permute-start(bf16[1,16,256,256]{3,2,1,0:T(8,128)(2,1)S(1)} %collective-permute-done.4.refs_2_), channel_id=1, source_target_pairs={{0,1},{1,0},{2,3},{3,2},{4,5},{5,4},{6,7},{7,6},{8,9},{9,8},{10,11... | collective-permute-start | bytes 6291464 | tf_op jit(solution)/shard_map/ppermute | solution.py:109
  71.8 28.2 %collective-permute-start.10 = (bf16[8,1,256,256]{3,2,1,0:T(8,128)(2,1)}, bf16[8,1,256,256]{3,2,1,0:T(8,128)(2,1)}, u32[]{:S(2)}, u32[]{:S(2)}) collective-permute-start(bf16[8,1,256,256]{3,2,1,0:T(8,128)(2,1)} %collective-permute-done.9.refs_5_), channel_id=1, source_target_pairs={{4,0},{5,1},{6,2},{7,3},{8,12},{9,13},{10,14},{11,15},{20,16},{21,... | collective-permute-start | bytes 3145736 | tf_op jit(solution)/shard_map/ppermute | solution.py:109
  73.1 55.6 %collective-permute-start.14 = (bf16[8,1,256,256]{3,2,1,0:T(8,128)(2,1)}, bf16[8,1,256,256]{3,2,1,0:T(8,128)(2,1)}, u32[]{:S(2)}, u32[]{:S(2)}) collective-permute-start(bf16[8,1,256,256]{3,2,1,0:T(8,128)(2,1)} %collective-permute-done.11.refs_5_), channel_id=1, source_target_pairs={{4,0},{5,1},{6,2},{7,3},{8,12},{9,13},{10,14},{11,15},{20,16},{21,... | collective-permute-start | bytes 3145736 | tf_op jit(solution)/shard_map/ppermute | solution.py:109
  75.5 1.0 copy-start.4
  76.5 64.5 %collective-permute-start.3 = (bf16[8,1,256,256]{3,2,1,0:T(8,128)(2,1)S(1)}, bf16[8,1,256,256]{3,2,1,0:T(8,128)(2,1)}, u32[]{:S(2)}, u32[]{:S(2)}) collective-permute-start(bf16[8,1,256,256]{3,2,1,0:T(8,128)(2,1)S(1)} %collective-permute-done.2.refs_0_), channel_id=1, source_target_pairs={{0,1},{1,0},{2,3},{3,2},{4,5},{5,4},{6,7},{7,6},{8,9},{9,8},{10,11... | collective-permute-start | bytes 3145736 | tf_op jit(solution)/shard_map/ppermute | solution.py:109
  100.0 1.6 copy-start
  101.6 1.2 copy-start.2
  102.8 1.2 copy-start.5
  104.0 0.7 copy-start.12
  104.7 11.1 %copy-start.9 = (bf16[8,1,256,256]{3,2,1,0:T(8,128)(2,1)S(1)}, bf16[8,1,256,256]{3,2,1,0:T(8,128)(2,1)}, u32[]{:S(2)}) copy-start(bf16[8,1,256,256]{3,2,1,0:T(8,128)(2,1)} %copy-done.8) | copy-start | bytes 3145732
  113.8 53.1 %collective-permute-start.12 = (bf16[2,256,256]{2,1,0:T(8,128)(2,1)S(1)}, bf16[2,256,256]{2,1,0:T(8,128)(2,1)S(1)}, u32[]{:S(2)}, u32[]{:S(2)}) collective-permute-start(bf16[2,256,256]{2,1,0:T(8,128)(2,1)S(1)} %shard_map.50), channel_id=1, source_target_pairs={{0,8},{1,9},{2,10},{3,11},{4,12},{5,13},{6,14},{7,15},{8,0},{9,1},... | collective-permute-start | bytes 786440 | tf_op jit(solution)/shard_map/ppermute | solution.py:109
  126.2 63.6 %collective-permute-start.7 = (bf16[2,256,256]{2,1,0:T(8,128)(2,1)S(1)}, bf16[2,256,256]{2,1,0:T(8,128)(2,1)S(1)}, u32[]{:S(2)}, u32[]{:S(2)}) collective-permute-start(bf16[2,256,256]{2,1,0:T(8,128)(2,1)S(1)} %shard_map.48), channel_id=1, source_target_pairs={{0,4},{1,5},{2,6},{3,7},{4,0},{5,1},{6,2},{7,3},{8,12},{9,13},{10,... | collective-permute-start | bytes 786440 | tf_op jit(solution)/shard_map/ppermute | solution.py:109
  137.8 52.0 %collective-permute-start.15 = (bf16[2,256,256]{2,1,0:T(8,128)(2,1)S(1)}, bf16[2,256,256]{2,1,0:T(8,128)(2,1)S(1)}, u32[]{:S(2)}, u32[]{:S(2)}) collective-permute-start(bf16[2,256,256]{2,1,0:T(8,128)(2,1)S(1)} %shard_map.52), channel_id=1, source_target_pairs={{0,12},{1,13},{2,14},{3,15},{4,8},{5,9},{6,10},{7,11},{8,4},{9,5},... | collective-permute-start | bytes 786440 | tf_op jit(solution)/shard_map/ppermute | solution.py:109
  148.8 41.0 %collective-permute-start.13 = (bf16[2,256,256]{2,1,0:T(8,128)(2,1)S(1)}, bf16[2,256,256]{2,1,0:T(8,128)(2,1)S(1)}, u32[]{:S(2)}, u32[]{:S(2)}) collective-permute-start(bf16[2,256,256]{2,1,0:T(8,128)(2,1)S(1)} %shard_map.51), channel_id=1, source_target_pairs={{0,8},{1,9},{2,10},{3,11},{4,12},{5,13},{6,14},{7,15},{8,0},{9,1},... | collective-permute-start | bytes 786440 | tf_op jit(solution)/shard_map/ppermute | solution.py:109
  156.6 13.0 %copy-start.1 = (bf16[1,16,256,256]{3,2,1,0:T(8,128)(2,1)S(1)}, bf16[1,16,256,256]{3,2,1,0:T(8,128)(2,1)}, u32[]{:S(2)}) copy-start(bf16[1,16,256,256]{3,2,1,0:T(8,128)(2,1)} %refs_2_.7) | copy-start | bytes 6291460
  156.6 13.0 %copy-start.3 = (bf16[8,1,256,256]{3,2,1,0:T(8,128)(2,1)S(1)}, bf16[8,1,256,256]{3,2,1,0:T(8,128)(2,1)}, u32[]{:S(2)}) copy-start(bf16[8,1,256,256]{3,2,1,0:T(8,128)(2,1)} %refs_0_.7) | copy-start | bytes 3145732
  156.6 13.0 %copy-start.6 = (bf16[8,1,256,256]{3,2,1,0:T(8,128)(2,1)S(1)}, bf16[8,1,256,256]{3,2,1,0:T(8,128)(2,1)}, u32[]{:S(2)}) copy-start(bf16[8,1,256,256]{3,2,1,0:T(8,128)(2,1)} %copy-done.4) | copy-start | bytes 3145732
  156.6 13.0 %copy-start.7 = (bf16[8,1,256,256]{3,2,1,0:T(8,128)(2,1)S(1)}, bf16[8,1,256,256]{3,2,1,0:T(8,128)(2,1)}, u32[]{:S(2)}) copy-start(bf16[8,1,256,256]{3,2,1,0:T(8,128)(2,1)} %refs_4_.3) | copy-start | bytes 3145732
  156.6 13.0 %copy-start.13 = (s32[8,16]{1,0:T(8,128)S(1)}, s32[8,16]{1,0:T(8,128)}, u32[]{:S(2)}) copy-start(s32[8,16]{1,0:T(8,128)} %source.15) | copy-start | bytes 1540
  156.6 33.2 %collective-permute-start.16 = (bf16[2,256,256]{2,1,0:T(8,128)(2,1)S(1)}, bf16[2,256,256]{2,1,0:T(8,128)(2,1)S(1)}, u32[]{:S(2)}, u32[]{:S(2)}) collective-permute-start(bf16[2,256,256]{2,1,0:T(8,128)(2,1)S(1)} %shard_map.53), channel_id=1, source_target_pairs={{0,12},{1,13},{2,14},{3,15},{4,8},{5,9},{6,10},{7,11},{8,4},{9,5},... | collective-permute-start | bytes 786440 | tf_op jit(solution)/shard_map/ppermute | solution.py:109
  166.9 13.1 %copy-start.14 = (bf16[2,256,256]{2,1,0:T(8,128)(2,1)}, bf16[2,256,256]{2,1,0:T(8,128)(2,1)S(1)}, u32[]{:S(2)}) copy-start(bf16[2,256,256]{2,1,0:T(8,128)(2,1)S(1)} %collective-permute-done.12.refs_4_) | copy-start | bytes 786436
  166.9 24.4 %collective-permute-start.8 = (bf16[2,256,256]{2,1,0:T(8,128)(2,1)S(1)}, bf16[2,256,256]{2,1,0:T(8,128)(2,1)}, u32[]{:S(2)}, u32[]{:S(2)}) collective-permute-start(bf16[2,256,256]{2,1,0:T(8,128)(2,1)S(1)} %shard_map.49), channel_id=1, source_target_pairs={{0,4},{1,5},{2,6},{3,7},{4,0},{5,1},{6,2},{7,3},{8,12},{9,13},{10,... | collective-permute-start | bytes 786440 | tf_op jit(solution)/shard_map/ppermute | solution.py:109
  180.0 9.1 %copy-start.10 = (bf16[2,256,256]{2,1,0:T(8,128)(2,1)}, bf16[2,256,256]{2,1,0:T(8,128)(2,1)S(1)}, u32[]{:S(2)}) copy-start(bf16[2,256,256]{2,1,0:T(8,128)(2,1)S(1)} %shard_map.46.refs_0_) | copy-start | bytes 786436
  189.0 0.7 copy-start.11
  189.7 0.7 copy-start.15
  189.8 0.8 copy-start.16
  189.8 0.9 copy-start.17
  190.7 0.7 copy-start.18

commit v2 on v1

v2 whole, which is shorter than its diff:
```python
import functools

import jax
import jax.numpy as jnp
from jax import lax
from jax.experimental import pallas as pl
from jax.experimental.pallas import tpu as pltpu
from jax.sharding import PartitionSpec as P

HBM = pl.BlockSpec(memory_space=pl.ANY)
SMEM = pl.BlockSpec(memory_space=pltpu.SMEM)
VMEM = pl.BlockSpec(memory_space=pltpu.VMEM)


def slot_kernel(shape, meta, source, *refs):
    parts, choices = shape
    count = len(parts)
    lefts, refs = refs[:count], refs[count:]
    psis = []
    for number in parts:
        psis.append(refs[:number])
        refs = refs[number:]
    rights = refs[:choices]
    out, left_buf, psi_buf, right_buf, mid_buf, left_sem, psi_sem, right_sem = refs[choices:]
    terms, rows, columns = left_buf.shape[1:]
    q = meta[0]

    def left_copy(i, k):
        return pltpu.make_async_copy(lefts[i].at[k, 0], left_buf.at[i, k], left_sem.at[i, k])

    def psi_copy(i, k, part, place):
        return pltpu.make_async_copy(psis[i][part].at[0, place], psi_buf.at[i, k], psi_sem.at[i, k])

    def right_copy(k, choice):
        return pltpu.make_async_copy(
            rights[choice].at[k, 0], right_buf.at[:, pl.ds(k * columns, columns)], right_sem.at[k]
        )

    for k in range(terms):
        for i in range(count):
            left_copy(i, k).start()
            sector = source[k, q]
            if parts[i] == 1:
                psi_copy(i, k, 0, sector).start()
            else:
                held = psis[i][0].shape[1]
                for part in range(parts[i]):

                    @pl.when((sector >= part * held) & (sector < (part + 1) * held))
                    def _(i=i, k=k, part=part, place=sector - part * held):
                        psi_copy(i, k, part, place).start()

    for k in range(terms):
        if choices == 1:
            right_copy(k, 0).start()
        else:
            for choice in range(choices):

                @pl.when(meta[1] == choice)
                def _(k=k, choice=choice):
                    right_copy(k, choice).start()

    for k in range(terms):
        for i in range(count):
            left_copy(i, k).wait()
            psi_copy(i, k, 0, 0).wait()
            mid = jnp.dot(left_buf[i, k], psi_buf[i, k], preferred_element_type=jnp.float32)
            mid_buf[pl.ds(i * rows, rows), pl.ds(k * columns, columns)] = mid.astype(jnp.bfloat16)
    for k in range(terms):
        right_copy(k, 0).wait()
    total = lax.dot_general(
        mid_buf[...], right_buf[...], (((1,), (1,)), ((), ())), preferred_element_type=jnp.float32
    )
    out[...] = total.reshape(out.shape).astype(out.dtype)


def slot(q, choice, source_map, lefts, psis, rights, dtype):
    terms, _, rows, columns = lefts[0].shape
    count = len(lefts)
    parts = tuple(len(psi) for psi in psis)
    meta = jnp.stack([q, choice]).astype(jnp.int32)
    block = rows * columns
    return pl.pallas_call(
        functools.partial(slot_kernel, (parts, len(rights))),
        out_shape=jax.ShapeDtypeStruct((count, rows, columns), dtype),
        in_specs=[SMEM, SMEM] + [HBM] * (count + sum(parts) + len(rights)),
        out_specs=VMEM,
        scratch_shapes=[
            pltpu.VMEM((count, terms, rows, columns), jnp.bfloat16),
            pltpu.VMEM((count, terms, rows, columns), jnp.bfloat16),
            pltpu.VMEM((rows, terms * columns), jnp.bfloat16),
            pltpu.VMEM((count * rows, terms * columns), jnp.bfloat16),
            pltpu.SemaphoreType.DMA((count, terms)),
            pltpu.SemaphoreType.DMA((count, terms)),
            pltpu.SemaphoreType.DMA((terms,)),
        ],
        compiler_params=pltpu.CompilerParams(vmem_limit_bytes=24 << 20),
        cost_estimate=pl.CostEstimate(
            flops=4 * count * terms * block * rows,
            bytes_accessed=2 * block * terms * (2 * count + 1) + 2 * block * count,
            transcendentals=0,
        ),
    )(meta, source_map, *lefts, *[part for psi in psis for part in psi], *rights)


def place_kernel(width, meta, *refs):
    pieces, out, sem = refs[:-2], refs[-2], refs[-1]
    me = meta[0]

    def copy(j):
        return pltpu.make_async_copy(pieces[j // width].at[j % width], out.at[me ^ j], sem.at[j])

    for j in range(len(pieces) * width):
        copy(j).start()
    for j in range(len(pieces) * width):
        copy(j).wait()


def place(me, pieces):
    width, rows, columns = pieces[0].shape
    sectors = width * len(pieces)
    return pl.pallas_call(
        functools.partial(place_kernel, width),
        out_shape=jax.ShapeDtypeStruct((sectors, rows, columns), pieces[0].dtype),
        in_specs=[SMEM] + [HBM] * len(pieces),
        out_specs=VMEM,
        scratch_shapes=[pltpu.SemaphoreType.DMA((sectors,))],
        compiler_params=pltpu.CompilerParams(vmem_limit_bytes=16 << 20),
    )(me[None].astype(jnp.int32), *pieces)


def exchange(array, bits, members):
    return lax.ppermute(array, "sec", [(s, s ^ bits) for s in members])


def on_device(ops, psi, left_env, right_env, source_map):
    me = lax.axis_index("sec")
    row = me // 4
    choice = jnp.where((row == 0) | (row == 3), 0, 1)
    dtype = jnp.bfloat16 if ops == 1 else jnp.float32
    every = range(16)
    inner = range(4, 12)
    half = psi.shape[1] // 2
    low, high = psi[:, :half], psi[:, half:]

    def products(step, lefts, psis, rights):
        return slot(me ^ (4 * step), choice, source_map, lefts, psis, rights, dtype)

    near = exchange(right_env, 4, every)
    middle = exchange(right_env, 12, inner)
    x_left = exchange(left_env, 2, every)
    x_low = exchange(low, 2, every)
    core_left = exchange(left_env, 1, every)
    core_psi = exchange(psi, 1, every)
    own = ([left_env, core_left], [(psi,), (core_psi,)])

    near, middle, high_next = lax.optimization_barrier((near, middle, high))
    far_in = exchange(near, 12, inner)
    second = exchange(middle, 4, inner)
    x_high = exchange(high_next, 2, every)
    own_1 = products(1, *own, (near,))
    sent_1 = exchange(own_1, 4, every)

    second, far_in, x_left, x_low, own_1 = lax.optimization_barrier((second, far_in, x_left, x_low, own_1))
    third = exchange(far_in, 4, inner)
    across_left = exchange(x_left, 1, every)
    across_low = exchange(x_low, 1, every)
    own_2 = products(2, *own, (second, far_in))
    sent_2 = exchange(own_2, 8, every)

    third, x_high, own_2 = lax.optimization_barrier((third, x_high, own_2))
    across_high = exchange(x_high, 1, every)
    own_3 = products(3, *own, (third, middle))
    sent_3 = exchange(own_3, 12, every)
    other = ([x_left, across_left], [(x_low, x_high), (across_low, across_high)])
    other_1 = products(1, *other, (near,))
    other_sent_1 = exchange(other_1, 4, every)
    other_2 = products(2, *other, (second, far_in))
    other_sent_2 = exchange(other_2, 8, every)
    other_3 = products(3, *other, (third, middle))
    other_sent_3 = exchange(other_3, 12, every)
    own_0 = products(0, *own, (right_env,))
    other_0 = products(0, *other, (right_env,))

    pieces = [own_0, other_0, sent_1, other_sent_1, sent_2, other_sent_2, sent_3, other_sent_3]
    out = place(me, pieces)[:, None]
    if ops > 1:
        out = lax.psum_scatter(out, "op", scatter_dimension=2, tiled=True).astype(jnp.bfloat16)
    return out


def solution(mesh):
    placed = (
        P(("group", "sec"), None, None, None),
        P(("group", "op"), "sec", None, None),
        P(("group", "op"), "sec", None, None),
        P(("group", "op"), None),
    )
    return jax.shard_map(
        functools.partial(on_device, mesh.shape["op"]),
        mesh=mesh,
        in_specs=placed,
        out_specs=P("group", "sec", "op", None),
        check_vma=False,
    )
```

time: 257 us -> 146 us (0.57)
  Pallas kernels: 137 us -> 68 us
  waiting for transfers between devices: 86.2 us -> 46.2 us
    pallas_call x1, Pallas kernels: 64.8 us -> 4.2 us  [place(): pl.pallas_call(functools.partial(place_kernel, width), out_shape=jax.Shap...]
    ppermute x17 -> x19, waiting for transfers between devices: 86.2 us -> 46.2 us  [exchange(): return lax.ppermute(array, 'sec', [(s, s ^ bits) for s in members])]
    pallas_call x8, Pallas kernels: 72.5 us -> 63.8 us  [slot(): pl.pallas_call(functools.partial(slot_kernel, (parts, len(rights))), out_...]
    unnamed x38 -> x20, local copies, waits for them, and re-layouts: 9.03 us -> 5.35 us
    slice x0 -> x1, local copies, waits for them, and re-layouts: none -> 3.07 us  [on_device(): low, high = (psi[:, :half], psi[:, half:])]
    ppermute x17 -> x19, starting transfers between devices: 23.1 us -> 22.5 us  [exchange(): return lax.ppermute(array, 'sec', [(s, s ^ bits) for s in members])]
  transfers between devices with their start and end apart: 17 -> 19, of which waited for: 4 -> 5; matrix products, arithmetic and copies ran while one was open for 0% -> 2% of each run, Pallas kernels for 28% -> 44%
where the time goes in v2:
time: 146 us
  Pallas kernels  68 us (47%)
  waiting for transfers between devices  46.2 us (32%)
  starting transfers between devices  22.5 us (15%)
  local copies, waits for them, and re-layouts  8.43 us (6%)
    pallas_call x8, Pallas kernels, slot(): pl.pallas_call(functools.partial(slot_kernel, (parts, len(rights))), out_...  63.8 us
    ppermute x19, waiting for transfers between devices, exchange(): return lax.ppermute(array, 'sec', [(s, s ^ bits) for s in members])  46.2 us
    ppermute x19, starting transfers between devices, exchange(): return lax.ppermute(array, 'sec', [(s, s ^ bits) for s in members])  22.5 us
    unnamed x20, local copies, waits for them, and re-layouts  5.35 us
    pallas_call x1, Pallas kernels, place(): pl.pallas_call(functools.partial(place_kernel, width), out_shape=jax.Shap...  4.2 us
    slice x1, local copies, waits for them, and re-layouts, on_device(): low, high = (psi[:, :half], psi[:, half:])  3.07 us
  transfers between devices with their start and end apart: 19, of which 5 were waited for; matrix products, arithmetic and copies ran while one was open for 2% of the time, Pallas kernels for 44%

profile of v2, /device:TPU:0, one launch (start us, length us, event | category | flops | bytes accessed | tf_op | source)
XLA Modules:
  0.0 145.8 jit_solution(1903681767082773906)
XLA Ops:
  0.0 0.5 collective-permute-start.1
  0.5 2.7 %collective-permute-start.2 = (bf16[8,1,256,256]{3,2,1,0:T(8,128)(2,1)}, bf16[8,1,256,256]{3,2,1,0:T(8,128)(2,1)}, u32[]{:S(2)}, u32[]{:S(2)}) collective-permute-start(bf16[8,1,256,256]{3,2,1,0:T(8,128)(2,1)} %refs_6_.1), channel_id=1, source_target_pairs={{0,4},{1,5},{2,6},{3,7},{4,0},{5,1},{6,2},{7,3},{8,12},{9,13},{10,... | collective-permute-start | bytes 3145736 | tf_op jit(solution)/shard_map/ppermute | solution.py:133
  3.2 1.7 %collective-permute-start.3 = (bf16[8,1,256,256]{3,2,1,0:T(8,128)(2,1)}, bf16[8,1,256,256]{3,2,1,0:T(8,128)(2,1)}, u32[]{:S(2)}, u32[]{:S(2)}) collective-permute-start(bf16[8,1,256,256]{3,2,1,0:T(8,128)(2,1)} %refs_6_.1), channel_id=1, source_target_pairs={{4,8},{5,9},{6,10},{7,11},{8,4},{9,5},{10,6},{11,7},{20,24},{21,25... | collective-permute-start | bytes 3145736 | tf_op jit(solution)/shard_map/ppermute | solution.py:133
  4.8 0.2 collective-permute-start
  5.0 1.5 %collective-permute-start.6 = (bf16[8,1,256,256]{3,2,1,0:T(8,128)(2,1)}, bf16[8,1,256,256]{3,2,1,0:T(8,128)(2,1)}, u32[]{:S(2)}, u32[]{:S(2)}) collective-permute-start(bf16[8,1,256,256]{3,2,1,0:T(8,128)(2,1)} %refs_0_.7), channel_id=1, source_target_pairs={{0,2},{1,3},{2,0},{3,1},{4,6},{5,7},{6,4},{7,5},{8,10},{9,11},{10,... | collective-permute-start | bytes 3145736 | tf_op jit(solution)/shard_map/ppermute | solution.py:133
  6.5 3.1 %fusion = (bf16[1,8,256,256]{3,2,1,0:T(8,128)(2,1)}, bf16[1,8,256,256]{3,2,1,0:T(8,128)(2,1)}) fusion(bf16[1,16,256,256]{3,2,1,0:T(8,128)(2,1)} %refs_2_.7), kind=kLoop, calls=%fused_computation.4 | loop fusion | bytes 4194304 | tf_op jit(solution)/shard_map/slice | solution.py:144
  9.6 17.7 %collective-permute-done.2.refs_4_.refs_6_ = bf16[8,1,256,256]{3,2,1,0:T(8,128)(2,1)} collective-permute-done((bf16[8,1,256,256]{3,2,1,0:T(8,128)(2,1)}, bf16[8,1,256,256]{3,2,1,0:T(8,128)(2,1)}, u32[]{:S(2)}, u32[]{:S(2)}) %collective-permute-start.2) | collective-permute-done | bytes 1048608 | tf_op jit(solution)/shard_map/ppermute | solution.py:133
  27.2 1.7 %collective-permute-start.7 = (bf16[1,8,256,256]{3,2,1,0:T(8,128)(2,1)}, bf16[1,8,256,256]{3,2,1,0:T(8,128)(2,1)}, u32[]{:S(2)}, u32[]{:S(2)}) collective-permute-start(bf16[1,8,256,256]{3,2,1,0:T(8,128)(2,1)} %get-tuple-element.23), channel_id=1, source_target_pairs={{0,2},{1,3},{2,0},{3,1},{4,6},{5,7},{6,4},{7,5},{8,10},{9,11},{10,... | collective-permute-start | bytes 3145736 | tf_op jit(solution)/shard_map/ppermute | solution.py:133
  28.9 1.3 collective-permute-start.4
  30.2 0.0 collective-permute-done.refs_1_
  30.2 0.0 copy-start.2
  30.2 1.0 copy-done.2
  31.2 1.7 %collective-permute-start.5 = (bf16[8,1,256,256]{3,2,1,0:T(8,128)(2,1)}, bf16[8,1,256,256]{3,2,1,0:T(8,128)(2,1)}, u32[]{:S(2)}, u32[]{:S(2)}) collective-permute-start(bf16[8,1,256,256]{3,2,1,0:T(8,128)(2,1)} %collective-permute-done.2.refs_4_.refs_6_), channel_id=1, source_target_pairs={{4,8},{5,9},{6,10},{7,11},{8,4},{9,5},{10,6},{11,7},{20,24},{21,25... | collective-permute-start | bytes 3145736 | tf_op jit(solution)/shard_map/ppermute | solution.py:133
  32.9 0.1 pad_add_fusion.1.meta
  33.0 0.4 collective-permute-start.10
  33.4 1.2 copy-done.3
  34.6 9.3 %shard_map.47 = bf16[2,256,256]{2,1,0:T(8,128)(2,1)S(1)} custom-call(s32[2]{0:T(128)S(1)} %pad_add_fusion.1.meta, s32[8,16]{1,0:T(8,128)S(1)} %copy-done.8, bf16[8,1,256,256]{3,2,1,0:T(8,128)(2,1)S(1)} %copy-done.1, bf16[8,1,256,256]{3,2,1,0:T(8,128)(2,1)S(1)} %copy-done.3, bf16[1,16,256,256]{3,2,1,0:T(8,128)(2,1)S(1)} %copy-done, ...), custom_call_target="tpu_custom_call" | custom-call | flops 1073741824 | bytes 5505024 | tf_op jit(solution)/shard_map/pallas_call | solution.py:83
  43.9 0.0 collective-permute-done.6.refs_0_
  43.9 9.9 %collective-permute-done.7.refs_2_ = bf16[1,8,256,256]{3,2,1,0:T(8,128)(2,1)} collective-permute-done((bf16[1,8,256,256]{3,2,1,0:T(8,128)(2,1)}, bf16[1,8,256,256]{3,2,1,0:T(8,128)(2,1)}, u32[]{:S(2)}, u32[]{:S(2)}) %collective-permute-start.7) | collective-permute-done | bytes 1048608 | tf_op jit(solution)/shard_map/ppermute | solution.py:133
  53.8 2.8 %collective-permute-done.4.refs_4_.refs_6_ = bf16[8,1,256,256]{3,2,1,0:T(8,128)(2,1)} collective-permute-done((bf16[8,1,256,256]{3,2,1,0:T(8,128)(2,1)}, bf16[8,1,256,256]{3,2,1,0:T(8,128)(2,1)}, u32[]{:S(2)}, u32[]{:S(2)}) %collective-permute-start.4) | collective-permute-done | bytes 1048608 | tf_op jit(solution)/shard_map/ppermute | solution.py:133
  56.6 0.0 collective-permute-done.5.refs_5_.refs_7_
  56.6 1.5 %collective-permute-start.9 = (bf16[8,1,256,256]{3,2,1,0:T(8,128)(2,1)}, bf16[8,1,256,256]{3,2,1,0:T(8,128)(2,1)}, u32[]{:S(2)}, u32[]{:S(2)}) collective-permute-start(bf16[8,1,256,256]{3,2,1,0:T(8,128)(2,1)} %collective-permute-done.5.refs_5_.refs_7_), channel_id=1, source_target_pairs={{4,0},{5,1},{6,2},{7,3},{8,12},{9,13},{10,14},{11,15},{20,16},{21,... | collective-permute-start | bytes 3145736 | tf_op jit(solution)/shard_map/ppermute | solution.py:133
  58.1 0.1 pad_add_fusion.2.meta
  58.1 0.0 collective-permute-start.8
  58.2 0.5 collective-permute-start.11
  58.7 1.2 copy-done.4
  59.9 9.3 %shard_map.48 = bf16[2,256,256]{2,1,0:T(8,128)(2,1)S(1)} custom-call(s32[2]{0:T(128)S(1)} %pad_add_fusion.2.meta, s32[8,16]{1,0:T(8,128)S(1)} %copy-done.8, bf16[8,1,256,256]{3,2,1,0:T(8,128)(2,1)S(1)} %copy-done.1, bf16[8,1,256,256]{3,2,1,0:T(8,128)(2,1)S(1)} %copy-done.4, bf16[1,16,256,256]{3,2,1,0:T(8,128)(2,1)S(1)} %copy-done, ...), custom_call_target="tpu_custom_call" | custom-call | flops 1073741824 | bytes 5505024 | tf_op jit(solution)/shard_map/pallas_call | solution.py:83
  69.2 0.7 copy-done.9
  69.9 5.7 %collective-permute-done.10.refs_3_ = bf16[1,8,256,256]{3,2,1,0:T(8,128)(2,1)} collective-permute-done((bf16[1,8,256,256]{3,2,1,0:T(8,128)(2,1)}, bf16[1,8,256,256]{3,2,1,0:T(8,128)(2,1)}, u32[]{:S(2)}, u32[]{:S(2)}) %collective-permute-start.10) | collective-permute-done | bytes 1048608 | tf_op jit(solution)/shard_map/ppermute | solution.py:133
  75.7 10.0 %collective-permute-done.9.refs_4_.refs_6_ = bf16[8,1,256,256]{3,2,1,0:T(8,128)(2,1)} collective-permute-done((bf16[8,1,256,256]{3,2,1,0:T(8,128)(2,1)}, bf16[8,1,256,256]{3,2,1,0:T(8,128)(2,1)}, u32[]{:S(2)}, u32[]{:S(2)}) %collective-permute-start.9) | collective-permute-done | bytes 1048608 | tf_op jit(solution)/shard_map/ppermute | solution.py:133
  85.7 0.1 pad_add_fusion.3.meta
  85.8 0.3 collective-permute-start.15
  86.1 2.5 %collective-permute-start.13 = (bf16[2,256,256]{2,1,0:T(8,128)(2,1)S(1)}, bf16[2,256,256]{2,1,0:T(8,128)(2,1)S(1)}, u32[]{:S(2)}, u32[]{:S(2)}) collective-permute-start(bf16[2,256,256]{2,1,0:T(8,128)(2,1)S(1)} %shard_map.47), channel_id=1, source_target_pairs={{0,4},{1,5},{2,6},{3,7},{4,0},{5,1},{6,2},{7,3},{8,12},{9,13},{10,... | collective-permute-start | bytes 786440 | tf_op jit(solution)/shard_map/ppermute | solution.py:133
  88.6 1.2 copy-done.5
  89.8 9.3 %shard_map.52 = bf16[2,256,256]{2,1,0:T(8,128)(2,1)S(1)} custom-call(s32[2]{0:T(128)S(1)} %pad_add_fusion.3.meta, s32[8,16]{1,0:T(8,128)S(1)} %copy-done.8, bf16[8,1,256,256]{3,2,1,0:T(8,128)(2,1)S(1)} %copy-done.1, bf16[8,1,256,256]{3,2,1,0:T(8,128)(2,1)S(1)} %copy-done.5, bf16[1,16,256,256]{3,2,1,0:T(8,128)(2,1)S(1)} %copy-done, ...), custom_call_target="tpu_custom_call" | custom-call | flops 1073741824 | bytes 5505024 | tf_op jit(solution)/shard_map/pallas_call | solution.py:83
  99.2 1.7 %collective-permute-start.17 = (bf16[2,256,256]{2,1,0:T(8,128)(2,1)S(1)}, bf16[2,256,256]{2,1,0:T(8,128)(2,1)S(1)}, u32[]{:S(2)}, u32[]{:S(2)}) collective-permute-start(bf16[2,256,256]{2,1,0:T(8,128)(2,1)S(1)} %shard_map.52), channel_id=1, source_target_pairs={{0,12},{1,13},{2,14},{3,15},{4,8},{5,9},{6,10},{7,11},{8,4},{9,5},... | collective-permute-start | bytes 786440 | tf_op jit(solution)/shard_map/ppermute | solution.py:133
  100.8 6.5 %shard_map.50 = bf16[2,256,256]{2,1,0:T(8,128)(2,1)S(1)} custom-call(s32[2]{0:T(128)S(1)} %pad_add_fusion.1.meta, s32[8,16]{1,0:T(8,128)S(1)} %copy-done.8, bf16[8,1,256,256]{3,2,1,0:T(8,128)(2,1)} %collective-permute-done.6.refs_0_, bf16[8,1,256,256]{3,2,1,0:T(8,128)(2,1)} %collective-permute-done.8.refs_1_, ...), custom_call_target="tpu_custom_call" | custom-call | flops 1073741824 | bytes 5505024 | tf_op jit(solution)/shard_map/pallas_call | solution.py:83
  107.4 0.1 collective-permute-start.14
  107.5 6.5 %shard_map.51 = bf16[2,256,256]{2,1,0:T(8,128)(2,1)S(1)} custom-call(s32[2]{0:T(128)S(1)} %pad_add_fusion.2.meta, s32[8,16]{1,0:T(8,128)S(1)} %copy-done.8, bf16[8,1,256,256]{3,2,1,0:T(8,128)(2,1)} %collective-permute-done.6.refs_0_, bf16[8,1,256,256]{3,2,1,0:T(8,128)(2,1)} %collective-permute-done.8.refs_1_, ...), custom_call_target="tpu_custom_call" | custom-call | flops 1073741824 | bytes 5505024 | tf_op jit(solution)/shard_map/pallas_call | solution.py:83
  114.0 0.0 copy-start.6
  114.0 0.0 copy-start.7
  114.0 2.9 %collective-permute-start.16 = (bf16[2,256,256]{2,1,0:T(8,128)(2,1)S(1)}, bf16[2,256,256]{2,1,0:T(8,128)(2,1)S(1)}, u32[]{:S(2)}, u32[]{:S(2)}) collective-permute-start(bf16[2,256,256]{2,1,0:T(8,128)(2,1)S(1)} %shard_map.51), channel_id=1, source_target_pairs={{0,8},{1,9},{2,10},{3,11},{4,12},{5,13},{6,14},{7,15},{8,0},{9,1},... | collective-permute-start | bytes 786440 | tf_op jit(solution)/shard_map/ppermute | solution.py:133
  116.9 6.5 %shard_map.53 = bf16[2,256,256]{2,1,0:T(8,128)(2,1)S(1)} custom-call(s32[2]{0:T(128)S(1)} %pad_add_fusion.3.meta, s32[8,16]{1,0:T(8,128)S(1)} %copy-done.8, bf16[8,1,256,256]{3,2,1,0:T(8,128)(2,1)} %collective-permute-done.6.refs_0_, bf16[8,1,256,256]{3,2,1,0:T(8,128)(2,1)} %collective-permute-done.8.refs_1_, ...), custom_call_target="tpu_custom_call" | custom-call | flops 1073741824 | bytes 5505024 | tf_op jit(solution)/shard_map/pallas_call | solution.py:83
  123.4 1.6 %collective-permute-start.18 = (bf16[2,256,256]{2,1,0:T(8,128)(2,1)S(1)}, bf16[2,256,256]{2,1,0:T(8,128)(2,1)S(1)}, u32[]{:S(2)}, u32[]{:S(2)}) collective-permute-start(bf16[2,256,256]{2,1,0:T(8,128)(2,1)S(1)} %shard_map.53), channel_id=1, source_target_pairs={{0,12},{1,13},{2,14},{3,15},{4,8},{5,9},{6,10},{7,11},{8,4},{9,5},... | collective-permute-start | bytes 786440 | tf_op jit(solution)/shard_map/ppermute | solution.py:133
  125.1 0.1 pad_add_fusion.meta
  125.1 9.7 %shard_map.46.refs_0_ = bf16[2,256,256]{2,1,0:T(8,128)(2,1)S(1)} custom-call(s32[2]{0:T(128)S(1)} %pad_add_fusion.meta, s32[8,16]{1,0:T(8,128)S(1)} %copy-done.8, bf16[8,1,256,256]{3,2,1,0:T(8,128)(2,1)S(1)} %copy-done.1, bf16[8,1,256,256]{3,2,1,0:T(8,128)(2,1)S(1)} %copy-done.6, bf16[1,16,256,256]{3,2,1,0:T(8,128)(2,1)S(1)} %copy-done, ...), custom_call_target="tpu_custom_call" | custom-call | flops 1073741824 | bytes 5505024 | tf_op jit(solution)/shard_map/pallas_call | solution.py:83
  134.8 6.5 %shard_map.49.refs_1_ = bf16[2,256,256]{2,1,0:T(8,128)(2,1)S(1)} custom-call(s32[2]{0:T(128)S(1)} %pad_add_fusion.meta, s32[8,16]{1,0:T(8,128)S(1)} %copy-done.8, bf16[8,1,256,256]{3,2,1,0:T(8,128)(2,1)} %collective-permute-done.6.refs_0_, bf16[8,1,256,256]{3,2,1,0:T(8,128)(2,1)} %collective-permute-done.8.refs_1_, ...), custom_call_target="tpu_custom_call" | custom-call | flops 1073741824 | bytes 5505024 | tf_op jit(solution)/shard_map/pallas_call | solution.py:83
  141.4 4.2 %shard_map.54 = bf16[16,256,256]{2,1,0:T(8,128)(2,1)} custom-call(s32[1]{0:T(128)} %bitcast.meta, bf16[2,256,256]{2,1,0:T(8,128)(2,1)S(1)} %shard_map.46.refs_0_, bf16[2,256,256]{2,1,0:T(8,128)(2,1)S(1)} %shard_map.49.refs_1_, bf16[2,256,256]{2,1,0:T(8,128)(2,1)S(1)} %collective-permute-done.13.refs_2_, ...), custom_call_target="tpu_custom_call" | custom-call | tf_op jit(solution)/shard_map/pallas_call | solution.py:122
  (24 shorter events, 0.1 us)
Async XLA Ops:
  0.0 33.3 %copy-start = (bf16[1,16,256,256]{3,2,1,0:T(8,128)(2,1)S(1)}, bf16[1,16,256,256]{3,2,1,0:T(8,128)(2,1)}, u32[]{:S(2)}) copy-start(bf16[1,16,256,256]{3,2,1,0:T(8,128)(2,1)} %refs_2_.7) | copy-start | bytes 6291460
  0.0 33.3 %copy-start.1 = (bf16[8,1,256,256]{3,2,1,0:T(8,128)(2,1)S(1)}, bf16[8,1,256,256]{3,2,1,0:T(8,128)(2,1)}, u32[]{:S(2)}) copy-start(bf16[8,1,256,256]{3,2,1,0:T(8,128)(2,1)} %refs_0_.7) | copy-start | bytes 3145732
  0.0 33.3 %copy-start.8 = (s32[8,16]{1,0:T(8,128)S(1)}, s32[8,16]{1,0:T(8,128)}, u32[]{:S(2)}) copy-start(s32[8,16]{1,0:T(8,128)} %source.15) | copy-start | bytes 1540
  0.0 33.0 %collective-permute-start.1 = (bf16[1,16,256,256]{3,2,1,0:T(8,128)(2,1)}, bf16[1,16,256,256]{3,2,1,0:T(8,128)(2,1)}, u32[]{:S(2)}, u32[]{:S(2)}) collective-permute-start(bf16[1,16,256,256]{3,2,1,0:T(8,128)(2,1)} %refs_2_.7), channel_id=1, source_target_pairs={{0,1},{1,0},{2,3},{3,2},{4,5},{5,4},{6,7},{7,6},{8,9},{9,8},{10,11... | collective-permute-start | bytes 6291464 | tf_op jit(solution)/shard_map/ppermute | solution.py:133
  0.5 26.7 %collective-permute-start.2 = (bf16[8,1,256,256]{3,2,1,0:T(8,128)(2,1)}, bf16[8,1,256,256]{3,2,1,0:T(8,128)(2,1)}, u32[]{:S(2)}, u32[]{:S(2)}) collective-permute-start(bf16[8,1,256,256]{3,2,1,0:T(8,128)(2,1)} %refs_6_.1), channel_id=1, source_target_pairs={{0,4},{1,5},{2,6},{3,7},{4,0},{5,1},{6,2},{7,3},{8,12},{9,13},{10,... | collective-permute-start | bytes 3145736 | tf_op jit(solution)/shard_map/ppermute | solution.py:133
  3.2 25.7 %collective-permute-start.3 = (bf16[8,1,256,256]{3,2,1,0:T(8,128)(2,1)}, bf16[8,1,256,256]{3,2,1,0:T(8,128)(2,1)}, u32[]{:S(2)}, u32[]{:S(2)}) collective-permute-start(bf16[8,1,256,256]{3,2,1,0:T(8,128)(2,1)} %refs_6_.1), channel_id=1, source_target_pairs={{4,8},{5,9},{6,10},{7,11},{8,4},{9,5},{10,6},{11,7},{20,24},{21,25... | collective-permute-start | bytes 3145736 | tf_op jit(solution)/shard_map/ppermute | solution.py:133
  4.8 25.4 %collective-permute-start = (bf16[8,1,256,256]{3,2,1,0:T(8,128)(2,1)}, bf16[8,1,256,256]{3,2,1,0:T(8,128)(2,1)S(1)}, u32[]{:S(2)}, u32[]{:S(2)}) collective-permute-start(bf16[8,1,256,256]{3,2,1,0:T(8,128)(2,1)} %refs_0_.7), channel_id=1, source_target_pairs={{0,1},{1,0},{2,3},{3,2},{4,5},{5,4},{6,7},{7,6},{8,9},{9,8},{10,11... | collective-permute-start | bytes 3145736 | tf_op jit(solution)/shard_map/ppermute | solution.py:133
  5.0 38.9 %collective-permute-start.6 = (bf16[8,1,256,256]{3,2,1,0:T(8,128)(2,1)}, bf16[8,1,256,256]{3,2,1,0:T(8,128)(2,1)}, u32[]{:S(2)}, u32[]{:S(2)}) collective-permute-start(bf16[8,1,256,256]{3,2,1,0:T(8,128)(2,1)} %refs_0_.7), channel_id=1, source_target_pairs={{0,2},{1,3},{2,0},{3,1},{4,6},{5,7},{6,4},{7,5},{8,10},{9,11},{10,... | collective-permute-start | bytes 3145736 | tf_op jit(solution)/shard_map/ppermute | solution.py:133
  27.2 26.5 %collective-permute-start.7 = (bf16[1,8,256,256]{3,2,1,0:T(8,128)(2,1)}, bf16[1,8,256,256]{3,2,1,0:T(8,128)(2,1)}, u32[]{:S(2)}, u32[]{:S(2)}) collective-permute-start(bf16[1,8,256,256]{3,2,1,0:T(8,128)(2,1)} %get-tuple-element.23), channel_id=1, source_target_pairs={{0,2},{1,3},{2,0},{3,1},{4,6},{5,7},{6,4},{7,5},{8,10},{9,11},{10,... | collective-permute-start | bytes 3145736 | tf_op jit(solution)/shard_map/ppermute | solution.py:133
  28.9 27.7 %collective-permute-start.4 = (bf16[8,1,256,256]{3,2,1,0:T(8,128)(2,1)}, bf16[8,1,256,256]{3,2,1,0:T(8,128)(2,1)}, u32[]{:S(2)}, u32[]{:S(2)}) collective-permute-start(bf16[8,1,256,256]{3,2,1,0:T(8,128)(2,1)} %collective-permute-done.3.refs_5_.refs_7_), channel_id=1, source_target_pairs={{4,0},{5,1},{6,2},{7,3},{8,12},{9,13},{10,14},{11,15},{20,16},{21,... | collective-permute-start | bytes 3145736 | tf_op jit(solution)/shard_map/ppermute | solution.py:133
  30.2 1.0 copy-start.2
  31.2 25.4 %collective-permute-start.5 = (bf16[8,1,256,256]{3,2,1,0:T(8,128)(2,1)}, bf16[8,1,256,256]{3,2,1,0:T(8,128)(2,1)}, u32[]{:S(2)}, u32[]{:S(2)}) collective-permute-start(bf16[8,1,256,256]{3,2,1,0:T(8,128)(2,1)} %collective-permute-done.2.refs_4_.refs_6_), channel_id=1, source_target_pairs={{4,8},{5,9},{6,10},{7,11},{8,4},{9,5},{10,6},{11,7},{20,24},{21,25... | collective-permute-start | bytes 3145736 | tf_op jit(solution)/shard_map/ppermute | solution.py:133
  33.0 42.7 %collective-permute-start.10 = (bf16[1,8,256,256]{3,2,1,0:T(8,128)(2,1)}, bf16[1,8,256,256]{3,2,1,0:T(8,128)(2,1)}, u32[]{:S(2)}, u32[]{:S(2)}) collective-permute-start(bf16[1,8,256,256]{3,2,1,0:T(8,128)(2,1)} %get-tuple-element.19), channel_id=1, source_target_pairs={{0,2},{1,3},{2,0},{3,1},{4,6},{5,7},{6,4},{7,5},{8,10},{9,11},{10,... | collective-permute-start | bytes 3145736 | tf_op jit(solution)/shard_map/ppermute | solution.py:133
  33.3 1.2 copy-start.3
  56.6 29.1 %collective-permute-start.9 = (bf16[8,1,256,256]{3,2,1,0:T(8,128)(2,1)}, bf16[8,1,256,256]{3,2,1,0:T(8,128)(2,1)}, u32[]{:S(2)}, u32[]{:S(2)}) collective-permute-start(bf16[8,1,256,256]{3,2,1,0:T(8,128)(2,1)} %collective-permute-done.5.refs_5_.refs_7_), channel_id=1, source_target_pairs={{4,0},{5,1},{6,2},{7,3},{8,12},{9,13},{10,14},{11,15},{20,16},{21,... | collective-permute-start | bytes 3145736 | tf_op jit(solution)/shard_map/ppermute | solution.py:133
  58.1 41.0 %collective-permute-start.8 = (bf16[8,1,256,256]{3,2,1,0:T(8,128)(2,1)}, bf16[8,1,256,256]{3,2,1,0:T(8,128)(2,1)}, u32[]{:S(2)}, u32[]{:S(2)}) collective-permute-start(bf16[8,1,256,256]{3,2,1,0:T(8,128)(2,1)} %collective-permute-done.6.refs_0_), channel_id=1, source_target_pairs={{0,1},{1,0},{2,3},{3,2},{4,5},{5,4},{6,7},{7,6},{8,9},{9,8},{10,11... | collective-permute-start | bytes 3145736 | tf_op jit(solution)/shard_map/ppermute | solution.py:133
  58.2 42.7 %collective-permute-start.11 = (bf16[1,8,256,256]{3,2,1,0:T(8,128)(2,1)}, bf16[1,8,256,256]{3,2,1,0:T(8,128)(2,1)}, u32[]{:S(2)}, u32[]{:S(2)}) collective-permute-start(bf16[1,8,256,256]{3,2,1,0:T(8,128)(2,1)} %collective-permute-done.7.refs_2_), channel_id=1, source_target_pairs={{0,1},{1,0},{2,3},{3,2},{4,5},{5,4},{6,7},{7,6},{8,9},{9,8},{10,11... | collective-permute-start | bytes 3145736 | tf_op jit(solution)/shard_map/ppermute | solution.py:133
  58.7 1.2 copy-start.4
  69.2 0.7 copy-start.9
  85.7 15.1 %collective-permute-start.12 = (bf16[1,8,256,256]{3,2,1,0:T(8,128)(2,1)}, bf16[1,8,256,256]{3,2,1,0:T(8,128)(2,1)}, u32[]{:S(2)}, u32[]{:S(2)}) collective-permute-start(bf16[1,8,256,256]{3,2,1,0:T(8,128)(2,1)} %collective-permute-done.10.refs_3_), channel_id=1, source_target_pairs={{0,1},{1,0},{2,3},{3,2},{4,5},{5,4},{6,7},{7,6},{8,9},{9,8},{10,11... | collective-permute-start | bytes 3145736 | tf_op jit(solution)/shard_map/ppermute | solution.py:133
  85.8 37.6 %collective-permute-start.15 = (bf16[2,256,256]{2,1,0:T(8,128)(2,1)}, bf16[2,256,256]{2,1,0:T(8,128)(2,1)S(1)}, u32[]{:S(2)}, u32[]{:S(2)}) collective-permute-start(bf16[2,256,256]{2,1,0:T(8,128)(2,1)} %copy-done.9), channel_id=1, source_target_pairs={{0,8},{1,9},{2,10},{3,11},{4,12},{5,13},{6,14},{7,15},{8,0},{9,1},... | collective-permute-start | bytes 786440 | tf_op jit(solution)/shard_map/ppermute | solution.py:133
  86.1 55.2 %collective-permute-start.13 = (bf16[2,256,256]{2,1,0:T(8,128)(2,1)S(1)}, bf16[2,256,256]{2,1,0:T(8,128)(2,1)S(1)}, u32[]{:S(2)}, u32[]{:S(2)}) collective-permute-start(bf16[2,256,256]{2,1,0:T(8,128)(2,1)S(1)} %shard_map.47), channel_id=1, source_target_pairs={{0,4},{1,5},{2,6},{3,7},{4,0},{5,1},{6,2},{7,3},{8,12},{9,13},{10,... | collective-permute-start | bytes 786440 | tf_op jit(solution)/shard_map/ppermute | solution.py:133
  88.6 1.2 copy-start.5
  99.2 42.2 %collective-permute-start.17 = (bf16[2,256,256]{2,1,0:T(8,128)(2,1)S(1)}, bf16[2,256,256]{2,1,0:T(8,128)(2,1)S(1)}, u32[]{:S(2)}, u32[]{:S(2)}) collective-permute-start(bf16[2,256,256]{2,1,0:T(8,128)(2,1)S(1)} %shard_map.52), channel_id=1, source_target_pairs={{0,12},{1,13},{2,14},{3,15},{4,8},{5,9},{6,10},{7,11},{8,4},{9,5},... | collective-permute-start | bytes 786440 | tf_op jit(solution)/shard_map/ppermute | solution.py:133
  107.4 34.0 %collective-permute-start.14 = (bf16[2,256,256]{2,1,0:T(8,128)(2,1)S(1)}, bf16[2,256,256]{2,1,0:T(8,128)(2,1)S(1)}, u32[]{:S(2)}, u32[]{:S(2)}) collective-permute-start(bf16[2,256,256]{2,1,0:T(8,128)(2,1)S(1)} %shard_map.50), channel_id=1, source_target_pairs={{0,4},{1,5},{2,6},{3,7},{4,0},{5,1},{6,2},{7,3},{8,12},{9,13},{10,... | collective-permute-start | bytes 786440 | tf_op jit(solution)/shard_map/ppermute | solution.py:133
  114.0 11.1 %copy-start.6 = (bf16[8,1,256,256]{3,2,1,0:T(8,128)(2,1)S(1)}, bf16[8,1,256,256]{3,2,1,0:T(8,128)(2,1)}, u32[]{:S(2)}) copy-start(bf16[8,1,256,256]{3,2,1,0:T(8,128)(2,1)} %copy-done.2) | copy-start | bytes 3145732
  114.0 11.1 %copy-start.7 = (bf16[8,1,256,256]{3,2,1,0:T(8,128)(2,1)S(1)}, bf16[8,1,256,256]{3,2,1,0:T(8,128)(2,1)}, u32[]{:S(2)}) copy-start(bf16[8,1,256,256]{3,2,1,0:T(8,128)(2,1)} %refs_6_.1) | copy-start | bytes 3145732
  114.0 27.4 %collective-permute-start.16 = (bf16[2,256,256]{2,1,0:T(8,128)(2,1)S(1)}, bf16[2,256,256]{2,1,0:T(8,128)(2,1)S(1)}, u32[]{:S(2)}, u32[]{:S(2)}) collective-permute-start(bf16[2,256,256]{2,1,0:T(8,128)(2,1)S(1)} %shard_map.51), channel_id=1, source_target_pairs={{0,8},{1,9},{2,10},{3,11},{4,12},{5,13},{6,14},{7,15},{8,0},{9,1},... | collective-permute-start | bytes 786440 | tf_op jit(solution)/shard_map/ppermute | solution.py:133
  123.4 18.0 %collective-permute-start.18 = (bf16[2,256,256]{2,1,0:T(8,128)(2,1)S(1)}, bf16[2,256,256]{2,1,0:T(8,128)(2,1)S(1)}, u32[]{:S(2)}, u32[]{:S(2)}) collective-permute-start(bf16[2,256,256]{2,1,0:T(8,128)(2,1)S(1)} %shard_map.53), channel_id=1, source_target_pairs={{0,12},{1,13},{2,14},{3,15},{4,8},{5,9},{6,10},{7,11},{8,4},{9,5},... | collective-permute-start | bytes 786440 | tf_op jit(solution)/shard_map/ppermute | solution.py:133

commit v3 on v2

v3 whole, which is shorter than its diff:
```python
import functools

import jax
import jax.numpy as jnp
from jax import lax
from jax.experimental import pallas as pl
from jax.experimental.pallas import tpu as pltpu
from jax.sharding import PartitionSpec as P

HBM = pl.BlockSpec(memory_space=pl.ANY)
SMEM = pl.BlockSpec(memory_space=pltpu.SMEM)
VMEM = pl.BlockSpec(memory_space=pltpu.VMEM)


def slot_kernel(shape, meta, source, *refs):
    parts, choices = shape
    count = len(parts)
    lefts, refs = refs[:count], refs[count:]
    psis = []
    for number in parts:
        psis.append(refs[:number])
        refs = refs[number:]
    rights = refs[:choices]
    out, right_buf, mid_buf = refs[choices:]
    terms, _, rows, columns = lefts[0].shape
    q = meta[0]

    def sector_block(held, sector):
        size = held[0].shape[1]
        block = held[0][0, sector % size]
        for part in range(1, len(held)):
            block = jnp.where(sector >= part * size, held[part][0, sector % size], block)
        return block

    for k in range(terms):
        span = pl.ds(k * columns, columns)
        right = rights[0][k, 0]
        for choice in range(1, choices):
            right = jnp.where(meta[1] >= choice, rights[choice][k, 0], right)
        right_buf[:, span] = right
        for i in range(count):
            mid = jnp.dot(lefts[i][k, 0], sector_block(psis[i], source[k, q]), preferred_element_type=jnp.float32)
            mid_buf[pl.ds(i * rows, rows), span] = mid.astype(jnp.bfloat16)
    total = lax.dot_general(
        mid_buf[...], right_buf[...], (((1,), (1,)), ((), ())), preferred_element_type=jnp.float32
    )
    out[...] = total.reshape(out.shape).astype(out.dtype)


def slot(q, choice, source_map, lefts, psis, rights, dtype):
    terms, _, rows, columns = lefts[0].shape
    count = len(lefts)
    parts = tuple(len(psi) for psi in psis)
    meta = jnp.stack([q, choice]).astype(jnp.int32)
    return pl.pallas_call(
        functools.partial(slot_kernel, (parts, len(rights))),
        out_shape=jax.ShapeDtypeStruct((count, rows, columns), dtype),
        in_specs=[SMEM, SMEM] + [VMEM] * (count + sum(parts) + len(rights)),
        out_specs=VMEM,
        scratch_shapes=[
            pltpu.VMEM((rows, terms * columns), jnp.bfloat16),
            pltpu.VMEM((count * rows, terms * columns), jnp.bfloat16),
        ],
        compiler_params=pltpu.CompilerParams(vmem_limit_bytes=24 << 20),
        cost_estimate=pl.CostEstimate(flops=1, bytes_accessed=1, transcendentals=0),
    )(meta, source_map, *lefts, *[part for psi in psis for part in psi], *rights)


def place_kernel(width, meta, *refs):
    pieces, out, sem = refs[:-2], refs[-2], refs[-1]
    me = meta[0]

    def copy(j):
        return pltpu.make_async_copy(pieces[j // width].at[j % width], out.at[me ^ j], sem.at[j])

    for j in range(len(pieces) * width):
        copy(j).start()
    for j in range(len(pieces) * width):
        copy(j).wait()


def place(me, pieces):
    width, rows, columns = pieces[0].shape
    sectors = width * len(pieces)
    return pl.pallas_call(
        functools.partial(place_kernel, width),
        out_shape=jax.ShapeDtypeStruct((sectors, rows, columns), pieces[0].dtype),
        in_specs=[SMEM] + [VMEM] * len(pieces),
        out_specs=HBM,
        scratch_shapes=[pltpu.SemaphoreType.DMA((sectors,))],
        compiler_params=pltpu.CompilerParams(vmem_limit_bytes=16 << 20),
    )(me[None].astype(jnp.int32), *pieces)


def exchange(array, bits, members):
    return lax.ppermute(array, "sec", [(s, s ^ bits) for s in members])


def on_device(ops, psi, left_env, right_env, source_map):
    me = lax.axis_index("sec")
    row = me // 4
    choice = jnp.where((row == 0) | (row == 3), 0, 1)
    dtype = jnp.bfloat16 if ops == 1 else jnp.float32
    every = range(16)
    inner = range(4, 12)

    def products(step, lefts, psis, rights):
        return slot(me ^ (4 * step), choice, source_map, lefts, [(psi,) for psi in psis], rights, dtype)

    near = exchange(right_env, 4, every)
    middle = exchange(right_env, 12, inner)
    x_psi = exchange(psi, 2, every)
    own = ([left_env, exchange(left_env, 1, every)], [psi, exchange(psi, 1, every)])

    near, middle = lax.optimization_barrier((near, middle))
    far_in = exchange(near, 12, inner)
    second = exchange(middle, 4, inner)
    own_1 = products(1, *own, (near,))
    own_0 = products(0, *own, (right_env,))

    second, far_in, x_psi, left_next, own_0, own_1 = lax.optimization_barrier(
        (second, far_in, x_psi, left_env, own_0, own_1)
    )
    sent_1 = exchange(own_1, 4, every)
    third = exchange(far_in, 4, inner)
    x_left = exchange(left_next, 2, every)
    across_psi = exchange(x_psi, 1, every)
    own_2 = products(2, *own, (second, far_in))
    sent_2 = exchange(own_2, 8, every)

    x_left, sent_1 = lax.optimization_barrier((x_left, sent_1))
    across_left = exchange(x_left, 1, every)
    other = ([x_left, across_left], [x_psi, across_psi])
    other_1 = products(1, *other, (near,))
    other_sent_1 = exchange(other_1, 4, every)
    other_2 = products(2, *other, (second, far_in))
    other_sent_2 = exchange(other_2, 8, every)

    third, sent_2 = lax.optimization_barrier((third, sent_2))
    own_3 = products(3, *own, (third, middle))
    sent_3 = exchange(own_3, 12, every)
    other_3 = products(3, *other, (third, middle))
    other_sent_3 = exchange(other_3, 12, every)
    other_0 = products(0, *other, (right_env,))

    pieces = [own_0, other_0, sent_1, other_sent_1, sent_2, other_sent_2, sent_3, other_sent_3]
    out = place(me, pieces)[:, None]
    if ops > 1:
        out = lax.psum_scatter(out, "op", scatter_dimension=2, tiled=True).astype(jnp.bfloat16)
    return out


def solution(mesh):
    placed = (
        P(("group", "sec"), None, None, None),
        P(("group", "op"), "sec", None, None),
        P(("group", "op"), "sec", None, None),
        P(("group", "op"), None),
    )
    return jax.shard_map(
        functools.partial(on_device, mesh.shape["op"]),
        mesh=mesh,
        in_specs=placed,
        out_specs=P("group", "sec", "op", None),
        check_vma=False,
    )
```

time: 146 us -> 149 us (1.021); the launches traced: 146 us -> 147 us
  Pallas kernels: 68 us -> 31.2 us
  waiting for transfers between devices: 46.2 us -> 70.1 us
  starting transfers between devices: 22.5 us -> 30 us
  local copies, waits for them, and re-layouts: 8.43 us -> 15 us
    pallas_call x8, Pallas kernels: 63.8 us -> 28.9 us  [slot(): pl.pallas_call(functools.partial(slot_kernel, (parts, len(rights))), out_...]
    ppermute x19 -> x17, waiting for transfers between devices: 46.2 us -> 70.1 us  [exchange(): return lax.ppermute(array, 'sec', [(s, s ^ bits) for s in members])]
    unnamed x20 -> x36, local copies, waits for them, and re-layouts: 5.35 us -> 15 us
    ppermute x19 -> x17, starting transfers between devices: 22.5 us -> 30 us  [exchange(): return lax.ppermute(array, 'sec', [(s, s ^ bits) for s in members])]
    slice x1 -> x0, local copies, waits for them, and re-layouts: 3.07 us -> none  [on_device(): low, high = (psi[:, :half], psi[:, half:])]
    pallas_call x1, Pallas kernels: 4.2 us -> 2.39 us  [place(): pl.pallas_call(functools.partial(place_kernel, width), out_shape=jax.Shap...]
  transfers between devices with their start and end apart: 19 -> 17, of which waited for: 5 -> 6; matrix products, arithmetic and copies ran while one was open for 2% -> 0% of each run, Pallas kernels for 44% -> 20%
where the time goes in v3:
time: 149 us; the launch traced here: 147 us
  waiting for transfers between devices  70.1 us (47%)
  Pallas kernels  31.2 us (21%)
  starting transfers between devices  30 us (20%)
  local copies, waits for them, and re-layouts  15 us (10%)
    ppermute x17, waiting for transfers between devices, exchange(): return lax.ppermute(array, 'sec', [(s, s ^ bits) for s in members])  70.1 us
    ppermute x17, starting transfers between devices, exchange(): return lax.ppermute(array, 'sec', [(s, s ^ bits) for s in members])  30 us
    pallas_call x8, Pallas kernels, slot(): pl.pallas_call(functools.partial(slot_kernel, (parts, len(rights))), out_...  28.9 us
    unnamed x36, local copies, waits for them, and re-layouts  15 us
  transfers between devices with their start and end apart: 17, of which 6 were waited for; matrix products, arithmetic and copies ran while one was open for 0% of the time, Pallas kernels for 20%

profile of v3, /device:TPU:0, one launch (start us, length us, event | category | flops | bytes accessed | tf_op | source)
XLA Modules:
  0.0 146.8 jit_solution(13633484070933618835)
XLA Ops:
  0.0 1.7 %collective-permute-start.1 = (bf16[8,1,256,256]{3,2,1,0:T(8,128)(2,1)}, bf16[8,1,256,256]{3,2,1,0:T(8,128)(2,1)}, u32[]{:S(2)}, u32[]{:S(2)}) collective-permute-start(bf16[8,1,256,256]{3,2,1,0:T(8,128)(2,1)} %refs_4_.3), channel_id=1, source_target_pairs={{4,8},{5,9},{6,10},{7,11},{8,4},{9,5},{10,6},{11,7},{20,24},{21,25... | collective-permute-start | bytes 3145736 | tf_op jit(solution)/shard_map/ppermute | solution.py:96
  1.7 0.5 collective-permute-start.6
  2.1 4.5 %collective-permute-start = (bf16[8,1,256,256]{3,2,1,0:T(8,128)(2,1)}, bf16[8,1,256,256]{3,2,1,0:T(8,128)(2,1)}, u32[]{:S(2)}, u32[]{:S(2)}) collective-permute-start(bf16[8,1,256,256]{3,2,1,0:T(8,128)(2,1)} %refs_4_.3), channel_id=1, source_target_pairs={{0,4},{1,5},{2,6},{3,7},{4,0},{5,1},{6,2},{7,3},{8,12},{9,13},{10,... | collective-permute-start | bytes 3145736 | tf_op jit(solution)/shard_map/ppermute | solution.py:96
  6.7 1.5 %collective-permute-start.4 = (bf16[1,16,256,256]{3,2,1,0:T(8,128)(2,1)}, bf16[1,16,256,256]{3,2,1,0:T(8,128)(2,1)}, u32[]{:S(2)}, u32[]{:S(2)}) collective-permute-start(bf16[1,16,256,256]{3,2,1,0:T(8,128)(2,1)} %refs_2_.7), channel_id=1, source_target_pairs={{0,2},{1,3},{2,0},{3,1},{4,6},{5,7},{6,4},{7,5},{8,10},{9,11},{10,... | collective-permute-start | bytes 6291464 | tf_op jit(solution)/shard_map/ppermute | solution.py:96
  8.2 22.6 %collective-permute-done.refs_4_ = bf16[8,1,256,256]{3,2,1,0:T(8,128)(2,1)} collective-permute-done((bf16[8,1,256,256]{3,2,1,0:T(8,128)(2,1)}, bf16[8,1,256,256]{3,2,1,0:T(8,128)(2,1)}, u32[]{:S(2)}, u32[]{:S(2)}) %collective-permute-start) | collective-permute-done | bytes 1048608 | tf_op jit(solution)/shard_map/ppermute | solution.py:96
  30.7 1.3 collective-permute-start.2
  32.0 1.7 %collective-permute-start.3 = (bf16[8,1,256,256]{3,2,1,0:T(8,128)(2,1)}, bf16[8,1,256,256]{3,2,1,0:T(8,128)(2,1)}, u32[]{:S(2)}, u32[]{:S(2)}) collective-permute-start(bf16[8,1,256,256]{3,2,1,0:T(8,128)(2,1)} %collective-permute-done.refs_4_), channel_id=1, source_target_pairs={{4,8},{5,9},{6,10},{7,11},{8,4},{9,5},{10,6},{11,7},{20,24},{21,25... | collective-permute-start | bytes 3145736 | tf_op jit(solution)/shard_map/ppermute | solution.py:96
  33.7 0.1 pad_add_fusion
  33.8 1.0 copy-done.8
  34.8 1.3 copy-done.2
  36.1 1.6 %copy-done = bf16[1,16,256,256]{3,2,1,0:T(8,128)(2,1)S(1)} copy-done((bf16[1,16,256,256]{3,2,1,0:T(8,128)(2,1)S(1)}, bf16[1,16,256,256]{3,2,1,0:T(8,128)(2,1)}, u32[]{:S(2)}) %copy-start) | copy-done | bytes 2097176
  37.7 1.6 %copy-done.3 = bf16[1,16,256,256]{3,2,1,0:T(8,128)(2,1)S(1)} copy-done((bf16[1,16,256,256]{3,2,1,0:T(8,128)(2,1)S(1)}, bf16[1,16,256,256]{3,2,1,0:T(8,128)(2,1)}, u32[]{:S(2)}) %copy-start.3) | copy-done | bytes 2097176
  39.3 1.2 copy-done.6
  40.5 1.2 copy-done.9
  41.8 0.7 copy-done.14
  42.5 2.7 %shard_map.47 = bf16[2,256,256]{2,1,0:T(8,128)(2,1)S(1)} custom-call(s32[2]{0:T(128)S(1)} %get-tuple-element.30.meta, s32[8,16]{1,0:T(8,128)S(1)} %copy-done.14, bf16[8,1,256,256]{3,2,1,0:T(8,128)(2,1)S(1)} %copy-done.6, bf16[8,1,256,256]{3,2,1,0:T(8,128)(2,1)S(1)} %copy-done.9, bf16[1,16,256,256]{3,2,1,0:T(8,128)(2,1)S(1)} %copy-done, ...), custom_call_target="tpu_custom_call" | custom-call | flops 1 | bytes 1 | tf_op jit(solution)/shard_map/pallas_call | solution.py:55
  45.1 1.9 %shard_map.46.refs_0_ = bf16[2,256,256]{2,1,0:T(8,128)(2,1)S(1)} custom-call(s32[2]{0:T(128)S(1)} %get-tuple-element.29.meta, s32[8,16]{1,0:T(8,128)S(1)} %copy-done.15, bf16[8,1,256,256]{3,2,1,0:T(8,128)(2,1)S(1)} %copy-done.7, bf16[8,1,256,256]{3,2,1,0:T(8,128)(2,1)S(1)} %copy-done.9, bf16[1,16,256,256]{3,2,1,0:T(8,128)(2,1)S(1)} %copy-done.1, ...), custom_call_target="tpu_custom_call" | custom-call | flops 1 | bytes 1 | tf_op jit(solution)/shard_map/pallas_call | solution.py:55
  47.1 10.8 %collective-permute-done.2.refs_4_ = bf16[8,1,256,256]{3,2,1,0:T(8,128)(2,1)} collective-permute-done((bf16[8,1,256,256]{3,2,1,0:T(8,128)(2,1)}, bf16[8,1,256,256]{3,2,1,0:T(8,128)(2,1)}, u32[]{:S(2)}, u32[]{:S(2)}) %collective-permute-start.2) | collective-permute-done | bytes 1048608 | tf_op jit(solution)/shard_map/ppermute | solution.py:96
  57.8 0.0 collective-permute-done.4.refs_2_
  57.8 1.5 %collective-permute-start.7 = (bf16[8,1,256,256]{3,2,1,0:T(8,128)(2,1)S(1)}, bf16[8,1,256,256]{3,2,1,0:T(8,128)(2,1)}, u32[]{:S(2)}, u32[]{:S(2)}) collective-permute-start(bf16[8,1,256,256]{3,2,1,0:T(8,128)(2,1)S(1)} %copy-done.7), channel_id=1, source_target_pairs={{0,2},{1,3},{2,0},{3,1},{4,6},{5,7},{6,4},{7,5},{8,10},{9,11},{10,... | collective-permute-start | bytes 3145736 | tf_op jit(solution)/shard_map/ppermute | solution.py:96
  59.3 4.7 %collective-permute-start.8 = (bf16[2,256,256]{2,1,0:T(8,128)(2,1)S(1)}, bf16[2,256,256]{2,1,0:T(8,128)(2,1)S(1)}, u32[]{:S(2)}, u32[]{:S(2)}) collective-permute-start(bf16[2,256,256]{2,1,0:T(8,128)(2,1)S(1)} %shard_map.47), channel_id=1, source_target_pairs={{0,4},{1,5},{2,6},{3,7},{4,0},{5,1},{6,2},{7,3},{8,12},{9,13},{10,... | collective-permute-start | bytes 786440 | tf_op jit(solution)/shard_map/ppermute | solution.py:96
  64.0 1.3 collective-permute-start.12
  65.3 5.9 %collective-permute-done.8.refs_2_ = bf16[2,256,256]{2,1,0:T(8,128)(2,1)S(1)} collective-permute-done((bf16[2,256,256]{2,1,0:T(8,128)(2,1)S(1)}, bf16[2,256,256]{2,1,0:T(8,128)(2,1)S(1)}, u32[]{:S(2)}, u32[]{:S(2)}) %collective-permute-start.8) | collective-permute-done | bytes 262176 | tf_op jit(solution)/shard_map/ppermute | solution.py:96
  71.2 0.7 copy-done.16
  71.9 10.1 %collective-permute-done.7.refs_0_ = bf16[8,1,256,256]{3,2,1,0:T(8,128)(2,1)} collective-permute-done((bf16[8,1,256,256]{3,2,1,0:T(8,128)(2,1)S(1)}, bf16[8,1,256,256]{3,2,1,0:T(8,128)(2,1)}, u32[]{:S(2)}, u32[]{:S(2)}) %collective-permute-start.7) | collective-permute-done | bytes 1048608 | tf_op jit(solution)/shard_map/ppermute | solution.py:96
  82.0 0.0 collective-permute-start.9
  82.0 0.1 pad_add_fusion.2.meta
  82.1 1.6 %copy-done.4 = bf16[1,16,256,256]{3,2,1,0:T(8,128)(2,1)S(1)} copy-done((bf16[1,16,256,256]{3,2,1,0:T(8,128)(2,1)S(1)}, bf16[1,16,256,256]{3,2,1,0:T(8,128)(2,1)}, u32[]{:S(2)}) %copy-start.4) | copy-done | bytes 2097176
  83.7 1.2 copy-done.10
  84.9 3.6 %shard_map.50 = bf16[2,256,256]{2,1,0:T(8,128)(2,1)} custom-call(s32[2]{0:T(128)S(1)} %pad_add_fusion.2.meta, s32[8,16]{1,0:T(8,128)S(1)} %copy-done.15, bf16[8,1,256,256]{3,2,1,0:T(8,128)(2,1)S(1)} %copy-done.7, bf16[8,1,256,256]{3,2,1,0:T(8,128)(2,1)S(1)} %copy-done.10, bf16[1,16,256,256]{3,2,1,0:T(8,128)(2,1)S(1)} %copy-done.1, ...), custom_call_target="tpu_custom_call" | custom-call | flops 1 | bytes 1 | tf_op jit(solution)/shard_map/pallas_call | solution.py:55
  88.4 4.6 %collective-permute-start.13 = (bf16[2,256,256]{2,1,0:T(8,128)(2,1)}, bf16[2,256,256]{2,1,0:T(8,128)(2,1)}, u32[]{:S(2)}, u32[]{:S(2)}) collective-permute-start(bf16[2,256,256]{2,1,0:T(8,128)(2,1)} %shard_map.50), channel_id=1, source_target_pairs={{0,8},{1,9},{2,10},{3,11},{4,12},{5,13},{6,14},{7,15},{8,0},{9,1},... | collective-permute-start | bytes 786440 | tf_op jit(solution)/shard_map/ppermute | solution.py:96
  93.0 0.1 pad_add_fusion.3.meta
  93.1 12.8 %collective-permute-done.13.refs_4_ = bf16[2,256,256]{2,1,0:T(8,128)(2,1)} collective-permute-done((bf16[2,256,256]{2,1,0:T(8,128)(2,1)}, bf16[2,256,256]{2,1,0:T(8,128)(2,1)}, u32[]{:S(2)}, u32[]{:S(2)}) %collective-permute-start.13) | collective-permute-done | bytes 262176 | tf_op jit(solution)/shard_map/ppermute | solution.py:96
  105.9 0.0 collective-permute-done.12.refs_4_
  105.9 1.6 %copy-done.5 = bf16[1,16,256,256]{3,2,1,0:T(8,128)(2,1)S(1)} copy-done((bf16[1,16,256,256]{3,2,1,0:T(8,128)(2,1)S(1)}, bf16[1,16,256,256]{3,2,1,0:T(8,128)(2,1)}, u32[]{:S(2)}) %copy-start.5) | copy-done | bytes 2097176
  107.5 1.2 copy-done.11
  108.8 2.8 %shard_map.52 = bf16[2,256,256]{2,1,0:T(8,128)(2,1)S(1)} custom-call(s32[2]{0:T(128)S(1)} %pad_add_fusion.3.meta, s32[8,16]{1,0:T(8,128)S(1)} %copy-done.15, bf16[8,1,256,256]{3,2,1,0:T(8,128)(2,1)S(1)} %copy-done.7, bf16[8,1,256,256]{3,2,1,0:T(8,128)(2,1)S(1)} %copy-done.11, bf16[1,16,256,256]{3,2,1,0:T(8,128)(2,1)S(1)} %copy-done.1, ...), custom_call_target="tpu_custom_call" | custom-call | flops 1 | bytes 1 | tf_op jit(solution)/shard_map/pallas_call | solution.py:55
  111.6 2.2 %collective-permute-start.15 = (bf16[2,256,256]{2,1,0:T(8,128)(2,1)S(1)}, bf16[2,256,256]{2,1,0:T(8,128)(2,1)S(1)}, u32[]{:S(2)}, u32[]{:S(2)}) collective-permute-start(bf16[2,256,256]{2,1,0:T(8,128)(2,1)S(1)} %shard_map.52), channel_id=1, source_target_pairs={{0,12},{1,13},{2,14},{3,15},{4,8},{5,9},{6,10},{7,11},{8,4},{9,5},... | collective-permute-start | bytes 786440 | tf_op jit(solution)/shard_map/ppermute | solution.py:96
  113.8 4.4 %shard_map.49 = bf16[2,256,256]{2,1,0:T(8,128)(2,1)S(1)} custom-call(s32[2]{0:T(128)S(1)} %get-tuple-element.30.meta, s32[8,16]{1,0:T(8,128)S(1)} %copy-done.15, bf16[8,1,256,256]{3,2,1,0:T(8,128)(2,1)} %collective-permute-done.7.refs_0_, bf16[8,1,256,256]{3,2,1,0:T(8,128)(2,1)} %collective-permute-done.9.refs_1_, ...), custom_call_target="tpu_custom_call" | custom-call | flops 1 | bytes 1 | tf_op jit(solution)/shard_map/pallas_call | solution.py:55
  118.2 0.1 collective-permute-start.11
  118.3 4.7 %shard_map.51 = bf16[2,256,256]{2,1,0:T(8,128)(2,1)S(1)} custom-call(s32[2]{0:T(128)S(1)} %pad_add_fusion.2.meta, s32[8,16]{1,0:T(8,128)S(1)} %copy-done.15, bf16[8,1,256,256]{3,2,1,0:T(8,128)(2,1)} %collective-permute-done.7.refs_0_, bf16[8,1,256,256]{3,2,1,0:T(8,128)(2,1)} %collective-permute-done.9.refs_1_, ...), custom_call_target="tpu_custom_call" | custom-call | flops 1 | bytes 1 | tf_op jit(solution)/shard_map/pallas_call | solution.py:55
  123.0 0.0 copy-start.13
  123.0 2.3 %collective-permute-start.14 = (bf16[2,256,256]{2,1,0:T(8,128)(2,1)S(1)}, bf16[2,256,256]{2,1,0:T(8,128)(2,1)S(1)}, u32[]{:S(2)}, u32[]{:S(2)}) collective-permute-start(bf16[2,256,256]{2,1,0:T(8,128)(2,1)S(1)} %shard_map.51), channel_id=1, source_target_pairs={{0,8},{1,9},{2,10},{3,11},{4,12},{5,13},{6,14},{7,15},{8,0},{9,1},... | collective-permute-start | bytes 786440 | tf_op jit(solution)/shard_map/ppermute | solution.py:96
  125.3 4.7 %shard_map.53 = bf16[2,256,256]{2,1,0:T(8,128)(2,1)S(1)} custom-call(s32[2]{0:T(128)S(1)} %pad_add_fusion.3.meta, s32[8,16]{1,0:T(8,128)S(1)} %copy-done.15, bf16[8,1,256,256]{3,2,1,0:T(8,128)(2,1)} %collective-permute-done.7.refs_0_, bf16[8,1,256,256]{3,2,1,0:T(8,128)(2,1)} %collective-permute-done.9.refs_1_, ...), custom_call_target="tpu_custom_call" | custom-call | flops 1 | bytes 1 | tf_op jit(solution)/shard_map/pallas_call | solution.py:55
  130.0 2.2 %collective-permute-start.16 = (bf16[2,256,256]{2,1,0:T(8,128)(2,1)S(1)}, bf16[2,256,256]{2,1,0:T(8,128)(2,1)S(1)}, u32[]{:S(2)}, u32[]{:S(2)}) collective-permute-start(bf16[2,256,256]{2,1,0:T(8,128)(2,1)S(1)} %shard_map.53), channel_id=1, source_target_pairs={{0,12},{1,13},{2,14},{3,15},{4,8},{5,9},{6,10},{7,11},{8,4},{9,5},... | collective-permute-start | bytes 786440 | tf_op jit(solution)/shard_map/ppermute | solution.py:96
  132.2 4.2 %shard_map.48.refs_1_ = bf16[2,256,256]{2,1,0:T(8,128)(2,1)S(1)} custom-call(s32[2]{0:T(128)S(1)} %get-tuple-element.29.meta, s32[8,16]{1,0:T(8,128)S(1)} %copy-done.15, bf16[8,1,256,256]{3,2,1,0:T(8,128)(2,1)} %collective-permute-done.7.refs_0_, bf16[8,1,256,256]{3,2,1,0:T(8,128)(2,1)} %collective-permute-done.9.refs_1_, ...), custom_call_target="tpu_custom_call" | custom-call | flops 1 | bytes 1 | tf_op jit(solution)/shard_map/pallas_call | solution.py:55
  136.4 8.0 %collective-permute-done.14.refs_5_ = bf16[2,256,256]{2,1,0:T(8,128)(2,1)S(1)} collective-permute-done((bf16[2,256,256]{2,1,0:T(8,128)(2,1)S(1)}, bf16[2,256,256]{2,1,0:T(8,128)(2,1)S(1)}, u32[]{:S(2)}, u32[]{:S(2)}) %collective-permute-start.14) | collective-permute-done | bytes 262176 | tf_op jit(solution)/shard_map/ppermute | solution.py:96
  144.4 2.4 %shard_map.54 = bf16[16,256,256]{2,1,0:T(8,128)(2,1)} custom-call(s32[1]{0:T(128)} %bitcast.meta, bf16[2,256,256]{2,1,0:T(8,128)(2,1)S(1)} %shard_map.46.refs_0_, bf16[2,256,256]{2,1,0:T(8,128)(2,1)S(1)} %shard_map.48.refs_1_, bf16[2,256,256]{2,1,0:T(8,128)(2,1)S(1)} %copy-done.17, bf16[2,256,256]{2,1,0:T(8,128)(2,1)S(1)} %collective-permute-done.11.refs_3_, ...), custom_call_target="tpu_custom_call" | custom-call | tf_op jit(solution)/shard_map/pallas_call | solution.py:85
  (34 shorter events, 0.1 us)
Async XLA Ops:
  0.0 8.2 %collective-permute-start.1 = (bf16[8,1,256,256]{3,2,1,0:T(8,128)(2,1)}, bf16[8,1,256,256]{3,2,1,0:T(8,128)(2,1)}, u32[]{:S(2)}, u32[]{:S(2)}) collective-permute-start(bf16[8,1,256,256]{3,2,1,0:T(8,128)(2,1)} %refs_4_.3), channel_id=1, source_target_pairs={{4,8},{5,9},{6,10},{7,11},{8,4},{9,5},{10,6},{11,7},{20,24},{21,25... | collective-permute-start | bytes 3145736 | tf_op jit(solution)/shard_map/ppermute | solution.py:96
  1.7 33.1 %collective-permute-start.6 = (bf16[1,16,256,256]{3,2,1,0:T(8,128)(2,1)}, bf16[1,16,256,256]{3,2,1,0:T(8,128)(2,1)S(1)}, u32[]{:S(2)}, u32[]{:S(2)}) collective-permute-start(bf16[1,16,256,256]{3,2,1,0:T(8,128)(2,1)} %refs_2_.7), channel_id=1, source_target_pairs={{0,1},{1,0},{2,3},{3,2},{4,5},{5,4},{6,7},{7,6},{8,9},{9,8},{10,11... | collective-permute-start | bytes 6291464 | tf_op jit(solution)/shard_map/ppermute | solution.py:96
  2.1 28.6 %collective-permute-start = (bf16[8,1,256,256]{3,2,1,0:T(8,128)(2,1)}, bf16[8,1,256,256]{3,2,1,0:T(8,128)(2,1)}, u32[]{:S(2)}, u32[]{:S(2)}) collective-permute-start(bf16[8,1,256,256]{3,2,1,0:T(8,128)(2,1)} %refs_4_.3), channel_id=1, source_target_pairs={{0,4},{1,5},{2,6},{3,7},{4,0},{5,1},{6,2},{7,3},{8,12},{9,13},{10,... | collective-permute-start | bytes 3145736 | tf_op jit(solution)/shard_map/ppermute | solution.py:96
  6.7 51.2 %collective-permute-start.4 = (bf16[1,16,256,256]{3,2,1,0:T(8,128)(2,1)}, bf16[1,16,256,256]{3,2,1,0:T(8,128)(2,1)}, u32[]{:S(2)}, u32[]{:S(2)}) collective-permute-start(bf16[1,16,256,256]{3,2,1,0:T(8,128)(2,1)} %refs_2_.7), channel_id=1, source_target_pairs={{0,2},{1,3},{2,0},{3,1},{4,6},{5,7},{6,4},{7,5},{8,10},{9,11},{10,... | collective-permute-start | bytes 6291464 | tf_op jit(solution)/shard_map/ppermute | solution.py:96
  8.1 25.6 %collective-permute-start.5 = (bf16[8,1,256,256]{3,2,1,0:T(8,128)(2,1)}, bf16[8,1,256,256]{3,2,1,0:T(8,128)(2,1)S(1)}, u32[]{:S(2)}, u32[]{:S(2)}) collective-permute-start(bf16[8,1,256,256]{3,2,1,0:T(8,128)(2,1)} %refs_0_.7), channel_id=1, source_target_pairs={{0,1},{1,0},{2,3},{3,2},{4,5},{5,4},{6,7},{7,6},{8,9},{9,8},{10,11... | collective-permute-start | bytes 3145736 | tf_op jit(solution)/shard_map/ppermute | solution.py:96
  30.7 27.1 %collective-permute-start.2 = (bf16[8,1,256,256]{3,2,1,0:T(8,128)(2,1)}, bf16[8,1,256,256]{3,2,1,0:T(8,128)(2,1)}, u32[]{:S(2)}, u32[]{:S(2)}) collective-permute-start(bf16[8,1,256,256]{3,2,1,0:T(8,128)(2,1)} %collective-permute-done.1.refs_5_), channel_id=1, source_target_pairs={{4,0},{5,1},{6,2},{7,3},{8,12},{9,13},{10,14},{11,15},{20,16},{21,... | collective-permute-start | bytes 3145736 | tf_op jit(solution)/shard_map/ppermute | solution.py:96
  32.0 25.8 %collective-permute-start.3 = (bf16[8,1,256,256]{3,2,1,0:T(8,128)(2,1)}, bf16[8,1,256,256]{3,2,1,0:T(8,128)(2,1)}, u32[]{:S(2)}, u32[]{:S(2)}) collective-permute-start(bf16[8,1,256,256]{3,2,1,0:T(8,128)(2,1)} %collective-permute-done.refs_4_), channel_id=1, source_target_pairs={{4,8},{5,9},{6,10},{7,11},{8,4},{9,5},{10,6},{11,7},{20,24},{21,25... | collective-permute-start | bytes 3145736 | tf_op jit(solution)/shard_map/ppermute | solution.py:96
  33.8 1.0 copy-start.8
  34.8 1.3 copy-start.2
  36.1 1.6 %copy-start = (bf16[1,16,256,256]{3,2,1,0:T(8,128)(2,1)S(1)}, bf16[1,16,256,256]{3,2,1,0:T(8,128)(2,1)}, u32[]{:S(2)}) copy-start(bf16[1,16,256,256]{3,2,1,0:T(8,128)(2,1)} %refs_2_.7) | copy-start | bytes 6291460
  37.7 1.6 %copy-start.3 = (bf16[1,16,256,256]{3,2,1,0:T(8,128)(2,1)S(1)}, bf16[1,16,256,256]{3,2,1,0:T(8,128)(2,1)}, u32[]{:S(2)}) copy-start(bf16[1,16,256,256]{3,2,1,0:T(8,128)(2,1)} %copy-done.2) | copy-start | bytes 6291460
  39.3 1.2 copy-start.6
  40.5 1.2 copy-start.9
  41.8 0.7 copy-start.14
  42.4 2.7 %copy-start.1 = (bf16[1,16,256,256]{3,2,1,0:T(8,128)(2,1)S(1)}, bf16[1,16,256,256]{3,2,1,0:T(8,128)(2,1)}, u32[]{:S(2)}) copy-start(bf16[1,16,256,256]{3,2,1,0:T(8,128)(2,1)} %refs_2_.7) | copy-start | bytes 6291460
  42.4 2.7 %copy-start.7 = (bf16[8,1,256,256]{3,2,1,0:T(8,128)(2,1)S(1)}, bf16[8,1,256,256]{3,2,1,0:T(8,128)(2,1)}, u32[]{:S(2)}) copy-start(bf16[8,1,256,256]{3,2,1,0:T(8,128)(2,1)} %refs_0_.7) | copy-start | bytes 3145732
  42.4 2.7 %copy-start.12 = (bf16[8,1,256,256]{3,2,1,0:T(8,128)(2,1)S(1)}, bf16[8,1,256,256]{3,2,1,0:T(8,128)(2,1)}, u32[]{:S(2)}) copy-start(bf16[8,1,256,256]{3,2,1,0:T(8,128)(2,1)} %refs_4_.3) | copy-start | bytes 3145732
  42.4 2.7 %copy-start.15 = (s32[8,16]{1,0:T(8,128)S(1)}, s32[8,16]{1,0:T(8,128)}, u32[]{:S(2)}) copy-start(s32[8,16]{1,0:T(8,128)} %source.15) | copy-start | bytes 1540
  57.8 24.1 %collective-permute-start.7 = (bf16[8,1,256,256]{3,2,1,0:T(8,128)(2,1)S(1)}, bf16[8,1,256,256]{3,2,1,0:T(8,128)(2,1)}, u32[]{:S(2)}, u32[]{:S(2)}) collective-permute-start(bf16[8,1,256,256]{3,2,1,0:T(8,128)(2,1)S(1)} %copy-done.7), channel_id=1, source_target_pairs={{0,2},{1,3},{2,0},{3,1},{4,6},{5,7},{6,4},{7,5},{8,10},{9,11},{10,... | collective-permute-start | bytes 3145736 | tf_op jit(solution)/shard_map/ppermute | solution.py:96
  59.3 54.5 %collective-permute-start.10 = (bf16[1,16,256,256]{3,2,1,0:T(8,128)(2,1)}, bf16[1,16,256,256]{3,2,1,0:T(8,128)(2,1)}, u32[]{:S(2)}, u32[]{:S(2)}) collective-permute-start(bf16[1,16,256,256]{3,2,1,0:T(8,128)(2,1)} %collective-permute-done.4.refs_2_), channel_id=1, source_target_pairs={{0,1},{1,0},{2,3},{3,2},{4,5},{5,4},{6,7},{7,6},{8,9},{9,8},{10,11... | collective-permute-start | bytes 6291464 | tf_op jit(solution)/shard_map/ppermute | solution.py:96
  59.3 11.9 %collective-permute-start.8 = (bf16[2,256,256]{2,1,0:T(8,128)(2,1)S(1)}, bf16[2,256,256]{2,1,0:T(8,128)(2,1)S(1)}, u32[]{:S(2)}, u32[]{:S(2)}) collective-permute-start(bf16[2,256,256]{2,1,0:T(8,128)(2,1)S(1)} %shard_map.47), channel_id=1, source_target_pairs={{0,4},{1,5},{2,6},{3,7},{4,0},{5,1},{6,2},{7,3},{8,12},{9,13},{10,... | collective-permute-start | bytes 786440 | tf_op jit(solution)/shard_map/ppermute | solution.py:96
  64.0 41.9 %collective-permute-start.12 = (bf16[8,1,256,256]{3,2,1,0:T(8,128)(2,1)}, bf16[8,1,256,256]{3,2,1,0:T(8,128)(2,1)}, u32[]{:S(2)}, u32[]{:S(2)}) collective-permute-start(bf16[8,1,256,256]{3,2,1,0:T(8,128)(2,1)} %collective-permute-done.3.refs_5_), channel_id=1, source_target_pairs={{4,0},{5,1},{6,2},{7,3},{8,12},{9,13},{10,14},{11,15},{20,16},{21,... | collective-permute-start | bytes 3145736 | tf_op jit(solution)/shard_map/ppermute | solution.py:96
  71.2 0.7 copy-start.16
  82.0 31.9 %collective-permute-start.9 = (bf16[8,1,256,256]{3,2,1,0:T(8,128)(2,1)}, bf16[8,1,256,256]{3,2,1,0:T(8,128)(2,1)}, u32[]{:S(2)}, u32[]{:S(2)}) collective-permute-start(bf16[8,1,256,256]{3,2,1,0:T(8,128)(2,1)} %collective-permute-done.7.refs_0_), channel_id=1, source_target_pairs={{0,1},{1,0},{2,3},{3,2},{4,5},{5,4},{6,7},{7,6},{8,9},{9,8},{10,11... | collective-permute-start | bytes 3145736 | tf_op jit(solution)/shard_map/ppermute | solution.py:96
  82.1 1.6 %copy-start.4 = (bf16[1,16,256,256]{3,2,1,0:T(8,128)(2,1)S(1)}, bf16[1,16,256,256]{3,2,1,0:T(8,128)(2,1)}, u32[]{:S(2)}) copy-start(bf16[1,16,256,256]{3,2,1,0:T(8,128)(2,1)} %copy-done.2) | copy-start | bytes 6291460
  83.7 1.2 copy-start.10
  88.4 17.5 %collective-permute-start.13 = (bf16[2,256,256]{2,1,0:T(8,128)(2,1)}, bf16[2,256,256]{2,1,0:T(8,128)(2,1)}, u32[]{:S(2)}, u32[]{:S(2)}) collective-permute-start(bf16[2,256,256]{2,1,0:T(8,128)(2,1)} %shard_map.50), channel_id=1, source_target_pairs={{0,8},{1,9},{2,10},{3,11},{4,12},{5,13},{6,14},{7,15},{8,0},{9,1},... | collective-permute-start | bytes 786440 | tf_op jit(solution)/shard_map/ppermute | solution.py:96
  105.9 1.6 %copy-start.5 = (bf16[1,16,256,256]{3,2,1,0:T(8,128)(2,1)S(1)}, bf16[1,16,256,256]{3,2,1,0:T(8,128)(2,1)}, u32[]{:S(2)}) copy-start(bf16[1,16,256,256]{3,2,1,0:T(8,128)(2,1)} %copy-done.2) | copy-start | bytes 6291460
  107.5 1.2 copy-start.11
  111.6 24.7 %collective-permute-start.15 = (bf16[2,256,256]{2,1,0:T(8,128)(2,1)S(1)}, bf16[2,256,256]{2,1,0:T(8,128)(2,1)S(1)}, u32[]{:S(2)}, u32[]{:S(2)}) collective-permute-start(bf16[2,256,256]{2,1,0:T(8,128)(2,1)S(1)} %shard_map.52), channel_id=1, source_target_pairs={{0,12},{1,13},{2,14},{3,15},{4,8},{5,9},{6,10},{7,11},{8,4},{9,5},... | collective-permute-start | bytes 786440 | tf_op jit(solution)/shard_map/ppermute | solution.py:96
  118.2 18.1 %collective-permute-start.11 = (bf16[2,256,256]{2,1,0:T(8,128)(2,1)S(1)}, bf16[2,256,256]{2,1,0:T(8,128)(2,1)S(1)}, u32[]{:S(2)}, u32[]{:S(2)}) collective-permute-start(bf16[2,256,256]{2,1,0:T(8,128)(2,1)S(1)} %shard_map.49), channel_id=1, source_target_pairs={{0,4},{1,5},{2,6},{3,7},{4,0},{5,1},{6,2},{7,3},{8,12},{9,13},{10,... | collective-permute-start | bytes 786440 | tf_op jit(solution)/shard_map/ppermute | solution.py:96
  123.0 9.2 %copy-start.13 = (bf16[8,1,256,256]{3,2,1,0:T(8,128)(2,1)S(1)}, bf16[8,1,256,256]{3,2,1,0:T(8,128)(2,1)}, u32[]{:S(2)}) copy-start(bf16[8,1,256,256]{3,2,1,0:T(8,128)(2,1)} %refs_4_.3) | copy-start | bytes 3145732
  123.0 21.4 %collective-permute-start.14 = (bf16[2,256,256]{2,1,0:T(8,128)(2,1)S(1)}, bf16[2,256,256]{2,1,0:T(8,128)(2,1)S(1)}, u32[]{:S(2)}, u32[]{:S(2)}) collective-permute-start(bf16[2,256,256]{2,1,0:T(8,128)(2,1)S(1)} %shard_map.51), channel_id=1, source_target_pairs={{0,8},{1,9},{2,10},{3,11},{4,12},{5,13},{6,14},{7,15},{8,0},{9,1},... | collective-permute-start | bytes 786440 | tf_op jit(solution)/shard_map/ppermute | solution.py:96
  129.9 14.4 %copy-start.17 = (bf16[2,256,256]{2,1,0:T(8,128)(2,1)S(1)}, bf16[2,256,256]{2,1,0:T(8,128)(2,1)}, u32[]{:S(2)}) copy-start(bf16[2,256,256]{2,1,0:T(8,128)(2,1)} %copy-done.16) | copy-start | bytes 786436
  130.0 14.4 %collective-permute-start.16 = (bf16[2,256,256]{2,1,0:T(8,128)(2,1)S(1)}, bf16[2,256,256]{2,1,0:T(8,128)(2,1)S(1)}, u32[]{:S(2)}, u32[]{:S(2)}) collective-permute-start(bf16[2,256,256]{2,1,0:T(8,128)(2,1)S(1)} %shard_map.53), channel_id=1, source_target_pairs={{0,12},{1,13},{2,14},{3,15},{4,8},{5,9},{6,10},{7,11},{8,4},{9,5},... | collective-permute-start | bytes 786440 | tf_op jit(solution)/shard_map/ppermute | solution.py:96

commit v4 on v3

v4 whole, which is shorter than its diff:
```python
import functools

import jax
import jax.numpy as jnp
from jax import lax
from jax.experimental import pallas as pl
from jax.experimental.pallas import tpu as pltpu
from jax.sharding import PartitionSpec as P

HBM = pl.BlockSpec(memory_space=pltpu.HBM)
SMEM = pl.BlockSpec(memory_space=pltpu.SMEM)
VMEM = pl.BlockSpec(memory_space=pltpu.VMEM)


def slot_kernel(count, choices, meta, source, *refs):
    parts = (len(refs) - choices - 8) // count - 1
    lefts, refs = refs[: parts * count], refs[parts * count :]
    psis, rights = refs[:count], refs[count : count + choices]
    out, left_buf, psi_buf, right_buf, mid_buf, left_sem, psi_sem, right_sem = refs[count + choices :]
    terms, rows, columns = left_buf.shape[1:]
    q = meta[0]

    def left_copy(i, k):
        part, place = divmod(k, terms // parts)
        return pltpu.make_async_copy(lefts[i * parts + part].at[place, 0], left_buf.at[i, k], left_sem.at[i, k])

    def psi_copy(i, k):
        return pltpu.make_async_copy(psis[i].at[0, source[k, q]], psi_buf.at[i, k], psi_sem.at[i, k])

    def right_copy(k, choice):
        return pltpu.make_async_copy(
            rights[choice].at[k, 0], right_buf.at[:, pl.ds(k * columns, columns)], right_sem.at[k]
        )

    for k in range(terms):
        for i in range(count):
            left_copy(i, k).start()
            psi_copy(i, k).start()
    for choice in range(choices):

        @pl.when(meta[1] == choice)
        def _(choice=choice):
            for k in range(terms):
                right_copy(k, choice).start()

    for k in range(terms):
        for i in range(count):
            left_copy(i, k).wait()
            psi_copy(i, k).wait()
            mid = jnp.dot(left_buf[i, k], psi_buf[i, k], preferred_element_type=jnp.float32)
            mid_buf[pl.ds(i * rows, rows), pl.ds(k * columns, columns)] = mid.astype(jnp.bfloat16)
    for k in range(terms):
        right_copy(k, 0).wait()
    total = lax.dot_general(
        mid_buf[...], right_buf[...], (((1,), (1,)), ((), ())), preferred_element_type=jnp.float32
    )
    out[...] = total.reshape(out.shape).astype(out.dtype)


def slot(q, choice, source_map, lefts, psis, rights, dtype, flops):
    terms, _, rows, columns = rights[0].shape
    count = len(psis)
    meta = jnp.stack([q, choice if len(rights) > 1 else 0 * q]).astype(jnp.int32)
    return pl.pallas_call(
        functools.partial(slot_kernel, count, len(rights)),
        out_shape=jax.ShapeDtypeStruct((count, rows, columns), dtype),
        in_specs=[SMEM, SMEM] + [HBM] * (len(lefts) + count + len(rights)),
        out_specs=VMEM,
        scratch_shapes=[
            pltpu.VMEM((count, terms, rows, columns), jnp.bfloat16),
            pltpu.VMEM((count, terms, rows, columns), jnp.bfloat16),
            pltpu.VMEM((rows, terms * columns), jnp.bfloat16),
            pltpu.VMEM((count * rows, terms * columns), jnp.bfloat16),
            pltpu.SemaphoreType.DMA((count, terms)),
            pltpu.SemaphoreType.DMA((count, terms)),
            pltpu.SemaphoreType.DMA((terms,)),
        ],
        compiler_params=pltpu.CompilerParams(vmem_limit_bytes=60 << 20),
        cost_estimate=pl.CostEstimate(flops=flops, bytes_accessed=1, transcendentals=0),
    )(meta, source_map, *lefts, *psis, *rights)


def place_kernel(width, meta, *refs):
    pieces, out, sem = refs[:-2], refs[-2], refs[-1]
    me = meta[0]

    def copy(j):
        return pltpu.make_async_copy(pieces[j // width].at[j % width], out.at[me ^ j], sem.at[j])

    for j in range(len(pieces) * width):
        copy(j).start()
    for j in range(len(pieces) * width):
        copy(j).wait()


def place(me, pieces):
    width, rows, columns = pieces[0].shape
    sectors = width * len(pieces)
    return pl.pallas_call(
        functools.partial(place_kernel, width),
        out_shape=jax.ShapeDtypeStruct((sectors, rows, columns), pieces[0].dtype),
        in_specs=[SMEM] + [VMEM] * len(pieces),
        out_specs=HBM,
        scratch_shapes=[pltpu.SemaphoreType.DMA((sectors,))],
        compiler_params=pltpu.CompilerParams(vmem_limit_bytes=16 << 20),
    )(me[None].astype(jnp.int32), *pieces)


def exchange(array, bits, members):
    return lax.ppermute(array, "sec", [(s, s ^ bits) for s in members])


def on_device(ops, psi, left_env, right_env, source_map):
    me = lax.axis_index("sec")
    row = me // 4
    choice = jnp.where((row == 0) | (row == 3), 0, 1)
    dtype = jnp.bfloat16 if ops == 1 else jnp.float32
    every = range(16)
    inner = range(4, 12)
    half = left_env.shape[0] // 2

    def products(step, lefts, psis, rights, flops=1):
        return slot(me ^ (4 * step), choice, source_map, lefts, psis, rights, dtype, flops)

    near = exchange(right_env, 4, every)
    middle = exchange(right_env, 12, inner)
    x_psi = exchange(psi, 2, every)
    own = ([left_env, exchange(left_env, 1, every)], [psi, exchange(psi, 1, every)])
    own_0 = products(0, *own, (right_env,))

    near, middle, own_0 = lax.optimization_barrier((near, middle, own_0))
    far_in = exchange(near, 12, inner)
    second = exchange(middle, 4, inner)
    own_1 = products(1, *own, (near,))
    sent_1 = exchange(own_1, 4, every)

    x_psi, low_next, sent_1 = lax.optimization_barrier((x_psi, left_env[:half], sent_1))
    x_low = exchange(low_next, 2, every)
    across_psi = exchange(x_psi, 1, every)

    second, far_in = lax.optimization_barrier((second, far_in))
    third = exchange(far_in, 4, inner)
    own_2 = products(2, *own, (second, far_in))
    sent_2 = exchange(own_2, 8, every)

    own_2, high_next = lax.optimization_barrier((own_2, left_env[half:]))
    x_high = exchange(high_next, 2, every)
    x_low, x_high, sent_2 = lax.optimization_barrier((x_low, x_high, sent_2))
    across_low = exchange(x_low, 1, every)
    across_high = exchange(x_high, 1, every)
    other = ([x_low, x_high, across_low, across_high], [x_psi, across_psi])
    other_2 = products(2, *other, (second, far_in))
    other_sent_2 = exchange(other_2, 8, every)
    other_1 = products(1, *other, (near,))
    other_sent_1 = exchange(other_1, 4, every)

    third, other_1, other_2 = lax.optimization_barrier((third, other_1, other_2))
    own_3 = products(3, *own, (third, middle))
    sent_3 = exchange(own_3, 12, every)
    other_3 = products(3, *other, (third, middle))
    other_sent_3 = exchange(other_3, 12, every)
    right_last, other_sent_1, other_sent_2 = lax.optimization_barrier((right_env, other_sent_1, other_sent_2))
    other_0 = products(0, *other, (right_last,), flops=10**10)

    pieces = [own_0, other_0, sent_1, other_sent_1, sent_2, other_sent_2, sent_3, other_sent_3]
    out = place(me, pieces)[:, None]
    if ops > 1:
        out = lax.psum_scatter(out, "op", scatter_dimension=2, tiled=True).astype(jnp.bfloat16)
    return out


def solution(mesh):
    placed = (
        P(("group", "sec"), None, None, None),
        P(("group", "op"), "sec", None, None),
        P(("group", "op"), "sec", None, None),
        P(("group", "op"), None),
    )
    return jax.shard_map(
        functools.partial(on_device, mesh.shape["op"]),
        mesh=mesh,
        in_specs=placed,
        out_specs=P("group", "sec", "op", None),
        check_vma=False,
    )
```

time: 149 us -> 145 us (0.973)
  the two profiles are of different devices: /device:TPU:0 before, /device:TPU:8 now
where the time goes in v4:
time: 145 us; the launch traced here: 144 us
  Pallas kernels  57.9 us (40%)
  waiting for transfers between devices  50.3 us (35%)
  starting transfers between devices  26.7 us (18%)
  local copies, waits for them, and re-layouts  6.49 us (4%)
  other arithmetic  2.34 us (2%)
    pallas_call x8, Pallas kernels, slot(): pl.pallas_call(functools.partial(slot_kernel, count, len(rights)), out_sh...  56.5 us
    ppermute x19, waiting for transfers between devices, exchange(): return lax.ppermute(array, 'sec', [(s, s ^ bits) for s in members])  50.3 us
    ppermute x19, starting transfers between devices, exchange(): return lax.ppermute(array, 'sec', [(s, s ^ bits) for s in members])  26.7 us
    unnamed x20, local copies, waits for them, and re-layouts  5.44 us
  transfers between devices with their start and end apart: 19, of which 10 were waited for; matrix products, arithmetic and copies ran while one was open for 2% of the time, Pallas kernels for 39%

profile of v4, /device:TPU:8, one launch (start us, length us, event | category | flops | bytes accessed | tf_op | source)
XLA Modules:
  0.0 144.1 jit_solution(1108250103273560103)
XLA Ops:
  0.0 1.5 %collective-permute-start.4 = (bf16[1,16,256,256]{3,2,1,0:T(8,128)(2,1)}, bf16[1,16,256,256]{3,2,1,0:T(8,128)(2,1)}, u32[]{:S(2)}, u32[]{:S(2)}) collective-permute-start(bf16[1,16,256,256]{3,2,1,0:T(8,128)(2,1)} %refs_2_.7), channel_id=1, source_target_pairs={{0,2},{1,3},{2,0},{3,1},{4,6},{5,7},{6,4},{7,5},{8,10},{9,11},{10,... | collective-permute-start | bytes 6291464 | tf_op jit(solution)/shard_map/ppermute | solution.py:110
  1.5 0.2 collective-permute-start.2
  1.7 0.4 collective-permute-start
  2.2 4.6 %collective-permute-start.1 = (bf16[8,1,256,256]{3,2,1,0:T(8,128)(2,1)}, bf16[8,1,256,256]{3,2,1,0:T(8,128)(2,1)}, u32[]{:S(2)}, u32[]{:S(2)}) collective-permute-start(bf16[8,1,256,256]{3,2,1,0:T(8,128)(2,1)} %refs_6_), channel_id=1, source_target_pairs={{4,8},{5,9},{6,10},{7,11},{8,4},{9,5},{10,6},{11,7},{20,24},{21,25... | collective-permute-start | bytes 3145736 | tf_op jit(solution)/shard_map/ppermute | solution.py:110
  6.8 0.6 pad_add_fusion.1.meta
  7.4 0.6 pad_add_fusion.meta
  8.0 0.0 collective-permute-done.2.refs_1_
  8.0 1.0 copy-done.5
  8.9 1.3 copy-done.2
  10.3 7.1 %shard_map.46.refs_0_ = bf16[2,256,256]{2,1,0:T(8,128)(2,1)} custom-call(s32[2]{0:T(128)} %pad_add_fusion.1.meta, s32[8,16]{1,0:T(8,128)} %source.15, bf16[8,1,256,256]{3,2,1,0:T(8,128)(2,1)} %refs_0_.7, bf16[8,1,256,256]{3,2,1,0:T(8,128)(2,1)} %copy-done.5, bf16[1,16,256,256]{3,2,1,0:T(8,128)(2,1)} %refs_2_.7, bf16[1,16,256,256]{3,2,1,0:T(8,128)(2,1)} %copy-done.2, ...), custom_call_target="tpu_custom_call" | custom-call | flops 1 | bytes 1 | tf_op jit(solution)/shard_map/pallas_call | solution.py:64
  17.3 0.0 copy-start.3
  17.4 10.0 %collective-permute-done.refs_4_.refs_6_ = bf16[8,1,256,256]{3,2,1,0:T(8,128)(2,1)} collective-permute-done((bf16[8,1,256,256]{3,2,1,0:T(8,128)(2,1)}, bf16[8,1,256,256]{3,2,1,0:T(8,128)(2,1)}, u32[]{:S(2)}, u32[]{:S(2)}) %collective-permute-start) | collective-permute-done | bytes 1048608 | tf_op jit(solution)/shard_map/ppermute | solution.py:110
  27.4 3.0 %collective-permute-done.1.refs_5_.refs_7_ = bf16[8,1,256,256]{3,2,1,0:T(8,128)(2,1)} collective-permute-done((bf16[8,1,256,256]{3,2,1,0:T(8,128)(2,1)}, bf16[8,1,256,256]{3,2,1,0:T(8,128)(2,1)}, u32[]{:S(2)}, u32[]{:S(2)}) %collective-permute-start.1) | collective-permute-done | bytes 1048608 | tf_op jit(solution)/shard_map/ppermute | solution.py:110
  30.4 2.3 %collective-permute-start.7 = (bf16[8,1,256,256]{3,2,1,0:T(8,128)(2,1)}, bf16[8,1,256,256]{3,2,1,0:T(8,128)(2,1)}, u32[]{:S(2)}, u32[]{:S(2)}) collective-permute-start(bf16[8,1,256,256]{3,2,1,0:T(8,128)(2,1)} %collective-permute-done.1.refs_5_.refs_7_), channel_id=1, source_target_pairs={{4,0},{5,1},{6,2},{7,3},{8,12},{9,13},{10,14},{11,15},{20,16},{21,... | collective-permute-start | bytes 3145736 | tf_op jit(solution)/shard_map/ppermute | solution.py:110
  32.7 3.6 %collective-permute-start.8 = (bf16[8,1,256,256]{3,2,1,0:T(8,128)(2,1)}, bf16[8,1,256,256]{3,2,1,0:T(8,128)(2,1)}, u32[]{:S(2)}, u32[]{:S(2)}) collective-permute-start(bf16[8,1,256,256]{3,2,1,0:T(8,128)(2,1)} %collective-permute-done.refs_4_.refs_6_), channel_id=1, source_target_pairs={{4,8},{5,9},{6,10},{7,11},{8,4},{9,5},{10,6},{11,7},{20,24},{21,25... | collective-permute-start | bytes 3145736 | tf_op jit(solution)/shard_map/ppermute | solution.py:110
  36.3 7.1 %shard_map.47 = bf16[2,256,256]{2,1,0:T(8,128)(2,1)} custom-call(s32[2]{0:T(128)} %pad_add_fusion.meta, s32[8,16]{1,0:T(8,128)} %source.15, bf16[8,1,256,256]{3,2,1,0:T(8,128)(2,1)} %refs_0_.7, bf16[8,1,256,256]{3,2,1,0:T(8,128)(2,1)} %copy-done.5, bf16[1,16,256,256]{3,2,1,0:T(8,128)(2,1)} %refs_2_.7, bf16[1,16,256,256]{3,2,1,0:T(8,128)(2,1)} %copy-done.2, ...), custom_call_target="tpu_custom_call" | custom-call | flops 1 | bytes 1 | tf_op jit(solution)/shard_map/pallas_call | solution.py:64
  43.4 0.1 collective-permute-start.5
  43.5 1.1 fusion
  44.5 3.8 %collective-permute-done.4.refs_4_ = bf16[1,16,256,256]{3,2,1,0:T(8,128)(2,1)} collective-permute-done((bf16[1,16,256,256]{3,2,1,0:T(8,128)(2,1)}, bf16[1,16,256,256]{3,2,1,0:T(8,128)(2,1)}, u32[]{:S(2)}, u32[]{:S(2)}) %collective-permute-start.4) | collective-permute-done | bytes 2097184 | tf_op jit(solution)/shard_map/ppermute | solution.py:110
  48.4 11.6 %collective-permute-done.5.refs_2_ = bf16[2,256,256]{2,1,0:T(8,128)(2,1)S(1)} collective-permute-done((bf16[2,256,256]{2,1,0:T(8,128)(2,1)}, bf16[2,256,256]{2,1,0:T(8,128)(2,1)S(1)}, u32[]{:S(2)}, u32[]{:S(2)}) %collective-permute-start.5) | collective-permute-done | bytes 262176 | tf_op jit(solution)/shard_map/ppermute | solution.py:110
  59.9 0.6 pad_add_fusion.2.meta
  60.5 0.5 collective-permute-start.6
  61.1 7.1 %shard_map.48 = bf16[2,256,256]{2,1,0:T(8,128)(2,1)} custom-call(s32[2]{0:T(128)} %pad_add_fusion.2.meta, s32[8,16]{1,0:T(8,128)} %source.15, bf16[8,1,256,256]{3,2,1,0:T(8,128)(2,1)} %refs_0_.7, bf16[8,1,256,256]{3,2,1,0:T(8,128)(2,1)} %copy-done.5, bf16[1,16,256,256]{3,2,1,0:T(8,128)(2,1)} %refs_2_.7, bf16[1,16,256,256]{3,2,1,0:T(8,128)(2,1)} %copy-done.2, ...), custom_call_target="tpu_custom_call" | custom-call | flops 1 | bytes 1 | tf_op jit(solution)/shard_map/pallas_call | solution.py:64
  68.1 1.6 %collective-permute-start.9 = (bf16[4,1,256,256]{3,2,1,0:T(8,128)(2,1)}, bf16[4,1,256,256]{3,2,1,0:T(8,128)(2,1)S(1)}, u32[]{:S(2)}, u32[]{:S(2)}) collective-permute-start(bf16[4,1,256,256]{3,2,1,0:T(8,128)(2,1)} %get-tuple-element.27), channel_id=1, source_target_pairs={{0,2},{1,3},{2,0},{3,1},{4,6},{5,7},{6,4},{7,5},{8,10},{9,11},{10,... | collective-permute-start | bytes 1572872 | tf_op jit(solution)/shard_map/ppermute | solution.py:110
  69.7 3.2 %collective-permute-start.10 = (bf16[2,256,256]{2,1,0:T(8,128)(2,1)}, bf16[2,256,256]{2,1,0:T(8,128)(2,1)S(1)}, u32[]{:S(2)}, u32[]{:S(2)}) collective-permute-start(bf16[2,256,256]{2,1,0:T(8,128)(2,1)} %shard_map.48), channel_id=1, source_target_pairs={{0,8},{1,9},{2,10},{3,11},{4,12},{5,13},{6,14},{7,15},{8,0},{9,1},... | collective-permute-start | bytes 786440 | tf_op jit(solution)/shard_map/ppermute | solution.py:110
  72.9 2.6 %collective-permute-start.16 = (bf16[8,1,256,256]{3,2,1,0:T(8,128)(2,1)}, bf16[8,1,256,256]{3,2,1,0:T(8,128)(2,1)}, u32[]{:S(2)}, u32[]{:S(2)}) collective-permute-start(bf16[8,1,256,256]{3,2,1,0:T(8,128)(2,1)} %collective-permute-done.8.refs_5_.refs_7_), channel_id=1, source_target_pairs={{4,0},{5,1},{6,2},{7,3},{8,12},{9,13},{10,14},{11,15},{20,16},{21,... | collective-permute-start | bytes 3145736 | tf_op jit(solution)/shard_map/ppermute | solution.py:110
  75.5 8.1 %collective-permute-done.10.refs_4_ = bf16[2,256,256]{2,1,0:T(8,128)(2,1)S(1)} collective-permute-done((bf16[2,256,256]{2,1,0:T(8,128)(2,1)}, bf16[2,256,256]{2,1,0:T(8,128)(2,1)S(1)}, u32[]{:S(2)}, u32[]{:S(2)}) %collective-permute-start.10) | collective-permute-done | bytes 262176 | tf_op jit(solution)/shard_map/ppermute | solution.py:110
  83.7 2.6 %collective-permute-done.9.refs_1_ = bf16[4,1,256,256]{3,2,1,0:T(8,128)(2,1)S(1)} collective-permute-done((bf16[4,1,256,256]{3,2,1,0:T(8,128)(2,1)}, bf16[4,1,256,256]{3,2,1,0:T(8,128)(2,1)S(1)}, u32[]{:S(2)}, u32[]{:S(2)}) %collective-permute-start.9) | collective-permute-done | bytes 524320 | tf_op jit(solution)/shard_map/ppermute | solution.py:110
  86.3 0.5 collective-permute-start.12
  86.8 1.4 collective-permute-done.11.refs_2_
  88.2 0.7 collective-permute-done.12.refs_3_
  89.0 0.1 copy-done.8
  89.0 0.8 copy-done.9
  89.9 1.3 copy-done.4
  91.2 7.1 %shard_map.50 = bf16[2,256,256]{2,1,0:T(8,128)(2,1)} custom-call(s32[2]{0:T(128)} %pad_add_fusion.2.meta, s32[8,16]{1,0:T(8,128)} %source.15, bf16[4,1,256,256]{3,2,1,0:T(8,128)(2,1)} %copy-done.6, bf16[4,1,256,256]{3,2,1,0:T(8,128)(2,1)} %copy-done.7, bf16[4,1,256,256]{3,2,1,0:T(8,128)(2,1)} %copy-done.8, bf16[4,1,256,256]{3,2,1,0:T(8,128)(2,1)} %copy-done.9, ...), custom_call_target="tpu_custom_call" | custom-call | flops 1 | bytes 1 | tf_op jit(solution)/shard_map/pallas_call | solution.py:64
  98.2 3.3 %collective-permute-start.15 = (bf16[2,256,256]{2,1,0:T(8,128)(2,1)}, bf16[2,256,256]{2,1,0:T(8,128)(2,1)S(1)}, u32[]{:S(2)}, u32[]{:S(2)}) collective-permute-start(bf16[2,256,256]{2,1,0:T(8,128)(2,1)} %shard_map.50), channel_id=1, source_target_pairs={{0,8},{1,9},{2,10},{3,11},{4,12},{5,13},{6,14},{7,15},{8,0},{9,1},... | collective-permute-start | bytes 786440 | tf_op jit(solution)/shard_map/ppermute | solution.py:110
  101.5 7.1 %shard_map.49 = bf16[2,256,256]{2,1,0:T(8,128)(2,1)} custom-call(s32[2]{0:T(128)} %pad_add_fusion.meta, s32[8,16]{1,0:T(8,128)} %source.15, bf16[4,1,256,256]{3,2,1,0:T(8,128)(2,1)} %copy-done.6, bf16[4,1,256,256]{3,2,1,0:T(8,128)(2,1)} %copy-done.7, bf16[4,1,256,256]{3,2,1,0:T(8,128)(2,1)} %copy-done.8, bf16[4,1,256,256]{3,2,1,0:T(8,128)(2,1)} %copy-done.9, ...), custom_call_target="tpu_custom_call" | custom-call | flops 1 | bytes 1 | tf_op jit(solution)/shard_map/pallas_call | solution.py:64
  108.6 0.1 collective-permute-start.14
  108.7 0.6 pad_add_fusion.3.meta
  109.3 7.1 %shard_map.53 = bf16[2,256,256]{2,1,0:T(8,128)(2,1)} custom-call(s32[2]{0:T(128)} %pad_add_fusion.3.meta, s32[8,16]{1,0:T(8,128)} %source.15, bf16[4,1,256,256]{3,2,1,0:T(8,128)(2,1)} %copy-done.6, bf16[4,1,256,256]{3,2,1,0:T(8,128)(2,1)} %copy-done.7, bf16[4,1,256,256]{3,2,1,0:T(8,128)(2,1)} %copy-done.8, bf16[4,1,256,256]{3,2,1,0:T(8,128)(2,1)} %copy-done.9, ...), custom_call_target="tpu_custom_call" | custom-call | flops 1 | bytes 1 | tf_op jit(solution)/shard_map/pallas_call | solution.py:64
  116.3 0.7 collective-permute-start.18
  117.0 7.1 %shard_map.52 = bf16[2,256,256]{2,1,0:T(8,128)(2,1)} custom-call(s32[2]{0:T(128)} %pad_add_fusion.3.meta, s32[8,16]{1,0:T(8,128)} %source.15, bf16[8,1,256,256]{3,2,1,0:T(8,128)(2,1)} %refs_0_.7, bf16[8,1,256,256]{3,2,1,0:T(8,128)(2,1)} %copy-done.5, bf16[1,16,256,256]{3,2,1,0:T(8,128)(2,1)} %refs_2_.7, bf16[1,16,256,256]{3,2,1,0:T(8,128)(2,1)} %copy-done.2, ...), custom_call_target="tpu_custom_call" | custom-call | flops 1 | bytes 1 | tf_op jit(solution)/shard_map/pallas_call | solution.py:64
  124.1 1.5 %collective-permute-start.17 = (bf16[2,256,256]{2,1,0:T(8,128)(2,1)}, bf16[2,256,256]{2,1,0:T(8,128)(2,1)S(1)}, u32[]{:S(2)}, u32[]{:S(2)}) collective-permute-start(bf16[2,256,256]{2,1,0:T(8,128)(2,1)} %shard_map.52), channel_id=1, source_target_pairs={{0,12},{1,13},{2,14},{3,15},{4,8},{5,9},{6,10},{7,11},{8,4},{9,5},... | collective-permute-start | bytes 786440 | tf_op jit(solution)/shard_map/ppermute | solution.py:110
  125.6 7.1 %shard_map.51.refs_1_ = bf16[2,256,256]{2,1,0:T(8,128)(2,1)} custom-call(s32[2]{0:T(128)} %pad_add_fusion.1.meta, s32[8,16]{1,0:T(8,128)} %source.15, bf16[4,1,256,256]{3,2,1,0:T(8,128)(2,1)} %copy-done.6, bf16[4,1,256,256]{3,2,1,0:T(8,128)(2,1)} %copy-done.7, bf16[4,1,256,256]{3,2,1,0:T(8,128)(2,1)} %copy-done.8, bf16[4,1,256,256]{3,2,1,0:T(8,128)(2,1)} %copy-done.9, ...), custom_call_target="tpu_custom_call" | custom-call | flops 10000000000 | bytes 1 | tf_op jit(solution)/shard_map/pallas_call | solution.py:64
  132.6 4.4 %collective-permute-done.18.refs_7_ = bf16[2,256,256]{2,1,0:T(8,128)(2,1)S(1)} collective-permute-done((bf16[2,256,256]{2,1,0:T(8,128)(2,1)}, bf16[2,256,256]{2,1,0:T(8,128)(2,1)S(1)}, u32[]{:S(2)}, u32[]{:S(2)}) %collective-permute-start.18) | collective-permute-done | bytes 262176 | tf_op jit(solution)/shard_map/ppermute | solution.py:110
  137.0 4.5 %collective-permute-done.17.refs_6_ = bf16[2,256,256]{2,1,0:T(8,128)(2,1)S(1)} collective-permute-done((bf16[2,256,256]{2,1,0:T(8,128)(2,1)}, bf16[2,256,256]{2,1,0:T(8,128)(2,1)S(1)}, u32[]{:S(2)}, u32[]{:S(2)}) %collective-permute-start.17) | collective-permute-done | bytes 262176 | tf_op jit(solution)/shard_map/ppermute | solution.py:110
  141.5 0.9 copy-done.1
  142.5 1.4 shard_map.54
  (24 shorter events, 0.1 us)
Async XLA Ops:
  0.0 8.0 %collective-permute-start.3 = (bf16[1,16,256,256]{3,2,1,0:T(8,128)(2,1)}, bf16[1,16,256,256]{3,2,1,0:T(8,128)(2,1)S(1)}, u32[]{:S(2)}, u32[]{:S(2)}) collective-permute-start(bf16[1,16,256,256]{3,2,1,0:T(8,128)(2,1)} %refs_2_.7), channel_id=1, source_target_pairs={{0,1},{1,0},{2,3},{3,2},{4,5},{5,4},{6,7},{7,6},{8,9},{9,8},{10,11... | collective-permute-start | bytes 6291464 | tf_op jit(solution)/shard_map/ppermute | solution.py:110
  0.0 48.4 %collective-permute-start.4 = (bf16[1,16,256,256]{3,2,1,0:T(8,128)(2,1)}, bf16[1,16,256,256]{3,2,1,0:T(8,128)(2,1)}, u32[]{:S(2)}, u32[]{:S(2)}) collective-permute-start(bf16[1,16,256,256]{3,2,1,0:T(8,128)(2,1)} %refs_2_.7), channel_id=1, source_target_pairs={{0,2},{1,3},{2,0},{3,1},{4,6},{5,7},{6,4},{7,5},{8,10},{9,11},{10,... | collective-permute-start | bytes 6291464 | tf_op jit(solution)/shard_map/ppermute | solution.py:110
  1.5 6.5 %collective-permute-start.2 = (bf16[8,1,256,256]{3,2,1,0:T(8,128)(2,1)}, bf16[8,1,256,256]{3,2,1,0:T(8,128)(2,1)S(1)}, u32[]{:S(2)}, u32[]{:S(2)}) collective-permute-start(bf16[8,1,256,256]{3,2,1,0:T(8,128)(2,1)} %refs_0_.7), channel_id=1, source_target_pairs={{0,1},{1,0},{2,3},{3,2},{4,5},{5,4},{6,7},{7,6},{8,9},{9,8},{10,11... | collective-permute-start | bytes 3145736 | tf_op jit(solution)/shard_map/ppermute | solution.py:110
  1.7 25.7 %collective-permute-start = (bf16[8,1,256,256]{3,2,1,0:T(8,128)(2,1)}, bf16[8,1,256,256]{3,2,1,0:T(8,128)(2,1)}, u32[]{:S(2)}, u32[]{:S(2)}) collective-permute-start(bf16[8,1,256,256]{3,2,1,0:T(8,128)(2,1)} %refs_6_), channel_id=1, source_target_pairs={{0,4},{1,5},{2,6},{3,7},{4,0},{5,1},{6,2},{7,3},{8,12},{9,13},{10,... | collective-permute-start | bytes 3145736 | tf_op jit(solution)/shard_map/ppermute | solution.py:110
  2.2 28.2 %collective-permute-start.1 = (bf16[8,1,256,256]{3,2,1,0:T(8,128)(2,1)}, bf16[8,1,256,256]{3,2,1,0:T(8,128)(2,1)}, u32[]{:S(2)}, u32[]{:S(2)}) collective-permute-start(bf16[8,1,256,256]{3,2,1,0:T(8,128)(2,1)} %refs_6_), channel_id=1, source_target_pairs={{4,8},{5,9},{6,10},{7,11},{8,4},{9,5},{10,6},{11,7},{20,24},{21,25... | collective-permute-start | bytes 3145736 | tf_op jit(solution)/shard_map/ppermute | solution.py:110
  8.0 1.0 copy-start.5
  8.9 1.3 copy-start.2
  17.3 26.1 %copy-start.3 = (bf16[8,1,256,256]{3,2,1,0:T(8,128)(2,1)S(1)}, bf16[8,1,256,256]{3,2,1,0:T(8,128)(2,1)}, u32[]{:S(2)}) copy-start(bf16[8,1,256,256]{3,2,1,0:T(8,128)(2,1)} %refs_0_.7) | copy-start | bytes 3145732
  30.4 30.7 %collective-permute-start.7 = (bf16[8,1,256,256]{3,2,1,0:T(8,128)(2,1)}, bf16[8,1,256,256]{3,2,1,0:T(8,128)(2,1)}, u32[]{:S(2)}, u32[]{:S(2)}) collective-permute-start(bf16[8,1,256,256]{3,2,1,0:T(8,128)(2,1)} %collective-permute-done.1.refs_5_.refs_7_), channel_id=1, source_target_pairs={{4,0},{5,1},{6,2},{7,3},{8,12},{9,13},{10,14},{11,15},{20,16},{21,... | collective-permute-start | bytes 3145736 | tf_op jit(solution)/shard_map/ppermute | solution.py:110
  32.7 28.4 %collective-permute-start.8 = (bf16[8,1,256,256]{3,2,1,0:T(8,128)(2,1)}, bf16[8,1,256,256]{3,2,1,0:T(8,128)(2,1)}, u32[]{:S(2)}, u32[]{:S(2)}) collective-permute-start(bf16[8,1,256,256]{3,2,1,0:T(8,128)(2,1)} %collective-permute-done.refs_4_.refs_6_), channel_id=1, source_target_pairs={{4,8},{5,9},{6,10},{7,11},{8,4},{9,5},{10,6},{11,7},{20,24},{21,25... | collective-permute-start | bytes 3145736 | tf_op jit(solution)/shard_map/ppermute | solution.py:110
  43.4 16.5 %collective-permute-start.5 = (bf16[2,256,256]{2,1,0:T(8,128)(2,1)}, bf16[2,256,256]{2,1,0:T(8,128)(2,1)S(1)}, u32[]{:S(2)}, u32[]{:S(2)}) collective-permute-start(bf16[2,256,256]{2,1,0:T(8,128)(2,1)} %shard_map.47), channel_id=1, source_target_pairs={{0,4},{1,5},{2,6},{3,7},{4,0},{5,1},{6,2},{7,3},{8,12},{9,13},{10,... | collective-permute-start | bytes 786440 | tf_op jit(solution)/shard_map/ppermute | solution.py:110
  59.9 29.9 %collective-permute-start.13 = (bf16[1,16,256,256]{3,2,1,0:T(8,128)(2,1)}, bf16[1,16,256,256]{3,2,1,0:T(8,128)(2,1)S(1)}, u32[]{:S(2)}, u32[]{:S(2)}) collective-permute-start(bf16[1,16,256,256]{3,2,1,0:T(8,128)(2,1)} %collective-permute-done.4.refs_4_), channel_id=1, source_target_pairs={{0,1},{1,0},{2,3},{3,2},{4,5},{5,4},{6,7},{7,6},{8,9},{9,8},{10,11... | collective-permute-start | bytes 6291464 | tf_op jit(solution)/shard_map/ppermute | solution.py:110
  60.5 15.0 %collective-permute-start.6 = (bf16[4,1,256,256]{3,2,1,0:T(8,128)(2,1)}, bf16[4,1,256,256]{3,2,1,0:T(8,128)(2,1)S(1)}, u32[]{:S(2)}, u32[]{:S(2)}) collective-permute-start(bf16[4,1,256,256]{3,2,1,0:T(8,128)(2,1)} %get-tuple-element.23), channel_id=1, source_target_pairs={{0,2},{1,3},{2,0},{3,1},{4,6},{5,7},{6,4},{7,5},{8,10},{9,11},{10,... | collective-permute-start | bytes 1572872 | tf_op jit(solution)/shard_map/ppermute | solution.py:110
  68.1 18.2 %collective-permute-start.9 = (bf16[4,1,256,256]{3,2,1,0:T(8,128)(2,1)}, bf16[4,1,256,256]{3,2,1,0:T(8,128)(2,1)S(1)}, u32[]{:S(2)}, u32[]{:S(2)}) collective-permute-start(bf16[4,1,256,256]{3,2,1,0:T(8,128)(2,1)} %get-tuple-element.27), channel_id=1, source_target_pairs={{0,2},{1,3},{2,0},{3,1},{4,6},{5,7},{6,4},{7,5},{8,10},{9,11},{10,... | collective-permute-start | bytes 1572872 | tf_op jit(solution)/shard_map/ppermute | solution.py:110
  69.7 14.0 %collective-permute-start.10 = (bf16[2,256,256]{2,1,0:T(8,128)(2,1)}, bf16[2,256,256]{2,1,0:T(8,128)(2,1)S(1)}, u32[]{:S(2)}, u32[]{:S(2)}) collective-permute-start(bf16[2,256,256]{2,1,0:T(8,128)(2,1)} %shard_map.48), channel_id=1, source_target_pairs={{0,8},{1,9},{2,10},{3,11},{4,12},{5,13},{6,14},{7,15},{8,0},{9,1},... | collective-permute-start | bytes 786440 | tf_op jit(solution)/shard_map/ppermute | solution.py:110
  72.9 36.3 %collective-permute-start.16 = (bf16[8,1,256,256]{3,2,1,0:T(8,128)(2,1)}, bf16[8,1,256,256]{3,2,1,0:T(8,128)(2,1)}, u32[]{:S(2)}, u32[]{:S(2)}) collective-permute-start(bf16[8,1,256,256]{3,2,1,0:T(8,128)(2,1)} %collective-permute-done.8.refs_5_.refs_7_), channel_id=1, source_target_pairs={{4,0},{5,1},{6,2},{7,3},{8,12},{9,13},{10,14},{11,15},{20,16},{21,... | collective-permute-start | bytes 3145736 | tf_op jit(solution)/shard_map/ppermute | solution.py:110
  75.5 14.3 %copy-start.6 = (bf16[4,1,256,256]{3,2,1,0:T(8,128)(2,1)}, bf16[4,1,256,256]{3,2,1,0:T(8,128)(2,1)S(1)}, u32[]{:S(2)}) copy-start(bf16[4,1,256,256]{3,2,1,0:T(8,128)(2,1)S(1)} %collective-permute-done.6.refs_0_) | copy-start | bytes 1572868
  86.3 3.5 %copy-start.7 = (bf16[4,1,256,256]{3,2,1,0:T(8,128)(2,1)}, bf16[4,1,256,256]{3,2,1,0:T(8,128)(2,1)S(1)}, u32[]{:S(2)}) copy-start(bf16[4,1,256,256]{3,2,1,0:T(8,128)(2,1)S(1)} %collective-permute-done.9.refs_1_) | copy-start | bytes 1572868
  86.3 1.9 %collective-permute-start.11 = (bf16[4,1,256,256]{3,2,1,0:T(8,128)(2,1)S(1)}, bf16[4,1,256,256]{3,2,1,0:T(8,128)(2,1)S(1)}, u32[]{:S(2)}, u32[]{:S(2)}) collective-permute-start(bf16[4,1,256,256]{3,2,1,0:T(8,128)(2,1)S(1)} %collective-permute-done.6.refs_0_), channel_id=1, source_target_pairs={{0,1},{1,0},{2,3},{3,2},{4,5},{5,4},{6,7},{7,6},{8,9},{9,8},{10,11... | collective-permute-start | bytes 1572872 | tf_op jit(solution)/shard_map/ppermute | solution.py:110
  86.3 2.7 %collective-permute-start.12 = (bf16[4,1,256,256]{3,2,1,0:T(8,128)(2,1)S(1)}, bf16[4,1,256,256]{3,2,1,0:T(8,128)(2,1)S(1)}, u32[]{:S(2)}, u32[]{:S(2)}) collective-permute-start(bf16[4,1,256,256]{3,2,1,0:T(8,128)(2,1)S(1)} %collective-permute-done.9.refs_1_), channel_id=1, source_target_pairs={{0,1},{1,0},{2,3},{3,2},{4,5},{5,4},{6,7},{7,6},{8,9},{9,8},{10,11... | collective-permute-start | bytes 1572872 | tf_op jit(solution)/shard_map/ppermute | solution.py:110
  88.2 0.8 copy-start.8
  89.0 0.8 copy-start.9
  89.9 1.3 copy-start.4
  98.2 27.3 %collective-permute-start.15 = (bf16[2,256,256]{2,1,0:T(8,128)(2,1)}, bf16[2,256,256]{2,1,0:T(8,128)(2,1)S(1)}, u32[]{:S(2)}, u32[]{:S(2)}) collective-permute-start(bf16[2,256,256]{2,1,0:T(8,128)(2,1)} %shard_map.50), channel_id=1, source_target_pairs={{0,8},{1,9},{2,10},{3,11},{4,12},{5,13},{6,14},{7,15},{8,0},{9,1},... | collective-permute-start | bytes 786440 | tf_op jit(solution)/shard_map/ppermute | solution.py:110
  108.6 17.0 %collective-permute-start.14 = (bf16[2,256,256]{2,1,0:T(8,128)(2,1)}, bf16[2,256,256]{2,1,0:T(8,128)(2,1)S(1)}, u32[]{:S(2)}, u32[]{:S(2)}) collective-permute-start(bf16[2,256,256]{2,1,0:T(8,128)(2,1)} %shard_map.49), channel_id=1, source_target_pairs={{0,4},{1,5},{2,6},{3,7},{4,0},{5,1},{6,2},{7,3},{8,12},{9,13},{10,... | collective-permute-start | bytes 786440 | tf_op jit(solution)/shard_map/ppermute | solution.py:110
  116.3 20.7 %collective-permute-start.18 = (bf16[2,256,256]{2,1,0:T(8,128)(2,1)}, bf16[2,256,256]{2,1,0:T(8,128)(2,1)S(1)}, u32[]{:S(2)}, u32[]{:S(2)}) collective-permute-start(bf16[2,256,256]{2,1,0:T(8,128)(2,1)} %shard_map.53), channel_id=1, source_target_pairs={{0,12},{1,13},{2,14},{3,15},{4,8},{5,9},{6,10},{7,11},{8,4},{9,5},... | collective-permute-start | bytes 786440 | tf_op jit(solution)/shard_map/ppermute | solution.py:110
  124.1 17.5 %copy-start = (bf16[2,256,256]{2,1,0:T(8,128)(2,1)S(1)}, bf16[2,256,256]{2,1,0:T(8,128)(2,1)}, u32[]{:S(2)}) copy-start(bf16[2,256,256]{2,1,0:T(8,128)(2,1)} %shard_map.46.refs_0_) | copy-start | bytes 786436
  124.1 17.4 %collective-permute-start.17 = (bf16[2,256,256]{2,1,0:T(8,128)(2,1)}, bf16[2,256,256]{2,1,0:T(8,128)(2,1)S(1)}, u32[]{:S(2)}, u32[]{:S(2)}) collective-permute-start(bf16[2,256,256]{2,1,0:T(8,128)(2,1)} %shard_map.52), channel_id=1, source_target_pairs={{0,12},{1,13},{2,14},{3,15},{4,8},{5,9},{6,10},{7,11},{8,4},{9,5},... | collective-permute-start | bytes 786440 | tf_op jit(solution)/shard_map/ppermute | solution.py:110
  141.5 1.0 copy-start.1

commit v5 on v4

v5 whole, which is shorter than its diff:
```python
import functools

import jax
import jax.numpy as jnp
from jax import lax
from jax.experimental import pallas as pl
from jax.experimental.pallas import tpu as pltpu
from jax.sharding import PartitionSpec as P

HBM = pl.BlockSpec(memory_space=pltpu.HBM)
SMEM = pl.BlockSpec(memory_space=pltpu.SMEM)
VMEM = pl.BlockSpec(memory_space=pltpu.VMEM)


def slot_kernel(step, count, choices, source, *refs):
    parts = (len(refs) - choices - 3) // count - 1
    lefts, refs = refs[: parts * count], refs[parts * count :]
    psis, rights = refs[:count], refs[count : count + choices]
    out, right_buf, mid_buf = refs[count + choices :]
    terms, _, rows, columns = rights[0].shape
    me = lax.axis_index("sec")
    row = me >> 2
    q = me ^ (4 * step)
    outer = (row == 0) | (row == 3)

    for k in range(terms):
        span = pl.ds(k * columns, columns)
        part, place = divmod(k, terms // parts)
        right = rights[0][k, 0]
        if choices > 1:
            right = jnp.where(outer, right, rights[1][k, 0])
        right_buf[:, span] = right
        for i in range(count):
            mid = jnp.dot(
                lefts[i * parts + part][place, 0], psis[i][0, source[k, q]], preferred_element_type=jnp.float32
            )
            mid_buf[pl.ds(i * rows, rows), span] = mid.astype(jnp.bfloat16)
    total = lax.dot_general(
        mid_buf[...], right_buf[...], (((1,), (1,)), ((), ())), preferred_element_type=jnp.float32
    )
    out[...] = total.reshape(out.shape).astype(out.dtype)


def slot(step, source_map, lefts, psis, rights, dtype, flops):
    terms, _, rows, columns = rights[0].shape
    count = len(psis)
    return pl.pallas_call(
        functools.partial(slot_kernel, step, count, len(rights)),
        out_shape=jax.ShapeDtypeStruct((count, rows, columns), dtype),
        in_specs=[SMEM] + [VMEM] * (len(lefts) + count + len(rights)),
        out_specs=VMEM,
        scratch_shapes=[
            pltpu.VMEM((rows, terms * columns), jnp.bfloat16),
            pltpu.VMEM((count * rows, terms * columns), jnp.bfloat16),
        ],
        compiler_params=pltpu.CompilerParams(vmem_limit_bytes=24 << 20),
        cost_estimate=pl.CostEstimate(flops=flops, bytes_accessed=1, transcendentals=0),
    )(source_map, *lefts, *psis, *rights)


def split_kernel(whole, low, high):
    half = low.shape[0]
    low[...] = whole[:half]
    high[...] = whole[half:]


def split(array):
    half = jax.ShapeDtypeStruct((array.shape[0] // 2,) + array.shape[1:], array.dtype)
    return pl.pallas_call(
        split_kernel,
        out_shape=(half, half),
        in_specs=[VMEM],
        out_specs=(VMEM, VMEM),
        compiler_params=pltpu.CompilerParams(vmem_limit_bytes=8 << 20),
        cost_estimate=pl.CostEstimate(flops=1, bytes_accessed=1, transcendentals=0),
    )(array)


def place_kernel(width, *refs):
    pieces, out, sem = refs[:-2], refs[-2], refs[-1]
    me = lax.axis_index("sec")

    def copy(j):
        return pltpu.make_async_copy(pieces[j // width].at[j % width], out.at[me ^ j], sem.at[j])

    for j in range(len(pieces) * width):
        copy(j).start()
    for j in range(len(pieces) * width):
        copy(j).wait()


def place(pieces):
    width, rows, columns = pieces[0].shape
    sectors = width * len(pieces)
    return pl.pallas_call(
        functools.partial(place_kernel, width),
        out_shape=jax.ShapeDtypeStruct((sectors, rows, columns), pieces[0].dtype),
        in_specs=[VMEM] * len(pieces),
        out_specs=HBM,
        scratch_shapes=[pltpu.SemaphoreType.DMA((sectors,))],
        compiler_params=pltpu.CompilerParams(vmem_limit_bytes=16 << 20),
    )(*pieces)


def exchange(array, bits, members):
    return lax.ppermute(array, "sec", [(s, s ^ bits) for s in members])


def on_device(ops, psi, left_env, right_env, source_map):
    dtype = jnp.bfloat16 if ops == 1 else jnp.float32
    every = range(16)
    inner = range(4, 12)
    low, high = split(left_env)

    def products(step, lefts, psis, rights, flops=1):
        return slot(step, source_map, lefts, psis, rights, dtype, flops)

    near = exchange(right_env, 4, every)
    middle = exchange(right_env, 12, inner)
    x_psi = exchange(psi, 2, every)
    own = ([left_env, exchange(left_env, 1, every)], [psi, exchange(psi, 1, every)])
    own_0 = products(0, *own, (right_env,))

    near, middle, own_0 = lax.optimization_barrier((near, middle, own_0))
    far_in = exchange(near, 12, inner)
    second = exchange(middle, 4, inner)
    own_1 = products(1, *own, (near,))
    sent_1 = exchange(own_1, 4, every)

    x_psi, low = lax.optimization_barrier((x_psi, low))
    x_low = exchange(low, 2, every)
    across_psi = exchange(x_psi, 1, every)

    second, far_in = lax.optimization_barrier((second, far_in))
    third = exchange(far_in, 4, inner)
    own_2 = products(2, *own, (second, far_in))
    sent_2 = exchange(own_2, 8, every)

    own_2, sent_1, high = lax.optimization_barrier((own_2, sent_1, high))
    x_high = exchange(high, 2, every)
    x_low, x_high, sent_2 = lax.optimization_barrier((x_low, x_high, sent_2))
    across_low = exchange(x_low, 1, every)
    across_high = exchange(x_high, 1, every)
    other = ([x_low, x_high, across_low, across_high], [x_psi, across_psi])
    other_2 = products(2, *other, (second, far_in))
    other_sent_2 = exchange(other_2, 8, every)
    other_1 = products(1, *other, (near,))
    other_sent_1 = exchange(other_1, 4, every)

    third, other_1, other_2 = lax.optimization_barrier((third, other_1, other_2))
    own_3 = products(3, *own, (third, middle))
    sent_3 = exchange(own_3, 12, every)
    other_3 = products(3, *other, (third, middle))
    other_sent_3 = exchange(other_3, 12, every)
    right_last, other_sent_1, other_sent_2 = lax.optimization_barrier((right_env, other_sent_1, other_sent_2))
    other_0 = products(0, *other, (right_last,), flops=10**10)

    pieces = [own_0, other_0, sent_1, other_sent_1, sent_2, other_sent_2, sent_3, other_sent_3]
    out = place(pieces)[:, None]
    if ops > 1:
        out = lax.psum_scatter(out, "op", scatter_dimension=2, tiled=True).astype(jnp.bfloat16)
    return out


def solution(mesh):
    placed = (
        P(("group", "sec"), None, None, None),
        P(("group", "op"), "sec", None, None),
        P(("group", "op"), "sec", None, None),
        P(("group", "op"), None),
    )
    return jax.shard_map(
        functools.partial(on_device, mesh.shape["op"]),
        mesh=mesh,
        in_specs=placed,
        out_specs=P("group", "sec", "op", None),
        check_vma=False,
    )
```

time: 145 us -> 125 us (0.86)
  the two profiles are of different devices: /device:TPU:8 before, /device:TPU:20 now
where the time goes in v5:
time: 125 us; the launch traced here: 124 us
  waiting for transfers between devices  82.8 us (66%)
  starting transfers between devices  20.1 us (16%)
  Pallas kernels  16.6 us (13%)
  local copies, waits for them, and re-layouts  4.75 us (4%)
    ppermute x19, waiting for transfers between devices, exchange(): return lax.ppermute(array, 'sec', [(s, s ^ bits) for s in members])  82.8 us
    ppermute x19, starting transfers between devices, exchange(): return lax.ppermute(array, 'sec', [(s, s ^ bits) for s in members])  20.1 us
    pallas_call x8, Pallas kernels, slot(): pl.pallas_call(functools.partial(slot_kernel, step, count, len(rights)),...  15.1 us
    unnamed x14, local copies, waits for them, and re-layouts  4.75 us
  transfers between devices with their start and end apart: 19, of which 15 were waited for; matrix products, arithmetic and copies ran while one was open for 0% of the time, Pallas kernels for 12%

profile of v5, /device:TPU:20, one launch (start us, length us, event | category | flops | bytes accessed | tf_op | source)
XLA Modules:
  0.0 124.4 jit_solution(2935856719949757881)
XLA Ops:
  0.0 1.5 %collective-permute-start.4 = (bf16[1,16,256,256]{3,2,1,0:T(8,128)(2,1)}, bf16[1,16,256,256]{3,2,1,0:T(8,128)(2,1)S(1)}, u32[]{:S(2)}, u32[]{:S(2)}) collective-permute-start(bf16[1,16,256,256]{3,2,1,0:T(8,128)(2,1)} %refs_2_.7), channel_id=1, source_target_pairs={{0,2},{1,3},{2,0},{3,1},{4,6},{5,7},{6,4},{7,5},{8,10},{9,11},{10,... | collective-permute-start | bytes 6291464 | tf_op jit(solution)/shard_map/ppermute | solution.py:106
  1.5 0.2 collective-permute-start.2
  1.7 1.6 %collective-permute-start = (bf16[8,1,256,256]{3,2,1,0:T(8,128)(2,1)}, bf16[8,1,256,256]{3,2,1,0:T(8,128)(2,1)S(1)}, u32[]{:S(2)}, u32[]{:S(2)}) collective-permute-start(bf16[8,1,256,256]{3,2,1,0:T(8,128)(2,1)} %refs_6_), channel_id=1, source_target_pairs={{0,4},{1,5},{2,6},{3,7},{4,0},{5,1},{6,2},{7,3},{8,12},{9,13},{10,... | collective-permute-start | bytes 3145736 | tf_op jit(solution)/shard_map/ppermute | solution.py:106
  3.3 1.9 %collective-permute-start.1 = (bf16[8,1,256,256]{3,2,1,0:T(8,128)(2,1)}, bf16[8,1,256,256]{3,2,1,0:T(8,128)(2,1)S(1)}, u32[]{:S(2)}, u32[]{:S(2)}) collective-permute-start(bf16[8,1,256,256]{3,2,1,0:T(8,128)(2,1)} %refs_6_), channel_id=1, source_target_pairs={{4,8},{5,9},{6,10},{7,11},{8,4},{9,5},{10,6},{11,7},{20,24},{21,25... | collective-permute-start | bytes 3145736 | tf_op jit(solution)/shard_map/ppermute | solution.py:106
  5.2 0.7 collective-permute-done.2.refs_1_
  5.9 1.6 %copy-done = bf16[1,16,256,256]{3,2,1,0:T(8,128)(2,1)S(1)} copy-done((bf16[1,16,256,256]{3,2,1,0:T(8,128)(2,1)S(1)}, bf16[1,16,256,256]{3,2,1,0:T(8,128)(2,1)}, u32[]{:S(2)}) %copy-start) | copy-done | bytes 2097176
  7.5 1.2 copy-done.2
  8.7 1.2 copy-done.4
  9.9 0.7 copy-done.6
  10.6 1.9 %shard_map.46.refs_0_ = bf16[2,256,256]{2,1,0:T(8,128)(2,1)S(1)} custom-call(s32[8,16]{1,0:T(8,128)S(1)} %copy-done.6, bf16[8,1,256,256]{3,2,1,0:T(8,128)(2,1)S(1)} %copy-done.2, bf16[8,1,256,256]{3,2,1,0:T(8,128)(2,1)S(1)} %collective-permute-done.2.refs_1_, bf16[1,16,256,256]{3,2,1,0:T(8,128)(2,1)S(1)} %copy-done, ...), custom_call_target="tpu_custom_call" | custom-call | flops 1 | bytes 1 | tf_op jit(solution)/shard_map/pallas_call | solution.py:47
  12.5 14.8 %collective-permute-done.refs_4_.refs_6_ = bf16[8,1,256,256]{3,2,1,0:T(8,128)(2,1)S(1)} collective-permute-done((bf16[8,1,256,256]{3,2,1,0:T(8,128)(2,1)}, bf16[8,1,256,256]{3,2,1,0:T(8,128)(2,1)S(1)}, u32[]{:S(2)}, u32[]{:S(2)}) %collective-permute-start) | collective-permute-done | bytes 1048608 | tf_op jit(solution)/shard_map/ppermute | solution.py:106
  27.3 3.2 %collective-permute-done.1.refs_5_.refs_7_ = bf16[8,1,256,256]{3,2,1,0:T(8,128)(2,1)S(1)} collective-permute-done((bf16[8,1,256,256]{3,2,1,0:T(8,128)(2,1)}, bf16[8,1,256,256]{3,2,1,0:T(8,128)(2,1)S(1)}, u32[]{:S(2)}, u32[]{:S(2)}) %collective-permute-start.1) | collective-permute-done | bytes 1048608 | tf_op jit(solution)/shard_map/ppermute | solution.py:106
  30.5 1.3 %collective-permute-start.6 = (bf16[8,1,256,256]{3,2,1,0:T(8,128)(2,1)S(1)}, bf16[8,1,256,256]{3,2,1,0:T(8,128)(2,1)S(1)}, u32[]{:S(2)}, u32[]{:S(2)}) collective-permute-start(bf16[8,1,256,256]{3,2,1,0:T(8,128)(2,1)S(1)} %collective-permute-done.1.refs_5_.refs_7_), channel_id=1, source_target_pairs={{4,0},{5,1},{6,2},{7,3},{8,12},{9,13},{10,14},{11,15},{20,16},{21,... | collective-permute-start | bytes 3145736 | tf_op jit(solution)/shard_map/ppermute | solution.py:106
  31.8 2.2 %collective-permute-start.7 = (bf16[8,1,256,256]{3,2,1,0:T(8,128)(2,1)S(1)}, bf16[8,1,256,256]{3,2,1,0:T(8,128)(2,1)S(1)}, u32[]{:S(2)}, u32[]{:S(2)}) collective-permute-start(bf16[8,1,256,256]{3,2,1,0:T(8,128)(2,1)S(1)} %collective-permute-done.refs_4_.refs_6_), channel_id=1, source_target_pairs={{4,8},{5,9},{6,10},{7,11},{8,4},{9,5},{10,6},{11,7},{20,24},{21,25... | collective-permute-start | bytes 3145736 | tf_op jit(solution)/shard_map/ppermute | solution.py:106
  34.0 0.1 shard_map.47
  34.1 14.2 %collective-permute-done.4.refs_4_ = bf16[1,16,256,256]{3,2,1,0:T(8,128)(2,1)S(1)} collective-permute-done((bf16[1,16,256,256]{3,2,1,0:T(8,128)(2,1)}, bf16[1,16,256,256]{3,2,1,0:T(8,128)(2,1)S(1)}, u32[]{:S(2)}, u32[]{:S(2)}) %collective-permute-start.4) | collective-permute-done | bytes 2097184 | tf_op jit(solution)/shard_map/ppermute | solution.py:106
  48.3 1.9 %shard_map.49 = bf16[2,256,256]{2,1,0:T(8,128)(2,1)S(1)} custom-call(s32[8,16]{1,0:T(8,128)S(1)} %copy-done.6, bf16[8,1,256,256]{3,2,1,0:T(8,128)(2,1)S(1)} %copy-done.2, bf16[8,1,256,256]{3,2,1,0:T(8,128)(2,1)S(1)} %collective-permute-done.2.refs_1_, bf16[1,16,256,256]{3,2,1,0:T(8,128)(2,1)S(1)} %copy-done, ...), custom_call_target="tpu_custom_call" | custom-call | flops 1 | bytes 1 | tf_op jit(solution)/shard_map/pallas_call | solution.py:47
  50.1 1.6 %collective-permute-start.8 = (bf16[2,256,256]{2,1,0:T(8,128)(2,1)S(1)}, bf16[2,256,256]{2,1,0:T(8,128)(2,1)S(1)}, u32[]{:S(2)}, u32[]{:S(2)}) collective-permute-start(bf16[2,256,256]{2,1,0:T(8,128)(2,1)S(1)} %shard_map.49), channel_id=1, source_target_pairs={{0,4},{1,5},{2,6},{3,7},{4,0},{5,1},{6,2},{7,3},{8,12},{9,13},{10,... | collective-permute-start | bytes 786440 | tf_op jit(solution)/shard_map/ppermute | solution.py:106
  51.8 1.5 %collective-permute-start.5 = (bf16[4,1,256,256]{3,2,1,0:T(8,128)(2,1)S(1)}, bf16[4,1,256,256]{3,2,1,0:T(8,128)(2,1)S(1)}, u32[]{:S(2)}, u32[]{:S(2)}) collective-permute-start(bf16[4,1,256,256]{3,2,1,0:T(8,128)(2,1)S(1)} %get-tuple-element.25), channel_id=1, source_target_pairs={{0,2},{1,3},{2,0},{3,1},{4,6},{5,7},{6,4},{7,5},{8,10},{9,11},{10,... | collective-permute-start | bytes 1572872 | tf_op jit(solution)/shard_map/ppermute | solution.py:106
  53.3 1.7 %collective-permute-done.6.refs_4_.refs_6_ = bf16[8,1,256,256]{3,2,1,0:T(8,128)(2,1)S(1)} collective-permute-done((bf16[8,1,256,256]{3,2,1,0:T(8,128)(2,1)S(1)}, bf16[8,1,256,256]{3,2,1,0:T(8,128)(2,1)S(1)}, u32[]{:S(2)}, u32[]{:S(2)}) %collective-permute-start.6) | collective-permute-done | bytes 1048608 | tf_op jit(solution)/shard_map/ppermute | solution.py:106
  55.0 2.9 %collective-permute-done.7.refs_5_.refs_7_ = bf16[8,1,256,256]{3,2,1,0:T(8,128)(2,1)S(1)} collective-permute-done((bf16[8,1,256,256]{3,2,1,0:T(8,128)(2,1)S(1)}, bf16[8,1,256,256]{3,2,1,0:T(8,128)(2,1)S(1)}, u32[]{:S(2)}, u32[]{:S(2)}) %collective-permute-start.7) | collective-permute-done | bytes 1048608 | tf_op jit(solution)/shard_map/ppermute | solution.py:106
  57.9 1.9 %shard_map.48 = bf16[2,256,256]{2,1,0:T(8,128)(2,1)S(1)} custom-call(s32[8,16]{1,0:T(8,128)S(1)} %copy-done.6, bf16[8,1,256,256]{3,2,1,0:T(8,128)(2,1)S(1)} %copy-done.2, bf16[8,1,256,256]{3,2,1,0:T(8,128)(2,1)S(1)} %collective-permute-done.2.refs_1_, bf16[1,16,256,256]{3,2,1,0:T(8,128)(2,1)S(1)} %copy-done, ...), custom_call_target="tpu_custom_call" | custom-call | flops 1 | bytes 1 | tf_op jit(solution)/shard_map/pallas_call | solution.py:47
  59.8 0.6 collective-permute-start.9
  60.4 2.0 %collective-permute-start.10 = (bf16[2,256,256]{2,1,0:T(8,128)(2,1)S(1)}, bf16[2,256,256]{2,1,0:T(8,128)(2,1)S(1)}, u32[]{:S(2)}, u32[]{:S(2)}) collective-permute-start(bf16[2,256,256]{2,1,0:T(8,128)(2,1)S(1)} %shard_map.48), channel_id=1, source_target_pairs={{0,8},{1,9},{2,10},{3,11},{4,12},{5,13},{6,14},{7,15},{8,0},{9,1},... | collective-permute-start | bytes 786440 | tf_op jit(solution)/shard_map/ppermute | solution.py:106
  62.4 2.1 %collective-permute-start.16 = (bf16[8,1,256,256]{3,2,1,0:T(8,128)(2,1)S(1)}, bf16[8,1,256,256]{3,2,1,0:T(8,128)(2,1)S(1)}, u32[]{:S(2)}, u32[]{:S(2)}) collective-permute-start(bf16[8,1,256,256]{3,2,1,0:T(8,128)(2,1)S(1)} %collective-permute-done.7.refs_5_.refs_7_), channel_id=1, source_target_pairs={{4,0},{5,1},{6,2},{7,3},{8,12},{9,13},{10,14},{11,15},{20,16},{21,... | collective-permute-start | bytes 3145736 | tf_op jit(solution)/shard_map/ppermute | solution.py:106
  64.5 2.1 %collective-permute-done.5.refs_0_ = bf16[4,1,256,256]{3,2,1,0:T(8,128)(2,1)S(1)} collective-permute-done((bf16[4,1,256,256]{3,2,1,0:T(8,128)(2,1)S(1)}, bf16[4,1,256,256]{3,2,1,0:T(8,128)(2,1)S(1)}, u32[]{:S(2)}, u32[]{:S(2)}) %collective-permute-start.5) | collective-permute-done | bytes 524320 | tf_op jit(solution)/shard_map/ppermute | solution.py:106
  66.5 5.9 %collective-permute-done.10.refs_4_ = bf16[2,256,256]{2,1,0:T(8,128)(2,1)S(1)} collective-permute-done((bf16[2,256,256]{2,1,0:T(8,128)(2,1)S(1)}, bf16[2,256,256]{2,1,0:T(8,128)(2,1)S(1)}, u32[]{:S(2)}, u32[]{:S(2)}) %collective-permute-start.10) | collective-permute-done | bytes 262176 | tf_op jit(solution)/shard_map/ppermute | solution.py:106
  72.4 4.7 %collective-permute-done.9.refs_1_ = bf16[4,1,256,256]{3,2,1,0:T(8,128)(2,1)S(1)} collective-permute-done((bf16[4,1,256,256]{3,2,1,0:T(8,128)(2,1)S(1)}, bf16[4,1,256,256]{3,2,1,0:T(8,128)(2,1)S(1)}, u32[]{:S(2)}, u32[]{:S(2)}) %collective-permute-start.9) | collective-permute-done | bytes 524320 | tf_op jit(solution)/shard_map/ppermute | solution.py:106
  77.1 0.5 collective-permute-start.12
  77.6 1.4 %collective-permute-done.11.refs_2_ = bf16[4,1,256,256]{3,2,1,0:T(8,128)(2,1)S(1)} collective-permute-done((bf16[4,1,256,256]{3,2,1,0:T(8,128)(2,1)S(1)}, bf16[4,1,256,256]{3,2,1,0:T(8,128)(2,1)S(1)}, u32[]{:S(2)}, u32[]{:S(2)}) %collective-permute-start.11) | collective-permute-done | bytes 524320 | tf_op jit(solution)/shard_map/ppermute | solution.py:106
  79.0 0.7 collective-permute-done.12.refs_3_
  79.7 1.9 %shard_map.51 = bf16[2,256,256]{2,1,0:T(8,128)(2,1)S(1)} custom-call(s32[8,16]{1,0:T(8,128)S(1)} %copy-done.6, bf16[4,1,256,256]{3,2,1,0:T(8,128)(2,1)S(1)} %collective-permute-done.5.refs_0_, bf16[4,1,256,256]{3,2,1,0:T(8,128)(2,1)S(1)} %collective-permute-done.9.refs_1_, bf16[4,1,256,256]{3,2,1,0:T(8,128)(2,1)S(1)} %collective-permute-done.11.refs_2_, ...), custom_call_target="tpu_custom_call" | custom-call | flops 1 | bytes 1 | tf_op jit(solution)/shard_map/pallas_call | solution.py:47
  81.7 0.4 collective-permute-start.15
  82.1 1.9 %shard_map.50 = bf16[2,256,256]{2,1,0:T(8,128)(2,1)S(1)} custom-call(s32[8,16]{1,0:T(8,128)S(1)} %copy-done.6, bf16[4,1,256,256]{3,2,1,0:T(8,128)(2,1)S(1)} %collective-permute-done.5.refs_0_, bf16[4,1,256,256]{3,2,1,0:T(8,128)(2,1)S(1)} %collective-permute-done.9.refs_1_, bf16[4,1,256,256]{3,2,1,0:T(8,128)(2,1)S(1)} %collective-permute-done.11.refs_2_, ...), custom_call_target="tpu_custom_call" | custom-call | flops 1 | bytes 1 | tf_op jit(solution)/shard_map/pallas_call | solution.py:47
  83.9 0.0 copy-start.1
  83.9 0.0 copy-start.3
  84.0 0.5 collective-permute-start.14
  84.5 14.7 %collective-permute-done.16.refs_4_.refs_6_ = bf16[8,1,256,256]{3,2,1,0:T(8,128)(2,1)S(1)} collective-permute-done((bf16[8,1,256,256]{3,2,1,0:T(8,128)(2,1)S(1)}, bf16[8,1,256,256]{3,2,1,0:T(8,128)(2,1)S(1)}, u32[]{:S(2)}, u32[]{:S(2)}) %collective-permute-start.16) | collective-permute-done | bytes 1048608 | tf_op jit(solution)/shard_map/ppermute | solution.py:106
  99.2 1.9 %shard_map.54 = bf16[2,256,256]{2,1,0:T(8,128)(2,1)S(1)} custom-call(s32[8,16]{1,0:T(8,128)S(1)} %copy-done.6, bf16[4,1,256,256]{3,2,1,0:T(8,128)(2,1)S(1)} %collective-permute-done.5.refs_0_, bf16[4,1,256,256]{3,2,1,0:T(8,128)(2,1)S(1)} %collective-permute-done.9.refs_1_, bf16[4,1,256,256]{3,2,1,0:T(8,128)(2,1)S(1)} %collective-permute-done.11.refs_2_, ...), custom_call_target="tpu_custom_call" | custom-call | flops 1 | bytes 1 | tf_op jit(solution)/shard_map/pallas_call | solution.py:47
  101.1 0.0 copy-start.5
  101.1 0.9 collective-permute-start.18
  102.0 1.9 %shard_map.53 = bf16[2,256,256]{2,1,0:T(8,128)(2,1)S(1)} custom-call(s32[8,16]{1,0:T(8,128)S(1)} %copy-done.6, bf16[8,1,256,256]{3,2,1,0:T(8,128)(2,1)S(1)} %copy-done.3, bf16[8,1,256,256]{3,2,1,0:T(8,128)(2,1)S(1)} %collective-permute-done.2.refs_1_, bf16[1,16,256,256]{3,2,1,0:T(8,128)(2,1)S(1)} %copy-done.1, ...), custom_call_target="tpu_custom_call" | custom-call | flops 1 | bytes 1 | tf_op jit(solution)/shard_map/pallas_call | solution.py:47
  103.9 1.3 %collective-permute-start.17 = (bf16[2,256,256]{2,1,0:T(8,128)(2,1)S(1)}, bf16[2,256,256]{2,1,0:T(8,128)(2,1)S(1)}, u32[]{:S(2)}, u32[]{:S(2)}) collective-permute-start(bf16[2,256,256]{2,1,0:T(8,128)(2,1)S(1)} %shard_map.53), channel_id=1, source_target_pairs={{0,12},{1,13},{2,14},{3,15},{4,8},{5,9},{6,10},{7,11},{8,4},{9,5},... | collective-permute-start | bytes 786440 | tf_op jit(solution)/shard_map/ppermute | solution.py:106
  105.2 9.2 %collective-permute-done.14.refs_3_ = bf16[2,256,256]{2,1,0:T(8,128)(2,1)S(1)} collective-permute-done((bf16[2,256,256]{2,1,0:T(8,128)(2,1)S(1)}, bf16[2,256,256]{2,1,0:T(8,128)(2,1)S(1)}, u32[]{:S(2)}, u32[]{:S(2)}) %collective-permute-start.14) | collective-permute-done | bytes 262176 | tf_op jit(solution)/shard_map/ppermute | solution.py:106
  114.4 1.9 %shard_map.52.refs_1_ = bf16[2,256,256]{2,1,0:T(8,128)(2,1)S(1)} custom-call(s32[8,16]{1,0:T(8,128)S(1)} %copy-done.6, bf16[4,1,256,256]{3,2,1,0:T(8,128)(2,1)S(1)} %collective-permute-done.5.refs_0_, bf16[4,1,256,256]{3,2,1,0:T(8,128)(2,1)S(1)} %collective-permute-done.9.refs_1_, bf16[4,1,256,256]{3,2,1,0:T(8,128)(2,1)S(1)} %collective-permute-done.11.refs_2_, ...), custom_call_target="tpu_custom_call" | custom-call | flops 10000000000 | bytes 1 | tf_op jit(solution)/shard_map/pallas_call | solution.py:47
  116.3 3.9 %collective-permute-done.18.refs_7_ = bf16[2,256,256]{2,1,0:T(8,128)(2,1)S(1)} collective-permute-done((bf16[2,256,256]{2,1,0:T(8,128)(2,1)S(1)}, bf16[2,256,256]{2,1,0:T(8,128)(2,1)S(1)}, u32[]{:S(2)}, u32[]{:S(2)}) %collective-permute-start.18) | collective-permute-done | bytes 262176 | tf_op jit(solution)/shard_map/ppermute | solution.py:106
  120.2 2.8 %collective-permute-done.17.refs_6_ = bf16[2,256,256]{2,1,0:T(8,128)(2,1)S(1)} collective-permute-done((bf16[2,256,256]{2,1,0:T(8,128)(2,1)S(1)}, bf16[2,256,256]{2,1,0:T(8,128)(2,1)S(1)}, u32[]{:S(2)}, u32[]{:S(2)}) %collective-permute-start.17) | collective-permute-done | bytes 262176 | tf_op jit(solution)/shard_map/ppermute | solution.py:106
  123.0 1.4 %shard_map.55 = bf16[16,256,256]{2,1,0:T(8,128)(2,1)} custom-call(bf16[2,256,256]{2,1,0:T(8,128)(2,1)S(1)} %shard_map.46.refs_0_, bf16[2,256,256]{2,1,0:T(8,128)(2,1)S(1)} %shard_map.52.refs_1_, bf16[2,256,256]{2,1,0:T(8,128)(2,1)S(1)} %collective-permute-done.8.refs_2_, bf16[2,256,256]{2,1,0:T(8,128)(2,1)S(1)} %collective-permute-done.14.refs_3_, ...), custom_call_target="tpu_custom_call" | custom-call | tf_op jit(solution)/shard_map/pallas_call | solution.py:95
  (14 shorter events, 0.0 us)
Async XLA Ops:
  0.0 5.9 %collective-permute-start.3 = (bf16[1,16,256,256]{3,2,1,0:T(8,128)(2,1)}, bf16[1,16,256,256]{3,2,1,0:T(8,128)(2,1)S(1)}, u32[]{:S(2)}, u32[]{:S(2)}) collective-permute-start(bf16[1,16,256,256]{3,2,1,0:T(8,128)(2,1)} %refs_2_.7), channel_id=1, source_target_pairs={{0,1},{1,0},{2,3},{3,2},{4,5},{5,4},{6,7},{7,6},{8,9},{9,8},{10,11... | collective-permute-start | bytes 6291464 | tf_op jit(solution)/shard_map/ppermute | solution.py:106
  0.0 48.3 %collective-permute-start.4 = (bf16[1,16,256,256]{3,2,1,0:T(8,128)(2,1)}, bf16[1,16,256,256]{3,2,1,0:T(8,128)(2,1)S(1)}, u32[]{:S(2)}, u32[]{:S(2)}) collective-permute-start(bf16[1,16,256,256]{3,2,1,0:T(8,128)(2,1)} %refs_2_.7), channel_id=1, source_target_pairs={{0,2},{1,3},{2,0},{3,1},{4,6},{5,7},{6,4},{7,5},{8,10},{9,11},{10,... | collective-permute-start | bytes 6291464 | tf_op jit(solution)/shard_map/ppermute | solution.py:106
  1.5 4.4 %collective-permute-start.2 = (bf16[8,1,256,256]{3,2,1,0:T(8,128)(2,1)}, bf16[8,1,256,256]{3,2,1,0:T(8,128)(2,1)S(1)}, u32[]{:S(2)}, u32[]{:S(2)}) collective-permute-start(bf16[8,1,256,256]{3,2,1,0:T(8,128)(2,1)} %refs_0_.7), channel_id=1, source_target_pairs={{0,1},{1,0},{2,3},{3,2},{4,5},{5,4},{6,7},{7,6},{8,9},{9,8},{10,11... | collective-permute-start | bytes 3145736 | tf_op jit(solution)/shard_map/ppermute | solution.py:106
  1.7 25.6 %collective-permute-start = (bf16[8,1,256,256]{3,2,1,0:T(8,128)(2,1)}, bf16[8,1,256,256]{3,2,1,0:T(8,128)(2,1)S(1)}, u32[]{:S(2)}, u32[]{:S(2)}) collective-permute-start(bf16[8,1,256,256]{3,2,1,0:T(8,128)(2,1)} %refs_6_), channel_id=1, source_target_pairs={{0,4},{1,5},{2,6},{3,7},{4,0},{5,1},{6,2},{7,3},{8,12},{9,13},{10,... | collective-permute-start | bytes 3145736 | tf_op jit(solution)/shard_map/ppermute | solution.py:106
  3.3 27.2 %collective-permute-start.1 = (bf16[8,1,256,256]{3,2,1,0:T(8,128)(2,1)}, bf16[8,1,256,256]{3,2,1,0:T(8,128)(2,1)S(1)}, u32[]{:S(2)}, u32[]{:S(2)}) collective-permute-start(bf16[8,1,256,256]{3,2,1,0:T(8,128)(2,1)} %refs_6_), channel_id=1, source_target_pairs={{4,8},{5,9},{6,10},{7,11},{8,4},{9,5},{10,6},{11,7},{20,24},{21,25... | collective-permute-start | bytes 3145736 | tf_op jit(solution)/shard_map/ppermute | solution.py:106
  5.9 1.6 %copy-start = (bf16[1,16,256,256]{3,2,1,0:T(8,128)(2,1)S(1)}, bf16[1,16,256,256]{3,2,1,0:T(8,128)(2,1)}, u32[]{:S(2)}) copy-start(bf16[1,16,256,256]{3,2,1,0:T(8,128)(2,1)} %refs_2_.7) | copy-start | bytes 6291460
  7.5 1.2 copy-start.2
  8.7 1.2 copy-start.4
  9.9 0.7 copy-start.6
  30.5 24.6 %collective-permute-start.6 = (bf16[8,1,256,256]{3,2,1,0:T(8,128)(2,1)S(1)}, bf16[8,1,256,256]{3,2,1,0:T(8,128)(2,1)S(1)}, u32[]{:S(2)}, u32[]{:S(2)}) collective-permute-start(bf16[8,1,256,256]{3,2,1,0:T(8,128)(2,1)S(1)} %collective-permute-done.1.refs_5_.refs_7_), channel_id=1, source_target_pairs={{4,0},{5,1},{6,2},{7,3},{8,12},{9,13},{10,14},{11,15},{20,16},{21,... | collective-permute-start | bytes 3145736 | tf_op jit(solution)/shard_map/ppermute | solution.py:106
  31.8 26.1 %collective-permute-start.7 = (bf16[8,1,256,256]{3,2,1,0:T(8,128)(2,1)S(1)}, bf16[8,1,256,256]{3,2,1,0:T(8,128)(2,1)S(1)}, u32[]{:S(2)}, u32[]{:S(2)}) collective-permute-start(bf16[8,1,256,256]{3,2,1,0:T(8,128)(2,1)S(1)} %collective-permute-done.refs_4_.refs_6_), channel_id=1, source_target_pairs={{4,8},{5,9},{6,10},{7,11},{8,4},{9,5},{10,6},{11,7},{20,24},{21,25... | collective-permute-start | bytes 3145736 | tf_op jit(solution)/shard_map/ppermute | solution.py:106
  48.3 31.5 %collective-permute-start.13 = (bf16[1,16,256,256]{3,2,1,0:T(8,128)(2,1)S(1)}, bf16[1,16,256,256]{3,2,1,0:T(8,128)(2,1)S(1)}, u32[]{:S(2)}, u32[]{:S(2)}) collective-permute-start(bf16[1,16,256,256]{3,2,1,0:T(8,128)(2,1)S(1)} %collective-permute-done.4.refs_4_), channel_id=1, source_target_pairs={{0,1},{1,0},{2,3},{3,2},{4,5},{5,4},{6,7},{7,6},{8,9},{9,8},{10,11... | collective-permute-start | bytes 6291464 | tf_op jit(solution)/shard_map/ppermute | solution.py:106
  50.1 9.7 %collective-permute-start.8 = (bf16[2,256,256]{2,1,0:T(8,128)(2,1)S(1)}, bf16[2,256,256]{2,1,0:T(8,128)(2,1)S(1)}, u32[]{:S(2)}, u32[]{:S(2)}) collective-permute-start(bf16[2,256,256]{2,1,0:T(8,128)(2,1)S(1)} %shard_map.49), channel_id=1, source_target_pairs={{0,4},{1,5},{2,6},{3,7},{4,0},{5,1},{6,2},{7,3},{8,12},{9,13},{10,... | collective-permute-start | bytes 786440 | tf_op jit(solution)/shard_map/ppermute | solution.py:106
  51.8 14.8 %collective-permute-start.5 = (bf16[4,1,256,256]{3,2,1,0:T(8,128)(2,1)S(1)}, bf16[4,1,256,256]{3,2,1,0:T(8,128)(2,1)S(1)}, u32[]{:S(2)}, u32[]{:S(2)}) collective-permute-start(bf16[4,1,256,256]{3,2,1,0:T(8,128)(2,1)S(1)} %get-tuple-element.25), channel_id=1, source_target_pairs={{0,2},{1,3},{2,0},{3,1},{4,6},{5,7},{6,4},{7,5},{8,10},{9,11},{10,... | collective-permute-start | bytes 1572872 | tf_op jit(solution)/shard_map/ppermute | solution.py:106
  59.8 17.2 %collective-permute-start.9 = (bf16[4,1,256,256]{3,2,1,0:T(8,128)(2,1)S(1)}, bf16[4,1,256,256]{3,2,1,0:T(8,128)(2,1)S(1)}, u32[]{:S(2)}, u32[]{:S(2)}) collective-permute-start(bf16[4,1,256,256]{3,2,1,0:T(8,128)(2,1)S(1)} %get-tuple-element.31), channel_id=1, source_target_pairs={{0,2},{1,3},{2,0},{3,1},{4,6},{5,7},{6,4},{7,5},{8,10},{9,11},{10,... | collective-permute-start | bytes 1572872 | tf_op jit(solution)/shard_map/ppermute | solution.py:106
  60.4 12.0 %collective-permute-start.10 = (bf16[2,256,256]{2,1,0:T(8,128)(2,1)S(1)}, bf16[2,256,256]{2,1,0:T(8,128)(2,1)S(1)}, u32[]{:S(2)}, u32[]{:S(2)}) collective-permute-start(bf16[2,256,256]{2,1,0:T(8,128)(2,1)S(1)} %shard_map.48), channel_id=1, source_target_pairs={{0,8},{1,9},{2,10},{3,11},{4,12},{5,13},{6,14},{7,15},{8,0},{9,1},... | collective-permute-start | bytes 786440 | tf_op jit(solution)/shard_map/ppermute | solution.py:106
  62.4 36.7 %collective-permute-start.16 = (bf16[8,1,256,256]{3,2,1,0:T(8,128)(2,1)S(1)}, bf16[8,1,256,256]{3,2,1,0:T(8,128)(2,1)S(1)}, u32[]{:S(2)}, u32[]{:S(2)}) collective-permute-start(bf16[8,1,256,256]{3,2,1,0:T(8,128)(2,1)S(1)} %collective-permute-done.7.refs_5_.refs_7_), channel_id=1, source_target_pairs={{4,0},{5,1},{6,2},{7,3},{8,12},{9,13},{10,14},{11,15},{20,16},{21,... | collective-permute-start | bytes 3145736 | tf_op jit(solution)/shard_map/ppermute | solution.py:106
  77.1 1.9 %collective-permute-start.11 = (bf16[4,1,256,256]{3,2,1,0:T(8,128)(2,1)S(1)}, bf16[4,1,256,256]{3,2,1,0:T(8,128)(2,1)S(1)}, u32[]{:S(2)}, u32[]{:S(2)}) collective-permute-start(bf16[4,1,256,256]{3,2,1,0:T(8,128)(2,1)S(1)} %collective-permute-done.5.refs_0_), channel_id=1, source_target_pairs={{0,1},{1,0},{2,3},{3,2},{4,5},{5,4},{6,7},{7,6},{8,9},{9,8},{10,11... | collective-permute-start | bytes 1572872 | tf_op jit(solution)/shard_map/ppermute | solution.py:106
  77.1 2.7 %collective-permute-start.12 = (bf16[4,1,256,256]{3,2,1,0:T(8,128)(2,1)S(1)}, bf16[4,1,256,256]{3,2,1,0:T(8,128)(2,1)S(1)}, u32[]{:S(2)}, u32[]{:S(2)}) collective-permute-start(bf16[4,1,256,256]{3,2,1,0:T(8,128)(2,1)S(1)} %collective-permute-done.9.refs_1_), channel_id=1, source_target_pairs={{0,1},{1,0},{2,3},{3,2},{4,5},{5,4},{6,7},{7,6},{8,9},{9,8},{10,11... | collective-permute-start | bytes 1572872 | tf_op jit(solution)/shard_map/ppermute | solution.py:106
  81.7 23.5 %collective-permute-start.15 = (bf16[2,256,256]{2,1,0:T(8,128)(2,1)S(1)}, bf16[2,256,256]{2,1,0:T(8,128)(2,1)S(1)}, u32[]{:S(2)}, u32[]{:S(2)}) collective-permute-start(bf16[2,256,256]{2,1,0:T(8,128)(2,1)S(1)} %shard_map.51), channel_id=1, source_target_pairs={{0,8},{1,9},{2,10},{3,11},{4,12},{5,13},{6,14},{7,15},{8,0},{9,1},... | collective-permute-start | bytes 786440 | tf_op jit(solution)/shard_map/ppermute | solution.py:106
  83.9 18.0 %copy-start.1 = (bf16[1,16,256,256]{3,2,1,0:T(8,128)(2,1)S(1)}, bf16[1,16,256,256]{3,2,1,0:T(8,128)(2,1)}, u32[]{:S(2)}) copy-start(bf16[1,16,256,256]{3,2,1,0:T(8,128)(2,1)} %refs_2_.7) | copy-start | bytes 6291460
  83.9 18.0 %copy-start.3 = (bf16[8,1,256,256]{3,2,1,0:T(8,128)(2,1)S(1)}, bf16[8,1,256,256]{3,2,1,0:T(8,128)(2,1)}, u32[]{:S(2)}) copy-start(bf16[8,1,256,256]{3,2,1,0:T(8,128)(2,1)} %refs_0_.7) | copy-start | bytes 3145732
  84.0 30.4 %collective-permute-start.14 = (bf16[2,256,256]{2,1,0:T(8,128)(2,1)S(1)}, bf16[2,256,256]{2,1,0:T(8,128)(2,1)S(1)}, u32[]{:S(2)}, u32[]{:S(2)}) collective-permute-start(bf16[2,256,256]{2,1,0:T(8,128)(2,1)S(1)} %shard_map.50), channel_id=1, source_target_pairs={{0,4},{1,5},{2,6},{3,7},{4,0},{5,1},{6,2},{7,3},{8,12},{9,13},{10,... | collective-permute-start | bytes 786440 | tf_op jit(solution)/shard_map/ppermute | solution.py:106
  101.1 13.3 %copy-start.5 = (bf16[8,1,256,256]{3,2,1,0:T(8,128)(2,1)S(1)}, bf16[8,1,256,256]{3,2,1,0:T(8,128)(2,1)}, u32[]{:S(2)}) copy-start(bf16[8,1,256,256]{3,2,1,0:T(8,128)(2,1)} %refs_6_) | copy-start | bytes 3145732
  101.1 19.1 %collective-permute-start.18 = (bf16[2,256,256]{2,1,0:T(8,128)(2,1)S(1)}, bf16[2,256,256]{2,1,0:T(8,128)(2,1)S(1)}, u32[]{:S(2)}, u32[]{:S(2)}) collective-permute-start(bf16[2,256,256]{2,1,0:T(8,128)(2,1)S(1)} %shard_map.54), channel_id=1, source_target_pairs={{0,12},{1,13},{2,14},{3,15},{4,8},{5,9},{6,10},{7,11},{8,4},{9,5},... | collective-permute-start | bytes 786440 | tf_op jit(solution)/shard_map/ppermute | solution.py:106
  103.9 19.1 %collective-permute-start.17 = (bf16[2,256,256]{2,1,0:T(8,128)(2,1)S(1)}, bf16[2,256,256]{2,1,0:T(8,128)(2,1)S(1)}, u32[]{:S(2)}, u32[]{:S(2)}) collective-permute-start(bf16[2,256,256]{2,1,0:T(8,128)(2,1)S(1)} %shard_map.53), channel_id=1, source_target_pairs={{0,12},{1,13},{2,14},{3,15},{4,8},{5,9},{6,10},{7,11},{8,4},{9,5},... | collective-permute-start | bytes 786440 | tf_op jit(solution)/shard_map/ppermute | solution.py:106

commit v6 on v5

v6 whole, which is shorter than its diff:
```python
import functools

import jax
import jax.numpy as jnp
from jax import lax
from jax.experimental import pallas as pl
from jax.experimental.pallas import tpu as pltpu
from jax.sharding import PartitionSpec as P

HBM = pl.BlockSpec(memory_space=pltpu.HBM)
SMEM = pl.BlockSpec(memory_space=pltpu.SMEM)
VMEM = pl.BlockSpec(memory_space=pltpu.VMEM)


def slot_kernel(step, parts, choices, source, *refs):
    count = len(parts)
    lefts, refs = refs[:count], refs[count:]
    psis = []
    for number in parts:
        psis.append(refs[:number])
        refs = refs[number:]
    rights = refs[:choices]
    out, right_buf, mid_buf = refs[choices:]
    terms, _, rows, columns = rights[0].shape
    me = lax.axis_index("sec")
    row = me >> 2
    q = me ^ (4 * step)
    outer = (row == 0) | (row == 3)

    def psi_block(held, sector):
        block, first = None, 0
        for part in held:
            size = part.shape[1]
            if block is None:
                block = part[0, jnp.minimum(sector, size - 1)]
            else:
                block = jnp.where(sector >= first, part[0, jnp.maximum(sector - first, 0)], block)
            first += size
        return block

    for k in range(terms):
        span = pl.ds(k * columns, columns)
        right = rights[0][k, 0]
        if choices > 1:
            right = jnp.where(outer, right, rights[1][k, 0])
        right_buf[:, span] = right
        for i in range(count):
            mid = jnp.dot(lefts[i][k, 0], psi_block(psis[i], source[k, q]), preferred_element_type=jnp.float32)
            mid_buf[pl.ds(i * rows, rows), span] = mid.astype(jnp.bfloat16)
    total = lax.dot_general(
        mid_buf[...], right_buf[...], (((1,), (1,)), ((), ())), preferred_element_type=jnp.float32
    )
    out[...] = total.reshape(out.shape).astype(out.dtype)


def slot(step, source_map, lefts, psis, rights, dtype, flops):
    terms, _, rows, columns = rights[0].shape
    count = len(psis)
    parts = tuple(len(psi) for psi in psis)
    return pl.pallas_call(
        functools.partial(slot_kernel, step, parts, len(rights)),
        out_shape=jax.ShapeDtypeStruct((count, rows, columns), dtype),
        in_specs=[SMEM] + [VMEM] * (count + sum(parts) + len(rights)),
        out_specs=VMEM,
        scratch_shapes=[
            pltpu.VMEM((rows, terms * columns), jnp.bfloat16),
            pltpu.VMEM((count * rows, terms * columns), jnp.bfloat16),
        ],
        compiler_params=pltpu.CompilerParams(vmem_limit_bytes=24 << 20),
        cost_estimate=pl.CostEstimate(flops=flops, bytes_accessed=1, transcendentals=0),
    )(source_map, *lefts, *[part for psi in psis for part in psi], *rights)


def split_kernel(whole, low, high):
    first = low.shape[1]
    low[...] = whole[:, :first]
    high[...] = whole[:, first:]


def split(array, first):
    sizes = (first, array.shape[1] - first)
    return pl.pallas_call(
        split_kernel,
        out_shape=tuple(
            jax.ShapeDtypeStruct((array.shape[0], size) + array.shape[2:], array.dtype) for size in sizes
        ),
        in_specs=[VMEM],
        out_specs=(VMEM, VMEM),
        compiler_params=pltpu.CompilerParams(vmem_limit_bytes=12 << 20),
        cost_estimate=pl.CostEstimate(flops=1, bytes_accessed=1, transcendentals=0),
    )(array)


def place_kernel(*refs):
    pieces, out, sem = refs[:-2], refs[-2], refs[-1]
    me = lax.axis_index("sec")
    blocks = [piece.at[i] for piece in pieces for i in range(piece.shape[0])]
    copies = [pltpu.make_async_copy(block, out.at[me ^ j], sem.at[j]) for j, block in enumerate(blocks)]
    for copy in copies:
        copy.start()
    for copy in copies:
        copy.wait()


def place(pieces):
    sectors = sum(piece.shape[0] for piece in pieces)
    return pl.pallas_call(
        place_kernel,
        out_shape=jax.ShapeDtypeStruct((sectors,) + pieces[0].shape[1:], pieces[0].dtype),
        in_specs=[VMEM] * len(pieces),
        out_specs=HBM,
        scratch_shapes=[pltpu.SemaphoreType.DMA((sectors,))],
        compiler_params=pltpu.CompilerParams(vmem_limit_bytes=16 << 20),
    )(*pieces)


def exchange(array, bits, members):
    return lax.ppermute(array, "sec", [(s, s ^ bits) for s in members])


def on_device(ops, psi, left_env, right_env, source_map):
    dtype = jnp.bfloat16 if ops == 1 else jnp.float32
    every = range(16)
    inner = range(4, 12)
    low, high = split(psi, 9 * psi.shape[1] // 16)

    def products(step, lefts, psis, rights, flops=1):
        return slot(step, source_map, lefts, psis, rights, dtype, flops)

    near = exchange(right_env, 4, every)
    middle = exchange(right_env, 12, inner)
    x_left = exchange(left_env, 2, every)
    own = ([left_env, exchange(left_env, 1, every)], [(psi,), (exchange(psi, 1, every),)])
    own_0 = products(0, *own, (right_env,))

    near, middle, x_left, own_0, low = lax.optimization_barrier((near, middle, x_left, own_0, low))
    far_in = exchange(near, 12, inner)
    second = exchange(middle, 4, inner)
    x_low = exchange(low, 2, every)
    across_left = exchange(x_left, 1, every)
    own_1 = products(1, *own, (near,))
    sent_1 = exchange(own_1, 4, every)

    third = exchange(far_in, 4, inner)
    sent_1, high = lax.optimization_barrier((sent_1, high))
    x_high = exchange(high, 2, every)
    across_low = exchange(x_low, 1, every)
    own_2 = products(2, *own, (second, far_in))
    sent_2 = exchange(own_2, 8, every)

    x_high, sent_2 = lax.optimization_barrier((x_high, sent_2))
    across_high = exchange(x_high, 1, every)
    other = ([x_left, across_left], [(x_low, x_high), (across_low, across_high)])
    other_2 = products(2, *other, (second, far_in))
    other_sent_2 = exchange(other_2, 8, every)
    other_1 = products(1, *other, (near,))
    other_sent_1 = exchange(other_1, 4, every)

    third, other_1, other_2 = lax.optimization_barrier((third, other_1, other_2))
    last_3 = products(3, own[0] + other[0], own[1] + other[1], (third, middle), flops=10**10)
    sent_3 = exchange(last_3, 12, every)
    right_last, other_sent_1, other_sent_2 = lax.optimization_barrier((right_env, other_sent_1, other_sent_2))
    other_0 = products(0, *other, (right_last,), flops=10**10)

    pieces = [own_0, other_0, sent_1, other_sent_1, sent_2, other_sent_2, sent_3]
    out = place(pieces)[:, None]
    if ops > 1:
        out = lax.psum_scatter(out, "op", scatter_dimension=2, tiled=True).astype(jnp.bfloat16)
    return out


def solution(mesh):
    placed = (
        P(("group", "sec"), None, None, None),
        P(("group", "op"), "sec", None, None),
        P(("group", "op"), "sec", None, None),
        P(("group", "op"), None),
    )
    return jax.shard_map(
        functools.partial(on_device, mesh.shape["op"]),
        mesh=mesh,
        in_specs=placed,
        out_specs=P("group", "sec", "op", None),
        check_vma=False,
    )
```

time: 125 us -> 132 us (1.056)
  the two profiles are of different devices: /device:TPU:20 before, /device:TPU:8 now
where the time goes in v6:
time: 132 us
  waiting for transfers between devices  87.1 us (66%)
  starting transfers between devices  22.5 us (17%)
  Pallas kernels  15.9 us (12%)
  local copies, waits for them, and re-layouts  6.17 us (5%)
    ppermute x18, waiting for transfers between devices, exchange(): return lax.ppermute(array, 'sec', [(s, s ^ bits) for s in members])  87.1 us
    ppermute x18, starting transfers between devices, exchange(): return lax.ppermute(array, 'sec', [(s, s ^ bits) for s in members])  22.5 us
    pallas_call x7, Pallas kernels, slot(): pl.pallas_call(functools.partial(slot_kernel, step, parts, len(rights)),...  14.3 us
    unnamed x14, local copies, waits for them, and re-layouts  6.17 us
  transfers between devices with their start and end apart: 18, of which 9 were waited for; matrix products, arithmetic and copies ran while one was open for 0% of the time, Pallas kernels for 11%

profile of v6, /device:TPU:8, one launch (start us, length us, event | category | flops | bytes accessed | tf_op | source)
XLA Modules:
  0.0 131.7 jit_solution(17573409945689759912)
XLA Ops:
  0.0 0.0 collective-permute-start.4
  0.0 0.5 collective-permute-start.3
  0.5 0.0 collective-permute-start
  0.5 5.0 %collective-permute-start.1 = (bf16[8,1,256,256]{3,2,1,0:T(8,128)(2,1)}, bf16[8,1,256,256]{3,2,1,0:T(8,128)(2,1)S(1)}, u32[]{:S(2)}, u32[]{:S(2)}) collective-permute-start(bf16[8,1,256,256]{3,2,1,0:T(8,128)(2,1)} %refs_6_), channel_id=1, source_target_pairs={{4,8},{5,9},{6,10},{7,11},{8,4},{9,5},{10,6},{11,7},{20,24},{21,25... | collective-permute-start | bytes 3145736 | tf_op jit(solution)/shard_map/ppermute | solution.py:118
  5.6 1.6 %collective-permute-start.2 = (bf16[8,1,256,256]{3,2,1,0:T(8,128)(2,1)}, bf16[8,1,256,256]{3,2,1,0:T(8,128)(2,1)S(1)}, u32[]{:S(2)}, u32[]{:S(2)}) collective-permute-start(bf16[8,1,256,256]{3,2,1,0:T(8,128)(2,1)} %refs_0_.7), channel_id=1, source_target_pairs={{0,2},{1,3},{2,0},{3,1},{4,6},{5,7},{6,4},{7,5},{8,10},{9,11},{10,... | collective-permute-start | bytes 3145736 | tf_op jit(solution)/shard_map/ppermute | solution.py:118
  7.1 1.6 %copy-done = bf16[1,16,256,256]{3,2,1,0:T(8,128)(2,1)S(1)} copy-done((bf16[1,16,256,256]{3,2,1,0:T(8,128)(2,1)S(1)}, bf16[1,16,256,256]{3,2,1,0:T(8,128)(2,1)}, u32[]{:S(2)}) %copy-start) | copy-done | bytes 2097176
  8.7 0.1 shard_map.47
  8.9 0.0 collective-permute-done.3.refs_1_
  8.9 0.0 collective-permute-done.4.refs_3_.refs_5_
  8.9 1.4 %copy-done.1 = bf16[1,16,256,256]{3,2,1,0:T(8,128)(2,1)S(1)} copy-done((bf16[1,16,256,256]{3,2,1,0:T(8,128)(2,1)S(1)}, bf16[1,16,256,256]{3,2,1,0:T(8,128)(2,1)}, u32[]{:S(2)}) %copy-start.1) | copy-done | bytes 2097176
  10.3 1.2 copy-done.2
  11.5 1.2 copy-done.4
  12.8 0.7 copy-done.6
  13.4 1.9 %shard_map.46.refs_0_ = bf16[2,256,256]{2,1,0:T(8,128)(2,1)S(1)} custom-call(s32[8,16]{1,0:T(8,128)S(1)} %copy-done.6, bf16[8,1,256,256]{3,2,1,0:T(8,128)(2,1)S(1)} %copy-done.2, bf16[8,1,256,256]{3,2,1,0:T(8,128)(2,1)S(1)} %collective-permute-done.3.refs_1_, bf16[1,16,256,256]{3,2,1,0:T(8,128)(2,1)S(1)} %copy-done.1, ...), custom_call_target="tpu_custom_call" | custom-call | flops 1 | bytes 1 | tf_op jit(solution)/shard_map/pallas_call | solution.py:60
  15.3 10.5 %collective-permute-done.refs_4_.refs_6_ = bf16[8,1,256,256]{3,2,1,0:T(8,128)(2,1)S(1)} collective-permute-done((bf16[8,1,256,256]{3,2,1,0:T(8,128)(2,1)}, bf16[8,1,256,256]{3,2,1,0:T(8,128)(2,1)S(1)}, u32[]{:S(2)}, u32[]{:S(2)}) %collective-permute-start) | collective-permute-done | bytes 1048608 | tf_op jit(solution)/shard_map/ppermute | solution.py:118
  25.8 3.0 %collective-permute-done.1.refs_11_ = bf16[8,1,256,256]{3,2,1,0:T(8,128)(2,1)S(1)} collective-permute-done((bf16[8,1,256,256]{3,2,1,0:T(8,128)(2,1)}, bf16[8,1,256,256]{3,2,1,0:T(8,128)(2,1)S(1)}, u32[]{:S(2)}, u32[]{:S(2)}) %collective-permute-start.1) | collective-permute-done | bytes 1048608 | tf_op jit(solution)/shard_map/ppermute | solution.py:118
  28.8 1.5 %collective-permute-done.2.refs_0_.refs_2_ = bf16[8,1,256,256]{3,2,1,0:T(8,128)(2,1)S(1)} collective-permute-done((bf16[8,1,256,256]{3,2,1,0:T(8,128)(2,1)}, bf16[8,1,256,256]{3,2,1,0:T(8,128)(2,1)S(1)}, u32[]{:S(2)}, u32[]{:S(2)}) %collective-permute-start.2) | collective-permute-done | bytes 1048608 | tf_op jit(solution)/shard_map/ppermute | solution.py:118
  30.4 1.5 %collective-permute-start.6 = (bf16[1,9,256,256]{3,2,1,0:T(8,128)(2,1)S(1)}, bf16[1,9,256,256]{3,2,1,0:T(8,128)(2,1)S(1)}, u32[]{:S(2)}, u32[]{:S(2)}) collective-permute-start(bf16[1,9,256,256]{3,2,1,0:T(8,128)(2,1)S(1)} %get-tuple-element.23), channel_id=1, source_target_pairs={{0,2},{1,3},{2,0},{3,1},{4,6},{5,7},{6,4},{7,5},{8,10},{9,11},{10,... | collective-permute-start | bytes 3538952 | tf_op jit(solution)/shard_map/ppermute | solution.py:118
  31.8 2.2 %collective-permute-start.10 = (bf16[8,1,256,256]{3,2,1,0:T(8,128)(2,1)S(1)}, bf16[8,1,256,256]{3,2,1,0:T(8,128)(2,1)S(1)}, u32[]{:S(2)}, u32[]{:S(2)}) collective-permute-start(bf16[8,1,256,256]{3,2,1,0:T(8,128)(2,1)S(1)} %collective-permute-done.refs_4_.refs_6_), channel_id=1, source_target_pairs={{4,8},{5,9},{6,10},{7,11},{8,4},{9,5},{10,6},{11,7},{20,24},{21,25... | collective-permute-start | bytes 3145736 | tf_op jit(solution)/shard_map/ppermute | solution.py:118
  34.0 1.4 %collective-permute-start.9 = (bf16[8,1,256,256]{3,2,1,0:T(8,128)(2,1)S(1)}, bf16[8,1,256,256]{3,2,1,0:T(8,128)(2,1)S(1)}, u32[]{:S(2)}, u32[]{:S(2)}) collective-permute-start(bf16[8,1,256,256]{3,2,1,0:T(8,128)(2,1)S(1)} %collective-permute-done.1.refs_11_), channel_id=1, source_target_pairs={{4,0},{5,1},{6,2},{7,3},{8,12},{9,13},{10,14},{11,15},{20,16},{21,... | collective-permute-start | bytes 3145736 | tf_op jit(solution)/shard_map/ppermute | solution.py:118
  35.4 1.9 %shard_map.48 = bf16[2,256,256]{2,1,0:T(8,128)(2,1)S(1)} custom-call(s32[8,16]{1,0:T(8,128)S(1)} %copy-done.6, bf16[8,1,256,256]{3,2,1,0:T(8,128)(2,1)S(1)} %copy-done.2, bf16[8,1,256,256]{3,2,1,0:T(8,128)(2,1)S(1)} %collective-permute-done.3.refs_1_, bf16[1,16,256,256]{3,2,1,0:T(8,128)(2,1)S(1)} %copy-done.1, ...), custom_call_target="tpu_custom_call" | custom-call | flops 1 | bytes 1 | tf_op jit(solution)/shard_map/pallas_call | solution.py:60
  37.3 0.1 collective-permute-start.7
  37.4 24.7 %collective-permute-done.7.refs_2_ = bf16[2,256,256]{2,1,0:T(8,128)(2,1)S(1)} collective-permute-done((bf16[2,256,256]{2,1,0:T(8,128)(2,1)S(1)}, bf16[2,256,256]{2,1,0:T(8,128)(2,1)S(1)}, u32[]{:S(2)}, u32[]{:S(2)}) %collective-permute-start.7) | collective-permute-done | bytes 262176 | tf_op jit(solution)/shard_map/ppermute | solution.py:118
  62.1 0.5 collective-permute-start.8
  62.6 0.0 collective-permute-done.10.refs_5_.refs_7_
  62.6 0.0 collective-permute-done.9.refs_4_.refs_6_
  62.6 1.9 %shard_map.49 = bf16[2,256,256]{2,1,0:T(8,128)(2,1)S(1)} custom-call(s32[8,16]{1,0:T(8,128)S(1)} %copy-done.6, bf16[8,1,256,256]{3,2,1,0:T(8,128)(2,1)S(1)} %copy-done.2, bf16[8,1,256,256]{3,2,1,0:T(8,128)(2,1)S(1)} %collective-permute-done.3.refs_1_, bf16[1,16,256,256]{3,2,1,0:T(8,128)(2,1)S(1)} %copy-done.1, ...), custom_call_target="tpu_custom_call" | custom-call | flops 1 | bytes 1 | tf_op jit(solution)/shard_map/pallas_call | solution.py:60
  64.5 3.4 %collective-permute-start.11 = (bf16[2,256,256]{2,1,0:T(8,128)(2,1)S(1)}, bf16[2,256,256]{2,1,0:T(8,128)(2,1)S(1)}, u32[]{:S(2)}, u32[]{:S(2)}) collective-permute-start(bf16[2,256,256]{2,1,0:T(8,128)(2,1)S(1)} %shard_map.49), channel_id=1, source_target_pairs={{0,8},{1,9},{2,10},{3,11},{4,12},{5,13},{6,14},{7,15},{8,0},{9,1},... | collective-permute-start | bytes 786440 | tf_op jit(solution)/shard_map/ppermute | solution.py:118
  67.9 0.0 collective-permute-done.6.refs_2_.refs_6_
  67.9 0.0 collective-permute-start.12
  67.9 0.5 collective-permute-start.5
  68.5 1.5 %collective-permute-start.16 = (bf16[8,1,256,256]{3,2,1,0:T(8,128)(2,1)S(1)}, bf16[8,1,256,256]{3,2,1,0:T(8,128)(2,1)S(1)}, u32[]{:S(2)}, u32[]{:S(2)}) collective-permute-start(bf16[8,1,256,256]{3,2,1,0:T(8,128)(2,1)S(1)} %collective-permute-done.10.refs_5_.refs_7_), channel_id=1, source_target_pairs={{4,0},{5,1},{6,2},{7,3},{8,12},{9,13},{10,14},{11,15},{20,16},{21,... | collective-permute-start | bytes 3145736 | tf_op jit(solution)/shard_map/ppermute | solution.py:118
  70.0 12.0 %collective-permute-done.8.refs_3_.refs_7_ = bf16[1,7,256,256]{3,2,1,0:T(8,128)(2,1)S(1)} collective-permute-done((bf16[1,7,256,256]{3,2,1,0:T(8,128)(2,1)S(1)}, bf16[1,7,256,256]{3,2,1,0:T(8,128)(2,1)S(1)}, u32[]{:S(2)}, u32[]{:S(2)}) %collective-permute-start.8) | collective-permute-done | bytes 917536 | tf_op jit(solution)/shard_map/ppermute | solution.py:118
  82.0 0.0 collective-permute-done.11.refs_4_
  82.0 2.5 %collective-permute-done.13.refs_5_.refs_9_ = bf16[1,7,256,256]{3,2,1,0:T(8,128)(2,1)S(1)} collective-permute-done((bf16[1,7,256,256]{3,2,1,0:T(8,128)(2,1)S(1)}, bf16[1,7,256,256]{3,2,1,0:T(8,128)(2,1)S(1)}, u32[]{:S(2)}, u32[]{:S(2)}) %collective-permute-start.13) | collective-permute-done | bytes 917536 | tf_op jit(solution)/shard_map/ppermute | solution.py:118
  84.4 1.9 %shard_map.51 = bf16[2,256,256]{2,1,0:T(8,128)(2,1)S(1)} custom-call(s32[8,16]{1,0:T(8,128)S(1)} %copy-done.6, bf16[8,1,256,256]{3,2,1,0:T(8,128)(2,1)S(1)} %collective-permute-done.2.refs_0_.refs_2_, bf16[8,1,256,256]{3,2,1,0:T(8,128)(2,1)S(1)} %collective-permute-done.5.refs_1_.refs_3_, ...), custom_call_target="tpu_custom_call" | custom-call | flops 1 | bytes 1 | tf_op jit(solution)/shard_map/pallas_call | solution.py:60
  86.4 0.0 copy-start.3
  86.4 3.1 %collective-permute-start.15 = (bf16[2,256,256]{2,1,0:T(8,128)(2,1)S(1)}, bf16[2,256,256]{2,1,0:T(8,128)(2,1)S(1)}, u32[]{:S(2)}, u32[]{:S(2)}) collective-permute-start(bf16[2,256,256]{2,1,0:T(8,128)(2,1)S(1)} %shard_map.51), channel_id=1, source_target_pairs={{0,8},{1,9},{2,10},{3,11},{4,12},{5,13},{6,14},{7,15},{8,0},{9,1},... | collective-permute-start | bytes 786440 | tf_op jit(solution)/shard_map/ppermute | solution.py:118
  89.5 1.9 %shard_map.50 = bf16[2,256,256]{2,1,0:T(8,128)(2,1)S(1)} custom-call(s32[8,16]{1,0:T(8,128)S(1)} %copy-done.6, bf16[8,1,256,256]{3,2,1,0:T(8,128)(2,1)S(1)} %collective-permute-done.2.refs_0_.refs_2_, bf16[8,1,256,256]{3,2,1,0:T(8,128)(2,1)S(1)} %collective-permute-done.5.refs_1_.refs_3_, ...), custom_call_target="tpu_custom_call" | custom-call | flops 1 | bytes 1 | tf_op jit(solution)/shard_map/pallas_call | solution.py:60
  91.3 0.0 copy-start.5
  91.3 0.1 collective-permute-start.14
  91.4 12.2 %collective-permute-done.16.refs_10_ = bf16[8,1,256,256]{3,2,1,0:T(8,128)(2,1)S(1)} collective-permute-done((bf16[8,1,256,256]{3,2,1,0:T(8,128)(2,1)S(1)}, bf16[8,1,256,256]{3,2,1,0:T(8,128)(2,1)S(1)}, u32[]{:S(2)}, u32[]{:S(2)}) %collective-permute-start.16) | collective-permute-done | bytes 1048608 | tf_op jit(solution)/shard_map/ppermute | solution.py:118
  103.7 3.0 %shard_map.53 = bf16[4,256,256]{2,1,0:T(8,128)(2,1)S(1)} custom-call(s32[8,16]{1,0:T(8,128)S(1)} %copy-done.6, bf16[8,1,256,256]{3,2,1,0:T(8,128)(2,1)S(1)} %copy-done.3, bf16[8,1,256,256]{3,2,1,0:T(8,128)(2,1)S(1)} %collective-permute-done.3.refs_1_, bf16[8,1,256,256]{3,2,1,0:T(8,128)(2,1)S(1)} %collective-permute-done.2.refs_0_.refs_2_, ...), custom_call_target="tpu_custom_call" | custom-call | flops 10000000000 | bytes 1 | tf_op jit(solution)/shard_map/pallas_call | solution.py:60
  106.7 1.1 collective-permute-start.17
  107.8 0.7 collective-permute-done.14.refs_3_
  108.5 1.9 %shard_map.52.refs_1_ = bf16[2,256,256]{2,1,0:T(8,128)(2,1)S(1)} custom-call(s32[8,16]{1,0:T(8,128)S(1)} %copy-done.6, bf16[8,1,256,256]{3,2,1,0:T(8,128)(2,1)S(1)} %collective-permute-done.2.refs_0_.refs_2_, bf16[8,1,256,256]{3,2,1,0:T(8,128)(2,1)S(1)} %collective-permute-done.5.refs_1_.refs_3_, ...), custom_call_target="tpu_custom_call" | custom-call | flops 10000000000 | bytes 1 | tf_op jit(solution)/shard_map/pallas_call | solution.py:60
  110.4 19.9 %collective-permute-done.17.refs_6_ = bf16[4,256,256]{2,1,0:T(8,128)(2,1)S(1)} collective-permute-done((bf16[4,256,256]{2,1,0:T(8,128)(2,1)S(1)}, bf16[4,256,256]{2,1,0:T(8,128)(2,1)S(1)}, u32[]{:S(2)}, u32[]{:S(2)}) %collective-permute-start.17) | collective-permute-done | bytes 524320 | tf_op jit(solution)/shard_map/ppermute | solution.py:118
  130.3 1.4 %shard_map.54 = bf16[16,256,256]{2,1,0:T(8,128)(2,1)} custom-call(bf16[2,256,256]{2,1,0:T(8,128)(2,1)S(1)} %shard_map.46.refs_0_, bf16[2,256,256]{2,1,0:T(8,128)(2,1)S(1)} %shard_map.52.refs_1_, bf16[2,256,256]{2,1,0:T(8,128)(2,1)S(1)} %collective-permute-done.7.refs_2_, bf16[2,256,256]{2,1,0:T(8,128)(2,1)S(1)} %collective-permute-done.14.refs_3_, ...), custom_call_target="tpu_custom_call" | custom-call | tf_op jit(solution)/shard_map/pallas_call | solution.py:107
  (11 shorter events, 0.0 us)
Async XLA Ops:
  0.0 8.9 %collective-permute-start.4 = (bf16[1,16,256,256]{3,2,1,0:T(8,128)(2,1)}, bf16[1,16,256,256]{3,2,1,0:T(8,128)(2,1)S(1)}, u32[]{:S(2)}, u32[]{:S(2)}) collective-permute-start(bf16[1,16,256,256]{3,2,1,0:T(8,128)(2,1)} %refs_4_.3), channel_id=1, source_target_pairs={{0,1},{1,0},{2,3},{3,2},{4,5},{5,4},{6,7},{7,6},{8,9},{9,8},{10,11... | collective-permute-start | bytes 6291464 | tf_op jit(solution)/shard_map/ppermute | solution.py:118
  0.0 8.9 %collective-permute-start.3 = (bf16[8,1,256,256]{3,2,1,0:T(8,128)(2,1)}, bf16[8,1,256,256]{3,2,1,0:T(8,128)(2,1)S(1)}, u32[]{:S(2)}, u32[]{:S(2)}) collective-permute-start(bf16[8,1,256,256]{3,2,1,0:T(8,128)(2,1)} %refs_0_.7), channel_id=1, source_target_pairs={{0,1},{1,0},{2,3},{3,2},{4,5},{5,4},{6,7},{7,6},{8,9},{9,8},{10,11... | collective-permute-start | bytes 3145736 | tf_op jit(solution)/shard_map/ppermute | solution.py:118
  0.5 25.3 %collective-permute-start = (bf16[8,1,256,256]{3,2,1,0:T(8,128)(2,1)}, bf16[8,1,256,256]{3,2,1,0:T(8,128)(2,1)S(1)}, u32[]{:S(2)}, u32[]{:S(2)}) collective-permute-start(bf16[8,1,256,256]{3,2,1,0:T(8,128)(2,1)} %refs_6_), channel_id=1, source_target_pairs={{0,4},{1,5},{2,6},{3,7},{4,0},{5,1},{6,2},{7,3},{8,12},{9,13},{10,... | collective-permute-start | bytes 3145736 | tf_op jit(solution)/shard_map/ppermute | solution.py:118
  0.5 28.3 %collective-permute-start.1 = (bf16[8,1,256,256]{3,2,1,0:T(8,128)(2,1)}, bf16[8,1,256,256]{3,2,1,0:T(8,128)(2,1)S(1)}, u32[]{:S(2)}, u32[]{:S(2)}) collective-permute-start(bf16[8,1,256,256]{3,2,1,0:T(8,128)(2,1)} %refs_6_), channel_id=1, source_target_pairs={{4,8},{5,9},{6,10},{7,11},{8,4},{9,5},{10,6},{11,7},{20,24},{21,25... | collective-permute-start | bytes 3145736 | tf_op jit(solution)/shard_map/ppermute | solution.py:118
  5.6 24.8 %collective-permute-start.2 = (bf16[8,1,256,256]{3,2,1,0:T(8,128)(2,1)}, bf16[8,1,256,256]{3,2,1,0:T(8,128)(2,1)S(1)}, u32[]{:S(2)}, u32[]{:S(2)}) collective-permute-start(bf16[8,1,256,256]{3,2,1,0:T(8,128)(2,1)} %refs_0_.7), channel_id=1, source_target_pairs={{0,2},{1,3},{2,0},{3,1},{4,6},{5,7},{6,4},{7,5},{8,10},{9,11},{10,... | collective-permute-start | bytes 3145736 | tf_op jit(solution)/shard_map/ppermute | solution.py:118
  7.1 1.6 %copy-start = (bf16[1,16,256,256]{3,2,1,0:T(8,128)(2,1)S(1)}, bf16[1,16,256,256]{3,2,1,0:T(8,128)(2,1)}, u32[]{:S(2)}) copy-start(bf16[1,16,256,256]{3,2,1,0:T(8,128)(2,1)} %refs_4_.3) | copy-start | bytes 6291460
  8.7 1.6 %copy-start.1 = (bf16[1,16,256,256]{3,2,1,0:T(8,128)(2,1)S(1)}, bf16[1,16,256,256]{3,2,1,0:T(8,128)(2,1)}, u32[]{:S(2)}) copy-start(bf16[1,16,256,256]{3,2,1,0:T(8,128)(2,1)} %refs_4_.3) | copy-start | bytes 6291460
  10.3 1.2 copy-start.2
  11.5 1.2 copy-start.4
  12.8 0.7 copy-start.6
  30.4 37.6 %collective-permute-start.6 = (bf16[1,9,256,256]{3,2,1,0:T(8,128)(2,1)S(1)}, bf16[1,9,256,256]{3,2,1,0:T(8,128)(2,1)S(1)}, u32[]{:S(2)}, u32[]{:S(2)}) collective-permute-start(bf16[1,9,256,256]{3,2,1,0:T(8,128)(2,1)S(1)} %get-tuple-element.23), channel_id=1, source_target_pairs={{0,2},{1,3},{2,0},{3,1},{4,6},{5,7},{6,4},{7,5},{8,10},{9,11},{10,... | collective-permute-start | bytes 3538952 | tf_op jit(solution)/shard_map/ppermute | solution.py:118
  31.8 30.8 %collective-permute-start.10 = (bf16[8,1,256,256]{3,2,1,0:T(8,128)(2,1)S(1)}, bf16[8,1,256,256]{3,2,1,0:T(8,128)(2,1)S(1)}, u32[]{:S(2)}, u32[]{:S(2)}) collective-permute-start(bf16[8,1,256,256]{3,2,1,0:T(8,128)(2,1)S(1)} %collective-permute-done.refs_4_.refs_6_), channel_id=1, source_target_pairs={{4,8},{5,9},{6,10},{7,11},{8,4},{9,5},{10,6},{11,7},{20,24},{21,25... | collective-permute-start | bytes 3145736 | tf_op jit(solution)/shard_map/ppermute | solution.py:118
  34.0 28.6 %collective-permute-start.9 = (bf16[8,1,256,256]{3,2,1,0:T(8,128)(2,1)S(1)}, bf16[8,1,256,256]{3,2,1,0:T(8,128)(2,1)S(1)}, u32[]{:S(2)}, u32[]{:S(2)}) collective-permute-start(bf16[8,1,256,256]{3,2,1,0:T(8,128)(2,1)S(1)} %collective-permute-done.1.refs_11_), channel_id=1, source_target_pairs={{4,0},{5,1},{6,2},{7,3},{8,12},{9,13},{10,14},{11,15},{20,16},{21,... | collective-permute-start | bytes 3145736 | tf_op jit(solution)/shard_map/ppermute | solution.py:118
  37.3 24.8 %collective-permute-start.7 = (bf16[2,256,256]{2,1,0:T(8,128)(2,1)S(1)}, bf16[2,256,256]{2,1,0:T(8,128)(2,1)S(1)}, u32[]{:S(2)}, u32[]{:S(2)}) collective-permute-start(bf16[2,256,256]{2,1,0:T(8,128)(2,1)S(1)} %shard_map.48), channel_id=1, source_target_pairs={{0,4},{1,5},{2,6},{3,7},{4,0},{5,1},{6,2},{7,3},{8,12},{9,13},{10,... | collective-permute-start | bytes 786440 | tf_op jit(solution)/shard_map/ppermute | solution.py:118
  62.1 19.9 %collective-permute-start.8 = (bf16[1,7,256,256]{3,2,1,0:T(8,128)(2,1)S(1)}, bf16[1,7,256,256]{3,2,1,0:T(8,128)(2,1)S(1)}, u32[]{:S(2)}, u32[]{:S(2)}) collective-permute-start(bf16[1,7,256,256]{3,2,1,0:T(8,128)(2,1)S(1)} %get-tuple-element.26), channel_id=1, source_target_pairs={{0,2},{1,3},{2,0},{3,1},{4,6},{5,7},{6,4},{7,5},{8,10},{9,11},{10,... | collective-permute-start | bytes 2752520 | tf_op jit(solution)/shard_map/ppermute | solution.py:118
  64.5 17.4 %collective-permute-start.11 = (bf16[2,256,256]{2,1,0:T(8,128)(2,1)S(1)}, bf16[2,256,256]{2,1,0:T(8,128)(2,1)S(1)}, u32[]{:S(2)}, u32[]{:S(2)}) collective-permute-start(bf16[2,256,256]{2,1,0:T(8,128)(2,1)S(1)} %shard_map.49), channel_id=1, source_target_pairs={{0,8},{1,9},{2,10},{3,11},{4,12},{5,13},{6,14},{7,15},{8,0},{9,1},... | collective-permute-start | bytes 786440 | tf_op jit(solution)/shard_map/ppermute | solution.py:118
  67.9 16.5 %collective-permute-start.12 = (bf16[1,9,256,256]{3,2,1,0:T(8,128)(2,1)S(1)}, bf16[1,9,256,256]{3,2,1,0:T(8,128)(2,1)S(1)}, u32[]{:S(2)}, u32[]{:S(2)}) collective-permute-start(bf16[1,9,256,256]{3,2,1,0:T(8,128)(2,1)S(1)} %collective-permute-done.6.refs_2_.refs_6_), channel_id=1, source_target_pairs={{0,1},{1,0},{2,3},{3,2},{4,5},{5,4},{6,7},{7,6},{8,9},{9,8},{10,11... | collective-permute-start | bytes 3538952 | tf_op jit(solution)/shard_map/ppermute | solution.py:118
  67.9 14.0 %collective-permute-start.5 = (bf16[8,1,256,256]{3,2,1,0:T(8,128)(2,1)S(1)}, bf16[8,1,256,256]{3,2,1,0:T(8,128)(2,1)S(1)}, u32[]{:S(2)}, u32[]{:S(2)}) collective-permute-start(bf16[8,1,256,256]{3,2,1,0:T(8,128)(2,1)S(1)} %collective-permute-done.2.refs_0_.refs_2_), channel_id=1, source_target_pairs={{0,1},{1,0},{2,3},{3,2},{4,5},{5,4},{6,7},{7,6},{8,9},{9,8},{10,11... | collective-permute-start | bytes 3145736 | tf_op jit(solution)/shard_map/ppermute | solution.py:118
  68.5 35.2 %collective-permute-start.16 = (bf16[8,1,256,256]{3,2,1,0:T(8,128)(2,1)S(1)}, bf16[8,1,256,256]{3,2,1,0:T(8,128)(2,1)S(1)}, u32[]{:S(2)}, u32[]{:S(2)}) collective-permute-start(bf16[8,1,256,256]{3,2,1,0:T(8,128)(2,1)S(1)} %collective-permute-done.10.refs_5_.refs_7_), channel_id=1, source_target_pairs={{4,0},{5,1},{6,2},{7,3},{8,12},{9,13},{10,14},{11,15},{20,16},{21,... | collective-permute-start | bytes 3145736 | tf_op jit(solution)/shard_map/ppermute | solution.py:118
  82.0 2.5 %collective-permute-start.13 = (bf16[1,7,256,256]{3,2,1,0:T(8,128)(2,1)S(1)}, bf16[1,7,256,256]{3,2,1,0:T(8,128)(2,1)S(1)}, u32[]{:S(2)}, u32[]{:S(2)}) collective-permute-start(bf16[1,7,256,256]{3,2,1,0:T(8,128)(2,1)S(1)} %collective-permute-done.8.refs_3_.refs_7_), channel_id=1, source_target_pairs={{0,1},{1,0},{2,3},{3,2},{4,5},{5,4},{6,7},{7,6},{8,9},{9,8},{10,11... | collective-permute-start | bytes 2752520 | tf_op jit(solution)/shard_map/ppermute | solution.py:118
  86.4 17.3 %copy-start.3 = (bf16[8,1,256,256]{3,2,1,0:T(8,128)(2,1)S(1)}, bf16[8,1,256,256]{3,2,1,0:T(8,128)(2,1)}, u32[]{:S(2)}) copy-start(bf16[8,1,256,256]{3,2,1,0:T(8,128)(2,1)} %refs_0_.7) | copy-start | bytes 3145732
  86.4 21.4 %collective-permute-start.15 = (bf16[2,256,256]{2,1,0:T(8,128)(2,1)S(1)}, bf16[2,256,256]{2,1,0:T(8,128)(2,1)S(1)}, u32[]{:S(2)}, u32[]{:S(2)}) collective-permute-start(bf16[2,256,256]{2,1,0:T(8,128)(2,1)S(1)} %shard_map.51), channel_id=1, source_target_pairs={{0,8},{1,9},{2,10},{3,11},{4,12},{5,13},{6,14},{7,15},{8,0},{9,1},... | collective-permute-start | bytes 786440 | tf_op jit(solution)/shard_map/ppermute | solution.py:118
  91.3 17.2 %copy-start.5 = (bf16[8,1,256,256]{3,2,1,0:T(8,128)(2,1)S(1)}, bf16[8,1,256,256]{3,2,1,0:T(8,128)(2,1)}, u32[]{:S(2)}) copy-start(bf16[8,1,256,256]{3,2,1,0:T(8,128)(2,1)} %refs_6_) | copy-start | bytes 3145732
  91.3 17.1 %collective-permute-start.14 = (bf16[2,256,256]{2,1,0:T(8,128)(2,1)S(1)}, bf16[2,256,256]{2,1,0:T(8,128)(2,1)S(1)}, u32[]{:S(2)}, u32[]{:S(2)}) collective-permute-start(bf16[2,256,256]{2,1,0:T(8,128)(2,1)S(1)} %shard_map.50), channel_id=1, source_target_pairs={{0,4},{1,5},{2,6},{3,7},{4,0},{5,1},{6,2},{7,3},{8,12},{9,13},{10,... | collective-permute-start | bytes 786440 | tf_op jit(solution)/shard_map/ppermute | solution.py:118
  106.7 23.6 %collective-permute-start.17 = (bf16[4,256,256]{2,1,0:T(8,128)(2,1)S(1)}, bf16[4,256,256]{2,1,0:T(8,128)(2,1)S(1)}, u32[]{:S(2)}, u32[]{:S(2)}) collective-permute-start(bf16[4,256,256]{2,1,0:T(8,128)(2,1)S(1)} %shard_map.53), channel_id=1, source_target_pairs={{0,12},{1,13},{2,14},{3,15},{4,8},{5,9},{6,10},{7,11},{8,4},{9,5},... | collective-permute-start | bytes 1572872 | tf_op jit(solution)/shard_map/ppermute | solution.py:118

commit v7 on v6

v7 whole, which is shorter than its diff:
```python
import functools

import jax
import jax.numpy as jnp
from jax import lax
from jax.experimental import pallas as pl
from jax.experimental.pallas import tpu as pltpu
from jax.sharding import PartitionSpec as P

HBM = pl.BlockSpec(memory_space=pltpu.HBM)
SMEM = pl.BlockSpec(memory_space=pltpu.SMEM)
VMEM = pl.BlockSpec(memory_space=pltpu.VMEM)


def slot_kernel(step, parts, choices, source, *refs):
    count = len(parts)
    lefts, psis = [], []
    for number, _ in parts:
        lefts.append(refs[:number])
        refs = refs[number:]
    for _, number in parts:
        psis.append(refs[:number])
        refs = refs[number:]
    rights = refs[:choices]
    out, right_buf, mid_buf = refs[choices:]
    terms, _, rows, columns = rights[0].shape
    me = lax.axis_index("sec")
    row = me >> 2
    q = me ^ (4 * step)
    outer = (row == 0) | (row == 3)

    def psi_block(held, sector):
        if len(held) == 1:
            return held[0][0, sector]
        low, high = held
        size = low.shape[1]
        return jnp.where(
            sector < size, low[0, jnp.minimum(sector, size - 1)], high[0, jnp.maximum(sector - size, 0)]
        )

    for k in range(terms):
        span = pl.ds(k * columns, columns)
        right = rights[0][k, 0]
        if choices > 1:
            right = jnp.where(outer, right, rights[1][k, 0])
        right_buf[:, span] = right
        for i in range(count):
            part, place = divmod(k, terms // len(lefts[i]))
            mid = jnp.dot(lefts[i][part][place, 0], psi_block(psis[i], source[k, q]), preferred_element_type=jnp.float32)
            mid_buf[pl.ds(i * rows, rows), span] = mid.astype(jnp.bfloat16)
    total = lax.dot_general(
        mid_buf[...], right_buf[...], (((1,), (1,)), ((), ())), preferred_element_type=jnp.float32
    )
    out[...] = total.reshape(out.shape).astype(out.dtype)


def slot(step, source_map, lefts, psis, rights, dtype, flops):
    terms, _, rows, columns = rights[0].shape
    count = len(psis)
    parts = tuple((len(left), len(psi)) for left, psi in zip(lefts, psis))
    held = [part for left in lefts for part in left] + [part for psi in psis for part in psi] + list(rights)
    return pl.pallas_call(
        functools.partial(slot_kernel, step, parts, len(rights)),
        out_shape=jax.ShapeDtypeStruct((count, rows, columns), dtype),
        in_specs=[SMEM] + [VMEM] * len(held),
        out_specs=VMEM,
        scratch_shapes=[
            pltpu.VMEM((rows, terms * columns), jnp.bfloat16),
            pltpu.VMEM((count * rows, terms * columns), jnp.bfloat16),
        ],
        compiler_params=pltpu.CompilerParams(vmem_limit_bytes=24 << 20),
        cost_estimate=pl.CostEstimate(flops=flops, bytes_accessed=1, transcendentals=0),
    )(source_map, *held)


def split_kernel(axis, whole, low, high):
    half = low.shape[axis]
    before = (slice(None),) * axis
    low[...] = whole[(*before, slice(0, half))]
    high[...] = whole[(*before, slice(half, None))]


def split(array, axis):
    shape = list(array.shape)
    shape[axis] //= 2
    half = jax.ShapeDtypeStruct(tuple(shape), array.dtype)
    return pl.pallas_call(
        functools.partial(split_kernel, axis),
        out_shape=(half, half),
        in_specs=[VMEM],
        out_specs=(VMEM, VMEM),
        compiler_params=pltpu.CompilerParams(vmem_limit_bytes=12 << 20),
        cost_estimate=pl.CostEstimate(flops=1, bytes_accessed=1, transcendentals=0),
    )(array)


def place_kernel(*refs):
    pieces, out, sem = refs[:-2], refs[-2], refs[-1]
    me = lax.axis_index("sec")
    row = me >> 2
    outer = (row == 0) | (row == 3)

    def copies(pieces, first):
        blocks = [piece.at[i] for piece in pieces for i in range(piece.shape[0])]
        return [
            pltpu.make_async_copy(block, out.at[me ^ (j ^ 2)], sem.at[j]) for j, block in enumerate(blocks, first)
        ]

    last = out.shape[0] - pieces[-1].shape[0]
    shared = copies(pieces[:-2], 0)
    for copy in shared:
        copy.start()

    @pl.when(outer)
    def _():
        for copy in copies(pieces[-2:-1], last):
            copy.start()

    @pl.when(jnp.logical_not(outer))
    def _():
        for copy in copies(pieces[-1:], last):
            copy.start()

    for copy in shared + copies(pieces[-1:], last):
        copy.wait()


def place(pieces):
    sectors = sum(piece.shape[0] for piece in pieces[:-1])
    return pl.pallas_call(
        place_kernel,
        out_shape=jax.ShapeDtypeStruct((sectors,) + pieces[0].shape[1:], pieces[0].dtype),
        in_specs=[VMEM] * len(pieces),
        out_specs=HBM,
        scratch_shapes=[pltpu.SemaphoreType.DMA((sectors,))],
        compiler_params=pltpu.CompilerParams(vmem_limit_bytes=16 << 20),
    )(*pieces)


def exchange(array, bits, members):
    return lax.ppermute(array, "sec", [(s, s ^ bits) for s in members])


def on_device(ops, psi, left_env, right_env, source_map):
    dtype = jnp.bfloat16 if ops == 1 else jnp.float32
    every = range(16)
    inner = range(4, 12)
    outer = [s for s in every if s not in inner]

    def products(step, lefts, psis, rights, flops=1):
        return slot(step, source_map, lefts, psis, rights, dtype, flops)

    near = exchange(right_env, 4, every)
    middle = exchange(right_env, 12, inner)
    x_psi = exchange(psi, 2, every)
    own = ([(left_env,), (exchange(left_env, 1, every),)], [(psi,), (exchange(psi, 1, every),)])
    own_0 = products(0, *own, (right_env,))

    near, middle, own_0 = lax.optimization_barrier((near, middle, own_0))
    far_in = exchange(near, 12, inner)
    second = exchange(middle, 4, inner)
    own_1 = products(1, *own, (near,))
    sent_1 = exchange(own_1, 4, every)

    x_psi, left_next = lax.optimization_barrier((x_psi, left_env))
    x_left = exchange(left_next, 2, every)
    across_psi = [exchange(part, 1, every) for part in split(x_psi, 1)]

    second, far_in = lax.optimization_barrier((second, far_in))
    third = exchange(far_in, 4, inner)
    second, *across_psi = lax.optimization_barrier((second, *across_psi))
    own_2 = products(2, *own, (second, far_in))
    sent_2 = exchange(own_2, 8, every)
    own_middle = products(3, *own, (middle,))
    sent_middle = exchange(own_middle, 12, inner)

    x_left, sent_1, sent_2 = lax.optimization_barrier((x_left, sent_1, sent_2))
    across_left = [exchange(part, 1, every) for part in split(x_left, 0)]
    other = ([(x_left,), across_left], [(x_psi,), across_psi])
    other_2 = products(2, *other, (second, far_in))
    other_sent_2 = exchange(other_2, 8, every)
    near, sent_middle, other_2 = lax.optimization_barrier((near, sent_middle, other_2))
    other_1 = products(1, *other, (near,))
    other_sent_1 = exchange(other_1, 4, every)

    third, other_1, other_2 = lax.optimization_barrier((third, other_1, other_2))
    other_3 = products(3, *other, (third, middle), flops=10**10)
    other_sent_3 = exchange(other_3, 12, every)
    third, other_3 = lax.optimization_barrier((third, other_3))
    own_third = products(3, *own, (third,))
    sent_third = exchange(own_third, 12, outer)
    right_last, other_sent_1, other_sent_2 = lax.optimization_barrier((right_env, other_sent_1, other_sent_2))
    other_0 = products(0, *other, (right_last,), flops=10**10)

    pieces = [other_0, own_0, other_sent_1, sent_1, other_sent_2, sent_2, other_sent_3, sent_third, sent_middle]
    out = place(pieces)[:, None]
    if ops > 1:
        out = lax.psum_scatter(out, "op", scatter_dimension=2, tiled=True).astype(jnp.bfloat16)
    return out


def solution(mesh):
    placed = (
        P(("group", "sec"), None, None, None),
        P(("group", "op"), "sec", None, None),
        P(("group", "op"), "sec", None, None),
        P(("group", "op"), None),
    )
    return jax.shard_map(
        functools.partial(on_device, mesh.shape["op"]),
        mesh=mesh,
        in_specs=placed,
        out_specs=P("group", "sec", "op", None),
        check_vma=False,
    )
```

time: 132 us -> 140 us (1.061)
  the two profiles are of different devices: /device:TPU:8 before, /device:TPU:0 now
where the time goes in v7:
time: 140 us; the launch traced here: 139 us
  waiting for transfers between devices  77.1 us (55%)
  starting transfers between devices  36.5 us (26%)
  Pallas kernels  21.9 us (16%)
  local copies, waits for them, and re-layouts  3.51 us (3%)
    ppermute x20, waiting for transfers between devices, exchange(): return lax.ppermute(array, 'sec', [(s, s ^ bits) for s in members])  77.1 us
    ppermute x20, starting transfers between devices, exchange(): return lax.ppermute(array, 'sec', [(s, s ^ bits) for s in members])  36.5 us
    pallas_call x9, Pallas kernels, slot(): pl.pallas_call(functools.partial(slot_kernel, step, parts, len(rights)),...  20.2 us
    unnamed x10, local copies, waits for them, and re-layouts  3.51 us
  transfers between devices with their start and end apart: 20, of which 6 were waited for; matrix products, arithmetic and copies ran while one was open for 0% of the time, Pallas kernels for 15%

profile of v7, /device:TPU:0, one launch (start us, length us, event | category | flops | bytes accessed | tf_op | source)
XLA Modules:
  0.0 139.3 jit_solution(14472366505115394754)
XLA Ops:
  0.0 0.5 collective-permute-start.3
  0.5 2.5 %collective-permute-start = (bf16[1,16,256,256]{3,2,1,0:T(8,128)(2,1)}, bf16[1,16,256,256]{3,2,1,0:T(8,128)(2,1)S(1)}, u32[]{:S(2)}, u32[]{:S(2)}) collective-permute-start(bf16[1,16,256,256]{3,2,1,0:T(8,128)(2,1)} %refs_2_.9), channel_id=1, source_target_pairs={{0,2},{1,3},{2,0},{3,1},{4,6},{5,7},{6,4},{7,5},{8,10},{9,11},{10,... | collective-permute-start | bytes 6291464 | tf_op jit(solution)/shard_map/ppermute | solution.py:141
  2.9 0.2 collective-permute-start.2
  3.2 1.6 %collective-permute-start.4 = (bf16[8,1,256,256]{3,2,1,0:T(8,128)(2,1)}, bf16[8,1,256,256]{3,2,1,0:T(8,128)(2,1)S(1)}, u32[]{:S(2)}, u32[]{:S(2)}) collective-permute-start(bf16[8,1,256,256]{3,2,1,0:T(8,128)(2,1)} %refs_6_), channel_id=1, source_target_pairs={{0,4},{1,5},{2,6},{3,7},{4,0},{5,1},{6,2},{7,3},{8,12},{9,13},{10,... | collective-permute-start | bytes 3145736 | tf_op jit(solution)/shard_map/ppermute | solution.py:141
  4.7 0.7 collective-permute-start.5
  5.5 0.5 collective-permute-done.2.refs_1_
  6.0 0.0 collective-permute-done.3.refs_3_
  6.0 1.6 %copy-done = bf16[1,16,256,256]{3,2,1,0:T(8,128)(2,1)S(1)} copy-done((bf16[1,16,256,256]{3,2,1,0:T(8,128)(2,1)S(1)}, bf16[1,16,256,256]{3,2,1,0:T(8,128)(2,1)}, u32[]{:S(2)}) %copy-start) | copy-done | bytes 2097176
  7.5 1.2 copy-done.2
  8.8 0.7 copy-done.4
  9.5 2.5 %shard_map.46.refs_1_ = bf16[2,256,256]{2,1,0:T(8,128)(2,1)S(1)} custom-call(s32[8,16]{1,0:T(8,128)S(1)} %copy-done.4, bf16[8,1,256,256]{3,2,1,0:T(8,128)(2,1)} %refs_0_.9, bf16[8,1,256,256]{3,2,1,0:T(8,128)(2,1)S(1)} %collective-permute-done.2.refs_1_, bf16[1,16,256,256]{3,2,1,0:T(8,128)(2,1)S(1)} %copy-done, ...), custom_call_target="tpu_custom_call" | custom-call | flops 1 | bytes 1 | tf_op jit(solution)/shard_map/pallas_call | solution.py:62
  12.0 0.0 copy-start.1
  12.0 16.7 %collective-permute-done.4.refs_4_.refs_6_ = bf16[8,1,256,256]{3,2,1,0:T(8,128)(2,1)S(1)} collective-permute-done((bf16[8,1,256,256]{3,2,1,0:T(8,128)(2,1)}, bf16[8,1,256,256]{3,2,1,0:T(8,128)(2,1)S(1)}, u32[]{:S(2)}, u32[]{:S(2)}) %collective-permute-start.4) | collective-permute-done | bytes 1048608 | tf_op jit(solution)/shard_map/ppermute | solution.py:141
  28.7 1.3 collective-permute-start.7
  30.0 0.7 collective-permute-start.8
  30.8 18.7 %collective-permute-done.whole.refs_3_ = bf16[1,16,256,256]{3,2,1,0:T(8,128)(2,1)S(1)} collective-permute-done((bf16[1,16,256,256]{3,2,1,0:T(8,128)(2,1)}, bf16[1,16,256,256]{3,2,1,0:T(8,128)(2,1)S(1)}, u32[]{:S(2)}, u32[]{:S(2)}) %collective-permute-start) | collective-permute-done | bytes 2097184 | tf_op jit(solution)/shard_map/ppermute | solution.py:141
  49.5 0.1 shard_map.48
  49.6 0.1 collective-permute-start.10
  49.7 0.5 collective-permute-start.9
  50.2 1.7 %collective-permute-start.1 = (bf16[8,1,256,256]{3,2,1,0:T(8,128)(2,1)}, bf16[8,1,256,256]{3,2,1,0:T(8,128)(2,1)S(1)}, u32[]{:S(2)}, u32[]{:S(2)}) collective-permute-start(bf16[8,1,256,256]{3,2,1,0:T(8,128)(2,1)} %refs_0_.9), channel_id=1, source_target_pairs={{0,2},{1,3},{2,0},{3,1},{4,6},{5,7},{6,4},{7,5},{8,10},{9,11},{10,... | collective-permute-start | bytes 3145736 | tf_op jit(solution)/shard_map/ppermute | solution.py:141
  51.9 5.5 %collective-permute-done.7.refs_4_.refs_6_ = bf16[8,1,256,256]{3,2,1,0:T(8,128)(2,1)S(1)} collective-permute-done((bf16[8,1,256,256]{3,2,1,0:T(8,128)(2,1)S(1)}, bf16[8,1,256,256]{3,2,1,0:T(8,128)(2,1)S(1)}, u32[]{:S(2)}, u32[]{:S(2)}) %collective-permute-start.7) | collective-permute-done | bytes 1048608 | tf_op jit(solution)/shard_map/ppermute | solution.py:141
  57.4 0.0 collective-permute-done.8.refs_5_.refs_7_
  57.4 1.3 collective-permute-start.17
  58.7 2.5 %shard_map.47 = bf16[2,256,256]{2,1,0:T(8,128)(2,1)S(1)} custom-call(s32[8,16]{1,0:T(8,128)S(1)} %copy-done.4, bf16[8,1,256,256]{3,2,1,0:T(8,128)(2,1)} %refs_0_.9, bf16[8,1,256,256]{3,2,1,0:T(8,128)(2,1)S(1)} %collective-permute-done.2.refs_1_, bf16[1,16,256,256]{3,2,1,0:T(8,128)(2,1)S(1)} %copy-done.1, ...), custom_call_target="tpu_custom_call" | custom-call | flops 1 | bytes 1 | tf_op jit(solution)/shard_map/pallas_call | solution.py:62
  61.2 3.8 %collective-permute-start.6 = (bf16[2,256,256]{2,1,0:T(8,128)(2,1)S(1)}, bf16[2,256,256]{2,1,0:T(8,128)(2,1)S(1)}, u32[]{:S(2)}, u32[]{:S(2)}) collective-permute-start(bf16[2,256,256]{2,1,0:T(8,128)(2,1)S(1)} %shard_map.47), channel_id=1, source_target_pairs={{0,4},{1,5},{2,6},{3,7},{4,0},{5,1},{6,2},{7,3},{8,12},{9,13},{10,... | collective-permute-start | bytes 786440 | tf_op jit(solution)/shard_map/ppermute | solution.py:141
  65.1 2.6 %shard_map.49 = bf16[2,256,256]{2,1,0:T(8,128)(2,1)S(1)} custom-call(s32[8,16]{1,0:T(8,128)S(1)} %copy-done.4, bf16[8,1,256,256]{3,2,1,0:T(8,128)(2,1)} %refs_0_.9, bf16[8,1,256,256]{3,2,1,0:T(8,128)(2,1)S(1)} %collective-permute-done.2.refs_1_, bf16[1,16,256,256]{3,2,1,0:T(8,128)(2,1)S(1)} %copy-done.1, ...), custom_call_target="tpu_custom_call" | custom-call | flops 1 | bytes 1 | tf_op jit(solution)/shard_map/pallas_call | solution.py:62
  67.6 0.9 collective-permute-start.11
  68.6 26.9 %collective-permute-done.6.refs_3_ = bf16[2,256,256]{2,1,0:T(8,128)(2,1)S(1)} collective-permute-done((bf16[2,256,256]{2,1,0:T(8,128)(2,1)S(1)}, bf16[2,256,256]{2,1,0:T(8,128)(2,1)S(1)}, u32[]{:S(2)}, u32[]{:S(2)}) %collective-permute-start.6) | collective-permute-done | bytes 262176 | tf_op jit(solution)/shard_map/ppermute | solution.py:141
  95.5 0.1 shard_map.50
  95.6 0.1 collective-permute-start.12
  95.6 0.5 collective-permute-start.13
  96.1 2.5 %shard_map.51 = bf16[2,256,256]{2,1,0:T(8,128)(2,1)S(1)} custom-call(s32[8,16]{1,0:T(8,128)S(1)} %copy-done.4, bf16[8,1,256,256]{3,2,1,0:T(8,128)(2,1)} %refs_0_.9, bf16[8,1,256,256]{3,2,1,0:T(8,128)(2,1)S(1)} %collective-permute-done.2.refs_1_, bf16[1,16,256,256]{3,2,1,0:T(8,128)(2,1)S(1)} %copy-done.1, ...), custom_call_target="tpu_custom_call" | custom-call | flops 1 | bytes 1 | tf_op jit(solution)/shard_map/pallas_call | solution.py:62
  98.7 0.7 collective-permute-start.14
  99.4 0.0 collective-permute-done.13.refs_2_
  99.4 1.9 %shard_map.52 = bf16[2,256,256]{2,1,0:T(8,128)(2,1)S(1)} custom-call(s32[8,16]{1,0:T(8,128)S(1)} %copy-done.4, bf16[8,1,256,256]{3,2,1,0:T(8,128)(2,1)S(1)} %collective-permute-done.1.whole.refs_0_, bf16[4,1,256,256]{3,2,1,0:T(8,128)(2,1)S(1)} %collective-permute-done.12.refs_1_, bf16[4,1,256,256]{3,2,1,0:T(8,128)(2,1)S(1)} %collective-permute-done.13.refs_2_, ...), custom_call_target="tpu_custom_call" | custom-call | flops 1 | bytes 1 | tf_op jit(solution)/shard_map/pallas_call | solution.py:62
  101.3 2.3 %collective-permute-start.16 = (bf16[2,256,256]{2,1,0:T(8,128)(2,1)S(1)}, bf16[2,256,256]{2,1,0:T(8,128)(2,1)S(1)}, u32[]{:S(2)}, u32[]{:S(2)}) collective-permute-start(bf16[2,256,256]{2,1,0:T(8,128)(2,1)S(1)} %shard_map.52), channel_id=1, source_target_pairs={{0,8},{1,9},{2,10},{3,11},{4,12},{5,13},{6,14},{7,15},{8,0},{9,1},... | collective-permute-start | bytes 786440 | tf_op jit(solution)/shard_map/ppermute | solution.py:141
  103.6 1.9 %shard_map.53 = bf16[2,256,256]{2,1,0:T(8,128)(2,1)S(1)} custom-call(s32[8,16]{1,0:T(8,128)S(1)} %copy-done.4, bf16[8,1,256,256]{3,2,1,0:T(8,128)(2,1)S(1)} %collective-permute-done.1.whole.refs_0_, bf16[4,1,256,256]{3,2,1,0:T(8,128)(2,1)S(1)} %collective-permute-done.12.refs_1_, bf16[4,1,256,256]{3,2,1,0:T(8,128)(2,1)S(1)} %collective-permute-done.13.refs_2_, ...), custom_call_target="tpu_custom_call" | custom-call | flops 1 | bytes 1 | tf_op jit(solution)/shard_map/pallas_call | solution.py:62
  105.5 11.3 %collective-permute-start.15 = (bf16[2,256,256]{2,1,0:T(8,128)(2,1)S(1)}, bf16[2,256,256]{2,1,0:T(8,128)(2,1)S(1)}, u32[]{:S(2)}, u32[]{:S(2)}) collective-permute-start(bf16[2,256,256]{2,1,0:T(8,128)(2,1)S(1)} %shard_map.53), channel_id=1, source_target_pairs={{0,4},{1,5},{2,6},{3,7},{4,0},{5,1},{6,2},{7,3},{8,12},{9,13},{10,... | collective-permute-start | bytes 786440 | tf_op jit(solution)/shard_map/ppermute | solution.py:141
  116.8 1.9 %shard_map.55 = bf16[2,256,256]{2,1,0:T(8,128)(2,1)S(1)} custom-call(s32[8,16]{1,0:T(8,128)S(1)} %copy-done.4, bf16[8,1,256,256]{3,2,1,0:T(8,128)(2,1)S(1)} %collective-permute-done.1.whole.refs_0_, bf16[4,1,256,256]{3,2,1,0:T(8,128)(2,1)S(1)} %collective-permute-done.12.refs_1_, bf16[4,1,256,256]{3,2,1,0:T(8,128)(2,1)S(1)} %collective-permute-done.13.refs_2_, ...), custom_call_target="tpu_custom_call" | custom-call | flops 10000000000 | bytes 1 | tf_op jit(solution)/shard_map/pallas_call | solution.py:62
  118.8 0.0 copy-start.3
  118.8 2.1 %collective-permute-start.18 = (bf16[2,256,256]{2,1,0:T(8,128)(2,1)S(1)}, bf16[2,256,256]{2,1,0:T(8,128)(2,1)S(1)}, u32[]{:S(2)}, u32[]{:S(2)}) collective-permute-start(bf16[2,256,256]{2,1,0:T(8,128)(2,1)S(1)} %shard_map.55), channel_id=1, source_target_pairs={{0,12},{1,13},{2,14},{3,15},{4,8},{5,9},{6,10},{7,11},{8,4},{9,5},... | collective-permute-start | bytes 786440 | tf_op jit(solution)/shard_map/ppermute | solution.py:141
  120.8 2.5 %shard_map.56 = bf16[2,256,256]{2,1,0:T(8,128)(2,1)S(1)} custom-call(s32[8,16]{1,0:T(8,128)S(1)} %copy-done.4, bf16[8,1,256,256]{3,2,1,0:T(8,128)(2,1)} %refs_0_.9, bf16[8,1,256,256]{3,2,1,0:T(8,128)(2,1)S(1)} %collective-permute-done.2.refs_1_, bf16[1,16,256,256]{3,2,1,0:T(8,128)(2,1)S(1)} %copy-done.1, ...), custom_call_target="tpu_custom_call" | custom-call | flops 1 | bytes 1 | tf_op jit(solution)/shard_map/pallas_call | solution.py:62
  123.3 3.7 %collective-permute-start.19 = (bf16[2,256,256]{2,1,0:T(8,128)(2,1)S(1)}, bf16[2,256,256]{2,1,0:T(8,128)(2,1)S(1)}, u32[]{:S(2)}, u32[]{:S(2)}) collective-permute-start(bf16[2,256,256]{2,1,0:T(8,128)(2,1)S(1)} %shard_map.56), channel_id=1, source_target_pairs={{0,12},{1,13},{2,14},{3,15},{12,0},{13,1},{14,2},{15,3},{16,28},{1... | collective-permute-start | bytes 786440 | tf_op jit(solution)/shard_map/ppermute | solution.py:141
  127.1 8.8 %collective-permute-done.15.refs_2_ = bf16[2,256,256]{2,1,0:T(8,128)(2,1)S(1)} collective-permute-done((bf16[2,256,256]{2,1,0:T(8,128)(2,1)S(1)}, bf16[2,256,256]{2,1,0:T(8,128)(2,1)S(1)}, u32[]{:S(2)}, u32[]{:S(2)}) %collective-permute-start.15) | collective-permute-done | bytes 262176 | tf_op jit(solution)/shard_map/ppermute | solution.py:141
  135.9 1.9 %shard_map.54.refs_0_ = bf16[2,256,256]{2,1,0:T(8,128)(2,1)S(1)} custom-call(s32[8,16]{1,0:T(8,128)S(1)} %copy-done.4, bf16[8,1,256,256]{3,2,1,0:T(8,128)(2,1)S(1)} %collective-permute-done.1.whole.refs_0_, bf16[4,1,256,256]{3,2,1,0:T(8,128)(2,1)S(1)} %collective-permute-done.12.refs_1_, bf16[4,1,256,256]{3,2,1,0:T(8,128)(2,1)S(1)} %collective-permute-done.13.refs_2_, ...), custom_call_target="tpu_custom_call" | custom-call | flops 10000000000 | bytes 1 | tf_op jit(solution)/shard_map/pallas_call | solution.py:62
  137.8 0.0 collective-permute-done.19.refs_7_
  137.8 0.0 collective-permute-done.18.refs_6_
  137.8 1.4 %shard_map.57 = bf16[16,256,256]{2,1,0:T(8,128)(2,1)} custom-call(bf16[2,256,256]{2,1,0:T(8,128)(2,1)S(1)} %shard_map.54.refs_0_, bf16[2,256,256]{2,1,0:T(8,128)(2,1)S(1)} %shard_map.46.refs_1_, bf16[2,256,256]{2,1,0:T(8,128)(2,1)S(1)} %collective-permute-done.15.refs_2_, bf16[2,256,256]{2,1,0:T(8,128)(2,1)S(1)} %collective-permute-done.6.refs_3_, ...), custom_call_target="tpu_custom_call" | custom-call | tf_op jit(solution)/shard_map/pallas_call | solution.py:130
  (14 shorter events, 0.0 us)
Async XLA Ops:
  0.0 6.0 %collective-permute-start.3 = (bf16[1,16,256,256]{3,2,1,0:T(8,128)(2,1)}, bf16[1,16,256,256]{3,2,1,0:T(8,128)(2,1)S(1)}, u32[]{:S(2)}, u32[]{:S(2)}) collective-permute-start(bf16[1,16,256,256]{3,2,1,0:T(8,128)(2,1)} %refs_2_.9), channel_id=1, source_target_pairs={{0,1},{1,0},{2,3},{3,2},{4,5},{5,4},{6,7},{7,6},{8,9},{9,8},{10,11... | collective-permute-start | bytes 6291464 | tf_op jit(solution)/shard_map/ppermute | solution.py:141
  0.5 49.0 %collective-permute-start = (bf16[1,16,256,256]{3,2,1,0:T(8,128)(2,1)}, bf16[1,16,256,256]{3,2,1,0:T(8,128)(2,1)S(1)}, u32[]{:S(2)}, u32[]{:S(2)}) collective-permute-start(bf16[1,16,256,256]{3,2,1,0:T(8,128)(2,1)} %refs_2_.9), channel_id=1, source_target_pairs={{0,2},{1,3},{2,0},{3,1},{4,6},{5,7},{6,4},{7,5},{8,10},{9,11},{10,... | collective-permute-start | bytes 6291464 | tf_op jit(solution)/shard_map/ppermute | solution.py:141
  2.9 3.0 %collective-permute-start.2 = (bf16[8,1,256,256]{3,2,1,0:T(8,128)(2,1)}, bf16[8,1,256,256]{3,2,1,0:T(8,128)(2,1)S(1)}, u32[]{:S(2)}, u32[]{:S(2)}) collective-permute-start(bf16[8,1,256,256]{3,2,1,0:T(8,128)(2,1)} %refs_0_.9), channel_id=1, source_target_pairs={{0,1},{1,0},{2,3},{3,2},{4,5},{5,4},{6,7},{7,6},{8,9},{9,8},{10,11... | collective-permute-start | bytes 3145736 | tf_op jit(solution)/shard_map/ppermute | solution.py:141
  3.2 25.6 %collective-permute-start.4 = (bf16[8,1,256,256]{3,2,1,0:T(8,128)(2,1)}, bf16[8,1,256,256]{3,2,1,0:T(8,128)(2,1)S(1)}, u32[]{:S(2)}, u32[]{:S(2)}) collective-permute-start(bf16[8,1,256,256]{3,2,1,0:T(8,128)(2,1)} %refs_6_), channel_id=1, source_target_pairs={{0,4},{1,5},{2,6},{3,7},{4,0},{5,1},{6,2},{7,3},{8,12},{9,13},{10,... | collective-permute-start | bytes 3145736 | tf_op jit(solution)/shard_map/ppermute | solution.py:141
  4.7 24.0 %collective-permute-start.5 = (bf16[8,1,256,256]{3,2,1,0:T(8,128)(2,1)}, bf16[8,1,256,256]{3,2,1,0:T(8,128)(2,1)S(1)}, u32[]{:S(2)}, u32[]{:S(2)}) collective-permute-start(bf16[8,1,256,256]{3,2,1,0:T(8,128)(2,1)} %refs_6_), channel_id=1, source_target_pairs={{4,8},{5,9},{6,10},{7,11},{8,4},{9,5},{10,6},{11,7},{20,24},{21,25... | collective-permute-start | bytes 3145736 | tf_op jit(solution)/shard_map/ppermute | solution.py:141
  6.0 1.6 %copy-start = (bf16[1,16,256,256]{3,2,1,0:T(8,128)(2,1)S(1)}, bf16[1,16,256,256]{3,2,1,0:T(8,128)(2,1)}, u32[]{:S(2)}) copy-start(bf16[1,16,256,256]{3,2,1,0:T(8,128)(2,1)} %refs_2_.9) | copy-start | bytes 6291460
  7.5 1.2 copy-start.2
  8.8 0.7 copy-start.4
  12.0 46.7 %copy-start.1 = (bf16[1,16,256,256]{3,2,1,0:T(8,128)(2,1)S(1)}, bf16[1,16,256,256]{3,2,1,0:T(8,128)(2,1)}, u32[]{:S(2)}) copy-start(bf16[1,16,256,256]{3,2,1,0:T(8,128)(2,1)} %refs_2_.9) | copy-start | bytes 6291460
  28.7 28.7 %collective-permute-start.7 = (bf16[8,1,256,256]{3,2,1,0:T(8,128)(2,1)S(1)}, bf16[8,1,256,256]{3,2,1,0:T(8,128)(2,1)S(1)}, u32[]{:S(2)}, u32[]{:S(2)}) collective-permute-start(bf16[8,1,256,256]{3,2,1,0:T(8,128)(2,1)S(1)} %collective-permute-done.5.refs_4_.refs_7_), channel_id=1, source_target_pairs={{4,0},{5,1},{6,2},{7,3},{8,12},{9,13},{10,14},{11,15},{20,16},{21,... | collective-permute-start | bytes 3145736 | tf_op jit(solution)/shard_map/ppermute | solution.py:141
  30.0 27.4 %collective-permute-start.8 = (bf16[8,1,256,256]{3,2,1,0:T(8,128)(2,1)S(1)}, bf16[8,1,256,256]{3,2,1,0:T(8,128)(2,1)S(1)}, u32[]{:S(2)}, u32[]{:S(2)}) collective-permute-start(bf16[8,1,256,256]{3,2,1,0:T(8,128)(2,1)S(1)} %collective-permute-done.4.refs_4_.refs_6_), channel_id=1, source_target_pairs={{4,8},{5,9},{6,10},{7,11},{8,4},{9,5},{10,6},{11,7},{20,24},{21,25... | collective-permute-start | bytes 3145736 | tf_op jit(solution)/shard_map/ppermute | solution.py:141
  49.6 15.5 %collective-permute-start.10 = (bf16[1,8,256,256]{3,2,1,0:T(8,128)(2,1)S(1)}, bf16[1,8,256,256]{3,2,1,0:T(8,128)(2,1)S(1)}, u32[]{:S(2)}, u32[]{:S(2)}) collective-permute-start(bf16[1,8,256,256]{3,2,1,0:T(8,128)(2,1)S(1)} %get-tuple-element.35), channel_id=1, source_target_pairs={{0,1},{1,0},{2,3},{3,2},{4,5},{5,4},{6,7},{7,6},{8,9},{9,8},{10,11... | collective-permute-start | bytes 3145736 | tf_op jit(solution)/shard_map/ppermute | solution.py:141
  49.7 15.4 %collective-permute-start.9 = (bf16[1,8,256,256]{3,2,1,0:T(8,128)(2,1)S(1)}, bf16[1,8,256,256]{3,2,1,0:T(8,128)(2,1)S(1)}, u32[]{:S(2)}, u32[]{:S(2)}) collective-permute-start(bf16[1,8,256,256]{3,2,1,0:T(8,128)(2,1)S(1)} %get-tuple-element.34), channel_id=1, source_target_pairs={{0,1},{1,0},{2,3},{3,2},{4,5},{5,4},{6,7},{7,6},{8,9},{9,8},{10,11... | collective-permute-start | bytes 3145736 | tf_op jit(solution)/shard_map/ppermute | solution.py:141
  50.2 45.3 %collective-permute-start.1 = (bf16[8,1,256,256]{3,2,1,0:T(8,128)(2,1)}, bf16[8,1,256,256]{3,2,1,0:T(8,128)(2,1)S(1)}, u32[]{:S(2)}, u32[]{:S(2)}) collective-permute-start(bf16[8,1,256,256]{3,2,1,0:T(8,128)(2,1)} %refs_0_.9), channel_id=1, source_target_pairs={{0,2},{1,3},{2,0},{3,1},{4,6},{5,7},{6,4},{7,5},{8,10},{9,11},{10,... | collective-permute-start | bytes 3145736 | tf_op jit(solution)/shard_map/ppermute | solution.py:141
  57.4 59.4 %collective-permute-start.17 = (bf16[8,1,256,256]{3,2,1,0:T(8,128)(2,1)S(1)}, bf16[8,1,256,256]{3,2,1,0:T(8,128)(2,1)S(1)}, u32[]{:S(2)}, u32[]{:S(2)}) collective-permute-start(bf16[8,1,256,256]{3,2,1,0:T(8,128)(2,1)S(1)} %collective-permute-done.8.refs_5_.refs_7_), channel_id=1, source_target_pairs={{4,0},{5,1},{6,2},{7,3},{8,12},{9,13},{10,14},{11,15},{20,16},{21,... | collective-permute-start | bytes 3145736 | tf_op jit(solution)/shard_map/ppermute | solution.py:141
  61.2 34.3 %collective-permute-start.6 = (bf16[2,256,256]{2,1,0:T(8,128)(2,1)S(1)}, bf16[2,256,256]{2,1,0:T(8,128)(2,1)S(1)}, u32[]{:S(2)}, u32[]{:S(2)}) collective-permute-start(bf16[2,256,256]{2,1,0:T(8,128)(2,1)S(1)} %shard_map.47), channel_id=1, source_target_pairs={{0,4},{1,5},{2,6},{3,7},{4,0},{5,1},{6,2},{7,3},{8,12},{9,13},{10,... | collective-permute-start | bytes 786440 | tf_op jit(solution)/shard_map/ppermute | solution.py:141
  67.6 27.9 %collective-permute-start.11 = (bf16[2,256,256]{2,1,0:T(8,128)(2,1)S(1)}, bf16[2,256,256]{2,1,0:T(8,128)(2,1)S(1)}, u32[]{:S(2)}, u32[]{:S(2)}) collective-permute-start(bf16[2,256,256]{2,1,0:T(8,128)(2,1)S(1)} %shard_map.49), channel_id=1, source_target_pairs={{0,8},{1,9},{2,10},{3,11},{4,12},{5,13},{6,14},{7,15},{8,0},{9,1},... | collective-permute-start | bytes 786440 | tf_op jit(solution)/shard_map/ppermute | solution.py:141
  95.6 3.8 %collective-permute-start.12 = (bf16[4,1,256,256]{3,2,1,0:T(8,128)(2,1)S(1)}, bf16[4,1,256,256]{3,2,1,0:T(8,128)(2,1)S(1)}, u32[]{:S(2)}, u32[]{:S(2)}) collective-permute-start(bf16[4,1,256,256]{3,2,1,0:T(8,128)(2,1)S(1)} %get-tuple-element.39), channel_id=1, source_target_pairs={{0,1},{1,0},{2,3},{3,2},{4,5},{5,4},{6,7},{7,6},{8,9},{9,8},{10,11... | collective-permute-start | bytes 1572872 | tf_op jit(solution)/shard_map/ppermute | solution.py:141
  95.6 3.7 %collective-permute-start.13 = (bf16[4,1,256,256]{3,2,1,0:T(8,128)(2,1)S(1)}, bf16[4,1,256,256]{3,2,1,0:T(8,128)(2,1)S(1)}, u32[]{:S(2)}, u32[]{:S(2)}) collective-permute-start(bf16[4,1,256,256]{3,2,1,0:T(8,128)(2,1)S(1)} %get-tuple-element.40), channel_id=1, source_target_pairs={{0,1},{1,0},{2,3},{3,2},{4,5},{5,4},{6,7},{7,6},{8,9},{9,8},{10,11... | collective-permute-start | bytes 1572872 | tf_op jit(solution)/shard_map/ppermute | solution.py:141
  98.7 4.9 %collective-permute-start.14 = (bf16[2,256,256]{2,1,0:T(8,128)(2,1)S(1)}, bf16[2,256,256]{2,1,0:T(8,128)(2,1)S(1)}, u32[]{:S(2)}, u32[]{:S(2)}) collective-permute-start(bf16[2,256,256]{2,1,0:T(8,128)(2,1)S(1)} %shard_map.51), channel_id=1, source_target_pairs={{4,8},{5,9},{6,10},{7,11},{8,4},{9,5},{10,6},{11,7},{20,24},{21,25... | collective-permute-start | bytes 786440 | tf_op jit(solution)/shard_map/ppermute | solution.py:141
  101.3 34.6 %collective-permute-start.16 = (bf16[2,256,256]{2,1,0:T(8,128)(2,1)S(1)}, bf16[2,256,256]{2,1,0:T(8,128)(2,1)S(1)}, u32[]{:S(2)}, u32[]{:S(2)}) collective-permute-start(bf16[2,256,256]{2,1,0:T(8,128)(2,1)S(1)} %shard_map.52), channel_id=1, source_target_pairs={{0,8},{1,9},{2,10},{3,11},{4,12},{5,13},{6,14},{7,15},{8,0},{9,1},... | collective-permute-start | bytes 786440 | tf_op jit(solution)/shard_map/ppermute | solution.py:141
  105.5 30.4 %collective-permute-start.15 = (bf16[2,256,256]{2,1,0:T(8,128)(2,1)S(1)}, bf16[2,256,256]{2,1,0:T(8,128)(2,1)S(1)}, u32[]{:S(2)}, u32[]{:S(2)}) collective-permute-start(bf16[2,256,256]{2,1,0:T(8,128)(2,1)S(1)} %shard_map.53), channel_id=1, source_target_pairs={{0,4},{1,5},{2,6},{3,7},{4,0},{5,1},{6,2},{7,3},{8,12},{9,13},{10,... | collective-permute-start | bytes 786440 | tf_op jit(solution)/shard_map/ppermute | solution.py:141
  118.8 17.2 %copy-start.3 = (bf16[8,1,256,256]{3,2,1,0:T(8,128)(2,1)S(1)}, bf16[8,1,256,256]{3,2,1,0:T(8,128)(2,1)}, u32[]{:S(2)}) copy-start(bf16[8,1,256,256]{3,2,1,0:T(8,128)(2,1)} %refs_6_) | copy-start | bytes 3145732
  118.8 19.1 %collective-permute-start.18 = (bf16[2,256,256]{2,1,0:T(8,128)(2,1)S(1)}, bf16[2,256,256]{2,1,0:T(8,128)(2,1)S(1)}, u32[]{:S(2)}, u32[]{:S(2)}) collective-permute-start(bf16[2,256,256]{2,1,0:T(8,128)(2,1)S(1)} %shard_map.55), channel_id=1, source_target_pairs={{0,12},{1,13},{2,14},{3,15},{4,8},{5,9},{6,10},{7,11},{8,4},{9,5},... | collective-permute-start | bytes 786440 | tf_op jit(solution)/shard_map/ppermute | solution.py:141
  123.3 14.5 %collective-permute-start.19 = (bf16[2,256,256]{2,1,0:T(8,128)(2,1)S(1)}, bf16[2,256,256]{2,1,0:T(8,128)(2,1)S(1)}, u32[]{:S(2)}, u32[]{:S(2)}) collective-permute-start(bf16[2,256,256]{2,1,0:T(8,128)(2,1)S(1)} %shard_map.56), channel_id=1, source_target_pairs={{0,12},{1,13},{2,14},{3,15},{12,0},{13,1},{14,2},{15,3},{16,28},{1... | collective-permute-start | bytes 786440 | tf_op jit(solution)/shard_map/ppermute | solution.py:141

commit v8 on v7

--- a/solution.py
+++ b/solution.py
@@ -73,23 +73,20 @@
     )(source_map, *held)
 
 
-def split_kernel(axis, whole, low, high):
-    half = low.shape[axis]
-    before = (slice(None),) * axis
-    low[...] = whole[(*before, slice(0, half))]
-    high[...] = whole[(*before, slice(half, None))]
-
-
-def split(array, axis):
-    shape = list(array.shape)
-    shape[axis] //= 2
-    half = jax.ShapeDtypeStruct(tuple(shape), array.dtype)
+def split_kernel(whole, low, high):
+    half = low.shape[0]
+    low[...] = whole[:half]
+    high[...] = whole[half:]
+
+
+def split(array):
+    half = jax.ShapeDtypeStruct((array.shape[0] // 2,) + array.shape[1:], array.dtype)
     return pl.pallas_call(
-        functools.partial(split_kernel, axis),
+        split_kernel,
         out_shape=(half, half),
         in_specs=[VMEM],
         out_specs=(VMEM, VMEM),
-        compiler_params=pltpu.CompilerParams(vmem_limit_bytes=12 << 20),
+        compiler_params=pltpu.CompilerParams(vmem_limit_bytes=8 << 20),
         cost_estimate=pl.CostEstimate(flops=1, bytes_accessed=1, transcendentals=0),
     )(array)
 
@@ -103,7 +100,7 @@
     def copies(pieces, first):
         blocks = [piece.at[i] for piece in pieces for i in range(piece.shape[0])]
         return [
-            pltpu.make_async_copy(block, out.at[me ^ (j ^ 2)], sem.at[j]) for j, block in enumerate(blocks, first)
+            pltpu.make_async_copy(block, out.at[me ^ j], sem.at[j]) for j, block in enumerate(blocks, first)
         ]
 
     last = out.shape[0] - pieces[-1].shape[0]
@@ -146,6 +143,7 @@
     every = range(16)
     inner = range(4, 12)
     outer = [s for s in every if s not in inner]
+    low, high = split(left_env)
 
     def products(step, lefts, psis, rights, flops=1):
         return slot(step, source_map, lefts, psis, rights, dtype, flops)
@@ -162,37 +160,37 @@
     own_1 = products(1, *own, (near,))
     sent_1 = exchange(own_1, 4, every)
 
-    x_psi, left_next = lax.optimization_barrier((x_psi, left_env))
-    x_left = exchange(left_next, 2, every)
-    across_psi = [exchange(part, 1, every) for part in split(x_psi, 1)]
+    x_psi, low = lax.optimization_barrier((x_psi, low))
+    x_low = exchange(low, 2, every)
+    across_psi = exchange(x_psi, 1, every)
 
     second, far_in = lax.optimization_barrier((second, far_in))
     third = exchange(far_in, 4, inner)
-    second, *across_psi = lax.optimization_barrier((second, *across_psi))
     own_2 = products(2, *own, (second, far_in))
     sent_2 = exchange(own_2, 8, every)
-    own_middle = products(3, *own, (middle,))
-    sent_middle = exchange(own_middle, 12, inner)
-
-    x_left, sent_1, sent_2 = lax.optimization_barrier((x_left, sent_1, sent_2))
-    across_left = [exchange(part, 1, every) for part in split(x_left, 0)]
-    other = ([(x_left,), across_left], [(x_psi,), across_psi])
+
+    own_2, sent_1, high = lax.optimization_barrier((own_2, sent_1, high))
+    x_high = exchange(high, 2, every)
+    x_low, x_high, sent_2 = lax.optimization_barrier((x_low, x_high, sent_2))
+    across_low = exchange(x_low, 1, every)
+    across_high = exchange(x_high, 1, every)
+    other = ([(x_low, x_high), (across_low, across_high)], [(x_psi,), (across_psi,)])
     other_2 = products(2, *other, (second, far_in))
     other_sent_2 = exchange(other_2, 8, every)
-    near, sent_middle, other_2 = lax.optimization_barrier((near, sent_middle, other_2))
+    both = (own[0] + other[0], own[1] + other[1])
+    last_middle = products(3, *both, (middle,))
+    sent_middle = exchange(last_middle, 12, inner)
+    near, other_2, last_middle = lax.optimization_barrier((near, other_2, last_middle))
     other_1 = products(1, *other, (near,))
     other_sent_1 = exchange(other_1, 4, every)
 
-    third, other_1, other_2 = lax.optimization_barrier((third, other_1, other_2))
-    other_3 = products(3, *other, (third, middle), flops=10**10)
-    other_sent_3 = exchange(other_3, 12, every)
-    third, other_3 = lax.optimization_barrier((third, other_3))
-    own_third = products(3, *own, (third,))
-    sent_third = exchange(own_third, 12, outer)
+    third, other_1 = lax.optimization_barrier((third, other_1))
+    last_third = products(3, *both, (third,))
+    sent_third = exchange(last_third, 12, outer)
     right_last, other_sent_1, other_sent_2 = lax.optimization_barrier((right_env, other_sent_1, other_sent_2))
     other_0 = products(0, *other, (right_last,), flops=10**10)
 
-    pieces = [other_0, own_0, other_sent_1, sent_1, other_sent_2, sent_2, other_sent_3, sent_third, sent_middle]
+    pieces = [own_0, other_0, sent_1, other_sent_1, sent_2, other_sent_2, sent_third, sent_middle]
     out = place(pieces)[:, None]
     if ops > 1:
         out = lax.psum_scatter(out, "op", scatter_dimension=2, tiled=True).astype(jnp.bfloat16)

time: 140 us -> 126 us (0.900)
  the two profiles are of different devices: /device:TPU:0 before, /device:TPU:20 now
where the time goes in v8:
time: 126 us
  waiting for transfers between devices  76.7 us (61%)
  starting transfers between devices  25.4 us (20%)
  Pallas kernels  18.7 us (15%)
  local copies, waits for them, and re-layouts  4.75 us (4%)
    ppermute x19, waiting for transfers between devices, exchange(): return lax.ppermute(array, 'sec', [(s, s ^ bits) for s in members])  76.7 us
    ppermute x19, starting transfers between devices, exchange(): return lax.ppermute(array, 'sec', [(s, s ^ bits) for s in members])  25.4 us
    pallas_call x8, Pallas kernels, slot(): pl.pallas_call(functools.partial(slot_kernel, step, parts, len(rights)),...  17.2 us
    unnamed x14, local copies, waits for them, and re-layouts  4.75 us
  transfers between devices with their start and end apart: 19, of which 14 were waited for; matrix products, arithmetic and copies ran while one was open for 0% of the time, Pallas kernels for 14%

profile of v8, /device:TPU:20, one launch (start us, length us, event | category | flops | bytes accessed | tf_op | source)
XLA Modules:
  0.0 125.9 jit_solution(14238334727702180688)
XLA Ops:
  0.0 0.0 collective-permute-start.3
  0.0 1.5 %collective-permute-start.4 = (bf16[1,16,256,256]{3,2,1,0:T(8,128)(2,1)}, bf16[1,16,256,256]{3,2,1,0:T(8,128)(2,1)S(1)}, u32[]{:S(2)}, u32[]{:S(2)}) collective-permute-start(bf16[1,16,256,256]{3,2,1,0:T(8,128)(2,1)} %refs_6_.4), channel_id=1, source_target_pairs={{0,2},{1,3},{2,0},{3,1},{4,6},{5,7},{6,4},{7,5},{8,10},{9,11},{10,... | collective-permute-start | bytes 6291464 | tf_op jit(solution)/shard_map/ppermute | solution.py:138
  1.5 0.2 collective-permute-start.2
  1.7 2.3 %collective-permute-start.1 = (bf16[8,1,256,256]{3,2,1,0:T(8,128)(2,1)}, bf16[8,1,256,256]{3,2,1,0:T(8,128)(2,1)S(1)}, u32[]{:S(2)}, u32[]{:S(2)}) collective-permute-start(bf16[8,1,256,256]{3,2,1,0:T(8,128)(2,1)} %refs_6_.3), channel_id=1, source_target_pairs={{4,8},{5,9},{6,10},{7,11},{8,4},{9,5},{10,6},{11,7},{20,24},{21,25... | collective-permute-start | bytes 3145736 | tf_op jit(solution)/shard_map/ppermute | solution.py:138
  4.1 0.1 collective-permute-start
  4.2 1.7 %collective-permute-done.2.refs_1_ = bf16[8,1,256,256]{3,2,1,0:T(8,128)(2,1)S(1)} collective-permute-done((bf16[8,1,256,256]{3,2,1,0:T(8,128)(2,1)}, bf16[8,1,256,256]{3,2,1,0:T(8,128)(2,1)S(1)}, u32[]{:S(2)}, u32[]{:S(2)}) %collective-permute-start.2) | collective-permute-done | bytes 1048608 | tf_op jit(solution)/shard_map/ppermute | solution.py:138
  5.9 1.6 %copy-done = bf16[1,16,256,256]{3,2,1,0:T(8,128)(2,1)S(1)} copy-done((bf16[1,16,256,256]{3,2,1,0:T(8,128)(2,1)S(1)}, bf16[1,16,256,256]{3,2,1,0:T(8,128)(2,1)}, u32[]{:S(2)}) %copy-start) | copy-done | bytes 2097176
  7.5 1.2 copy-done.2
  8.7 1.2 copy-done.4
  9.9 0.7 copy-done.6
  10.6 1.9 %shard_map.46.refs_0_ = bf16[2,256,256]{2,1,0:T(8,128)(2,1)S(1)} custom-call(s32[8,16]{1,0:T(8,128)S(1)} %copy-done.6, bf16[8,1,256,256]{3,2,1,0:T(8,128)(2,1)S(1)} %copy-done.2, bf16[8,1,256,256]{3,2,1,0:T(8,128)(2,1)S(1)} %collective-permute-done.2.refs_1_, bf16[1,16,256,256]{3,2,1,0:T(8,128)(2,1)S(1)} %copy-done, ...), custom_call_target="tpu_custom_call" | custom-call | flops 1 | bytes 1 | tf_op jit(solution)/shard_map/pallas_call | solution.py:62
  12.5 16.7 %collective-permute-done.1.refs_10_ = bf16[8,1,256,256]{3,2,1,0:T(8,128)(2,1)S(1)} collective-permute-done((bf16[8,1,256,256]{3,2,1,0:T(8,128)(2,1)}, bf16[8,1,256,256]{3,2,1,0:T(8,128)(2,1)S(1)}, u32[]{:S(2)}, u32[]{:S(2)}) %collective-permute-start.1) | collective-permute-done | bytes 1048608 | tf_op jit(solution)/shard_map/ppermute | solution.py:138
  29.2 0.3 collective-permute-done.refs_4_.refs_6_
  29.4 2.2 %collective-permute-start.6 = (bf16[8,1,256,256]{3,2,1,0:T(8,128)(2,1)S(1)}, bf16[8,1,256,256]{3,2,1,0:T(8,128)(2,1)S(1)}, u32[]{:S(2)}, u32[]{:S(2)}) collective-permute-start(bf16[8,1,256,256]{3,2,1,0:T(8,128)(2,1)S(1)} %collective-permute-done.1.refs_10_), channel_id=1, source_target_pairs={{4,0},{5,1},{6,2},{7,3},{8,12},{9,13},{10,14},{11,15},{20,16},{21,... | collective-permute-start | bytes 3145736 | tf_op jit(solution)/shard_map/ppermute | solution.py:138
  31.7 3.5 %collective-permute-start.7 = (bf16[8,1,256,256]{3,2,1,0:T(8,128)(2,1)S(1)}, bf16[8,1,256,256]{3,2,1,0:T(8,128)(2,1)S(1)}, u32[]{:S(2)}, u32[]{:S(2)}) collective-permute-start(bf16[8,1,256,256]{3,2,1,0:T(8,128)(2,1)S(1)} %collective-permute-done.refs_4_.refs_6_), channel_id=1, source_target_pairs={{4,8},{5,9},{6,10},{7,11},{8,4},{9,5},{10,6},{11,7},{20,24},{21,25... | collective-permute-start | bytes 3145736 | tf_op jit(solution)/shard_map/ppermute | solution.py:138
  35.2 0.1 shard_map.47
  35.2 13.0 %collective-permute-done.4.refs_4_.refs_8_ = bf16[1,16,256,256]{3,2,1,0:T(8,128)(2,1)S(1)} collective-permute-done((bf16[1,16,256,256]{3,2,1,0:T(8,128)(2,1)}, bf16[1,16,256,256]{3,2,1,0:T(8,128)(2,1)S(1)}, u32[]{:S(2)}, u32[]{:S(2)}) %collective-permute-start.4) | collective-permute-done | bytes 2097184 | tf_op jit(solution)/shard_map/ppermute | solution.py:138
  48.3 1.9 %shard_map.49 = bf16[2,256,256]{2,1,0:T(8,128)(2,1)S(1)} custom-call(s32[8,16]{1,0:T(8,128)S(1)} %copy-done.6, bf16[8,1,256,256]{3,2,1,0:T(8,128)(2,1)S(1)} %copy-done.2, bf16[8,1,256,256]{3,2,1,0:T(8,128)(2,1)S(1)} %collective-permute-done.2.refs_1_, bf16[1,16,256,256]{3,2,1,0:T(8,128)(2,1)S(1)} %copy-done, ...), custom_call_target="tpu_custom_call" | custom-call | flops 1 | bytes 1 | tf_op jit(solution)/shard_map/pallas_call | solution.py:62
  50.1 1.6 %collective-permute-start.8 = (bf16[2,256,256]{2,1,0:T(8,128)(2,1)S(1)}, bf16[2,256,256]{2,1,0:T(8,128)(2,1)S(1)}, u32[]{:S(2)}, u32[]{:S(2)}) collective-permute-start(bf16[2,256,256]{2,1,0:T(8,128)(2,1)S(1)} %shard_map.49), channel_id=1, source_target_pairs={{0,4},{1,5},{2,6},{3,7},{4,0},{5,1},{6,2},{7,3},{8,12},{9,13},{10,... | collective-permute-start | bytes 786440 | tf_op jit(solution)/shard_map/ppermute | solution.py:138
  51.8 1.5 %collective-permute-start.5 = (bf16[4,1,256,256]{3,2,1,0:T(8,128)(2,1)S(1)}, bf16[4,1,256,256]{3,2,1,0:T(8,128)(2,1)S(1)}, u32[]{:S(2)}, u32[]{:S(2)}) collective-permute-start(bf16[4,1,256,256]{3,2,1,0:T(8,128)(2,1)S(1)} %get-tuple-element.26), channel_id=1, source_target_pairs={{0,2},{1,3},{2,0},{3,1},{4,6},{5,7},{6,4},{7,5},{8,10},{9,11},{10,... | collective-permute-start | bytes 1572872 | tf_op jit(solution)/shard_map/ppermute | solution.py:138
  53.3 1.5 %collective-permute-done.6.refs_4_.refs_6_ = bf16[8,1,256,256]{3,2,1,0:T(8,128)(2,1)S(1)} collective-permute-done((bf16[8,1,256,256]{3,2,1,0:T(8,128)(2,1)S(1)}, bf16[8,1,256,256]{3,2,1,0:T(8,128)(2,1)S(1)}, u32[]{:S(2)}, u32[]{:S(2)}) %collective-permute-start.6) | collective-permute-done | bytes 1048608 | tf_op jit(solution)/shard_map/ppermute | solution.py:138
  54.8 3.0 %collective-permute-done.7.refs_5_.refs_7_ = bf16[8,1,256,256]{3,2,1,0:T(8,128)(2,1)S(1)} collective-permute-done((bf16[8,1,256,256]{3,2,1,0:T(8,128)(2,1)S(1)}, bf16[8,1,256,256]{3,2,1,0:T(8,128)(2,1)S(1)}, u32[]{:S(2)}, u32[]{:S(2)}) %collective-permute-start.7) | collective-permute-done | bytes 1048608 | tf_op jit(solution)/shard_map/ppermute | solution.py:138
  57.8 1.9 %shard_map.48 = bf16[2,256,256]{2,1,0:T(8,128)(2,1)S(1)} custom-call(s32[8,16]{1,0:T(8,128)S(1)} %copy-done.6, bf16[8,1,256,256]{3,2,1,0:T(8,128)(2,1)S(1)} %copy-done.2, bf16[8,1,256,256]{3,2,1,0:T(8,128)(2,1)S(1)} %collective-permute-done.2.refs_1_, bf16[1,16,256,256]{3,2,1,0:T(8,128)(2,1)S(1)} %copy-done, ...), custom_call_target="tpu_custom_call" | custom-call | flops 1 | bytes 1 | tf_op jit(solution)/shard_map/pallas_call | solution.py:62
  59.7 0.0 copy-start.1
  59.8 0.0 copy-start.3
  59.8 0.6 collective-permute-start.9
  60.4 2.9 %collective-permute-start.10 = (bf16[2,256,256]{2,1,0:T(8,128)(2,1)S(1)}, bf16[2,256,256]{2,1,0:T(8,128)(2,1)S(1)}, u32[]{:S(2)}, u32[]{:S(2)}) collective-permute-start(bf16[2,256,256]{2,1,0:T(8,128)(2,1)S(1)} %shard_map.48), channel_id=1, source_target_pairs={{0,8},{1,9},{2,10},{3,11},{4,12},{5,13},{6,14},{7,15},{8,0},{9,1},... | collective-permute-start | bytes 786440 | tf_op jit(solution)/shard_map/ppermute | solution.py:138
  63.3 2.1 %collective-permute-start.16 = (bf16[8,1,256,256]{3,2,1,0:T(8,128)(2,1)S(1)}, bf16[8,1,256,256]{3,2,1,0:T(8,128)(2,1)S(1)}, u32[]{:S(2)}, u32[]{:S(2)}) collective-permute-start(bf16[8,1,256,256]{3,2,1,0:T(8,128)(2,1)S(1)} %collective-permute-done.7.refs_5_.refs_7_), channel_id=1, source_target_pairs={{4,0},{5,1},{6,2},{7,3},{8,12},{9,13},{10,14},{11,15},{20,16},{21,... | collective-permute-start | bytes 3145736 | tf_op jit(solution)/shard_map/ppermute | solution.py:138
  65.4 1.2 collective-permute-done.5.refs_0_.refs_2_
  66.5 6.4 %collective-permute-done.10.refs_4_ = bf16[2,256,256]{2,1,0:T(8,128)(2,1)S(1)} collective-permute-done((bf16[2,256,256]{2,1,0:T(8,128)(2,1)S(1)}, bf16[2,256,256]{2,1,0:T(8,128)(2,1)S(1)}, u32[]{:S(2)}, u32[]{:S(2)}) %collective-permute-start.10) | collective-permute-done | bytes 262176 | tf_op jit(solution)/shard_map/ppermute | solution.py:138
  73.0 4.1 %collective-permute-done.9.refs_1_.refs_3_ = bf16[4,1,256,256]{3,2,1,0:T(8,128)(2,1)S(1)} collective-permute-done((bf16[4,1,256,256]{3,2,1,0:T(8,128)(2,1)S(1)}, bf16[4,1,256,256]{3,2,1,0:T(8,128)(2,1)S(1)}, u32[]{:S(2)}, u32[]{:S(2)}) %collective-permute-start.9) | collective-permute-done | bytes 524320 | tf_op jit(solution)/shard_map/ppermute | solution.py:138
  77.1 0.5 collective-permute-start.12
  77.6 1.4 %collective-permute-done.11.refs_2_.refs_4_ = bf16[4,1,256,256]{3,2,1,0:T(8,128)(2,1)S(1)} collective-permute-done((bf16[4,1,256,256]{3,2,1,0:T(8,128)(2,1)S(1)}, bf16[4,1,256,256]{3,2,1,0:T(8,128)(2,1)S(1)}, u32[]{:S(2)}, u32[]{:S(2)}) %collective-permute-start.11) | collective-permute-done | bytes 524320 | tf_op jit(solution)/shard_map/ppermute | solution.py:138
  79.0 0.7 collective-permute-done.12.refs_3_.refs_5_
  79.7 1.9 %shard_map.50 = bf16[2,256,256]{2,1,0:T(8,128)(2,1)S(1)} custom-call(s32[8,16]{1,0:T(8,128)S(1)} %copy-done.6, bf16[4,1,256,256]{3,2,1,0:T(8,128)(2,1)S(1)} %collective-permute-done.5.refs_0_.refs_2_, bf16[4,1,256,256]{3,2,1,0:T(8,128)(2,1)S(1)} %collective-permute-done.9.refs_1_.refs_3_, ...), custom_call_target="tpu_custom_call" | custom-call | flops 1 | bytes 1 | tf_op jit(solution)/shard_map/pallas_call | solution.py:62
  81.7 3.0 %shard_map.51 = bf16[4,256,256]{2,1,0:T(8,128)(2,1)S(1)} custom-call(s32[8,16]{1,0:T(8,128)S(1)} %copy-done.6, bf16[8,1,256,256]{3,2,1,0:T(8,128)(2,1)S(1)} %copy-done.3, bf16[8,1,256,256]{3,2,1,0:T(8,128)(2,1)S(1)} %collective-permute-done.2.refs_1_, bf16[4,1,256,256]{3,2,1,0:T(8,128)(2,1)S(1)} %collective-permute-done.5.refs_0_.refs_2_, ...), custom_call_target="tpu_custom_call" | custom-call | flops 1 | bytes 1 | tf_op jit(solution)/shard_map/pallas_call | solution.py:62
  84.6 1.9 %shard_map.52 = bf16[2,256,256]{2,1,0:T(8,128)(2,1)S(1)} custom-call(s32[8,16]{1,0:T(8,128)S(1)} %copy-done.6, bf16[4,1,256,256]{3,2,1,0:T(8,128)(2,1)S(1)} %collective-permute-done.5.refs_0_.refs_2_, bf16[4,1,256,256]{3,2,1,0:T(8,128)(2,1)S(1)} %collective-permute-done.9.refs_1_.refs_3_, ...), custom_call_target="tpu_custom_call" | custom-call | flops 1 | bytes 1 | tf_op jit(solution)/shard_map/pallas_call | solution.py:62
  86.5 0.0 copy-start.5
  86.5 0.5 collective-permute-start.14
  87.0 0.3 collective-permute-start.15
  87.4 4.8 %collective-permute-start.18 = (bf16[4,256,256]{2,1,0:T(8,128)(2,1)S(1)}, bf16[4,256,256]{2,1,0:T(8,128)(2,1)S(1)}, u32[]{:S(2)}, u32[]{:S(2)}) collective-permute-start(bf16[4,256,256]{2,1,0:T(8,128)(2,1)S(1)} %shard_map.51), channel_id=1, source_target_pairs={{4,8},{5,9},{6,10},{7,11},{8,4},{9,5},{10,6},{11,7},{20,24},{21,25... | collective-permute-start | bytes 1572872 | tf_op jit(solution)/shard_map/ppermute | solution.py:138
  92.2 5.5 %collective-permute-done.16.refs_10_ = bf16[8,1,256,256]{3,2,1,0:T(8,128)(2,1)S(1)} collective-permute-done((bf16[8,1,256,256]{3,2,1,0:T(8,128)(2,1)S(1)}, bf16[8,1,256,256]{3,2,1,0:T(8,128)(2,1)S(1)}, u32[]{:S(2)}, u32[]{:S(2)}) %collective-permute-start.16) | collective-permute-done | bytes 1048608 | tf_op jit(solution)/shard_map/ppermute | solution.py:138
  97.7 3.0 %shard_map.54 = bf16[4,256,256]{2,1,0:T(8,128)(2,1)S(1)} custom-call(s32[8,16]{1,0:T(8,128)S(1)} %copy-done.6, bf16[8,1,256,256]{3,2,1,0:T(8,128)(2,1)S(1)} %copy-done.3, bf16[8,1,256,256]{3,2,1,0:T(8,128)(2,1)S(1)} %collective-permute-done.2.refs_1_, bf16[4,1,256,256]{3,2,1,0:T(8,128)(2,1)S(1)} %collective-permute-done.5.refs_0_.refs_2_, ...), custom_call_target="tpu_custom_call" | custom-call | flops 1 | bytes 1 | tf_op jit(solution)/shard_map/pallas_call | solution.py:62
  100.6 0.7 collective-permute-start.17
  101.3 1.8 %collective-permute-done.14.refs_3_ = bf16[2,256,256]{2,1,0:T(8,128)(2,1)S(1)} collective-permute-done((bf16[2,256,256]{2,1,0:T(8,128)(2,1)S(1)}, bf16[2,256,256]{2,1,0:T(8,128)(2,1)S(1)}, u32[]{:S(2)}, u32[]{:S(2)}) %collective-permute-start.14) | collective-permute-done | bytes 262176 | tf_op jit(solution)/shard_map/ppermute | solution.py:138
  103.1 1.9 %shard_map.53.refs_1_ = bf16[2,256,256]{2,1,0:T(8,128)(2,1)S(1)} custom-call(s32[8,16]{1,0:T(8,128)S(1)} %copy-done.6, bf16[4,1,256,256]{3,2,1,0:T(8,128)(2,1)S(1)} %collective-permute-done.5.refs_0_.refs_2_, bf16[4,1,256,256]{3,2,1,0:T(8,128)(2,1)S(1)} %collective-permute-done.9.refs_1_.refs_3_, ...), custom_call_target="tpu_custom_call" | custom-call | flops 10000000000 | bytes 1 | tf_op jit(solution)/shard_map/pallas_call | solution.py:62
  105.0 19.3 %collective-permute-done.18.refs_7_ = bf16[4,256,256]{2,1,0:T(8,128)(2,1)S(1)} collective-permute-done((bf16[4,256,256]{2,1,0:T(8,128)(2,1)S(1)}, bf16[4,256,256]{2,1,0:T(8,128)(2,1)S(1)}, u32[]{:S(2)}, u32[]{:S(2)}) %collective-permute-start.18) | collective-permute-done | bytes 524320 | tf_op jit(solution)/shard_map/ppermute | solution.py:138
  124.3 1.4 %shard_map.55 = bf16[16,256,256]{2,1,0:T(8,128)(2,1)} custom-call(bf16[2,256,256]{2,1,0:T(8,128)(2,1)S(1)} %shard_map.46.refs_0_, bf16[2,256,256]{2,1,0:T(8,128)(2,1)S(1)} %shard_map.53.refs_1_, bf16[2,256,256]{2,1,0:T(8,128)(2,1)S(1)} %collective-permute-done.8.refs_2_, bf16[2,256,256]{2,1,0:T(8,128)(2,1)S(1)} %collective-permute-done.14.refs_3_, ...), custom_call_target="tpu_custom_call" | custom-call | tf_op jit(solution)/shard_map/pallas_call | solution.py:127
  (14 shorter events, 0.0 us)
Async XLA Ops:
  0.0 5.9 %collective-permute-start.3 = (bf16[1,16,256,256]{3,2,1,0:T(8,128)(2,1)}, bf16[1,16,256,256]{3,2,1,0:T(8,128)(2,1)S(1)}, u32[]{:S(2)}, u32[]{:S(2)}) collective-permute-start(bf16[1,16,256,256]{3,2,1,0:T(8,128)(2,1)} %refs_6_.4), channel_id=1, source_target_pairs={{0,1},{1,0},{2,3},{3,2},{4,5},{5,4},{6,7},{7,6},{8,9},{9,8},{10,11... | collective-permute-start | bytes 6291464 | tf_op jit(solution)/shard_map/ppermute | solution.py:138
  0.0 48.3 %collective-permute-start.4 = (bf16[1,16,256,256]{3,2,1,0:T(8,128)(2,1)}, bf16[1,16,256,256]{3,2,1,0:T(8,128)(2,1)S(1)}, u32[]{:S(2)}, u32[]{:S(2)}) collective-permute-start(bf16[1,16,256,256]{3,2,1,0:T(8,128)(2,1)} %refs_6_.4), channel_id=1, source_target_pairs={{0,2},{1,3},{2,0},{3,1},{4,6},{5,7},{6,4},{7,5},{8,10},{9,11},{10,... | collective-permute-start | bytes 6291464 | tf_op jit(solution)/shard_map/ppermute | solution.py:138
  1.5 4.4 %collective-permute-start.2 = (bf16[8,1,256,256]{3,2,1,0:T(8,128)(2,1)}, bf16[8,1,256,256]{3,2,1,0:T(8,128)(2,1)S(1)}, u32[]{:S(2)}, u32[]{:S(2)}) collective-permute-start(bf16[8,1,256,256]{3,2,1,0:T(8,128)(2,1)} %refs_0_.9), channel_id=1, source_target_pairs={{0,1},{1,0},{2,3},{3,2},{4,5},{5,4},{6,7},{7,6},{8,9},{9,8},{10,11... | collective-permute-start | bytes 3145736 | tf_op jit(solution)/shard_map/ppermute | solution.py:138
  1.7 27.4 %collective-permute-start.1 = (bf16[8,1,256,256]{3,2,1,0:T(8,128)(2,1)}, bf16[8,1,256,256]{3,2,1,0:T(8,128)(2,1)S(1)}, u32[]{:S(2)}, u32[]{:S(2)}) collective-permute-start(bf16[8,1,256,256]{3,2,1,0:T(8,128)(2,1)} %refs_6_.3), channel_id=1, source_target_pairs={{4,8},{5,9},{6,10},{7,11},{8,4},{9,5},{10,6},{11,7},{20,24},{21,25... | collective-permute-start | bytes 3145736 | tf_op jit(solution)/shard_map/ppermute | solution.py:138
  4.1 25.3 %collective-permute-start = (bf16[8,1,256,256]{3,2,1,0:T(8,128)(2,1)}, bf16[8,1,256,256]{3,2,1,0:T(8,128)(2,1)S(1)}, u32[]{:S(2)}, u32[]{:S(2)}) collective-permute-start(bf16[8,1,256,256]{3,2,1,0:T(8,128)(2,1)} %refs_6_.3), channel_id=1, source_target_pairs={{0,4},{1,5},{2,6},{3,7},{4,0},{5,1},{6,2},{7,3},{8,12},{9,13},{10,... | collective-permute-start | bytes 3145736 | tf_op jit(solution)/shard_map/ppermute | solution.py:138
  5.9 1.6 %copy-start = (bf16[1,16,256,256]{3,2,1,0:T(8,128)(2,1)S(1)}, bf16[1,16,256,256]{3,2,1,0:T(8,128)(2,1)}, u32[]{:S(2)}) copy-start(bf16[1,16,256,256]{3,2,1,0:T(8,128)(2,1)} %refs_6_.4) | copy-start | bytes 6291460
  7.5 1.2 copy-start.2
  8.7 1.2 copy-start.4
  9.9 0.7 copy-start.6
  29.4 25.4 %collective-permute-start.6 = (bf16[8,1,256,256]{3,2,1,0:T(8,128)(2,1)S(1)}, bf16[8,1,256,256]{3,2,1,0:T(8,128)(2,1)S(1)}, u32[]{:S(2)}, u32[]{:S(2)}) collective-permute-start(bf16[8,1,256,256]{3,2,1,0:T(8,128)(2,1)S(1)} %collective-permute-done.1.refs_10_), channel_id=1, source_target_pairs={{4,0},{5,1},{6,2},{7,3},{8,12},{9,13},{10,14},{11,15},{20,16},{21,... | collective-permute-start | bytes 3145736 | tf_op jit(solution)/shard_map/ppermute | solution.py:138
  31.7 26.1 %collective-permute-start.7 = (bf16[8,1,256,256]{3,2,1,0:T(8,128)(2,1)S(1)}, bf16[8,1,256,256]{3,2,1,0:T(8,128)(2,1)S(1)}, u32[]{:S(2)}, u32[]{:S(2)}) collective-permute-start(bf16[8,1,256,256]{3,2,1,0:T(8,128)(2,1)S(1)} %collective-permute-done.refs_4_.refs_6_), channel_id=1, source_target_pairs={{4,8},{5,9},{6,10},{7,11},{8,4},{9,5},{10,6},{11,7},{20,24},{21,25... | collective-permute-start | bytes 3145736 | tf_op jit(solution)/shard_map/ppermute | solution.py:138
  48.3 31.5 %collective-permute-start.13 = (bf16[1,16,256,256]{3,2,1,0:T(8,128)(2,1)S(1)}, bf16[1,16,256,256]{3,2,1,0:T(8,128)(2,1)S(1)}, u32[]{:S(2)}, u32[]{:S(2)}) collective-permute-start(bf16[1,16,256,256]{3,2,1,0:T(8,128)(2,1)S(1)} %collective-permute-done.4.refs_4_.refs_8_), channel_id=1, source_target_pairs={{0,1},{1,0},{2,3},{3,2},{4,5},{5,4},{6,7},{7,6},{8,9},{9,8},{10,11... | collective-permute-start | bytes 6291464 | tf_op jit(solution)/shard_map/ppermute | solution.py:138
  50.1 9.6 %collective-permute-start.8 = (bf16[2,256,256]{2,1,0:T(8,128)(2,1)S(1)}, bf16[2,256,256]{2,1,0:T(8,128)(2,1)S(1)}, u32[]{:S(2)}, u32[]{:S(2)}) collective-permute-start(bf16[2,256,256]{2,1,0:T(8,128)(2,1)S(1)} %shard_map.49), channel_id=1, source_target_pairs={{0,4},{1,5},{2,6},{3,7},{4,0},{5,1},{6,2},{7,3},{8,12},{9,13},{10,... | collective-permute-start | bytes 786440 | tf_op jit(solution)/shard_map/ppermute | solution.py:138
  51.8 14.8 %collective-permute-start.5 = (bf16[4,1,256,256]{3,2,1,0:T(8,128)(2,1)S(1)}, bf16[4,1,256,256]{3,2,1,0:T(8,128)(2,1)S(1)}, u32[]{:S(2)}, u32[]{:S(2)}) collective-permute-start(bf16[4,1,256,256]{3,2,1,0:T(8,128)(2,1)S(1)} %get-tuple-element.26), channel_id=1, source_target_pairs={{0,2},{1,3},{2,0},{3,1},{4,6},{5,7},{6,4},{7,5},{8,10},{9,11},{10,... | collective-permute-start | bytes 1572872 | tf_op jit(solution)/shard_map/ppermute | solution.py:138
  59.7 21.9 %copy-start.1 = (bf16[1,16,256,256]{3,2,1,0:T(8,128)(2,1)S(1)}, bf16[1,16,256,256]{3,2,1,0:T(8,128)(2,1)}, u32[]{:S(2)}) copy-start(bf16[1,16,256,256]{3,2,1,0:T(8,128)(2,1)} %refs_6_.4) | copy-start | bytes 6291460
  59.8 21.9 %copy-start.3 = (bf16[8,1,256,256]{3,2,1,0:T(8,128)(2,1)S(1)}, bf16[8,1,256,256]{3,2,1,0:T(8,128)(2,1)}, u32[]{:S(2)}) copy-start(bf16[8,1,256,256]{3,2,1,0:T(8,128)(2,1)} %refs_0_.9) | copy-start | bytes 3145732
  59.8 17.3 %collective-permute-start.9 = (bf16[4,1,256,256]{3,2,1,0:T(8,128)(2,1)S(1)}, bf16[4,1,256,256]{3,2,1,0:T(8,128)(2,1)S(1)}, u32[]{:S(2)}, u32[]{:S(2)}) collective-permute-start(bf16[4,1,256,256]{3,2,1,0:T(8,128)(2,1)S(1)} %get-tuple-element.32), channel_id=1, source_target_pairs={{0,2},{1,3},{2,0},{3,1},{4,6},{5,7},{6,4},{7,5},{8,10},{9,11},{10,... | collective-permute-start | bytes 1572872 | tf_op jit(solution)/shard_map/ppermute | solution.py:138
  60.4 12.5 %collective-permute-start.10 = (bf16[2,256,256]{2,1,0:T(8,128)(2,1)S(1)}, bf16[2,256,256]{2,1,0:T(8,128)(2,1)S(1)}, u32[]{:S(2)}, u32[]{:S(2)}) collective-permute-start(bf16[2,256,256]{2,1,0:T(8,128)(2,1)S(1)} %shard_map.48), channel_id=1, source_target_pairs={{0,8},{1,9},{2,10},{3,11},{4,12},{5,13},{6,14},{7,15},{8,0},{9,1},... | collective-permute-start | bytes 786440 | tf_op jit(solution)/shard_map/ppermute | solution.py:138
  63.3 34.4 %collective-permute-start.16 = (bf16[8,1,256,256]{3,2,1,0:T(8,128)(2,1)S(1)}, bf16[8,1,256,256]{3,2,1,0:T(8,128)(2,1)S(1)}, u32[]{:S(2)}, u32[]{:S(2)}) collective-permute-start(bf16[8,1,256,256]{3,2,1,0:T(8,128)(2,1)S(1)} %collective-permute-done.7.refs_5_.refs_7_), channel_id=1, source_target_pairs={{4,0},{5,1},{6,2},{7,3},{8,12},{9,13},{10,14},{11,15},{20,16},{21,... | collective-permute-start | bytes 3145736 | tf_op jit(solution)/shard_map/ppermute | solution.py:138
  77.1 1.9 %collective-permute-start.11 = (bf16[4,1,256,256]{3,2,1,0:T(8,128)(2,1)S(1)}, bf16[4,1,256,256]{3,2,1,0:T(8,128)(2,1)S(1)}, u32[]{:S(2)}, u32[]{:S(2)}) collective-permute-start(bf16[4,1,256,256]{3,2,1,0:T(8,128)(2,1)S(1)} %collective-permute-done.5.refs_0_.refs_2_), channel_id=1, source_target_pairs={{0,1},{1,0},{2,3},{3,2},{4,5},{5,4},{6,7},{7,6},{8,9},{9,8},{10,11... | collective-permute-start | bytes 1572872 | tf_op jit(solution)/shard_map/ppermute | solution.py:138
  77.1 2.7 %collective-permute-start.12 = (bf16[4,1,256,256]{3,2,1,0:T(8,128)(2,1)S(1)}, bf16[4,1,256,256]{3,2,1,0:T(8,128)(2,1)S(1)}, u32[]{:S(2)}, u32[]{:S(2)}) collective-permute-start(bf16[4,1,256,256]{3,2,1,0:T(8,128)(2,1)S(1)} %collective-permute-done.9.refs_1_.refs_3_), channel_id=1, source_target_pairs={{0,1},{1,0},{2,3},{3,2},{4,5},{5,4},{6,7},{7,6},{8,9},{9,8},{10,11... | collective-permute-start | bytes 1572872 | tf_op jit(solution)/shard_map/ppermute | solution.py:138
  86.5 16.6 %copy-start.5 = (bf16[8,1,256,256]{3,2,1,0:T(8,128)(2,1)S(1)}, bf16[8,1,256,256]{3,2,1,0:T(8,128)(2,1)}, u32[]{:S(2)}) copy-start(bf16[8,1,256,256]{3,2,1,0:T(8,128)(2,1)} %refs_6_.3) | copy-start | bytes 3145732
  86.5 16.6 %collective-permute-start.14 = (bf16[2,256,256]{2,1,0:T(8,128)(2,1)S(1)}, bf16[2,256,256]{2,1,0:T(8,128)(2,1)S(1)}, u32[]{:S(2)}, u32[]{:S(2)}) collective-permute-start(bf16[2,256,256]{2,1,0:T(8,128)(2,1)S(1)} %shard_map.52), channel_id=1, source_target_pairs={{0,4},{1,5},{2,6},{3,7},{4,0},{5,1},{6,2},{7,3},{8,12},{9,13},{10,... | collective-permute-start | bytes 786440 | tf_op jit(solution)/shard_map/ppermute | solution.py:138
  87.0 16.1 %collective-permute-start.15 = (bf16[2,256,256]{2,1,0:T(8,128)(2,1)S(1)}, bf16[2,256,256]{2,1,0:T(8,128)(2,1)S(1)}, u32[]{:S(2)}, u32[]{:S(2)}) collective-permute-start(bf16[2,256,256]{2,1,0:T(8,128)(2,1)S(1)} %shard_map.50), channel_id=1, source_target_pairs={{0,8},{1,9},{2,10},{3,11},{4,12},{5,13},{6,14},{7,15},{8,0},{9,1},... | collective-permute-start | bytes 786440 | tf_op jit(solution)/shard_map/ppermute | solution.py:138
  87.4 36.9 %collective-permute-start.18 = (bf16[4,256,256]{2,1,0:T(8,128)(2,1)S(1)}, bf16[4,256,256]{2,1,0:T(8,128)(2,1)S(1)}, u32[]{:S(2)}, u32[]{:S(2)}) collective-permute-start(bf16[4,256,256]{2,1,0:T(8,128)(2,1)S(1)} %shard_map.51), channel_id=1, source_target_pairs={{4,8},{5,9},{6,10},{7,11},{8,4},{9,5},{10,6},{11,7},{20,24},{21,25... | collective-permute-start | bytes 1572872 | tf_op jit(solution)/shard_map/ppermute | solution.py:138
  100.6 23.7 %collective-permute-start.17 = (bf16[4,256,256]{2,1,0:T(8,128)(2,1)S(1)}, bf16[4,256,256]{2,1,0:T(8,128)(2,1)S(1)}, u32[]{:S(2)}, u32[]{:S(2)}) collective-permute-start(bf16[4,256,256]{2,1,0:T(8,128)(2,1)S(1)} %shard_map.54), channel_id=1, source_target_pairs={{0,12},{1,13},{2,14},{3,15},{12,0},{13,1},{14,2},{15,3},{16,28},{1... | collective-permute-start | bytes 1572872 | tf_op jit(solution)/shard_map/ppermute | solution.py:138

commit v9 on v8

--- a/solution.py
+++ b/solution.py
@@ -175,19 +175,18 @@
     across_low = exchange(x_low, 1, every)
     across_high = exchange(x_high, 1, every)
     other = ([(x_low, x_high), (across_low, across_high)], [(x_psi,), (across_psi,)])
+    both = (own[0] + other[0], own[1] + other[1])
     other_2 = products(2, *other, (second, far_in))
     other_sent_2 = exchange(other_2, 8, every)
-    both = (own[0] + other[0], own[1] + other[1])
     last_middle = products(3, *both, (middle,))
     sent_middle = exchange(last_middle, 12, inner)
-    near, other_2, last_middle = lax.optimization_barrier((near, other_2, last_middle))
     other_1 = products(1, *other, (near,))
     other_sent_1 = exchange(other_1, 4, every)
 
-    third, other_1 = lax.optimization_barrier((third, other_1))
+    third, other_1, other_2, last_middle = lax.optimization_barrier((third, other_1, other_2, last_middle))
     last_third = products(3, *both, (third,))
     sent_third = exchange(last_third, 12, outer)
-    right_last, other_sent_1, other_sent_2 = lax.optimization_barrier((right_env, other_sent_1, other_sent_2))
+    right_last, other_sent_2, other_sent_1 = lax.optimization_barrier((right_env, other_sent_2, other_sent_1))
     other_0 = products(0, *other, (right_last,), flops=10**10)
 
     pieces = [own_0, other_0, sent_1, other_sent_1, sent_2, other_sent_2, sent_third, sent_middle]

time: 126 us -> 122 us (0.968)
  the two profiles are of different devices: /device:TPU:20 before, /device:TPU:0 now
where the time goes in v9:
time: 122 us
  waiting for transfers between devices  73.6 us (60%)
  starting transfers between devices  24.6 us (20%)
  Pallas kernels  18.7 us (15%)
  local copies, waits for them, and re-layouts  4.74 us (4%)
    ppermute x19, waiting for transfers between devices, exchange(): return lax.ppermute(array, 'sec', [(s, s ^ bits) for s in members])  73.6 us
    ppermute x19, starting transfers between devices, exchange(): return lax.ppermute(array, 'sec', [(s, s ^ bits) for s in members])  24.6 us
    pallas_call x8, Pallas kernels, slot(): pl.pallas_call(functools.partial(slot_kernel, step, parts, len(rights)),...  17.2 us
    unnamed x14, local copies, waits for them, and re-layouts  4.74 us
  transfers between devices with their start and end apart: 19, of which 11 were waited for; matrix products, arithmetic and copies ran while one was open for 0% of the time, Pallas kernels for 14%

profile of v9, /device:TPU:0, one launch (start us, length us, event | category | flops | bytes accessed | tf_op | source)
XLA Modules:
  0.0 122.0 jit_solution(15437422259200116612)
XLA Ops:
  0.0 0.5 collective-permute-start.3
  0.5 2.5 %collective-permute-start.4 = (bf16[1,16,256,256]{3,2,1,0:T(8,128)(2,1)}, bf16[1,16,256,256]{3,2,1,0:T(8,128)(2,1)S(1)}, u32[]{:S(2)}, u32[]{:S(2)}) collective-permute-start(bf16[1,16,256,256]{3,2,1,0:T(8,128)(2,1)} %refs_6_.4), channel_id=1, source_target_pairs={{0,2},{1,3},{2,0},{3,1},{4,6},{5,7},{6,4},{7,5},{8,10},{9,11},{10,... | collective-permute-start | bytes 6291464 | tf_op jit(solution)/shard_map/ppermute | solution.py:138
  2.9 0.2 collective-permute-start.2
  3.2 0.7 collective-permute-start.1
  3.9 4.4 %collective-permute-start = (bf16[8,1,256,256]{3,2,1,0:T(8,128)(2,1)}, bf16[8,1,256,256]{3,2,1,0:T(8,128)(2,1)S(1)}, u32[]{:S(2)}, u32[]{:S(2)}) collective-permute-start(bf16[8,1,256,256]{3,2,1,0:T(8,128)(2,1)} %refs_6_.2), channel_id=1, source_target_pairs={{0,4},{1,5},{2,6},{3,7},{4,0},{5,1},{6,2},{7,3},{8,12},{9,13},{10,... | collective-permute-start | bytes 3145736 | tf_op jit(solution)/shard_map/ppermute | solution.py:138
  8.3 1.6 %copy-done = bf16[1,16,256,256]{3,2,1,0:T(8,128)(2,1)S(1)} copy-done((bf16[1,16,256,256]{3,2,1,0:T(8,128)(2,1)S(1)}, bf16[1,16,256,256]{3,2,1,0:T(8,128)(2,1)}, u32[]{:S(2)}) %copy-start) | copy-done | bytes 2097176
  9.9 1.2 %copy-done.2 = bf16[8,1,256,256]{3,2,1,0:T(8,128)(2,1)S(1)} copy-done((bf16[8,1,256,256]{3,2,1,0:T(8,128)(2,1)S(1)}, bf16[8,1,256,256]{3,2,1,0:T(8,128)(2,1)}, u32[]{:S(2)}) %copy-start.2) | copy-done | bytes 1048600
  11.1 1.2 %copy-done.4 = bf16[8,1,256,256]{3,2,1,0:T(8,128)(2,1)S(1)} copy-done((bf16[8,1,256,256]{3,2,1,0:T(8,128)(2,1)S(1)}, bf16[8,1,256,256]{3,2,1,0:T(8,128)(2,1)}, u32[]{:S(2)}) %copy-start.4) | copy-done | bytes 1048600
  12.3 0.7 copy-done.6
  13.0 1.9 %shard_map.46.refs_0_ = bf16[2,256,256]{2,1,0:T(8,128)(2,1)S(1)} custom-call(s32[8,16]{1,0:T(8,128)S(1)} %copy-done.6, bf16[8,1,256,256]{3,2,1,0:T(8,128)(2,1)S(1)} %copy-done.2, bf16[8,1,256,256]{3,2,1,0:T(8,128)(2,1)S(1)} %collective-permute-done.2.refs_1_, bf16[1,16,256,256]{3,2,1,0:T(8,128)(2,1)S(1)} %copy-done, ...), custom_call_target="tpu_custom_call" | custom-call | flops 1 | bytes 1 | tf_op jit(solution)/shard_map/pallas_call | solution.py:62
  14.9 0.0 collective-permute-done.1.refs_10_
  14.9 16.9 %collective-permute-done.refs_4_.refs_6_ = bf16[8,1,256,256]{3,2,1,0:T(8,128)(2,1)S(1)} collective-permute-done((bf16[8,1,256,256]{3,2,1,0:T(8,128)(2,1)}, bf16[8,1,256,256]{3,2,1,0:T(8,128)(2,1)S(1)}, u32[]{:S(2)}, u32[]{:S(2)}) %collective-permute-start) | collective-permute-done | bytes 1048608 | tf_op jit(solution)/shard_map/ppermute | solution.py:138
  31.8 1.3 %collective-permute-start.6 = (bf16[8,1,256,256]{3,2,1,0:T(8,128)(2,1)S(1)}, bf16[8,1,256,256]{3,2,1,0:T(8,128)(2,1)S(1)}, u32[]{:S(2)}, u32[]{:S(2)}) collective-permute-start(bf16[8,1,256,256]{3,2,1,0:T(8,128)(2,1)S(1)} %collective-permute-done.1.refs_10_), channel_id=1, source_target_pairs={{4,0},{5,1},{6,2},{7,3},{8,12},{9,13},{10,14},{11,15},{20,16},{21,... | collective-permute-start | bytes 3145736 | tf_op jit(solution)/shard_map/ppermute | solution.py:138
  33.1 0.7 collective-permute-start.7
  33.9 0.1 shard_map.47
  33.9 15.5 %collective-permute-done.4.refs_4_.refs_8_ = bf16[1,16,256,256]{3,2,1,0:T(8,128)(2,1)S(1)} collective-permute-done((bf16[1,16,256,256]{3,2,1,0:T(8,128)(2,1)}, bf16[1,16,256,256]{3,2,1,0:T(8,128)(2,1)S(1)}, u32[]{:S(2)}, u32[]{:S(2)}) %collective-permute-start.4) | collective-permute-done | bytes 2097184 | tf_op jit(solution)/shard_map/ppermute | solution.py:138
  49.5 0.0 collective-permute-start.13
  49.5 1.9 %shard_map.49 = bf16[2,256,256]{2,1,0:T(8,128)(2,1)S(1)} custom-call(s32[8,16]{1,0:T(8,128)S(1)} %copy-done.6, bf16[8,1,256,256]{3,2,1,0:T(8,128)(2,1)S(1)} %copy-done.2, bf16[8,1,256,256]{3,2,1,0:T(8,128)(2,1)S(1)} %collective-permute-done.2.refs_1_, bf16[1,16,256,256]{3,2,1,0:T(8,128)(2,1)S(1)} %copy-done, ...), custom_call_target="tpu_custom_call" | custom-call | flops 1 | bytes 1 | tf_op jit(solution)/shard_map/pallas_call | solution.py:62
  51.3 1.9 %collective-permute-start.8 = (bf16[2,256,256]{2,1,0:T(8,128)(2,1)S(1)}, bf16[2,256,256]{2,1,0:T(8,128)(2,1)S(1)}, u32[]{:S(2)}, u32[]{:S(2)}) collective-permute-start(bf16[2,256,256]{2,1,0:T(8,128)(2,1)S(1)} %shard_map.49), channel_id=1, source_target_pairs={{0,4},{1,5},{2,6},{3,7},{4,0},{5,1},{6,2},{7,3},{8,12},{9,13},{10,... | collective-permute-start | bytes 786440 | tf_op jit(solution)/shard_map/ppermute | solution.py:138
  53.2 1.5 %collective-permute-start.5 = (bf16[4,1,256,256]{3,2,1,0:T(8,128)(2,1)S(1)}, bf16[4,1,256,256]{3,2,1,0:T(8,128)(2,1)S(1)}, u32[]{:S(2)}, u32[]{:S(2)}) collective-permute-start(bf16[4,1,256,256]{3,2,1,0:T(8,128)(2,1)S(1)} %get-tuple-element.25), channel_id=1, source_target_pairs={{0,2},{1,3},{2,0},{3,1},{4,6},{5,7},{6,4},{7,5},{8,10},{9,11},{10,... | collective-permute-start | bytes 1572872 | tf_op jit(solution)/shard_map/ppermute | solution.py:138
  54.7 5.1 %collective-permute-done.6.refs_4_.refs_6_ = bf16[8,1,256,256]{3,2,1,0:T(8,128)(2,1)S(1)} collective-permute-done((bf16[8,1,256,256]{3,2,1,0:T(8,128)(2,1)S(1)}, bf16[8,1,256,256]{3,2,1,0:T(8,128)(2,1)S(1)}, u32[]{:S(2)}, u32[]{:S(2)}) %collective-permute-start.6) | collective-permute-done | bytes 1048608 | tf_op jit(solution)/shard_map/ppermute | solution.py:138
  59.8 1.9 %shard_map.48 = bf16[2,256,256]{2,1,0:T(8,128)(2,1)S(1)} custom-call(s32[8,16]{1,0:T(8,128)S(1)} %copy-done.6, bf16[8,1,256,256]{3,2,1,0:T(8,128)(2,1)S(1)} %copy-done.2, bf16[8,1,256,256]{3,2,1,0:T(8,128)(2,1)S(1)} %collective-permute-done.2.refs_1_, bf16[1,16,256,256]{3,2,1,0:T(8,128)(2,1)S(1)} %copy-done, ...), custom_call_target="tpu_custom_call" | custom-call | flops 1 | bytes 1 | tf_op jit(solution)/shard_map/pallas_call | solution.py:62
  61.7 2.1 %collective-permute-done.8.refs_2_ = bf16[2,256,256]{2,1,0:T(8,128)(2,1)S(1)} collective-permute-done((bf16[2,256,256]{2,1,0:T(8,128)(2,1)S(1)}, bf16[2,256,256]{2,1,0:T(8,128)(2,1)S(1)}, u32[]{:S(2)}, u32[]{:S(2)}) %collective-permute-start.8) | collective-permute-done | bytes 262176 | tf_op jit(solution)/shard_map/ppermute | solution.py:138
  63.9 0.5 collective-permute-start.9
  64.4 0.0 collective-permute-start.10
  64.5 1.3 %collective-permute-start.16 = (bf16[8,1,256,256]{3,2,1,0:T(8,128)(2,1)S(1)}, bf16[8,1,256,256]{3,2,1,0:T(8,128)(2,1)S(1)}, u32[]{:S(2)}, u32[]{:S(2)}) collective-permute-start(bf16[8,1,256,256]{3,2,1,0:T(8,128)(2,1)S(1)} %collective-permute-done.7.refs_5_.refs_7_), channel_id=1, source_target_pairs={{4,0},{5,1},{6,2},{7,3},{8,12},{9,13},{10,14},{11,15},{20,16},{21,... | collective-permute-start | bytes 3145736 | tf_op jit(solution)/shard_map/ppermute | solution.py:138
  65.7 2.2 %collective-permute-done.5.refs_0_.refs_2_ = bf16[4,1,256,256]{3,2,1,0:T(8,128)(2,1)S(1)} collective-permute-done((bf16[4,1,256,256]{3,2,1,0:T(8,128)(2,1)S(1)}, bf16[4,1,256,256]{3,2,1,0:T(8,128)(2,1)S(1)}, u32[]{:S(2)}, u32[]{:S(2)}) %collective-permute-start.5) | collective-permute-done | bytes 524320 | tf_op jit(solution)/shard_map/ppermute | solution.py:138
  68.0 9.5 %collective-permute-done.10.refs_4_ = bf16[2,256,256]{2,1,0:T(8,128)(2,1)S(1)} collective-permute-done((bf16[2,256,256]{2,1,0:T(8,128)(2,1)S(1)}, bf16[2,256,256]{2,1,0:T(8,128)(2,1)S(1)}, u32[]{:S(2)}, u32[]{:S(2)}) %collective-permute-start.10) | collective-permute-done | bytes 262176 | tf_op jit(solution)/shard_map/ppermute | solution.py:138
  77.5 1.0 collective-permute-done.9.refs_1_.refs_3_
  78.5 0.5 collective-permute-start.12
  79.0 1.4 %collective-permute-done.11.refs_2_.refs_4_ = bf16[4,1,256,256]{3,2,1,0:T(8,128)(2,1)S(1)} collective-permute-done((bf16[4,1,256,256]{3,2,1,0:T(8,128)(2,1)S(1)}, bf16[4,1,256,256]{3,2,1,0:T(8,128)(2,1)S(1)}, u32[]{:S(2)}, u32[]{:S(2)}) %collective-permute-start.11) | collective-permute-done | bytes 524320 | tf_op jit(solution)/shard_map/ppermute | solution.py:138
  80.4 0.7 collective-permute-done.12.refs_3_.refs_5_
  81.2 0.0 collective-permute-done.13.refs_5_.refs_9_
  81.2 1.9 %shard_map.50 = bf16[2,256,256]{2,1,0:T(8,128)(2,1)S(1)} custom-call(s32[8,16]{1,0:T(8,128)S(1)} %copy-done.6, bf16[4,1,256,256]{3,2,1,0:T(8,128)(2,1)S(1)} %collective-permute-done.5.refs_0_.refs_2_, bf16[4,1,256,256]{3,2,1,0:T(8,128)(2,1)S(1)} %collective-permute-done.9.refs_1_.refs_3_, ...), custom_call_target="tpu_custom_call" | custom-call | flops 1 | bytes 1 | tf_op jit(solution)/shard_map/pallas_call | solution.py:62
  83.1 0.0 copy-start.1
  83.1 0.0 copy-start.3
  83.1 2.7 %collective-permute-start.14 = (bf16[2,256,256]{2,1,0:T(8,128)(2,1)S(1)}, bf16[2,256,256]{2,1,0:T(8,128)(2,1)S(1)}, u32[]{:S(2)}, u32[]{:S(2)}) collective-permute-start(bf16[2,256,256]{2,1,0:T(8,128)(2,1)S(1)} %shard_map.50), channel_id=1, source_target_pairs={{0,8},{1,9},{2,10},{3,11},{4,12},{5,13},{6,14},{7,15},{8,0},{9,1},... | collective-permute-start | bytes 786440 | tf_op jit(solution)/shard_map/ppermute | solution.py:138
  85.8 1.9 %shard_map.51 = bf16[2,256,256]{2,1,0:T(8,128)(2,1)S(1)} custom-call(s32[8,16]{1,0:T(8,128)S(1)} %copy-done.6, bf16[4,1,256,256]{3,2,1,0:T(8,128)(2,1)S(1)} %collective-permute-done.5.refs_0_.refs_2_, bf16[4,1,256,256]{3,2,1,0:T(8,128)(2,1)S(1)} %collective-permute-done.9.refs_1_.refs_3_, ...), custom_call_target="tpu_custom_call" | custom-call | flops 1 | bytes 1 | tf_op jit(solution)/shard_map/pallas_call | solution.py:62
  87.7 0.5 collective-permute-start.15
  88.2 3.0 %shard_map.53 = bf16[4,256,256]{2,1,0:T(8,128)(2,1)S(1)} custom-call(s32[8,16]{1,0:T(8,128)S(1)} %copy-done.6, bf16[8,1,256,256]{3,2,1,0:T(8,128)(2,1)S(1)} %copy-done.3, bf16[8,1,256,256]{3,2,1,0:T(8,128)(2,1)S(1)} %collective-permute-done.2.refs_1_, bf16[4,1,256,256]{3,2,1,0:T(8,128)(2,1)S(1)} %collective-permute-done.5.refs_0_.refs_2_, ...), custom_call_target="tpu_custom_call" | custom-call | flops 1 | bytes 1 | tf_op jit(solution)/shard_map/pallas_call | solution.py:62
  91.1 0.0 copy-start.5
  91.2 1.0 collective-permute-start.18
  92.2 11.3 %collective-permute-done.16.refs_10_ = bf16[8,1,256,256]{3,2,1,0:T(8,128)(2,1)S(1)} collective-permute-done((bf16[8,1,256,256]{3,2,1,0:T(8,128)(2,1)S(1)}, bf16[8,1,256,256]{3,2,1,0:T(8,128)(2,1)S(1)}, u32[]{:S(2)}, u32[]{:S(2)}) %collective-permute-start.16) | collective-permute-done | bytes 1048608 | tf_op jit(solution)/shard_map/ppermute | solution.py:138
  103.5 3.0 %shard_map.54 = bf16[4,256,256]{2,1,0:T(8,128)(2,1)S(1)} custom-call(s32[8,16]{1,0:T(8,128)S(1)} %copy-done.6, bf16[8,1,256,256]{3,2,1,0:T(8,128)(2,1)S(1)} %copy-done.3, bf16[8,1,256,256]{3,2,1,0:T(8,128)(2,1)S(1)} %collective-permute-done.2.refs_1_, bf16[4,1,256,256]{3,2,1,0:T(8,128)(2,1)S(1)} %collective-permute-done.5.refs_0_.refs_2_, ...), custom_call_target="tpu_custom_call" | custom-call | flops 1 | bytes 1 | tf_op jit(solution)/shard_map/pallas_call | solution.py:62
  106.5 4.4 %collective-permute-start.17 = (bf16[4,256,256]{2,1,0:T(8,128)(2,1)S(1)}, bf16[4,256,256]{2,1,0:T(8,128)(2,1)S(1)}, u32[]{:S(2)}, u32[]{:S(2)}) collective-permute-start(bf16[4,256,256]{2,1,0:T(8,128)(2,1)S(1)} %shard_map.54), channel_id=1, source_target_pairs={{0,12},{1,13},{2,14},{3,15},{12,0},{13,1},{14,2},{15,3},{16,28},{1... | collective-permute-start | bytes 1572872 | tf_op jit(solution)/shard_map/ppermute | solution.py:138
  110.9 1.9 %shard_map.52.refs_1_ = bf16[2,256,256]{2,1,0:T(8,128)(2,1)S(1)} custom-call(s32[8,16]{1,0:T(8,128)S(1)} %copy-done.6, bf16[4,1,256,256]{3,2,1,0:T(8,128)(2,1)S(1)} %collective-permute-done.5.refs_0_.refs_2_, bf16[4,1,256,256]{3,2,1,0:T(8,128)(2,1)S(1)} %collective-permute-done.9.refs_1_.refs_3_, ...), custom_call_target="tpu_custom_call" | custom-call | flops 10000000000 | bytes 1 | tf_op jit(solution)/shard_map/pallas_call | solution.py:62
  112.8 7.6 %collective-permute-done.17.refs_6_ = bf16[4,256,256]{2,1,0:T(8,128)(2,1)S(1)} collective-permute-done((bf16[4,256,256]{2,1,0:T(8,128)(2,1)S(1)}, bf16[4,256,256]{2,1,0:T(8,128)(2,1)S(1)}, u32[]{:S(2)}, u32[]{:S(2)}) %collective-permute-start.17) | collective-permute-done | bytes 524320 | tf_op jit(solution)/shard_map/ppermute | solution.py:138
  120.4 1.4 %shard_map.55 = bf16[16,256,256]{2,1,0:T(8,128)(2,1)} custom-call(bf16[2,256,256]{2,1,0:T(8,128)(2,1)S(1)} %shard_map.46.refs_0_, bf16[2,256,256]{2,1,0:T(8,128)(2,1)S(1)} %shard_map.52.refs_1_, bf16[2,256,256]{2,1,0:T(8,128)(2,1)S(1)} %collective-permute-done.8.refs_2_, bf16[2,256,256]{2,1,0:T(8,128)(2,1)S(1)} %collective-permute-done.15.refs_3_, ...), custom_call_target="tpu_custom_call" | custom-call | tf_op jit(solution)/shard_map/pallas_call | solution.py:127
  (14 shorter events, 0.0 us)
Async XLA Ops:
  0.0 8.3 %collective-permute-start.3 = (bf16[1,16,256,256]{3,2,1,0:T(8,128)(2,1)}, bf16[1,16,256,256]{3,2,1,0:T(8,128)(2,1)S(1)}, u32[]{:S(2)}, u32[]{:S(2)}) collective-permute-start(bf16[1,16,256,256]{3,2,1,0:T(8,128)(2,1)} %refs_6_.4), channel_id=1, source_target_pairs={{0,1},{1,0},{2,3},{3,2},{4,5},{5,4},{6,7},{7,6},{8,9},{9,8},{10,11... | collective-permute-start | bytes 6291464 | tf_op jit(solution)/shard_map/ppermute | solution.py:138
  0.5 49.0 %collective-permute-start.4 = (bf16[1,16,256,256]{3,2,1,0:T(8,128)(2,1)}, bf16[1,16,256,256]{3,2,1,0:T(8,128)(2,1)S(1)}, u32[]{:S(2)}, u32[]{:S(2)}) collective-permute-start(bf16[1,16,256,256]{3,2,1,0:T(8,128)(2,1)} %refs_6_.4), channel_id=1, source_target_pairs={{0,2},{1,3},{2,0},{3,1},{4,6},{5,7},{6,4},{7,5},{8,10},{9,11},{10,... | collective-permute-start | bytes 6291464 | tf_op jit(solution)/shard_map/ppermute | solution.py:138
  2.9 5.4 %collective-permute-start.2 = (bf16[8,1,256,256]{3,2,1,0:T(8,128)(2,1)}, bf16[8,1,256,256]{3,2,1,0:T(8,128)(2,1)S(1)}, u32[]{:S(2)}, u32[]{:S(2)}) collective-permute-start(bf16[8,1,256,256]{3,2,1,0:T(8,128)(2,1)} %refs_0_.9), channel_id=1, source_target_pairs={{0,1},{1,0},{2,3},{3,2},{4,5},{5,4},{6,7},{7,6},{8,9},{9,8},{10,11... | collective-permute-start | bytes 3145736 | tf_op jit(solution)/shard_map/ppermute | solution.py:138
  3.2 11.7 %collective-permute-start.1 = (bf16[8,1,256,256]{3,2,1,0:T(8,128)(2,1)}, bf16[8,1,256,256]{3,2,1,0:T(8,128)(2,1)S(1)}, u32[]{:S(2)}, u32[]{:S(2)}) collective-permute-start(bf16[8,1,256,256]{3,2,1,0:T(8,128)(2,1)} %refs_6_.2), channel_id=1, source_target_pairs={{4,8},{5,9},{6,10},{7,11},{8,4},{9,5},{10,6},{11,7},{20,24},{21,25... | collective-permute-start | bytes 3145736 | tf_op jit(solution)/shard_map/ppermute | solution.py:138
  3.9 27.9 %collective-permute-start = (bf16[8,1,256,256]{3,2,1,0:T(8,128)(2,1)}, bf16[8,1,256,256]{3,2,1,0:T(8,128)(2,1)S(1)}, u32[]{:S(2)}, u32[]{:S(2)}) collective-permute-start(bf16[8,1,256,256]{3,2,1,0:T(8,128)(2,1)} %refs_6_.2), channel_id=1, source_target_pairs={{0,4},{1,5},{2,6},{3,7},{4,0},{5,1},{6,2},{7,3},{8,12},{9,13},{10,... | collective-permute-start | bytes 3145736 | tf_op jit(solution)/shard_map/ppermute | solution.py:138
  8.3 1.6 %copy-start = (bf16[1,16,256,256]{3,2,1,0:T(8,128)(2,1)S(1)}, bf16[1,16,256,256]{3,2,1,0:T(8,128)(2,1)}, u32[]{:S(2)}) copy-start(bf16[1,16,256,256]{3,2,1,0:T(8,128)(2,1)} %refs_6_.4) | copy-start | bytes 6291460
  9.9 1.2 %copy-start.2 = (bf16[8,1,256,256]{3,2,1,0:T(8,128)(2,1)S(1)}, bf16[8,1,256,256]{3,2,1,0:T(8,128)(2,1)}, u32[]{:S(2)}) copy-start(bf16[8,1,256,256]{3,2,1,0:T(8,128)(2,1)} %refs_0_.9) | copy-start | bytes 3145732
  11.1 1.2 %copy-start.4 = (bf16[8,1,256,256]{3,2,1,0:T(8,128)(2,1)S(1)}, bf16[8,1,256,256]{3,2,1,0:T(8,128)(2,1)}, u32[]{:S(2)}) copy-start(bf16[8,1,256,256]{3,2,1,0:T(8,128)(2,1)} %refs_6_.2) | copy-start | bytes 3145732
  12.3 0.7 copy-start.6
  31.8 28.0 %collective-permute-start.6 = (bf16[8,1,256,256]{3,2,1,0:T(8,128)(2,1)S(1)}, bf16[8,1,256,256]{3,2,1,0:T(8,128)(2,1)S(1)}, u32[]{:S(2)}, u32[]{:S(2)}) collective-permute-start(bf16[8,1,256,256]{3,2,1,0:T(8,128)(2,1)S(1)} %collective-permute-done.1.refs_10_), channel_id=1, source_target_pairs={{4,0},{5,1},{6,2},{7,3},{8,12},{9,13},{10,14},{11,15},{20,16},{21,... | collective-permute-start | bytes 3145736 | tf_op jit(solution)/shard_map/ppermute | solution.py:138
  33.1 26.7 %collective-permute-start.7 = (bf16[8,1,256,256]{3,2,1,0:T(8,128)(2,1)S(1)}, bf16[8,1,256,256]{3,2,1,0:T(8,128)(2,1)S(1)}, u32[]{:S(2)}, u32[]{:S(2)}) collective-permute-start(bf16[8,1,256,256]{3,2,1,0:T(8,128)(2,1)S(1)} %collective-permute-done.refs_4_.refs_6_), channel_id=1, source_target_pairs={{4,8},{5,9},{6,10},{7,11},{8,4},{9,5},{10,6},{11,7},{20,24},{21,25... | collective-permute-start | bytes 3145736 | tf_op jit(solution)/shard_map/ppermute | solution.py:138
  49.5 31.7 %collective-permute-start.13 = (bf16[1,16,256,256]{3,2,1,0:T(8,128)(2,1)S(1)}, bf16[1,16,256,256]{3,2,1,0:T(8,128)(2,1)S(1)}, u32[]{:S(2)}, u32[]{:S(2)}) collective-permute-start(bf16[1,16,256,256]{3,2,1,0:T(8,128)(2,1)S(1)} %collective-permute-done.4.refs_4_.refs_8_), channel_id=1, source_target_pairs={{0,1},{1,0},{2,3},{3,2},{4,5},{5,4},{6,7},{7,6},{8,9},{9,8},{10,11... | collective-permute-start | bytes 6291464 | tf_op jit(solution)/shard_map/ppermute | solution.py:138
  51.3 12.5 %collective-permute-start.8 = (bf16[2,256,256]{2,1,0:T(8,128)(2,1)S(1)}, bf16[2,256,256]{2,1,0:T(8,128)(2,1)S(1)}, u32[]{:S(2)}, u32[]{:S(2)}) collective-permute-start(bf16[2,256,256]{2,1,0:T(8,128)(2,1)S(1)} %shard_map.49), channel_id=1, source_target_pairs={{0,4},{1,5},{2,6},{3,7},{4,0},{5,1},{6,2},{7,3},{8,12},{9,13},{10,... | collective-permute-start | bytes 786440 | tf_op jit(solution)/shard_map/ppermute | solution.py:138
  53.2 14.8 %collective-permute-start.5 = (bf16[4,1,256,256]{3,2,1,0:T(8,128)(2,1)S(1)}, bf16[4,1,256,256]{3,2,1,0:T(8,128)(2,1)S(1)}, u32[]{:S(2)}, u32[]{:S(2)}) collective-permute-start(bf16[4,1,256,256]{3,2,1,0:T(8,128)(2,1)S(1)} %get-tuple-element.25), channel_id=1, source_target_pairs={{0,2},{1,3},{2,0},{3,1},{4,6},{5,7},{6,4},{7,5},{8,10},{9,11},{10,... | collective-permute-start | bytes 1572872 | tf_op jit(solution)/shard_map/ppermute | solution.py:138
  63.9 14.7 %collective-permute-start.9 = (bf16[4,1,256,256]{3,2,1,0:T(8,128)(2,1)S(1)}, bf16[4,1,256,256]{3,2,1,0:T(8,128)(2,1)S(1)}, u32[]{:S(2)}, u32[]{:S(2)}) collective-permute-start(bf16[4,1,256,256]{3,2,1,0:T(8,128)(2,1)S(1)} %get-tuple-element.31), channel_id=1, source_target_pairs={{0,2},{1,3},{2,0},{3,1},{4,6},{5,7},{6,4},{7,5},{8,10},{9,11},{10,... | collective-permute-start | bytes 1572872 | tf_op jit(solution)/shard_map/ppermute | solution.py:138
  64.4 13.1 %collective-permute-start.10 = (bf16[2,256,256]{2,1,0:T(8,128)(2,1)S(1)}, bf16[2,256,256]{2,1,0:T(8,128)(2,1)S(1)}, u32[]{:S(2)}, u32[]{:S(2)}) collective-permute-start(bf16[2,256,256]{2,1,0:T(8,128)(2,1)S(1)} %shard_map.48), channel_id=1, source_target_pairs={{0,8},{1,9},{2,10},{3,11},{4,12},{5,13},{6,14},{7,15},{8,0},{9,1},... | collective-permute-start | bytes 786440 | tf_op jit(solution)/shard_map/ppermute | solution.py:138
  64.5 39.1 %collective-permute-start.16 = (bf16[8,1,256,256]{3,2,1,0:T(8,128)(2,1)S(1)}, bf16[8,1,256,256]{3,2,1,0:T(8,128)(2,1)S(1)}, u32[]{:S(2)}, u32[]{:S(2)}) collective-permute-start(bf16[8,1,256,256]{3,2,1,0:T(8,128)(2,1)S(1)} %collective-permute-done.7.refs_5_.refs_7_), channel_id=1, source_target_pairs={{4,0},{5,1},{6,2},{7,3},{8,12},{9,13},{10,14},{11,15},{20,16},{21,... | collective-permute-start | bytes 3145736 | tf_op jit(solution)/shard_map/ppermute | solution.py:138
  78.5 1.9 %collective-permute-start.11 = (bf16[4,1,256,256]{3,2,1,0:T(8,128)(2,1)S(1)}, bf16[4,1,256,256]{3,2,1,0:T(8,128)(2,1)S(1)}, u32[]{:S(2)}, u32[]{:S(2)}) collective-permute-start(bf16[4,1,256,256]{3,2,1,0:T(8,128)(2,1)S(1)} %collective-permute-done.5.refs_0_.refs_2_), channel_id=1, source_target_pairs={{0,1},{1,0},{2,3},{3,2},{4,5},{5,4},{6,7},{7,6},{8,9},{9,8},{10,11... | collective-permute-start | bytes 1572872 | tf_op jit(solution)/shard_map/ppermute | solution.py:138
  78.5 2.7 %collective-permute-start.12 = (bf16[4,1,256,256]{3,2,1,0:T(8,128)(2,1)S(1)}, bf16[4,1,256,256]{3,2,1,0:T(8,128)(2,1)S(1)}, u32[]{:S(2)}, u32[]{:S(2)}) collective-permute-start(bf16[4,1,256,256]{3,2,1,0:T(8,128)(2,1)S(1)} %collective-permute-done.9.refs_1_.refs_3_), channel_id=1, source_target_pairs={{0,1},{1,0},{2,3},{3,2},{4,5},{5,4},{6,7},{7,6},{8,9},{9,8},{10,11... | collective-permute-start | bytes 1572872 | tf_op jit(solution)/shard_map/ppermute | solution.py:138
  83.1 5.1 %copy-start.1 = (bf16[1,16,256,256]{3,2,1,0:T(8,128)(2,1)S(1)}, bf16[1,16,256,256]{3,2,1,0:T(8,128)(2,1)}, u32[]{:S(2)}) copy-start(bf16[1,16,256,256]{3,2,1,0:T(8,128)(2,1)} %refs_6_.4) | copy-start | bytes 6291460
  83.1 5.1 %copy-start.3 = (bf16[8,1,256,256]{3,2,1,0:T(8,128)(2,1)S(1)}, bf16[8,1,256,256]{3,2,1,0:T(8,128)(2,1)}, u32[]{:S(2)}) copy-start(bf16[8,1,256,256]{3,2,1,0:T(8,128)(2,1)} %refs_0_.9) | copy-start | bytes 3145732
  83.1 27.7 %collective-permute-start.14 = (bf16[2,256,256]{2,1,0:T(8,128)(2,1)S(1)}, bf16[2,256,256]{2,1,0:T(8,128)(2,1)S(1)}, u32[]{:S(2)}, u32[]{:S(2)}) collective-permute-start(bf16[2,256,256]{2,1,0:T(8,128)(2,1)S(1)} %shard_map.50), channel_id=1, source_target_pairs={{0,8},{1,9},{2,10},{3,11},{4,12},{5,13},{6,14},{7,15},{8,0},{9,1},... | collective-permute-start | bytes 786440 | tf_op jit(solution)/shard_map/ppermute | solution.py:138
  87.7 23.2 %collective-permute-start.15 = (bf16[2,256,256]{2,1,0:T(8,128)(2,1)S(1)}, bf16[2,256,256]{2,1,0:T(8,128)(2,1)S(1)}, u32[]{:S(2)}, u32[]{:S(2)}) collective-permute-start(bf16[2,256,256]{2,1,0:T(8,128)(2,1)S(1)} %shard_map.51), channel_id=1, source_target_pairs={{0,4},{1,5},{2,6},{3,7},{4,0},{5,1},{6,2},{7,3},{8,12},{9,13},{10,... | collective-permute-start | bytes 786440 | tf_op jit(solution)/shard_map/ppermute | solution.py:138
  91.1 19.7 %copy-start.5 = (bf16[8,1,256,256]{3,2,1,0:T(8,128)(2,1)S(1)}, bf16[8,1,256,256]{3,2,1,0:T(8,128)(2,1)}, u32[]{:S(2)}) copy-start(bf16[8,1,256,256]{3,2,1,0:T(8,128)(2,1)} %refs_6_.2) | copy-start | bytes 3145732
  91.2 21.6 %collective-permute-start.18 = (bf16[4,256,256]{2,1,0:T(8,128)(2,1)S(1)}, bf16[4,256,256]{2,1,0:T(8,128)(2,1)S(1)}, u32[]{:S(2)}, u32[]{:S(2)}) collective-permute-start(bf16[4,256,256]{2,1,0:T(8,128)(2,1)S(1)} %shard_map.53), channel_id=1, source_target_pairs={{4,8},{5,9},{6,10},{7,11},{8,4},{9,5},{10,6},{11,7},{20,24},{21,25... | collective-permute-start | bytes 1572872 | tf_op jit(solution)/shard_map/ppermute | solution.py:138
  106.5 13.9 %collective-permute-start.17 = (bf16[4,256,256]{2,1,0:T(8,128)(2,1)S(1)}, bf16[4,256,256]{2,1,0:T(8,128)(2,1)S(1)}, u32[]{:S(2)}, u32[]{:S(2)}) collective-permute-start(bf16[4,256,256]{2,1,0:T(8,128)(2,1)S(1)} %shard_map.54), channel_id=1, source_target_pairs={{0,12},{1,13},{2,14},{3,15},{12,0},{13,1},{14,2},{15,3},{16,28},{1... | collective-permute-start | bytes 1572872 | tf_op jit(solution)/shard_map/ppermute | solution.py:138

commit v10 on v9

v10 whole, which is shorter than its diff:
```python
import functools

import jax
import jax.numpy as jnp
from jax import lax
from jax.experimental import pallas as pl
from jax.experimental.pallas import tpu as pltpu
from jax.sharding import PartitionSpec as P

HBM = pl.BlockSpec(memory_space=pltpu.HBM)
SMEM = pl.BlockSpec(memory_space=pltpu.SMEM)
VMEM = pl.BlockSpec(memory_space=pltpu.VMEM)


def slot_kernel(step, parts, choices, source, *refs):
    count = len(parts)
    lefts, psis = [], []
    for number, _ in parts:
        lefts.append(refs[:number])
        refs = refs[number:]
    for _, number in parts:
        psis.append(refs[:number])
        refs = refs[number:]
    rights = refs[:choices]
    out, mid_buf, right_buf = refs[choices:]
    terms, _, rows, columns = rights[0].shape
    me = lax.axis_index("sec")
    row = me >> 2
    q = me ^ (4 * step)
    outer = (row == 0) | (row == 3)

    def psi_block(held, sector):
        if len(held) == 1:
            return held[0][0, sector]
        low, high = held
        size = low.shape[1]
        return jnp.where(
            sector < size, low[0, jnp.minimum(sector, size - 1)], high[0, jnp.maximum(sector - size, 0)]
        )

    def left_block(held, k):
        for part in held:
            if k < part.shape[0]:
                return part[k, 0]
            k -= part.shape[0]

    for k in range(terms):
        span = pl.ds(k * columns, columns)
        right = rights[0][k, 0]
        if choices > 1:
            right = jnp.where(outer, right, rights[1][k, 0])
        right_buf[:, span] = right
        for i in range(count):
            mid = jnp.dot(
                left_block(lefts[i], k), psi_block(psis[i], source[k, q]), preferred_element_type=jnp.float32
            )
            mid_buf[pl.ds(i * rows, rows), span] = mid.astype(jnp.bfloat16)
    second_product(mid_buf, right_buf, out)


def second_product(mid, right, out):
    total = lax.dot_general(mid[...], right[...], (((1,), (1,)), ((), ())), preferred_element_type=jnp.float32)
    out[...] = total.reshape(out.shape).astype(out.dtype)


def second_kernel(mid, right, out, right_buf):
    terms, _, _, columns = right.shape
    for k in range(terms):
        right_buf[:, pl.ds(k * columns, columns)] = right[k, 0]
    second_product(mid, right_buf, out)


def second(mid, right, dtype):
    terms, _, rows, columns = right.shape
    return pl.pallas_call(
        second_kernel,
        out_shape=jax.ShapeDtypeStruct((mid.shape[0] // rows, rows, columns), dtype),
        in_specs=[VMEM, VMEM],
        out_specs=VMEM,
        scratch_shapes=[pltpu.VMEM((rows, terms * columns), jnp.bfloat16)],
        compiler_params=pltpu.CompilerParams(vmem_limit_bytes=16 << 20),
        cost_estimate=pl.CostEstimate(flops=1, bytes_accessed=1, transcendentals=0),
    )(mid, right)


def slot(step, source_map, lefts, psis, rights, dtype, flops, keep_mid):
    terms, _, rows, columns = rights[0].shape
    count = len(psis)
    parts = tuple((len(left), len(psi)) for left, psi in zip(lefts, psis))
    held = [part for left in lefts for part in left] + [part for psi in psis for part in psi] + list(rights)
    out = jax.ShapeDtypeStruct((count, rows, columns), dtype)
    mid = jax.ShapeDtypeStruct((count * rows, terms * columns), jnp.bfloat16)
    scratch = [pltpu.VMEM((rows, terms * columns), jnp.bfloat16)]
    if not keep_mid:
        scratch = [pltpu.VMEM(mid.shape, mid.dtype)] + scratch
    return pl.pallas_call(
        functools.partial(slot_kernel, step, parts, len(rights)),
        out_shape=(out, mid) if keep_mid else out,
        in_specs=[SMEM] + [VMEM] * len(held),
        out_specs=(VMEM, VMEM) if keep_mid else VMEM,
        scratch_shapes=scratch,
        compiler_params=pltpu.CompilerParams(vmem_limit_bytes=24 << 20),
        cost_estimate=pl.CostEstimate(flops=flops, bytes_accessed=1, transcendentals=0),
    )(source_map, *held)


def split_kernel(whole, low, high):
    first = low.shape[0]
    low[...] = whole[:first]
    high[...] = whole[first:]


def split(array, first):
    sizes = (first, array.shape[0] - first)
    return pl.pallas_call(
        split_kernel,
        out_shape=tuple(jax.ShapeDtypeStruct((size,) + array.shape[1:], array.dtype) for size in sizes),
        in_specs=[VMEM],
        out_specs=(VMEM, VMEM),
        compiler_params=pltpu.CompilerParams(vmem_limit_bytes=8 << 20),
        cost_estimate=pl.CostEstimate(flops=1, bytes_accessed=1, transcendentals=0),
    )(array)


def place_kernel(first, choices, *refs):
    *pieces, out, sem = refs
    me = lax.axis_index("sec")
    row = me >> 2
    outer = (row == 0) | (row == 3)

    def copies(pieces):
        blocks = [piece.at[i] for piece in pieces for i in range(piece.shape[0])]
        return [
            pltpu.make_async_copy(block, out.at[me ^ j], sem.at[j - first]) for j, block in enumerate(blocks, first)
        ]

    if choices == 1:
        for copy in copies(pieces):
            copy.start()
    else:
        pieces = pieces[-2:]

        @pl.when(outer)
        def _():
            for copy in copies(pieces[:1]):
                copy.start()

        @pl.when(jnp.logical_not(outer))
        def _():
            for copy in copies(pieces[1:]):
                copy.start()

    for copy in copies(pieces[-1:] if choices == 2 else pieces):
        copy.wait()


def place(first, sectors, pieces, out=None):
    blocks = sum(piece.shape[0] for piece in pieces)
    held = [] if out is None else [out]
    return pl.pallas_call(
        functools.partial(place_kernel, first, 1 if out is None else 2),
        out_shape=jax.ShapeDtypeStruct((sectors,) + pieces[0].shape[1:], pieces[0].dtype),
        in_specs=[HBM] * len(held) + [VMEM] * len(pieces),
        out_specs=HBM,
        scratch_shapes=[pltpu.SemaphoreType.DMA((blocks,))],
        input_output_aliases={} if out is None else {0: 0},
        compiler_params=pltpu.CompilerParams(vmem_limit_bytes=16 << 20),
        cost_estimate=pl.CostEstimate(flops=1, bytes_accessed=1, transcendentals=0),
    )(*held, *pieces)


def exchange(array, bits, members):
    return lax.ppermute(array, "sec", [(s, s ^ bits) for s in members])


def on_device(ops, psi, left_env, right_env, source_map):
    dtype = jnp.bfloat16 if ops == 1 else jnp.float32
    every = range(16)
    inner = range(4, 12)
    outer = [s for s in every if s not in inner]
    low, high = split(left_env, 3 * left_env.shape[0] // 4)

    def products(step, lefts, psis, rights, flops=1, keep_mid=False):
        return slot(step, source_map, lefts, psis, rights, dtype, flops, keep_mid)

    near = exchange(right_env, 4, every)
    middle = exchange(right_env, 12, inner)
    x_psi = exchange(psi, 2, every)
    own = ([(left_env,), (exchange(left_env, 1, every),)], [(psi,), (exchange(psi, 1, every),)])
    own_0 = products(0, *own, (right_env,))

    near, middle, own_0 = lax.optimization_barrier((near, middle, own_0))
    far_in = exchange(near, 12, inner)
    far_out = exchange(middle, 4, inner)
    own_1 = products(1, *own, (near,))
    sent_1 = exchange(own_1, 4, every)

    x_psi, low = lax.optimization_barrier((x_psi, low))
    x_low = exchange(low, 2, every)
    across_psi = exchange(x_psi, 1, every)

    far_out, far_in = lax.optimization_barrier((far_out, far_in))
    third = exchange(far_in, 4, inner)
    own_2 = products(2, *own, (far_out, far_in))
    sent_2 = exchange(own_2, 8, every)

    own_2, sent_1, high = lax.optimization_barrier((own_2, sent_1, high))
    x_high = exchange(high, 2, every)
    x_low, x_high, sent_2 = lax.optimization_barrier((x_low, x_high, sent_2))
    across_low = exchange(x_low, 1, every)
    across_high = exchange(x_high, 1, every)
    other = ([(x_low, x_high), (across_low, across_high)], [(x_psi,), (across_psi,)])
    both = (own[0] + other[0], own[1] + other[1])
    other_2 = products(2, *other, (far_out, far_in))
    other_sent_2 = exchange(other_2, 8, every)
    last_middle, mid = products(3, *both, (middle,), keep_mid=True)
    sent_middle = exchange(last_middle, 12, inner)
    other_1 = products(1, *other, (near,))
    other_sent_1 = exchange(other_1, 4, every)

    third, other_1, other_2, last_middle = lax.optimization_barrier((third, other_1, other_2, last_middle))
    last_third = second(mid, third, dtype)
    sent_third = exchange(last_third, 12, outer)
    right_last, other_sent_2, other_sent_1 = lax.optimization_barrier((right_env, other_sent_2, other_sent_1))
    other_0 = products(0, *other, (right_last,), flops=10**10)

    out = place(0, 16, [own_0, other_0, sent_1, other_sent_1, sent_2, other_sent_2])
    out = place(12, 16, [sent_third, sent_middle], out)[:, None]
    if ops > 1:
        out = lax.psum_scatter(out, "op", scatter_dimension=2, tiled=True).astype(jnp.bfloat16)
    return out


def solution(mesh):
    placed = (
        P(("group", "sec"), None, None, None),
        P(("group", "op"), "sec", None, None),
        P(("group", "op"), "sec", None, None),
        P(("group", "op"), None),
    )
    return jax.shard_map(
        functools.partial(on_device, mesh.shape["op"]),
        mesh=mesh,
        in_specs=placed,
        out_specs=P("group", "sec", "op", None),
        check_vma=False,
    )
```

time: 122 us -> 120 us (0.984)
    pallas_call x8 -> x7, Pallas kernels: 17.2 us -> 14.2 us  [slot(): pl.pallas_call(functools.partial(slot_kernel, step, parts, len(rights)),...]
    pallas_call x2 -> x4, Pallas kernels: 1.51 us -> 3.44 us  [the longest x2 2.09 us: place(): pl.pallas_call(functools.partial(place_kernel, first, 1 if out is None el...]
    unnamed x14 -> x12, local copies, waits for them, and re-layouts: 4.74 us -> 4.74 us
  transfers between devices with their start and end apart: 19 -> 19, of which waited for: 11 -> 10; matrix products, arithmetic and copies ran while one was open for 0% -> 0% of each run, Pallas kernels for 14% -> 14%
where the time goes in v10:
time: 120 us; the launch traced here: 119 us
  waiting for transfers between devices  72.7 us (61%)
  starting transfers between devices  24.1 us (20%)
  Pallas kernels  17.7 us (15%)
  local copies, waits for them, and re-layouts  4.74 us (4%)
    ppermute x19, waiting for transfers between devices, exchange(): return lax.ppermute(array, 'sec', [(s, s ^ bits) for s in members])  72.7 us
    ppermute x19, starting transfers between devices, exchange(): return lax.ppermute(array, 'sec', [(s, s ^ bits) for s in members])  24.1 us
    pallas_call x7, Pallas kernels, slot(): pl.pallas_call(functools.partial(slot_kernel, step, parts, len(rights)),...  14.2 us
    unnamed x12, local copies, waits for them, and re-layouts  4.74 us
  transfers between devices with their start and end apart: 19, of which 10 were waited for; matrix products, arithmetic and copies ran while one was open for 0% of the time, Pallas kernels for 14%

profile of v10, /device:TPU:0, one launch (start us, length us, event | category | flops | bytes accessed | tf_op | source)
XLA Modules:
  0.0 119.4 jit_solution(11010367065403895835)
XLA Ops:
  0.0 0.5 collective-permute-start.3
  0.5 2.5 %collective-permute-start.4 = (bf16[1,16,256,256]{3,2,1,0:T(8,128)(2,1)}, bf16[1,16,256,256]{3,2,1,0:T(8,128)(2,1)S(1)}, u32[]{:S(2)}, u32[]{:S(2)}) collective-permute-start(bf16[1,16,256,256]{3,2,1,0:T(8,128)(2,1)} %refs_6_.2), channel_id=1, source_target_pairs={{0,2},{1,3},{2,0},{3,1},{4,6},{5,7},{6,4},{7,5},{8,10},{9,11},{10,... | collective-permute-start | bytes 6291464 | tf_op jit(solution)/shard_map/ppermute | solution.py:173
  2.9 0.2 collective-permute-start.2
  3.2 0.7 collective-permute-start.1
  3.9 4.4 %collective-permute-start = (bf16[8,1,256,256]{3,2,1,0:T(8,128)(2,1)}, bf16[8,1,256,256]{3,2,1,0:T(8,128)(2,1)S(1)}, u32[]{:S(2)}, u32[]{:S(2)}) collective-permute-start(bf16[8,1,256,256]{3,2,1,0:T(8,128)(2,1)} %refs_6_.1), channel_id=1, source_target_pairs={{0,4},{1,5},{2,6},{3,7},{4,0},{5,1},{6,2},{7,3},{8,12},{9,13},{10,... | collective-permute-start | bytes 3145736 | tf_op jit(solution)/shard_map/ppermute | solution.py:173
  8.3 0.0 collective-permute-done.2.refs_1_
  8.3 0.0 collective-permute-done.3.refs_3_.refs_7_
  8.3 1.6 %copy-done = bf16[1,16,256,256]{3,2,1,0:T(8,128)(2,1)S(1)} copy-done((bf16[1,16,256,256]{3,2,1,0:T(8,128)(2,1)S(1)}, bf16[1,16,256,256]{3,2,1,0:T(8,128)(2,1)}, u32[]{:S(2)}) %copy-start) | copy-done | bytes 2097176
  9.9 1.2 %copy-done.2 = bf16[8,1,256,256]{3,2,1,0:T(8,128)(2,1)S(1)} copy-done((bf16[8,1,256,256]{3,2,1,0:T(8,128)(2,1)S(1)}, bf16[8,1,256,256]{3,2,1,0:T(8,128)(2,1)}, u32[]{:S(2)}) %copy-start.2) | copy-done | bytes 1048600
  11.1 1.2 %copy-done.4 = bf16[8,1,256,256]{3,2,1,0:T(8,128)(2,1)S(1)} copy-done((bf16[8,1,256,256]{3,2,1,0:T(8,128)(2,1)S(1)}, bf16[8,1,256,256]{3,2,1,0:T(8,128)(2,1)}, u32[]{:S(2)}) %copy-start.4) | copy-done | bytes 1048600
  12.3 0.7 copy-done.5
  13.0 1.9 %shard_map.46.refs_0_ = bf16[2,256,256]{2,1,0:T(8,128)(2,1)S(1)} custom-call(s32[8,16]{1,0:T(8,128)S(1)} %copy-done.5, bf16[8,1,256,256]{3,2,1,0:T(8,128)(2,1)S(1)} %copy-done.2, bf16[8,1,256,256]{3,2,1,0:T(8,128)(2,1)S(1)} %collective-permute-done.2.refs_1_, bf16[1,16,256,256]{3,2,1,0:T(8,128)(2,1)S(1)} %copy-done, ...), custom_call_target="tpu_custom_call" | custom-call | flops 1 | bytes 1 | tf_op jit(solution)/shard_map/pallas_call | solution.py:96
  14.9 0.0 collective-permute-done.1.refs_10_
  14.9 16.9 %collective-permute-done.refs_4_.refs_6_ = bf16[8,1,256,256]{3,2,1,0:T(8,128)(2,1)S(1)} collective-permute-done((bf16[8,1,256,256]{3,2,1,0:T(8,128)(2,1)}, bf16[8,1,256,256]{3,2,1,0:T(8,128)(2,1)S(1)}, u32[]{:S(2)}, u32[]{:S(2)}) %collective-permute-start) | collective-permute-done | bytes 1048608 | tf_op jit(solution)/shard_map/ppermute | solution.py:173
  31.8 1.3 %collective-permute-start.6 = (bf16[8,1,256,256]{3,2,1,0:T(8,128)(2,1)S(1)}, bf16[8,1,256,256]{3,2,1,0:T(8,128)(2,1)S(1)}, u32[]{:S(2)}, u32[]{:S(2)}) collective-permute-start(bf16[8,1,256,256]{3,2,1,0:T(8,128)(2,1)S(1)} %collective-permute-done.1.refs_10_), channel_id=1, source_target_pairs={{4,0},{5,1},{6,2},{7,3},{8,12},{9,13},{10,14},{11,15},{20,16},{21,... | collective-permute-start | bytes 3145736 | tf_op jit(solution)/shard_map/ppermute | solution.py:173
  33.1 0.7 collective-permute-start.7
  33.9 0.1 shard_map.47
  33.9 15.5 %collective-permute-done.4.refs_4_.refs_8_ = bf16[1,16,256,256]{3,2,1,0:T(8,128)(2,1)S(1)} collective-permute-done((bf16[1,16,256,256]{3,2,1,0:T(8,128)(2,1)}, bf16[1,16,256,256]{3,2,1,0:T(8,128)(2,1)S(1)}, u32[]{:S(2)}, u32[]{:S(2)}) %collective-permute-start.4) | collective-permute-done | bytes 2097184 | tf_op jit(solution)/shard_map/ppermute | solution.py:173
  49.5 0.0 collective-permute-start.13
  49.5 1.7 %collective-permute-start.5 = (bf16[6,1,256,256]{3,2,1,0:T(8,128)(2,1)S(1)}, bf16[6,1,256,256]{3,2,1,0:T(8,128)(2,1)S(1)}, u32[]{:S(2)}, u32[]{:S(2)}) collective-permute-start(bf16[6,1,256,256]{3,2,1,0:T(8,128)(2,1)S(1)} %get-tuple-element.27), channel_id=1, source_target_pairs={{0,2},{1,3},{2,0},{3,1},{4,6},{5,7},{6,4},{7,5},{8,10},{9,11},{10,... | collective-permute-start | bytes 2359304 | tf_op jit(solution)/shard_map/ppermute | solution.py:173
  51.2 1.9 %shard_map.49 = bf16[2,256,256]{2,1,0:T(8,128)(2,1)S(1)} custom-call(s32[8,16]{1,0:T(8,128)S(1)} %copy-done.5, bf16[8,1,256,256]{3,2,1,0:T(8,128)(2,1)S(1)} %copy-done.2, bf16[8,1,256,256]{3,2,1,0:T(8,128)(2,1)S(1)} %collective-permute-done.2.refs_1_, bf16[1,16,256,256]{3,2,1,0:T(8,128)(2,1)S(1)} %copy-done, ...), custom_call_target="tpu_custom_call" | custom-call | flops 1 | bytes 1 | tf_op jit(solution)/shard_map/pallas_call | solution.py:96
  53.1 1.6 %collective-permute-start.8 = (bf16[2,256,256]{2,1,0:T(8,128)(2,1)S(1)}, bf16[2,256,256]{2,1,0:T(8,128)(2,1)S(1)}, u32[]{:S(2)}, u32[]{:S(2)}) collective-permute-start(bf16[2,256,256]{2,1,0:T(8,128)(2,1)S(1)} %shard_map.49), channel_id=1, source_target_pairs={{0,4},{1,5},{2,6},{3,7},{4,0},{5,1},{6,2},{7,3},{8,12},{9,13},{10,... | collective-permute-start | bytes 786440 | tf_op jit(solution)/shard_map/ppermute | solution.py:173
  54.7 5.1 %collective-permute-done.6.refs_4_.refs_6_ = bf16[8,1,256,256]{3,2,1,0:T(8,128)(2,1)S(1)} collective-permute-done((bf16[8,1,256,256]{3,2,1,0:T(8,128)(2,1)S(1)}, bf16[8,1,256,256]{3,2,1,0:T(8,128)(2,1)S(1)}, u32[]{:S(2)}, u32[]{:S(2)}) %collective-permute-start.6) | collective-permute-done | bytes 1048608 | tf_op jit(solution)/shard_map/ppermute | solution.py:173
  59.8 1.9 %shard_map.48 = bf16[2,256,256]{2,1,0:T(8,128)(2,1)S(1)} custom-call(s32[8,16]{1,0:T(8,128)S(1)} %copy-done.5, bf16[8,1,256,256]{3,2,1,0:T(8,128)(2,1)S(1)} %copy-done.2, bf16[8,1,256,256]{3,2,1,0:T(8,128)(2,1)S(1)} %collective-permute-done.2.refs_1_, bf16[1,16,256,256]{3,2,1,0:T(8,128)(2,1)S(1)} %copy-done, ...), custom_call_target="tpu_custom_call" | custom-call | flops 1 | bytes 1 | tf_op jit(solution)/shard_map/pallas_call | solution.py:96
  61.7 2.1 %collective-permute-done.8.refs_2_ = bf16[2,256,256]{2,1,0:T(8,128)(2,1)S(1)} collective-permute-done((bf16[2,256,256]{2,1,0:T(8,128)(2,1)S(1)}, bf16[2,256,256]{2,1,0:T(8,128)(2,1)S(1)}, u32[]{:S(2)}, u32[]{:S(2)}) %collective-permute-start.8) | collective-permute-done | bytes 262176 | tf_op jit(solution)/shard_map/ppermute | solution.py:173
  63.9 0.5 collective-permute-start.9
  64.4 0.3 collective-permute-start.10
  64.7 1.3 %collective-permute-start.16 = (bf16[8,1,256,256]{3,2,1,0:T(8,128)(2,1)S(1)}, bf16[8,1,256,256]{3,2,1,0:T(8,128)(2,1)S(1)}, u32[]{:S(2)}, u32[]{:S(2)}) collective-permute-start(bf16[8,1,256,256]{3,2,1,0:T(8,128)(2,1)S(1)} %collective-permute-done.7.refs_5_.refs_7_), channel_id=1, source_target_pairs={{4,0},{5,1},{6,2},{7,3},{8,12},{9,13},{10,14},{11,15},{20,16},{21,... | collective-permute-start | bytes 3145736 | tf_op jit(solution)/shard_map/ppermute | solution.py:173
  66.0 3.8 %collective-permute-done.5.refs_0_.refs_2_ = bf16[6,1,256,256]{3,2,1,0:T(8,128)(2,1)S(1)} collective-permute-done((bf16[6,1,256,256]{3,2,1,0:T(8,128)(2,1)S(1)}, bf16[6,1,256,256]{3,2,1,0:T(8,128)(2,1)S(1)}, u32[]{:S(2)}, u32[]{:S(2)}) %collective-permute-start.5) | collective-permute-done | bytes 786464 | tf_op jit(solution)/shard_map/ppermute | solution.py:173
  69.8 5.2 %collective-permute-done.9.refs_1_.refs_3_ = bf16[2,1,256,256]{3,2,1,0:T(8,128)(2,1)S(1)} collective-permute-done((bf16[2,1,256,256]{3,2,1,0:T(8,128)(2,1)S(1)}, bf16[2,1,256,256]{3,2,1,0:T(8,128)(2,1)S(1)}, u32[]{:S(2)}, u32[]{:S(2)}) %collective-permute-start.9) | collective-permute-done | bytes 262176 | tf_op jit(solution)/shard_map/ppermute | solution.py:173
  75.0 2.1 %collective-permute-done.10.refs_4_ = bf16[2,256,256]{2,1,0:T(8,128)(2,1)S(1)} collective-permute-done((bf16[2,256,256]{2,1,0:T(8,128)(2,1)S(1)}, bf16[2,256,256]{2,1,0:T(8,128)(2,1)S(1)}, u32[]{:S(2)}, u32[]{:S(2)}) %collective-permute-start.10) | collective-permute-done | bytes 262176 | tf_op jit(solution)/shard_map/ppermute | solution.py:173
  77.1 0.5 collective-permute-start.12
  77.6 2.1 %collective-permute-done.12.refs_3_.refs_5_ = bf16[2,1,256,256]{3,2,1,0:T(8,128)(2,1)S(1)} collective-permute-done((bf16[2,1,256,256]{3,2,1,0:T(8,128)(2,1)S(1)}, bf16[2,1,256,256]{3,2,1,0:T(8,128)(2,1)S(1)}, u32[]{:S(2)}, u32[]{:S(2)}) %collective-permute-start.12) | collective-permute-done | bytes 262176 | tf_op jit(solution)/shard_map/ppermute | solution.py:173
  79.8 1.9 %shard_map.50 = bf16[2,256,256]{2,1,0:T(8,128)(2,1)S(1)} custom-call(s32[8,16]{1,0:T(8,128)S(1)} %copy-done.5, bf16[6,1,256,256]{3,2,1,0:T(8,128)(2,1)S(1)} %collective-permute-done.5.refs_0_.refs_2_, bf16[2,1,256,256]{3,2,1,0:T(8,128)(2,1)S(1)} %collective-permute-done.9.refs_1_.refs_3_, ...), custom_call_target="tpu_custom_call" | custom-call | flops 1 | bytes 1 | tf_op jit(solution)/shard_map/pallas_call | solution.py:96
  81.7 0.0 copy-start.1
  81.7 0.0 copy-start.3
  81.7 0.8 collective-permute-start.14
  82.5 1.9 %shard_map.51 = bf16[2,256,256]{2,1,0:T(8,128)(2,1)S(1)} custom-call(s32[8,16]{1,0:T(8,128)S(1)} %copy-done.5, bf16[6,1,256,256]{3,2,1,0:T(8,128)(2,1)S(1)} %collective-permute-done.5.refs_0_.refs_2_, bf16[2,1,256,256]{3,2,1,0:T(8,128)(2,1)S(1)} %collective-permute-done.9.refs_1_.refs_3_, ...), custom_call_target="tpu_custom_call" | custom-call | flops 1 | bytes 1 | tf_op jit(solution)/shard_map/pallas_call | solution.py:96
  84.4 2.3 %collective-permute-start.15 = (bf16[2,256,256]{2,1,0:T(8,128)(2,1)S(1)}, bf16[2,256,256]{2,1,0:T(8,128)(2,1)S(1)}, u32[]{:S(2)}, u32[]{:S(2)}) collective-permute-start(bf16[2,256,256]{2,1,0:T(8,128)(2,1)S(1)} %shard_map.51), channel_id=1, source_target_pairs={{0,4},{1,5},{2,6},{3,7},{4,0},{5,1},{6,2},{7,3},{8,12},{9,13},{10,... | collective-permute-start | bytes 786440 | tf_op jit(solution)/shard_map/ppermute | solution.py:173
  86.8 3.0 %shard_map.54 = (bf16[4,256,256]{2,1,0:T(8,128)(2,1)S(1)}, bf16[1024,2048]{1,0:T(8,128)(2,1)S(1)}) custom-call(s32[8,16]{1,0:T(8,128)S(1)} %copy-done.5, bf16[8,1,256,256]{3,2,1,0:T(8,128)(2,1)S(1)} %copy-done.3, bf16[8,1,256,256]{3,2,1,0:T(8,128)(2,1)S(1)} %collective-permute-done.2.refs_1_, ...), custom_call_target="tpu_custom_call" | custom-call | flops 1 | bytes 1 | tf_op jit(solution)/shard_map/pallas_call | solution.py:96
  89.7 0.7 collective-permute-start.18
  90.4 13.4 %collective-permute-done.16.right = bf16[8,1,256,256]{3,2,1,0:T(8,128)(2,1)S(1)} collective-permute-done((bf16[8,1,256,256]{3,2,1,0:T(8,128)(2,1)S(1)}, bf16[8,1,256,256]{3,2,1,0:T(8,128)(2,1)S(1)}, u32[]{:S(2)}, u32[]{:S(2)}) %collective-permute-start.16) | collective-permute-done | bytes 1048608 | tf_op jit(solution)/shard_map/ppermute | solution.py:173
  103.8 1.3 %shard_map.55 = bf16[4,256,256]{2,1,0:T(8,128)(2,1)S(1)} custom-call(bf16[1024,2048]{1,0:T(8,128)(2,1)S(1)} %get-tuple-element.42.mid, bf16[8,1,256,256]{3,2,1,0:T(8,128)(2,1)S(1)} %collective-permute-done.16.right), custom_call_target="tpu_custom_call" | custom-call | flops 1 | bytes 1 | tf_op jit(solution)/shard_map/pallas_call | solution.py:75
  105.1 3.9 %collective-permute-start.17 = (bf16[4,256,256]{2,1,0:T(8,128)(2,1)S(1)}, bf16[4,256,256]{2,1,0:T(8,128)(2,1)S(1)}, u32[]{:S(2)}, u32[]{:S(2)}) collective-permute-start(bf16[4,256,256]{2,1,0:T(8,128)(2,1)S(1)} %shard_map.55), channel_id=1, source_target_pairs={{0,12},{1,13},{2,14},{3,15},{12,0},{13,1},{14,2},{15,3},{16,28},{1... | collective-permute-start | bytes 1572872 | tf_op jit(solution)/shard_map/ppermute | solution.py:173
  109.0 1.9 %shard_map.52.refs_1_ = bf16[2,256,256]{2,1,0:T(8,128)(2,1)S(1)} custom-call(s32[8,16]{1,0:T(8,128)S(1)} %copy-done.5, bf16[6,1,256,256]{3,2,1,0:T(8,128)(2,1)S(1)} %collective-permute-done.5.refs_0_.refs_2_, bf16[2,1,256,256]{3,2,1,0:T(8,128)(2,1)S(1)} %collective-permute-done.9.refs_1_.refs_3_, ...), custom_call_target="tpu_custom_call" | custom-call | flops 10000000000 | bytes 1 | tf_op jit(solution)/shard_map/pallas_call | solution.py:96
  110.9 1.2 %shard_map.53.refs_0_ = bf16[16,256,256]{2,1,0:T(8,128)(2,1)} custom-call(bf16[2,256,256]{2,1,0:T(8,128)(2,1)S(1)} %shard_map.46.refs_0_, bf16[2,256,256]{2,1,0:T(8,128)(2,1)S(1)} %shard_map.52.refs_1_, bf16[2,256,256]{2,1,0:T(8,128)(2,1)S(1)} %collective-permute-done.8.refs_2_, bf16[2,256,256]{2,1,0:T(8,128)(2,1)S(1)} %collective-permute-done.15.refs_3_, ...), custom_call_target="tpu_custom_call" | custom-call | flops 1 | bytes 1 | tf_op jit(solution)/shard_map/pallas_call | solution.py:160
  112.2 6.3 %collective-permute-done.17.refs_1_ = bf16[4,256,256]{2,1,0:T(8,128)(2,1)S(1)} collective-permute-done((bf16[4,256,256]{2,1,0:T(8,128)(2,1)S(1)}, bf16[4,256,256]{2,1,0:T(8,128)(2,1)S(1)}, u32[]{:S(2)}, u32[]{:S(2)}) %collective-permute-start.17) | collective-permute-done | bytes 524320 | tf_op jit(solution)/shard_map/ppermute | solution.py:173
  118.5 0.9 shard_map.56
  (13 shorter events, 0.0 us)
Async XLA Ops:
  0.0 8.3 %collective-permute-start.3 = (bf16[1,16,256,256]{3,2,1,0:T(8,128)(2,1)}, bf16[1,16,256,256]{3,2,1,0:T(8,128)(2,1)S(1)}, u32[]{:S(2)}, u32[]{:S(2)}) collective-permute-start(bf16[1,16,256,256]{3,2,1,0:T(8,128)(2,1)} %refs_6_.2), channel_id=1, source_target_pairs={{0,1},{1,0},{2,3},{3,2},{4,5},{5,4},{6,7},{7,6},{8,9},{9,8},{10,11... | collective-permute-start | bytes 6291464 | tf_op jit(solution)/shard_map/ppermute | solution.py:173
  0.5 49.0 %collective-permute-start.4 = (bf16[1,16,256,256]{3,2,1,0:T(8,128)(2,1)}, bf16[1,16,256,256]{3,2,1,0:T(8,128)(2,1)S(1)}, u32[]{:S(2)}, u32[]{:S(2)}) collective-permute-start(bf16[1,16,256,256]{3,2,1,0:T(8,128)(2,1)} %refs_6_.2), channel_id=1, source_target_pairs={{0,2},{1,3},{2,0},{3,1},{4,6},{5,7},{6,4},{7,5},{8,10},{9,11},{10,... | collective-permute-start | bytes 6291464 | tf_op jit(solution)/shard_map/ppermute | solution.py:173
  2.9 5.4 %collective-permute-start.2 = (bf16[8,1,256,256]{3,2,1,0:T(8,128)(2,1)}, bf16[8,1,256,256]{3,2,1,0:T(8,128)(2,1)S(1)}, u32[]{:S(2)}, u32[]{:S(2)}) collective-permute-start(bf16[8,1,256,256]{3,2,1,0:T(8,128)(2,1)} %refs_0_.7), channel_id=1, source_target_pairs={{0,1},{1,0},{2,3},{3,2},{4,5},{5,4},{6,7},{7,6},{8,9},{9,8},{10,11... | collective-permute-start | bytes 3145736 | tf_op jit(solution)/shard_map/ppermute | solution.py:173
  3.2 11.7 %collective-permute-start.1 = (bf16[8,1,256,256]{3,2,1,0:T(8,128)(2,1)}, bf16[8,1,256,256]{3,2,1,0:T(8,128)(2,1)S(1)}, u32[]{:S(2)}, u32[]{:S(2)}) collective-permute-start(bf16[8,1,256,256]{3,2,1,0:T(8,128)(2,1)} %refs_6_.1), channel_id=1, source_target_pairs={{4,8},{5,9},{6,10},{7,11},{8,4},{9,5},{10,6},{11,7},{20,24},{21,25... | collective-permute-start | bytes 3145736 | tf_op jit(solution)/shard_map/ppermute | solution.py:173
  3.9 27.9 %collective-permute-start = (bf16[8,1,256,256]{3,2,1,0:T(8,128)(2,1)}, bf16[8,1,256,256]{3,2,1,0:T(8,128)(2,1)S(1)}, u32[]{:S(2)}, u32[]{:S(2)}) collective-permute-start(bf16[8,1,256,256]{3,2,1,0:T(8,128)(2,1)} %refs_6_.1), channel_id=1, source_target_pairs={{0,4},{1,5},{2,6},{3,7},{4,0},{5,1},{6,2},{7,3},{8,12},{9,13},{10,... | collective-permute-start | bytes 3145736 | tf_op jit(solution)/shard_map/ppermute | solution.py:173
  8.3 1.6 %copy-start = (bf16[1,16,256,256]{3,2,1,0:T(8,128)(2,1)S(1)}, bf16[1,16,256,256]{3,2,1,0:T(8,128)(2,1)}, u32[]{:S(2)}) copy-start(bf16[1,16,256,256]{3,2,1,0:T(8,128)(2,1)} %refs_6_.2) | copy-start | bytes 6291460
  9.9 1.2 %copy-start.2 = (bf16[8,1,256,256]{3,2,1,0:T(8,128)(2,1)S(1)}, bf16[8,1,256,256]{3,2,1,0:T(8,128)(2,1)}, u32[]{:S(2)}) copy-start(bf16[8,1,256,256]{3,2,1,0:T(8,128)(2,1)} %refs_0_.7) | copy-start | bytes 3145732
  11.1 1.2 %copy-start.4 = (bf16[8,1,256,256]{3,2,1,0:T(8,128)(2,1)S(1)}, bf16[8,1,256,256]{3,2,1,0:T(8,128)(2,1)}, u32[]{:S(2)}) copy-start(bf16[8,1,256,256]{3,2,1,0:T(8,128)(2,1)} %refs_6_.1) | copy-start | bytes 3145732
  12.3 0.7 copy-start.5
  31.8 28.0 %collective-permute-start.6 = (bf16[8,1,256,256]{3,2,1,0:T(8,128)(2,1)S(1)}, bf16[8,1,256,256]{3,2,1,0:T(8,128)(2,1)S(1)}, u32[]{:S(2)}, u32[]{:S(2)}) collective-permute-start(bf16[8,1,256,256]{3,2,1,0:T(8,128)(2,1)S(1)} %collective-permute-done.1.refs_10_), channel_id=1, source_target_pairs={{4,0},{5,1},{6,2},{7,3},{8,12},{9,13},{10,14},{11,15},{20,16},{21,... | collective-permute-start | bytes 3145736 | tf_op jit(solution)/shard_map/ppermute | solution.py:173
  33.1 26.7 %collective-permute-start.7 = (bf16[8,1,256,256]{3,2,1,0:T(8,128)(2,1)S(1)}, bf16[8,1,256,256]{3,2,1,0:T(8,128)(2,1)S(1)}, u32[]{:S(2)}, u32[]{:S(2)}) collective-permute-start(bf16[8,1,256,256]{3,2,1,0:T(8,128)(2,1)S(1)} %collective-permute-done.refs_4_.refs_6_), channel_id=1, source_target_pairs={{4,8},{5,9},{6,10},{7,11},{8,4},{9,5},{10,6},{11,7},{20,24},{21,25... | collective-permute-start | bytes 3145736 | tf_op jit(solution)/shard_map/ppermute | solution.py:173
  49.5 30.3 %collective-permute-start.13 = (bf16[1,16,256,256]{3,2,1,0:T(8,128)(2,1)S(1)}, bf16[1,16,256,256]{3,2,1,0:T(8,128)(2,1)S(1)}, u32[]{:S(2)}, u32[]{:S(2)}) collective-permute-start(bf16[1,16,256,256]{3,2,1,0:T(8,128)(2,1)S(1)} %collective-permute-done.4.refs_4_.refs_8_), channel_id=1, source_target_pairs={{0,1},{1,0},{2,3},{3,2},{4,5},{5,4},{6,7},{7,6},{8,9},{9,8},{10,11... | collective-permute-start | bytes 6291464 | tf_op jit(solution)/shard_map/ppermute | solution.py:173
  49.5 20.3 %collective-permute-start.5 = (bf16[6,1,256,256]{3,2,1,0:T(8,128)(2,1)S(1)}, bf16[6,1,256,256]{3,2,1,0:T(8,128)(2,1)S(1)}, u32[]{:S(2)}, u32[]{:S(2)}) collective-permute-start(bf16[6,1,256,256]{3,2,1,0:T(8,128)(2,1)S(1)} %get-tuple-element.27), channel_id=1, source_target_pairs={{0,2},{1,3},{2,0},{3,1},{4,6},{5,7},{6,4},{7,5},{8,10},{9,11},{10,... | collective-permute-start | bytes 2359304 | tf_op jit(solution)/shard_map/ppermute | solution.py:173
  53.1 10.8 %collective-permute-start.8 = (bf16[2,256,256]{2,1,0:T(8,128)(2,1)S(1)}, bf16[2,256,256]{2,1,0:T(8,128)(2,1)S(1)}, u32[]{:S(2)}, u32[]{:S(2)}) collective-permute-start(bf16[2,256,256]{2,1,0:T(8,128)(2,1)S(1)} %shard_map.49), channel_id=1, source_target_pairs={{0,4},{1,5},{2,6},{3,7},{4,0},{5,1},{6,2},{7,3},{8,12},{9,13},{10,... | collective-permute-start | bytes 786440 | tf_op jit(solution)/shard_map/ppermute | solution.py:173
  63.9 11.2 %collective-permute-start.9 = (bf16[2,1,256,256]{3,2,1,0:T(8,128)(2,1)S(1)}, bf16[2,1,256,256]{3,2,1,0:T(8,128)(2,1)S(1)}, u32[]{:S(2)}, u32[]{:S(2)}) collective-permute-start(bf16[2,1,256,256]{3,2,1,0:T(8,128)(2,1)S(1)} %get-tuple-element.33), channel_id=1, source_target_pairs={{0,2},{1,3},{2,0},{3,1},{4,6},{5,7},{6,4},{7,5},{8,10},{9,11},{10,... | collective-permute-start | bytes 786440 | tf_op jit(solution)/shard_map/ppermute | solution.py:173
  64.4 12.7 %collective-permute-start.10 = (bf16[2,256,256]{2,1,0:T(8,128)(2,1)S(1)}, bf16[2,256,256]{2,1,0:T(8,128)(2,1)S(1)}, u32[]{:S(2)}, u32[]{:S(2)}) collective-permute-start(bf16[2,256,256]{2,1,0:T(8,128)(2,1)S(1)} %shard_map.48), channel_id=1, source_target_pairs={{0,8},{1,9},{2,10},{3,11},{4,12},{5,13},{6,14},{7,15},{8,0},{9,1},... | collective-permute-start | bytes 786440 | tf_op jit(solution)/shard_map/ppermute | solution.py:173
  64.7 39.1 %collective-permute-start.16 = (bf16[8,1,256,256]{3,2,1,0:T(8,128)(2,1)S(1)}, bf16[8,1,256,256]{3,2,1,0:T(8,128)(2,1)S(1)}, u32[]{:S(2)}, u32[]{:S(2)}) collective-permute-start(bf16[8,1,256,256]{3,2,1,0:T(8,128)(2,1)S(1)} %collective-permute-done.7.refs_5_.refs_7_), channel_id=1, source_target_pairs={{4,0},{5,1},{6,2},{7,3},{8,12},{9,13},{10,14},{11,15},{20,16},{21,... | collective-permute-start | bytes 3145736 | tf_op jit(solution)/shard_map/ppermute | solution.py:173
  77.1 2.7 %collective-permute-start.11 = (bf16[6,1,256,256]{3,2,1,0:T(8,128)(2,1)S(1)}, bf16[6,1,256,256]{3,2,1,0:T(8,128)(2,1)S(1)}, u32[]{:S(2)}, u32[]{:S(2)}) collective-permute-start(bf16[6,1,256,256]{3,2,1,0:T(8,128)(2,1)S(1)} %collective-permute-done.5.refs_0_.refs_2_), channel_id=1, source_target_pairs={{0,1},{1,0},{2,3},{3,2},{4,5},{5,4},{6,7},{7,6},{8,9},{9,8},{10,11... | collective-permute-start | bytes 2359304 | tf_op jit(solution)/shard_map/ppermute | solution.py:173
  77.1 2.7 %collective-permute-start.12 = (bf16[2,1,256,256]{3,2,1,0:T(8,128)(2,1)S(1)}, bf16[2,1,256,256]{3,2,1,0:T(8,128)(2,1)S(1)}, u32[]{:S(2)}, u32[]{:S(2)}) collective-permute-start(bf16[2,1,256,256]{3,2,1,0:T(8,128)(2,1)S(1)} %collective-permute-done.9.refs_1_.refs_3_), channel_id=1, source_target_pairs={{0,1},{1,0},{2,3},{3,2},{4,5},{5,4},{6,7},{7,6},{8,9},{9,8},{10,11... | collective-permute-start | bytes 786440 | tf_op jit(solution)/shard_map/ppermute | solution.py:173
  81.7 5.1 %copy-start.1 = (bf16[1,16,256,256]{3,2,1,0:T(8,128)(2,1)S(1)}, bf16[1,16,256,256]{3,2,1,0:T(8,128)(2,1)}, u32[]{:S(2)}) copy-start(bf16[1,16,256,256]{3,2,1,0:T(8,128)(2,1)} %refs_6_.2) | copy-start | bytes 6291460
  81.7 5.1 %copy-start.3 = (bf16[8,1,256,256]{3,2,1,0:T(8,128)(2,1)S(1)}, bf16[8,1,256,256]{3,2,1,0:T(8,128)(2,1)}, u32[]{:S(2)}) copy-start(bf16[8,1,256,256]{3,2,1,0:T(8,128)(2,1)} %refs_0_.7) | copy-start | bytes 3145732
  81.7 27.3 %collective-permute-start.14 = (bf16[2,256,256]{2,1,0:T(8,128)(2,1)S(1)}, bf16[2,256,256]{2,1,0:T(8,128)(2,1)S(1)}, u32[]{:S(2)}, u32[]{:S(2)}) collective-permute-start(bf16[2,256,256]{2,1,0:T(8,128)(2,1)S(1)} %shard_map.50), channel_id=1, source_target_pairs={{0,8},{1,9},{2,10},{3,11},{4,12},{5,13},{6,14},{7,15},{8,0},{9,1},... | collective-permute-start | bytes 786440 | tf_op jit(solution)/shard_map/ppermute | solution.py:173
  84.4 24.6 %collective-permute-start.15 = (bf16[2,256,256]{2,1,0:T(8,128)(2,1)S(1)}, bf16[2,256,256]{2,1,0:T(8,128)(2,1)S(1)}, u32[]{:S(2)}, u32[]{:S(2)}) collective-permute-start(bf16[2,256,256]{2,1,0:T(8,128)(2,1)S(1)} %shard_map.51), channel_id=1, source_target_pairs={{0,4},{1,5},{2,6},{3,7},{4,0},{5,1},{6,2},{7,3},{8,12},{9,13},{10,... | collective-permute-start | bytes 786440 | tf_op jit(solution)/shard_map/ppermute | solution.py:173
  89.7 22.4 %collective-permute-start.18 = (bf16[4,256,256]{2,1,0:T(8,128)(2,1)S(1)}, bf16[4,256,256]{2,1,0:T(8,128)(2,1)S(1)}, u32[]{:S(2)}, u32[]{:S(2)}) collective-permute-start(bf16[4,256,256]{2,1,0:T(8,128)(2,1)S(1)} %get-tuple-element.43), channel_id=1, source_target_pairs={{4,8},{5,9},{6,10},{7,11},{8,4},{9,5},{10,6},{11,7},{20,24},{21,25... | collective-permute-start | bytes 1572872 | tf_op jit(solution)/shard_map/ppermute | solution.py:173
  105.1 13.4 %collective-permute-start.17 = (bf16[4,256,256]{2,1,0:T(8,128)(2,1)S(1)}, bf16[4,256,256]{2,1,0:T(8,128)(2,1)S(1)}, u32[]{:S(2)}, u32[]{:S(2)}) collective-permute-start(bf16[4,256,256]{2,1,0:T(8,128)(2,1)S(1)} %shard_map.55), channel_id=1, source_target_pairs={{0,12},{1,13},{2,14},{3,15},{12,0},{13,1},{14,2},{15,3},{16,28},{1... | collective-permute-start | bytes 1572872 | tf_op jit(solution)/shard_map/ppermute | solution.py:173

commit v11 on v10

--- a/solution.py
+++ b/solution.py
@@ -189,7 +189,7 @@
     own = ([(left_env,), (exchange(left_env, 1, every),)], [(psi,), (exchange(psi, 1, every),)])
     own_0 = products(0, *own, (right_env,))
 
-    near, middle, own_0 = lax.optimization_barrier((near, middle, own_0))
+    middle, near, own_0 = lax.optimization_barrier((middle, near, own_0))
     far_in = exchange(near, 12, inner)
     far_out = exchange(middle, 4, inner)
     own_1 = products(1, *own, (near,))

time: 120 us -> 119 us (level)
  starting transfers between devices: 24.1 us -> 22 us
  waiting for transfers between devices: 72.7 us -> 74.4 us
    ppermute x19, starting transfers between devices: 24.1 us -> 22 us  [exchange(): return lax.ppermute(array, 'sec', [(s, s ^ bits) for s in members])]
    ppermute x19, waiting for transfers between devices: 72.7 us -> 74.4 us  [exchange(): return lax.ppermute(array, 'sec', [(s, s ^ bits) for s in members])]
  transfers between devices with their start and end apart: 19 -> 19, of which waited for: 10 -> 11; matrix products, arithmetic and copies ran while one was open for 0% -> 0% of each run, Pallas kernels for 14% -> 14%
where the time goes in v11:
time: 119 us
  waiting for transfers between devices  74.4 us (63%)
  starting transfers between devices  22 us (18%)
  Pallas kernels  17.7 us (15%)
  local copies, waits for them, and re-layouts  4.74 us (4%)
    ppermute x19, waiting for transfers between devices, exchange(): return lax.ppermute(array, 'sec', [(s, s ^ bits) for s in members])  74.4 us
    ppermute x19, starting transfers between devices, exchange(): return lax.ppermute(array, 'sec', [(s, s ^ bits) for s in members])  22 us
    pallas_call x7, Pallas kernels, slot(): pl.pallas_call(functools.partial(slot_kernel, step, parts, len(rights)),...  14.2 us
    unnamed x12, local copies, waits for them, and re-layouts  4.74 us
  transfers between devices with their start and end apart: 19, of which 11 were waited for; matrix products, arithmetic and copies ran while one was open for 0% of the time, Pallas kernels for 14%

profile of v11, /device:TPU:0, one launch (start us, length us, event | category | flops | bytes accessed | tf_op | source)
XLA Modules:
  0.0 119.0 jit_solution(14345529646752877691)
XLA Ops:
  0.0 0.5 collective-permute-start.3
  0.5 2.5 %collective-permute-start.4 = (bf16[1,16,256,256]{3,2,1,0:T(8,128)(2,1)}, bf16[1,16,256,256]{3,2,1,0:T(8,128)(2,1)S(1)}, u32[]{:S(2)}, u32[]{:S(2)}) collective-permute-start(bf16[1,16,256,256]{3,2,1,0:T(8,128)(2,1)} %refs_6_.2), channel_id=1, source_target_pairs={{0,2},{1,3},{2,0},{3,1},{4,6},{5,7},{6,4},{7,5},{8,10},{9,11},{10,... | collective-permute-start | bytes 6291464 | tf_op jit(solution)/shard_map/ppermute | solution.py:173
  2.9 0.2 collective-permute-start.2
  3.2 1.6 %collective-permute-start.1 = (bf16[8,1,256,256]{3,2,1,0:T(8,128)(2,1)}, bf16[8,1,256,256]{3,2,1,0:T(8,128)(2,1)S(1)}, u32[]{:S(2)}, u32[]{:S(2)}) collective-permute-start(bf16[8,1,256,256]{3,2,1,0:T(8,128)(2,1)} %refs_6_.1), channel_id=1, source_target_pairs={{0,4},{1,5},{2,6},{3,7},{4,0},{5,1},{6,2},{7,3},{8,12},{9,13},{10,... | collective-permute-start | bytes 3145736 | tf_op jit(solution)/shard_map/ppermute | solution.py:173
  4.7 0.7 collective-permute-start
  5.5 0.5 collective-permute-done.2.refs_1_
  6.0 0.0 collective-permute-done.3.refs_3_.refs_7_
  6.0 1.6 %copy-done = bf16[1,16,256,256]{3,2,1,0:T(8,128)(2,1)S(1)} copy-done((bf16[1,16,256,256]{3,2,1,0:T(8,128)(2,1)S(1)}, bf16[1,16,256,256]{3,2,1,0:T(8,128)(2,1)}, u32[]{:S(2)}) %copy-start) | copy-done | bytes 2097176
  7.5 1.2 %copy-done.2 = bf16[8,1,256,256]{3,2,1,0:T(8,128)(2,1)S(1)} copy-done((bf16[8,1,256,256]{3,2,1,0:T(8,128)(2,1)S(1)}, bf16[8,1,256,256]{3,2,1,0:T(8,128)(2,1)}, u32[]{:S(2)}) %copy-start.2) | copy-done | bytes 1048600
  8.8 1.2 %copy-done.4 = bf16[8,1,256,256]{3,2,1,0:T(8,128)(2,1)S(1)} copy-done((bf16[8,1,256,256]{3,2,1,0:T(8,128)(2,1)S(1)}, bf16[8,1,256,256]{3,2,1,0:T(8,128)(2,1)}, u32[]{:S(2)}) %copy-start.4) | copy-done | bytes 1048600
  10.0 0.7 copy-done.5
  10.7 1.9 %shard_map.46.refs_0_ = bf16[2,256,256]{2,1,0:T(8,128)(2,1)S(1)} custom-call(s32[8,16]{1,0:T(8,128)S(1)} %copy-done.5, bf16[8,1,256,256]{3,2,1,0:T(8,128)(2,1)S(1)} %copy-done.2, bf16[8,1,256,256]{3,2,1,0:T(8,128)(2,1)S(1)} %collective-permute-done.2.refs_1_, bf16[1,16,256,256]{3,2,1,0:T(8,128)(2,1)S(1)} %copy-done, ...), custom_call_target="tpu_custom_call" | custom-call | flops 1 | bytes 1 | tf_op jit(solution)/shard_map/pallas_call | solution.py:96
  12.6 16.2 %collective-permute-done.1.refs_4_.refs_6_ = bf16[8,1,256,256]{3,2,1,0:T(8,128)(2,1)S(1)} collective-permute-done((bf16[8,1,256,256]{3,2,1,0:T(8,128)(2,1)}, bf16[8,1,256,256]{3,2,1,0:T(8,128)(2,1)S(1)}, u32[]{:S(2)}, u32[]{:S(2)}) %collective-permute-start.1) | collective-permute-done | bytes 1048608 | tf_op jit(solution)/shard_map/ppermute | solution.py:173
  28.7 0.0 collective-permute-done.refs_10_
  28.7 1.3 %collective-permute-start.6 = (bf16[8,1,256,256]{3,2,1,0:T(8,128)(2,1)S(1)}, bf16[8,1,256,256]{3,2,1,0:T(8,128)(2,1)S(1)}, u32[]{:S(2)}, u32[]{:S(2)}) collective-permute-start(bf16[8,1,256,256]{3,2,1,0:T(8,128)(2,1)S(1)} %collective-permute-done.refs_10_), channel_id=1, source_target_pairs={{4,0},{5,1},{6,2},{7,3},{8,12},{9,13},{10,14},{11,15},{20,16},{21,... | collective-permute-start | bytes 3145736 | tf_op jit(solution)/shard_map/ppermute | solution.py:173
  30.0 0.7 collective-permute-start.7
  30.8 0.1 shard_map.47
  30.8 18.6 %collective-permute-done.4.refs_4_.refs_8_ = bf16[1,16,256,256]{3,2,1,0:T(8,128)(2,1)S(1)} collective-permute-done((bf16[1,16,256,256]{3,2,1,0:T(8,128)(2,1)}, bf16[1,16,256,256]{3,2,1,0:T(8,128)(2,1)S(1)}, u32[]{:S(2)}, u32[]{:S(2)}) %collective-permute-start.4) | collective-permute-done | bytes 2097184 | tf_op jit(solution)/shard_map/ppermute | solution.py:173
  49.5 1.7 %collective-permute-start.5 = (bf16[6,1,256,256]{3,2,1,0:T(8,128)(2,1)S(1)}, bf16[6,1,256,256]{3,2,1,0:T(8,128)(2,1)S(1)}, u32[]{:S(2)}, u32[]{:S(2)}) collective-permute-start(bf16[6,1,256,256]{3,2,1,0:T(8,128)(2,1)S(1)} %get-tuple-element.27), channel_id=1, source_target_pairs={{0,2},{1,3},{2,0},{3,1},{4,6},{5,7},{6,4},{7,5},{8,10},{9,11},{10,... | collective-permute-start | bytes 2359304 | tf_op jit(solution)/shard_map/ppermute | solution.py:173
  51.2 1.9 %shard_map.49 = bf16[2,256,256]{2,1,0:T(8,128)(2,1)S(1)} custom-call(s32[8,16]{1,0:T(8,128)S(1)} %copy-done.5, bf16[8,1,256,256]{3,2,1,0:T(8,128)(2,1)S(1)} %copy-done.2, bf16[8,1,256,256]{3,2,1,0:T(8,128)(2,1)S(1)} %collective-permute-done.2.refs_1_, bf16[1,16,256,256]{3,2,1,0:T(8,128)(2,1)S(1)} %copy-done, ...), custom_call_target="tpu_custom_call" | custom-call | flops 1 | bytes 1 | tf_op jit(solution)/shard_map/pallas_call | solution.py:96
  53.1 1.6 %collective-permute-start.8 = (bf16[2,256,256]{2,1,0:T(8,128)(2,1)S(1)}, bf16[2,256,256]{2,1,0:T(8,128)(2,1)S(1)}, u32[]{:S(2)}, u32[]{:S(2)}) collective-permute-start(bf16[2,256,256]{2,1,0:T(8,128)(2,1)S(1)} %shard_map.49), channel_id=1, source_target_pairs={{0,4},{1,5},{2,6},{3,7},{4,0},{5,1},{6,2},{7,3},{8,12},{9,13},{10,... | collective-permute-start | bytes 786440 | tf_op jit(solution)/shard_map/ppermute | solution.py:173
  54.7 3.9 %collective-permute-done.6.refs_4_.refs_6_ = bf16[8,1,256,256]{3,2,1,0:T(8,128)(2,1)S(1)} collective-permute-done((bf16[8,1,256,256]{3,2,1,0:T(8,128)(2,1)S(1)}, bf16[8,1,256,256]{3,2,1,0:T(8,128)(2,1)S(1)}, u32[]{:S(2)}, u32[]{:S(2)}) %collective-permute-start.6) | collective-permute-done | bytes 1048608 | tf_op jit(solution)/shard_map/ppermute | solution.py:173
  58.6 0.0 collective-permute-done.7.refs_5_.refs_7_
  58.6 1.9 %shard_map.48 = bf16[2,256,256]{2,1,0:T(8,128)(2,1)S(1)} custom-call(s32[8,16]{1,0:T(8,128)S(1)} %copy-done.5, bf16[8,1,256,256]{3,2,1,0:T(8,128)(2,1)S(1)} %copy-done.2, bf16[8,1,256,256]{3,2,1,0:T(8,128)(2,1)S(1)} %collective-permute-done.2.refs_1_, bf16[1,16,256,256]{3,2,1,0:T(8,128)(2,1)S(1)} %copy-done, ...), custom_call_target="tpu_custom_call" | custom-call | flops 1 | bytes 1 | tf_op jit(solution)/shard_map/pallas_call | solution.py:96
  60.5 2.5 %collective-permute-done.8.refs_2_ = bf16[2,256,256]{2,1,0:T(8,128)(2,1)S(1)} collective-permute-done((bf16[2,256,256]{2,1,0:T(8,128)(2,1)S(1)}, bf16[2,256,256]{2,1,0:T(8,128)(2,1)S(1)}, u32[]{:S(2)}, u32[]{:S(2)}) %collective-permute-start.8) | collective-permute-done | bytes 262176 | tf_op jit(solution)/shard_map/ppermute | solution.py:173
  63.0 0.5 collective-permute-start.9
  63.5 1.2 collective-permute-start.10
  64.7 1.3 %collective-permute-start.16 = (bf16[8,1,256,256]{3,2,1,0:T(8,128)(2,1)S(1)}, bf16[8,1,256,256]{3,2,1,0:T(8,128)(2,1)S(1)}, u32[]{:S(2)}, u32[]{:S(2)}) collective-permute-start(bf16[8,1,256,256]{3,2,1,0:T(8,128)(2,1)S(1)} %collective-permute-done.7.refs_5_.refs_7_), channel_id=1, source_target_pairs={{4,0},{5,1},{6,2},{7,3},{8,12},{9,13},{10,14},{11,15},{20,16},{21,... | collective-permute-start | bytes 3145736 | tf_op jit(solution)/shard_map/ppermute | solution.py:173
  66.0 3.8 %collective-permute-done.5.refs_0_.refs_2_ = bf16[6,1,256,256]{3,2,1,0:T(8,128)(2,1)S(1)} collective-permute-done((bf16[6,1,256,256]{3,2,1,0:T(8,128)(2,1)S(1)}, bf16[6,1,256,256]{3,2,1,0:T(8,128)(2,1)S(1)}, u32[]{:S(2)}, u32[]{:S(2)}) %collective-permute-start.5) | collective-permute-done | bytes 786464 | tf_op jit(solution)/shard_map/ppermute | solution.py:173
  69.8 5.2 %collective-permute-done.9.refs_1_.refs_3_ = bf16[2,1,256,256]{3,2,1,0:T(8,128)(2,1)S(1)} collective-permute-done((bf16[2,1,256,256]{3,2,1,0:T(8,128)(2,1)S(1)}, bf16[2,1,256,256]{3,2,1,0:T(8,128)(2,1)S(1)}, u32[]{:S(2)}, u32[]{:S(2)}) %collective-permute-start.9) | collective-permute-done | bytes 262176 | tf_op jit(solution)/shard_map/ppermute | solution.py:173
  75.0 1.9 %collective-permute-done.10.refs_4_ = bf16[2,256,256]{2,1,0:T(8,128)(2,1)S(1)} collective-permute-done((bf16[2,256,256]{2,1,0:T(8,128)(2,1)S(1)}, bf16[2,256,256]{2,1,0:T(8,128)(2,1)S(1)}, u32[]{:S(2)}, u32[]{:S(2)}) %collective-permute-start.10) | collective-permute-done | bytes 262176 | tf_op jit(solution)/shard_map/ppermute | solution.py:173
  77.0 0.5 collective-permute-start.12
  77.5 2.1 %collective-permute-done.12.refs_3_.refs_5_ = bf16[2,1,256,256]{3,2,1,0:T(8,128)(2,1)S(1)} collective-permute-done((bf16[2,1,256,256]{3,2,1,0:T(8,128)(2,1)S(1)}, bf16[2,1,256,256]{3,2,1,0:T(8,128)(2,1)S(1)}, u32[]{:S(2)}, u32[]{:S(2)}) %collective-permute-start.12) | collective-permute-done | bytes 262176 | tf_op jit(solution)/shard_map/ppermute | solution.py:173
  79.6 1.9 %shard_map.50 = bf16[2,256,256]{2,1,0:T(8,128)(2,1)S(1)} custom-call(s32[8,16]{1,0:T(8,128)S(1)} %copy-done.5, bf16[6,1,256,256]{3,2,1,0:T(8,128)(2,1)S(1)} %collective-permute-done.5.refs_0_.refs_2_, bf16[2,1,256,256]{3,2,1,0:T(8,128)(2,1)S(1)} %collective-permute-done.9.refs_1_.refs_3_, ...), custom_call_target="tpu_custom_call" | custom-call | flops 1 | bytes 1 | tf_op jit(solution)/shard_map/pallas_call | solution.py:96
  81.5 0.0 copy-start.1
  81.5 0.0 copy-start.3
  81.6 1.0 collective-permute-start.14
  82.5 1.9 %shard_map.51 = bf16[2,256,256]{2,1,0:T(8,128)(2,1)S(1)} custom-call(s32[8,16]{1,0:T(8,128)S(1)} %copy-done.5, bf16[6,1,256,256]{3,2,1,0:T(8,128)(2,1)S(1)} %collective-permute-done.5.refs_0_.refs_2_, bf16[2,1,256,256]{3,2,1,0:T(8,128)(2,1)S(1)} %collective-permute-done.9.refs_1_.refs_3_, ...), custom_call_target="tpu_custom_call" | custom-call | flops 1 | bytes 1 | tf_op jit(solution)/shard_map/pallas_call | solution.py:96
  84.4 2.3 %collective-permute-start.15 = (bf16[2,256,256]{2,1,0:T(8,128)(2,1)S(1)}, bf16[2,256,256]{2,1,0:T(8,128)(2,1)S(1)}, u32[]{:S(2)}, u32[]{:S(2)}) collective-permute-start(bf16[2,256,256]{2,1,0:T(8,128)(2,1)S(1)} %shard_map.51), channel_id=1, source_target_pairs={{0,4},{1,5},{2,6},{3,7},{4,0},{5,1},{6,2},{7,3},{8,12},{9,13},{10,... | collective-permute-start | bytes 786440 | tf_op jit(solution)/shard_map/ppermute | solution.py:173
  86.8 3.0 %shard_map.54 = (bf16[4,256,256]{2,1,0:T(8,128)(2,1)S(1)}, bf16[1024,2048]{1,0:T(8,128)(2,1)S(1)}) custom-call(s32[8,16]{1,0:T(8,128)S(1)} %copy-done.5, bf16[8,1,256,256]{3,2,1,0:T(8,128)(2,1)S(1)} %copy-done.3, bf16[8,1,256,256]{3,2,1,0:T(8,128)(2,1)S(1)} %collective-permute-done.2.refs_1_, ...), custom_call_target="tpu_custom_call" | custom-call | flops 1 | bytes 1 | tf_op jit(solution)/shard_map/pallas_call | solution.py:96
  89.7 0.7 collective-permute-start.18
  90.4 13.0 %collective-permute-done.16.right = bf16[8,1,256,256]{3,2,1,0:T(8,128)(2,1)S(1)} collective-permute-done((bf16[8,1,256,256]{3,2,1,0:T(8,128)(2,1)S(1)}, bf16[8,1,256,256]{3,2,1,0:T(8,128)(2,1)S(1)}, u32[]{:S(2)}, u32[]{:S(2)}) %collective-permute-start.16) | collective-permute-done | bytes 1048608 | tf_op jit(solution)/shard_map/ppermute | solution.py:173
  103.5 1.3 %shard_map.55 = bf16[4,256,256]{2,1,0:T(8,128)(2,1)S(1)} custom-call(bf16[1024,2048]{1,0:T(8,128)(2,1)S(1)} %get-tuple-element.42.mid, bf16[8,1,256,256]{3,2,1,0:T(8,128)(2,1)S(1)} %collective-permute-done.16.right), custom_call_target="tpu_custom_call" | custom-call | flops 1 | bytes 1 | tf_op jit(solution)/shard_map/pallas_call | solution.py:75
  104.8 3.6 %collective-permute-start.17 = (bf16[4,256,256]{2,1,0:T(8,128)(2,1)S(1)}, bf16[4,256,256]{2,1,0:T(8,128)(2,1)S(1)}, u32[]{:S(2)}, u32[]{:S(2)}) collective-permute-start(bf16[4,256,256]{2,1,0:T(8,128)(2,1)S(1)} %shard_map.55), channel_id=1, source_target_pairs={{0,12},{1,13},{2,14},{3,15},{12,0},{13,1},{14,2},{15,3},{16,28},{1... | collective-permute-start | bytes 1572872 | tf_op jit(solution)/shard_map/ppermute | solution.py:173
  108.4 1.9 %shard_map.52.refs_1_ = bf16[2,256,256]{2,1,0:T(8,128)(2,1)S(1)} custom-call(s32[8,16]{1,0:T(8,128)S(1)} %copy-done.5, bf16[6,1,256,256]{3,2,1,0:T(8,128)(2,1)S(1)} %collective-permute-done.5.refs_0_.refs_2_, bf16[2,1,256,256]{3,2,1,0:T(8,128)(2,1)S(1)} %collective-permute-done.9.refs_1_.refs_3_, ...), custom_call_target="tpu_custom_call" | custom-call | flops 10000000000 | bytes 1 | tf_op jit(solution)/shard_map/pallas_call | solution.py:96
  110.3 1.2 %shard_map.53.refs_0_ = bf16[16,256,256]{2,1,0:T(8,128)(2,1)} custom-call(bf16[2,256,256]{2,1,0:T(8,128)(2,1)S(1)} %shard_map.46.refs_0_, bf16[2,256,256]{2,1,0:T(8,128)(2,1)S(1)} %shard_map.52.refs_1_, bf16[2,256,256]{2,1,0:T(8,128)(2,1)S(1)} %collective-permute-done.8.refs_2_, bf16[2,256,256]{2,1,0:T(8,128)(2,1)S(1)} %collective-permute-done.15.refs_3_, ...), custom_call_target="tpu_custom_call" | custom-call | flops 1 | bytes 1 | tf_op jit(solution)/shard_map/pallas_call | solution.py:160
  111.5 6.6 %collective-permute-done.17.refs_1_ = bf16[4,256,256]{2,1,0:T(8,128)(2,1)S(1)} collective-permute-done((bf16[4,256,256]{2,1,0:T(8,128)(2,1)S(1)}, bf16[4,256,256]{2,1,0:T(8,128)(2,1)S(1)}, u32[]{:S(2)}, u32[]{:S(2)}) %collective-permute-start.17) | collective-permute-done | bytes 524320 | tf_op jit(solution)/shard_map/ppermute | solution.py:173
  118.1 0.9 shard_map.56
  (13 shorter events, 0.0 us)
Async XLA Ops:
  0.0 6.0 %collective-permute-start.3 = (bf16[1,16,256,256]{3,2,1,0:T(8,128)(2,1)}, bf16[1,16,256,256]{3,2,1,0:T(8,128)(2,1)S(1)}, u32[]{:S(2)}, u32[]{:S(2)}) collective-permute-start(bf16[1,16,256,256]{3,2,1,0:T(8,128)(2,1)} %refs_6_.2), channel_id=1, source_target_pairs={{0,1},{1,0},{2,3},{3,2},{4,5},{5,4},{6,7},{7,6},{8,9},{9,8},{10,11... | collective-permute-start | bytes 6291464 | tf_op jit(solution)/shard_map/ppermute | solution.py:173
  0.5 49.0 %collective-permute-start.4 = (bf16[1,16,256,256]{3,2,1,0:T(8,128)(2,1)}, bf16[1,16,256,256]{3,2,1,0:T(8,128)(2,1)S(1)}, u32[]{:S(2)}, u32[]{:S(2)}) collective-permute-start(bf16[1,16,256,256]{3,2,1,0:T(8,128)(2,1)} %refs_6_.2), channel_id=1, source_target_pairs={{0,2},{1,3},{2,0},{3,1},{4,6},{5,7},{6,4},{7,5},{8,10},{9,11},{10,... | collective-permute-start | bytes 6291464 | tf_op jit(solution)/shard_map/ppermute | solution.py:173
  2.9 3.0 %collective-permute-start.2 = (bf16[8,1,256,256]{3,2,1,0:T(8,128)(2,1)}, bf16[8,1,256,256]{3,2,1,0:T(8,128)(2,1)S(1)}, u32[]{:S(2)}, u32[]{:S(2)}) collective-permute-start(bf16[8,1,256,256]{3,2,1,0:T(8,128)(2,1)} %refs_0_.7), channel_id=1, source_target_pairs={{0,1},{1,0},{2,3},{3,2},{4,5},{5,4},{6,7},{7,6},{8,9},{9,8},{10,11... | collective-permute-start | bytes 3145736 | tf_op jit(solution)/shard_map/ppermute | solution.py:173
  3.2 25.6 %collective-permute-start.1 = (bf16[8,1,256,256]{3,2,1,0:T(8,128)(2,1)}, bf16[8,1,256,256]{3,2,1,0:T(8,128)(2,1)S(1)}, u32[]{:S(2)}, u32[]{:S(2)}) collective-permute-start(bf16[8,1,256,256]{3,2,1,0:T(8,128)(2,1)} %refs_6_.1), channel_id=1, source_target_pairs={{0,4},{1,5},{2,6},{3,7},{4,0},{5,1},{6,2},{7,3},{8,12},{9,13},{10,... | collective-permute-start | bytes 3145736 | tf_op jit(solution)/shard_map/ppermute | solution.py:173
  4.7 24.0 %collective-permute-start = (bf16[8,1,256,256]{3,2,1,0:T(8,128)(2,1)}, bf16[8,1,256,256]{3,2,1,0:T(8,128)(2,1)S(1)}, u32[]{:S(2)}, u32[]{:S(2)}) collective-permute-start(bf16[8,1,256,256]{3,2,1,0:T(8,128)(2,1)} %refs_6_.1), channel_id=1, source_target_pairs={{4,8},{5,9},{6,10},{7,11},{8,4},{9,5},{10,6},{11,7},{20,24},{21,25... | collective-permute-start | bytes 3145736 | tf_op jit(solution)/shard_map/ppermute | solution.py:173
  6.0 1.6 %copy-start = (bf16[1,16,256,256]{3,2,1,0:T(8,128)(2,1)S(1)}, bf16[1,16,256,256]{3,2,1,0:T(8,128)(2,1)}, u32[]{:S(2)}) copy-start(bf16[1,16,256,256]{3,2,1,0:T(8,128)(2,1)} %refs_6_.2) | copy-start | bytes 6291460
  7.5 1.2 %copy-start.2 = (bf16[8,1,256,256]{3,2,1,0:T(8,128)(2,1)S(1)}, bf16[8,1,256,256]{3,2,1,0:T(8,128)(2,1)}, u32[]{:S(2)}) copy-start(bf16[8,1,256,256]{3,2,1,0:T(8,128)(2,1)} %refs_0_.7) | copy-start | bytes 3145732
  8.8 1.2 %copy-start.4 = (bf16[8,1,256,256]{3,2,1,0:T(8,128)(2,1)S(1)}, bf16[8,1,256,256]{3,2,1,0:T(8,128)(2,1)}, u32[]{:S(2)}) copy-start(bf16[8,1,256,256]{3,2,1,0:T(8,128)(2,1)} %refs_6_.1) | copy-start | bytes 3145732
  10.0 0.7 copy-start.5
  28.7 29.9 %collective-permute-start.6 = (bf16[8,1,256,256]{3,2,1,0:T(8,128)(2,1)S(1)}, bf16[8,1,256,256]{3,2,1,0:T(8,128)(2,1)S(1)}, u32[]{:S(2)}, u32[]{:S(2)}) collective-permute-start(bf16[8,1,256,256]{3,2,1,0:T(8,128)(2,1)S(1)} %collective-permute-done.refs_10_), channel_id=1, source_target_pairs={{4,0},{5,1},{6,2},{7,3},{8,12},{9,13},{10,14},{11,15},{20,16},{21,... | collective-permute-start | bytes 3145736 | tf_op jit(solution)/shard_map/ppermute | solution.py:173
  30.0 28.6 %collective-permute-start.7 = (bf16[8,1,256,256]{3,2,1,0:T(8,128)(2,1)S(1)}, bf16[8,1,256,256]{3,2,1,0:T(8,128)(2,1)S(1)}, u32[]{:S(2)}, u32[]{:S(2)}) collective-permute-start(bf16[8,1,256,256]{3,2,1,0:T(8,128)(2,1)S(1)} %collective-permute-done.1.refs_4_.refs_6_), channel_id=1, source_target_pairs={{4,8},{5,9},{6,10},{7,11},{8,4},{9,5},{10,6},{11,7},{20,24},{21,25... | collective-permute-start | bytes 3145736 | tf_op jit(solution)/shard_map/ppermute | solution.py:173
  49.5 30.2 %collective-permute-start.13 = (bf16[1,16,256,256]{3,2,1,0:T(8,128)(2,1)S(1)}, bf16[1,16,256,256]{3,2,1,0:T(8,128)(2,1)S(1)}, u32[]{:S(2)}, u32[]{:S(2)}) collective-permute-start(bf16[1,16,256,256]{3,2,1,0:T(8,128)(2,1)S(1)} %collective-permute-done.4.refs_4_.refs_8_), channel_id=1, source_target_pairs={{0,1},{1,0},{2,3},{3,2},{4,5},{5,4},{6,7},{7,6},{8,9},{9,8},{10,11... | collective-permute-start | bytes 6291464 | tf_op jit(solution)/shard_map/ppermute | solution.py:173
  49.5 20.3 %collective-permute-start.5 = (bf16[6,1,256,256]{3,2,1,0:T(8,128)(2,1)S(1)}, bf16[6,1,256,256]{3,2,1,0:T(8,128)(2,1)S(1)}, u32[]{:S(2)}, u32[]{:S(2)}) collective-permute-start(bf16[6,1,256,256]{3,2,1,0:T(8,128)(2,1)S(1)} %get-tuple-element.27), channel_id=1, source_target_pairs={{0,2},{1,3},{2,0},{3,1},{4,6},{5,7},{6,4},{7,5},{8,10},{9,11},{10,... | collective-permute-start | bytes 2359304 | tf_op jit(solution)/shard_map/ppermute | solution.py:173
  53.1 9.9 %collective-permute-start.8 = (bf16[2,256,256]{2,1,0:T(8,128)(2,1)S(1)}, bf16[2,256,256]{2,1,0:T(8,128)(2,1)S(1)}, u32[]{:S(2)}, u32[]{:S(2)}) collective-permute-start(bf16[2,256,256]{2,1,0:T(8,128)(2,1)S(1)} %shard_map.49), channel_id=1, source_target_pairs={{0,4},{1,5},{2,6},{3,7},{4,0},{5,1},{6,2},{7,3},{8,12},{9,13},{10,... | collective-permute-start | bytes 786440 | tf_op jit(solution)/shard_map/ppermute | solution.py:173
  63.0 12.0 %collective-permute-start.9 = (bf16[2,1,256,256]{3,2,1,0:T(8,128)(2,1)S(1)}, bf16[2,1,256,256]{3,2,1,0:T(8,128)(2,1)S(1)}, u32[]{:S(2)}, u32[]{:S(2)}) collective-permute-start(bf16[2,1,256,256]{3,2,1,0:T(8,128)(2,1)S(1)} %get-tuple-element.33), channel_id=1, source_target_pairs={{0,2},{1,3},{2,0},{3,1},{4,6},{5,7},{6,4},{7,5},{8,10},{9,11},{10,... | collective-permute-start | bytes 786440 | tf_op jit(solution)/shard_map/ppermute | solution.py:173
  63.5 13.4 %collective-permute-start.10 = (bf16[2,256,256]{2,1,0:T(8,128)(2,1)S(1)}, bf16[2,256,256]{2,1,0:T(8,128)(2,1)S(1)}, u32[]{:S(2)}, u32[]{:S(2)}) collective-permute-start(bf16[2,256,256]{2,1,0:T(8,128)(2,1)S(1)} %shard_map.48), channel_id=1, source_target_pairs={{0,8},{1,9},{2,10},{3,11},{4,12},{5,13},{6,14},{7,15},{8,0},{9,1},... | collective-permute-start | bytes 786440 | tf_op jit(solution)/shard_map/ppermute | solution.py:173
  64.7 38.8 %collective-permute-start.16 = (bf16[8,1,256,256]{3,2,1,0:T(8,128)(2,1)S(1)}, bf16[8,1,256,256]{3,2,1,0:T(8,128)(2,1)S(1)}, u32[]{:S(2)}, u32[]{:S(2)}) collective-permute-start(bf16[8,1,256,256]{3,2,1,0:T(8,128)(2,1)S(1)} %collective-permute-done.7.refs_5_.refs_7_), channel_id=1, source_target_pairs={{4,0},{5,1},{6,2},{7,3},{8,12},{9,13},{10,14},{11,15},{20,16},{21,... | collective-permute-start | bytes 3145736 | tf_op jit(solution)/shard_map/ppermute | solution.py:173
  77.0 2.7 %collective-permute-start.11 = (bf16[6,1,256,256]{3,2,1,0:T(8,128)(2,1)S(1)}, bf16[6,1,256,256]{3,2,1,0:T(8,128)(2,1)S(1)}, u32[]{:S(2)}, u32[]{:S(2)}) collective-permute-start(bf16[6,1,256,256]{3,2,1,0:T(8,128)(2,1)S(1)} %collective-permute-done.5.refs_0_.refs_2_), channel_id=1, source_target_pairs={{0,1},{1,0},{2,3},{3,2},{4,5},{5,4},{6,7},{7,6},{8,9},{9,8},{10,11... | collective-permute-start | bytes 2359304 | tf_op jit(solution)/shard_map/ppermute | solution.py:173
  77.0 2.7 %collective-permute-start.12 = (bf16[2,1,256,256]{3,2,1,0:T(8,128)(2,1)S(1)}, bf16[2,1,256,256]{3,2,1,0:T(8,128)(2,1)S(1)}, u32[]{:S(2)}, u32[]{:S(2)}) collective-permute-start(bf16[2,1,256,256]{3,2,1,0:T(8,128)(2,1)S(1)} %collective-permute-done.9.refs_1_.refs_3_), channel_id=1, source_target_pairs={{0,1},{1,0},{2,3},{3,2},{4,5},{5,4},{6,7},{7,6},{8,9},{9,8},{10,11... | collective-permute-start | bytes 786440 | tf_op jit(solution)/shard_map/ppermute | solution.py:173
  81.5 5.2 %copy-start.1 = (bf16[1,16,256,256]{3,2,1,0:T(8,128)(2,1)S(1)}, bf16[1,16,256,256]{3,2,1,0:T(8,128)(2,1)}, u32[]{:S(2)}) copy-start(bf16[1,16,256,256]{3,2,1,0:T(8,128)(2,1)} %refs_6_.2) | copy-start | bytes 6291460
  81.5 5.2 %copy-start.3 = (bf16[8,1,256,256]{3,2,1,0:T(8,128)(2,1)S(1)}, bf16[8,1,256,256]{3,2,1,0:T(8,128)(2,1)}, u32[]{:S(2)}) copy-start(bf16[8,1,256,256]{3,2,1,0:T(8,128)(2,1)} %refs_0_.7) | copy-start | bytes 3145732
  81.6 26.8 %collective-permute-start.14 = (bf16[2,256,256]{2,1,0:T(8,128)(2,1)S(1)}, bf16[2,256,256]{2,1,0:T(8,128)(2,1)S(1)}, u32[]{:S(2)}, u32[]{:S(2)}) collective-permute-start(bf16[2,256,256]{2,1,0:T(8,128)(2,1)S(1)} %shard_map.50), channel_id=1, source_target_pairs={{0,8},{1,9},{2,10},{3,11},{4,12},{5,13},{6,14},{7,15},{8,0},{9,1},... | collective-permute-start | bytes 786440 | tf_op jit(solution)/shard_map/ppermute | solution.py:173
  84.4 24.0 %collective-permute-start.15 = (bf16[2,256,256]{2,1,0:T(8,128)(2,1)S(1)}, bf16[2,256,256]{2,1,0:T(8,128)(2,1)S(1)}, u32[]{:S(2)}, u32[]{:S(2)}) collective-permute-start(bf16[2,256,256]{2,1,0:T(8,128)(2,1)S(1)} %shard_map.51), channel_id=1, source_target_pairs={{0,4},{1,5},{2,6},{3,7},{4,0},{5,1},{6,2},{7,3},{8,12},{9,13},{10,... | collective-permute-start | bytes 786440 | tf_op jit(solution)/shard_map/ppermute | solution.py:173
  89.7 21.8 %collective-permute-start.18 = (bf16[4,256,256]{2,1,0:T(8,128)(2,1)S(1)}, bf16[4,256,256]{2,1,0:T(8,128)(2,1)S(1)}, u32[]{:S(2)}, u32[]{:S(2)}) collective-permute-start(bf16[4,256,256]{2,1,0:T(8,128)(2,1)S(1)} %get-tuple-element.43), channel_id=1, source_target_pairs={{4,8},{5,9},{6,10},{7,11},{8,4},{9,5},{10,6},{11,7},{20,24},{21,25... | collective-permute-start | bytes 1572872 | tf_op jit(solution)/shard_map/ppermute | solution.py:173
  104.8 13.4 %collective-permute-start.17 = (bf16[4,256,256]{2,1,0:T(8,128)(2,1)S(1)}, bf16[4,256,256]{2,1,0:T(8,128)(2,1)S(1)}, u32[]{:S(2)}, u32[]{:S(2)}) collective-permute-start(bf16[4,256,256]{2,1,0:T(8,128)(2,1)S(1)} %shard_map.55), channel_id=1, source_target_pairs={{0,12},{1,13},{2,14},{3,15},{12,0},{13,1},{14,2},{15,3},{16,28},{1... | collective-permute-start | bytes 1572872 | tf_op jit(solution)/shard_map/ppermute | solution.py:173

commit v12 on v10

--- a/solution.py
+++ b/solution.py
@@ -63,24 +63,27 @@
     out[...] = total.reshape(out.shape).astype(out.dtype)
 
 
-def second_kernel(mid, right, out, right_buf):
+def second_kernel(*refs):
+    *mids, right, out, right_buf = refs
     terms, _, _, columns = right.shape
     for k in range(terms):
         right_buf[:, pl.ds(k * columns, columns)] = right[k, 0]
-    second_product(mid, right_buf, out)
-
-
-def second(mid, right, dtype):
+    size = out.shape[0] // len(mids)
+    for i, mid in enumerate(mids):
+        second_product(mid, right_buf, out.at[pl.ds(i * size, size)])
+
+
+def second(mids, right, dtype, flops):
     terms, _, rows, columns = right.shape
     return pl.pallas_call(
         second_kernel,
-        out_shape=jax.ShapeDtypeStruct((mid.shape[0] // rows, rows, columns), dtype),
-        in_specs=[VMEM, VMEM],
+        out_shape=jax.ShapeDtypeStruct((sum(mid.shape[0] for mid in mids) // rows, rows, columns), dtype),
+        in_specs=[VMEM] * (len(mids) + 1),
         out_specs=VMEM,
         scratch_shapes=[pltpu.VMEM((rows, terms * columns), jnp.bfloat16)],
         compiler_params=pltpu.CompilerParams(vmem_limit_bytes=16 << 20),
-        cost_estimate=pl.CostEstimate(flops=1, bytes_accessed=1, transcendentals=0),
-    )(mid, right)
+        cost_estimate=pl.CostEstimate(flops=flops, bytes_accessed=1, transcendentals=0),
+    )(*mids, right)
 
 
 def slot(step, source_map, lefts, psis, rights, dtype, flops, keep_mid):
@@ -104,20 +107,24 @@
     )(source_map, *held)
 
 
-def split_kernel(whole, low, high):
-    first = low.shape[0]
-    low[...] = whole[:first]
-    high[...] = whole[first:]
-
-
-def split(array, first):
-    sizes = (first, array.shape[0] - first)
-    return pl.pallas_call(
-        split_kernel,
-        out_shape=tuple(jax.ShapeDtypeStruct((size,) + array.shape[1:], array.dtype) for size in sizes),
+def split_kernel(axis, whole, low, high):
+    first = low.shape[axis]
+    before = (slice(None),) * axis
+    low[...] = whole[(*before, slice(0, first))]
+    high[...] = whole[(*before, slice(first, None))]
+
+
+def split(array, axis, first):
+    def part(size):
+        shape = array.shape[:axis] + (size,) + array.shape[axis + 1 :]
+        return jax.ShapeDtypeStruct(shape, array.dtype)
+
+    return pl.pallas_call(
+        functools.partial(split_kernel, axis),
+        out_shape=(part(first), part(array.shape[axis] - first)),
         in_specs=[VMEM],
         out_specs=(VMEM, VMEM),
-        compiler_params=pltpu.CompilerParams(vmem_limit_bytes=8 << 20),
+        compiler_params=pltpu.CompilerParams(vmem_limit_bytes=12 << 20),
         cost_estimate=pl.CostEstimate(flops=1, bytes_accessed=1, transcendentals=0),
     )(array)
 
@@ -138,7 +145,7 @@
         for copy in copies(pieces):
             copy.start()
     else:
-        pieces = pieces[-2:]
+        pieces = pieces[1:]
 
         @pl.when(outer)
         def _():
@@ -150,12 +157,14 @@
             for copy in copies(pieces[1:]):
                 copy.start()
 
-    for copy in copies(pieces[-1:] if choices == 2 else pieces):
+        pieces = pieces[:1]
+
+    for copy in copies(pieces):
         copy.wait()
 
 
 def place(first, sectors, pieces, out=None):
-    blocks = sum(piece.shape[0] for piece in pieces)
+    blocks = sum(piece.shape[0] for piece in (pieces if out is None else pieces[:1]))
     held = [] if out is None else [out]
     return pl.pallas_call(
         functools.partial(place_kernel, first, 1 if out is None else 2),
@@ -178,7 +187,7 @@
     every = range(16)
     inner = range(4, 12)
     outer = [s for s in every if s not in inner]
-    low, high = split(left_env, 3 * left_env.shape[0] // 4)
+    low, high = split(left_env, 0, 5 * left_env.shape[0] // 8)
 
     def products(step, lefts, psis, rights, flops=1, keep_mid=False):
         return slot(step, source_map, lefts, psis, rights, dtype, flops, keep_mid)
@@ -192,40 +201,39 @@
     near, middle, own_0 = lax.optimization_barrier((near, middle, own_0))
     far_in = exchange(near, 12, inner)
     far_out = exchange(middle, 4, inner)
-    own_1 = products(1, *own, (near,))
-    sent_1 = exchange(own_1, 4, every)
 
     x_psi, low = lax.optimization_barrier((x_psi, low))
     x_low = exchange(low, 2, every)
-    across_psi = exchange(x_psi, 1, every)
+    across_psi = [exchange(part, 1, every) for part in split(x_psi, 1, 5 * x_psi.shape[1] // 8)]
 
     far_out, far_in = lax.optimization_barrier((far_out, far_in))
     third = exchange(far_in, 4, inner)
+    own_middle, own_mid = products(3, *own, (middle,), keep_mid=True)
+    sent_own_middle = exchange(own_middle, 12, inner)
     own_2 = products(2, *own, (far_out, far_in))
     sent_2 = exchange(own_2, 8, every)
 
-    own_2, sent_1, high = lax.optimization_barrier((own_2, sent_1, high))
+    own_2, sent_own_middle, high = lax.optimization_barrier((own_2, sent_own_middle, high))
     x_high = exchange(high, 2, every)
-    x_low, x_high, sent_2 = lax.optimization_barrier((x_low, x_high, sent_2))
     across_low = exchange(x_low, 1, every)
+    x_high, sent_2 = lax.optimization_barrier((x_high, sent_2))
     across_high = exchange(x_high, 1, every)
-    other = ([(x_low, x_high), (across_low, across_high)], [(x_psi,), (across_psi,)])
-    both = (own[0] + other[0], own[1] + other[1])
+    other = ([(x_low, x_high), (across_low, across_high)], [(x_psi,), across_psi])
     other_2 = products(2, *other, (far_out, far_in))
     other_sent_2 = exchange(other_2, 8, every)
-    last_middle, mid = products(3, *both, (middle,), keep_mid=True)
-    sent_middle = exchange(last_middle, 12, inner)
-    other_1 = products(1, *other, (near,))
-    other_sent_1 = exchange(other_1, 4, every)
-
-    third, other_1, other_2, last_middle = lax.optimization_barrier((third, other_1, other_2, last_middle))
-    last_third = second(mid, third, dtype)
+    other_middle, other_mid = products(3, *other, (middle,), keep_mid=True)
+    sent_other_middle = exchange(other_middle, 12, inner)
+    both_1 = products(1, own[0] + other[0], own[1] + other[1], (near,))
+    sent_1 = exchange(both_1, 4, every)
+
+    third, both_1, other_2, other_middle = lax.optimization_barrier((third, both_1, other_2, other_middle))
+    last_third = second((own_mid, other_mid), third, dtype, 10**10)
     sent_third = exchange(last_third, 12, outer)
-    right_last, other_sent_2, other_sent_1 = lax.optimization_barrier((right_env, other_sent_2, other_sent_1))
+    right_last, other_sent_2, sent_1 = lax.optimization_barrier((right_env, other_sent_2, sent_1))
     other_0 = products(0, *other, (right_last,), flops=10**10)
 
-    out = place(0, 16, [own_0, other_0, sent_1, other_sent_1, sent_2, other_sent_2])
-    out = place(12, 16, [sent_third, sent_middle], out)[:, None]
+    out = place(0, 16, [own_0, other_0, sent_1, sent_2, other_sent_2])
+    out = place(12, 16, [sent_third, sent_own_middle, sent_other_middle], out)[:, None]
     if ops > 1:
         out = lax.psum_scatter(out, "op", scatter_dimension=2, tiled=True).astype(jnp.bfloat16)
     return out

time: 120 us -> 122 us (1.017)
  starting transfers between devices: 24.1 us -> 27.6 us
    ppermute x19 -> x20, starting transfers between devices: 24.1 us -> 27.6 us  [exchange(): return lax.ppermute(array, 'sec', [(s, s ^ bits) for s in members])]
    ppermute x19 -> x20, waiting for transfers between devices: 72.7 us -> 71.6 us  [exchange(): return lax.ppermute(array, 'sec', [(s, s ^ bits) for s in members])]
  transfers between devices with their start and end apart: 19 -> 20, of which waited for: 10 -> 9; matrix products, arithmetic and copies ran while one was open for 0% -> 0% of each run, Pallas kernels for 14% -> 14%
where the time goes in v12:
time: 122 us
  waiting for transfers between devices  71.6 us (59%)
  starting transfers between devices  27.6 us (23%)
  Pallas kernels  17.8 us (15%)
  local copies, waits for them, and re-layouts  4.73 us (4%)
    ppermute x20, waiting for transfers between devices, exchange(): return lax.ppermute(array, 'sec', [(s, s ^ bits) for s in members])  71.6 us
    ppermute x20, starting transfers between devices, exchange(): return lax.ppermute(array, 'sec', [(s, s ^ bits) for s in members])  27.6 us
    pallas_call x7, Pallas kernels, slot(): pl.pallas_call(functools.partial(slot_kernel, step, parts, len(rights)),...  14.3 us
    unnamed x12, local copies, waits for them, and re-layouts  4.73 us
  transfers between devices with their start and end apart: 20, of which 9 were waited for; matrix products, arithmetic and copies ran while one was open for 0% of the time, Pallas kernels for 14%

profile of v12, /device:TPU:0, one launch (start us, length us, event | category | flops | bytes accessed | tf_op | source)
XLA Modules:
  0.0 121.9 jit_solution(17559749472747834633)
XLA Ops:
  0.0 0.5 collective-permute-start.3
  0.5 2.5 %collective-permute-start.4 = (bf16[1,16,256,256]{3,2,1,0:T(8,128)(2,1)}, bf16[1,16,256,256]{3,2,1,0:T(8,128)(2,1)S(1)}, u32[]{:S(2)}, u32[]{:S(2)}) collective-permute-start(bf16[1,16,256,256]{3,2,1,0:T(8,128)(2,1)} %refs_6_.1), channel_id=1, source_target_pairs={{0,2},{1,3},{2,0},{3,1},{4,6},{5,7},{6,4},{7,5},{8,10},{9,11},{10,... | collective-permute-start | bytes 6291464 | tf_op jit(solution)/shard_map/ppermute | solution.py:182
  2.9 0.2 collective-permute-start.2
  3.2 1.6 %collective-permute-start = (bf16[8,1,256,256]{3,2,1,0:T(8,128)(2,1)}, bf16[8,1,256,256]{3,2,1,0:T(8,128)(2,1)S(1)}, u32[]{:S(2)}, u32[]{:S(2)}) collective-permute-start(bf16[8,1,256,256]{3,2,1,0:T(8,128)(2,1)} %refs_7_), channel_id=1, source_target_pairs={{0,4},{1,5},{2,6},{3,7},{4,0},{5,1},{6,2},{7,3},{8,12},{9,13},{10,... | collective-permute-start | bytes 3145736 | tf_op jit(solution)/shard_map/ppermute | solution.py:182
  4.7 0.7 collective-permute-start.1
  5.5 0.5 collective-permute-done.2.refs_1_
  6.0 0.0 collective-permute-done.3.refs_3_.refs_7_
  6.0 1.6 %copy-done = bf16[1,16,256,256]{3,2,1,0:T(8,128)(2,1)S(1)} copy-done((bf16[1,16,256,256]{3,2,1,0:T(8,128)(2,1)S(1)}, bf16[1,16,256,256]{3,2,1,0:T(8,128)(2,1)}, u32[]{:S(2)}) %copy-start) | copy-done | bytes 2097176
  7.5 1.2 %copy-done.2 = bf16[8,1,256,256]{3,2,1,0:T(8,128)(2,1)S(1)} copy-done((bf16[8,1,256,256]{3,2,1,0:T(8,128)(2,1)S(1)}, bf16[8,1,256,256]{3,2,1,0:T(8,128)(2,1)}, u32[]{:S(2)}) %copy-start.2) | copy-done | bytes 1048600
  8.8 1.2 %copy-done.3 = bf16[8,1,256,256]{3,2,1,0:T(8,128)(2,1)S(1)} copy-done((bf16[8,1,256,256]{3,2,1,0:T(8,128)(2,1)S(1)}, bf16[8,1,256,256]{3,2,1,0:T(8,128)(2,1)}, u32[]{:S(2)}) %copy-start.3) | copy-done | bytes 1048600
  10.0 0.7 copy-done.5
  10.7 1.9 %shard_map.46.refs_0_ = bf16[2,256,256]{2,1,0:T(8,128)(2,1)S(1)} custom-call(s32[8,16]{1,0:T(8,128)S(1)} %copy-done.5, bf16[8,1,256,256]{3,2,1,0:T(8,128)(2,1)S(1)} %copy-done.2, bf16[8,1,256,256]{3,2,1,0:T(8,128)(2,1)S(1)} %collective-permute-done.2.refs_1_, bf16[1,16,256,256]{3,2,1,0:T(8,128)(2,1)S(1)} %copy-done, ...), custom_call_target="tpu_custom_call" | custom-call | flops 1 | bytes 1 | tf_op jit(solution)/shard_map/pallas_call | solution.py:99
  12.6 16.2 %collective-permute-done.refs_11_ = bf16[8,1,256,256]{3,2,1,0:T(8,128)(2,1)S(1)} collective-permute-done((bf16[8,1,256,256]{3,2,1,0:T(8,128)(2,1)}, bf16[8,1,256,256]{3,2,1,0:T(8,128)(2,1)S(1)}, u32[]{:S(2)}, u32[]{:S(2)}) %collective-permute-start) | collective-permute-done | bytes 1048608 | tf_op jit(solution)/shard_map/ppermute | solution.py:182
  28.7 1.3 %collective-permute-start.6 = (bf16[8,1,256,256]{3,2,1,0:T(8,128)(2,1)S(1)}, bf16[8,1,256,256]{3,2,1,0:T(8,128)(2,1)S(1)}, u32[]{:S(2)}, u32[]{:S(2)}) collective-permute-start(bf16[8,1,256,256]{3,2,1,0:T(8,128)(2,1)S(1)} %collective-permute-done.1.refs_4_.refs_7_), channel_id=1, source_target_pairs={{4,0},{5,1},{6,2},{7,3},{8,12},{9,13},{10,14},{11,15},{20,16},{21,... | collective-permute-start | bytes 3145736 | tf_op jit(solution)/shard_map/ppermute | solution.py:182
  30.0 0.7 collective-permute-start.7
  30.8 0.1 shard_map.47
  30.8 18.6 %collective-permute-done.4.whole.refs_4_.refs_8_ = bf16[1,16,256,256]{3,2,1,0:T(8,128)(2,1)S(1)} collective-permute-done((bf16[1,16,256,256]{3,2,1,0:T(8,128)(2,1)}, bf16[1,16,256,256]{3,2,1,0:T(8,128)(2,1)S(1)}, u32[]{:S(2)}, u32[]{:S(2)}) %collective-permute-start.4) | collective-permute-done | bytes 2097184 | tf_op jit(solution)/shard_map/ppermute | solution.py:182
  49.5 1.7 %collective-permute-start.5 = (bf16[5,1,256,256]{3,2,1,0:T(8,128)(2,1)S(1)}, bf16[5,1,256,256]{3,2,1,0:T(8,128)(2,1)S(1)}, u32[]{:S(2)}, u32[]{:S(2)}) collective-permute-start(bf16[5,1,256,256]{3,2,1,0:T(8,128)(2,1)S(1)} %get-tuple-element.30), channel_id=1, source_target_pairs={{0,2},{1,3},{2,0},{3,1},{4,6},{5,7},{6,4},{7,5},{8,10},{9,11},{10,... | collective-permute-start | bytes 1966088 | tf_op jit(solution)/shard_map/ppermute | solution.py:182
  51.2 0.1 shard_map.50
  51.3 0.1 collective-permute-start.13
  51.4 1.9 %shard_map.49 = (bf16[2,256,256]{2,1,0:T(8,128)(2,1)S(1)}, bf16[512,2048]{1,0:T(8,128)(2,1)S(1)}) custom-call(s32[8,16]{1,0:T(8,128)S(1)} %copy-done.5, bf16[8,1,256,256]{3,2,1,0:T(8,128)(2,1)S(1)} %copy-done.2, bf16[8,1,256,256]{3,2,1,0:T(8,128)(2,1)S(1)} %collective-permute-done.2.refs_1_, bf16[1,16,256,256]{3,2,1,0:T(8,128)(2,1)S(1)} %copy-done, ...), custom_call_target="tpu_custom_call" | custom-call | flops 1 | bytes 1 | tf_op jit(solution)/shard_map/pallas_call | solution.py:99
  53.3 0.7 collective-permute-start.8
  54.0 3.4 %collective-permute-done.6.refs_4_.refs_7_ = bf16[8,1,256,256]{3,2,1,0:T(8,128)(2,1)S(1)} collective-permute-done((bf16[8,1,256,256]{3,2,1,0:T(8,128)(2,1)S(1)}, bf16[8,1,256,256]{3,2,1,0:T(8,128)(2,1)S(1)}, u32[]{:S(2)}, u32[]{:S(2)}) %collective-permute-start.6) | collective-permute-done | bytes 1048608 | tf_op jit(solution)/shard_map/ppermute | solution.py:182
  57.4 0.0 collective-permute-done.7.refs_5_.refs_8_
  57.4 1.3 %collective-permute-start.17 = (bf16[8,1,256,256]{3,2,1,0:T(8,128)(2,1)S(1)}, bf16[8,1,256,256]{3,2,1,0:T(8,128)(2,1)S(1)}, u32[]{:S(2)}, u32[]{:S(2)}) collective-permute-start(bf16[8,1,256,256]{3,2,1,0:T(8,128)(2,1)S(1)} %collective-permute-done.7.refs_5_.refs_8_), channel_id=1, source_target_pairs={{4,0},{5,1},{6,2},{7,3},{8,12},{9,13},{10,14},{11,15},{20,16},{21,... | collective-permute-start | bytes 3145736 | tf_op jit(solution)/shard_map/ppermute | solution.py:182
  58.7 1.9 %shard_map.48 = bf16[2,256,256]{2,1,0:T(8,128)(2,1)S(1)} custom-call(s32[8,16]{1,0:T(8,128)S(1)} %copy-done.5, bf16[8,1,256,256]{3,2,1,0:T(8,128)(2,1)S(1)} %copy-done.2, bf16[8,1,256,256]{3,2,1,0:T(8,128)(2,1)S(1)} %collective-permute-done.2.refs_1_, bf16[1,16,256,256]{3,2,1,0:T(8,128)(2,1)S(1)} %copy-done, ...), custom_call_target="tpu_custom_call" | custom-call | flops 1 | bytes 1 | tf_op jit(solution)/shard_map/pallas_call | solution.py:99
  60.6 5.7 %collective-permute-start.10 = (bf16[2,256,256]{2,1,0:T(8,128)(2,1)S(1)}, bf16[2,256,256]{2,1,0:T(8,128)(2,1)S(1)}, u32[]{:S(2)}, u32[]{:S(2)}) collective-permute-start(bf16[2,256,256]{2,1,0:T(8,128)(2,1)S(1)} %shard_map.48), channel_id=1, source_target_pairs={{0,8},{1,9},{2,10},{3,11},{4,12},{5,13},{6,14},{7,15},{8,0},{9,1},... | collective-permute-start | bytes 786440 | tf_op jit(solution)/shard_map/ppermute | solution.py:182
  66.3 0.0 collective-permute-done.8.refs_2_
  66.3 0.5 collective-permute-start.9
  66.9 0.0 collective-permute-done.5.refs_0_.refs_2_
  66.9 10.6 %collective-permute-done.10.refs_3_ = bf16[2,256,256]{2,1,0:T(8,128)(2,1)S(1)} collective-permute-done((bf16[2,256,256]{2,1,0:T(8,128)(2,1)S(1)}, bf16[2,256,256]{2,1,0:T(8,128)(2,1)S(1)}, u32[]{:S(2)}, u32[]{:S(2)}) %collective-permute-start.10) | collective-permute-done | bytes 262176 | tf_op jit(solution)/shard_map/ppermute | solution.py:182
  77.5 0.5 collective-permute-start.12
  78.0 1.6 %collective-permute-done.11.refs_2_.refs_4_ = bf16[5,1,256,256]{3,2,1,0:T(8,128)(2,1)S(1)} collective-permute-done((bf16[5,1,256,256]{3,2,1,0:T(8,128)(2,1)S(1)}, bf16[5,1,256,256]{3,2,1,0:T(8,128)(2,1)S(1)}, u32[]{:S(2)}, u32[]{:S(2)}) %collective-permute-start.11) | collective-permute-done | bytes 655392 | tf_op jit(solution)/shard_map/ppermute | solution.py:182
  79.6 0.6 collective-permute-done.12.refs_3_.refs_5_
  80.2 1.9 %shard_map.51 = bf16[2,256,256]{2,1,0:T(8,128)(2,1)S(1)} custom-call(s32[8,16]{1,0:T(8,128)S(1)} %copy-done.5, bf16[5,1,256,256]{3,2,1,0:T(8,128)(2,1)S(1)} %collective-permute-done.5.refs_0_.refs_2_, bf16[3,1,256,256]{3,2,1,0:T(8,128)(2,1)S(1)} %collective-permute-done.9.refs_1_.refs_3_, ...), custom_call_target="tpu_custom_call" | custom-call | flops 1 | bytes 1 | tf_op jit(solution)/shard_map/pallas_call | solution.py:99
  82.1 3.6 %collective-permute-start.15 = (bf16[2,256,256]{2,1,0:T(8,128)(2,1)S(1)}, bf16[2,256,256]{2,1,0:T(8,128)(2,1)S(1)}, u32[]{:S(2)}, u32[]{:S(2)}) collective-permute-start(bf16[2,256,256]{2,1,0:T(8,128)(2,1)S(1)} %shard_map.51), channel_id=1, source_target_pairs={{0,8},{1,9},{2,10},{3,11},{4,12},{5,13},{6,14},{7,15},{8,0},{9,1},... | collective-permute-start | bytes 786440 | tf_op jit(solution)/shard_map/ppermute | solution.py:182
  85.7 3.0 %shard_map.52 = bf16[4,256,256]{2,1,0:T(8,128)(2,1)S(1)} custom-call(s32[8,16]{1,0:T(8,128)S(1)} %copy-done.5, bf16[8,1,256,256]{3,2,1,0:T(8,128)(2,1)S(1)} %copy-done.2, bf16[8,1,256,256]{3,2,1,0:T(8,128)(2,1)S(1)} %collective-permute-done.2.refs_1_, bf16[5,1,256,256]{3,2,1,0:T(8,128)(2,1)S(1)} %collective-permute-done.5.refs_0_.refs_2_, ...), custom_call_target="tpu_custom_call" | custom-call | flops 1 | bytes 1 | tf_op jit(solution)/shard_map/pallas_call | solution.py:99
  88.7 0.1 collective-permute-start.16
  88.8 1.9 %shard_map.55 = (bf16[2,256,256]{2,1,0:T(8,128)(2,1)S(1)}, bf16[512,2048]{1,0:T(8,128)(2,1)S(1)}) custom-call(s32[8,16]{1,0:T(8,128)S(1)} %copy-done.5, bf16[5,1,256,256]{3,2,1,0:T(8,128)(2,1)S(1)} %collective-permute-done.5.refs_0_.refs_2_, bf16[3,1,256,256]{3,2,1,0:T(8,128)(2,1)S(1)} %collective-permute-done.9.refs_1_.refs_3_, ...), custom_call_target="tpu_custom_call" | custom-call | flops 1 | bytes 1 | tf_op jit(solution)/shard_map/pallas_call | solution.py:99
  90.6 0.7 collective-permute-start.19
  91.3 0.0 collective-permute-done.17.refs_2_
  91.4 1.3 %shard_map.56 = bf16[4,256,256]{2,1,0:T(8,128)(2,1)S(1)} custom-call(bf16[512,2048]{1,0:T(8,128)(2,1)S(1)} %get-tuple-element.46.refs_0_, bf16[512,2048]{1,0:T(8,128)(2,1)S(1)} %get-tuple-element.47.refs_1_, bf16[8,1,256,256]{3,2,1,0:T(8,128)(2,1)S(1)} %collective-permute-done.17.refs_2_), custom_call_target="tpu_custom_call" | custom-call | flops 10000000000 | bytes 1 | tf_op jit(solution)/shard_map/pallas_call | solution.py:78
  92.6 5.2 %collective-permute-start.18 = (bf16[4,256,256]{2,1,0:T(8,128)(2,1)S(1)}, bf16[4,256,256]{2,1,0:T(8,128)(2,1)S(1)}, u32[]{:S(2)}, u32[]{:S(2)}) collective-permute-start(bf16[4,256,256]{2,1,0:T(8,128)(2,1)S(1)} %shard_map.56), channel_id=1, source_target_pairs={{0,12},{1,13},{2,14},{3,15},{12,0},{13,1},{14,2},{15,3},{16,28},{1... | collective-permute-start | bytes 1572872 | tf_op jit(solution)/shard_map/ppermute | solution.py:182
  97.8 0.7 collective-permute-done.15.refs_4_
  98.5 19.4 %collective-permute-done.16.refs_2_ = bf16[4,256,256]{2,1,0:T(8,128)(2,1)S(1)} collective-permute-done((bf16[4,256,256]{2,1,0:T(8,128)(2,1)S(1)}, bf16[4,256,256]{2,1,0:T(8,128)(2,1)S(1)}, u32[]{:S(2)}, u32[]{:S(2)}) %collective-permute-start.16) | collective-permute-done | bytes 524320 | tf_op jit(solution)/shard_map/ppermute | solution.py:182
  117.9 1.9 %shard_map.53.refs_1_ = bf16[2,256,256]{2,1,0:T(8,128)(2,1)S(1)} custom-call(s32[8,16]{1,0:T(8,128)S(1)} %copy-done.5, bf16[5,1,256,256]{3,2,1,0:T(8,128)(2,1)S(1)} %collective-permute-done.5.refs_0_.refs_2_, bf16[3,1,256,256]{3,2,1,0:T(8,128)(2,1)S(1)} %collective-permute-done.9.refs_1_.refs_3_, ...), custom_call_target="tpu_custom_call" | custom-call | flops 10000000000 | bytes 1 | tf_op jit(solution)/shard_map/pallas_call | solution.py:99
  119.8 1.2 %shard_map.54.refs_0_ = bf16[16,256,256]{2,1,0:T(8,128)(2,1)} custom-call(bf16[2,256,256]{2,1,0:T(8,128)(2,1)S(1)} %shard_map.46.refs_0_, bf16[2,256,256]{2,1,0:T(8,128)(2,1)S(1)} %shard_map.53.refs_1_, bf16[4,256,256]{2,1,0:T(8,128)(2,1)S(1)} %collective-permute-done.16.refs_2_, bf16[2,256,256]{2,1,0:T(8,128)(2,1)S(1)} %collective-permute-done.10.refs_3_, ...), custom_call_target="tpu_custom_call" | custom-call | flops 1 | bytes 1 | tf_op jit(solution)/shard_map/pallas_call | solution.py:169
  121.1 0.8 shard_map.57
  (16 shorter events, 0.0 us)
Async XLA Ops:
  0.0 6.0 %collective-permute-start.3 = (bf16[1,16,256,256]{3,2,1,0:T(8,128)(2,1)}, bf16[1,16,256,256]{3,2,1,0:T(8,128)(2,1)S(1)}, u32[]{:S(2)}, u32[]{:S(2)}) collective-permute-start(bf16[1,16,256,256]{3,2,1,0:T(8,128)(2,1)} %refs_6_.1), channel_id=1, source_target_pairs={{0,1},{1,0},{2,3},{3,2},{4,5},{5,4},{6,7},{7,6},{8,9},{9,8},{10,11... | collective-permute-start | bytes 6291464 | tf_op jit(solution)/shard_map/ppermute | solution.py:182
  0.5 49.0 %collective-permute-start.4 = (bf16[1,16,256,256]{3,2,1,0:T(8,128)(2,1)}, bf16[1,16,256,256]{3,2,1,0:T(8,128)(2,1)S(1)}, u32[]{:S(2)}, u32[]{:S(2)}) collective-permute-start(bf16[1,16,256,256]{3,2,1,0:T(8,128)(2,1)} %refs_6_.1), channel_id=1, source_target_pairs={{0,2},{1,3},{2,0},{3,1},{4,6},{5,7},{6,4},{7,5},{8,10},{9,11},{10,... | collective-permute-start | bytes 6291464 | tf_op jit(solution)/shard_map/ppermute | solution.py:182
  2.9 3.0 %collective-permute-start.2 = (bf16[8,1,256,256]{3,2,1,0:T(8,128)(2,1)}, bf16[8,1,256,256]{3,2,1,0:T(8,128)(2,1)S(1)}, u32[]{:S(2)}, u32[]{:S(2)}) collective-permute-start(bf16[8,1,256,256]{3,2,1,0:T(8,128)(2,1)} %refs_0_.7), channel_id=1, source_target_pairs={{0,1},{1,0},{2,3},{3,2},{4,5},{5,4},{6,7},{7,6},{8,9},{9,8},{10,11... | collective-permute-start | bytes 3145736 | tf_op jit(solution)/shard_map/ppermute | solution.py:182
  3.2 25.6 %collective-permute-start = (bf16[8,1,256,256]{3,2,1,0:T(8,128)(2,1)}, bf16[8,1,256,256]{3,2,1,0:T(8,128)(2,1)S(1)}, u32[]{:S(2)}, u32[]{:S(2)}) collective-permute-start(bf16[8,1,256,256]{3,2,1,0:T(8,128)(2,1)} %refs_7_), channel_id=1, source_target_pairs={{0,4},{1,5},{2,6},{3,7},{4,0},{5,1},{6,2},{7,3},{8,12},{9,13},{10,... | collective-permute-start | bytes 3145736 | tf_op jit(solution)/shard_map/ppermute | solution.py:182
  4.7 24.0 %collective-permute-start.1 = (bf16[8,1,256,256]{3,2,1,0:T(8,128)(2,1)}, bf16[8,1,256,256]{3,2,1,0:T(8,128)(2,1)S(1)}, u32[]{:S(2)}, u32[]{:S(2)}) collective-permute-start(bf16[8,1,256,256]{3,2,1,0:T(8,128)(2,1)} %refs_7_), channel_id=1, source_target_pairs={{4,8},{5,9},{6,10},{7,11},{8,4},{9,5},{10,6},{11,7},{20,24},{21,25... | collective-permute-start | bytes 3145736 | tf_op jit(solution)/shard_map/ppermute | solution.py:182
  6.0 1.6 %copy-start = (bf16[1,16,256,256]{3,2,1,0:T(8,128)(2,1)S(1)}, bf16[1,16,256,256]{3,2,1,0:T(8,128)(2,1)}, u32[]{:S(2)}) copy-start(bf16[1,16,256,256]{3,2,1,0:T(8,128)(2,1)} %refs_6_.1) | copy-start | bytes 6291460
  7.5 1.2 %copy-start.2 = (bf16[8,1,256,256]{3,2,1,0:T(8,128)(2,1)S(1)}, bf16[8,1,256,256]{3,2,1,0:T(8,128)(2,1)}, u32[]{:S(2)}) copy-start(bf16[8,1,256,256]{3,2,1,0:T(8,128)(2,1)} %refs_0_.7) | copy-start | bytes 3145732
  8.8 1.2 %copy-start.3 = (bf16[8,1,256,256]{3,2,1,0:T(8,128)(2,1)S(1)}, bf16[8,1,256,256]{3,2,1,0:T(8,128)(2,1)}, u32[]{:S(2)}) copy-start(bf16[8,1,256,256]{3,2,1,0:T(8,128)(2,1)} %refs_7_) | copy-start | bytes 3145732
  10.0 0.7 copy-start.5
  28.7 28.7 %collective-permute-start.6 = (bf16[8,1,256,256]{3,2,1,0:T(8,128)(2,1)S(1)}, bf16[8,1,256,256]{3,2,1,0:T(8,128)(2,1)S(1)}, u32[]{:S(2)}, u32[]{:S(2)}) collective-permute-start(bf16[8,1,256,256]{3,2,1,0:T(8,128)(2,1)S(1)} %collective-permute-done.1.refs_4_.refs_7_), channel_id=1, source_target_pairs={{4,0},{5,1},{6,2},{7,3},{8,12},{9,13},{10,14},{11,15},{20,16},{21,... | collective-permute-start | bytes 3145736 | tf_op jit(solution)/shard_map/ppermute | solution.py:182
  30.0 27.4 %collective-permute-start.7 = (bf16[8,1,256,256]{3,2,1,0:T(8,128)(2,1)S(1)}, bf16[8,1,256,256]{3,2,1,0:T(8,128)(2,1)S(1)}, u32[]{:S(2)}, u32[]{:S(2)}) collective-permute-start(bf16[8,1,256,256]{3,2,1,0:T(8,128)(2,1)S(1)} %collective-permute-done.refs_11_), channel_id=1, source_target_pairs={{4,8},{5,9},{6,10},{7,11},{8,4},{9,5},{10,6},{11,7},{20,24},{21,25... | collective-permute-start | bytes 3145736 | tf_op jit(solution)/shard_map/ppermute | solution.py:182
  49.5 17.4 %collective-permute-start.5 = (bf16[5,1,256,256]{3,2,1,0:T(8,128)(2,1)S(1)}, bf16[5,1,256,256]{3,2,1,0:T(8,128)(2,1)S(1)}, u32[]{:S(2)}, u32[]{:S(2)}) collective-permute-start(bf16[5,1,256,256]{3,2,1,0:T(8,128)(2,1)S(1)} %get-tuple-element.30), channel_id=1, source_target_pairs={{0,2},{1,3},{2,0},{3,1},{4,6},{5,7},{6,4},{7,5},{8,10},{9,11},{10,... | collective-permute-start | bytes 1966088 | tf_op jit(solution)/shard_map/ppermute | solution.py:182
  51.3 28.3 %collective-permute-start.13 = (bf16[1,10,256,256]{3,2,1,0:T(8,128)(2,1)S(1)}, bf16[1,10,256,256]{3,2,1,0:T(8,128)(2,1)S(1)}, u32[]{:S(2)}, u32[]{:S(2)}) collective-permute-start(bf16[1,10,256,256]{3,2,1,0:T(8,128)(2,1)S(1)} %get-tuple-element.40), channel_id=1, source_target_pairs={{0,1},{1,0},{2,3},{3,2},{4,5},{5,4},{6,7},{7,6},{8,9},{9,8},{10,11... | collective-permute-start | bytes 3932168 | tf_op jit(solution)/shard_map/ppermute | solution.py:182
  53.3 13.0 %collective-permute-start.8 = (bf16[2,256,256]{2,1,0:T(8,128)(2,1)S(1)}, bf16[2,256,256]{2,1,0:T(8,128)(2,1)S(1)}, u32[]{:S(2)}, u32[]{:S(2)}) collective-permute-start(bf16[2,256,256]{2,1,0:T(8,128)(2,1)S(1)} %get-tuple-element.35), channel_id=1, source_target_pairs={{4,8},{5,9},{6,10},{7,11},{8,4},{9,5},{10,6},{11,7},{20,24},{21,25... | collective-permute-start | bytes 786440 | tf_op jit(solution)/shard_map/ppermute | solution.py:182
  57.4 34.0 %collective-permute-start.17 = (bf16[8,1,256,256]{3,2,1,0:T(8,128)(2,1)S(1)}, bf16[8,1,256,256]{3,2,1,0:T(8,128)(2,1)S(1)}, u32[]{:S(2)}, u32[]{:S(2)}) collective-permute-start(bf16[8,1,256,256]{3,2,1,0:T(8,128)(2,1)S(1)} %collective-permute-done.7.refs_5_.refs_8_), channel_id=1, source_target_pairs={{4,0},{5,1},{6,2},{7,3},{8,12},{9,13},{10,14},{11,15},{20,16},{21,... | collective-permute-start | bytes 3145736 | tf_op jit(solution)/shard_map/ppermute | solution.py:182
  60.6 16.9 %collective-permute-start.10 = (bf16[2,256,256]{2,1,0:T(8,128)(2,1)S(1)}, bf16[2,256,256]{2,1,0:T(8,128)(2,1)S(1)}, u32[]{:S(2)}, u32[]{:S(2)}) collective-permute-start(bf16[2,256,256]{2,1,0:T(8,128)(2,1)S(1)} %shard_map.48), channel_id=1, source_target_pairs={{0,8},{1,9},{2,10},{3,11},{4,12},{5,13},{6,14},{7,15},{8,0},{9,1},... | collective-permute-start | bytes 786440 | tf_op jit(solution)/shard_map/ppermute | solution.py:182
  66.3 11.2 %collective-permute-start.9 = (bf16[3,1,256,256]{3,2,1,0:T(8,128)(2,1)S(1)}, bf16[3,1,256,256]{3,2,1,0:T(8,128)(2,1)S(1)}, u32[]{:S(2)}, u32[]{:S(2)}) collective-permute-start(bf16[3,1,256,256]{3,2,1,0:T(8,128)(2,1)S(1)} %get-tuple-element.37), channel_id=1, source_target_pairs={{0,2},{1,3},{2,0},{3,1},{4,6},{5,7},{6,4},{7,5},{8,10},{9,11},{10,... | collective-permute-start | bytes 1179656 | tf_op jit(solution)/shard_map/ppermute | solution.py:182
  66.9 18.8 %copy-start.1 = (bf16[1,16,256,256]{3,2,1,0:T(8,128)(2,1)S(1)}, bf16[1,16,256,256]{3,2,1,0:T(8,128)(2,1)}, u32[]{:S(2)}) copy-start(bf16[1,16,256,256]{3,2,1,0:T(8,128)(2,1)} %refs_6_.1) | copy-start | bytes 6291460
  66.9 11.1 %collective-permute-start.14 = (bf16[1,6,256,256]{3,2,1,0:T(8,128)(2,1)S(1)}, bf16[1,6,256,256]{3,2,1,0:T(8,128)(2,1)S(1)}, u32[]{:S(2)}, u32[]{:S(2)}) collective-permute-start(bf16[1,6,256,256]{3,2,1,0:T(8,128)(2,1)S(1)} %get-tuple-element.41), channel_id=1, source_target_pairs={{0,1},{1,0},{2,3},{3,2},{4,5},{5,4},{6,7},{7,6},{8,9},{9,8},{10,11... | collective-permute-start | bytes 2359304 | tf_op jit(solution)/shard_map/ppermute | solution.py:182
  77.5 2.1 %collective-permute-start.11 = (bf16[5,1,256,256]{3,2,1,0:T(8,128)(2,1)S(1)}, bf16[5,1,256,256]{3,2,1,0:T(8,128)(2,1)S(1)}, u32[]{:S(2)}, u32[]{:S(2)}) collective-permute-start(bf16[5,1,256,256]{3,2,1,0:T(8,128)(2,1)S(1)} %collective-permute-done.5.refs_0_.refs_2_), channel_id=1, source_target_pairs={{0,1},{1,0},{2,3},{3,2},{4,5},{5,4},{6,7},{7,6},{8,9},{9,8},{10,11... | collective-permute-start | bytes 1966088 | tf_op jit(solution)/shard_map/ppermute | solution.py:182
  77.5 2.7 %collective-permute-start.12 = (bf16[3,1,256,256]{3,2,1,0:T(8,128)(2,1)S(1)}, bf16[3,1,256,256]{3,2,1,0:T(8,128)(2,1)S(1)}, u32[]{:S(2)}, u32[]{:S(2)}) collective-permute-start(bf16[3,1,256,256]{3,2,1,0:T(8,128)(2,1)S(1)} %collective-permute-done.9.refs_1_.refs_3_), channel_id=1, source_target_pairs={{0,1},{1,0},{2,3},{3,2},{4,5},{5,4},{6,7},{7,6},{8,9},{9,8},{10,11... | collective-permute-start | bytes 1179656 | tf_op jit(solution)/shard_map/ppermute | solution.py:182
  82.1 16.4 %collective-permute-start.15 = (bf16[2,256,256]{2,1,0:T(8,128)(2,1)S(1)}, bf16[2,256,256]{2,1,0:T(8,128)(2,1)S(1)}, u32[]{:S(2)}, u32[]{:S(2)}) collective-permute-start(bf16[2,256,256]{2,1,0:T(8,128)(2,1)S(1)} %shard_map.51), channel_id=1, source_target_pairs={{0,8},{1,9},{2,10},{3,11},{4,12},{5,13},{6,14},{7,15},{8,0},{9,1},... | collective-permute-start | bytes 786440 | tf_op jit(solution)/shard_map/ppermute | solution.py:182
  88.7 29.3 %collective-permute-start.16 = (bf16[4,256,256]{2,1,0:T(8,128)(2,1)S(1)}, bf16[4,256,256]{2,1,0:T(8,128)(2,1)S(1)}, u32[]{:S(2)}, u32[]{:S(2)}) collective-permute-start(bf16[4,256,256]{2,1,0:T(8,128)(2,1)S(1)} %shard_map.52), channel_id=1, source_target_pairs={{0,4},{1,5},{2,6},{3,7},{4,0},{5,1},{6,2},{7,3},{8,12},{9,13},{10,... | collective-permute-start | bytes 1572872 | tf_op jit(solution)/shard_map/ppermute | solution.py:182
  90.6 30.5 %collective-permute-start.19 = (bf16[2,256,256]{2,1,0:T(8,128)(2,1)S(1)}, bf16[2,256,256]{2,1,0:T(8,128)(2,1)S(1)}, u32[]{:S(2)}, u32[]{:S(2)}) collective-permute-start(bf16[2,256,256]{2,1,0:T(8,128)(2,1)S(1)} %get-tuple-element.48), channel_id=1, source_target_pairs={{4,8},{5,9},{6,10},{7,11},{8,4},{9,5},{10,6},{11,7},{20,24},{21,25... | collective-permute-start | bytes 786440 | tf_op jit(solution)/shard_map/ppermute | solution.py:182
  91.4 26.6 %copy-start.4 = (bf16[8,1,256,256]{3,2,1,0:T(8,128)(2,1)S(1)}, bf16[8,1,256,256]{3,2,1,0:T(8,128)(2,1)}, u32[]{:S(2)}) copy-start(bf16[8,1,256,256]{3,2,1,0:T(8,128)(2,1)} %refs_7_) | copy-start | bytes 3145732
  92.6 28.5 %collective-permute-start.18 = (bf16[4,256,256]{2,1,0:T(8,128)(2,1)S(1)}, bf16[4,256,256]{2,1,0:T(8,128)(2,1)S(1)}, u32[]{:S(2)}, u32[]{:S(2)}) collective-permute-start(bf16[4,256,256]{2,1,0:T(8,128)(2,1)S(1)} %shard_map.56), channel_id=1, source_target_pairs={{0,12},{1,13},{2,14},{3,15},{12,0},{13,1},{14,2},{15,3},{16,28},{1... | collective-permute-start | bytes 1572872 | tf_op jit(solution)/shard_map/ppermute | solution.py:182

commit v13 on v12

--- a/solution.py
+++ b/solution.py
@@ -129,53 +129,54 @@
     )(array)
 
 
-def place_kernel(first, choices, *refs):
+def place_kernel(starts, chosen, *refs):
     *pieces, out, sem = refs
+    pieces = pieces[-len(starts) :]
     me = lax.axis_index("sec")
     row = me >> 2
     outer = (row == 0) | (row == 3)
 
-    def copies(pieces):
-        blocks = [piece.at[i] for piece in pieces for i in range(piece.shape[0])]
+    def copies(chosen_pieces):
         return [
-            pltpu.make_async_copy(block, out.at[me ^ j], sem.at[j - first]) for j, block in enumerate(blocks, first)
+            pltpu.make_async_copy(piece.at[i], out.at[me ^ (start + i)], sem.at[start + i])
+            for start, piece in chosen_pieces
+            for i in range(piece.shape[0])
         ]
 
-    if choices == 1:
-        for copy in copies(pieces):
-            copy.start()
-    else:
-        pieces = pieces[1:]
+    held = list(zip(starts, pieces))
+    if chosen:
 
         @pl.when(outer)
         def _():
-            for copy in copies(pieces[:1]):
+            for copy in copies(held[:1]):
                 copy.start()
 
         @pl.when(jnp.logical_not(outer))
         def _():
-            for copy in copies(pieces[1:]):
+            for copy in copies(held[1:]):
                 copy.start()
 
-        pieces = pieces[:1]
-
-    for copy in copies(pieces):
+        held = held[:1]
+    else:
+        for copy in copies(held):
+            copy.start()
+    for copy in copies(held):
         copy.wait()
 
 
-def place(first, sectors, pieces, out=None):
-    blocks = sum(piece.shape[0] for piece in (pieces if out is None else pieces[:1]))
-    held = [] if out is None else [out]
-    return pl.pallas_call(
-        functools.partial(place_kernel, first, 1 if out is None else 2),
+def place(sectors, held, out=None, flops=1):
+    starts, pieces = zip(*held)
+    before = [] if out is None else [out]
+    return pl.pallas_call(
+        functools.partial(place_kernel, starts, out is not None),
         out_shape=jax.ShapeDtypeStruct((sectors,) + pieces[0].shape[1:], pieces[0].dtype),
-        in_specs=[HBM] * len(held) + [VMEM] * len(pieces),
+        in_specs=[HBM] * len(before) + [VMEM] * len(pieces),
         out_specs=HBM,
-        scratch_shapes=[pltpu.SemaphoreType.DMA((blocks,))],
+        scratch_shapes=[pltpu.SemaphoreType.DMA((sectors,))],
         input_output_aliases={} if out is None else {0: 0},
         compiler_params=pltpu.CompilerParams(vmem_limit_bytes=16 << 20),
-        cost_estimate=pl.CostEstimate(flops=1, bytes_accessed=1, transcendentals=0),
-    )(*held, *pieces)
+        cost_estimate=pl.CostEstimate(flops=flops, bytes_accessed=1, transcendentals=0),
+    )(*before, *pieces)
 
 
 def exchange(array, bits, members):
@@ -187,7 +188,6 @@
     every = range(16)
     inner = range(4, 12)
     outer = [s for s in every if s not in inner]
-    low, high = split(left_env, 0, 5 * left_env.shape[0] // 8)
 
     def products(step, lefts, psis, rights, flops=1, keep_mid=False):
         return slot(step, source_map, lefts, psis, rights, dtype, flops, keep_mid)
@@ -202,38 +202,40 @@
     far_in = exchange(near, 12, inner)
     far_out = exchange(middle, 4, inner)
 
-    x_psi, low = lax.optimization_barrier((x_psi, low))
-    x_low = exchange(low, 2, every)
-    across_psi = [exchange(part, 1, every) for part in split(x_psi, 1, 5 * x_psi.shape[1] // 8)]
+    x_psi, left_next = lax.optimization_barrier((x_psi, left_env))
+    x_left = exchange(left_next, 2, every)
+    across_psi = [exchange(part, 1, every) for part in split(x_psi, 1, 6 * x_psi.shape[1] // 8)]
+    own_1 = products(1, *own, (near,))
+    sent_1 = exchange(own_1, 4, every)
 
     far_out, far_in = lax.optimization_barrier((far_out, far_in))
     third = exchange(far_in, 4, inner)
+    far_out, sent_1 = lax.optimization_barrier((far_out, sent_1))
+    own_2 = products(2, *own, (far_out, far_in))
+    sent_2 = exchange(own_2, 8, every)
     own_middle, own_mid = products(3, *own, (middle,), keep_mid=True)
     sent_own_middle = exchange(own_middle, 12, inner)
-    own_2 = products(2, *own, (far_out, far_in))
-    sent_2 = exchange(own_2, 8, every)
-
-    own_2, sent_own_middle, high = lax.optimization_barrier((own_2, sent_own_middle, high))
-    x_high = exchange(high, 2, every)
-    across_low = exchange(x_low, 1, every)
-    x_high, sent_2 = lax.optimization_barrier((x_high, sent_2))
-    across_high = exchange(x_high, 1, every)
-    other = ([(x_low, x_high), (across_low, across_high)], [(x_psi,), across_psi])
+
+    x_left, sent_2, sent_own_middle = lax.optimization_barrier((x_left, sent_2, sent_own_middle))
+    across_left = [exchange(part, 1, every) for part in split(x_left, 0, 5 * x_left.shape[0] // 8)]
+    other = ([(x_left,), across_left], [(x_psi,), across_psi])
     other_2 = products(2, *other, (far_out, far_in))
     other_sent_2 = exchange(other_2, 8, every)
     other_middle, other_mid = products(3, *other, (middle,), keep_mid=True)
     sent_other_middle = exchange(other_middle, 12, inner)
-    both_1 = products(1, own[0] + other[0], own[1] + other[1], (near,))
-    sent_1 = exchange(both_1, 4, every)
-
-    third, both_1, other_2, other_middle = lax.optimization_barrier((third, both_1, other_2, other_middle))
+    other_1 = products(1, *other, (near,))
+    other_sent_1 = exchange(other_1, 4, every)
+
+    third, other_1, other_middle, other_2 = lax.optimization_barrier((third, other_1, other_middle, other_2))
     last_third = second((own_mid, other_mid), third, dtype, 10**10)
     sent_third = exchange(last_third, 12, outer)
-    right_last, other_sent_2, sent_1 = lax.optimization_barrier((right_env, other_sent_2, sent_1))
-    other_0 = products(0, *other, (right_last,), flops=10**10)
-
-    out = place(0, 16, [own_0, other_0, sent_1, sent_2, other_sent_2])
-    out = place(12, 16, [sent_third, sent_own_middle, sent_other_middle], out)[:, None]
+    right_last, last_third = lax.optimization_barrier((right_env, last_third))
+    other_0 = products(0, *other, (right_last,))
+
+    other_sent_2, other_sent_1 = lax.optimization_barrier((other_sent_2, other_sent_1))
+    held = [(0, own_0), (2, other_0), (8, sent_2), (10, other_sent_2), (4, sent_1), (6, other_sent_1)]
+    out = place(16, held, flops=10**10)
+    out = place(16, [(12, sent_third), (12, sent_own_middle), (14, sent_other_middle)], out)[:, None]
     if ops > 1:
         out = lax.psum_scatter(out, "op", scatter_dimension=2, tiled=True).astype(jnp.bfloat16)
     return out

time: 122 us -> 119 us (0.975)
  starting transfers between devices: 27.6 us -> 24.5 us
    ppermute x20, starting transfers between devices: 27.6 us -> 24.5 us  [exchange(): return lax.ppermute(array, 'sec', [(s, s ^ bits) for s in members])]
    pallas_call x7 -> x8, Pallas kernels: 14.3 us -> 15.1 us  [slot(): pl.pallas_call(functools.partial(slot_kernel, step, parts, len(rights)),...]
    unnamed x12 -> x10, local copies, waits for them, and re-layouts: 4.73 us -> 4.73 us
  transfers between devices with their start and end apart: 20 -> 20, of which waited for: 9 -> 11; matrix products, arithmetic and copies ran while one was open for 0% -> 0% of each run, Pallas kernels for 14% -> 15%
where the time goes in v13:
time: 119 us
  waiting for transfers between devices  70.9 us (60%)
  starting transfers between devices  24.5 us (21%)
  Pallas kernels  18.8 us (16%)
  local copies, waits for them, and re-layouts  4.73 us (4%)
    ppermute x20, waiting for transfers between devices, exchange(): return lax.ppermute(array, 'sec', [(s, s ^ bits) for s in members])  70.9 us
    ppermute x20, starting transfers between devices, exchange(): return lax.ppermute(array, 'sec', [(s, s ^ bits) for s in members])  24.5 us
    pallas_call x8, Pallas kernels, slot(): pl.pallas_call(functools.partial(slot_kernel, step, parts, len(rights)),...  15.1 us
    unnamed x10, local copies, waits for them, and re-layouts  4.73 us
  transfers between devices with their start and end apart: 20, of which 11 were waited for; matrix products, arithmetic and copies ran while one was open for 0% of the time, Pallas kernels for 15%

profile of v13, /device:TPU:0, one launch (start us, length us, event | category | flops | bytes accessed | tf_op | source)
XLA Modules:
  0.0 119.1 jit_solution(16818102785020901990)
XLA Ops:
  0.0 0.5 collective-permute-start.3
  0.5 2.5 %collective-permute-start.4 = (bf16[1,16,256,256]{3,2,1,0:T(8,128)(2,1)}, bf16[1,16,256,256]{3,2,1,0:T(8,128)(2,1)S(1)}, u32[]{:S(2)}, u32[]{:S(2)}) collective-permute-start(bf16[1,16,256,256]{3,2,1,0:T(8,128)(2,1)} %refs_2_.7), channel_id=1, source_target_pairs={{0,2},{1,3},{2,0},{3,1},{4,6},{5,7},{6,4},{7,5},{8,10},{9,11},{10,... | collective-permute-start | bytes 6291464 | tf_op jit(solution)/shard_map/ppermute | solution.py:183
  2.9 0.2 collective-permute-start.2
  3.2 1.6 %collective-permute-start = (bf16[8,1,256,256]{3,2,1,0:T(8,128)(2,1)}, bf16[8,1,256,256]{3,2,1,0:T(8,128)(2,1)S(1)}, u32[]{:S(2)}, u32[]{:S(2)}) collective-permute-start(bf16[8,1,256,256]{3,2,1,0:T(8,128)(2,1)} %refs_6_), channel_id=1, source_target_pairs={{0,4},{1,5},{2,6},{3,7},{4,0},{5,1},{6,2},{7,3},{8,12},{9,13},{10,... | collective-permute-start | bytes 3145736 | tf_op jit(solution)/shard_map/ppermute | solution.py:183
  4.7 0.7 collective-permute-start.1
  5.5 0.5 collective-permute-done.2.refs_1_
  6.0 1.6 %copy-done = bf16[1,16,256,256]{3,2,1,0:T(8,128)(2,1)S(1)} copy-done((bf16[1,16,256,256]{3,2,1,0:T(8,128)(2,1)S(1)}, bf16[1,16,256,256]{3,2,1,0:T(8,128)(2,1)}, u32[]{:S(2)}) %copy-start) | copy-done | bytes 2097176
  7.5 1.2 %copy-done.1 = bf16[8,1,256,256]{3,2,1,0:T(8,128)(2,1)S(1)} copy-done((bf16[8,1,256,256]{3,2,1,0:T(8,128)(2,1)S(1)}, bf16[8,1,256,256]{3,2,1,0:T(8,128)(2,1)}, u32[]{:S(2)}) %copy-start.1) | copy-done | bytes 1048600
  8.8 1.2 %copy-done.2 = bf16[8,1,256,256]{3,2,1,0:T(8,128)(2,1)S(1)} copy-done((bf16[8,1,256,256]{3,2,1,0:T(8,128)(2,1)S(1)}, bf16[8,1,256,256]{3,2,1,0:T(8,128)(2,1)}, u32[]{:S(2)}) %copy-start.2) | copy-done | bytes 1048600
  10.0 0.7 copy-done.4
  10.7 1.9 %shard_map.46.refs_0_ = bf16[2,256,256]{2,1,0:T(8,128)(2,1)S(1)} custom-call(s32[8,16]{1,0:T(8,128)S(1)} %copy-done.4, bf16[8,1,256,256]{3,2,1,0:T(8,128)(2,1)S(1)} %copy-done.1, bf16[8,1,256,256]{3,2,1,0:T(8,128)(2,1)S(1)} %collective-permute-done.2.refs_1_, bf16[1,16,256,256]{3,2,1,0:T(8,128)(2,1)S(1)} %copy-done, ...), custom_call_target="tpu_custom_call" | custom-call | flops 1 | bytes 1 | tf_op jit(solution)/shard_map/pallas_call | solution.py:99
  12.6 16.2 %collective-permute-done.refs_4_.refs_6_ = bf16[8,1,256,256]{3,2,1,0:T(8,128)(2,1)S(1)} collective-permute-done((bf16[8,1,256,256]{3,2,1,0:T(8,128)(2,1)}, bf16[8,1,256,256]{3,2,1,0:T(8,128)(2,1)S(1)}, u32[]{:S(2)}, u32[]{:S(2)}) %collective-permute-start) | collective-permute-done | bytes 1048608 | tf_op jit(solution)/shard_map/ppermute | solution.py:183
  28.7 1.3 %collective-permute-start.6 = (bf16[8,1,256,256]{3,2,1,0:T(8,128)(2,1)S(1)}, bf16[8,1,256,256]{3,2,1,0:T(8,128)(2,1)S(1)}, u32[]{:S(2)}, u32[]{:S(2)}) collective-permute-start(bf16[8,1,256,256]{3,2,1,0:T(8,128)(2,1)S(1)} %collective-permute-done.1.refs_4_.refs_6_), channel_id=1, source_target_pairs={{4,0},{5,1},{6,2},{7,3},{8,12},{9,13},{10,14},{11,15},{20,16},{21,... | collective-permute-start | bytes 3145736 | tf_op jit(solution)/shard_map/ppermute | solution.py:183
  30.0 0.7 collective-permute-start.7
  30.8 18.7 %collective-permute-done.4.whole.refs_3_ = bf16[1,16,256,256]{3,2,1,0:T(8,128)(2,1)S(1)} collective-permute-done((bf16[1,16,256,256]{3,2,1,0:T(8,128)(2,1)}, bf16[1,16,256,256]{3,2,1,0:T(8,128)(2,1)S(1)}, u32[]{:S(2)}, u32[]{:S(2)}) %collective-permute-start.4) | collective-permute-done | bytes 2097184 | tf_op jit(solution)/shard_map/ppermute | solution.py:183
  49.5 1.7 %collective-permute-start.5 = (bf16[8,1,256,256]{3,2,1,0:T(8,128)(2,1)S(1)}, bf16[8,1,256,256]{3,2,1,0:T(8,128)(2,1)S(1)}, u32[]{:S(2)}, u32[]{:S(2)}) collective-permute-start(bf16[8,1,256,256]{3,2,1,0:T(8,128)(2,1)S(1)} %copy-done.1), channel_id=1, source_target_pairs={{0,2},{1,3},{2,0},{3,1},{4,6},{5,7},{6,4},{7,5},{8,10},{9,11},{10,... | collective-permute-start | bytes 3145736 | tf_op jit(solution)/shard_map/ppermute | solution.py:183
  51.2 0.1 shard_map.51
  51.3 0.1 collective-permute-start.13
  51.4 1.9 %shard_map.47 = bf16[2,256,256]{2,1,0:T(8,128)(2,1)S(1)} custom-call(s32[8,16]{1,0:T(8,128)S(1)} %copy-done.4, bf16[8,1,256,256]{3,2,1,0:T(8,128)(2,1)S(1)} %copy-done.1, bf16[8,1,256,256]{3,2,1,0:T(8,128)(2,1)S(1)} %collective-permute-done.2.refs_1_, bf16[1,16,256,256]{3,2,1,0:T(8,128)(2,1)S(1)} %copy-done, ...), custom_call_target="tpu_custom_call" | custom-call | flops 1 | bytes 1 | tf_op jit(solution)/shard_map/pallas_call | solution.py:99
  53.3 1.6 %collective-permute-start.8 = (bf16[2,256,256]{2,1,0:T(8,128)(2,1)S(1)}, bf16[2,256,256]{2,1,0:T(8,128)(2,1)S(1)}, u32[]{:S(2)}, u32[]{:S(2)}) collective-permute-start(bf16[2,256,256]{2,1,0:T(8,128)(2,1)S(1)} %shard_map.47), channel_id=1, source_target_pairs={{0,4},{1,5},{2,6},{3,7},{4,0},{5,1},{6,2},{7,3},{8,12},{9,13},{10,... | collective-permute-start | bytes 786440 | tf_op jit(solution)/shard_map/ppermute | solution.py:183
  54.9 3.3 %collective-permute-done.6.refs_4_.refs_6_ = bf16[8,1,256,256]{3,2,1,0:T(8,128)(2,1)S(1)} collective-permute-done((bf16[8,1,256,256]{3,2,1,0:T(8,128)(2,1)S(1)}, bf16[8,1,256,256]{3,2,1,0:T(8,128)(2,1)S(1)}, u32[]{:S(2)}, u32[]{:S(2)}) %collective-permute-start.6) | collective-permute-done | bytes 1048608 | tf_op jit(solution)/shard_map/ppermute | solution.py:183
  58.2 1.3 %collective-permute-start.15 = (bf16[8,1,256,256]{3,2,1,0:T(8,128)(2,1)S(1)}, bf16[8,1,256,256]{3,2,1,0:T(8,128)(2,1)S(1)}, u32[]{:S(2)}, u32[]{:S(2)}) collective-permute-start(bf16[8,1,256,256]{3,2,1,0:T(8,128)(2,1)S(1)} %collective-permute-done.7.refs_5_.refs_7_), channel_id=1, source_target_pairs={{4,0},{5,1},{6,2},{7,3},{8,12},{9,13},{10,14},{11,15},{20,16},{21,... | collective-permute-start | bytes 3145736 | tf_op jit(solution)/shard_map/ppermute | solution.py:183
  59.5 1.9 %shard_map.49 = (bf16[2,256,256]{2,1,0:T(8,128)(2,1)S(1)}, bf16[512,2048]{1,0:T(8,128)(2,1)S(1)}) custom-call(s32[8,16]{1,0:T(8,128)S(1)} %copy-done.4, bf16[8,1,256,256]{3,2,1,0:T(8,128)(2,1)S(1)} %copy-done.1, bf16[8,1,256,256]{3,2,1,0:T(8,128)(2,1)S(1)} %collective-permute-done.2.refs_1_, bf16[1,16,256,256]{3,2,1,0:T(8,128)(2,1)S(1)} %copy-done, ...), custom_call_target="tpu_custom_call" | custom-call | flops 1 | bytes 1 | tf_op jit(solution)/shard_map/pallas_call | solution.py:99
  61.4 0.7 collective-permute-start.10
  62.1 1.8 %collective-permute-done.8.refs_4_ = bf16[2,256,256]{2,1,0:T(8,128)(2,1)S(1)} collective-permute-done((bf16[2,256,256]{2,1,0:T(8,128)(2,1)S(1)}, bf16[2,256,256]{2,1,0:T(8,128)(2,1)S(1)}, u32[]{:S(2)}, u32[]{:S(2)}) %collective-permute-start.8) | collective-permute-done | bytes 262176 | tf_op jit(solution)/shard_map/ppermute | solution.py:183
  63.9 1.9 %shard_map.48 = bf16[2,256,256]{2,1,0:T(8,128)(2,1)S(1)} custom-call(s32[8,16]{1,0:T(8,128)S(1)} %copy-done.4, bf16[8,1,256,256]{3,2,1,0:T(8,128)(2,1)S(1)} %copy-done.1, bf16[8,1,256,256]{3,2,1,0:T(8,128)(2,1)S(1)} %collective-permute-done.2.refs_1_, bf16[1,16,256,256]{3,2,1,0:T(8,128)(2,1)S(1)} %copy-done, ...), custom_call_target="tpu_custom_call" | custom-call | flops 1 | bytes 1 | tf_op jit(solution)/shard_map/pallas_call | solution.py:99
  65.8 3.9 %collective-permute-start.9 = (bf16[2,256,256]{2,1,0:T(8,128)(2,1)S(1)}, bf16[2,256,256]{2,1,0:T(8,128)(2,1)S(1)}, u32[]{:S(2)}, u32[]{:S(2)}) collective-permute-start(bf16[2,256,256]{2,1,0:T(8,128)(2,1)S(1)} %shard_map.48), channel_id=1, source_target_pairs={{0,8},{1,9},{2,10},{3,11},{4,12},{5,13},{6,14},{7,15},{8,0},{9,1},... | collective-permute-start | bytes 786440 | tf_op jit(solution)/shard_map/ppermute | solution.py:183
  69.7 4.7 %collective-permute-done.5.whole.refs_0_ = bf16[8,1,256,256]{3,2,1,0:T(8,128)(2,1)S(1)} collective-permute-done((bf16[8,1,256,256]{3,2,1,0:T(8,128)(2,1)S(1)}, bf16[8,1,256,256]{3,2,1,0:T(8,128)(2,1)S(1)}, u32[]{:S(2)}, u32[]{:S(2)}) %collective-permute-start.5) | collective-permute-done | bytes 1048608 | tf_op jit(solution)/shard_map/ppermute | solution.py:183
  74.4 9.3 %collective-permute-done.9.refs_2_ = bf16[2,256,256]{2,1,0:T(8,128)(2,1)S(1)} collective-permute-done((bf16[2,256,256]{2,1,0:T(8,128)(2,1)S(1)}, bf16[2,256,256]{2,1,0:T(8,128)(2,1)S(1)}, u32[]{:S(2)}, u32[]{:S(2)}) %collective-permute-start.9) | collective-permute-done | bytes 262176 | tf_op jit(solution)/shard_map/ppermute | solution.py:183
  83.8 0.1 shard_map.50
  83.8 0.1 collective-permute-start.11
  83.9 0.5 collective-permute-start.14
  84.4 0.1 collective-permute-start.12
  84.5 2.3 %collective-permute-done.14.refs_5_ = bf16[1,4,256,256]{3,2,1,0:T(8,128)(2,1)S(1)} collective-permute-done((bf16[1,4,256,256]{3,2,1,0:T(8,128)(2,1)S(1)}, bf16[1,4,256,256]{3,2,1,0:T(8,128)(2,1)S(1)}, u32[]{:S(2)}, u32[]{:S(2)}) %collective-permute-start.14) | collective-permute-done | bytes 524320 | tf_op jit(solution)/shard_map/ppermute | solution.py:183
  86.8 0.6 collective-permute-done.12.refs_2_
  87.3 1.9 %shard_map.54 = bf16[2,256,256]{2,1,0:T(8,128)(2,1)S(1)} custom-call(s32[8,16]{1,0:T(8,128)S(1)} %copy-done.4, bf16[8,1,256,256]{3,2,1,0:T(8,128)(2,1)S(1)} %collective-permute-done.5.whole.refs_0_, bf16[5,1,256,256]{3,2,1,0:T(8,128)(2,1)S(1)} %collective-permute-done.11.refs_1_, bf16[3,1,256,256]{3,2,1,0:T(8,128)(2,1)S(1)} %collective-permute-done.12.refs_2_, ...), custom_call_target="tpu_custom_call" | custom-call | flops 1 | bytes 1 | tf_op jit(solution)/shard_map/pallas_call | solution.py:99
  89.2 0.1 collective-permute-start.16
  89.3 1.9 %shard_map.53 = bf16[2,256,256]{2,1,0:T(8,128)(2,1)S(1)} custom-call(s32[8,16]{1,0:T(8,128)S(1)} %copy-done.4, bf16[8,1,256,256]{3,2,1,0:T(8,128)(2,1)S(1)} %collective-permute-done.5.whole.refs_0_, bf16[5,1,256,256]{3,2,1,0:T(8,128)(2,1)S(1)} %collective-permute-done.11.refs_1_, bf16[3,1,256,256]{3,2,1,0:T(8,128)(2,1)S(1)} %collective-permute-done.12.refs_2_, ...), custom_call_target="tpu_custom_call" | custom-call | flops 1 | bytes 1 | tf_op jit(solution)/shard_map/pallas_call | solution.py:99
  91.2 2.6 %collective-permute-start.17 = (bf16[2,256,256]{2,1,0:T(8,128)(2,1)S(1)}, bf16[2,256,256]{2,1,0:T(8,128)(2,1)S(1)}, u32[]{:S(2)}, u32[]{:S(2)}) collective-permute-start(bf16[2,256,256]{2,1,0:T(8,128)(2,1)S(1)} %shard_map.53), channel_id=1, source_target_pairs={{0,4},{1,5},{2,6},{3,7},{4,0},{5,1},{6,2},{7,3},{8,12},{9,13},{10,... | collective-permute-start | bytes 786440 | tf_op jit(solution)/shard_map/ppermute | solution.py:183
  93.8 1.9 %shard_map.52 = (bf16[2,256,256]{2,1,0:T(8,128)(2,1)S(1)}, bf16[512,2048]{1,0:T(8,128)(2,1)S(1)}) custom-call(s32[8,16]{1,0:T(8,128)S(1)} %copy-done.4, bf16[8,1,256,256]{3,2,1,0:T(8,128)(2,1)S(1)} %collective-permute-done.5.whole.refs_0_, bf16[5,1,256,256]{3,2,1,0:T(8,128)(2,1)S(1)} %collective-permute-done.11.refs_1_, ...), custom_call_target="tpu_custom_call" | custom-call | flops 1 | bytes 1 | tf_op jit(solution)/shard_map/pallas_call | solution.py:99
  95.7 0.7 collective-permute-start.19
  96.4 1.3 %shard_map.55 = bf16[4,256,256]{2,1,0:T(8,128)(2,1)S(1)} custom-call(bf16[512,2048]{1,0:T(8,128)(2,1)S(1)} %get-tuple-element.43.refs_0_, bf16[512,2048]{1,0:T(8,128)(2,1)S(1)} %get-tuple-element.44.refs_1_, bf16[8,1,256,256]{3,2,1,0:T(8,128)(2,1)S(1)} %collective-permute-done.15.refs_2_), custom_call_target="tpu_custom_call" | custom-call | flops 10000000000 | bytes 1 | tf_op jit(solution)/shard_map/pallas_call | solution.py:78
  97.7 3.7 %collective-permute-start.18 = (bf16[4,256,256]{2,1,0:T(8,128)(2,1)S(1)}, bf16[4,256,256]{2,1,0:T(8,128)(2,1)S(1)}, u32[]{:S(2)}, u32[]{:S(2)}) collective-permute-start(bf16[4,256,256]{2,1,0:T(8,128)(2,1)S(1)} %shard_map.55), channel_id=1, source_target_pairs={{0,12},{1,13},{2,14},{3,15},{12,0},{13,1},{14,2},{15,3},{16,28},{1... | collective-permute-start | bytes 1572872 | tf_op jit(solution)/shard_map/ppermute | solution.py:183
  101.4 1.9 %shard_map.56.refs_1_ = bf16[2,256,256]{2,1,0:T(8,128)(2,1)S(1)} custom-call(s32[8,16]{1,0:T(8,128)S(1)} %copy-done.4, bf16[8,1,256,256]{3,2,1,0:T(8,128)(2,1)S(1)} %collective-permute-done.5.whole.refs_0_, bf16[5,1,256,256]{3,2,1,0:T(8,128)(2,1)S(1)} %collective-permute-done.11.refs_1_, bf16[3,1,256,256]{3,2,1,0:T(8,128)(2,1)S(1)} %collective-permute-done.12.refs_2_, ...), custom_call_target="tpu_custom_call" | custom-call | flops 1 | bytes 1 | tf_op jit(solution)/shard_map/pallas_call | solution.py:99
  103.3 0.3 collective-permute-done.16.refs_3_
  103.7 13.2 %collective-permute-done.17.refs_5_ = bf16[2,256,256]{2,1,0:T(8,128)(2,1)S(1)} collective-permute-done((bf16[2,256,256]{2,1,0:T(8,128)(2,1)S(1)}, bf16[2,256,256]{2,1,0:T(8,128)(2,1)S(1)}, u32[]{:S(2)}, u32[]{:S(2)}) %collective-permute-start.17) | collective-permute-done | bytes 262176 | tf_op jit(solution)/shard_map/ppermute | solution.py:183
  116.9 1.3 %shard_map.57.refs_0_ = bf16[16,256,256]{2,1,0:T(8,128)(2,1)} custom-call(bf16[2,256,256]{2,1,0:T(8,128)(2,1)S(1)} %shard_map.46.refs_0_, bf16[2,256,256]{2,1,0:T(8,128)(2,1)S(1)} %shard_map.56.refs_1_, bf16[2,256,256]{2,1,0:T(8,128)(2,1)S(1)} %collective-permute-done.9.refs_2_, bf16[2,256,256]{2,1,0:T(8,128)(2,1)S(1)} %collective-permute-done.16.refs_3_, ...), custom_call_target="tpu_custom_call" | custom-call | flops 10000000000 | bytes 1 | tf_op jit(solution)/shard_map/pallas_call | solution.py:170
  118.2 0.9 shard_map.58
  (15 shorter events, 0.0 us)
Async XLA Ops:
  0.0 6.0 %collective-permute-start.3 = (bf16[1,16,256,256]{3,2,1,0:T(8,128)(2,1)}, bf16[1,16,256,256]{3,2,1,0:T(8,128)(2,1)S(1)}, u32[]{:S(2)}, u32[]{:S(2)}) collective-permute-start(bf16[1,16,256,256]{3,2,1,0:T(8,128)(2,1)} %refs_2_.7), channel_id=1, source_target_pairs={{0,1},{1,0},{2,3},{3,2},{4,5},{5,4},{6,7},{7,6},{8,9},{9,8},{10,11... | collective-permute-start | bytes 6291464 | tf_op jit(solution)/shard_map/ppermute | solution.py:183
  0.5 49.0 %collective-permute-start.4 = (bf16[1,16,256,256]{3,2,1,0:T(8,128)(2,1)}, bf16[1,16,256,256]{3,2,1,0:T(8,128)(2,1)S(1)}, u32[]{:S(2)}, u32[]{:S(2)}) collective-permute-start(bf16[1,16,256,256]{3,2,1,0:T(8,128)(2,1)} %refs_2_.7), channel_id=1, source_target_pairs={{0,2},{1,3},{2,0},{3,1},{4,6},{5,7},{6,4},{7,5},{8,10},{9,11},{10,... | collective-permute-start | bytes 6291464 | tf_op jit(solution)/shard_map/ppermute | solution.py:183
  2.9 3.0 %collective-permute-start.2 = (bf16[8,1,256,256]{3,2,1,0:T(8,128)(2,1)}, bf16[8,1,256,256]{3,2,1,0:T(8,128)(2,1)S(1)}, u32[]{:S(2)}, u32[]{:S(2)}) collective-permute-start(bf16[8,1,256,256]{3,2,1,0:T(8,128)(2,1)} %refs_0_.7), channel_id=1, source_target_pairs={{0,1},{1,0},{2,3},{3,2},{4,5},{5,4},{6,7},{7,6},{8,9},{9,8},{10,11... | collective-permute-start | bytes 3145736 | tf_op jit(solution)/shard_map/ppermute | solution.py:183
  3.2 25.6 %collective-permute-start = (bf16[8,1,256,256]{3,2,1,0:T(8,128)(2,1)}, bf16[8,1,256,256]{3,2,1,0:T(8,128)(2,1)S(1)}, u32[]{:S(2)}, u32[]{:S(2)}) collective-permute-start(bf16[8,1,256,256]{3,2,1,0:T(8,128)(2,1)} %refs_6_), channel_id=1, source_target_pairs={{0,4},{1,5},{2,6},{3,7},{4,0},{5,1},{6,2},{7,3},{8,12},{9,13},{10,... | collective-permute-start | bytes 3145736 | tf_op jit(solution)/shard_map/ppermute | solution.py:183
  4.7 24.0 %collective-permute-start.1 = (bf16[8,1,256,256]{3,2,1,0:T(8,128)(2,1)}, bf16[8,1,256,256]{3,2,1,0:T(8,128)(2,1)S(1)}, u32[]{:S(2)}, u32[]{:S(2)}) collective-permute-start(bf16[8,1,256,256]{3,2,1,0:T(8,128)(2,1)} %refs_6_), channel_id=1, source_target_pairs={{4,8},{5,9},{6,10},{7,11},{8,4},{9,5},{10,6},{11,7},{20,24},{21,25... | collective-permute-start | bytes 3145736 | tf_op jit(solution)/shard_map/ppermute | solution.py:183
  6.0 1.6 %copy-start = (bf16[1,16,256,256]{3,2,1,0:T(8,128)(2,1)S(1)}, bf16[1,16,256,256]{3,2,1,0:T(8,128)(2,1)}, u32[]{:S(2)}) copy-start(bf16[1,16,256,256]{3,2,1,0:T(8,128)(2,1)} %refs_2_.7) | copy-start | bytes 6291460
  7.5 1.2 %copy-start.1 = (bf16[8,1,256,256]{3,2,1,0:T(8,128)(2,1)S(1)}, bf16[8,1,256,256]{3,2,1,0:T(8,128)(2,1)}, u32[]{:S(2)}) copy-start(bf16[8,1,256,256]{3,2,1,0:T(8,128)(2,1)} %refs_0_.7) | copy-start | bytes 3145732
  8.8 1.2 %copy-start.2 = (bf16[8,1,256,256]{3,2,1,0:T(8,128)(2,1)S(1)}, bf16[8,1,256,256]{3,2,1,0:T(8,128)(2,1)}, u32[]{:S(2)}) copy-start(bf16[8,1,256,256]{3,2,1,0:T(8,128)(2,1)} %refs_6_) | copy-start | bytes 3145732
  10.0 0.7 copy-start.4
  28.7 29.5 %collective-permute-start.6 = (bf16[8,1,256,256]{3,2,1,0:T(8,128)(2,1)S(1)}, bf16[8,1,256,256]{3,2,1,0:T(8,128)(2,1)S(1)}, u32[]{:S(2)}, u32[]{:S(2)}) collective-permute-start(bf16[8,1,256,256]{3,2,1,0:T(8,128)(2,1)S(1)} %collective-permute-done.1.refs_4_.refs_6_), channel_id=1, source_target_pairs={{4,0},{5,1},{6,2},{7,3},{8,12},{9,13},{10,14},{11,15},{20,16},{21,... | collective-permute-start | bytes 3145736 | tf_op jit(solution)/shard_map/ppermute | solution.py:183
  30.0 28.2 %collective-permute-start.7 = (bf16[8,1,256,256]{3,2,1,0:T(8,128)(2,1)S(1)}, bf16[8,1,256,256]{3,2,1,0:T(8,128)(2,1)S(1)}, u32[]{:S(2)}, u32[]{:S(2)}) collective-permute-start(bf16[8,1,256,256]{3,2,1,0:T(8,128)(2,1)S(1)} %collective-permute-done.refs_4_.refs_6_), channel_id=1, source_target_pairs={{4,8},{5,9},{6,10},{7,11},{8,4},{9,5},{10,6},{11,7},{20,24},{21,25... | collective-permute-start | bytes 3145736 | tf_op jit(solution)/shard_map/ppermute | solution.py:183
  49.5 25.0 %collective-permute-start.5 = (bf16[8,1,256,256]{3,2,1,0:T(8,128)(2,1)S(1)}, bf16[8,1,256,256]{3,2,1,0:T(8,128)(2,1)S(1)}, u32[]{:S(2)}, u32[]{:S(2)}) collective-permute-start(bf16[8,1,256,256]{3,2,1,0:T(8,128)(2,1)S(1)} %copy-done.1), channel_id=1, source_target_pairs={{0,2},{1,3},{2,0},{3,1},{4,6},{5,7},{6,4},{7,5},{8,10},{9,11},{10,... | collective-permute-start | bytes 3145736 | tf_op jit(solution)/shard_map/ppermute | solution.py:183
  51.3 35.4 %collective-permute-start.13 = (bf16[1,12,256,256]{3,2,1,0:T(8,128)(2,1)S(1)}, bf16[1,12,256,256]{3,2,1,0:T(8,128)(2,1)S(1)}, u32[]{:S(2)}, u32[]{:S(2)}) collective-permute-start(bf16[1,12,256,256]{3,2,1,0:T(8,128)(2,1)S(1)} %get-tuple-element.41), channel_id=1, source_target_pairs={{0,1},{1,0},{2,3},{3,2},{4,5},{5,4},{6,7},{7,6},{8,9},{9,8},{10,11... | collective-permute-start | bytes 4718600 | tf_op jit(solution)/shard_map/ppermute | solution.py:183
  53.3 10.6 %collective-permute-start.8 = (bf16[2,256,256]{2,1,0:T(8,128)(2,1)S(1)}, bf16[2,256,256]{2,1,0:T(8,128)(2,1)S(1)}, u32[]{:S(2)}, u32[]{:S(2)}) collective-permute-start(bf16[2,256,256]{2,1,0:T(8,128)(2,1)S(1)} %shard_map.47), channel_id=1, source_target_pairs={{0,4},{1,5},{2,6},{3,7},{4,0},{5,1},{6,2},{7,3},{8,12},{9,13},{10,... | collective-permute-start | bytes 786440 | tf_op jit(solution)/shard_map/ppermute | solution.py:183
  58.2 38.1 %collective-permute-start.15 = (bf16[8,1,256,256]{3,2,1,0:T(8,128)(2,1)S(1)}, bf16[8,1,256,256]{3,2,1,0:T(8,128)(2,1)S(1)}, u32[]{:S(2)}, u32[]{:S(2)}) collective-permute-start(bf16[8,1,256,256]{3,2,1,0:T(8,128)(2,1)S(1)} %collective-permute-done.7.refs_5_.refs_7_), channel_id=1, source_target_pairs={{4,0},{5,1},{6,2},{7,3},{8,12},{9,13},{10,14},{11,15},{20,16},{21,... | collective-permute-start | bytes 3145736 | tf_op jit(solution)/shard_map/ppermute | solution.py:183
  61.4 8.3 %collective-permute-start.10 = (bf16[2,256,256]{2,1,0:T(8,128)(2,1)S(1)}, bf16[2,256,256]{2,1,0:T(8,128)(2,1)S(1)}, u32[]{:S(2)}, u32[]{:S(2)}) collective-permute-start(bf16[2,256,256]{2,1,0:T(8,128)(2,1)S(1)} %get-tuple-element.36), channel_id=1, source_target_pairs={{4,8},{5,9},{6,10},{7,11},{8,4},{9,5},{10,6},{11,7},{20,24},{21,25... | collective-permute-start | bytes 786440 | tf_op jit(solution)/shard_map/ppermute | solution.py:183
  65.8 18.0 %collective-permute-start.9 = (bf16[2,256,256]{2,1,0:T(8,128)(2,1)S(1)}, bf16[2,256,256]{2,1,0:T(8,128)(2,1)S(1)}, u32[]{:S(2)}, u32[]{:S(2)}) collective-permute-start(bf16[2,256,256]{2,1,0:T(8,128)(2,1)S(1)} %shard_map.48), channel_id=1, source_target_pairs={{0,8},{1,9},{2,10},{3,11},{4,12},{5,13},{6,14},{7,15},{8,0},{9,1},... | collective-permute-start | bytes 786440 | tf_op jit(solution)/shard_map/ppermute | solution.py:183
  83.8 3.5 %collective-permute-start.11 = (bf16[5,1,256,256]{3,2,1,0:T(8,128)(2,1)S(1)}, bf16[5,1,256,256]{3,2,1,0:T(8,128)(2,1)S(1)}, u32[]{:S(2)}, u32[]{:S(2)}) collective-permute-start(bf16[5,1,256,256]{3,2,1,0:T(8,128)(2,1)S(1)} %get-tuple-element.38), channel_id=1, source_target_pairs={{0,1},{1,0},{2,3},{3,2},{4,5},{5,4},{6,7},{7,6},{8,9},{9,8},{10,11... | collective-permute-start | bytes 1966088 | tf_op jit(solution)/shard_map/ppermute | solution.py:183
  83.9 2.8 %collective-permute-start.14 = (bf16[1,4,256,256]{3,2,1,0:T(8,128)(2,1)S(1)}, bf16[1,4,256,256]{3,2,1,0:T(8,128)(2,1)S(1)}, u32[]{:S(2)}, u32[]{:S(2)}) collective-permute-start(bf16[1,4,256,256]{3,2,1,0:T(8,128)(2,1)S(1)} %get-tuple-element.42), channel_id=1, source_target_pairs={{0,1},{1,0},{2,3},{3,2},{4,5},{5,4},{6,7},{7,6},{8,9},{9,8},{10,11... | collective-permute-start | bytes 1572872 | tf_op jit(solution)/shard_map/ppermute | solution.py:183
  84.4 2.9 %collective-permute-start.12 = (bf16[3,1,256,256]{3,2,1,0:T(8,128)(2,1)S(1)}, bf16[3,1,256,256]{3,2,1,0:T(8,128)(2,1)S(1)}, u32[]{:S(2)}, u32[]{:S(2)}) collective-permute-start(bf16[3,1,256,256]{3,2,1,0:T(8,128)(2,1)S(1)} %get-tuple-element.39), channel_id=1, source_target_pairs={{0,1},{1,0},{2,3},{3,2},{4,5},{5,4},{6,7},{7,6},{8,9},{9,8},{10,11... | collective-permute-start | bytes 1179656 | tf_op jit(solution)/shard_map/ppermute | solution.py:183
  89.2 14.4 %collective-permute-start.16 = (bf16[2,256,256]{2,1,0:T(8,128)(2,1)S(1)}, bf16[2,256,256]{2,1,0:T(8,128)(2,1)S(1)}, u32[]{:S(2)}, u32[]{:S(2)}) collective-permute-start(bf16[2,256,256]{2,1,0:T(8,128)(2,1)S(1)} %shard_map.54), channel_id=1, source_target_pairs={{0,8},{1,9},{2,10},{3,11},{4,12},{5,13},{6,14},{7,15},{8,0},{9,1},... | collective-permute-start | bytes 786440 | tf_op jit(solution)/shard_map/ppermute | solution.py:183
  91.2 25.7 %collective-permute-start.17 = (bf16[2,256,256]{2,1,0:T(8,128)(2,1)S(1)}, bf16[2,256,256]{2,1,0:T(8,128)(2,1)S(1)}, u32[]{:S(2)}, u32[]{:S(2)}) collective-permute-start(bf16[2,256,256]{2,1,0:T(8,128)(2,1)S(1)} %shard_map.53), channel_id=1, source_target_pairs={{0,4},{1,5},{2,6},{3,7},{4,0},{5,1},{6,2},{7,3},{8,12},{9,13},{10,... | collective-permute-start | bytes 786440 | tf_op jit(solution)/shard_map/ppermute | solution.py:183
  95.7 22.5 %collective-permute-start.19 = (bf16[2,256,256]{2,1,0:T(8,128)(2,1)S(1)}, bf16[2,256,256]{2,1,0:T(8,128)(2,1)S(1)}, u32[]{:S(2)}, u32[]{:S(2)}) collective-permute-start(bf16[2,256,256]{2,1,0:T(8,128)(2,1)S(1)} %get-tuple-element.45), channel_id=1, source_target_pairs={{4,8},{5,9},{6,10},{7,11},{8,4},{9,5},{10,6},{11,7},{20,24},{21,25... | collective-permute-start | bytes 786440 | tf_op jit(solution)/shard_map/ppermute | solution.py:183
  96.4 5.0 %copy-start.3 = (bf16[8,1,256,256]{3,2,1,0:T(8,128)(2,1)S(1)}, bf16[8,1,256,256]{3,2,1,0:T(8,128)(2,1)}, u32[]{:S(2)}) copy-start(bf16[8,1,256,256]{3,2,1,0:T(8,128)(2,1)} %refs_6_) | copy-start | bytes 3145732
  97.7 20.5 %collective-permute-start.18 = (bf16[4,256,256]{2,1,0:T(8,128)(2,1)S(1)}, bf16[4,256,256]{2,1,0:T(8,128)(2,1)S(1)}, u32[]{:S(2)}, u32[]{:S(2)}) collective-permute-start(bf16[4,256,256]{2,1,0:T(8,128)(2,1)S(1)} %shard_map.55), channel_id=1, source_target_pairs={{0,12},{1,13},{2,14},{3,15},{12,0},{13,1},{14,2},{15,3},{16,28},{1... | collective-permute-start | bytes 1572872 | tf_op jit(solution)/shard_map/ppermute | solution.py:183

commit v14 on v13

--- a/solution.py
+++ b/solution.py
@@ -210,13 +210,13 @@
 
     far_out, far_in = lax.optimization_barrier((far_out, far_in))
     third = exchange(far_in, 4, inner)
-    far_out, sent_1 = lax.optimization_barrier((far_out, sent_1))
     own_2 = products(2, *own, (far_out, far_in))
+    own_2, sent_1 = lax.optimization_barrier((own_2, sent_1))
     sent_2 = exchange(own_2, 8, every)
+
+    x_left, sent_2 = lax.optimization_barrier((x_left, sent_2))
     own_middle, own_mid = products(3, *own, (middle,), keep_mid=True)
     sent_own_middle = exchange(own_middle, 12, inner)
-
-    x_left, sent_2, sent_own_middle = lax.optimization_barrier((x_left, sent_2, sent_own_middle))
     across_left = [exchange(part, 1, every) for part in split(x_left, 0, 5 * x_left.shape[0] // 8)]
     other = ([(x_left,), across_left], [(x_psi,), across_psi])
     other_2 = products(2, *other, (far_out, far_in))
@@ -226,13 +226,12 @@
     other_1 = products(1, *other, (near,))
     other_sent_1 = exchange(other_1, 4, every)
 
-    third, other_1, other_middle, other_2 = lax.optimization_barrier((third, other_1, other_middle, other_2))
+    third, other_2, other_middle, other_1, sent_own_middle = lax.optimization_barrier((third, other_2, other_middle, other_1, sent_own_middle))
     last_third = second((own_mid, other_mid), third, dtype, 10**10)
     sent_third = exchange(last_third, 12, outer)
     right_last, last_third = lax.optimization_barrier((right_env, last_third))
     other_0 = products(0, *other, (right_last,))
 
-    other_sent_2, other_sent_1 = lax.optimization_barrier((other_sent_2, other_sent_1))
     held = [(0, own_0), (2, other_0), (8, sent_2), (10, other_sent_2), (4, sent_1), (6, other_sent_1)]
     out = place(16, held, flops=10**10)
     out = place(16, [(12, sent_third), (12, sent_own_middle), (14, sent_other_middle)], out)[:, None]

time: 119 us -> 117 us (0.983)
  waiting for transfers between devices: 70.9 us -> 69.6 us
  starting transfers between devices: 24.5 us -> 23.3 us
    ppermute x20, waiting for transfers between devices: 70.9 us -> 69.6 us  [exchange(): return lax.ppermute(array, 'sec', [(s, s ^ bits) for s in members])]
    ppermute x20, starting transfers between devices: 24.5 us -> 23.3 us  [exchange(): return lax.ppermute(array, 'sec', [(s, s ^ bits) for s in members])]
  transfers between devices with their start and end apart: 20 -> 20, of which waited for: 11 -> 9; matrix products, arithmetic and copies ran while one was open for 0% -> 0% of each run, Pallas kernels for 15% -> 15%
where the time goes in v14:
time: 117 us
  waiting for transfers between devices  69.6 us (59%)
  starting transfers between devices  23.3 us (20%)
  Pallas kernels  18.8 us (16%)
  local copies, waits for them, and re-layouts  4.73 us (4%)
    ppermute x20, waiting for transfers between devices, exchange(): return lax.ppermute(array, 'sec', [(s, s ^ bits) for s in members])  69.6 us
    ppermute x20, starting transfers between devices, exchange(): return lax.ppermute(array, 'sec', [(s, s ^ bits) for s in members])  23.3 us
    pallas_call x8, Pallas kernels, slot(): pl.pallas_call(functools.partial(slot_kernel, step, parts, len(rights)),...  15.1 us
    unnamed x10, local copies, waits for them, and re-layouts  4.73 us
  transfers between devices with their start and end apart: 20, of which 9 were waited for; matrix products, arithmetic and copies ran while one was open for 0% of the time, Pallas kernels for 15%

profile of v14, /device:TPU:0, one launch (start us, length us, event | category | flops | bytes accessed | tf_op | source)
XLA Modules:
  0.0 116.7 jit_solution(4152051679815075460)
XLA Ops:
  0.0 0.5 collective-permute-start.3
  0.5 2.5 %collective-permute-start.4 = (bf16[1,16,256,256]{3,2,1,0:T(8,128)(2,1)}, bf16[1,16,256,256]{3,2,1,0:T(8,128)(2,1)S(1)}, u32[]{:S(2)}, u32[]{:S(2)}) collective-permute-start(bf16[1,16,256,256]{3,2,1,0:T(8,128)(2,1)} %refs_2_.7), channel_id=1, source_target_pairs={{0,2},{1,3},{2,0},{3,1},{4,6},{5,7},{6,4},{7,5},{8,10},{9,11},{10,... | collective-permute-start | bytes 6291464 | tf_op jit(solution)/shard_map/ppermute | solution.py:183
  2.9 0.2 collective-permute-start.2
  3.2 0.7 collective-permute-start.1
  3.9 4.4 %collective-permute-start = (bf16[8,1,256,256]{3,2,1,0:T(8,128)(2,1)}, bf16[8,1,256,256]{3,2,1,0:T(8,128)(2,1)S(1)}, u32[]{:S(2)}, u32[]{:S(2)}) collective-permute-start(bf16[8,1,256,256]{3,2,1,0:T(8,128)(2,1)} %refs_6_), channel_id=1, source_target_pairs={{0,4},{1,5},{2,6},{3,7},{4,0},{5,1},{6,2},{7,3},{8,12},{9,13},{10,... | collective-permute-start | bytes 3145736 | tf_op jit(solution)/shard_map/ppermute | solution.py:183
  8.3 0.0 collective-permute-done.2.refs_1_
  8.3 0.0 collective-permute-done.3.refs_3_
  8.3 1.6 %copy-done = bf16[1,16,256,256]{3,2,1,0:T(8,128)(2,1)S(1)} copy-done((bf16[1,16,256,256]{3,2,1,0:T(8,128)(2,1)S(1)}, bf16[1,16,256,256]{3,2,1,0:T(8,128)(2,1)}, u32[]{:S(2)}) %copy-start) | copy-done | bytes 2097176
  9.9 1.2 %copy-done.1 = bf16[8,1,256,256]{3,2,1,0:T(8,128)(2,1)S(1)} copy-done((bf16[8,1,256,256]{3,2,1,0:T(8,128)(2,1)S(1)}, bf16[8,1,256,256]{3,2,1,0:T(8,128)(2,1)}, u32[]{:S(2)}) %copy-start.1) | copy-done | bytes 1048600
  11.1 1.2 %copy-done.2 = bf16[8,1,256,256]{3,2,1,0:T(8,128)(2,1)S(1)} copy-done((bf16[8,1,256,256]{3,2,1,0:T(8,128)(2,1)S(1)}, bf16[8,1,256,256]{3,2,1,0:T(8,128)(2,1)}, u32[]{:S(2)}) %copy-start.2) | copy-done | bytes 1048600
  12.3 0.7 copy-done.4
  13.0 1.9 %shard_map.46.refs_0_ = bf16[2,256,256]{2,1,0:T(8,128)(2,1)S(1)} custom-call(s32[8,16]{1,0:T(8,128)S(1)} %copy-done.4, bf16[8,1,256,256]{3,2,1,0:T(8,128)(2,1)S(1)} %copy-done.1, bf16[8,1,256,256]{3,2,1,0:T(8,128)(2,1)S(1)} %collective-permute-done.2.refs_1_, bf16[1,16,256,256]{3,2,1,0:T(8,128)(2,1)S(1)} %copy-done, ...), custom_call_target="tpu_custom_call" | custom-call | flops 1 | bytes 1 | tf_op jit(solution)/shard_map/pallas_call | solution.py:99
  14.9 16.9 %collective-permute-done.refs_4_.refs_6_ = bf16[8,1,256,256]{3,2,1,0:T(8,128)(2,1)S(1)} collective-permute-done((bf16[8,1,256,256]{3,2,1,0:T(8,128)(2,1)}, bf16[8,1,256,256]{3,2,1,0:T(8,128)(2,1)S(1)}, u32[]{:S(2)}, u32[]{:S(2)}) %collective-permute-start) | collective-permute-done | bytes 1048608 | tf_op jit(solution)/shard_map/ppermute | solution.py:183
  31.8 1.3 %collective-permute-start.6 = (bf16[8,1,256,256]{3,2,1,0:T(8,128)(2,1)S(1)}, bf16[8,1,256,256]{3,2,1,0:T(8,128)(2,1)S(1)}, u32[]{:S(2)}, u32[]{:S(2)}) collective-permute-start(bf16[8,1,256,256]{3,2,1,0:T(8,128)(2,1)S(1)} %collective-permute-done.1.refs_4_.refs_6_), channel_id=1, source_target_pairs={{4,0},{5,1},{6,2},{7,3},{8,12},{9,13},{10,14},{11,15},{20,16},{21,... | collective-permute-start | bytes 3145736 | tf_op jit(solution)/shard_map/ppermute | solution.py:183
  33.1 0.7 collective-permute-start.7
  33.9 15.6 %collective-permute-done.4.whole.refs_3_ = bf16[1,16,256,256]{3,2,1,0:T(8,128)(2,1)S(1)} collective-permute-done((bf16[1,16,256,256]{3,2,1,0:T(8,128)(2,1)}, bf16[1,16,256,256]{3,2,1,0:T(8,128)(2,1)S(1)}, u32[]{:S(2)}, u32[]{:S(2)}) %collective-permute-start.4) | collective-permute-done | bytes 2097184 | tf_op jit(solution)/shard_map/ppermute | solution.py:183
  49.5 1.7 %collective-permute-start.5 = (bf16[8,1,256,256]{3,2,1,0:T(8,128)(2,1)S(1)}, bf16[8,1,256,256]{3,2,1,0:T(8,128)(2,1)S(1)}, u32[]{:S(2)}, u32[]{:S(2)}) collective-permute-start(bf16[8,1,256,256]{3,2,1,0:T(8,128)(2,1)S(1)} %copy-done.1), channel_id=1, source_target_pairs={{0,2},{1,3},{2,0},{3,1},{4,6},{5,7},{6,4},{7,5},{8,10},{9,11},{10,... | collective-permute-start | bytes 3145736 | tf_op jit(solution)/shard_map/ppermute | solution.py:183
  51.2 0.1 shard_map.50
  51.3 0.1 collective-permute-start.12
  51.4 1.9 %shard_map.48 = bf16[2,256,256]{2,1,0:T(8,128)(2,1)S(1)} custom-call(s32[8,16]{1,0:T(8,128)S(1)} %copy-done.4, bf16[8,1,256,256]{3,2,1,0:T(8,128)(2,1)S(1)} %copy-done.1, bf16[8,1,256,256]{3,2,1,0:T(8,128)(2,1)S(1)} %collective-permute-done.2.refs_1_, bf16[1,16,256,256]{3,2,1,0:T(8,128)(2,1)S(1)} %copy-done, ...), custom_call_target="tpu_custom_call" | custom-call | flops 1 | bytes 1 | tf_op jit(solution)/shard_map/pallas_call | solution.py:99
  53.3 1.6 %collective-permute-start.8 = (bf16[2,256,256]{2,1,0:T(8,128)(2,1)S(1)}, bf16[2,256,256]{2,1,0:T(8,128)(2,1)S(1)}, u32[]{:S(2)}, u32[]{:S(2)}) collective-permute-start(bf16[2,256,256]{2,1,0:T(8,128)(2,1)S(1)} %shard_map.48), channel_id=1, source_target_pairs={{0,4},{1,5},{2,6},{3,7},{4,0},{5,1},{6,2},{7,3},{8,12},{9,13},{10,... | collective-permute-start | bytes 786440 | tf_op jit(solution)/shard_map/ppermute | solution.py:183
  54.9 4.9 %collective-permute-done.6.refs_4_.refs_6_ = bf16[8,1,256,256]{3,2,1,0:T(8,128)(2,1)S(1)} collective-permute-done((bf16[8,1,256,256]{3,2,1,0:T(8,128)(2,1)S(1)}, bf16[8,1,256,256]{3,2,1,0:T(8,128)(2,1)S(1)}, u32[]{:S(2)}, u32[]{:S(2)}) %collective-permute-start.6) | collective-permute-done | bytes 1048608 | tf_op jit(solution)/shard_map/ppermute | solution.py:183
  59.8 1.3 %collective-permute-start.14 = (bf16[8,1,256,256]{3,2,1,0:T(8,128)(2,1)S(1)}, bf16[8,1,256,256]{3,2,1,0:T(8,128)(2,1)S(1)}, u32[]{:S(2)}, u32[]{:S(2)}) collective-permute-start(bf16[8,1,256,256]{3,2,1,0:T(8,128)(2,1)S(1)} %collective-permute-done.7.refs_5_.refs_7_), channel_id=1, source_target_pairs={{4,0},{5,1},{6,2},{7,3},{8,12},{9,13},{10,14},{11,15},{20,16},{21,... | collective-permute-start | bytes 3145736 | tf_op jit(solution)/shard_map/ppermute | solution.py:183
  61.1 1.9 %shard_map.47 = bf16[2,256,256]{2,1,0:T(8,128)(2,1)S(1)} custom-call(s32[8,16]{1,0:T(8,128)S(1)} %copy-done.4, bf16[8,1,256,256]{3,2,1,0:T(8,128)(2,1)S(1)} %copy-done.1, bf16[8,1,256,256]{3,2,1,0:T(8,128)(2,1)S(1)} %collective-permute-done.2.refs_1_, bf16[1,16,256,256]{3,2,1,0:T(8,128)(2,1)S(1)} %copy-done, ...), custom_call_target="tpu_custom_call" | custom-call | flops 1 | bytes 1 | tf_op jit(solution)/shard_map/pallas_call | solution.py:99
  63.0 2.3 %collective-permute-done.8.refs_4_ = bf16[2,256,256]{2,1,0:T(8,128)(2,1)S(1)} collective-permute-done((bf16[2,256,256]{2,1,0:T(8,128)(2,1)S(1)}, bf16[2,256,256]{2,1,0:T(8,128)(2,1)S(1)}, u32[]{:S(2)}, u32[]{:S(2)}) %collective-permute-start.8) | collective-permute-done | bytes 262176 | tf_op jit(solution)/shard_map/ppermute | solution.py:183
  65.3 0.0 collective-permute-start.9
  65.3 9.1 %collective-permute-done.5.whole.refs_0_ = bf16[8,1,256,256]{3,2,1,0:T(8,128)(2,1)S(1)} collective-permute-done((bf16[8,1,256,256]{3,2,1,0:T(8,128)(2,1)S(1)}, bf16[8,1,256,256]{3,2,1,0:T(8,128)(2,1)S(1)}, u32[]{:S(2)}, u32[]{:S(2)}) %collective-permute-start.5) | collective-permute-done | bytes 1048608 | tf_op jit(solution)/shard_map/ppermute | solution.py:183
  74.4 2.8 %collective-permute-done.9.refs_2_ = bf16[2,256,256]{2,1,0:T(8,128)(2,1)S(1)} collective-permute-done((bf16[2,256,256]{2,1,0:T(8,128)(2,1)S(1)}, bf16[2,256,256]{2,1,0:T(8,128)(2,1)S(1)}, u32[]{:S(2)}, u32[]{:S(2)}) %collective-permute-start.9) | collective-permute-done | bytes 262176 | tf_op jit(solution)/shard_map/ppermute | solution.py:183
  77.2 0.1 shard_map.49
  77.3 0.1 collective-permute-start.10
  77.4 0.5 collective-permute-start.11
  77.9 1.9 %shard_map.51 = (bf16[2,256,256]{2,1,0:T(8,128)(2,1)S(1)}, bf16[512,2048]{1,0:T(8,128)(2,1)S(1)}) custom-call(s32[8,16]{1,0:T(8,128)S(1)} %copy-done.4, bf16[8,1,256,256]{3,2,1,0:T(8,128)(2,1)S(1)} %copy-done.1, bf16[8,1,256,256]{3,2,1,0:T(8,128)(2,1)S(1)} %collective-permute-done.2.refs_1_, bf16[1,16,256,256]{3,2,1,0:T(8,128)(2,1)S(1)} %copy-done, ...), custom_call_target="tpu_custom_call" | custom-call | flops 1 | bytes 1 | tf_op jit(solution)/shard_map/pallas_call | solution.py:99
  79.8 0.0 collective-permute-done.13.refs_5_
  79.8 0.7 collective-permute-start.15
  80.5 1.9 %shard_map.53 = bf16[2,256,256]{2,1,0:T(8,128)(2,1)S(1)} custom-call(s32[8,16]{1,0:T(8,128)S(1)} %copy-done.4, bf16[8,1,256,256]{3,2,1,0:T(8,128)(2,1)S(1)} %collective-permute-done.5.whole.refs_0_, bf16[5,1,256,256]{3,2,1,0:T(8,128)(2,1)S(1)} %collective-permute-done.10.refs_1_, bf16[3,1,256,256]{3,2,1,0:T(8,128)(2,1)S(1)} %collective-permute-done.11.refs_2_, ...), custom_call_target="tpu_custom_call" | custom-call | flops 1 | bytes 1 | tf_op jit(solution)/shard_map/pallas_call | solution.py:99
  82.4 2.7 %collective-permute-start.16 = (bf16[2,256,256]{2,1,0:T(8,128)(2,1)S(1)}, bf16[2,256,256]{2,1,0:T(8,128)(2,1)S(1)}, u32[]{:S(2)}, u32[]{:S(2)}) collective-permute-start(bf16[2,256,256]{2,1,0:T(8,128)(2,1)S(1)} %shard_map.53), channel_id=1, source_target_pairs={{0,8},{1,9},{2,10},{3,11},{4,12},{5,13},{6,14},{7,15},{8,0},{9,1},... | collective-permute-start | bytes 786440 | tf_op jit(solution)/shard_map/ppermute | solution.py:183
  85.1 1.9 %shard_map.54 = bf16[2,256,256]{2,1,0:T(8,128)(2,1)S(1)} custom-call(s32[8,16]{1,0:T(8,128)S(1)} %copy-done.4, bf16[8,1,256,256]{3,2,1,0:T(8,128)(2,1)S(1)} %collective-permute-done.5.whole.refs_0_, bf16[5,1,256,256]{3,2,1,0:T(8,128)(2,1)S(1)} %collective-permute-done.10.refs_1_, bf16[3,1,256,256]{3,2,1,0:T(8,128)(2,1)S(1)} %collective-permute-done.11.refs_2_, ...), custom_call_target="tpu_custom_call" | custom-call | flops 1 | bytes 1 | tf_op jit(solution)/shard_map/pallas_call | solution.py:99
  87.0 0.8 collective-permute-start.17
  87.9 1.9 %shard_map.52 = (bf16[2,256,256]{2,1,0:T(8,128)(2,1)S(1)}, bf16[512,2048]{1,0:T(8,128)(2,1)S(1)}) custom-call(s32[8,16]{1,0:T(8,128)S(1)} %copy-done.4, bf16[8,1,256,256]{3,2,1,0:T(8,128)(2,1)S(1)} %collective-permute-done.5.whole.refs_0_, bf16[5,1,256,256]{3,2,1,0:T(8,128)(2,1)S(1)} %collective-permute-done.10.refs_1_, ...), custom_call_target="tpu_custom_call" | custom-call | flops 1 | bytes 1 | tf_op jit(solution)/shard_map/pallas_call | solution.py:99
  89.7 0.7 collective-permute-start.19
  90.4 3.0 %collective-permute-done.14.refs_2_ = bf16[8,1,256,256]{3,2,1,0:T(8,128)(2,1)S(1)} collective-permute-done((bf16[8,1,256,256]{3,2,1,0:T(8,128)(2,1)S(1)}, bf16[8,1,256,256]{3,2,1,0:T(8,128)(2,1)S(1)}, u32[]{:S(2)}, u32[]{:S(2)}) %collective-permute-start.14) | collective-permute-done | bytes 1048608 | tf_op jit(solution)/shard_map/ppermute | solution.py:183
  93.4 1.3 %shard_map.55 = bf16[4,256,256]{2,1,0:T(8,128)(2,1)S(1)} custom-call(bf16[512,2048]{1,0:T(8,128)(2,1)S(1)} %get-tuple-element.40.refs_0_, bf16[512,2048]{1,0:T(8,128)(2,1)S(1)} %get-tuple-element.41.refs_1_, bf16[8,1,256,256]{3,2,1,0:T(8,128)(2,1)S(1)} %collective-permute-done.14.refs_2_), custom_call_target="tpu_custom_call" | custom-call | flops 10000000000 | bytes 1 | tf_op jit(solution)/shard_map/pallas_call | solution.py:78
  94.7 2.8 %collective-permute-start.18 = (bf16[4,256,256]{2,1,0:T(8,128)(2,1)S(1)}, bf16[4,256,256]{2,1,0:T(8,128)(2,1)S(1)}, u32[]{:S(2)}, u32[]{:S(2)}) collective-permute-start(bf16[4,256,256]{2,1,0:T(8,128)(2,1)S(1)} %shard_map.55), channel_id=1, source_target_pairs={{0,12},{1,13},{2,14},{3,15},{12,0},{13,1},{14,2},{15,3},{16,28},{1... | collective-permute-start | bytes 1572872 | tf_op jit(solution)/shard_map/ppermute | solution.py:183
  97.5 1.9 %shard_map.56.refs_1_ = bf16[2,256,256]{2,1,0:T(8,128)(2,1)S(1)} custom-call(s32[8,16]{1,0:T(8,128)S(1)} %copy-done.4, bf16[8,1,256,256]{3,2,1,0:T(8,128)(2,1)S(1)} %collective-permute-done.5.whole.refs_0_, bf16[5,1,256,256]{3,2,1,0:T(8,128)(2,1)S(1)} %collective-permute-done.10.refs_1_, bf16[3,1,256,256]{3,2,1,0:T(8,128)(2,1)S(1)} %collective-permute-done.11.refs_2_, ...), custom_call_target="tpu_custom_call" | custom-call | flops 1 | bytes 1 | tf_op jit(solution)/shard_map/pallas_call | solution.py:99
  99.4 13.4 %collective-permute-done.16.refs_3_ = bf16[2,256,256]{2,1,0:T(8,128)(2,1)S(1)} collective-permute-done((bf16[2,256,256]{2,1,0:T(8,128)(2,1)S(1)}, bf16[2,256,256]{2,1,0:T(8,128)(2,1)S(1)}, u32[]{:S(2)}, u32[]{:S(2)}) %collective-permute-start.16) | collective-permute-done | bytes 262176 | tf_op jit(solution)/shard_map/ppermute | solution.py:183
  112.8 1.7 %collective-permute-done.17.refs_5_ = bf16[2,256,256]{2,1,0:T(8,128)(2,1)S(1)} collective-permute-done((bf16[2,256,256]{2,1,0:T(8,128)(2,1)S(1)}, bf16[2,256,256]{2,1,0:T(8,128)(2,1)S(1)}, u32[]{:S(2)}, u32[]{:S(2)}) %collective-permute-start.17) | collective-permute-done | bytes 262176 | tf_op jit(solution)/shard_map/ppermute | solution.py:183
  114.4 1.3 %shard_map.57.refs_0_ = bf16[16,256,256]{2,1,0:T(8,128)(2,1)} custom-call(bf16[2,256,256]{2,1,0:T(8,128)(2,1)S(1)} %shard_map.46.refs_0_, bf16[2,256,256]{2,1,0:T(8,128)(2,1)S(1)} %shard_map.56.refs_1_, bf16[2,256,256]{2,1,0:T(8,128)(2,1)S(1)} %collective-permute-done.9.refs_2_, bf16[2,256,256]{2,1,0:T(8,128)(2,1)S(1)} %collective-permute-done.16.refs_3_, ...), custom_call_target="tpu_custom_call" | custom-call | flops 10000000000 | bytes 1 | tf_op jit(solution)/shard_map/pallas_call | solution.py:170
  115.7 0.9 shard_map.58
  (15 shorter events, 0.0 us)
Async XLA Ops:
  0.0 8.3 %collective-permute-start.3 = (bf16[1,16,256,256]{3,2,1,0:T(8,128)(2,1)}, bf16[1,16,256,256]{3,2,1,0:T(8,128)(2,1)S(1)}, u32[]{:S(2)}, u32[]{:S(2)}) collective-permute-start(bf16[1,16,256,256]{3,2,1,0:T(8,128)(2,1)} %refs_2_.7), channel_id=1, source_target_pairs={{0,1},{1,0},{2,3},{3,2},{4,5},{5,4},{6,7},{7,6},{8,9},{9,8},{10,11... | collective-permute-start | bytes 6291464 | tf_op jit(solution)/shard_map/ppermute | solution.py:183
  0.5 49.0 %collective-permute-start.4 = (bf16[1,16,256,256]{3,2,1,0:T(8,128)(2,1)}, bf16[1,16,256,256]{3,2,1,0:T(8,128)(2,1)S(1)}, u32[]{:S(2)}, u32[]{:S(2)}) collective-permute-start(bf16[1,16,256,256]{3,2,1,0:T(8,128)(2,1)} %refs_2_.7), channel_id=1, source_target_pairs={{0,2},{1,3},{2,0},{3,1},{4,6},{5,7},{6,4},{7,5},{8,10},{9,11},{10,... | collective-permute-start | bytes 6291464 | tf_op jit(solution)/shard_map/ppermute | solution.py:183
  2.9 5.4 %collective-permute-start.2 = (bf16[8,1,256,256]{3,2,1,0:T(8,128)(2,1)}, bf16[8,1,256,256]{3,2,1,0:T(8,128)(2,1)S(1)}, u32[]{:S(2)}, u32[]{:S(2)}) collective-permute-start(bf16[8,1,256,256]{3,2,1,0:T(8,128)(2,1)} %refs_0_.7), channel_id=1, source_target_pairs={{0,1},{1,0},{2,3},{3,2},{4,5},{5,4},{6,7},{7,6},{8,9},{9,8},{10,11... | collective-permute-start | bytes 3145736 | tf_op jit(solution)/shard_map/ppermute | solution.py:183
  3.2 11.7 %collective-permute-start.1 = (bf16[8,1,256,256]{3,2,1,0:T(8,128)(2,1)}, bf16[8,1,256,256]{3,2,1,0:T(8,128)(2,1)S(1)}, u32[]{:S(2)}, u32[]{:S(2)}) collective-permute-start(bf16[8,1,256,256]{3,2,1,0:T(8,128)(2,1)} %refs_6_), channel_id=1, source_target_pairs={{4,8},{5,9},{6,10},{7,11},{8,4},{9,5},{10,6},{11,7},{20,24},{21,25... | collective-permute-start | bytes 3145736 | tf_op jit(solution)/shard_map/ppermute | solution.py:183
  3.9 27.9 %collective-permute-start = (bf16[8,1,256,256]{3,2,1,0:T(8,128)(2,1)}, bf16[8,1,256,256]{3,2,1,0:T(8,128)(2,1)S(1)}, u32[]{:S(2)}, u32[]{:S(2)}) collective-permute-start(bf16[8,1,256,256]{3,2,1,0:T(8,128)(2,1)} %refs_6_), channel_id=1, source_target_pairs={{0,4},{1,5},{2,6},{3,7},{4,0},{5,1},{6,2},{7,3},{8,12},{9,13},{10,... | collective-permute-start | bytes 3145736 | tf_op jit(solution)/shard_map/ppermute | solution.py:183
  8.3 1.6 %copy-start = (bf16[1,16,256,256]{3,2,1,0:T(8,128)(2,1)S(1)}, bf16[1,16,256,256]{3,2,1,0:T(8,128)(2,1)}, u32[]{:S(2)}) copy-start(bf16[1,16,256,256]{3,2,1,0:T(8,128)(2,1)} %refs_2_.7) | copy-start | bytes 6291460
  9.9 1.2 %copy-start.1 = (bf16[8,1,256,256]{3,2,1,0:T(8,128)(2,1)S(1)}, bf16[8,1,256,256]{3,2,1,0:T(8,128)(2,1)}, u32[]{:S(2)}) copy-start(bf16[8,1,256,256]{3,2,1,0:T(8,128)(2,1)} %refs_0_.7) | copy-start | bytes 3145732
  11.1 1.2 %copy-start.2 = (bf16[8,1,256,256]{3,2,1,0:T(8,128)(2,1)S(1)}, bf16[8,1,256,256]{3,2,1,0:T(8,128)(2,1)}, u32[]{:S(2)}) copy-start(bf16[8,1,256,256]{3,2,1,0:T(8,128)(2,1)} %refs_6_) | copy-start | bytes 3145732
  12.3 0.7 copy-start.4
  31.8 28.0 %collective-permute-start.6 = (bf16[8,1,256,256]{3,2,1,0:T(8,128)(2,1)S(1)}, bf16[8,1,256,256]{3,2,1,0:T(8,128)(2,1)S(1)}, u32[]{:S(2)}, u32[]{:S(2)}) collective-permute-start(bf16[8,1,256,256]{3,2,1,0:T(8,128)(2,1)S(1)} %collective-permute-done.1.refs_4_.refs_6_), channel_id=1, source_target_pairs={{4,0},{5,1},{6,2},{7,3},{8,12},{9,13},{10,14},{11,15},{20,16},{21,... | collective-permute-start | bytes 3145736 | tf_op jit(solution)/shard_map/ppermute | solution.py:183
  33.1 26.7 %collective-permute-start.7 = (bf16[8,1,256,256]{3,2,1,0:T(8,128)(2,1)S(1)}, bf16[8,1,256,256]{3,2,1,0:T(8,128)(2,1)S(1)}, u32[]{:S(2)}, u32[]{:S(2)}) collective-permute-start(bf16[8,1,256,256]{3,2,1,0:T(8,128)(2,1)S(1)} %collective-permute-done.refs_4_.refs_6_), channel_id=1, source_target_pairs={{4,8},{5,9},{6,10},{7,11},{8,4},{9,5},{10,6},{11,7},{20,24},{21,25... | collective-permute-start | bytes 3145736 | tf_op jit(solution)/shard_map/ppermute | solution.py:183
  49.5 25.0 %collective-permute-start.5 = (bf16[8,1,256,256]{3,2,1,0:T(8,128)(2,1)S(1)}, bf16[8,1,256,256]{3,2,1,0:T(8,128)(2,1)S(1)}, u32[]{:S(2)}, u32[]{:S(2)}) collective-permute-start(bf16[8,1,256,256]{3,2,1,0:T(8,128)(2,1)S(1)} %copy-done.1), channel_id=1, source_target_pairs={{0,2},{1,3},{2,0},{3,1},{4,6},{5,7},{6,4},{7,5},{8,10},{9,11},{10,... | collective-permute-start | bytes 3145736 | tf_op jit(solution)/shard_map/ppermute | solution.py:183
  51.3 29.1 %collective-permute-start.12 = (bf16[1,12,256,256]{3,2,1,0:T(8,128)(2,1)S(1)}, bf16[1,12,256,256]{3,2,1,0:T(8,128)(2,1)S(1)}, u32[]{:S(2)}, u32[]{:S(2)}) collective-permute-start(bf16[1,12,256,256]{3,2,1,0:T(8,128)(2,1)S(1)} %get-tuple-element.38), channel_id=1, source_target_pairs={{0,1},{1,0},{2,3},{3,2},{4,5},{5,4},{6,7},{7,6},{8,9},{9,8},{10,11... | collective-permute-start | bytes 4718600 | tf_op jit(solution)/shard_map/ppermute | solution.py:183
  53.3 12.0 %collective-permute-start.8 = (bf16[2,256,256]{2,1,0:T(8,128)(2,1)S(1)}, bf16[2,256,256]{2,1,0:T(8,128)(2,1)S(1)}, u32[]{:S(2)}, u32[]{:S(2)}) collective-permute-start(bf16[2,256,256]{2,1,0:T(8,128)(2,1)S(1)} %shard_map.48), channel_id=1, source_target_pairs={{0,4},{1,5},{2,6},{3,7},{4,0},{5,1},{6,2},{7,3},{8,12},{9,13},{10,... | collective-permute-start | bytes 786440 | tf_op jit(solution)/shard_map/ppermute | solution.py:183
  59.8 33.6 %collective-permute-start.14 = (bf16[8,1,256,256]{3,2,1,0:T(8,128)(2,1)S(1)}, bf16[8,1,256,256]{3,2,1,0:T(8,128)(2,1)S(1)}, u32[]{:S(2)}, u32[]{:S(2)}) collective-permute-start(bf16[8,1,256,256]{3,2,1,0:T(8,128)(2,1)S(1)} %collective-permute-done.7.refs_5_.refs_7_), channel_id=1, source_target_pairs={{4,0},{5,1},{6,2},{7,3},{8,12},{9,13},{10,14},{11,15},{20,16},{21,... | collective-permute-start | bytes 3145736 | tf_op jit(solution)/shard_map/ppermute | solution.py:183
  65.3 11.9 %collective-permute-start.9 = (bf16[2,256,256]{2,1,0:T(8,128)(2,1)S(1)}, bf16[2,256,256]{2,1,0:T(8,128)(2,1)S(1)}, u32[]{:S(2)}, u32[]{:S(2)}) collective-permute-start(bf16[2,256,256]{2,1,0:T(8,128)(2,1)S(1)} %shard_map.47), channel_id=1, source_target_pairs={{0,8},{1,9},{2,10},{3,11},{4,12},{5,13},{6,14},{7,15},{8,0},{9,1},... | collective-permute-start | bytes 786440 | tf_op jit(solution)/shard_map/ppermute | solution.py:183
  65.3 14.5 %collective-permute-start.13 = (bf16[1,4,256,256]{3,2,1,0:T(8,128)(2,1)S(1)}, bf16[1,4,256,256]{3,2,1,0:T(8,128)(2,1)S(1)}, u32[]{:S(2)}, u32[]{:S(2)}) collective-permute-start(bf16[1,4,256,256]{3,2,1,0:T(8,128)(2,1)S(1)} %get-tuple-element.39), channel_id=1, source_target_pairs={{0,1},{1,0},{2,3},{3,2},{4,5},{5,4},{6,7},{7,6},{8,9},{9,8},{10,11... | collective-permute-start | bytes 1572872 | tf_op jit(solution)/shard_map/ppermute | solution.py:183
  77.3 3.2 %collective-permute-start.10 = (bf16[5,1,256,256]{3,2,1,0:T(8,128)(2,1)S(1)}, bf16[5,1,256,256]{3,2,1,0:T(8,128)(2,1)S(1)}, u32[]{:S(2)}, u32[]{:S(2)}) collective-permute-start(bf16[5,1,256,256]{3,2,1,0:T(8,128)(2,1)S(1)} %get-tuple-element.35), channel_id=1, source_target_pairs={{0,1},{1,0},{2,3},{3,2},{4,5},{5,4},{6,7},{7,6},{8,9},{9,8},{10,11... | collective-permute-start | bytes 1966088 | tf_op jit(solution)/shard_map/ppermute | solution.py:183
  77.4 3.1 %collective-permute-start.11 = (bf16[3,1,256,256]{3,2,1,0:T(8,128)(2,1)S(1)}, bf16[3,1,256,256]{3,2,1,0:T(8,128)(2,1)S(1)}, u32[]{:S(2)}, u32[]{:S(2)}) collective-permute-start(bf16[3,1,256,256]{3,2,1,0:T(8,128)(2,1)S(1)} %get-tuple-element.36), channel_id=1, source_target_pairs={{0,1},{1,0},{2,3},{3,2},{4,5},{5,4},{6,7},{7,6},{8,9},{9,8},{10,11... | collective-permute-start | bytes 1179656 | tf_op jit(solution)/shard_map/ppermute | solution.py:183
  79.8 10.7 %collective-permute-start.15 = (bf16[2,256,256]{2,1,0:T(8,128)(2,1)S(1)}, bf16[2,256,256]{2,1,0:T(8,128)(2,1)S(1)}, u32[]{:S(2)}, u32[]{:S(2)}) collective-permute-start(bf16[2,256,256]{2,1,0:T(8,128)(2,1)S(1)} %get-tuple-element.43), channel_id=1, source_target_pairs={{4,8},{5,9},{6,10},{7,11},{8,4},{9,5},{10,6},{11,7},{20,24},{21,25... | collective-permute-start | bytes 786440 | tf_op jit(solution)/shard_map/ppermute | solution.py:183
  82.4 30.4 %collective-permute-start.16 = (bf16[2,256,256]{2,1,0:T(8,128)(2,1)S(1)}, bf16[2,256,256]{2,1,0:T(8,128)(2,1)S(1)}, u32[]{:S(2)}, u32[]{:S(2)}) collective-permute-start(bf16[2,256,256]{2,1,0:T(8,128)(2,1)S(1)} %shard_map.53), channel_id=1, source_target_pairs={{0,8},{1,9},{2,10},{3,11},{4,12},{5,13},{6,14},{7,15},{8,0},{9,1},... | collective-permute-start | bytes 786440 | tf_op jit(solution)/shard_map/ppermute | solution.py:183
  87.0 27.4 %collective-permute-start.17 = (bf16[2,256,256]{2,1,0:T(8,128)(2,1)S(1)}, bf16[2,256,256]{2,1,0:T(8,128)(2,1)S(1)}, u32[]{:S(2)}, u32[]{:S(2)}) collective-permute-start(bf16[2,256,256]{2,1,0:T(8,128)(2,1)S(1)} %shard_map.54), channel_id=1, source_target_pairs={{0,4},{1,5},{2,6},{3,7},{4,0},{5,1},{6,2},{7,3},{8,12},{9,13},{10,... | collective-permute-start | bytes 786440 | tf_op jit(solution)/shard_map/ppermute | solution.py:183
  89.7 26.0 %collective-permute-start.19 = (bf16[2,256,256]{2,1,0:T(8,128)(2,1)S(1)}, bf16[2,256,256]{2,1,0:T(8,128)(2,1)S(1)}, u32[]{:S(2)}, u32[]{:S(2)}) collective-permute-start(bf16[2,256,256]{2,1,0:T(8,128)(2,1)S(1)} %get-tuple-element.42), channel_id=1, source_target_pairs={{4,8},{5,9},{6,10},{7,11},{8,4},{9,5},{10,6},{11,7},{20,24},{21,25... | collective-permute-start | bytes 786440 | tf_op jit(solution)/shard_map/ppermute | solution.py:183
  93.4 4.1 %copy-start.3 = (bf16[8,1,256,256]{3,2,1,0:T(8,128)(2,1)S(1)}, bf16[8,1,256,256]{3,2,1,0:T(8,128)(2,1)}, u32[]{:S(2)}) copy-start(bf16[8,1,256,256]{3,2,1,0:T(8,128)(2,1)} %refs_6_) | copy-start | bytes 3145732
  94.7 21.0 %collective-permute-start.18 = (bf16[4,256,256]{2,1,0:T(8,128)(2,1)S(1)}, bf16[4,256,256]{2,1,0:T(8,128)(2,1)S(1)}, u32[]{:S(2)}, u32[]{:S(2)}) collective-permute-start(bf16[4,256,256]{2,1,0:T(8,128)(2,1)S(1)} %shard_map.55), channel_id=1, source_target_pairs={{0,12},{1,13},{2,14},{3,15},{12,0},{13,1},{14,2},{15,3},{16,28},{1... | collective-permute-start | bytes 1572872 | tf_op jit(solution)/shard_map/ppermute | solution.py:183

commit v15 on v14

--- a/solution.py
+++ b/solution.py
@@ -204,19 +204,19 @@
 
     x_psi, left_next = lax.optimization_barrier((x_psi, left_env))
     x_left = exchange(left_next, 2, every)
-    across_psi = [exchange(part, 1, every) for part in split(x_psi, 1, 6 * x_psi.shape[1] // 8)]
+    across_psi = [exchange(part, 1, every) for part in split(x_psi, 1, 9 * x_psi.shape[1] // 16)]
+    own_middle, own_mid = products(3, *own, (middle,), keep_mid=True)
+    sent_own_middle = exchange(own_middle, 12, inner)
     own_1 = products(1, *own, (near,))
     sent_1 = exchange(own_1, 4, every)
 
     far_out, far_in = lax.optimization_barrier((far_out, far_in))
     third = exchange(far_in, 4, inner)
     own_2 = products(2, *own, (far_out, far_in))
-    own_2, sent_1 = lax.optimization_barrier((own_2, sent_1))
+    own_2, sent_1, sent_own_middle = lax.optimization_barrier((own_2, sent_1, sent_own_middle))
     sent_2 = exchange(own_2, 8, every)
 
     x_left, sent_2 = lax.optimization_barrier((x_left, sent_2))
-    own_middle, own_mid = products(3, *own, (middle,), keep_mid=True)
-    sent_own_middle = exchange(own_middle, 12, inner)
     across_left = [exchange(part, 1, every) for part in split(x_left, 0, 5 * x_left.shape[0] // 8)]
     other = ([(x_left,), across_left], [(x_psi,), across_psi])
     other_2 = products(2, *other, (far_out, far_in))
@@ -226,7 +226,7 @@
     other_1 = products(1, *other, (near,))
     other_sent_1 = exchange(other_1, 4, every)
 
-    third, other_2, other_middle, other_1, sent_own_middle = lax.optimization_barrier((third, other_2, other_middle, other_1, sent_own_middle))
+    third, other_1, other_2, other_middle = lax.optimization_barrier((third, other_1, other_2, other_middle))
     last_third = second((own_mid, other_mid), third, dtype, 10**10)
     sent_third = exchange(last_third, 12, outer)
     right_last, last_third = lax.optimization_barrier((right_env, last_third))

time: 117 us -> 119 us (1.017)
  starting transfers between devices: 23.3 us -> 25.1 us
    ppermute x20, starting transfers between devices: 23.3 us -> 25.1 us  [exchange(): return lax.ppermute(array, 'sec', [(s, s ^ bits) for s in members])]
where the time goes in v15:
time: 119 us
  waiting for transfers between devices  70.1 us (59%)
  starting transfers between devices  25.1 us (21%)
  Pallas kernels  18.8 us (16%)
  local copies, waits for them, and re-layouts  4.73 us (4%)
    ppermute x20, waiting for transfers between devices, exchange(): return lax.ppermute(array, 'sec', [(s, s ^ bits) for s in members])  70.1 us
    ppermute x20, starting transfers between devices, exchange(): return lax.ppermute(array, 'sec', [(s, s ^ bits) for s in members])  25.1 us
    pallas_call x8, Pallas kernels, slot(): pl.pallas_call(functools.partial(slot_kernel, step, parts, len(rights)),...  15.1 us
    unnamed x10, local copies, waits for them, and re-layouts  4.73 us
  transfers between devices with their start and end apart: 20, of which 9 were waited for; matrix products, arithmetic and copies ran while one was open for 0% of the time, Pallas kernels for 15%

profile of v15, /device:TPU:0, one launch (start us, length us, event | category | flops | bytes accessed | tf_op | source)
XLA Modules:
  0.0 118.9 jit_solution(8360588732991296687)
XLA Ops:
  0.0 0.5 collective-permute-start.3
  0.5 2.5 %collective-permute-start.4 = (bf16[1,16,256,256]{3,2,1,0:T(8,128)(2,1)}, bf16[1,16,256,256]{3,2,1,0:T(8,128)(2,1)S(1)}, u32[]{:S(2)}, u32[]{:S(2)}) collective-permute-start(bf16[1,16,256,256]{3,2,1,0:T(8,128)(2,1)} %refs_2_.7), channel_id=1, source_target_pairs={{0,2},{1,3},{2,0},{3,1},{4,6},{5,7},{6,4},{7,5},{8,10},{9,11},{10,... | collective-permute-start | bytes 6291464 | tf_op jit(solution)/shard_map/ppermute | solution.py:183
  2.9 0.2 collective-permute-start.2
  3.2 1.6 %collective-permute-start = (bf16[8,1,256,256]{3,2,1,0:T(8,128)(2,1)}, bf16[8,1,256,256]{3,2,1,0:T(8,128)(2,1)S(1)}, u32[]{:S(2)}, u32[]{:S(2)}) collective-permute-start(bf16[8,1,256,256]{3,2,1,0:T(8,128)(2,1)} %refs_6_), channel_id=1, source_target_pairs={{0,4},{1,5},{2,6},{3,7},{4,0},{5,1},{6,2},{7,3},{8,12},{9,13},{10,... | collective-permute-start | bytes 3145736 | tf_op jit(solution)/shard_map/ppermute | solution.py:183
  4.7 0.7 collective-permute-start.1
  5.5 0.5 collective-permute-done.2.refs_1_
  6.0 1.6 %copy-done = bf16[1,16,256,256]{3,2,1,0:T(8,128)(2,1)S(1)} copy-done((bf16[1,16,256,256]{3,2,1,0:T(8,128)(2,1)S(1)}, bf16[1,16,256,256]{3,2,1,0:T(8,128)(2,1)}, u32[]{:S(2)}) %copy-start) | copy-done | bytes 2097176
  7.5 1.2 %copy-done.1 = bf16[8,1,256,256]{3,2,1,0:T(8,128)(2,1)S(1)} copy-done((bf16[8,1,256,256]{3,2,1,0:T(8,128)(2,1)S(1)}, bf16[8,1,256,256]{3,2,1,0:T(8,128)(2,1)}, u32[]{:S(2)}) %copy-start.1) | copy-done | bytes 1048600
  8.8 1.2 %copy-done.2 = bf16[8,1,256,256]{3,2,1,0:T(8,128)(2,1)S(1)} copy-done((bf16[8,1,256,256]{3,2,1,0:T(8,128)(2,1)S(1)}, bf16[8,1,256,256]{3,2,1,0:T(8,128)(2,1)}, u32[]{:S(2)}) %copy-start.2) | copy-done | bytes 1048600
  10.0 0.7 copy-done.4
  10.7 1.9 %shard_map.46.refs_0_ = bf16[2,256,256]{2,1,0:T(8,128)(2,1)S(1)} custom-call(s32[8,16]{1,0:T(8,128)S(1)} %copy-done.4, bf16[8,1,256,256]{3,2,1,0:T(8,128)(2,1)S(1)} %copy-done.1, bf16[8,1,256,256]{3,2,1,0:T(8,128)(2,1)S(1)} %collective-permute-done.2.refs_1_, bf16[1,16,256,256]{3,2,1,0:T(8,128)(2,1)S(1)} %copy-done, ...), custom_call_target="tpu_custom_call" | custom-call | flops 1 | bytes 1 | tf_op jit(solution)/shard_map/pallas_call | solution.py:99
  12.6 16.2 %collective-permute-done.refs_4_.refs_6_ = bf16[8,1,256,256]{3,2,1,0:T(8,128)(2,1)S(1)} collective-permute-done((bf16[8,1,256,256]{3,2,1,0:T(8,128)(2,1)}, bf16[8,1,256,256]{3,2,1,0:T(8,128)(2,1)S(1)}, u32[]{:S(2)}, u32[]{:S(2)}) %collective-permute-start) | collective-permute-done | bytes 1048608 | tf_op jit(solution)/shard_map/ppermute | solution.py:183
  28.7 0.0 collective-permute-done.1.refs_4_.refs_6_
  28.7 1.3 %collective-permute-start.6 = (bf16[8,1,256,256]{3,2,1,0:T(8,128)(2,1)S(1)}, bf16[8,1,256,256]{3,2,1,0:T(8,128)(2,1)S(1)}, u32[]{:S(2)}, u32[]{:S(2)}) collective-permute-start(bf16[8,1,256,256]{3,2,1,0:T(8,128)(2,1)S(1)} %collective-permute-done.1.refs_4_.refs_6_), channel_id=1, source_target_pairs={{4,0},{5,1},{6,2},{7,3},{8,12},{9,13},{10,14},{11,15},{20,16},{21,... | collective-permute-start | bytes 3145736 | tf_op jit(solution)/shard_map/ppermute | solution.py:183
  30.0 0.7 collective-permute-start.7
  30.8 18.7 %collective-permute-done.4.whole.refs_3_ = bf16[1,16,256,256]{3,2,1,0:T(8,128)(2,1)S(1)} collective-permute-done((bf16[1,16,256,256]{3,2,1,0:T(8,128)(2,1)}, bf16[1,16,256,256]{3,2,1,0:T(8,128)(2,1)S(1)}, u32[]{:S(2)}, u32[]{:S(2)}) %collective-permute-start.4) | collective-permute-done | bytes 2097184 | tf_op jit(solution)/shard_map/ppermute | solution.py:183
  49.5 1.7 %collective-permute-start.5 = (bf16[8,1,256,256]{3,2,1,0:T(8,128)(2,1)S(1)}, bf16[8,1,256,256]{3,2,1,0:T(8,128)(2,1)S(1)}, u32[]{:S(2)}, u32[]{:S(2)}) collective-permute-start(bf16[8,1,256,256]{3,2,1,0:T(8,128)(2,1)S(1)} %copy-done.1), channel_id=1, source_target_pairs={{0,2},{1,3},{2,0},{3,1},{4,6},{5,7},{6,4},{7,5},{8,10},{9,11},{10,... | collective-permute-start | bytes 3145736 | tf_op jit(solution)/shard_map/ppermute | solution.py:183
  51.2 1.9 %shard_map.49 = (bf16[2,256,256]{2,1,0:T(8,128)(2,1)S(1)}, bf16[512,2048]{1,0:T(8,128)(2,1)S(1)}) custom-call(s32[8,16]{1,0:T(8,128)S(1)} %copy-done.4, bf16[8,1,256,256]{3,2,1,0:T(8,128)(2,1)S(1)} %copy-done.1, bf16[8,1,256,256]{3,2,1,0:T(8,128)(2,1)S(1)} %collective-permute-done.2.refs_1_, bf16[1,16,256,256]{3,2,1,0:T(8,128)(2,1)S(1)} %copy-done, ...), custom_call_target="tpu_custom_call" | custom-call | flops 1 | bytes 1 | tf_op jit(solution)/shard_map/pallas_call | solution.py:99
  53.1 0.7 collective-permute-start.9
  53.8 1.9 %shard_map.48 = bf16[2,256,256]{2,1,0:T(8,128)(2,1)S(1)} custom-call(s32[8,16]{1,0:T(8,128)S(1)} %copy-done.4, bf16[8,1,256,256]{3,2,1,0:T(8,128)(2,1)S(1)} %copy-done.1, bf16[8,1,256,256]{3,2,1,0:T(8,128)(2,1)S(1)} %collective-permute-done.2.refs_1_, bf16[1,16,256,256]{3,2,1,0:T(8,128)(2,1)S(1)} %copy-done, ...), custom_call_target="tpu_custom_call" | custom-call | flops 1 | bytes 1 | tf_op jit(solution)/shard_map/pallas_call | solution.py:99
  55.6 4.4 %collective-permute-start.8 = (bf16[2,256,256]{2,1,0:T(8,128)(2,1)S(1)}, bf16[2,256,256]{2,1,0:T(8,128)(2,1)S(1)}, u32[]{:S(2)}, u32[]{:S(2)}) collective-permute-start(bf16[2,256,256]{2,1,0:T(8,128)(2,1)S(1)} %shard_map.48), channel_id=1, source_target_pairs={{0,4},{1,5},{2,6},{3,7},{4,0},{5,1},{6,2},{7,3},{8,12},{9,13},{10,... | collective-permute-start | bytes 786440 | tf_op jit(solution)/shard_map/ppermute | solution.py:183
  60.1 0.1 shard_map.51
  60.2 0.0 collective-permute-done.6.refs_4_.refs_6_
  60.2 0.1 collective-permute-start.13
  60.3 0.0 collective-permute-done.7.refs_5_.refs_7_
  60.3 1.3 %collective-permute-start.15 = (bf16[8,1,256,256]{3,2,1,0:T(8,128)(2,1)S(1)}, bf16[8,1,256,256]{3,2,1,0:T(8,128)(2,1)S(1)}, u32[]{:S(2)}, u32[]{:S(2)}) collective-permute-start(bf16[8,1,256,256]{3,2,1,0:T(8,128)(2,1)S(1)} %collective-permute-done.7.refs_5_.refs_7_), channel_id=1, source_target_pairs={{4,0},{5,1},{6,2},{7,3},{8,12},{9,13},{10,14},{11,15},{20,16},{21,... | collective-permute-start | bytes 3145736 | tf_op jit(solution)/shard_map/ppermute | solution.py:183
  61.6 1.9 %shard_map.47 = bf16[2,256,256]{2,1,0:T(8,128)(2,1)S(1)} custom-call(s32[8,16]{1,0:T(8,128)S(1)} %copy-done.4, bf16[8,1,256,256]{3,2,1,0:T(8,128)(2,1)S(1)} %copy-done.1, bf16[8,1,256,256]{3,2,1,0:T(8,128)(2,1)S(1)} %collective-permute-done.2.refs_1_, bf16[1,16,256,256]{3,2,1,0:T(8,128)(2,1)S(1)} %copy-done, ...), custom_call_target="tpu_custom_call" | custom-call | flops 1 | bytes 1 | tf_op jit(solution)/shard_map/pallas_call | solution.py:99
  63.5 2.6 %collective-permute-done.8.refs_4_ = bf16[2,256,256]{2,1,0:T(8,128)(2,1)S(1)} collective-permute-done((bf16[2,256,256]{2,1,0:T(8,128)(2,1)S(1)}, bf16[2,256,256]{2,1,0:T(8,128)(2,1)S(1)}, u32[]{:S(2)}, u32[]{:S(2)}) %collective-permute-start.8) | collective-permute-done | bytes 262176 | tf_op jit(solution)/shard_map/ppermute | solution.py:183
  66.1 1.5 %collective-permute-start.10 = (bf16[2,256,256]{2,1,0:T(8,128)(2,1)S(1)}, bf16[2,256,256]{2,1,0:T(8,128)(2,1)S(1)}, u32[]{:S(2)}, u32[]{:S(2)}) collective-permute-start(bf16[2,256,256]{2,1,0:T(8,128)(2,1)S(1)} %shard_map.47), channel_id=1, source_target_pairs={{0,8},{1,9},{2,10},{3,11},{4,12},{5,13},{6,14},{7,15},{8,0},{9,1},... | collective-permute-start | bytes 786440 | tf_op jit(solution)/shard_map/ppermute | solution.py:183
  67.6 6.9 %collective-permute-done.5.whole.refs_0_ = bf16[8,1,256,256]{3,2,1,0:T(8,128)(2,1)S(1)} collective-permute-done((bf16[8,1,256,256]{3,2,1,0:T(8,128)(2,1)S(1)}, bf16[8,1,256,256]{3,2,1,0:T(8,128)(2,1)S(1)}, u32[]{:S(2)}, u32[]{:S(2)}) %collective-permute-start.5) | collective-permute-done | bytes 1048608 | tf_op jit(solution)/shard_map/ppermute | solution.py:183
  74.4 4.7 %collective-permute-done.10.refs_2_ = bf16[2,256,256]{2,1,0:T(8,128)(2,1)S(1)} collective-permute-done((bf16[2,256,256]{2,1,0:T(8,128)(2,1)S(1)}, bf16[2,256,256]{2,1,0:T(8,128)(2,1)S(1)}, u32[]{:S(2)}, u32[]{:S(2)}) %collective-permute-start.10) | collective-permute-done | bytes 262176 | tf_op jit(solution)/shard_map/ppermute | solution.py:183
  79.1 0.1 shard_map.50
  79.2 0.1 collective-permute-start.11
  79.3 0.5 collective-permute-start.12
  79.8 2.1 %collective-permute-done.12.refs_2_ = bf16[3,1,256,256]{3,2,1,0:T(8,128)(2,1)S(1)} collective-permute-done((bf16[3,1,256,256]{3,2,1,0:T(8,128)(2,1)S(1)}, bf16[3,1,256,256]{3,2,1,0:T(8,128)(2,1)S(1)}, u32[]{:S(2)}, u32[]{:S(2)}) %collective-permute-start.12) | collective-permute-done | bytes 393248 | tf_op jit(solution)/shard_map/ppermute | solution.py:183
  81.9 1.9 %shard_map.54 = bf16[2,256,256]{2,1,0:T(8,128)(2,1)S(1)} custom-call(s32[8,16]{1,0:T(8,128)S(1)} %copy-done.4, bf16[8,1,256,256]{3,2,1,0:T(8,128)(2,1)S(1)} %collective-permute-done.5.whole.refs_0_, bf16[5,1,256,256]{3,2,1,0:T(8,128)(2,1)S(1)} %collective-permute-done.11.refs_1_, bf16[3,1,256,256]{3,2,1,0:T(8,128)(2,1)S(1)} %collective-permute-done.12.refs_2_, ...), custom_call_target="tpu_custom_call" | custom-call | flops 1 | bytes 1 | tf_op jit(solution)/shard_map/pallas_call | solution.py:99
  83.9 0.1 collective-permute-start.16
  83.9 1.9 %shard_map.53 = bf16[2,256,256]{2,1,0:T(8,128)(2,1)S(1)} custom-call(s32[8,16]{1,0:T(8,128)S(1)} %copy-done.4, bf16[8,1,256,256]{3,2,1,0:T(8,128)(2,1)S(1)} %collective-permute-done.5.whole.refs_0_, bf16[5,1,256,256]{3,2,1,0:T(8,128)(2,1)S(1)} %collective-permute-done.11.refs_1_, bf16[3,1,256,256]{3,2,1,0:T(8,128)(2,1)S(1)} %collective-permute-done.12.refs_2_, ...), custom_call_target="tpu_custom_call" | custom-call | flops 1 | bytes 1 | tf_op jit(solution)/shard_map/pallas_call | solution.py:99
  85.8 2.6 %collective-permute-start.17 = (bf16[2,256,256]{2,1,0:T(8,128)(2,1)S(1)}, bf16[2,256,256]{2,1,0:T(8,128)(2,1)S(1)}, u32[]{:S(2)}, u32[]{:S(2)}) collective-permute-start(bf16[2,256,256]{2,1,0:T(8,128)(2,1)S(1)} %shard_map.53), channel_id=1, source_target_pairs={{0,4},{1,5},{2,6},{3,7},{4,0},{5,1},{6,2},{7,3},{8,12},{9,13},{10,... | collective-permute-start | bytes 786440 | tf_op jit(solution)/shard_map/ppermute | solution.py:183
  88.4 1.9 %shard_map.52 = (bf16[2,256,256]{2,1,0:T(8,128)(2,1)S(1)}, bf16[512,2048]{1,0:T(8,128)(2,1)S(1)}) custom-call(s32[8,16]{1,0:T(8,128)S(1)} %copy-done.4, bf16[8,1,256,256]{3,2,1,0:T(8,128)(2,1)S(1)} %collective-permute-done.5.whole.refs_0_, bf16[5,1,256,256]{3,2,1,0:T(8,128)(2,1)S(1)} %collective-permute-done.11.refs_1_, ...), custom_call_target="tpu_custom_call" | custom-call | flops 1 | bytes 1 | tf_op jit(solution)/shard_map/pallas_call | solution.py:99
  90.3 0.7 collective-permute-start.19
  91.0 8.8 %collective-permute-done.15.refs_2_ = bf16[8,1,256,256]{3,2,1,0:T(8,128)(2,1)S(1)} collective-permute-done((bf16[8,1,256,256]{3,2,1,0:T(8,128)(2,1)S(1)}, bf16[8,1,256,256]{3,2,1,0:T(8,128)(2,1)S(1)}, u32[]{:S(2)}, u32[]{:S(2)}) %collective-permute-start.15) | collective-permute-done | bytes 1048608 | tf_op jit(solution)/shard_map/ppermute | solution.py:183
  99.8 1.3 %shard_map.55 = bf16[4,256,256]{2,1,0:T(8,128)(2,1)S(1)} custom-call(bf16[512,2048]{1,0:T(8,128)(2,1)S(1)} %get-tuple-element.41.refs_0_, bf16[512,2048]{1,0:T(8,128)(2,1)S(1)} %get-tuple-element.42.refs_1_, bf16[8,1,256,256]{3,2,1,0:T(8,128)(2,1)S(1)} %collective-permute-done.15.refs_2_), custom_call_target="tpu_custom_call" | custom-call | flops 10000000000 | bytes 1 | tf_op jit(solution)/shard_map/pallas_call | solution.py:78
  101.1 4.0 %collective-permute-start.18 = (bf16[4,256,256]{2,1,0:T(8,128)(2,1)S(1)}, bf16[4,256,256]{2,1,0:T(8,128)(2,1)S(1)}, u32[]{:S(2)}, u32[]{:S(2)}) collective-permute-start(bf16[4,256,256]{2,1,0:T(8,128)(2,1)S(1)} %shard_map.55), channel_id=1, source_target_pairs={{0,12},{1,13},{2,14},{3,15},{12,0},{13,1},{14,2},{15,3},{16,28},{1... | collective-permute-start | bytes 1572872 | tf_op jit(solution)/shard_map/ppermute | solution.py:183
  105.1 1.9 %shard_map.56.refs_1_ = bf16[2,256,256]{2,1,0:T(8,128)(2,1)S(1)} custom-call(s32[8,16]{1,0:T(8,128)S(1)} %copy-done.4, bf16[8,1,256,256]{3,2,1,0:T(8,128)(2,1)S(1)} %collective-permute-done.5.whole.refs_0_, bf16[5,1,256,256]{3,2,1,0:T(8,128)(2,1)S(1)} %collective-permute-done.11.refs_1_, bf16[3,1,256,256]{3,2,1,0:T(8,128)(2,1)S(1)} %collective-permute-done.12.refs_2_, ...), custom_call_target="tpu_custom_call" | custom-call | flops 1 | bytes 1 | tf_op jit(solution)/shard_map/pallas_call | solution.py:99
  107.0 1.3 %shard_map.57.refs_0_ = bf16[16,256,256]{2,1,0:T(8,128)(2,1)} custom-call(bf16[2,256,256]{2,1,0:T(8,128)(2,1)S(1)} %shard_map.46.refs_0_, bf16[2,256,256]{2,1,0:T(8,128)(2,1)S(1)} %shard_map.56.refs_1_, bf16[2,256,256]{2,1,0:T(8,128)(2,1)S(1)} %collective-permute-done.10.refs_2_, bf16[2,256,256]{2,1,0:T(8,128)(2,1)S(1)} %collective-permute-done.16.refs_3_, ...), custom_call_target="tpu_custom_call" | custom-call | flops 10000000000 | bytes 1 | tf_op jit(solution)/shard_map/pallas_call | solution.py:170
  108.3 9.7 %collective-permute-done.18.refs_1_ = bf16[4,256,256]{2,1,0:T(8,128)(2,1)S(1)} collective-permute-done((bf16[4,256,256]{2,1,0:T(8,128)(2,1)S(1)}, bf16[4,256,256]{2,1,0:T(8,128)(2,1)S(1)}, u32[]{:S(2)}, u32[]{:S(2)}) %collective-permute-start.18) | collective-permute-done | bytes 524320 | tf_op jit(solution)/shard_map/ppermute | solution.py:183
  118.0 0.9 shard_map.58
  (15 shorter events, 0.0 us)
Async XLA Ops:
  0.0 6.0 %collective-permute-start.3 = (bf16[1,16,256,256]{3,2,1,0:T(8,128)(2,1)}, bf16[1,16,256,256]{3,2,1,0:T(8,128)(2,1)S(1)}, u32[]{:S(2)}, u32[]{:S(2)}) collective-permute-start(bf16[1,16,256,256]{3,2,1,0:T(8,128)(2,1)} %refs_2_.7), channel_id=1, source_target_pairs={{0,1},{1,0},{2,3},{3,2},{4,5},{5,4},{6,7},{7,6},{8,9},{9,8},{10,11... | collective-permute-start | bytes 6291464 | tf_op jit(solution)/shard_map/ppermute | solution.py:183
  0.5 49.0 %collective-permute-start.4 = (bf16[1,16,256,256]{3,2,1,0:T(8,128)(2,1)}, bf16[1,16,256,256]{3,2,1,0:T(8,128)(2,1)S(1)}, u32[]{:S(2)}, u32[]{:S(2)}) collective-permute-start(bf16[1,16,256,256]{3,2,1,0:T(8,128)(2,1)} %refs_2_.7), channel_id=1, source_target_pairs={{0,2},{1,3},{2,0},{3,1},{4,6},{5,7},{6,4},{7,5},{8,10},{9,11},{10,... | collective-permute-start | bytes 6291464 | tf_op jit(solution)/shard_map/ppermute | solution.py:183
  2.9 3.0 %collective-permute-start.2 = (bf16[8,1,256,256]{3,2,1,0:T(8,128)(2,1)}, bf16[8,1,256,256]{3,2,1,0:T(8,128)(2,1)S(1)}, u32[]{:S(2)}, u32[]{:S(2)}) collective-permute-start(bf16[8,1,256,256]{3,2,1,0:T(8,128)(2,1)} %refs_0_.7), channel_id=1, source_target_pairs={{0,1},{1,0},{2,3},{3,2},{4,5},{5,4},{6,7},{7,6},{8,9},{9,8},{10,11... | collective-permute-start | bytes 3145736 | tf_op jit(solution)/shard_map/ppermute | solution.py:183
  3.2 25.6 %collective-permute-start = (bf16[8,1,256,256]{3,2,1,0:T(8,128)(2,1)}, bf16[8,1,256,256]{3,2,1,0:T(8,128)(2,1)S(1)}, u32[]{:S(2)}, u32[]{:S(2)}) collective-permute-start(bf16[8,1,256,256]{3,2,1,0:T(8,128)(2,1)} %refs_6_), channel_id=1, source_target_pairs={{0,4},{1,5},{2,6},{3,7},{4,0},{5,1},{6,2},{7,3},{8,12},{9,13},{10,... | collective-permute-start | bytes 3145736 | tf_op jit(solution)/shard_map/ppermute | solution.py:183
  4.7 24.0 %collective-permute-start.1 = (bf16[8,1,256,256]{3,2,1,0:T(8,128)(2,1)}, bf16[8,1,256,256]{3,2,1,0:T(8,128)(2,1)S(1)}, u32[]{:S(2)}, u32[]{:S(2)}) collective-permute-start(bf16[8,1,256,256]{3,2,1,0:T(8,128)(2,1)} %refs_6_), channel_id=1, source_target_pairs={{4,8},{5,9},{6,10},{7,11},{8,4},{9,5},{10,6},{11,7},{20,24},{21,25... | collective-permute-start | bytes 3145736 | tf_op jit(solution)/shard_map/ppermute | solution.py:183
  6.0 1.6 %copy-start = (bf16[1,16,256,256]{3,2,1,0:T(8,128)(2,1)S(1)}, bf16[1,16,256,256]{3,2,1,0:T(8,128)(2,1)}, u32[]{:S(2)}) copy-start(bf16[1,16,256,256]{3,2,1,0:T(8,128)(2,1)} %refs_2_.7) | copy-start | bytes 6291460
  7.5 1.2 %copy-start.1 = (bf16[8,1,256,256]{3,2,1,0:T(8,128)(2,1)S(1)}, bf16[8,1,256,256]{3,2,1,0:T(8,128)(2,1)}, u32[]{:S(2)}) copy-start(bf16[8,1,256,256]{3,2,1,0:T(8,128)(2,1)} %refs_0_.7) | copy-start | bytes 3145732
  8.8 1.2 %copy-start.2 = (bf16[8,1,256,256]{3,2,1,0:T(8,128)(2,1)S(1)}, bf16[8,1,256,256]{3,2,1,0:T(8,128)(2,1)}, u32[]{:S(2)}) copy-start(bf16[8,1,256,256]{3,2,1,0:T(8,128)(2,1)} %refs_6_) | copy-start | bytes 3145732
  10.0 0.7 copy-start.4
  28.7 31.5 %collective-permute-start.6 = (bf16[8,1,256,256]{3,2,1,0:T(8,128)(2,1)S(1)}, bf16[8,1,256,256]{3,2,1,0:T(8,128)(2,1)S(1)}, u32[]{:S(2)}, u32[]{:S(2)}) collective-permute-start(bf16[8,1,256,256]{3,2,1,0:T(8,128)(2,1)S(1)} %collective-permute-done.1.refs_4_.refs_6_), channel_id=1, source_target_pairs={{4,0},{5,1},{6,2},{7,3},{8,12},{9,13},{10,14},{11,15},{20,16},{21,... | collective-permute-start | bytes 3145736 | tf_op jit(solution)/shard_map/ppermute | solution.py:183
  30.0 30.3 %collective-permute-start.7 = (bf16[8,1,256,256]{3,2,1,0:T(8,128)(2,1)S(1)}, bf16[8,1,256,256]{3,2,1,0:T(8,128)(2,1)S(1)}, u32[]{:S(2)}, u32[]{:S(2)}) collective-permute-start(bf16[8,1,256,256]{3,2,1,0:T(8,128)(2,1)S(1)} %collective-permute-done.refs_4_.refs_6_), channel_id=1, source_target_pairs={{4,8},{5,9},{6,10},{7,11},{8,4},{9,5},{10,6},{11,7},{20,24},{21,25... | collective-permute-start | bytes 3145736 | tf_op jit(solution)/shard_map/ppermute | solution.py:183
  49.5 25.0 %collective-permute-start.5 = (bf16[8,1,256,256]{3,2,1,0:T(8,128)(2,1)S(1)}, bf16[8,1,256,256]{3,2,1,0:T(8,128)(2,1)S(1)}, u32[]{:S(2)}, u32[]{:S(2)}) collective-permute-start(bf16[8,1,256,256]{3,2,1,0:T(8,128)(2,1)S(1)} %copy-done.1), channel_id=1, source_target_pairs={{0,2},{1,3},{2,0},{3,1},{4,6},{5,7},{6,4},{7,5},{8,10},{9,11},{10,... | collective-permute-start | bytes 3145736 | tf_op jit(solution)/shard_map/ppermute | solution.py:183
  53.1 10.5 %collective-permute-start.9 = (bf16[2,256,256]{2,1,0:T(8,128)(2,1)S(1)}, bf16[2,256,256]{2,1,0:T(8,128)(2,1)S(1)}, u32[]{:S(2)}, u32[]{:S(2)}) collective-permute-start(bf16[2,256,256]{2,1,0:T(8,128)(2,1)S(1)} %get-tuple-element.33), channel_id=1, source_target_pairs={{4,8},{5,9},{6,10},{7,11},{8,4},{9,5},{10,6},{11,7},{20,24},{21,25... | collective-permute-start | bytes 786440 | tf_op jit(solution)/shard_map/ppermute | solution.py:183
  55.6 10.5 %collective-permute-start.8 = (bf16[2,256,256]{2,1,0:T(8,128)(2,1)S(1)}, bf16[2,256,256]{2,1,0:T(8,128)(2,1)S(1)}, u32[]{:S(2)}, u32[]{:S(2)}) collective-permute-start(bf16[2,256,256]{2,1,0:T(8,128)(2,1)S(1)} %shard_map.48), channel_id=1, source_target_pairs={{0,4},{1,5},{2,6},{3,7},{4,0},{5,1},{6,2},{7,3},{8,12},{9,13},{10,... | collective-permute-start | bytes 786440 | tf_op jit(solution)/shard_map/ppermute | solution.py:183
  60.2 19.6 %collective-permute-start.13 = (bf16[1,9,256,256]{3,2,1,0:T(8,128)(2,1)S(1)}, bf16[1,9,256,256]{3,2,1,0:T(8,128)(2,1)S(1)}, u32[]{:S(2)}, u32[]{:S(2)}) collective-permute-start(bf16[1,9,256,256]{3,2,1,0:T(8,128)(2,1)S(1)} %get-tuple-element.39), channel_id=1, source_target_pairs={{0,1},{1,0},{2,3},{3,2},{4,5},{5,4},{6,7},{7,6},{8,9},{9,8},{10,11... | collective-permute-start | bytes 3538952 | tf_op jit(solution)/shard_map/ppermute | solution.py:183
  60.3 39.5 %collective-permute-start.15 = (bf16[8,1,256,256]{3,2,1,0:T(8,128)(2,1)S(1)}, bf16[8,1,256,256]{3,2,1,0:T(8,128)(2,1)S(1)}, u32[]{:S(2)}, u32[]{:S(2)}) collective-permute-start(bf16[8,1,256,256]{3,2,1,0:T(8,128)(2,1)S(1)} %collective-permute-done.7.refs_5_.refs_7_), channel_id=1, source_target_pairs={{4,0},{5,1},{6,2},{7,3},{8,12},{9,13},{10,14},{11,15},{20,16},{21,... | collective-permute-start | bytes 3145736 | tf_op jit(solution)/shard_map/ppermute | solution.py:183
  66.1 13.0 %collective-permute-start.10 = (bf16[2,256,256]{2,1,0:T(8,128)(2,1)S(1)}, bf16[2,256,256]{2,1,0:T(8,128)(2,1)S(1)}, u32[]{:S(2)}, u32[]{:S(2)}) collective-permute-start(bf16[2,256,256]{2,1,0:T(8,128)(2,1)S(1)} %shard_map.47), channel_id=1, source_target_pairs={{0,8},{1,9},{2,10},{3,11},{4,12},{5,13},{6,14},{7,15},{8,0},{9,1},... | collective-permute-start | bytes 786440 | tf_op jit(solution)/shard_map/ppermute | solution.py:183
  67.6 12.2 %collective-permute-start.14 = (bf16[1,7,256,256]{3,2,1,0:T(8,128)(2,1)S(1)}, bf16[1,7,256,256]{3,2,1,0:T(8,128)(2,1)S(1)}, u32[]{:S(2)}, u32[]{:S(2)}) collective-permute-start(bf16[1,7,256,256]{3,2,1,0:T(8,128)(2,1)S(1)} %get-tuple-element.40), channel_id=1, source_target_pairs={{0,1},{1,0},{2,3},{3,2},{4,5},{5,4},{6,7},{7,6},{8,9},{9,8},{10,11... | collective-permute-start | bytes 2752520 | tf_op jit(solution)/shard_map/ppermute | solution.py:183
  79.2 2.7 %collective-permute-start.11 = (bf16[5,1,256,256]{3,2,1,0:T(8,128)(2,1)S(1)}, bf16[5,1,256,256]{3,2,1,0:T(8,128)(2,1)S(1)}, u32[]{:S(2)}, u32[]{:S(2)}) collective-permute-start(bf16[5,1,256,256]{3,2,1,0:T(8,128)(2,1)S(1)} %get-tuple-element.36), channel_id=1, source_target_pairs={{0,1},{1,0},{2,3},{3,2},{4,5},{5,4},{6,7},{7,6},{8,9},{9,8},{10,11... | collective-permute-start | bytes 1966088 | tf_op jit(solution)/shard_map/ppermute | solution.py:183
  79.3 2.6 %collective-permute-start.12 = (bf16[3,1,256,256]{3,2,1,0:T(8,128)(2,1)S(1)}, bf16[3,1,256,256]{3,2,1,0:T(8,128)(2,1)S(1)}, u32[]{:S(2)}, u32[]{:S(2)}) collective-permute-start(bf16[3,1,256,256]{3,2,1,0:T(8,128)(2,1)S(1)} %get-tuple-element.37), channel_id=1, source_target_pairs={{0,1},{1,0},{2,3},{3,2},{4,5},{5,4},{6,7},{7,6},{8,9},{9,8},{10,11... | collective-permute-start | bytes 1179656 | tf_op jit(solution)/shard_map/ppermute | solution.py:183
  83.9 23.1 %collective-permute-start.16 = (bf16[2,256,256]{2,1,0:T(8,128)(2,1)S(1)}, bf16[2,256,256]{2,1,0:T(8,128)(2,1)S(1)}, u32[]{:S(2)}, u32[]{:S(2)}) collective-permute-start(bf16[2,256,256]{2,1,0:T(8,128)(2,1)S(1)} %shard_map.54), channel_id=1, source_target_pairs={{0,8},{1,9},{2,10},{3,11},{4,12},{5,13},{6,14},{7,15},{8,0},{9,1},... | collective-permute-start | bytes 786440 | tf_op jit(solution)/shard_map/ppermute | solution.py:183
  85.8 21.2 %collective-permute-start.17 = (bf16[2,256,256]{2,1,0:T(8,128)(2,1)S(1)}, bf16[2,256,256]{2,1,0:T(8,128)(2,1)S(1)}, u32[]{:S(2)}, u32[]{:S(2)}) collective-permute-start(bf16[2,256,256]{2,1,0:T(8,128)(2,1)S(1)} %shard_map.53), channel_id=1, source_target_pairs={{0,4},{1,5},{2,6},{3,7},{4,0},{5,1},{6,2},{7,3},{8,12},{9,13},{10,... | collective-permute-start | bytes 786440 | tf_op jit(solution)/shard_map/ppermute | solution.py:183
  90.3 18.0 %collective-permute-start.19 = (bf16[2,256,256]{2,1,0:T(8,128)(2,1)S(1)}, bf16[2,256,256]{2,1,0:T(8,128)(2,1)S(1)}, u32[]{:S(2)}, u32[]{:S(2)}) collective-permute-start(bf16[2,256,256]{2,1,0:T(8,128)(2,1)S(1)} %get-tuple-element.43), channel_id=1, source_target_pairs={{4,8},{5,9},{6,10},{7,11},{8,4},{9,5},{10,6},{11,7},{20,24},{21,25... | collective-permute-start | bytes 786440 | tf_op jit(solution)/shard_map/ppermute | solution.py:183
  99.8 5.3 %copy-start.3 = (bf16[8,1,256,256]{3,2,1,0:T(8,128)(2,1)S(1)}, bf16[8,1,256,256]{3,2,1,0:T(8,128)(2,1)}, u32[]{:S(2)}) copy-start(bf16[8,1,256,256]{3,2,1,0:T(8,128)(2,1)} %refs_6_) | copy-start | bytes 3145732
  101.1 16.9 %collective-permute-start.18 = (bf16[4,256,256]{2,1,0:T(8,128)(2,1)S(1)}, bf16[4,256,256]{2,1,0:T(8,128)(2,1)S(1)}, u32[]{:S(2)}, u32[]{:S(2)}) collective-permute-start(bf16[4,256,256]{2,1,0:T(8,128)(2,1)S(1)} %shard_map.55), channel_id=1, source_target_pairs={{0,12},{1,13},{2,14},{3,15},{12,0},{13,1},{14,2},{15,3},{16,28},{1... | collective-permute-start | bytes 1572872 | tf_op jit(solution)/shard_map/ppermute | solution.py:183

commit v16 on v15

--- a/solution.py
+++ b/solution.py
@@ -202,13 +202,13 @@
     far_in = exchange(near, 12, inner)
     far_out = exchange(middle, 4, inner)
 
-    x_psi, left_next = lax.optimization_barrier((x_psi, left_env))
+    own_middle, own_mid = products(3, *own, (middle,), keep_mid=True)
+    own_1 = products(1, *own, (near,))
+    x_psi, left_next, own_1, own_middle = lax.optimization_barrier((x_psi, left_env, own_1, own_middle))
     x_left = exchange(left_next, 2, every)
     across_psi = [exchange(part, 1, every) for part in split(x_psi, 1, 9 * x_psi.shape[1] // 16)]
-    own_middle, own_mid = products(3, *own, (middle,), keep_mid=True)
+    sent_1 = exchange(own_1, 4, every)
     sent_own_middle = exchange(own_middle, 12, inner)
-    own_1 = products(1, *own, (near,))
-    sent_1 = exchange(own_1, 4, every)
 
     far_out, far_in = lax.optimization_barrier((far_out, far_in))
     third = exchange(far_in, 4, inner)

time: 119 us -> 120 us (level)
  transfers between devices with their start and end apart: 20 -> 20, of which waited for: 9 -> 10; matrix products, arithmetic and copies ran while one was open for 0% -> 0% of each run, Pallas kernels for 15% -> 15%
where the time goes in v16:
time: 120 us
  waiting for transfers between devices  70.8 us (59%)
  starting transfers between devices  25.5 us (21%)
  Pallas kernels  18.8 us (16%)
  local copies, waits for them, and re-layouts  4.73 us (4%)
    ppermute x20, waiting for transfers between devices, exchange(): return lax.ppermute(array, 'sec', [(s, s ^ bits) for s in members])  70.8 us
    ppermute x20, starting transfers between devices, exchange(): return lax.ppermute(array, 'sec', [(s, s ^ bits) for s in members])  25.5 us
    pallas_call x8, Pallas kernels, slot(): pl.pallas_call(functools.partial(slot_kernel, step, parts, len(rights)),...  15.1 us
    unnamed x10, local copies, waits for them, and re-layouts  4.73 us
  transfers between devices with their start and end apart: 20, of which 10 were waited for; matrix products, arithmetic and copies ran while one was open for 0% of the time, Pallas kernels for 15%

profile of v16, /device:TPU:0, one launch (start us, length us, event | category | flops | bytes accessed | tf_op | source)
XLA Modules:
  0.0 119.9 jit_solution(17152882737183753416)
XLA Ops:
  0.0 0.5 collective-permute-start.3
  0.5 2.5 %collective-permute-start.4 = (bf16[1,16,256,256]{3,2,1,0:T(8,128)(2,1)}, bf16[1,16,256,256]{3,2,1,0:T(8,128)(2,1)S(1)}, u32[]{:S(2)}, u32[]{:S(2)}) collective-permute-start(bf16[1,16,256,256]{3,2,1,0:T(8,128)(2,1)} %refs_2_.7), channel_id=1, source_target_pairs={{0,2},{1,3},{2,0},{3,1},{4,6},{5,7},{6,4},{7,5},{8,10},{9,11},{10,... | collective-permute-start | bytes 6291464 | tf_op jit(solution)/shard_map/ppermute | solution.py:183
  2.9 0.2 collective-permute-start.2
  3.2 1.6 %collective-permute-start = (bf16[8,1,256,256]{3,2,1,0:T(8,128)(2,1)}, bf16[8,1,256,256]{3,2,1,0:T(8,128)(2,1)S(1)}, u32[]{:S(2)}, u32[]{:S(2)}) collective-permute-start(bf16[8,1,256,256]{3,2,1,0:T(8,128)(2,1)} %refs_6_), channel_id=1, source_target_pairs={{0,4},{1,5},{2,6},{3,7},{4,0},{5,1},{6,2},{7,3},{8,12},{9,13},{10,... | collective-permute-start | bytes 3145736 | tf_op jit(solution)/shard_map/ppermute | solution.py:183
  4.7 0.7 collective-permute-start.1
  5.5 0.5 collective-permute-done.2.refs_1_
  6.0 1.6 %copy-done = bf16[1,16,256,256]{3,2,1,0:T(8,128)(2,1)S(1)} copy-done((bf16[1,16,256,256]{3,2,1,0:T(8,128)(2,1)S(1)}, bf16[1,16,256,256]{3,2,1,0:T(8,128)(2,1)}, u32[]{:S(2)}) %copy-start) | copy-done | bytes 2097176
  7.5 1.2 %copy-done.1 = bf16[8,1,256,256]{3,2,1,0:T(8,128)(2,1)S(1)} copy-done((bf16[8,1,256,256]{3,2,1,0:T(8,128)(2,1)S(1)}, bf16[8,1,256,256]{3,2,1,0:T(8,128)(2,1)}, u32[]{:S(2)}) %copy-start.1) | copy-done | bytes 1048600
  8.8 1.2 %copy-done.2 = bf16[8,1,256,256]{3,2,1,0:T(8,128)(2,1)S(1)} copy-done((bf16[8,1,256,256]{3,2,1,0:T(8,128)(2,1)S(1)}, bf16[8,1,256,256]{3,2,1,0:T(8,128)(2,1)}, u32[]{:S(2)}) %copy-start.2) | copy-done | bytes 1048600
  10.0 0.7 copy-done.4
  10.7 1.9 %shard_map.46.refs_0_ = bf16[2,256,256]{2,1,0:T(8,128)(2,1)S(1)} custom-call(s32[8,16]{1,0:T(8,128)S(1)} %copy-done.4, bf16[8,1,256,256]{3,2,1,0:T(8,128)(2,1)S(1)} %copy-done.1, bf16[8,1,256,256]{3,2,1,0:T(8,128)(2,1)S(1)} %collective-permute-done.2.refs_1_, bf16[1,16,256,256]{3,2,1,0:T(8,128)(2,1)S(1)} %copy-done, ...), custom_call_target="tpu_custom_call" | custom-call | flops 1 | bytes 1 | tf_op jit(solution)/shard_map/pallas_call | solution.py:99
  12.6 16.2 %collective-permute-done.refs_4_.refs_6_ = bf16[8,1,256,256]{3,2,1,0:T(8,128)(2,1)S(1)} collective-permute-done((bf16[8,1,256,256]{3,2,1,0:T(8,128)(2,1)}, bf16[8,1,256,256]{3,2,1,0:T(8,128)(2,1)S(1)}, u32[]{:S(2)}, u32[]{:S(2)}) %collective-permute-start) | collective-permute-done | bytes 1048608 | tf_op jit(solution)/shard_map/ppermute | solution.py:183
  28.7 0.0 collective-permute-done.1.refs_4_.refs_6_
  28.7 1.3 %collective-permute-start.6 = (bf16[8,1,256,256]{3,2,1,0:T(8,128)(2,1)S(1)}, bf16[8,1,256,256]{3,2,1,0:T(8,128)(2,1)S(1)}, u32[]{:S(2)}, u32[]{:S(2)}) collective-permute-start(bf16[8,1,256,256]{3,2,1,0:T(8,128)(2,1)S(1)} %collective-permute-done.1.refs_4_.refs_6_), channel_id=1, source_target_pairs={{4,0},{5,1},{6,2},{7,3},{8,12},{9,13},{10,14},{11,15},{20,16},{21,... | collective-permute-start | bytes 3145736 | tf_op jit(solution)/shard_map/ppermute | solution.py:183
  30.0 0.7 collective-permute-start.7
  30.8 1.9 %shard_map.48 = (bf16[2,256,256]{2,1,0:T(8,128)(2,1)S(1)}, bf16[512,2048]{1,0:T(8,128)(2,1)S(1)}) custom-call(s32[8,16]{1,0:T(8,128)S(1)} %copy-done.4, bf16[8,1,256,256]{3,2,1,0:T(8,128)(2,1)S(1)} %copy-done.1, bf16[8,1,256,256]{3,2,1,0:T(8,128)(2,1)S(1)} %collective-permute-done.2.refs_1_, bf16[1,16,256,256]{3,2,1,0:T(8,128)(2,1)S(1)} %copy-done, ...), custom_call_target="tpu_custom_call" | custom-call | flops 1 | bytes 1 | tf_op jit(solution)/shard_map/pallas_call | solution.py:99
  32.6 1.9 %shard_map.47 = bf16[2,256,256]{2,1,0:T(8,128)(2,1)S(1)} custom-call(s32[8,16]{1,0:T(8,128)S(1)} %copy-done.4, bf16[8,1,256,256]{3,2,1,0:T(8,128)(2,1)S(1)} %copy-done.1, bf16[8,1,256,256]{3,2,1,0:T(8,128)(2,1)S(1)} %collective-permute-done.2.refs_1_, bf16[1,16,256,256]{3,2,1,0:T(8,128)(2,1)S(1)} %copy-done, ...), custom_call_target="tpu_custom_call" | custom-call | flops 1 | bytes 1 | tf_op jit(solution)/shard_map/pallas_call | solution.py:99
  34.5 14.9 %collective-permute-done.4.whole.refs_3_ = bf16[1,16,256,256]{3,2,1,0:T(8,128)(2,1)S(1)} collective-permute-done((bf16[1,16,256,256]{3,2,1,0:T(8,128)(2,1)}, bf16[1,16,256,256]{3,2,1,0:T(8,128)(2,1)S(1)}, u32[]{:S(2)}, u32[]{:S(2)}) %collective-permute-start.4) | collective-permute-done | bytes 2097184 | tf_op jit(solution)/shard_map/ppermute | solution.py:183
  49.5 1.7 %collective-permute-start.5 = (bf16[8,1,256,256]{3,2,1,0:T(8,128)(2,1)S(1)}, bf16[8,1,256,256]{3,2,1,0:T(8,128)(2,1)S(1)}, u32[]{:S(2)}, u32[]{:S(2)}) collective-permute-start(bf16[8,1,256,256]{3,2,1,0:T(8,128)(2,1)S(1)} %copy-done.1), channel_id=1, source_target_pairs={{0,2},{1,3},{2,0},{3,1},{4,6},{5,7},{6,4},{7,5},{8,10},{9,11},{10,... | collective-permute-start | bytes 3145736 | tf_op jit(solution)/shard_map/ppermute | solution.py:183
  51.2 1.6 %collective-permute-start.8 = (bf16[2,256,256]{2,1,0:T(8,128)(2,1)S(1)}, bf16[2,256,256]{2,1,0:T(8,128)(2,1)S(1)}, u32[]{:S(2)}, u32[]{:S(2)}) collective-permute-start(bf16[2,256,256]{2,1,0:T(8,128)(2,1)S(1)} %shard_map.47), channel_id=1, source_target_pairs={{0,4},{1,5},{2,6},{3,7},{4,0},{5,1},{6,2},{7,3},{8,12},{9,13},{10,... | collective-permute-start | bytes 786440 | tf_op jit(solution)/shard_map/ppermute | solution.py:183
  52.8 0.7 collective-permute-start.9
  53.4 0.1 shard_map.51
  53.6 5.0 %collective-permute-done.6.refs_4_.refs_6_ = bf16[8,1,256,256]{3,2,1,0:T(8,128)(2,1)S(1)} collective-permute-done((bf16[8,1,256,256]{3,2,1,0:T(8,128)(2,1)S(1)}, bf16[8,1,256,256]{3,2,1,0:T(8,128)(2,1)S(1)}, u32[]{:S(2)}, u32[]{:S(2)}) %collective-permute-start.6) | collective-permute-done | bytes 1048608 | tf_op jit(solution)/shard_map/ppermute | solution.py:183
  58.6 1.3 %collective-permute-start.15 = (bf16[8,1,256,256]{3,2,1,0:T(8,128)(2,1)S(1)}, bf16[8,1,256,256]{3,2,1,0:T(8,128)(2,1)S(1)}, u32[]{:S(2)}, u32[]{:S(2)}) collective-permute-start(bf16[8,1,256,256]{3,2,1,0:T(8,128)(2,1)S(1)} %collective-permute-done.7.refs_5_.refs_7_), channel_id=1, source_target_pairs={{4,0},{5,1},{6,2},{7,3},{8,12},{9,13},{10,14},{11,15},{20,16},{21,... | collective-permute-start | bytes 3145736 | tf_op jit(solution)/shard_map/ppermute | solution.py:183
  59.9 1.9 %shard_map.49 = bf16[2,256,256]{2,1,0:T(8,128)(2,1)S(1)} custom-call(s32[8,16]{1,0:T(8,128)S(1)} %copy-done.4, bf16[8,1,256,256]{3,2,1,0:T(8,128)(2,1)S(1)} %copy-done.1, bf16[8,1,256,256]{3,2,1,0:T(8,128)(2,1)S(1)} %collective-permute-done.2.refs_1_, bf16[1,16,256,256]{3,2,1,0:T(8,128)(2,1)S(1)} %copy-done, ...), custom_call_target="tpu_custom_call" | custom-call | flops 1 | bytes 1 | tf_op jit(solution)/shard_map/pallas_call | solution.py:99
  61.8 1.2 collective-permute-done.8.refs_4_
  63.0 0.0 collective-permute-done.9.refs_2_
  63.0 4.6 %collective-permute-start.10 = (bf16[2,256,256]{2,1,0:T(8,128)(2,1)S(1)}, bf16[2,256,256]{2,1,0:T(8,128)(2,1)S(1)}, u32[]{:S(2)}, u32[]{:S(2)}) collective-permute-start(bf16[2,256,256]{2,1,0:T(8,128)(2,1)S(1)} %shard_map.49), channel_id=1, source_target_pairs={{0,8},{1,9},{2,10},{3,11},{4,12},{5,13},{6,14},{7,15},{8,0},{9,1},... | collective-permute-start | bytes 786440 | tf_op jit(solution)/shard_map/ppermute | solution.py:183
  67.6 0.0 collective-permute-start.14
  67.6 6.9 %collective-permute-done.5.whole.refs_0_ = bf16[8,1,256,256]{3,2,1,0:T(8,128)(2,1)S(1)} collective-permute-done((bf16[8,1,256,256]{3,2,1,0:T(8,128)(2,1)S(1)}, bf16[8,1,256,256]{3,2,1,0:T(8,128)(2,1)S(1)}, u32[]{:S(2)}, u32[]{:S(2)}) %collective-permute-start.5) | collective-permute-done | bytes 1048608 | tf_op jit(solution)/shard_map/ppermute | solution.py:183
  74.4 3.9 %collective-permute-done.10.refs_2_ = bf16[2,256,256]{2,1,0:T(8,128)(2,1)S(1)} collective-permute-done((bf16[2,256,256]{2,1,0:T(8,128)(2,1)S(1)}, bf16[2,256,256]{2,1,0:T(8,128)(2,1)S(1)}, u32[]{:S(2)}, u32[]{:S(2)}) %collective-permute-start.10) | collective-permute-done | bytes 262176 | tf_op jit(solution)/shard_map/ppermute | solution.py:183
  78.3 0.1 shard_map.50
  78.4 0.1 collective-permute-start.11
  78.5 0.5 collective-permute-start.12
  79.0 2.1 %collective-permute-done.12.refs_2_ = bf16[3,1,256,256]{3,2,1,0:T(8,128)(2,1)S(1)} collective-permute-done((bf16[3,1,256,256]{3,2,1,0:T(8,128)(2,1)S(1)}, bf16[3,1,256,256]{3,2,1,0:T(8,128)(2,1)S(1)}, u32[]{:S(2)}, u32[]{:S(2)}) %collective-permute-start.12) | collective-permute-done | bytes 393248 | tf_op jit(solution)/shard_map/ppermute | solution.py:183
  81.1 1.9 %shard_map.54 = bf16[2,256,256]{2,1,0:T(8,128)(2,1)S(1)} custom-call(s32[8,16]{1,0:T(8,128)S(1)} %copy-done.4, bf16[8,1,256,256]{3,2,1,0:T(8,128)(2,1)S(1)} %collective-permute-done.5.whole.refs_0_, bf16[5,1,256,256]{3,2,1,0:T(8,128)(2,1)S(1)} %collective-permute-done.11.refs_1_, bf16[3,1,256,256]{3,2,1,0:T(8,128)(2,1)S(1)} %collective-permute-done.12.refs_2_, ...), custom_call_target="tpu_custom_call" | custom-call | flops 1 | bytes 1 | tf_op jit(solution)/shard_map/pallas_call | solution.py:99
  83.0 0.1 collective-permute-start.16
  83.1 1.9 %shard_map.53 = bf16[2,256,256]{2,1,0:T(8,128)(2,1)S(1)} custom-call(s32[8,16]{1,0:T(8,128)S(1)} %copy-done.4, bf16[8,1,256,256]{3,2,1,0:T(8,128)(2,1)S(1)} %collective-permute-done.5.whole.refs_0_, bf16[5,1,256,256]{3,2,1,0:T(8,128)(2,1)S(1)} %collective-permute-done.11.refs_1_, bf16[3,1,256,256]{3,2,1,0:T(8,128)(2,1)S(1)} %collective-permute-done.12.refs_2_, ...), custom_call_target="tpu_custom_call" | custom-call | flops 1 | bytes 1 | tf_op jit(solution)/shard_map/pallas_call | solution.py:99
  85.0 2.3 %collective-permute-start.17 = (bf16[2,256,256]{2,1,0:T(8,128)(2,1)S(1)}, bf16[2,256,256]{2,1,0:T(8,128)(2,1)S(1)}, u32[]{:S(2)}, u32[]{:S(2)}) collective-permute-start(bf16[2,256,256]{2,1,0:T(8,128)(2,1)S(1)} %shard_map.53), channel_id=1, source_target_pairs={{0,4},{1,5},{2,6},{3,7},{4,0},{5,1},{6,2},{7,3},{8,12},{9,13},{10,... | collective-permute-start | bytes 786440 | tf_op jit(solution)/shard_map/ppermute | solution.py:183
  87.3 1.9 %shard_map.52 = (bf16[2,256,256]{2,1,0:T(8,128)(2,1)S(1)}, bf16[512,2048]{1,0:T(8,128)(2,1)S(1)}) custom-call(s32[8,16]{1,0:T(8,128)S(1)} %copy-done.4, bf16[8,1,256,256]{3,2,1,0:T(8,128)(2,1)S(1)} %collective-permute-done.5.whole.refs_0_, bf16[5,1,256,256]{3,2,1,0:T(8,128)(2,1)S(1)} %collective-permute-done.11.refs_1_, ...), custom_call_target="tpu_custom_call" | custom-call | flops 1 | bytes 1 | tf_op jit(solution)/shard_map/pallas_call | solution.py:99
  89.2 0.7 collective-permute-start.19
  89.8 15.0 %collective-permute-done.15.refs_2_ = bf16[8,1,256,256]{3,2,1,0:T(8,128)(2,1)S(1)} collective-permute-done((bf16[8,1,256,256]{3,2,1,0:T(8,128)(2,1)S(1)}, bf16[8,1,256,256]{3,2,1,0:T(8,128)(2,1)S(1)}, u32[]{:S(2)}, u32[]{:S(2)}) %collective-permute-start.15) | collective-permute-done | bytes 1048608 | tf_op jit(solution)/shard_map/ppermute | solution.py:183
  104.9 1.3 %shard_map.55 = bf16[4,256,256]{2,1,0:T(8,128)(2,1)S(1)} custom-call(bf16[512,2048]{1,0:T(8,128)(2,1)S(1)} %get-tuple-element.45.refs_0_, bf16[512,2048]{1,0:T(8,128)(2,1)S(1)} %get-tuple-element.46.refs_1_, bf16[8,1,256,256]{3,2,1,0:T(8,128)(2,1)S(1)} %collective-permute-done.15.refs_2_), custom_call_target="tpu_custom_call" | custom-call | flops 10000000000 | bytes 1 | tf_op jit(solution)/shard_map/pallas_call | solution.py:78
  106.1 4.5 %collective-permute-start.18 = (bf16[4,256,256]{2,1,0:T(8,128)(2,1)S(1)}, bf16[4,256,256]{2,1,0:T(8,128)(2,1)S(1)}, u32[]{:S(2)}, u32[]{:S(2)}) collective-permute-start(bf16[4,256,256]{2,1,0:T(8,128)(2,1)S(1)} %shard_map.55), channel_id=1, source_target_pairs={{0,12},{1,13},{2,14},{3,15},{12,0},{13,1},{14,2},{15,3},{16,28},{1... | collective-permute-start | bytes 1572872 | tf_op jit(solution)/shard_map/ppermute | solution.py:183
  110.7 1.9 %shard_map.56.refs_1_ = bf16[2,256,256]{2,1,0:T(8,128)(2,1)S(1)} custom-call(s32[8,16]{1,0:T(8,128)S(1)} %copy-done.4, bf16[8,1,256,256]{3,2,1,0:T(8,128)(2,1)S(1)} %collective-permute-done.5.whole.refs_0_, bf16[5,1,256,256]{3,2,1,0:T(8,128)(2,1)S(1)} %collective-permute-done.11.refs_1_, bf16[3,1,256,256]{3,2,1,0:T(8,128)(2,1)S(1)} %collective-permute-done.12.refs_2_, ...), custom_call_target="tpu_custom_call" | custom-call | flops 1 | bytes 1 | tf_op jit(solution)/shard_map/pallas_call | solution.py:99
  112.6 1.3 %shard_map.57.refs_0_ = bf16[16,256,256]{2,1,0:T(8,128)(2,1)} custom-call(bf16[2,256,256]{2,1,0:T(8,128)(2,1)S(1)} %shard_map.46.refs_0_, bf16[2,256,256]{2,1,0:T(8,128)(2,1)S(1)} %shard_map.56.refs_1_, bf16[2,256,256]{2,1,0:T(8,128)(2,1)S(1)} %collective-permute-done.10.refs_2_, bf16[2,256,256]{2,1,0:T(8,128)(2,1)S(1)} %collective-permute-done.16.refs_3_, ...), custom_call_target="tpu_custom_call" | custom-call | flops 10000000000 | bytes 1 | tf_op jit(solution)/shard_map/pallas_call | solution.py:170
  113.9 5.1 %collective-permute-done.18.refs_1_ = bf16[4,256,256]{2,1,0:T(8,128)(2,1)S(1)} collective-permute-done((bf16[4,256,256]{2,1,0:T(8,128)(2,1)S(1)}, bf16[4,256,256]{2,1,0:T(8,128)(2,1)S(1)}, u32[]{:S(2)}, u32[]{:S(2)}) %collective-permute-start.18) | collective-permute-done | bytes 524320 | tf_op jit(solution)/shard_map/ppermute | solution.py:183
  119.0 0.9 shard_map.58
  (15 shorter events, 0.0 us)
Async XLA Ops:
  0.0 6.0 %collective-permute-start.3 = (bf16[1,16,256,256]{3,2,1,0:T(8,128)(2,1)}, bf16[1,16,256,256]{3,2,1,0:T(8,128)(2,1)S(1)}, u32[]{:S(2)}, u32[]{:S(2)}) collective-permute-start(bf16[1,16,256,256]{3,2,1,0:T(8,128)(2,1)} %refs_2_.7), channel_id=1, source_target_pairs={{0,1},{1,0},{2,3},{3,2},{4,5},{5,4},{6,7},{7,6},{8,9},{9,8},{10,11... | collective-permute-start | bytes 6291464 | tf_op jit(solution)/shard_map/ppermute | solution.py:183
  0.5 49.0 %collective-permute-start.4 = (bf16[1,16,256,256]{3,2,1,0:T(8,128)(2,1)}, bf16[1,16,256,256]{3,2,1,0:T(8,128)(2,1)S(1)}, u32[]{:S(2)}, u32[]{:S(2)}) collective-permute-start(bf16[1,16,256,256]{3,2,1,0:T(8,128)(2,1)} %refs_2_.7), channel_id=1, source_target_pairs={{0,2},{1,3},{2,0},{3,1},{4,6},{5,7},{6,4},{7,5},{8,10},{9,11},{10,... | collective-permute-start | bytes 6291464 | tf_op jit(solution)/shard_map/ppermute | solution.py:183
  2.9 3.0 %collective-permute-start.2 = (bf16[8,1,256,256]{3,2,1,0:T(8,128)(2,1)}, bf16[8,1,256,256]{3,2,1,0:T(8,128)(2,1)S(1)}, u32[]{:S(2)}, u32[]{:S(2)}) collective-permute-start(bf16[8,1,256,256]{3,2,1,0:T(8,128)(2,1)} %refs_0_.7), channel_id=1, source_target_pairs={{0,1},{1,0},{2,3},{3,2},{4,5},{5,4},{6,7},{7,6},{8,9},{9,8},{10,11... | collective-permute-start | bytes 3145736 | tf_op jit(solution)/shard_map/ppermute | solution.py:183
  3.2 25.6 %collective-permute-start = (bf16[8,1,256,256]{3,2,1,0:T(8,128)(2,1)}, bf16[8,1,256,256]{3,2,1,0:T(8,128)(2,1)S(1)}, u32[]{:S(2)}, u32[]{:S(2)}) collective-permute-start(bf16[8,1,256,256]{3,2,1,0:T(8,128)(2,1)} %refs_6_), channel_id=1, source_target_pairs={{0,4},{1,5},{2,6},{3,7},{4,0},{5,1},{6,2},{7,3},{8,12},{9,13},{10,... | collective-permute-start | bytes 3145736 | tf_op jit(solution)/shard_map/ppermute | solution.py:183
  4.7 24.0 %collective-permute-start.1 = (bf16[8,1,256,256]{3,2,1,0:T(8,128)(2,1)}, bf16[8,1,256,256]{3,2,1,0:T(8,128)(2,1)S(1)}, u32[]{:S(2)}, u32[]{:S(2)}) collective-permute-start(bf16[8,1,256,256]{3,2,1,0:T(8,128)(2,1)} %refs_6_), channel_id=1, source_target_pairs={{4,8},{5,9},{6,10},{7,11},{8,4},{9,5},{10,6},{11,7},{20,24},{21,25... | collective-permute-start | bytes 3145736 | tf_op jit(solution)/shard_map/ppermute | solution.py:183
  6.0 1.6 %copy-start = (bf16[1,16,256,256]{3,2,1,0:T(8,128)(2,1)S(1)}, bf16[1,16,256,256]{3,2,1,0:T(8,128)(2,1)}, u32[]{:S(2)}) copy-start(bf16[1,16,256,256]{3,2,1,0:T(8,128)(2,1)} %refs_2_.7) | copy-start | bytes 6291460
  7.5 1.2 %copy-start.1 = (bf16[8,1,256,256]{3,2,1,0:T(8,128)(2,1)S(1)}, bf16[8,1,256,256]{3,2,1,0:T(8,128)(2,1)}, u32[]{:S(2)}) copy-start(bf16[8,1,256,256]{3,2,1,0:T(8,128)(2,1)} %refs_0_.7) | copy-start | bytes 3145732
  8.8 1.2 %copy-start.2 = (bf16[8,1,256,256]{3,2,1,0:T(8,128)(2,1)S(1)}, bf16[8,1,256,256]{3,2,1,0:T(8,128)(2,1)}, u32[]{:S(2)}) copy-start(bf16[8,1,256,256]{3,2,1,0:T(8,128)(2,1)} %refs_6_) | copy-start | bytes 3145732
  10.0 0.7 copy-start.4
  28.7 29.9 %collective-permute-start.6 = (bf16[8,1,256,256]{3,2,1,0:T(8,128)(2,1)S(1)}, bf16[8,1,256,256]{3,2,1,0:T(8,128)(2,1)S(1)}, u32[]{:S(2)}, u32[]{:S(2)}) collective-permute-start(bf16[8,1,256,256]{3,2,1,0:T(8,128)(2,1)S(1)} %collective-permute-done.1.refs_4_.refs_6_), channel_id=1, source_target_pairs={{4,0},{5,1},{6,2},{7,3},{8,12},{9,13},{10,14},{11,15},{20,16},{21,... | collective-permute-start | bytes 3145736 | tf_op jit(solution)/shard_map/ppermute | solution.py:183
  30.0 28.6 %collective-permute-start.7 = (bf16[8,1,256,256]{3,2,1,0:T(8,128)(2,1)S(1)}, bf16[8,1,256,256]{3,2,1,0:T(8,128)(2,1)S(1)}, u32[]{:S(2)}, u32[]{:S(2)}) collective-permute-start(bf16[8,1,256,256]{3,2,1,0:T(8,128)(2,1)S(1)} %collective-permute-done.refs_4_.refs_6_), channel_id=1, source_target_pairs={{4,8},{5,9},{6,10},{7,11},{8,4},{9,5},{10,6},{11,7},{20,24},{21,25... | collective-permute-start | bytes 3145736 | tf_op jit(solution)/shard_map/ppermute | solution.py:183
  49.5 25.0 %collective-permute-start.5 = (bf16[8,1,256,256]{3,2,1,0:T(8,128)(2,1)S(1)}, bf16[8,1,256,256]{3,2,1,0:T(8,128)(2,1)S(1)}, u32[]{:S(2)}, u32[]{:S(2)}) collective-permute-start(bf16[8,1,256,256]{3,2,1,0:T(8,128)(2,1)S(1)} %copy-done.1), channel_id=1, source_target_pairs={{0,2},{1,3},{2,0},{3,1},{4,6},{5,7},{6,4},{7,5},{8,10},{9,11},{10,... | collective-permute-start | bytes 3145736 | tf_op jit(solution)/shard_map/ppermute | solution.py:183
  51.2 11.8 %collective-permute-start.8 = (bf16[2,256,256]{2,1,0:T(8,128)(2,1)S(1)}, bf16[2,256,256]{2,1,0:T(8,128)(2,1)S(1)}, u32[]{:S(2)}, u32[]{:S(2)}) collective-permute-start(bf16[2,256,256]{2,1,0:T(8,128)(2,1)S(1)} %shard_map.47), channel_id=1, source_target_pairs={{0,4},{1,5},{2,6},{3,7},{4,0},{5,1},{6,2},{7,3},{8,12},{9,13},{10,... | collective-permute-start | bytes 786440 | tf_op jit(solution)/shard_map/ppermute | solution.py:183
  52.8 10.2 %collective-permute-start.9 = (bf16[2,256,256]{2,1,0:T(8,128)(2,1)S(1)}, bf16[2,256,256]{2,1,0:T(8,128)(2,1)S(1)}, u32[]{:S(2)}, u32[]{:S(2)}) collective-permute-start(bf16[2,256,256]{2,1,0:T(8,128)(2,1)S(1)} %get-tuple-element.37), channel_id=1, source_target_pairs={{4,8},{5,9},{6,10},{7,11},{8,4},{9,5},{10,6},{11,7},{20,24},{21,25... | collective-permute-start | bytes 786440 | tf_op jit(solution)/shard_map/ppermute | solution.py:183
  58.6 20.3 %collective-permute-start.13 = (bf16[1,9,256,256]{3,2,1,0:T(8,128)(2,1)S(1)}, bf16[1,9,256,256]{3,2,1,0:T(8,128)(2,1)S(1)}, u32[]{:S(2)}, u32[]{:S(2)}) collective-permute-start(bf16[1,9,256,256]{3,2,1,0:T(8,128)(2,1)S(1)} %get-tuple-element.43), channel_id=1, source_target_pairs={{0,1},{1,0},{2,3},{3,2},{4,5},{5,4},{6,7},{7,6},{8,9},{9,8},{10,11... | collective-permute-start | bytes 3538952 | tf_op jit(solution)/shard_map/ppermute | solution.py:183
  58.6 46.2 %collective-permute-start.15 = (bf16[8,1,256,256]{3,2,1,0:T(8,128)(2,1)S(1)}, bf16[8,1,256,256]{3,2,1,0:T(8,128)(2,1)S(1)}, u32[]{:S(2)}, u32[]{:S(2)}) collective-permute-start(bf16[8,1,256,256]{3,2,1,0:T(8,128)(2,1)S(1)} %collective-permute-done.7.refs_5_.refs_7_), channel_id=1, source_target_pairs={{4,0},{5,1},{6,2},{7,3},{8,12},{9,13},{10,14},{11,15},{20,16},{21,... | collective-permute-start | bytes 3145736 | tf_op jit(solution)/shard_map/ppermute | solution.py:183
  63.0 15.3 %collective-permute-start.10 = (bf16[2,256,256]{2,1,0:T(8,128)(2,1)S(1)}, bf16[2,256,256]{2,1,0:T(8,128)(2,1)S(1)}, u32[]{:S(2)}, u32[]{:S(2)}) collective-permute-start(bf16[2,256,256]{2,1,0:T(8,128)(2,1)S(1)} %shard_map.49), channel_id=1, source_target_pairs={{0,8},{1,9},{2,10},{3,11},{4,12},{5,13},{6,14},{7,15},{8,0},{9,1},... | collective-permute-start | bytes 786440 | tf_op jit(solution)/shard_map/ppermute | solution.py:183
  67.6 11.4 %collective-permute-start.14 = (bf16[1,7,256,256]{3,2,1,0:T(8,128)(2,1)S(1)}, bf16[1,7,256,256]{3,2,1,0:T(8,128)(2,1)S(1)}, u32[]{:S(2)}, u32[]{:S(2)}) collective-permute-start(bf16[1,7,256,256]{3,2,1,0:T(8,128)(2,1)S(1)} %get-tuple-element.44), channel_id=1, source_target_pairs={{0,1},{1,0},{2,3},{3,2},{4,5},{5,4},{6,7},{7,6},{8,9},{9,8},{10,11... | collective-permute-start | bytes 2752520 | tf_op jit(solution)/shard_map/ppermute | solution.py:183
  78.4 2.7 %collective-permute-start.11 = (bf16[5,1,256,256]{3,2,1,0:T(8,128)(2,1)S(1)}, bf16[5,1,256,256]{3,2,1,0:T(8,128)(2,1)S(1)}, u32[]{:S(2)}, u32[]{:S(2)}) collective-permute-start(bf16[5,1,256,256]{3,2,1,0:T(8,128)(2,1)S(1)} %get-tuple-element.40), channel_id=1, source_target_pairs={{0,1},{1,0},{2,3},{3,2},{4,5},{5,4},{6,7},{7,6},{8,9},{9,8},{10,11... | collective-permute-start | bytes 1966088 | tf_op jit(solution)/shard_map/ppermute | solution.py:183
  78.5 2.6 %collective-permute-start.12 = (bf16[3,1,256,256]{3,2,1,0:T(8,128)(2,1)S(1)}, bf16[3,1,256,256]{3,2,1,0:T(8,128)(2,1)S(1)}, u32[]{:S(2)}, u32[]{:S(2)}) collective-permute-start(bf16[3,1,256,256]{3,2,1,0:T(8,128)(2,1)S(1)} %get-tuple-element.41), channel_id=1, source_target_pairs={{0,1},{1,0},{2,3},{3,2},{4,5},{5,4},{6,7},{7,6},{8,9},{9,8},{10,11... | collective-permute-start | bytes 1179656 | tf_op jit(solution)/shard_map/ppermute | solution.py:183
  83.0 29.6 %collective-permute-start.16 = (bf16[2,256,256]{2,1,0:T(8,128)(2,1)S(1)}, bf16[2,256,256]{2,1,0:T(8,128)(2,1)S(1)}, u32[]{:S(2)}, u32[]{:S(2)}) collective-permute-start(bf16[2,256,256]{2,1,0:T(8,128)(2,1)S(1)} %shard_map.54), channel_id=1, source_target_pairs={{0,8},{1,9},{2,10},{3,11},{4,12},{5,13},{6,14},{7,15},{8,0},{9,1},... | collective-permute-start | bytes 786440 | tf_op jit(solution)/shard_map/ppermute | solution.py:183
  85.0 27.6 %collective-permute-start.17 = (bf16[2,256,256]{2,1,0:T(8,128)(2,1)S(1)}, bf16[2,256,256]{2,1,0:T(8,128)(2,1)S(1)}, u32[]{:S(2)}, u32[]{:S(2)}) collective-permute-start(bf16[2,256,256]{2,1,0:T(8,128)(2,1)S(1)} %shard_map.53), channel_id=1, source_target_pairs={{0,4},{1,5},{2,6},{3,7},{4,0},{5,1},{6,2},{7,3},{8,12},{9,13},{10,... | collective-permute-start | bytes 786440 | tf_op jit(solution)/shard_map/ppermute | solution.py:183
  89.2 24.8 %collective-permute-start.19 = (bf16[2,256,256]{2,1,0:T(8,128)(2,1)S(1)}, bf16[2,256,256]{2,1,0:T(8,128)(2,1)S(1)}, u32[]{:S(2)}, u32[]{:S(2)}) collective-permute-start(bf16[2,256,256]{2,1,0:T(8,128)(2,1)S(1)} %get-tuple-element.47), channel_id=1, source_target_pairs={{4,8},{5,9},{6,10},{7,11},{8,4},{9,5},{10,6},{11,7},{20,24},{21,25... | collective-permute-start | bytes 786440 | tf_op jit(solution)/shard_map/ppermute | solution.py:183
  104.9 5.8 %copy-start.3 = (bf16[8,1,256,256]{3,2,1,0:T(8,128)(2,1)S(1)}, bf16[8,1,256,256]{3,2,1,0:T(8,128)(2,1)}, u32[]{:S(2)}) copy-start(bf16[8,1,256,256]{3,2,1,0:T(8,128)(2,1)} %refs_6_) | copy-start | bytes 3145732
  106.1 12.9 %collective-permute-start.18 = (bf16[4,256,256]{2,1,0:T(8,128)(2,1)S(1)}, bf16[4,256,256]{2,1,0:T(8,128)(2,1)S(1)}, u32[]{:S(2)}, u32[]{:S(2)}) collective-permute-start(bf16[4,256,256]{2,1,0:T(8,128)(2,1)S(1)} %shard_map.55), channel_id=1, source_target_pairs={{0,12},{1,13},{2,14},{3,15},{12,0},{13,1},{14,2},{15,3},{16,28},{1... | collective-permute-start | bytes 1572872 | tf_op jit(solution)/shard_map/ppermute | solution.py:183

commit v17 on v16

--- a/solution.py
+++ b/solution.py
@@ -129,46 +129,44 @@
     )(array)
 
 
-def place_kernel(starts, chosen, *refs):
+def place_kernel(starts, shared, *refs):
     *pieces, out, sem = refs
     pieces = pieces[-len(starts) :]
     me = lax.axis_index("sec")
     row = me >> 2
     outer = (row == 0) | (row == 3)
 
-    def copies(chosen_pieces):
+    def copies(held):
         return [
             pltpu.make_async_copy(piece.at[i], out.at[me ^ (start + i)], sem.at[start + i])
-            for start, piece in chosen_pieces
+            for start, piece in held
             for i in range(piece.shape[0])
         ]
 
     held = list(zip(starts, pieces))
-    if chosen:
+    for copy in copies(held[:shared]):
+        copy.start()
+    if shared < len(held):
 
         @pl.when(outer)
         def _():
-            for copy in copies(held[:1]):
+            for copy in copies(held[shared : shared + 1]):
                 copy.start()
 
         @pl.when(jnp.logical_not(outer))
         def _():
-            for copy in copies(held[1:]):
+            for copy in copies(held[shared + 1 :]):
                 copy.start()
 
-        held = held[:1]
-    else:
-        for copy in copies(held):
-            copy.start()
-    for copy in copies(held):
+    for copy in copies(held[: shared + 1]):
         copy.wait()
 
 
-def place(sectors, held, out=None, flops=1):
+def place(sectors, held, out=None, shared=None, flops=1):
     starts, pieces = zip(*held)
     before = [] if out is None else [out]
     return pl.pallas_call(
-        functools.partial(place_kernel, starts, out is not None),
+        functools.partial(place_kernel, starts, len(held) if shared is None else shared),
         out_shape=jax.ShapeDtypeStruct((sectors,) + pieces[0].shape[1:], pieces[0].dtype),
         in_specs=[HBM] * len(before) + [VMEM] * len(pieces),
         out_specs=HBM,
@@ -224,17 +222,18 @@
     other_middle, other_mid = products(3, *other, (middle,), keep_mid=True)
     sent_other_middle = exchange(other_middle, 12, inner)
     other_1 = products(1, *other, (near,))
-    other_sent_1 = exchange(other_1, 4, every)
 
     third, other_1, other_2, other_middle = lax.optimization_barrier((third, other_1, other_2, other_middle))
     last_third = second((own_mid, other_mid), third, dtype, 10**10)
+    last_third, other_1 = lax.optimization_barrier((last_third, other_1))
     sent_third = exchange(last_third, 12, outer)
+    other_sent_1 = exchange(other_1, 4, every)
     right_last, last_third = lax.optimization_barrier((right_env, last_third))
     other_0 = products(0, *other, (right_last,))
 
-    held = [(0, own_0), (2, other_0), (8, sent_2), (10, other_sent_2), (4, sent_1), (6, other_sent_1)]
-    out = place(16, held, flops=10**10)
-    out = place(16, [(12, sent_third), (12, sent_own_middle), (14, sent_other_middle)], out)[:, None]
+    out = place(16, [(0, own_0), (2, other_0), (4, sent_1), (8, sent_2), (10, other_sent_2)], flops=10**10)
+    last = [(12, sent_third), (12, sent_own_middle), (14, sent_other_middle)]
+    out = place(16, [(6, other_sent_1)] + last, out, 1)[:, None]
     if ops > 1:
         out = lax.psum_scatter(out, "op", scatter_dimension=2, tiled=True).astype(jnp.bfloat16)
     return out

time: 120 us -> 121 us (level)
  starting transfers between devices: 25.5 us -> 29.4 us
  waiting for transfers between devices: 70.8 us -> 67.2 us
    ppermute x20, starting transfers between devices: 25.5 us -> 29.4 us  [exchange(): return lax.ppermute(array, 'sec', [(s, s ^ bits) for s in members])]
    ppermute x20, waiting for transfers between devices: 70.8 us -> 67.2 us  [exchange(): return lax.ppermute(array, 'sec', [(s, s ^ bits) for s in members])]
where the time goes in v17:
time: 121 us; the launch traced here: 120 us
  waiting for transfers between devices  67.2 us (56%)
  starting transfers between devices  29.4 us (24%)
  Pallas kernels  18.8 us (16%)
  local copies, waits for them, and re-layouts  4.73 us (4%)
    ppermute x20, waiting for transfers between devices, exchange(): return lax.ppermute(array, 'sec', [(s, s ^ bits) for s in members])  67.2 us
    ppermute x20, starting transfers between devices, exchange(): return lax.ppermute(array, 'sec', [(s, s ^ bits) for s in members])  29.4 us
    pallas_call x8, Pallas kernels, slot(): pl.pallas_call(functools.partial(slot_kernel, step, parts, len(rights)),...  15.1 us
    unnamed x10, local copies, waits for them, and re-layouts  4.73 us
  transfers between devices with their start and end apart: 20, of which 10 were waited for; matrix products, arithmetic and copies ran while one was open for 0% of the time, Pallas kernels for 15%

profile of v17, /device:TPU:0, one launch (start us, length us, event | category | flops | bytes accessed | tf_op | source)
XLA Modules:
  0.0 120.3 jit_solution(11611400590740371094)
XLA Ops:
  0.0 0.5 collective-permute-start.3
  0.5 2.5 %collective-permute-start.4 = (bf16[1,16,256,256]{3,2,1,0:T(8,128)(2,1)}, bf16[1,16,256,256]{3,2,1,0:T(8,128)(2,1)S(1)}, u32[]{:S(2)}, u32[]{:S(2)}) collective-permute-start(bf16[1,16,256,256]{3,2,1,0:T(8,128)(2,1)} %refs_2_.7), channel_id=1, source_target_pairs={{0,2},{1,3},{2,0},{3,1},{4,6},{5,7},{6,4},{7,5},{8,10},{9,11},{10,... | collective-permute-start | bytes 6291464 | tf_op jit(solution)/shard_map/ppermute | solution.py:181
  2.9 0.2 collective-permute-start.2
  3.2 1.6 %collective-permute-start = (bf16[8,1,256,256]{3,2,1,0:T(8,128)(2,1)}, bf16[8,1,256,256]{3,2,1,0:T(8,128)(2,1)S(1)}, u32[]{:S(2)}, u32[]{:S(2)}) collective-permute-start(bf16[8,1,256,256]{3,2,1,0:T(8,128)(2,1)} %refs_6_), channel_id=1, source_target_pairs={{0,4},{1,5},{2,6},{3,7},{4,0},{5,1},{6,2},{7,3},{8,12},{9,13},{10,... | collective-permute-start | bytes 3145736 | tf_op jit(solution)/shard_map/ppermute | solution.py:181
  4.7 0.7 collective-permute-start.1
  5.5 0.5 collective-permute-done.2.refs_1_
  6.0 0.0 collective-permute-done.3.refs_3_
  6.0 1.6 %copy-done = bf16[1,16,256,256]{3,2,1,0:T(8,128)(2,1)S(1)} copy-done((bf16[1,16,256,256]{3,2,1,0:T(8,128)(2,1)S(1)}, bf16[1,16,256,256]{3,2,1,0:T(8,128)(2,1)}, u32[]{:S(2)}) %copy-start) | copy-done | bytes 2097176
  7.5 1.2 %copy-done.1 = bf16[8,1,256,256]{3,2,1,0:T(8,128)(2,1)S(1)} copy-done((bf16[8,1,256,256]{3,2,1,0:T(8,128)(2,1)S(1)}, bf16[8,1,256,256]{3,2,1,0:T(8,128)(2,1)}, u32[]{:S(2)}) %copy-start.1) | copy-done | bytes 1048600
  8.8 1.2 %copy-done.2 = bf16[8,1,256,256]{3,2,1,0:T(8,128)(2,1)S(1)} copy-done((bf16[8,1,256,256]{3,2,1,0:T(8,128)(2,1)S(1)}, bf16[8,1,256,256]{3,2,1,0:T(8,128)(2,1)}, u32[]{:S(2)}) %copy-start.2) | copy-done | bytes 1048600
  10.0 0.7 copy-done.4
  10.7 1.9 %shard_map.46.refs_0_ = bf16[2,256,256]{2,1,0:T(8,128)(2,1)S(1)} custom-call(s32[8,16]{1,0:T(8,128)S(1)} %copy-done.4, bf16[8,1,256,256]{3,2,1,0:T(8,128)(2,1)S(1)} %copy-done.1, bf16[8,1,256,256]{3,2,1,0:T(8,128)(2,1)S(1)} %collective-permute-done.2.refs_1_, bf16[1,16,256,256]{3,2,1,0:T(8,128)(2,1)S(1)} %copy-done, ...), custom_call_target="tpu_custom_call" | custom-call | flops 1 | bytes 1 | tf_op jit(solution)/shard_map/pallas_call | solution.py:99
  12.6 16.2 %collective-permute-done.refs_4_.refs_6_ = bf16[8,1,256,256]{3,2,1,0:T(8,128)(2,1)S(1)} collective-permute-done((bf16[8,1,256,256]{3,2,1,0:T(8,128)(2,1)}, bf16[8,1,256,256]{3,2,1,0:T(8,128)(2,1)S(1)}, u32[]{:S(2)}, u32[]{:S(2)}) %collective-permute-start) | collective-permute-done | bytes 1048608 | tf_op jit(solution)/shard_map/ppermute | solution.py:181
  28.7 1.3 %collective-permute-start.6 = (bf16[8,1,256,256]{3,2,1,0:T(8,128)(2,1)S(1)}, bf16[8,1,256,256]{3,2,1,0:T(8,128)(2,1)S(1)}, u32[]{:S(2)}, u32[]{:S(2)}) collective-permute-start(bf16[8,1,256,256]{3,2,1,0:T(8,128)(2,1)S(1)} %collective-permute-done.1.refs_4_.refs_6_), channel_id=1, source_target_pairs={{4,0},{5,1},{6,2},{7,3},{8,12},{9,13},{10,14},{11,15},{20,16},{21,... | collective-permute-start | bytes 3145736 | tf_op jit(solution)/shard_map/ppermute | solution.py:181
  30.0 0.7 collective-permute-start.7
  30.8 1.9 %shard_map.48 = (bf16[2,256,256]{2,1,0:T(8,128)(2,1)S(1)}, bf16[512,2048]{1,0:T(8,128)(2,1)S(1)}) custom-call(s32[8,16]{1,0:T(8,128)S(1)} %copy-done.4, bf16[8,1,256,256]{3,2,1,0:T(8,128)(2,1)S(1)} %copy-done.1, bf16[8,1,256,256]{3,2,1,0:T(8,128)(2,1)S(1)} %collective-permute-done.2.refs_1_, bf16[1,16,256,256]{3,2,1,0:T(8,128)(2,1)S(1)} %copy-done, ...), custom_call_target="tpu_custom_call" | custom-call | flops 1 | bytes 1 | tf_op jit(solution)/shard_map/pallas_call | solution.py:99
  32.6 1.9 %shard_map.47 = bf16[2,256,256]{2,1,0:T(8,128)(2,1)S(1)} custom-call(s32[8,16]{1,0:T(8,128)S(1)} %copy-done.4, bf16[8,1,256,256]{3,2,1,0:T(8,128)(2,1)S(1)} %copy-done.1, bf16[8,1,256,256]{3,2,1,0:T(8,128)(2,1)S(1)} %collective-permute-done.2.refs_1_, bf16[1,16,256,256]{3,2,1,0:T(8,128)(2,1)S(1)} %copy-done, ...), custom_call_target="tpu_custom_call" | custom-call | flops 1 | bytes 1 | tf_op jit(solution)/shard_map/pallas_call | solution.py:99
  34.5 14.9 %collective-permute-done.4.whole.refs_3_ = bf16[1,16,256,256]{3,2,1,0:T(8,128)(2,1)S(1)} collective-permute-done((bf16[1,16,256,256]{3,2,1,0:T(8,128)(2,1)}, bf16[1,16,256,256]{3,2,1,0:T(8,128)(2,1)S(1)}, u32[]{:S(2)}, u32[]{:S(2)}) %collective-permute-start.4) | collective-permute-done | bytes 2097184 | tf_op jit(solution)/shard_map/ppermute | solution.py:181
  49.5 1.7 %collective-permute-start.5 = (bf16[8,1,256,256]{3,2,1,0:T(8,128)(2,1)S(1)}, bf16[8,1,256,256]{3,2,1,0:T(8,128)(2,1)S(1)}, u32[]{:S(2)}, u32[]{:S(2)}) collective-permute-start(bf16[8,1,256,256]{3,2,1,0:T(8,128)(2,1)S(1)} %copy-done.1), channel_id=1, source_target_pairs={{0,2},{1,3},{2,0},{3,1},{4,6},{5,7},{6,4},{7,5},{8,10},{9,11},{10,... | collective-permute-start | bytes 3145736 | tf_op jit(solution)/shard_map/ppermute | solution.py:181
  51.2 1.6 %collective-permute-start.8 = (bf16[2,256,256]{2,1,0:T(8,128)(2,1)S(1)}, bf16[2,256,256]{2,1,0:T(8,128)(2,1)S(1)}, u32[]{:S(2)}, u32[]{:S(2)}) collective-permute-start(bf16[2,256,256]{2,1,0:T(8,128)(2,1)S(1)} %shard_map.47), channel_id=1, source_target_pairs={{0,4},{1,5},{2,6},{3,7},{4,0},{5,1},{6,2},{7,3},{8,12},{9,13},{10,... | collective-permute-start | bytes 786440 | tf_op jit(solution)/shard_map/ppermute | solution.py:181
  52.8 0.7 collective-permute-start.9
  53.4 0.1 shard_map.51
  53.6 5.0 %collective-permute-done.6.refs_4_.refs_6_ = bf16[8,1,256,256]{3,2,1,0:T(8,128)(2,1)S(1)} collective-permute-done((bf16[8,1,256,256]{3,2,1,0:T(8,128)(2,1)S(1)}, bf16[8,1,256,256]{3,2,1,0:T(8,128)(2,1)S(1)}, u32[]{:S(2)}, u32[]{:S(2)}) %collective-permute-start.6) | collective-permute-done | bytes 1048608 | tf_op jit(solution)/shard_map/ppermute | solution.py:181
  58.6 0.0 collective-permute-start.13
  58.6 0.0 collective-permute-done.7.refs_5_.refs_7_
  58.6 1.3 %collective-permute-start.15 = (bf16[8,1,256,256]{3,2,1,0:T(8,128)(2,1)S(1)}, bf16[8,1,256,256]{3,2,1,0:T(8,128)(2,1)S(1)}, u32[]{:S(2)}, u32[]{:S(2)}) collective-permute-start(bf16[8,1,256,256]{3,2,1,0:T(8,128)(2,1)S(1)} %collective-permute-done.7.refs_5_.refs_7_), channel_id=1, source_target_pairs={{4,0},{5,1},{6,2},{7,3},{8,12},{9,13},{10,14},{11,15},{20,16},{21,... | collective-permute-start | bytes 3145736 | tf_op jit(solution)/shard_map/ppermute | solution.py:181
  59.9 1.9 %shard_map.49 = bf16[2,256,256]{2,1,0:T(8,128)(2,1)S(1)} custom-call(s32[8,16]{1,0:T(8,128)S(1)} %copy-done.4, bf16[8,1,256,256]{3,2,1,0:T(8,128)(2,1)S(1)} %copy-done.1, bf16[8,1,256,256]{3,2,1,0:T(8,128)(2,1)S(1)} %collective-permute-done.2.refs_1_, bf16[1,16,256,256]{3,2,1,0:T(8,128)(2,1)S(1)} %copy-done, ...), custom_call_target="tpu_custom_call" | custom-call | flops 1 | bytes 1 | tf_op jit(solution)/shard_map/pallas_call | solution.py:99
  61.8 1.2 collective-permute-done.8.refs_2_
  63.0 4.6 %collective-permute-start.10 = (bf16[2,256,256]{2,1,0:T(8,128)(2,1)S(1)}, bf16[2,256,256]{2,1,0:T(8,128)(2,1)S(1)}, u32[]{:S(2)}, u32[]{:S(2)}) collective-permute-start(bf16[2,256,256]{2,1,0:T(8,128)(2,1)S(1)} %shard_map.49), channel_id=1, source_target_pairs={{0,8},{1,9},{2,10},{3,11},{4,12},{5,13},{6,14},{7,15},{8,0},{9,1},... | collective-permute-start | bytes 786440 | tf_op jit(solution)/shard_map/ppermute | solution.py:181
  67.6 6.9 %collective-permute-done.5.whole.refs_0_ = bf16[8,1,256,256]{3,2,1,0:T(8,128)(2,1)S(1)} collective-permute-done((bf16[8,1,256,256]{3,2,1,0:T(8,128)(2,1)S(1)}, bf16[8,1,256,256]{3,2,1,0:T(8,128)(2,1)S(1)}, u32[]{:S(2)}, u32[]{:S(2)}) %collective-permute-start.5) | collective-permute-done | bytes 1048608 | tf_op jit(solution)/shard_map/ppermute | solution.py:181
  74.4 3.9 %collective-permute-done.10.refs_3_ = bf16[2,256,256]{2,1,0:T(8,128)(2,1)S(1)} collective-permute-done((bf16[2,256,256]{2,1,0:T(8,128)(2,1)S(1)}, bf16[2,256,256]{2,1,0:T(8,128)(2,1)S(1)}, u32[]{:S(2)}, u32[]{:S(2)}) %collective-permute-start.10) | collective-permute-done | bytes 262176 | tf_op jit(solution)/shard_map/ppermute | solution.py:181
  78.3 0.1 shard_map.50
  78.4 0.1 collective-permute-start.11
  78.5 0.5 collective-permute-start.12
  79.0 2.1 %collective-permute-done.12.refs_2_ = bf16[3,1,256,256]{3,2,1,0:T(8,128)(2,1)S(1)} collective-permute-done((bf16[3,1,256,256]{3,2,1,0:T(8,128)(2,1)S(1)}, bf16[3,1,256,256]{3,2,1,0:T(8,128)(2,1)S(1)}, u32[]{:S(2)}, u32[]{:S(2)}) %collective-permute-start.12) | collective-permute-done | bytes 393248 | tf_op jit(solution)/shard_map/ppermute | solution.py:181
  81.1 1.9 %shard_map.54 = bf16[2,256,256]{2,1,0:T(8,128)(2,1)S(1)} custom-call(s32[8,16]{1,0:T(8,128)S(1)} %copy-done.4, bf16[8,1,256,256]{3,2,1,0:T(8,128)(2,1)S(1)} %collective-permute-done.5.whole.refs_0_, bf16[5,1,256,256]{3,2,1,0:T(8,128)(2,1)S(1)} %collective-permute-done.11.refs_1_, bf16[3,1,256,256]{3,2,1,0:T(8,128)(2,1)S(1)} %collective-permute-done.12.refs_2_, ...), custom_call_target="tpu_custom_call" | custom-call | flops 1 | bytes 1 | tf_op jit(solution)/shard_map/pallas_call | solution.py:99
  83.0 0.1 collective-permute-start.16
  83.1 1.9 %shard_map.52 = (bf16[2,256,256]{2,1,0:T(8,128)(2,1)S(1)}, bf16[512,2048]{1,0:T(8,128)(2,1)S(1)}) custom-call(s32[8,16]{1,0:T(8,128)S(1)} %copy-done.4, bf16[8,1,256,256]{3,2,1,0:T(8,128)(2,1)S(1)} %collective-permute-done.5.whole.refs_0_, bf16[5,1,256,256]{3,2,1,0:T(8,128)(2,1)S(1)} %collective-permute-done.11.refs_1_, ...), custom_call_target="tpu_custom_call" | custom-call | flops 1 | bytes 1 | tf_op jit(solution)/shard_map/pallas_call | solution.py:99
  85.0 0.7 collective-permute-start.19
  85.7 1.9 %shard_map.53 = bf16[2,256,256]{2,1,0:T(8,128)(2,1)S(1)} custom-call(s32[8,16]{1,0:T(8,128)S(1)} %copy-done.4, bf16[8,1,256,256]{3,2,1,0:T(8,128)(2,1)S(1)} %collective-permute-done.5.whole.refs_0_, bf16[5,1,256,256]{3,2,1,0:T(8,128)(2,1)S(1)} %collective-permute-done.11.refs_1_, bf16[3,1,256,256]{3,2,1,0:T(8,128)(2,1)S(1)} %collective-permute-done.12.refs_2_, ...), custom_call_target="tpu_custom_call" | custom-call | flops 1 | bytes 1 | tf_op jit(solution)/shard_map/pallas_call | solution.py:99
  87.6 9.8 %collective-permute-done.15.refs_2_ = bf16[8,1,256,256]{3,2,1,0:T(8,128)(2,1)S(1)} collective-permute-done((bf16[8,1,256,256]{3,2,1,0:T(8,128)(2,1)S(1)}, bf16[8,1,256,256]{3,2,1,0:T(8,128)(2,1)S(1)}, u32[]{:S(2)}, u32[]{:S(2)}) %collective-permute-start.15) | collective-permute-done | bytes 1048608 | tf_op jit(solution)/shard_map/ppermute | solution.py:181
  97.3 1.3 %shard_map.55 = bf16[4,256,256]{2,1,0:T(8,128)(2,1)S(1)} custom-call(bf16[512,2048]{1,0:T(8,128)(2,1)S(1)} %get-tuple-element.48.refs_0_, bf16[512,2048]{1,0:T(8,128)(2,1)S(1)} %get-tuple-element.49.refs_1_, bf16[8,1,256,256]{3,2,1,0:T(8,128)(2,1)S(1)} %collective-permute-done.15.refs_2_), custom_call_target="tpu_custom_call" | custom-call | flops 10000000000 | bytes 1 | tf_op jit(solution)/shard_map/pallas_call | solution.py:78
  98.6 10.7 %collective-permute-start.18 = (bf16[4,256,256]{2,1,0:T(8,128)(2,1)S(1)}, bf16[4,256,256]{2,1,0:T(8,128)(2,1)S(1)}, u32[]{:S(2)}, u32[]{:S(2)}) collective-permute-start(bf16[4,256,256]{2,1,0:T(8,128)(2,1)S(1)} %shard_map.55), channel_id=1, source_target_pairs={{0,12},{1,13},{2,14},{3,15},{12,0},{13,1},{14,2},{15,3},{16,28},{1... | collective-permute-start | bytes 1572872 | tf_op jit(solution)/shard_map/ppermute | solution.py:181
  109.3 0.1 collective-permute-start.17
  109.4 1.9 %shard_map.56.refs_1_ = bf16[2,256,256]{2,1,0:T(8,128)(2,1)S(1)} custom-call(s32[8,16]{1,0:T(8,128)S(1)} %copy-done.4, bf16[8,1,256,256]{3,2,1,0:T(8,128)(2,1)S(1)} %collective-permute-done.5.whole.refs_0_, bf16[5,1,256,256]{3,2,1,0:T(8,128)(2,1)S(1)} %collective-permute-done.11.refs_1_, bf16[3,1,256,256]{3,2,1,0:T(8,128)(2,1)S(1)} %collective-permute-done.12.refs_2_, ...), custom_call_target="tpu_custom_call" | custom-call | flops 1 | bytes 1 | tf_op jit(solution)/shard_map/pallas_call | solution.py:99
  111.3 1.2 shard_map.57.refs_0_
  112.5 6.8 %collective-permute-done.17.refs_1_ = bf16[2,256,256]{2,1,0:T(8,128)(2,1)S(1)} collective-permute-done((bf16[2,256,256]{2,1,0:T(8,128)(2,1)S(1)}, bf16[2,256,256]{2,1,0:T(8,128)(2,1)S(1)}, u32[]{:S(2)}, u32[]{:S(2)}) %collective-permute-start.17) | collective-permute-done | bytes 262176 | tf_op jit(solution)/shard_map/ppermute | solution.py:181
  119.3 1.0 shard_map.58
  (15 shorter events, 0.0 us)
Async XLA Ops:
  0.0 6.0 %collective-permute-start.3 = (bf16[1,16,256,256]{3,2,1,0:T(8,128)(2,1)}, bf16[1,16,256,256]{3,2,1,0:T(8,128)(2,1)S(1)}, u32[]{:S(2)}, u32[]{:S(2)}) collective-permute-start(bf16[1,16,256,256]{3,2,1,0:T(8,128)(2,1)} %refs_2_.7), channel_id=1, source_target_pairs={{0,1},{1,0},{2,3},{3,2},{4,5},{5,4},{6,7},{7,6},{8,9},{9,8},{10,11... | collective-permute-start | bytes 6291464 | tf_op jit(solution)/shard_map/ppermute | solution.py:181
  0.5 49.0 %collective-permute-start.4 = (bf16[1,16,256,256]{3,2,1,0:T(8,128)(2,1)}, bf16[1,16,256,256]{3,2,1,0:T(8,128)(2,1)S(1)}, u32[]{:S(2)}, u32[]{:S(2)}) collective-permute-start(bf16[1,16,256,256]{3,2,1,0:T(8,128)(2,1)} %refs_2_.7), channel_id=1, source_target_pairs={{0,2},{1,3},{2,0},{3,1},{4,6},{5,7},{6,4},{7,5},{8,10},{9,11},{10,... | collective-permute-start | bytes 6291464 | tf_op jit(solution)/shard_map/ppermute | solution.py:181
  2.9 3.0 %collective-permute-start.2 = (bf16[8,1,256,256]{3,2,1,0:T(8,128)(2,1)}, bf16[8,1,256,256]{3,2,1,0:T(8,128)(2,1)S(1)}, u32[]{:S(2)}, u32[]{:S(2)}) collective-permute-start(bf16[8,1,256,256]{3,2,1,0:T(8,128)(2,1)} %refs_0_.7), channel_id=1, source_target_pairs={{0,1},{1,0},{2,3},{3,2},{4,5},{5,4},{6,7},{7,6},{8,9},{9,8},{10,11... | collective-permute-start | bytes 3145736 | tf_op jit(solution)/shard_map/ppermute | solution.py:181
  3.2 25.6 %collective-permute-start = (bf16[8,1,256,256]{3,2,1,0:T(8,128)(2,1)}, bf16[8,1,256,256]{3,2,1,0:T(8,128)(2,1)S(1)}, u32[]{:S(2)}, u32[]{:S(2)}) collective-permute-start(bf16[8,1,256,256]{3,2,1,0:T(8,128)(2,1)} %refs_6_), channel_id=1, source_target_pairs={{0,4},{1,5},{2,6},{3,7},{4,0},{5,1},{6,2},{7,3},{8,12},{9,13},{10,... | collective-permute-start | bytes 3145736 | tf_op jit(solution)/shard_map/ppermute | solution.py:181
  4.7 24.0 %collective-permute-start.1 = (bf16[8,1,256,256]{3,2,1,0:T(8,128)(2,1)}, bf16[8,1,256,256]{3,2,1,0:T(8,128)(2,1)S(1)}, u32[]{:S(2)}, u32[]{:S(2)}) collective-permute-start(bf16[8,1,256,256]{3,2,1,0:T(8,128)(2,1)} %refs_6_), channel_id=1, source_target_pairs={{4,8},{5,9},{6,10},{7,11},{8,4},{9,5},{10,6},{11,7},{20,24},{21,25... | collective-permute-start | bytes 3145736 | tf_op jit(solution)/shard_map/ppermute | solution.py:181
  6.0 1.6 %copy-start = (bf16[1,16,256,256]{3,2,1,0:T(8,128)(2,1)S(1)}, bf16[1,16,256,256]{3,2,1,0:T(8,128)(2,1)}, u32[]{:S(2)}) copy-start(bf16[1,16,256,256]{3,2,1,0:T(8,128)(2,1)} %refs_2_.7) | copy-start | bytes 6291460
  7.5 1.2 %copy-start.1 = (bf16[8,1,256,256]{3,2,1,0:T(8,128)(2,1)S(1)}, bf16[8,1,256,256]{3,2,1,0:T(8,128)(2,1)}, u32[]{:S(2)}) copy-start(bf16[8,1,256,256]{3,2,1,0:T(8,128)(2,1)} %refs_0_.7) | copy-start | bytes 3145732
  8.8 1.2 %copy-start.2 = (bf16[8,1,256,256]{3,2,1,0:T(8,128)(2,1)S(1)}, bf16[8,1,256,256]{3,2,1,0:T(8,128)(2,1)}, u32[]{:S(2)}) copy-start(bf16[8,1,256,256]{3,2,1,0:T(8,128)(2,1)} %refs_6_) | copy-start | bytes 3145732
  10.0 0.7 copy-start.4
  28.7 29.9 %collective-permute-start.6 = (bf16[8,1,256,256]{3,2,1,0:T(8,128)(2,1)S(1)}, bf16[8,1,256,256]{3,2,1,0:T(8,128)(2,1)S(1)}, u32[]{:S(2)}, u32[]{:S(2)}) collective-permute-start(bf16[8,1,256,256]{3,2,1,0:T(8,128)(2,1)S(1)} %collective-permute-done.1.refs_4_.refs_6_), channel_id=1, source_target_pairs={{4,0},{5,1},{6,2},{7,3},{8,12},{9,13},{10,14},{11,15},{20,16},{21,... | collective-permute-start | bytes 3145736 | tf_op jit(solution)/shard_map/ppermute | solution.py:181
  30.0 28.6 %collective-permute-start.7 = (bf16[8,1,256,256]{3,2,1,0:T(8,128)(2,1)S(1)}, bf16[8,1,256,256]{3,2,1,0:T(8,128)(2,1)S(1)}, u32[]{:S(2)}, u32[]{:S(2)}) collective-permute-start(bf16[8,1,256,256]{3,2,1,0:T(8,128)(2,1)S(1)} %collective-permute-done.refs_4_.refs_6_), channel_id=1, source_target_pairs={{4,8},{5,9},{6,10},{7,11},{8,4},{9,5},{10,6},{11,7},{20,24},{21,25... | collective-permute-start | bytes 3145736 | tf_op jit(solution)/shard_map/ppermute | solution.py:181
  49.5 25.0 %collective-permute-start.5 = (bf16[8,1,256,256]{3,2,1,0:T(8,128)(2,1)S(1)}, bf16[8,1,256,256]{3,2,1,0:T(8,128)(2,1)S(1)}, u32[]{:S(2)}, u32[]{:S(2)}) collective-permute-start(bf16[8,1,256,256]{3,2,1,0:T(8,128)(2,1)S(1)} %copy-done.1), channel_id=1, source_target_pairs={{0,2},{1,3},{2,0},{3,1},{4,6},{5,7},{6,4},{7,5},{8,10},{9,11},{10,... | collective-permute-start | bytes 3145736 | tf_op jit(solution)/shard_map/ppermute | solution.py:181
  51.2 11.8 %collective-permute-start.8 = (bf16[2,256,256]{2,1,0:T(8,128)(2,1)S(1)}, bf16[2,256,256]{2,1,0:T(8,128)(2,1)S(1)}, u32[]{:S(2)}, u32[]{:S(2)}) collective-permute-start(bf16[2,256,256]{2,1,0:T(8,128)(2,1)S(1)} %shard_map.47), channel_id=1, source_target_pairs={{0,4},{1,5},{2,6},{3,7},{4,0},{5,1},{6,2},{7,3},{8,12},{9,13},{10,... | collective-permute-start | bytes 786440 | tf_op jit(solution)/shard_map/ppermute | solution.py:181
  52.8 10.2 %collective-permute-start.9 = (bf16[2,256,256]{2,1,0:T(8,128)(2,1)S(1)}, bf16[2,256,256]{2,1,0:T(8,128)(2,1)S(1)}, u32[]{:S(2)}, u32[]{:S(2)}) collective-permute-start(bf16[2,256,256]{2,1,0:T(8,128)(2,1)S(1)} %get-tuple-element.40), channel_id=1, source_target_pairs={{4,8},{5,9},{6,10},{7,11},{8,4},{9,5},{10,6},{11,7},{20,24},{21,25... | collective-permute-start | bytes 786440 | tf_op jit(solution)/shard_map/ppermute | solution.py:181
  58.6 20.3 %collective-permute-start.13 = (bf16[1,9,256,256]{3,2,1,0:T(8,128)(2,1)S(1)}, bf16[1,9,256,256]{3,2,1,0:T(8,128)(2,1)S(1)}, u32[]{:S(2)}, u32[]{:S(2)}) collective-permute-start(bf16[1,9,256,256]{3,2,1,0:T(8,128)(2,1)S(1)} %get-tuple-element.46), channel_id=1, source_target_pairs={{0,1},{1,0},{2,3},{3,2},{4,5},{5,4},{6,7},{7,6},{8,9},{9,8},{10,11... | collective-permute-start | bytes 3538952 | tf_op jit(solution)/shard_map/ppermute | solution.py:181
  58.6 38.7 %collective-permute-start.15 = (bf16[8,1,256,256]{3,2,1,0:T(8,128)(2,1)S(1)}, bf16[8,1,256,256]{3,2,1,0:T(8,128)(2,1)S(1)}, u32[]{:S(2)}, u32[]{:S(2)}) collective-permute-start(bf16[8,1,256,256]{3,2,1,0:T(8,128)(2,1)S(1)} %collective-permute-done.7.refs_5_.refs_7_), channel_id=1, source_target_pairs={{4,0},{5,1},{6,2},{7,3},{8,12},{9,13},{10,14},{11,15},{20,16},{21,... | collective-permute-start | bytes 3145736 | tf_op jit(solution)/shard_map/ppermute | solution.py:181
  63.0 15.3 %collective-permute-start.10 = (bf16[2,256,256]{2,1,0:T(8,128)(2,1)S(1)}, bf16[2,256,256]{2,1,0:T(8,128)(2,1)S(1)}, u32[]{:S(2)}, u32[]{:S(2)}) collective-permute-start(bf16[2,256,256]{2,1,0:T(8,128)(2,1)S(1)} %shard_map.49), channel_id=1, source_target_pairs={{0,8},{1,9},{2,10},{3,11},{4,12},{5,13},{6,14},{7,15},{8,0},{9,1},... | collective-permute-start | bytes 786440 | tf_op jit(solution)/shard_map/ppermute | solution.py:181
  67.6 11.4 %collective-permute-start.14 = (bf16[1,7,256,256]{3,2,1,0:T(8,128)(2,1)S(1)}, bf16[1,7,256,256]{3,2,1,0:T(8,128)(2,1)S(1)}, u32[]{:S(2)}, u32[]{:S(2)}) collective-permute-start(bf16[1,7,256,256]{3,2,1,0:T(8,128)(2,1)S(1)} %get-tuple-element.47), channel_id=1, source_target_pairs={{0,1},{1,0},{2,3},{3,2},{4,5},{5,4},{6,7},{7,6},{8,9},{9,8},{10,11... | collective-permute-start | bytes 2752520 | tf_op jit(solution)/shard_map/ppermute | solution.py:181
  78.4 2.7 %collective-permute-start.11 = (bf16[5,1,256,256]{3,2,1,0:T(8,128)(2,1)S(1)}, bf16[5,1,256,256]{3,2,1,0:T(8,128)(2,1)S(1)}, u32[]{:S(2)}, u32[]{:S(2)}) collective-permute-start(bf16[5,1,256,256]{3,2,1,0:T(8,128)(2,1)S(1)} %get-tuple-element.43), channel_id=1, source_target_pairs={{0,1},{1,0},{2,3},{3,2},{4,5},{5,4},{6,7},{7,6},{8,9},{9,8},{10,11... | collective-permute-start | bytes 1966088 | tf_op jit(solution)/shard_map/ppermute | solution.py:181
  78.5 2.6 %collective-permute-start.12 = (bf16[3,1,256,256]{3,2,1,0:T(8,128)(2,1)S(1)}, bf16[3,1,256,256]{3,2,1,0:T(8,128)(2,1)S(1)}, u32[]{:S(2)}, u32[]{:S(2)}) collective-permute-start(bf16[3,1,256,256]{3,2,1,0:T(8,128)(2,1)S(1)} %get-tuple-element.44), channel_id=1, source_target_pairs={{0,1},{1,0},{2,3},{3,2},{4,5},{5,4},{6,7},{7,6},{8,9},{9,8},{10,11... | collective-permute-start | bytes 1179656 | tf_op jit(solution)/shard_map/ppermute | solution.py:181
  83.0 28.3 %collective-permute-start.16 = (bf16[2,256,256]{2,1,0:T(8,128)(2,1)S(1)}, bf16[2,256,256]{2,1,0:T(8,128)(2,1)S(1)}, u32[]{:S(2)}, u32[]{:S(2)}) collective-permute-start(bf16[2,256,256]{2,1,0:T(8,128)(2,1)S(1)} %shard_map.54), channel_id=1, source_target_pairs={{0,8},{1,9},{2,10},{3,11},{4,12},{5,13},{6,14},{7,15},{8,0},{9,1},... | collective-permute-start | bytes 786440 | tf_op jit(solution)/shard_map/ppermute | solution.py:181
  85.0 27.5 %collective-permute-start.19 = (bf16[2,256,256]{2,1,0:T(8,128)(2,1)S(1)}, bf16[2,256,256]{2,1,0:T(8,128)(2,1)S(1)}, u32[]{:S(2)}, u32[]{:S(2)}) collective-permute-start(bf16[2,256,256]{2,1,0:T(8,128)(2,1)S(1)} %get-tuple-element.50), channel_id=1, source_target_pairs={{4,8},{5,9},{6,10},{7,11},{8,4},{9,5},{10,6},{11,7},{20,24},{21,25... | collective-permute-start | bytes 786440 | tf_op jit(solution)/shard_map/ppermute | solution.py:181
  97.3 12.1 %copy-start.3 = (bf16[8,1,256,256]{3,2,1,0:T(8,128)(2,1)S(1)}, bf16[8,1,256,256]{3,2,1,0:T(8,128)(2,1)}, u32[]{:S(2)}) copy-start(bf16[8,1,256,256]{3,2,1,0:T(8,128)(2,1)} %refs_6_) | copy-start | bytes 3145732
  98.6 20.7 %collective-permute-start.18 = (bf16[4,256,256]{2,1,0:T(8,128)(2,1)S(1)}, bf16[4,256,256]{2,1,0:T(8,128)(2,1)S(1)}, u32[]{:S(2)}, u32[]{:S(2)}) collective-permute-start(bf16[4,256,256]{2,1,0:T(8,128)(2,1)S(1)} %shard_map.55), channel_id=1, source_target_pairs={{0,12},{1,13},{2,14},{3,15},{12,0},{13,1},{14,2},{15,3},{16,28},{1... | collective-permute-start | bytes 1572872 | tf_op jit(solution)/shard_map/ppermute | solution.py:181
  109.3 10.0 %collective-permute-start.17 = (bf16[2,256,256]{2,1,0:T(8,128)(2,1)S(1)}, bf16[2,256,256]{2,1,0:T(8,128)(2,1)S(1)}, u32[]{:S(2)}, u32[]{:S(2)}) collective-permute-start(bf16[2,256,256]{2,1,0:T(8,128)(2,1)S(1)} %shard_map.53), channel_id=1, source_target_pairs={{0,4},{1,5},{2,6},{3,7},{4,0},{5,1},{6,2},{7,3},{8,12},{9,13},{10,... | collective-permute-start | bytes 786440 | tf_op jit(solution)/shard_map/ppermute | solution.py:181

commit v18 on v14

--- a/solution.py
+++ b/solution.py
@@ -198,7 +198,7 @@
     own = ([(left_env,), (exchange(left_env, 1, every),)], [(psi,), (exchange(psi, 1, every),)])
     own_0 = products(0, *own, (right_env,))
 
-    near, middle, own_0 = lax.optimization_barrier((near, middle, own_0))
+    middle, near, own_0 = lax.optimization_barrier((middle, near, own_0))
     far_in = exchange(near, 12, inner)
     far_out = exchange(middle, 4, inner)
 

time: 117 us -> 116 us (level)
  transfers between devices with their start and end apart: 20 -> 20, of which waited for: 9 -> 10; matrix products, arithmetic and copies ran while one was open for 0% -> 0% of each run, Pallas kernels for 15% -> 15%
where the time goes in v18:
time: 116 us
  waiting for transfers between devices  68.6 us (59%)
  starting transfers between devices  23.5 us (20%)
  Pallas kernels  18.8 us (16%)
  local copies, waits for them, and re-layouts  4.73 us (4%)
    ppermute x20, waiting for transfers between devices, exchange(): return lax.ppermute(array, 'sec', [(s, s ^ bits) for s in members])  68.6 us
    ppermute x20, starting transfers between devices, exchange(): return lax.ppermute(array, 'sec', [(s, s ^ bits) for s in members])  23.5 us
    pallas_call x8, Pallas kernels, slot(): pl.pallas_call(functools.partial(slot_kernel, step, parts, len(rights)),...  15.1 us
    unnamed x10, local copies, waits for them, and re-layouts  4.73 us
  transfers between devices with their start and end apart: 20, of which 10 were waited for; matrix products, arithmetic and copies ran while one was open for 0% of the time, Pallas kernels for 15%

profile of v18, /device:TPU:0, one launch (start us, length us, event | category | flops | bytes accessed | tf_op | source)
XLA Modules:
  0.0 115.8 jit_solution(11257228670406216395)
XLA Ops:
  0.0 0.5 collective-permute-start.3
  0.5 2.5 %collective-permute-start.4 = (bf16[1,16,256,256]{3,2,1,0:T(8,128)(2,1)}, bf16[1,16,256,256]{3,2,1,0:T(8,128)(2,1)S(1)}, u32[]{:S(2)}, u32[]{:S(2)}) collective-permute-start(bf16[1,16,256,256]{3,2,1,0:T(8,128)(2,1)} %refs_2_.7), channel_id=1, source_target_pairs={{0,2},{1,3},{2,0},{3,1},{4,6},{5,7},{6,4},{7,5},{8,10},{9,11},{10,... | collective-permute-start | bytes 6291464 | tf_op jit(solution)/shard_map/ppermute | solution.py:183
  2.9 0.2 collective-permute-start.2
  3.2 1.6 %collective-permute-start.1 = (bf16[8,1,256,256]{3,2,1,0:T(8,128)(2,1)}, bf16[8,1,256,256]{3,2,1,0:T(8,128)(2,1)S(1)}, u32[]{:S(2)}, u32[]{:S(2)}) collective-permute-start(bf16[8,1,256,256]{3,2,1,0:T(8,128)(2,1)} %refs_6_), channel_id=1, source_target_pairs={{0,4},{1,5},{2,6},{3,7},{4,0},{5,1},{6,2},{7,3},{8,12},{9,13},{10,... | collective-permute-start | bytes 3145736 | tf_op jit(solution)/shard_map/ppermute | solution.py:183
  4.7 0.7 collective-permute-start
  5.5 0.5 collective-permute-done.2.refs_1_
  6.0 1.6 %copy-done = bf16[1,16,256,256]{3,2,1,0:T(8,128)(2,1)S(1)} copy-done((bf16[1,16,256,256]{3,2,1,0:T(8,128)(2,1)S(1)}, bf16[1,16,256,256]{3,2,1,0:T(8,128)(2,1)}, u32[]{:S(2)}) %copy-start) | copy-done | bytes 2097176
  7.5 1.2 %copy-done.1 = bf16[8,1,256,256]{3,2,1,0:T(8,128)(2,1)S(1)} copy-done((bf16[8,1,256,256]{3,2,1,0:T(8,128)(2,1)S(1)}, bf16[8,1,256,256]{3,2,1,0:T(8,128)(2,1)}, u32[]{:S(2)}) %copy-start.1) | copy-done | bytes 1048600
  8.8 1.2 %copy-done.2 = bf16[8,1,256,256]{3,2,1,0:T(8,128)(2,1)S(1)} copy-done((bf16[8,1,256,256]{3,2,1,0:T(8,128)(2,1)S(1)}, bf16[8,1,256,256]{3,2,1,0:T(8,128)(2,1)}, u32[]{:S(2)}) %copy-start.2) | copy-done | bytes 1048600
  10.0 0.7 copy-done.4
  10.7 1.9 %shard_map.46.refs_0_ = bf16[2,256,256]{2,1,0:T(8,128)(2,1)S(1)} custom-call(s32[8,16]{1,0:T(8,128)S(1)} %copy-done.4, bf16[8,1,256,256]{3,2,1,0:T(8,128)(2,1)S(1)} %copy-done.1, bf16[8,1,256,256]{3,2,1,0:T(8,128)(2,1)S(1)} %collective-permute-done.2.refs_1_, bf16[1,16,256,256]{3,2,1,0:T(8,128)(2,1)S(1)} %copy-done, ...), custom_call_target="tpu_custom_call" | custom-call | flops 1 | bytes 1 | tf_op jit(solution)/shard_map/pallas_call | solution.py:99
  12.6 16.2 %collective-permute-done.1.refs_4_.refs_6_ = bf16[8,1,256,256]{3,2,1,0:T(8,128)(2,1)S(1)} collective-permute-done((bf16[8,1,256,256]{3,2,1,0:T(8,128)(2,1)}, bf16[8,1,256,256]{3,2,1,0:T(8,128)(2,1)S(1)}, u32[]{:S(2)}, u32[]{:S(2)}) %collective-permute-start.1) | collective-permute-done | bytes 1048608 | tf_op jit(solution)/shard_map/ppermute | solution.py:183
  28.7 0.0 collective-permute-done.refs_4_.refs_6_
  28.7 1.3 %collective-permute-start.6 = (bf16[8,1,256,256]{3,2,1,0:T(8,128)(2,1)S(1)}, bf16[8,1,256,256]{3,2,1,0:T(8,128)(2,1)S(1)}, u32[]{:S(2)}, u32[]{:S(2)}) collective-permute-start(bf16[8,1,256,256]{3,2,1,0:T(8,128)(2,1)S(1)} %collective-permute-done.refs_4_.refs_6_), channel_id=1, source_target_pairs={{4,0},{5,1},{6,2},{7,3},{8,12},{9,13},{10,14},{11,15},{20,16},{21,... | collective-permute-start | bytes 3145736 | tf_op jit(solution)/shard_map/ppermute | solution.py:183
  30.0 0.7 collective-permute-start.7
  30.8 18.7 %collective-permute-done.4.whole.refs_3_ = bf16[1,16,256,256]{3,2,1,0:T(8,128)(2,1)S(1)} collective-permute-done((bf16[1,16,256,256]{3,2,1,0:T(8,128)(2,1)}, bf16[1,16,256,256]{3,2,1,0:T(8,128)(2,1)S(1)}, u32[]{:S(2)}, u32[]{:S(2)}) %collective-permute-start.4) | collective-permute-done | bytes 2097184 | tf_op jit(solution)/shard_map/ppermute | solution.py:183
  49.5 1.7 %collective-permute-start.5 = (bf16[8,1,256,256]{3,2,1,0:T(8,128)(2,1)S(1)}, bf16[8,1,256,256]{3,2,1,0:T(8,128)(2,1)S(1)}, u32[]{:S(2)}, u32[]{:S(2)}) collective-permute-start(bf16[8,1,256,256]{3,2,1,0:T(8,128)(2,1)S(1)} %copy-done.1), channel_id=1, source_target_pairs={{0,2},{1,3},{2,0},{3,1},{4,6},{5,7},{6,4},{7,5},{8,10},{9,11},{10,... | collective-permute-start | bytes 3145736 | tf_op jit(solution)/shard_map/ppermute | solution.py:183
  51.2 0.1 shard_map.50
  51.3 0.1 collective-permute-start.12
  51.4 1.9 %shard_map.48 = bf16[2,256,256]{2,1,0:T(8,128)(2,1)S(1)} custom-call(s32[8,16]{1,0:T(8,128)S(1)} %copy-done.4, bf16[8,1,256,256]{3,2,1,0:T(8,128)(2,1)S(1)} %copy-done.1, bf16[8,1,256,256]{3,2,1,0:T(8,128)(2,1)S(1)} %collective-permute-done.2.refs_1_, bf16[1,16,256,256]{3,2,1,0:T(8,128)(2,1)S(1)} %copy-done, ...), custom_call_target="tpu_custom_call" | custom-call | flops 1 | bytes 1 | tf_op jit(solution)/shard_map/pallas_call | solution.py:99
  53.3 1.6 %collective-permute-start.8 = (bf16[2,256,256]{2,1,0:T(8,128)(2,1)S(1)}, bf16[2,256,256]{2,1,0:T(8,128)(2,1)S(1)}, u32[]{:S(2)}, u32[]{:S(2)}) collective-permute-start(bf16[2,256,256]{2,1,0:T(8,128)(2,1)S(1)} %shard_map.48), channel_id=1, source_target_pairs={{0,4},{1,5},{2,6},{3,7},{4,0},{5,1},{6,2},{7,3},{8,12},{9,13},{10,... | collective-permute-start | bytes 786440 | tf_op jit(solution)/shard_map/ppermute | solution.py:183
  54.9 3.3 %collective-permute-done.6.refs_4_.refs_6_ = bf16[8,1,256,256]{3,2,1,0:T(8,128)(2,1)S(1)} collective-permute-done((bf16[8,1,256,256]{3,2,1,0:T(8,128)(2,1)S(1)}, bf16[8,1,256,256]{3,2,1,0:T(8,128)(2,1)S(1)}, u32[]{:S(2)}, u32[]{:S(2)}) %collective-permute-start.6) | collective-permute-done | bytes 1048608 | tf_op jit(solution)/shard_map/ppermute | solution.py:183
  58.2 0.0 collective-permute-done.7.refs_5_.refs_7_
  58.2 1.3 %collective-permute-start.14 = (bf16[8,1,256,256]{3,2,1,0:T(8,128)(2,1)S(1)}, bf16[8,1,256,256]{3,2,1,0:T(8,128)(2,1)S(1)}, u32[]{:S(2)}, u32[]{:S(2)}) collective-permute-start(bf16[8,1,256,256]{3,2,1,0:T(8,128)(2,1)S(1)} %collective-permute-done.7.refs_5_.refs_7_), channel_id=1, source_target_pairs={{4,0},{5,1},{6,2},{7,3},{8,12},{9,13},{10,14},{11,15},{20,16},{21,... | collective-permute-start | bytes 3145736 | tf_op jit(solution)/shard_map/ppermute | solution.py:183
  59.5 1.9 %shard_map.47 = bf16[2,256,256]{2,1,0:T(8,128)(2,1)S(1)} custom-call(s32[8,16]{1,0:T(8,128)S(1)} %copy-done.4, bf16[8,1,256,256]{3,2,1,0:T(8,128)(2,1)S(1)} %copy-done.1, bf16[8,1,256,256]{3,2,1,0:T(8,128)(2,1)S(1)} %collective-permute-done.2.refs_1_, bf16[1,16,256,256]{3,2,1,0:T(8,128)(2,1)S(1)} %copy-done, ...), custom_call_target="tpu_custom_call" | custom-call | flops 1 | bytes 1 | tf_op jit(solution)/shard_map/pallas_call | solution.py:99
  61.4 2.4 %collective-permute-done.8.refs_4_ = bf16[2,256,256]{2,1,0:T(8,128)(2,1)S(1)} collective-permute-done((bf16[2,256,256]{2,1,0:T(8,128)(2,1)S(1)}, bf16[2,256,256]{2,1,0:T(8,128)(2,1)S(1)}, u32[]{:S(2)}, u32[]{:S(2)}) %collective-permute-start.8) | collective-permute-done | bytes 262176 | tf_op jit(solution)/shard_map/ppermute | solution.py:183
  63.9 1.4 %collective-permute-start.9 = (bf16[2,256,256]{2,1,0:T(8,128)(2,1)S(1)}, bf16[2,256,256]{2,1,0:T(8,128)(2,1)S(1)}, u32[]{:S(2)}, u32[]{:S(2)}) collective-permute-start(bf16[2,256,256]{2,1,0:T(8,128)(2,1)S(1)} %shard_map.47), channel_id=1, source_target_pairs={{0,8},{1,9},{2,10},{3,11},{4,12},{5,13},{6,14},{7,15},{8,0},{9,1},... | collective-permute-start | bytes 786440 | tf_op jit(solution)/shard_map/ppermute | solution.py:183
  65.3 9.1 %collective-permute-done.5.whole.refs_0_ = bf16[8,1,256,256]{3,2,1,0:T(8,128)(2,1)S(1)} collective-permute-done((bf16[8,1,256,256]{3,2,1,0:T(8,128)(2,1)S(1)}, bf16[8,1,256,256]{3,2,1,0:T(8,128)(2,1)S(1)}, u32[]{:S(2)}, u32[]{:S(2)}) %collective-permute-start.5) | collective-permute-done | bytes 1048608 | tf_op jit(solution)/shard_map/ppermute | solution.py:183
  74.4 2.6 %collective-permute-done.9.refs_2_ = bf16[2,256,256]{2,1,0:T(8,128)(2,1)S(1)} collective-permute-done((bf16[2,256,256]{2,1,0:T(8,128)(2,1)S(1)}, bf16[2,256,256]{2,1,0:T(8,128)(2,1)S(1)}, u32[]{:S(2)}, u32[]{:S(2)}) %collective-permute-start.9) | collective-permute-done | bytes 262176 | tf_op jit(solution)/shard_map/ppermute | solution.py:183
  77.1 0.1 shard_map.49
  77.2 0.1 collective-permute-start.10
  77.2 0.5 collective-permute-start.11
  77.7 1.9 %shard_map.51 = (bf16[2,256,256]{2,1,0:T(8,128)(2,1)S(1)}, bf16[512,2048]{1,0:T(8,128)(2,1)S(1)}) custom-call(s32[8,16]{1,0:T(8,128)S(1)} %copy-done.4, bf16[8,1,256,256]{3,2,1,0:T(8,128)(2,1)S(1)} %copy-done.1, bf16[8,1,256,256]{3,2,1,0:T(8,128)(2,1)S(1)} %collective-permute-done.2.refs_1_, bf16[1,16,256,256]{3,2,1,0:T(8,128)(2,1)S(1)} %copy-done, ...), custom_call_target="tpu_custom_call" | custom-call | flops 1 | bytes 1 | tf_op jit(solution)/shard_map/pallas_call | solution.py:99
  79.6 0.7 collective-permute-start.15
  80.3 1.9 %shard_map.53 = bf16[2,256,256]{2,1,0:T(8,128)(2,1)S(1)} custom-call(s32[8,16]{1,0:T(8,128)S(1)} %copy-done.4, bf16[8,1,256,256]{3,2,1,0:T(8,128)(2,1)S(1)} %collective-permute-done.5.whole.refs_0_, bf16[5,1,256,256]{3,2,1,0:T(8,128)(2,1)S(1)} %collective-permute-done.10.refs_1_, bf16[3,1,256,256]{3,2,1,0:T(8,128)(2,1)S(1)} %collective-permute-done.11.refs_2_, ...), custom_call_target="tpu_custom_call" | custom-call | flops 1 | bytes 1 | tf_op jit(solution)/shard_map/pallas_call | solution.py:99
  82.3 2.9 %collective-permute-start.16 = (bf16[2,256,256]{2,1,0:T(8,128)(2,1)S(1)}, bf16[2,256,256]{2,1,0:T(8,128)(2,1)S(1)}, u32[]{:S(2)}, u32[]{:S(2)}) collective-permute-start(bf16[2,256,256]{2,1,0:T(8,128)(2,1)S(1)} %shard_map.53), channel_id=1, source_target_pairs={{0,8},{1,9},{2,10},{3,11},{4,12},{5,13},{6,14},{7,15},{8,0},{9,1},... | collective-permute-start | bytes 786440 | tf_op jit(solution)/shard_map/ppermute | solution.py:183
  85.1 1.9 %shard_map.54 = bf16[2,256,256]{2,1,0:T(8,128)(2,1)S(1)} custom-call(s32[8,16]{1,0:T(8,128)S(1)} %copy-done.4, bf16[8,1,256,256]{3,2,1,0:T(8,128)(2,1)S(1)} %collective-permute-done.5.whole.refs_0_, bf16[5,1,256,256]{3,2,1,0:T(8,128)(2,1)S(1)} %collective-permute-done.10.refs_1_, bf16[3,1,256,256]{3,2,1,0:T(8,128)(2,1)S(1)} %collective-permute-done.11.refs_2_, ...), custom_call_target="tpu_custom_call" | custom-call | flops 1 | bytes 1 | tf_op jit(solution)/shard_map/pallas_call | solution.py:99
  87.0 0.8 collective-permute-start.17
  87.9 1.9 %shard_map.52 = (bf16[2,256,256]{2,1,0:T(8,128)(2,1)S(1)}, bf16[512,2048]{1,0:T(8,128)(2,1)S(1)}) custom-call(s32[8,16]{1,0:T(8,128)S(1)} %copy-done.4, bf16[8,1,256,256]{3,2,1,0:T(8,128)(2,1)S(1)} %collective-permute-done.5.whole.refs_0_, bf16[5,1,256,256]{3,2,1,0:T(8,128)(2,1)S(1)} %collective-permute-done.10.refs_1_, ...), custom_call_target="tpu_custom_call" | custom-call | flops 1 | bytes 1 | tf_op jit(solution)/shard_map/pallas_call | solution.py:99
  89.7 0.7 collective-permute-start.19
  90.4 1.6 %collective-permute-done.14.refs_2_ = bf16[8,1,256,256]{3,2,1,0:T(8,128)(2,1)S(1)} collective-permute-done((bf16[8,1,256,256]{3,2,1,0:T(8,128)(2,1)S(1)}, bf16[8,1,256,256]{3,2,1,0:T(8,128)(2,1)S(1)}, u32[]{:S(2)}, u32[]{:S(2)}) %collective-permute-start.14) | collective-permute-done | bytes 1048608 | tf_op jit(solution)/shard_map/ppermute | solution.py:183
  92.1 1.3 %shard_map.55 = bf16[4,256,256]{2,1,0:T(8,128)(2,1)S(1)} custom-call(bf16[512,2048]{1,0:T(8,128)(2,1)S(1)} %get-tuple-element.40.refs_0_, bf16[512,2048]{1,0:T(8,128)(2,1)S(1)} %get-tuple-element.41.refs_1_, bf16[8,1,256,256]{3,2,1,0:T(8,128)(2,1)S(1)} %collective-permute-done.14.refs_2_), custom_call_target="tpu_custom_call" | custom-call | flops 10000000000 | bytes 1 | tf_op jit(solution)/shard_map/pallas_call | solution.py:78
  93.4 4.2 %collective-permute-start.18 = (bf16[4,256,256]{2,1,0:T(8,128)(2,1)S(1)}, bf16[4,256,256]{2,1,0:T(8,128)(2,1)S(1)}, u32[]{:S(2)}, u32[]{:S(2)}) collective-permute-start(bf16[4,256,256]{2,1,0:T(8,128)(2,1)S(1)} %shard_map.55), channel_id=1, source_target_pairs={{0,12},{1,13},{2,14},{3,15},{12,0},{13,1},{14,2},{15,3},{16,28},{1... | collective-permute-start | bytes 1572872 | tf_op jit(solution)/shard_map/ppermute | solution.py:183
  97.6 1.9 %shard_map.56.refs_1_ = bf16[2,256,256]{2,1,0:T(8,128)(2,1)S(1)} custom-call(s32[8,16]{1,0:T(8,128)S(1)} %copy-done.4, bf16[8,1,256,256]{3,2,1,0:T(8,128)(2,1)S(1)} %collective-permute-done.5.whole.refs_0_, bf16[5,1,256,256]{3,2,1,0:T(8,128)(2,1)S(1)} %collective-permute-done.10.refs_1_, bf16[3,1,256,256]{3,2,1,0:T(8,128)(2,1)S(1)} %collective-permute-done.11.refs_2_, ...), custom_call_target="tpu_custom_call" | custom-call | flops 1 | bytes 1 | tf_op jit(solution)/shard_map/pallas_call | solution.py:99
  99.5 13.3 %collective-permute-done.16.refs_3_ = bf16[2,256,256]{2,1,0:T(8,128)(2,1)S(1)} collective-permute-done((bf16[2,256,256]{2,1,0:T(8,128)(2,1)S(1)}, bf16[2,256,256]{2,1,0:T(8,128)(2,1)S(1)}, u32[]{:S(2)}, u32[]{:S(2)}) %collective-permute-start.16) | collective-permute-done | bytes 262176 | tf_op jit(solution)/shard_map/ppermute | solution.py:183
  112.8 0.8 collective-permute-done.17.refs_5_
  113.6 1.3 %shard_map.57.refs_0_ = bf16[16,256,256]{2,1,0:T(8,128)(2,1)} custom-call(bf16[2,256,256]{2,1,0:T(8,128)(2,1)S(1)} %shard_map.46.refs_0_, bf16[2,256,256]{2,1,0:T(8,128)(2,1)S(1)} %shard_map.56.refs_1_, bf16[2,256,256]{2,1,0:T(8,128)(2,1)S(1)} %collective-permute-done.9.refs_2_, bf16[2,256,256]{2,1,0:T(8,128)(2,1)S(1)} %collective-permute-done.16.refs_3_, ...), custom_call_target="tpu_custom_call" | custom-call | flops 10000000000 | bytes 1 | tf_op jit(solution)/shard_map/pallas_call | solution.py:170
  114.9 0.9 shard_map.58
  (15 shorter events, 0.0 us)
Async XLA Ops:
  0.0 6.0 %collective-permute-start.3 = (bf16[1,16,256,256]{3,2,1,0:T(8,128)(2,1)}, bf16[1,16,256,256]{3,2,1,0:T(8,128)(2,1)S(1)}, u32[]{:S(2)}, u32[]{:S(2)}) collective-permute-start(bf16[1,16,256,256]{3,2,1,0:T(8,128)(2,1)} %refs_2_.7), channel_id=1, source_target_pairs={{0,1},{1,0},{2,3},{3,2},{4,5},{5,4},{6,7},{7,6},{8,9},{9,8},{10,11... | collective-permute-start | bytes 6291464 | tf_op jit(solution)/shard_map/ppermute | solution.py:183
  0.5 49.0 %collective-permute-start.4 = (bf16[1,16,256,256]{3,2,1,0:T(8,128)(2,1)}, bf16[1,16,256,256]{3,2,1,0:T(8,128)(2,1)S(1)}, u32[]{:S(2)}, u32[]{:S(2)}) collective-permute-start(bf16[1,16,256,256]{3,2,1,0:T(8,128)(2,1)} %refs_2_.7), channel_id=1, source_target_pairs={{0,2},{1,3},{2,0},{3,1},{4,6},{5,7},{6,4},{7,5},{8,10},{9,11},{10,... | collective-permute-start | bytes 6291464 | tf_op jit(solution)/shard_map/ppermute | solution.py:183
  2.9 3.0 %collective-permute-start.2 = (bf16[8,1,256,256]{3,2,1,0:T(8,128)(2,1)}, bf16[8,1,256,256]{3,2,1,0:T(8,128)(2,1)S(1)}, u32[]{:S(2)}, u32[]{:S(2)}) collective-permute-start(bf16[8,1,256,256]{3,2,1,0:T(8,128)(2,1)} %refs_0_.7), channel_id=1, source_target_pairs={{0,1},{1,0},{2,3},{3,2},{4,5},{5,4},{6,7},{7,6},{8,9},{9,8},{10,11... | collective-permute-start | bytes 3145736 | tf_op jit(solution)/shard_map/ppermute | solution.py:183
  3.2 25.6 %collective-permute-start.1 = (bf16[8,1,256,256]{3,2,1,0:T(8,128)(2,1)}, bf16[8,1,256,256]{3,2,1,0:T(8,128)(2,1)S(1)}, u32[]{:S(2)}, u32[]{:S(2)}) collective-permute-start(bf16[8,1,256,256]{3,2,1,0:T(8,128)(2,1)} %refs_6_), channel_id=1, source_target_pairs={{0,4},{1,5},{2,6},{3,7},{4,0},{5,1},{6,2},{7,3},{8,12},{9,13},{10,... | collective-permute-start | bytes 3145736 | tf_op jit(solution)/shard_map/ppermute | solution.py:183
  4.7 24.0 %collective-permute-start = (bf16[8,1,256,256]{3,2,1,0:T(8,128)(2,1)}, bf16[8,1,256,256]{3,2,1,0:T(8,128)(2,1)S(1)}, u32[]{:S(2)}, u32[]{:S(2)}) collective-permute-start(bf16[8,1,256,256]{3,2,1,0:T(8,128)(2,1)} %refs_6_), channel_id=1, source_target_pairs={{4,8},{5,9},{6,10},{7,11},{8,4},{9,5},{10,6},{11,7},{20,24},{21,25... | collective-permute-start | bytes 3145736 | tf_op jit(solution)/shard_map/ppermute | solution.py:183
  6.0 1.6 %copy-start = (bf16[1,16,256,256]{3,2,1,0:T(8,128)(2,1)S(1)}, bf16[1,16,256,256]{3,2,1,0:T(8,128)(2,1)}, u32[]{:S(2)}) copy-start(bf16[1,16,256,256]{3,2,1,0:T(8,128)(2,1)} %refs_2_.7) | copy-start | bytes 6291460
  7.5 1.2 %copy-start.1 = (bf16[8,1,256,256]{3,2,1,0:T(8,128)(2,1)S(1)}, bf16[8,1,256,256]{3,2,1,0:T(8,128)(2,1)}, u32[]{:S(2)}) copy-start(bf16[8,1,256,256]{3,2,1,0:T(8,128)(2,1)} %refs_0_.7) | copy-start | bytes 3145732
  8.8 1.2 %copy-start.2 = (bf16[8,1,256,256]{3,2,1,0:T(8,128)(2,1)S(1)}, bf16[8,1,256,256]{3,2,1,0:T(8,128)(2,1)}, u32[]{:S(2)}) copy-start(bf16[8,1,256,256]{3,2,1,0:T(8,128)(2,1)} %refs_6_) | copy-start | bytes 3145732
  10.0 0.7 copy-start.4
  28.7 29.5 %collective-permute-start.6 = (bf16[8,1,256,256]{3,2,1,0:T(8,128)(2,1)S(1)}, bf16[8,1,256,256]{3,2,1,0:T(8,128)(2,1)S(1)}, u32[]{:S(2)}, u32[]{:S(2)}) collective-permute-start(bf16[8,1,256,256]{3,2,1,0:T(8,128)(2,1)S(1)} %collective-permute-done.refs_4_.refs_6_), channel_id=1, source_target_pairs={{4,0},{5,1},{6,2},{7,3},{8,12},{9,13},{10,14},{11,15},{20,16},{21,... | collective-permute-start | bytes 3145736 | tf_op jit(solution)/shard_map/ppermute | solution.py:183
  30.0 28.2 %collective-permute-start.7 = (bf16[8,1,256,256]{3,2,1,0:T(8,128)(2,1)S(1)}, bf16[8,1,256,256]{3,2,1,0:T(8,128)(2,1)S(1)}, u32[]{:S(2)}, u32[]{:S(2)}) collective-permute-start(bf16[8,1,256,256]{3,2,1,0:T(8,128)(2,1)S(1)} %collective-permute-done.1.refs_4_.refs_6_), channel_id=1, source_target_pairs={{4,8},{5,9},{6,10},{7,11},{8,4},{9,5},{10,6},{11,7},{20,24},{21,25... | collective-permute-start | bytes 3145736 | tf_op jit(solution)/shard_map/ppermute | solution.py:183
  49.5 25.0 %collective-permute-start.5 = (bf16[8,1,256,256]{3,2,1,0:T(8,128)(2,1)S(1)}, bf16[8,1,256,256]{3,2,1,0:T(8,128)(2,1)S(1)}, u32[]{:S(2)}, u32[]{:S(2)}) collective-permute-start(bf16[8,1,256,256]{3,2,1,0:T(8,128)(2,1)S(1)} %copy-done.1), channel_id=1, source_target_pairs={{0,2},{1,3},{2,0},{3,1},{4,6},{5,7},{6,4},{7,5},{8,10},{9,11},{10,... | collective-permute-start | bytes 3145736 | tf_op jit(solution)/shard_map/ppermute | solution.py:183
  51.3 29.0 %collective-permute-start.12 = (bf16[1,12,256,256]{3,2,1,0:T(8,128)(2,1)S(1)}, bf16[1,12,256,256]{3,2,1,0:T(8,128)(2,1)S(1)}, u32[]{:S(2)}, u32[]{:S(2)}) collective-permute-start(bf16[1,12,256,256]{3,2,1,0:T(8,128)(2,1)S(1)} %get-tuple-element.38), channel_id=1, source_target_pairs={{0,1},{1,0},{2,3},{3,2},{4,5},{5,4},{6,7},{7,6},{8,9},{9,8},{10,11... | collective-permute-start | bytes 4718600 | tf_op jit(solution)/shard_map/ppermute | solution.py:183
  53.3 10.6 %collective-permute-start.8 = (bf16[2,256,256]{2,1,0:T(8,128)(2,1)S(1)}, bf16[2,256,256]{2,1,0:T(8,128)(2,1)S(1)}, u32[]{:S(2)}, u32[]{:S(2)}) collective-permute-start(bf16[2,256,256]{2,1,0:T(8,128)(2,1)S(1)} %shard_map.48), channel_id=1, source_target_pairs={{0,4},{1,5},{2,6},{3,7},{4,0},{5,1},{6,2},{7,3},{8,12},{9,13},{10,... | collective-permute-start | bytes 786440 | tf_op jit(solution)/shard_map/ppermute | solution.py:183
  58.2 33.8 %collective-permute-start.14 = (bf16[8,1,256,256]{3,2,1,0:T(8,128)(2,1)S(1)}, bf16[8,1,256,256]{3,2,1,0:T(8,128)(2,1)S(1)}, u32[]{:S(2)}, u32[]{:S(2)}) collective-permute-start(bf16[8,1,256,256]{3,2,1,0:T(8,128)(2,1)S(1)} %collective-permute-done.7.refs_5_.refs_7_), channel_id=1, source_target_pairs={{4,0},{5,1},{6,2},{7,3},{8,12},{9,13},{10,14},{11,15},{20,16},{21,... | collective-permute-start | bytes 3145736 | tf_op jit(solution)/shard_map/ppermute | solution.py:183
  63.9 13.2 %collective-permute-start.9 = (bf16[2,256,256]{2,1,0:T(8,128)(2,1)S(1)}, bf16[2,256,256]{2,1,0:T(8,128)(2,1)S(1)}, u32[]{:S(2)}, u32[]{:S(2)}) collective-permute-start(bf16[2,256,256]{2,1,0:T(8,128)(2,1)S(1)} %shard_map.47), channel_id=1, source_target_pairs={{0,8},{1,9},{2,10},{3,11},{4,12},{5,13},{6,14},{7,15},{8,0},{9,1},... | collective-permute-start | bytes 786440 | tf_op jit(solution)/shard_map/ppermute | solution.py:183
  65.3 14.3 %collective-permute-start.13 = (bf16[1,4,256,256]{3,2,1,0:T(8,128)(2,1)S(1)}, bf16[1,4,256,256]{3,2,1,0:T(8,128)(2,1)S(1)}, u32[]{:S(2)}, u32[]{:S(2)}) collective-permute-start(bf16[1,4,256,256]{3,2,1,0:T(8,128)(2,1)S(1)} %get-tuple-element.39), channel_id=1, source_target_pairs={{0,1},{1,0},{2,3},{3,2},{4,5},{5,4},{6,7},{7,6},{8,9},{9,8},{10,11... | collective-permute-start | bytes 1572872 | tf_op jit(solution)/shard_map/ppermute | solution.py:183
  77.2 3.2 %collective-permute-start.10 = (bf16[5,1,256,256]{3,2,1,0:T(8,128)(2,1)S(1)}, bf16[5,1,256,256]{3,2,1,0:T(8,128)(2,1)S(1)}, u32[]{:S(2)}, u32[]{:S(2)}) collective-permute-start(bf16[5,1,256,256]{3,2,1,0:T(8,128)(2,1)S(1)} %get-tuple-element.35), channel_id=1, source_target_pairs={{0,1},{1,0},{2,3},{3,2},{4,5},{5,4},{6,7},{7,6},{8,9},{9,8},{10,11... | collective-permute-start | bytes 1966088 | tf_op jit(solution)/shard_map/ppermute | solution.py:183
  77.2 3.1 %collective-permute-start.11 = (bf16[3,1,256,256]{3,2,1,0:T(8,128)(2,1)S(1)}, bf16[3,1,256,256]{3,2,1,0:T(8,128)(2,1)S(1)}, u32[]{:S(2)}, u32[]{:S(2)}) collective-permute-start(bf16[3,1,256,256]{3,2,1,0:T(8,128)(2,1)S(1)} %get-tuple-element.36), channel_id=1, source_target_pairs={{0,1},{1,0},{2,3},{3,2},{4,5},{5,4},{6,7},{7,6},{8,9},{9,8},{10,11... | collective-permute-start | bytes 1179656 | tf_op jit(solution)/shard_map/ppermute | solution.py:183
  79.6 10.8 %collective-permute-start.15 = (bf16[2,256,256]{2,1,0:T(8,128)(2,1)S(1)}, bf16[2,256,256]{2,1,0:T(8,128)(2,1)S(1)}, u32[]{:S(2)}, u32[]{:S(2)}) collective-permute-start(bf16[2,256,256]{2,1,0:T(8,128)(2,1)S(1)} %get-tuple-element.43), channel_id=1, source_target_pairs={{4,8},{5,9},{6,10},{7,11},{8,4},{9,5},{10,6},{11,7},{20,24},{21,25... | collective-permute-start | bytes 786440 | tf_op jit(solution)/shard_map/ppermute | solution.py:183
  82.3 30.5 %collective-permute-start.16 = (bf16[2,256,256]{2,1,0:T(8,128)(2,1)S(1)}, bf16[2,256,256]{2,1,0:T(8,128)(2,1)S(1)}, u32[]{:S(2)}, u32[]{:S(2)}) collective-permute-start(bf16[2,256,256]{2,1,0:T(8,128)(2,1)S(1)} %shard_map.53), channel_id=1, source_target_pairs={{0,8},{1,9},{2,10},{3,11},{4,12},{5,13},{6,14},{7,15},{8,0},{9,1},... | collective-permute-start | bytes 786440 | tf_op jit(solution)/shard_map/ppermute | solution.py:183
  87.0 26.5 %collective-permute-start.17 = (bf16[2,256,256]{2,1,0:T(8,128)(2,1)S(1)}, bf16[2,256,256]{2,1,0:T(8,128)(2,1)S(1)}, u32[]{:S(2)}, u32[]{:S(2)}) collective-permute-start(bf16[2,256,256]{2,1,0:T(8,128)(2,1)S(1)} %shard_map.54), channel_id=1, source_target_pairs={{0,4},{1,5},{2,6},{3,7},{4,0},{5,1},{6,2},{7,3},{8,12},{9,13},{10,... | collective-permute-start | bytes 786440 | tf_op jit(solution)/shard_map/ppermute | solution.py:183
  89.7 25.1 %collective-permute-start.19 = (bf16[2,256,256]{2,1,0:T(8,128)(2,1)S(1)}, bf16[2,256,256]{2,1,0:T(8,128)(2,1)S(1)}, u32[]{:S(2)}, u32[]{:S(2)}) collective-permute-start(bf16[2,256,256]{2,1,0:T(8,128)(2,1)S(1)} %get-tuple-element.42), channel_id=1, source_target_pairs={{4,8},{5,9},{6,10},{7,11},{8,4},{9,5},{10,6},{11,7},{20,24},{21,25... | collective-permute-start | bytes 786440 | tf_op jit(solution)/shard_map/ppermute | solution.py:183
  92.1 5.5 %copy-start.3 = (bf16[8,1,256,256]{3,2,1,0:T(8,128)(2,1)S(1)}, bf16[8,1,256,256]{3,2,1,0:T(8,128)(2,1)}, u32[]{:S(2)}) copy-start(bf16[8,1,256,256]{3,2,1,0:T(8,128)(2,1)} %refs_6_) | copy-start | bytes 3145732
  93.4 21.5 %collective-permute-start.18 = (bf16[4,256,256]{2,1,0:T(8,128)(2,1)S(1)}, bf16[4,256,256]{2,1,0:T(8,128)(2,1)S(1)}, u32[]{:S(2)}, u32[]{:S(2)}) collective-permute-start(bf16[4,256,256]{2,1,0:T(8,128)(2,1)S(1)} %shard_map.55), channel_id=1, source_target_pairs={{0,12},{1,13},{2,14},{3,15},{12,0},{13,1},{14,2},{15,3},{16,28},{1... | collective-permute-start | bytes 1572872 | tf_op jit(solution)/shard_map/ppermute | solution.py:183

commit v19 on v16

--- a/solution.py
+++ b/solution.py
@@ -226,7 +226,7 @@
     other_1 = products(1, *other, (near,))
     other_sent_1 = exchange(other_1, 4, every)
 
-    third, other_1, other_2, other_middle = lax.optimization_barrier((third, other_1, other_2, other_middle))
+    third, other_1, other_2, sent_other_middle = lax.optimization_barrier((third, other_1, other_2, sent_other_middle))
     last_third = second((own_mid, other_mid), third, dtype, 10**10)
     sent_third = exchange(last_third, 12, outer)
     right_last, last_third = lax.optimization_barrier((right_env, last_third))

time: 120 us -> 124 us (1.033)
  waiting for transfers between devices: 70.8 us -> 76 us
    ppermute x20, waiting for transfers between devices: 70.8 us -> 76 us  [exchange(): return lax.ppermute(array, 'sec', [(s, s ^ bits) for s in members])]
  transfers between devices with their start and end apart: 20 -> 20, of which waited for: 10 -> 10; matrix products, arithmetic and copies ran while one was open for 0% -> 0% of each run, Pallas kernels for 15% -> 14%
where the time goes in v19:
time: 124 us
  waiting for transfers between devices  76 us (61%)
  starting transfers between devices  24.3 us (20%)
  Pallas kernels  18.8 us (15%)
  local copies, waits for them, and re-layouts  4.73 us (4%)
    ppermute x20, waiting for transfers between devices, exchange(): return lax.ppermute(array, 'sec', [(s, s ^ bits) for s in members])  76 us
    ppermute x20, starting transfers between devices, exchange(): return lax.ppermute(array, 'sec', [(s, s ^ bits) for s in members])  24.3 us
    pallas_call x8, Pallas kernels, slot(): pl.pallas_call(functools.partial(slot_kernel, step, parts, len(rights)),...  15.1 us
    unnamed x10, local copies, waits for them, and re-layouts  4.73 us
  transfers between devices with their start and end apart: 20, of which 10 were waited for; matrix products, arithmetic and copies ran while one was open for 0% of the time, Pallas kernels for 14%

profile of v19, /device:TPU:0, one launch (start us, length us, event | category | flops | bytes accessed | tf_op | source)
XLA Modules:
  0.0 124.1 jit_solution(13700420333222540573)
XLA Ops:
  0.0 0.5 collective-permute-start.3
  0.5 2.5 %collective-permute-start.4 = (bf16[1,16,256,256]{3,2,1,0:T(8,128)(2,1)}, bf16[1,16,256,256]{3,2,1,0:T(8,128)(2,1)S(1)}, u32[]{:S(2)}, u32[]{:S(2)}) collective-permute-start(bf16[1,16,256,256]{3,2,1,0:T(8,128)(2,1)} %refs_2_.7), channel_id=1, source_target_pairs={{0,2},{1,3},{2,0},{3,1},{4,6},{5,7},{6,4},{7,5},{8,10},{9,11},{10,... | collective-permute-start | bytes 6291464 | tf_op jit(solution)/shard_map/ppermute | solution.py:183
  2.9 0.2 collective-permute-start.2
  3.2 1.6 %collective-permute-start = (bf16[8,1,256,256]{3,2,1,0:T(8,128)(2,1)}, bf16[8,1,256,256]{3,2,1,0:T(8,128)(2,1)S(1)}, u32[]{:S(2)}, u32[]{:S(2)}) collective-permute-start(bf16[8,1,256,256]{3,2,1,0:T(8,128)(2,1)} %refs_6_), channel_id=1, source_target_pairs={{0,4},{1,5},{2,6},{3,7},{4,0},{5,1},{6,2},{7,3},{8,12},{9,13},{10,... | collective-permute-start | bytes 3145736 | tf_op jit(solution)/shard_map/ppermute | solution.py:183
  4.7 0.7 collective-permute-start.1
  5.5 0.5 collective-permute-done.2.refs_1_
  6.0 1.6 %copy-done = bf16[1,16,256,256]{3,2,1,0:T(8,128)(2,1)S(1)} copy-done((bf16[1,16,256,256]{3,2,1,0:T(8,128)(2,1)S(1)}, bf16[1,16,256,256]{3,2,1,0:T(8,128)(2,1)}, u32[]{:S(2)}) %copy-start) | copy-done | bytes 2097176
  7.5 1.2 copy-done.1
  8.8 1.2 copy-done.2
  10.0 0.7 copy-done.4
  10.7 1.9 %shard_map.46.refs_0_ = bf16[2,256,256]{2,1,0:T(8,128)(2,1)S(1)} custom-call(s32[8,16]{1,0:T(8,128)S(1)} %copy-done.4, bf16[8,1,256,256]{3,2,1,0:T(8,128)(2,1)S(1)} %copy-done.1, bf16[8,1,256,256]{3,2,1,0:T(8,128)(2,1)S(1)} %collective-permute-done.2.refs_1_, bf16[1,16,256,256]{3,2,1,0:T(8,128)(2,1)S(1)} %copy-done, ...), custom_call_target="tpu_custom_call" | custom-call | flops 1 | bytes 1 | tf_op jit(solution)/shard_map/pallas_call | solution.py:99
  12.6 16.2 %collective-permute-done.refs_4_.refs_6_ = bf16[8,1,256,256]{3,2,1,0:T(8,128)(2,1)S(1)} collective-permute-done((bf16[8,1,256,256]{3,2,1,0:T(8,128)(2,1)}, bf16[8,1,256,256]{3,2,1,0:T(8,128)(2,1)S(1)}, u32[]{:S(2)}, u32[]{:S(2)}) %collective-permute-start) | collective-permute-done | bytes 1048608 | tf_op jit(solution)/shard_map/ppermute | solution.py:183
  28.7 0.0 collective-permute-done.1.refs_4_.refs_6_
  28.7 1.3 %collective-permute-start.6 = (bf16[8,1,256,256]{3,2,1,0:T(8,128)(2,1)S(1)}, bf16[8,1,256,256]{3,2,1,0:T(8,128)(2,1)S(1)}, u32[]{:S(2)}, u32[]{:S(2)}) collective-permute-start(bf16[8,1,256,256]{3,2,1,0:T(8,128)(2,1)S(1)} %collective-permute-done.1.refs_4_.refs_6_), channel_id=1, source_target_pairs={{4,0},{5,1},{6,2},{7,3},{8,12},{9,13},{10,14},{11,15},{20,16},{21,... | collective-permute-start | bytes 3145736 | tf_op jit(solution)/shard_map/ppermute | solution.py:183
  30.0 0.7 collective-permute-start.7
  30.8 1.9 %shard_map.48 = (bf16[2,256,256]{2,1,0:T(8,128)(2,1)S(1)}, bf16[512,2048]{1,0:T(8,128)(2,1)S(1)}) custom-call(s32[8,16]{1,0:T(8,128)S(1)} %copy-done.4, bf16[8,1,256,256]{3,2,1,0:T(8,128)(2,1)S(1)} %copy-done.1, bf16[8,1,256,256]{3,2,1,0:T(8,128)(2,1)S(1)} %collective-permute-done.2.refs_1_, bf16[1,16,256,256]{3,2,1,0:T(8,128)(2,1)S(1)} %copy-done, ...), custom_call_target="tpu_custom_call" | custom-call | flops 1 | bytes 1 | tf_op jit(solution)/shard_map/pallas_call | solution.py:99
  32.6 1.9 %shard_map.47 = bf16[2,256,256]{2,1,0:T(8,128)(2,1)S(1)} custom-call(s32[8,16]{1,0:T(8,128)S(1)} %copy-done.4, bf16[8,1,256,256]{3,2,1,0:T(8,128)(2,1)S(1)} %copy-done.1, bf16[8,1,256,256]{3,2,1,0:T(8,128)(2,1)S(1)} %collective-permute-done.2.refs_1_, bf16[1,16,256,256]{3,2,1,0:T(8,128)(2,1)S(1)} %copy-done, ...), custom_call_target="tpu_custom_call" | custom-call | flops 1 | bytes 1 | tf_op jit(solution)/shard_map/pallas_call | solution.py:99
  34.5 14.9 %collective-permute-done.4.whole.refs_3_ = bf16[1,16,256,256]{3,2,1,0:T(8,128)(2,1)S(1)} collective-permute-done((bf16[1,16,256,256]{3,2,1,0:T(8,128)(2,1)}, bf16[1,16,256,256]{3,2,1,0:T(8,128)(2,1)S(1)}, u32[]{:S(2)}, u32[]{:S(2)}) %collective-permute-start.4) | collective-permute-done | bytes 2097184 | tf_op jit(solution)/shard_map/ppermute | solution.py:183
  49.5 1.7 %collective-permute-start.5 = (bf16[8,1,256,256]{3,2,1,0:T(8,128)(2,1)S(1)}, bf16[8,1,256,256]{3,2,1,0:T(8,128)(2,1)S(1)}, u32[]{:S(2)}, u32[]{:S(2)}) collective-permute-start(bf16[8,1,256,256]{3,2,1,0:T(8,128)(2,1)S(1)} %copy-done.1), channel_id=1, source_target_pairs={{0,2},{1,3},{2,0},{3,1},{4,6},{5,7},{6,4},{7,5},{8,10},{9,11},{10,... | collective-permute-start | bytes 3145736 | tf_op jit(solution)/shard_map/ppermute | solution.py:183
  51.2 1.6 %collective-permute-start.8 = (bf16[2,256,256]{2,1,0:T(8,128)(2,1)S(1)}, bf16[2,256,256]{2,1,0:T(8,128)(2,1)S(1)}, u32[]{:S(2)}, u32[]{:S(2)}) collective-permute-start(bf16[2,256,256]{2,1,0:T(8,128)(2,1)S(1)} %shard_map.47), channel_id=1, source_target_pairs={{0,4},{1,5},{2,6},{3,7},{4,0},{5,1},{6,2},{7,3},{8,12},{9,13},{10,... | collective-permute-start | bytes 786440 | tf_op jit(solution)/shard_map/ppermute | solution.py:183
  52.8 0.7 collective-permute-start.9
  53.4 0.1 shard_map.51
  53.6 5.0 %collective-permute-done.6.refs_4_.refs_6_ = bf16[8,1,256,256]{3,2,1,0:T(8,128)(2,1)S(1)} collective-permute-done((bf16[8,1,256,256]{3,2,1,0:T(8,128)(2,1)S(1)}, bf16[8,1,256,256]{3,2,1,0:T(8,128)(2,1)S(1)}, u32[]{:S(2)}, u32[]{:S(2)}) %collective-permute-start.6) | collective-permute-done | bytes 1048608 | tf_op jit(solution)/shard_map/ppermute | solution.py:183
  58.6 1.9 %shard_map.49 = bf16[2,256,256]{2,1,0:T(8,128)(2,1)S(1)} custom-call(s32[8,16]{1,0:T(8,128)S(1)} %copy-done.4, bf16[8,1,256,256]{3,2,1,0:T(8,128)(2,1)S(1)} %copy-done.1, bf16[8,1,256,256]{3,2,1,0:T(8,128)(2,1)S(1)} %collective-permute-done.2.refs_1_, bf16[1,16,256,256]{3,2,1,0:T(8,128)(2,1)S(1)} %copy-done, ...), custom_call_target="tpu_custom_call" | custom-call | flops 1 | bytes 1 | tf_op jit(solution)/shard_map/pallas_call | solution.py:99
  60.5 2.5 %collective-permute-done.8.refs_4_ = bf16[2,256,256]{2,1,0:T(8,128)(2,1)S(1)} collective-permute-done((bf16[2,256,256]{2,1,0:T(8,128)(2,1)S(1)}, bf16[2,256,256]{2,1,0:T(8,128)(2,1)S(1)}, u32[]{:S(2)}, u32[]{:S(2)}) %collective-permute-start.8) | collective-permute-done | bytes 262176 | tf_op jit(solution)/shard_map/ppermute | solution.py:183
  63.0 0.0 collective-permute-done.9.refs_2_
  63.0 4.6 %collective-permute-start.10 = (bf16[2,256,256]{2,1,0:T(8,128)(2,1)S(1)}, bf16[2,256,256]{2,1,0:T(8,128)(2,1)S(1)}, u32[]{:S(2)}, u32[]{:S(2)}) collective-permute-start(bf16[2,256,256]{2,1,0:T(8,128)(2,1)S(1)} %shard_map.49), channel_id=1, source_target_pairs={{0,8},{1,9},{2,10},{3,11},{4,12},{5,13},{6,14},{7,15},{8,0},{9,1},... | collective-permute-start | bytes 786440 | tf_op jit(solution)/shard_map/ppermute | solution.py:183
  67.6 0.0 collective-permute-start.14
  67.6 1.3 %collective-permute-start.15 = (bf16[8,1,256,256]{3,2,1,0:T(8,128)(2,1)S(1)}, bf16[8,1,256,256]{3,2,1,0:T(8,128)(2,1)S(1)}, u32[]{:S(2)}, u32[]{:S(2)}) collective-permute-start(bf16[8,1,256,256]{3,2,1,0:T(8,128)(2,1)S(1)} %collective-permute-done.7.refs_5_.refs_7_), channel_id=1, source_target_pairs={{4,0},{5,1},{6,2},{7,3},{8,12},{9,13},{10,14},{11,15},{20,16},{21,... | collective-permute-start | bytes 3145736 | tf_op jit(solution)/shard_map/ppermute | solution.py:183
  68.9 5.6 %collective-permute-done.5.whole.refs_0_ = bf16[8,1,256,256]{3,2,1,0:T(8,128)(2,1)S(1)} collective-permute-done((bf16[8,1,256,256]{3,2,1,0:T(8,128)(2,1)S(1)}, bf16[8,1,256,256]{3,2,1,0:T(8,128)(2,1)S(1)}, u32[]{:S(2)}, u32[]{:S(2)}) %collective-permute-start.5) | collective-permute-done | bytes 1048608 | tf_op jit(solution)/shard_map/ppermute | solution.py:183
  74.4 3.6 %collective-permute-done.10.refs_2_ = bf16[2,256,256]{2,1,0:T(8,128)(2,1)S(1)} collective-permute-done((bf16[2,256,256]{2,1,0:T(8,128)(2,1)S(1)}, bf16[2,256,256]{2,1,0:T(8,128)(2,1)S(1)}, u32[]{:S(2)}, u32[]{:S(2)}) %collective-permute-start.10) | collective-permute-done | bytes 262176 | tf_op jit(solution)/shard_map/ppermute | solution.py:183
  78.0 0.1 shard_map.50
  78.1 0.1 collective-permute-start.11
  78.2 0.5 collective-permute-start.12
  78.7 2.1 %collective-permute-done.12.refs_2_ = bf16[3,1,256,256]{3,2,1,0:T(8,128)(2,1)S(1)} collective-permute-done((bf16[3,1,256,256]{3,2,1,0:T(8,128)(2,1)S(1)}, bf16[3,1,256,256]{3,2,1,0:T(8,128)(2,1)S(1)}, u32[]{:S(2)}, u32[]{:S(2)}) %collective-permute-start.12) | collective-permute-done | bytes 393248 | tf_op jit(solution)/shard_map/ppermute | solution.py:183
  80.8 1.9 %shard_map.52 = (bf16[2,256,256]{2,1,0:T(8,128)(2,1)S(1)}, bf16[512,2048]{1,0:T(8,128)(2,1)S(1)}) custom-call(s32[8,16]{1,0:T(8,128)S(1)} %copy-done.4, bf16[8,1,256,256]{3,2,1,0:T(8,128)(2,1)S(1)} %collective-permute-done.5.whole.refs_0_, bf16[5,1,256,256]{3,2,1,0:T(8,128)(2,1)S(1)} %collective-permute-done.11.refs_1_, ...), custom_call_target="tpu_custom_call" | custom-call | flops 1 | bytes 1 | tf_op jit(solution)/shard_map/pallas_call | solution.py:99
  82.7 0.7 collective-permute-start.16
  83.4 1.9 %shard_map.54 = bf16[2,256,256]{2,1,0:T(8,128)(2,1)S(1)} custom-call(s32[8,16]{1,0:T(8,128)S(1)} %copy-done.4, bf16[8,1,256,256]{3,2,1,0:T(8,128)(2,1)S(1)} %collective-permute-done.5.whole.refs_0_, bf16[5,1,256,256]{3,2,1,0:T(8,128)(2,1)S(1)} %collective-permute-done.11.refs_1_, bf16[3,1,256,256]{3,2,1,0:T(8,128)(2,1)S(1)} %collective-permute-done.12.refs_2_, ...), custom_call_target="tpu_custom_call" | custom-call | flops 1 | bytes 1 | tf_op jit(solution)/shard_map/pallas_call | solution.py:99
  85.3 1.7 %collective-permute-start.17 = (bf16[2,256,256]{2,1,0:T(8,128)(2,1)S(1)}, bf16[2,256,256]{2,1,0:T(8,128)(2,1)S(1)}, u32[]{:S(2)}, u32[]{:S(2)}) collective-permute-start(bf16[2,256,256]{2,1,0:T(8,128)(2,1)S(1)} %shard_map.54), channel_id=1, source_target_pairs={{0,8},{1,9},{2,10},{3,11},{4,12},{5,13},{6,14},{7,15},{8,0},{9,1},... | collective-permute-start | bytes 786440 | tf_op jit(solution)/shard_map/ppermute | solution.py:183
  87.0 1.9 %shard_map.53 = bf16[2,256,256]{2,1,0:T(8,128)(2,1)S(1)} custom-call(s32[8,16]{1,0:T(8,128)S(1)} %copy-done.4, bf16[8,1,256,256]{3,2,1,0:T(8,128)(2,1)S(1)} %collective-permute-done.5.whole.refs_0_, bf16[5,1,256,256]{3,2,1,0:T(8,128)(2,1)S(1)} %collective-permute-done.11.refs_1_, bf16[3,1,256,256]{3,2,1,0:T(8,128)(2,1)S(1)} %collective-permute-done.12.refs_2_, ...), custom_call_target="tpu_custom_call" | custom-call | flops 1 | bytes 1 | tf_op jit(solution)/shard_map/pallas_call | solution.py:99
  88.9 0.8 collective-permute-start.18
  89.7 15.3 %collective-permute-done.15.refs_2_ = bf16[8,1,256,256]{3,2,1,0:T(8,128)(2,1)S(1)} collective-permute-done((bf16[8,1,256,256]{3,2,1,0:T(8,128)(2,1)S(1)}, bf16[8,1,256,256]{3,2,1,0:T(8,128)(2,1)S(1)}, u32[]{:S(2)}, u32[]{:S(2)}) %collective-permute-start.15) | collective-permute-done | bytes 1048608 | tf_op jit(solution)/shard_map/ppermute | solution.py:183
  105.0 1.3 %shard_map.55 = bf16[4,256,256]{2,1,0:T(8,128)(2,1)S(1)} custom-call(bf16[512,2048]{1,0:T(8,128)(2,1)S(1)} %get-tuple-element.46.refs_0_, bf16[512,2048]{1,0:T(8,128)(2,1)S(1)} %get-tuple-element.47.refs_1_, bf16[8,1,256,256]{3,2,1,0:T(8,128)(2,1)S(1)} %collective-permute-done.15.refs_2_), custom_call_target="tpu_custom_call" | custom-call | flops 10000000000 | bytes 1 | tf_op jit(solution)/shard_map/pallas_call | solution.py:78
  106.3 3.2 %collective-permute-start.19 = (bf16[4,256,256]{2,1,0:T(8,128)(2,1)S(1)}, bf16[4,256,256]{2,1,0:T(8,128)(2,1)S(1)}, u32[]{:S(2)}, u32[]{:S(2)}) collective-permute-start(bf16[4,256,256]{2,1,0:T(8,128)(2,1)S(1)} %shard_map.55), channel_id=1, source_target_pairs={{0,12},{1,13},{2,14},{3,15},{12,0},{13,1},{14,2},{15,3},{16,28},{1... | collective-permute-start | bytes 1572872 | tf_op jit(solution)/shard_map/ppermute | solution.py:183
  109.6 1.9 %shard_map.56.refs_1_ = bf16[2,256,256]{2,1,0:T(8,128)(2,1)S(1)} custom-call(s32[8,16]{1,0:T(8,128)S(1)} %copy-done.4, bf16[8,1,256,256]{3,2,1,0:T(8,128)(2,1)S(1)} %collective-permute-done.5.whole.refs_0_, bf16[5,1,256,256]{3,2,1,0:T(8,128)(2,1)S(1)} %collective-permute-done.11.refs_1_, bf16[3,1,256,256]{3,2,1,0:T(8,128)(2,1)S(1)} %collective-permute-done.12.refs_2_, ...), custom_call_target="tpu_custom_call" | custom-call | flops 1 | bytes 1 | tf_op jit(solution)/shard_map/pallas_call | solution.py:99
  111.5 1.3 %shard_map.57.refs_0_ = bf16[16,256,256]{2,1,0:T(8,128)(2,1)} custom-call(bf16[2,256,256]{2,1,0:T(8,128)(2,1)S(1)} %shard_map.46.refs_0_, bf16[2,256,256]{2,1,0:T(8,128)(2,1)S(1)} %shard_map.56.refs_1_, bf16[2,256,256]{2,1,0:T(8,128)(2,1)S(1)} %collective-permute-done.10.refs_2_, bf16[2,256,256]{2,1,0:T(8,128)(2,1)S(1)} %collective-permute-done.17.refs_3_, ...), custom_call_target="tpu_custom_call" | custom-call | flops 10000000000 | bytes 1 | tf_op jit(solution)/shard_map/pallas_call | solution.py:170
  112.8 10.4 %collective-permute-done.19.refs_1_ = bf16[4,256,256]{2,1,0:T(8,128)(2,1)S(1)} collective-permute-done((bf16[4,256,256]{2,1,0:T(8,128)(2,1)S(1)}, bf16[4,256,256]{2,1,0:T(8,128)(2,1)S(1)}, u32[]{:S(2)}, u32[]{:S(2)}) %collective-permute-start.19) | collective-permute-done | bytes 524320 | tf_op jit(solution)/shard_map/ppermute | solution.py:183
  123.2 0.9 shard_map.58
  (15 shorter events, 0.0 us)
Async XLA Ops:
  0.0 6.0 %collective-permute-start.3 = (bf16[1,16,256,256]{3,2,1,0:T(8,128)(2,1)}, bf16[1,16,256,256]{3,2,1,0:T(8,128)(2,1)S(1)}, u32[]{:S(2)}, u32[]{:S(2)}) collective-permute-start(bf16[1,16,256,256]{3,2,1,0:T(8,128)(2,1)} %refs_2_.7), channel_id=1, source_target_pairs={{0,1},{1,0},{2,3},{3,2},{4,5},{5,4},{6,7},{7,6},{8,9},{9,8},{10,11... | collective-permute-start | bytes 6291464 | tf_op jit(solution)/shard_map/ppermute | solution.py:183
  0.5 49.0 %collective-permute-start.4 = (bf16[1,16,256,256]{3,2,1,0:T(8,128)(2,1)}, bf16[1,16,256,256]{3,2,1,0:T(8,128)(2,1)S(1)}, u32[]{:S(2)}, u32[]{:S(2)}) collective-permute-start(bf16[1,16,256,256]{3,2,1,0:T(8,128)(2,1)} %refs_2_.7), channel_id=1, source_target_pairs={{0,2},{1,3},{2,0},{3,1},{4,6},{5,7},{6,4},{7,5},{8,10},{9,11},{10,... | collective-permute-start | bytes 6291464 | tf_op jit(solution)/shard_map/ppermute | solution.py:183
  2.9 3.0 %collective-permute-start.2 = (bf16[8,1,256,256]{3,2,1,0:T(8,128)(2,1)}, bf16[8,1,256,256]{3,2,1,0:T(8,128)(2,1)S(1)}, u32[]{:S(2)}, u32[]{:S(2)}) collective-permute-start(bf16[8,1,256,256]{3,2,1,0:T(8,128)(2,1)} %refs_0_.7), channel_id=1, source_target_pairs={{0,1},{1,0},{2,3},{3,2},{4,5},{5,4},{6,7},{7,6},{8,9},{9,8},{10,11... | collective-permute-start | bytes 3145736 | tf_op jit(solution)/shard_map/ppermute | solution.py:183
  3.2 25.6 %collective-permute-start = (bf16[8,1,256,256]{3,2,1,0:T(8,128)(2,1)}, bf16[8,1,256,256]{3,2,1,0:T(8,128)(2,1)S(1)}, u32[]{:S(2)}, u32[]{:S(2)}) collective-permute-start(bf16[8,1,256,256]{3,2,1,0:T(8,128)(2,1)} %refs_6_), channel_id=1, source_target_pairs={{0,4},{1,5},{2,6},{3,7},{4,0},{5,1},{6,2},{7,3},{8,12},{9,13},{10,... | collective-permute-start | bytes 3145736 | tf_op jit(solution)/shard_map/ppermute | solution.py:183
  4.7 24.0 %collective-permute-start.1 = (bf16[8,1,256,256]{3,2,1,0:T(8,128)(2,1)}, bf16[8,1,256,256]{3,2,1,0:T(8,128)(2,1)S(1)}, u32[]{:S(2)}, u32[]{:S(2)}) collective-permute-start(bf16[8,1,256,256]{3,2,1,0:T(8,128)(2,1)} %refs_6_), channel_id=1, source_target_pairs={{4,8},{5,9},{6,10},{7,11},{8,4},{9,5},{10,6},{11,7},{20,24},{21,25... | collective-permute-start | bytes 3145736 | tf_op jit(solution)/shard_map/ppermute | solution.py:183
  6.0 1.6 %copy-start = (bf16[1,16,256,256]{3,2,1,0:T(8,128)(2,1)S(1)}, bf16[1,16,256,256]{3,2,1,0:T(8,128)(2,1)}, u32[]{:S(2)}) copy-start(bf16[1,16,256,256]{3,2,1,0:T(8,128)(2,1)} %refs_2_.7) | copy-start | bytes 6291460
  7.5 1.2 copy-start.1
  8.8 1.2 copy-start.2
  10.0 0.7 copy-start.4
  28.7 29.9 %collective-permute-start.6 = (bf16[8,1,256,256]{3,2,1,0:T(8,128)(2,1)S(1)}, bf16[8,1,256,256]{3,2,1,0:T(8,128)(2,1)S(1)}, u32[]{:S(2)}, u32[]{:S(2)}) collective-permute-start(bf16[8,1,256,256]{3,2,1,0:T(8,128)(2,1)S(1)} %collective-permute-done.1.refs_4_.refs_6_), channel_id=1, source_target_pairs={{4,0},{5,1},{6,2},{7,3},{8,12},{9,13},{10,14},{11,15},{20,16},{21,... | collective-permute-start | bytes 3145736 | tf_op jit(solution)/shard_map/ppermute | solution.py:183
  30.0 28.6 %collective-permute-start.7 = (bf16[8,1,256,256]{3,2,1,0:T(8,128)(2,1)S(1)}, bf16[8,1,256,256]{3,2,1,0:T(8,128)(2,1)S(1)}, u32[]{:S(2)}, u32[]{:S(2)}) collective-permute-start(bf16[8,1,256,256]{3,2,1,0:T(8,128)(2,1)S(1)} %collective-permute-done.refs_4_.refs_6_), channel_id=1, source_target_pairs={{4,8},{5,9},{6,10},{7,11},{8,4},{9,5},{10,6},{11,7},{20,24},{21,25... | collective-permute-start | bytes 3145736 | tf_op jit(solution)/shard_map/ppermute | solution.py:183
  49.5 25.0 %collective-permute-start.5 = (bf16[8,1,256,256]{3,2,1,0:T(8,128)(2,1)S(1)}, bf16[8,1,256,256]{3,2,1,0:T(8,128)(2,1)S(1)}, u32[]{:S(2)}, u32[]{:S(2)}) collective-permute-start(bf16[8,1,256,256]{3,2,1,0:T(8,128)(2,1)S(1)} %copy-done.1), channel_id=1, source_target_pairs={{0,2},{1,3},{2,0},{3,1},{4,6},{5,7},{6,4},{7,5},{8,10},{9,11},{10,... | collective-permute-start | bytes 3145736 | tf_op jit(solution)/shard_map/ppermute | solution.py:183
  51.2 11.8 %collective-permute-start.8 = (bf16[2,256,256]{2,1,0:T(8,128)(2,1)S(1)}, bf16[2,256,256]{2,1,0:T(8,128)(2,1)S(1)}, u32[]{:S(2)}, u32[]{:S(2)}) collective-permute-start(bf16[2,256,256]{2,1,0:T(8,128)(2,1)S(1)} %shard_map.47), channel_id=1, source_target_pairs={{0,4},{1,5},{2,6},{3,7},{4,0},{5,1},{6,2},{7,3},{8,12},{9,13},{10,... | collective-permute-start | bytes 786440 | tf_op jit(solution)/shard_map/ppermute | solution.py:183
  52.8 10.2 %collective-permute-start.9 = (bf16[2,256,256]{2,1,0:T(8,128)(2,1)S(1)}, bf16[2,256,256]{2,1,0:T(8,128)(2,1)S(1)}, u32[]{:S(2)}, u32[]{:S(2)}) collective-permute-start(bf16[2,256,256]{2,1,0:T(8,128)(2,1)S(1)} %get-tuple-element.38), channel_id=1, source_target_pairs={{4,8},{5,9},{6,10},{7,11},{8,4},{9,5},{10,6},{11,7},{20,24},{21,25... | collective-permute-start | bytes 786440 | tf_op jit(solution)/shard_map/ppermute | solution.py:183
  58.6 20.0 %collective-permute-start.13 = (bf16[1,9,256,256]{3,2,1,0:T(8,128)(2,1)S(1)}, bf16[1,9,256,256]{3,2,1,0:T(8,128)(2,1)S(1)}, u32[]{:S(2)}, u32[]{:S(2)}) collective-permute-start(bf16[1,9,256,256]{3,2,1,0:T(8,128)(2,1)S(1)} %get-tuple-element.44), channel_id=1, source_target_pairs={{0,1},{1,0},{2,3},{3,2},{4,5},{5,4},{6,7},{7,6},{8,9},{9,8},{10,11... | collective-permute-start | bytes 3538952 | tf_op jit(solution)/shard_map/ppermute | solution.py:183
  63.0 15.0 %collective-permute-start.10 = (bf16[2,256,256]{2,1,0:T(8,128)(2,1)S(1)}, bf16[2,256,256]{2,1,0:T(8,128)(2,1)S(1)}, u32[]{:S(2)}, u32[]{:S(2)}) collective-permute-start(bf16[2,256,256]{2,1,0:T(8,128)(2,1)S(1)} %shard_map.49), channel_id=1, source_target_pairs={{0,8},{1,9},{2,10},{3,11},{4,12},{5,13},{6,14},{7,15},{8,0},{9,1},... | collective-permute-start | bytes 786440 | tf_op jit(solution)/shard_map/ppermute | solution.py:183
  67.6 11.1 %collective-permute-start.14 = (bf16[1,7,256,256]{3,2,1,0:T(8,128)(2,1)S(1)}, bf16[1,7,256,256]{3,2,1,0:T(8,128)(2,1)S(1)}, u32[]{:S(2)}, u32[]{:S(2)}) collective-permute-start(bf16[1,7,256,256]{3,2,1,0:T(8,128)(2,1)S(1)} %get-tuple-element.45), channel_id=1, source_target_pairs={{0,1},{1,0},{2,3},{3,2},{4,5},{5,4},{6,7},{7,6},{8,9},{9,8},{10,11... | collective-permute-start | bytes 2752520 | tf_op jit(solution)/shard_map/ppermute | solution.py:183
  67.6 37.4 %collective-permute-start.15 = (bf16[8,1,256,256]{3,2,1,0:T(8,128)(2,1)S(1)}, bf16[8,1,256,256]{3,2,1,0:T(8,128)(2,1)S(1)}, u32[]{:S(2)}, u32[]{:S(2)}) collective-permute-start(bf16[8,1,256,256]{3,2,1,0:T(8,128)(2,1)S(1)} %collective-permute-done.7.refs_5_.refs_7_), channel_id=1, source_target_pairs={{4,0},{5,1},{6,2},{7,3},{8,12},{9,13},{10,14},{11,15},{20,16},{21,... | collective-permute-start | bytes 3145736 | tf_op jit(solution)/shard_map/ppermute | solution.py:183
  78.1 2.7 %collective-permute-start.11 = (bf16[5,1,256,256]{3,2,1,0:T(8,128)(2,1)S(1)}, bf16[5,1,256,256]{3,2,1,0:T(8,128)(2,1)S(1)}, u32[]{:S(2)}, u32[]{:S(2)}) collective-permute-start(bf16[5,1,256,256]{3,2,1,0:T(8,128)(2,1)S(1)} %get-tuple-element.41), channel_id=1, source_target_pairs={{0,1},{1,0},{2,3},{3,2},{4,5},{5,4},{6,7},{7,6},{8,9},{9,8},{10,11... | collective-permute-start | bytes 1966088 | tf_op jit(solution)/shard_map/ppermute | solution.py:183
  78.2 2.6 %collective-permute-start.12 = (bf16[3,1,256,256]{3,2,1,0:T(8,128)(2,1)S(1)}, bf16[3,1,256,256]{3,2,1,0:T(8,128)(2,1)S(1)}, u32[]{:S(2)}, u32[]{:S(2)}) collective-permute-start(bf16[3,1,256,256]{3,2,1,0:T(8,128)(2,1)S(1)} %get-tuple-element.42), channel_id=1, source_target_pairs={{0,1},{1,0},{2,3},{3,2},{4,5},{5,4},{6,7},{7,6},{8,9},{9,8},{10,11... | collective-permute-start | bytes 1179656 | tf_op jit(solution)/shard_map/ppermute | solution.py:183
  82.7 22.3 %collective-permute-start.16 = (bf16[2,256,256]{2,1,0:T(8,128)(2,1)S(1)}, bf16[2,256,256]{2,1,0:T(8,128)(2,1)S(1)}, u32[]{:S(2)}, u32[]{:S(2)}) collective-permute-start(bf16[2,256,256]{2,1,0:T(8,128)(2,1)S(1)} %get-tuple-element.48), channel_id=1, source_target_pairs={{4,8},{5,9},{6,10},{7,11},{8,4},{9,5},{10,6},{11,7},{20,24},{21,25... | collective-permute-start | bytes 786440 | tf_op jit(solution)/shard_map/ppermute | solution.py:183
  85.3 26.2 %collective-permute-start.17 = (bf16[2,256,256]{2,1,0:T(8,128)(2,1)S(1)}, bf16[2,256,256]{2,1,0:T(8,128)(2,1)S(1)}, u32[]{:S(2)}, u32[]{:S(2)}) collective-permute-start(bf16[2,256,256]{2,1,0:T(8,128)(2,1)S(1)} %shard_map.54), channel_id=1, source_target_pairs={{0,8},{1,9},{2,10},{3,11},{4,12},{5,13},{6,14},{7,15},{8,0},{9,1},... | collective-permute-start | bytes 786440 | tf_op jit(solution)/shard_map/ppermute | solution.py:183
  88.9 22.6 %collective-permute-start.18 = (bf16[2,256,256]{2,1,0:T(8,128)(2,1)S(1)}, bf16[2,256,256]{2,1,0:T(8,128)(2,1)S(1)}, u32[]{:S(2)}, u32[]{:S(2)}) collective-permute-start(bf16[2,256,256]{2,1,0:T(8,128)(2,1)S(1)} %shard_map.53), channel_id=1, source_target_pairs={{0,4},{1,5},{2,6},{3,7},{4,0},{5,1},{6,2},{7,3},{8,12},{9,13},{10,... | collective-permute-start | bytes 786440 | tf_op jit(solution)/shard_map/ppermute | solution.py:183
  105.0 4.5 %copy-start.3 = (bf16[8,1,256,256]{3,2,1,0:T(8,128)(2,1)S(1)}, bf16[8,1,256,256]{3,2,1,0:T(8,128)(2,1)}, u32[]{:S(2)}) copy-start(bf16[8,1,256,256]{3,2,1,0:T(8,128)(2,1)} %refs_6_) | copy-start | bytes 3145732
  106.3 16.9 %collective-permute-start.19 = (bf16[4,256,256]{2,1,0:T(8,128)(2,1)S(1)}, bf16[4,256,256]{2,1,0:T(8,128)(2,1)S(1)}, u32[]{:S(2)}, u32[]{:S(2)}) collective-permute-start(bf16[4,256,256]{2,1,0:T(8,128)(2,1)S(1)} %shard_map.55), channel_id=1, source_target_pairs={{0,12},{1,13},{2,14},{3,15},{12,0},{13,1},{14,2},{15,3},{16,28},{1... | collective-permute-start | bytes 1572872 | tf_op jit(solution)/shard_map/ppermute | solution.py:183

commit v20 on v16

--- a/solution.py
+++ b/solution.py
@@ -219,18 +219,18 @@
     x_left, sent_2 = lax.optimization_barrier((x_left, sent_2))
     across_left = [exchange(part, 1, every) for part in split(x_left, 0, 5 * x_left.shape[0] // 8)]
     other = ([(x_left,), across_left], [(x_psi,), across_psi])
+    other_middle, other_mid = products(3, *other, (middle,), keep_mid=True)
+    sent_other_middle = exchange(other_middle, 12, inner)
+    other_0 = products(0, *other, (right_env,))
+    far_out, other_middle, other_0 = lax.optimization_barrier((far_out, other_middle, other_0))
     other_2 = products(2, *other, (far_out, far_in))
     other_sent_2 = exchange(other_2, 8, every)
-    other_middle, other_mid = products(3, *other, (middle,), keep_mid=True)
-    sent_other_middle = exchange(other_middle, 12, inner)
     other_1 = products(1, *other, (near,))
     other_sent_1 = exchange(other_1, 4, every)
 
     third, other_1, other_2, other_middle = lax.optimization_barrier((third, other_1, other_2, other_middle))
     last_third = second((own_mid, other_mid), third, dtype, 10**10)
     sent_third = exchange(last_third, 12, outer)
-    right_last, last_third = lax.optimization_barrier((right_env, last_third))
-    other_0 = products(0, *other, (right_last,))
 
     held = [(0, own_0), (2, other_0), (8, sent_2), (10, other_sent_2), (4, sent_1), (6, other_sent_1)]
     out = place(16, held, flops=10**10)

time: 120 us -> 119 us (level)
  waiting for transfers between devices: 70.8 us -> 66.2 us
  starting transfers between devices: 25.5 us -> 29 us
    ppermute x20, waiting for transfers between devices: 70.8 us -> 66.2 us  [exchange(): return lax.ppermute(array, 'sec', [(s, s ^ bits) for s in members])]
    ppermute x20, starting transfers between devices: 25.5 us -> 29 us  [exchange(): return lax.ppermute(array, 'sec', [(s, s ^ bits) for s in members])]
where the time goes in v20:
time: 119 us
  waiting for transfers between devices  66.2 us (56%)
  starting transfers between devices  29 us (24%)
  Pallas kernels  18.8 us (16%)
  local copies, waits for them, and re-layouts  4.73 us (4%)
    ppermute x20, waiting for transfers between devices, exchange(): return lax.ppermute(array, 'sec', [(s, s ^ bits) for s in members])  66.2 us
    ppermute x20, starting transfers between devices, exchange(): return lax.ppermute(array, 'sec', [(s, s ^ bits) for s in members])  29 us
    pallas_call x8, Pallas kernels, slot(): pl.pallas_call(functools.partial(slot_kernel, step, parts, len(rights)),...  15.1 us
    unnamed x10, local copies, waits for them, and re-layouts  4.73 us
  transfers between devices with their start and end apart: 20, of which 10 were waited for; matrix products, arithmetic and copies ran while one was open for 0% of the time, Pallas kernels for 15%

profile of v20, /device:TPU:0, one launch (start us, length us, event | category | flops | bytes accessed | tf_op | source)
XLA Modules:
  0.0 119.1 jit_solution(17659464952848585638)
XLA Ops:
  0.0 0.5 collective-permute-start.3
  0.5 2.5 %collective-permute-start.6 = (bf16[1,16,256,256]{3,2,1,0:T(8,128)(2,1)}, bf16[1,16,256,256]{3,2,1,0:T(8,128)(2,1)S(1)}, u32[]{:S(2)}, u32[]{:S(2)}) collective-permute-start(bf16[1,16,256,256]{3,2,1,0:T(8,128)(2,1)} %refs_2_.7), channel_id=1, source_target_pairs={{0,2},{1,3},{2,0},{3,1},{4,6},{5,7},{6,4},{7,5},{8,10},{9,11},{10,... | collective-permute-start | bytes 6291464 | tf_op jit(solution)/shard_map/ppermute | solution.py:183
  2.9 0.2 collective-permute-start.2
  3.2 1.6 %collective-permute-start = (bf16[8,1,256,256]{3,2,1,0:T(8,128)(2,1)}, bf16[8,1,256,256]{3,2,1,0:T(8,128)(2,1)S(1)}, u32[]{:S(2)}, u32[]{:S(2)}) collective-permute-start(bf16[8,1,256,256]{3,2,1,0:T(8,128)(2,1)} %refs_6_.1), channel_id=1, source_target_pairs={{0,4},{1,5},{2,6},{3,7},{4,0},{5,1},{6,2},{7,3},{8,12},{9,13},{10,... | collective-permute-start | bytes 3145736 | tf_op jit(solution)/shard_map/ppermute | solution.py:183
  4.7 0.7 collective-permute-start.1
  5.5 0.5 collective-permute-done.2.refs_1_
  6.0 1.6 %copy-done = bf16[1,16,256,256]{3,2,1,0:T(8,128)(2,1)S(1)} copy-done((bf16[1,16,256,256]{3,2,1,0:T(8,128)(2,1)S(1)}, bf16[1,16,256,256]{3,2,1,0:T(8,128)(2,1)}, u32[]{:S(2)}) %copy-start) | copy-done | bytes 2097176
  7.5 1.2 %copy-done.1 = bf16[8,1,256,256]{3,2,1,0:T(8,128)(2,1)S(1)} copy-done((bf16[8,1,256,256]{3,2,1,0:T(8,128)(2,1)S(1)}, bf16[8,1,256,256]{3,2,1,0:T(8,128)(2,1)}, u32[]{:S(2)}) %copy-start.1) | copy-done | bytes 1048600
  8.8 1.2 %copy-done.2 = bf16[8,1,256,256]{3,2,1,0:T(8,128)(2,1)S(1)} copy-done((bf16[8,1,256,256]{3,2,1,0:T(8,128)(2,1)S(1)}, bf16[8,1,256,256]{3,2,1,0:T(8,128)(2,1)}, u32[]{:S(2)}) %copy-start.2) | copy-done | bytes 1048600
  10.0 0.7 copy-done.4
  10.7 1.9 %shard_map.46.refs_0_ = bf16[2,256,256]{2,1,0:T(8,128)(2,1)S(1)} custom-call(s32[8,16]{1,0:T(8,128)S(1)} %copy-done.4, bf16[8,1,256,256]{3,2,1,0:T(8,128)(2,1)S(1)} %copy-done.1, bf16[8,1,256,256]{3,2,1,0:T(8,128)(2,1)S(1)} %collective-permute-done.2.refs_1_, bf16[1,16,256,256]{3,2,1,0:T(8,128)(2,1)S(1)} %copy-done, ...), custom_call_target="tpu_custom_call" | custom-call | flops 1 | bytes 1 | tf_op jit(solution)/shard_map/pallas_call | solution.py:99
  12.6 16.2 %collective-permute-done.refs_4_.refs_6_ = bf16[8,1,256,256]{3,2,1,0:T(8,128)(2,1)S(1)} collective-permute-done((bf16[8,1,256,256]{3,2,1,0:T(8,128)(2,1)}, bf16[8,1,256,256]{3,2,1,0:T(8,128)(2,1)S(1)}, u32[]{:S(2)}, u32[]{:S(2)}) %collective-permute-start) | collective-permute-done | bytes 1048608 | tf_op jit(solution)/shard_map/ppermute | solution.py:183
  28.7 0.0 collective-permute-done.1.refs_4_.refs_6_
  28.7 1.3 %collective-permute-start.4 = (bf16[8,1,256,256]{3,2,1,0:T(8,128)(2,1)S(1)}, bf16[8,1,256,256]{3,2,1,0:T(8,128)(2,1)S(1)}, u32[]{:S(2)}, u32[]{:S(2)}) collective-permute-start(bf16[8,1,256,256]{3,2,1,0:T(8,128)(2,1)S(1)} %collective-permute-done.1.refs_4_.refs_6_), channel_id=1, source_target_pairs={{4,0},{5,1},{6,2},{7,3},{8,12},{9,13},{10,14},{11,15},{20,16},{21,... | collective-permute-start | bytes 3145736 | tf_op jit(solution)/shard_map/ppermute | solution.py:183
  30.0 0.7 collective-permute-start.5
  30.8 1.9 %shard_map.48 = (bf16[2,256,256]{2,1,0:T(8,128)(2,1)S(1)}, bf16[512,2048]{1,0:T(8,128)(2,1)S(1)}) custom-call(s32[8,16]{1,0:T(8,128)S(1)} %copy-done.4, bf16[8,1,256,256]{3,2,1,0:T(8,128)(2,1)S(1)} %copy-done.1, bf16[8,1,256,256]{3,2,1,0:T(8,128)(2,1)S(1)} %collective-permute-done.2.refs_1_, bf16[1,16,256,256]{3,2,1,0:T(8,128)(2,1)S(1)} %copy-done, ...), custom_call_target="tpu_custom_call" | custom-call | flops 1 | bytes 1 | tf_op jit(solution)/shard_map/pallas_call | solution.py:99
  32.6 1.9 %shard_map.47 = bf16[2,256,256]{2,1,0:T(8,128)(2,1)S(1)} custom-call(s32[8,16]{1,0:T(8,128)S(1)} %copy-done.4, bf16[8,1,256,256]{3,2,1,0:T(8,128)(2,1)S(1)} %copy-done.1, bf16[8,1,256,256]{3,2,1,0:T(8,128)(2,1)S(1)} %collective-permute-done.2.refs_1_, bf16[1,16,256,256]{3,2,1,0:T(8,128)(2,1)S(1)} %copy-done, ...), custom_call_target="tpu_custom_call" | custom-call | flops 1 | bytes 1 | tf_op jit(solution)/shard_map/pallas_call | solution.py:99
  34.5 14.9 %collective-permute-done.6.whole.refs_3_ = bf16[1,16,256,256]{3,2,1,0:T(8,128)(2,1)S(1)} collective-permute-done((bf16[1,16,256,256]{3,2,1,0:T(8,128)(2,1)}, bf16[1,16,256,256]{3,2,1,0:T(8,128)(2,1)S(1)}, u32[]{:S(2)}, u32[]{:S(2)}) %collective-permute-start.6) | collective-permute-done | bytes 2097184 | tf_op jit(solution)/shard_map/ppermute | solution.py:183
  49.5 1.7 %collective-permute-start.7 = (bf16[8,1,256,256]{3,2,1,0:T(8,128)(2,1)S(1)}, bf16[8,1,256,256]{3,2,1,0:T(8,128)(2,1)S(1)}, u32[]{:S(2)}, u32[]{:S(2)}) collective-permute-start(bf16[8,1,256,256]{3,2,1,0:T(8,128)(2,1)S(1)} %copy-done.1), channel_id=1, source_target_pairs={{0,2},{1,3},{2,0},{3,1},{4,6},{5,7},{6,4},{7,5},{8,10},{9,11},{10,... | collective-permute-start | bytes 3145736 | tf_op jit(solution)/shard_map/ppermute | solution.py:183
  51.2 1.6 %collective-permute-start.8 = (bf16[2,256,256]{2,1,0:T(8,128)(2,1)S(1)}, bf16[2,256,256]{2,1,0:T(8,128)(2,1)S(1)}, u32[]{:S(2)}, u32[]{:S(2)}) collective-permute-start(bf16[2,256,256]{2,1,0:T(8,128)(2,1)S(1)} %shard_map.47), channel_id=1, source_target_pairs={{0,4},{1,5},{2,6},{3,7},{4,0},{5,1},{6,2},{7,3},{8,12},{9,13},{10,... | collective-permute-start | bytes 786440 | tf_op jit(solution)/shard_map/ppermute | solution.py:183
  52.8 0.7 collective-permute-start.9
  53.4 0.1 shard_map.51
  53.6 5.0 %collective-permute-done.4.refs_4_.refs_6_ = bf16[8,1,256,256]{3,2,1,0:T(8,128)(2,1)S(1)} collective-permute-done((bf16[8,1,256,256]{3,2,1,0:T(8,128)(2,1)S(1)}, bf16[8,1,256,256]{3,2,1,0:T(8,128)(2,1)S(1)}, u32[]{:S(2)}, u32[]{:S(2)}) %collective-permute-start.4) | collective-permute-done | bytes 1048608 | tf_op jit(solution)/shard_map/ppermute | solution.py:183
  58.6 1.3 %collective-permute-start.17 = (bf16[8,1,256,256]{3,2,1,0:T(8,128)(2,1)S(1)}, bf16[8,1,256,256]{3,2,1,0:T(8,128)(2,1)S(1)}, u32[]{:S(2)}, u32[]{:S(2)}) collective-permute-start(bf16[8,1,256,256]{3,2,1,0:T(8,128)(2,1)S(1)} %collective-permute-done.5.refs_5_.refs_7_), channel_id=1, source_target_pairs={{4,0},{5,1},{6,2},{7,3},{8,12},{9,13},{10,14},{11,15},{20,16},{21,... | collective-permute-start | bytes 3145736 | tf_op jit(solution)/shard_map/ppermute | solution.py:183
  59.9 1.9 %shard_map.49 = bf16[2,256,256]{2,1,0:T(8,128)(2,1)S(1)} custom-call(s32[8,16]{1,0:T(8,128)S(1)} %copy-done.4, bf16[8,1,256,256]{3,2,1,0:T(8,128)(2,1)S(1)} %copy-done.1, bf16[8,1,256,256]{3,2,1,0:T(8,128)(2,1)S(1)} %collective-permute-done.2.refs_1_, bf16[1,16,256,256]{3,2,1,0:T(8,128)(2,1)S(1)} %copy-done, ...), custom_call_target="tpu_custom_call" | custom-call | flops 1 | bytes 1 | tf_op jit(solution)/shard_map/pallas_call | solution.py:99
  61.8 1.2 collective-permute-done.8.refs_4_
  63.0 0.0 collective-permute-done.9.refs_2_
  63.0 4.6 %collective-permute-start.10 = (bf16[2,256,256]{2,1,0:T(8,128)(2,1)S(1)}, bf16[2,256,256]{2,1,0:T(8,128)(2,1)S(1)}, u32[]{:S(2)}, u32[]{:S(2)}) collective-permute-start(bf16[2,256,256]{2,1,0:T(8,128)(2,1)S(1)} %shard_map.49), channel_id=1, source_target_pairs={{0,8},{1,9},{2,10},{3,11},{4,12},{5,13},{6,14},{7,15},{8,0},{9,1},... | collective-permute-start | bytes 786440 | tf_op jit(solution)/shard_map/ppermute | solution.py:183
  67.6 6.9 %collective-permute-done.7.whole.refs_0_ = bf16[8,1,256,256]{3,2,1,0:T(8,128)(2,1)S(1)} collective-permute-done((bf16[8,1,256,256]{3,2,1,0:T(8,128)(2,1)S(1)}, bf16[8,1,256,256]{3,2,1,0:T(8,128)(2,1)S(1)}, u32[]{:S(2)}, u32[]{:S(2)}) %collective-permute-start.7) | collective-permute-done | bytes 1048608 | tf_op jit(solution)/shard_map/ppermute | solution.py:183
  74.4 3.9 %collective-permute-done.10.refs_2_ = bf16[2,256,256]{2,1,0:T(8,128)(2,1)S(1)} collective-permute-done((bf16[2,256,256]{2,1,0:T(8,128)(2,1)S(1)}, bf16[2,256,256]{2,1,0:T(8,128)(2,1)S(1)}, u32[]{:S(2)}, u32[]{:S(2)}) %collective-permute-start.10) | collective-permute-done | bytes 262176 | tf_op jit(solution)/shard_map/ppermute | solution.py:183
  78.3 0.1 shard_map.50
  78.4 0.1 collective-permute-start.11
  78.5 0.5 collective-permute-start.12
  79.0 2.1 %collective-permute-done.12.refs_2_ = bf16[3,1,256,256]{3,2,1,0:T(8,128)(2,1)S(1)} collective-permute-done((bf16[3,1,256,256]{3,2,1,0:T(8,128)(2,1)S(1)}, bf16[3,1,256,256]{3,2,1,0:T(8,128)(2,1)S(1)}, u32[]{:S(2)}, u32[]{:S(2)}) %collective-permute-start.12) | collective-permute-done | bytes 393248 | tf_op jit(solution)/shard_map/ppermute | solution.py:183
  81.1 1.9 %shard_map.52 = (bf16[2,256,256]{2,1,0:T(8,128)(2,1)S(1)}, bf16[512,2048]{1,0:T(8,128)(2,1)S(1)}) custom-call(s32[8,16]{1,0:T(8,128)S(1)} %copy-done.4, bf16[8,1,256,256]{3,2,1,0:T(8,128)(2,1)S(1)} %collective-permute-done.7.whole.refs_0_, bf16[5,1,256,256]{3,2,1,0:T(8,128)(2,1)S(1)} %collective-permute-done.11.refs_1_, ...), custom_call_target="tpu_custom_call" | custom-call | flops 1 | bytes 1 | tf_op jit(solution)/shard_map/pallas_call | solution.py:99
  83.0 0.0 copy-start.3
  83.0 1.0 collective-permute-start.19
  84.0 1.9 %shard_map.55 = bf16[2,256,256]{2,1,0:T(8,128)(2,1)S(1)} custom-call(s32[8,16]{1,0:T(8,128)S(1)} %copy-done.4, bf16[8,1,256,256]{3,2,1,0:T(8,128)(2,1)S(1)} %collective-permute-done.7.whole.refs_0_, bf16[5,1,256,256]{3,2,1,0:T(8,128)(2,1)S(1)} %collective-permute-done.11.refs_1_, bf16[3,1,256,256]{3,2,1,0:T(8,128)(2,1)S(1)} %collective-permute-done.12.refs_2_, ...), custom_call_target="tpu_custom_call" | custom-call | flops 1 | bytes 1 | tf_op jit(solution)/shard_map/pallas_call | solution.py:99
  85.9 1.9 %shard_map.53.refs_1_ = bf16[2,256,256]{2,1,0:T(8,128)(2,1)S(1)} custom-call(s32[8,16]{1,0:T(8,128)S(1)} %copy-done.4, bf16[8,1,256,256]{3,2,1,0:T(8,128)(2,1)S(1)} %collective-permute-done.7.whole.refs_0_, bf16[5,1,256,256]{3,2,1,0:T(8,128)(2,1)S(1)} %collective-permute-done.11.refs_1_, bf16[3,1,256,256]{3,2,1,0:T(8,128)(2,1)S(1)} %collective-permute-done.12.refs_2_, ...), custom_call_target="tpu_custom_call" | custom-call | flops 1 | bytes 1 | tf_op jit(solution)/shard_map/pallas_call | solution.py:99
  87.8 1.3 %collective-permute-start.16 = (bf16[2,256,256]{2,1,0:T(8,128)(2,1)S(1)}, bf16[2,256,256]{2,1,0:T(8,128)(2,1)S(1)}, u32[]{:S(2)}, u32[]{:S(2)}) collective-permute-start(bf16[2,256,256]{2,1,0:T(8,128)(2,1)S(1)} %shard_map.55), channel_id=1, source_target_pairs={{0,4},{1,5},{2,6},{3,7},{4,0},{5,1},{6,2},{7,3},{8,12},{9,13},{10,... | collective-permute-start | bytes 786440 | tf_op jit(solution)/shard_map/ppermute | solution.py:183
  89.1 1.9 %shard_map.54 = bf16[2,256,256]{2,1,0:T(8,128)(2,1)S(1)} custom-call(s32[8,16]{1,0:T(8,128)S(1)} %copy-done.4, bf16[8,1,256,256]{3,2,1,0:T(8,128)(2,1)S(1)} %collective-permute-done.7.whole.refs_0_, bf16[5,1,256,256]{3,2,1,0:T(8,128)(2,1)S(1)} %collective-permute-done.11.refs_1_, bf16[3,1,256,256]{3,2,1,0:T(8,128)(2,1)S(1)} %collective-permute-done.12.refs_2_, ...), custom_call_target="tpu_custom_call" | custom-call | flops 1 | bytes 1 | tf_op jit(solution)/shard_map/pallas_call | solution.py:99
  91.1 1.0 collective-permute-start.15
  92.1 0.7 collective-permute-done.17.refs_2_
  92.7 1.3 %shard_map.57 = bf16[4,256,256]{2,1,0:T(8,128)(2,1)S(1)} custom-call(bf16[512,2048]{1,0:T(8,128)(2,1)S(1)} %get-tuple-element.51.refs_0_, bf16[512,2048]{1,0:T(8,128)(2,1)S(1)} %get-tuple-element.52.refs_1_, bf16[8,1,256,256]{3,2,1,0:T(8,128)(2,1)S(1)} %collective-permute-done.17.refs_2_), custom_call_target="tpu_custom_call" | custom-call | flops 10000000000 | bytes 1 | tf_op jit(solution)/shard_map/pallas_call | solution.py:78
  94.0 7.8 %collective-permute-start.18 = (bf16[4,256,256]{2,1,0:T(8,128)(2,1)S(1)}, bf16[4,256,256]{2,1,0:T(8,128)(2,1)S(1)}, u32[]{:S(2)}, u32[]{:S(2)}) collective-permute-start(bf16[4,256,256]{2,1,0:T(8,128)(2,1)S(1)} %shard_map.57), channel_id=1, source_target_pairs={{0,12},{1,13},{2,14},{3,15},{12,0},{13,1},{14,2},{15,3},{16,28},{1... | collective-permute-start | bytes 1572872 | tf_op jit(solution)/shard_map/ppermute | solution.py:183
  101.8 14.9 %collective-permute-done.15.refs_3_ = bf16[2,256,256]{2,1,0:T(8,128)(2,1)S(1)} collective-permute-done((bf16[2,256,256]{2,1,0:T(8,128)(2,1)S(1)}, bf16[2,256,256]{2,1,0:T(8,128)(2,1)S(1)}, u32[]{:S(2)}, u32[]{:S(2)}) %collective-permute-start.15) | collective-permute-done | bytes 262176 | tf_op jit(solution)/shard_map/ppermute | solution.py:183
  116.7 1.3 %shard_map.56.refs_0_ = bf16[16,256,256]{2,1,0:T(8,128)(2,1)} custom-call(bf16[2,256,256]{2,1,0:T(8,128)(2,1)S(1)} %shard_map.46.refs_0_, bf16[2,256,256]{2,1,0:T(8,128)(2,1)S(1)} %shard_map.53.refs_1_, bf16[2,256,256]{2,1,0:T(8,128)(2,1)S(1)} %collective-permute-done.10.refs_2_, bf16[2,256,256]{2,1,0:T(8,128)(2,1)S(1)} %collective-permute-done.15.refs_3_, ...), custom_call_target="tpu_custom_call" | custom-call | flops 10000000000 | bytes 1 | tf_op jit(solution)/shard_map/pallas_call | solution.py:170
  118.0 0.9 shard_map.58
  (15 shorter events, 0.0 us)
Async XLA Ops:
  0.0 6.0 %collective-permute-start.3 = (bf16[1,16,256,256]{3,2,1,0:T(8,128)(2,1)}, bf16[1,16,256,256]{3,2,1,0:T(8,128)(2,1)S(1)}, u32[]{:S(2)}, u32[]{:S(2)}) collective-permute-start(bf16[1,16,256,256]{3,2,1,0:T(8,128)(2,1)} %refs_2_.7), channel_id=1, source_target_pairs={{0,1},{1,0},{2,3},{3,2},{4,5},{5,4},{6,7},{7,6},{8,9},{9,8},{10,11... | collective-permute-start | bytes 6291464 | tf_op jit(solution)/shard_map/ppermute | solution.py:183
  0.5 49.0 %collective-permute-start.6 = (bf16[1,16,256,256]{3,2,1,0:T(8,128)(2,1)}, bf16[1,16,256,256]{3,2,1,0:T(8,128)(2,1)S(1)}, u32[]{:S(2)}, u32[]{:S(2)}) collective-permute-start(bf16[1,16,256,256]{3,2,1,0:T(8,128)(2,1)} %refs_2_.7), channel_id=1, source_target_pairs={{0,2},{1,3},{2,0},{3,1},{4,6},{5,7},{6,4},{7,5},{8,10},{9,11},{10,... | collective-permute-start | bytes 6291464 | tf_op jit(solution)/shard_map/ppermute | solution.py:183
  2.9 3.0 %collective-permute-start.2 = (bf16[8,1,256,256]{3,2,1,0:T(8,128)(2,1)}, bf16[8,1,256,256]{3,2,1,0:T(8,128)(2,1)S(1)}, u32[]{:S(2)}, u32[]{:S(2)}) collective-permute-start(bf16[8,1,256,256]{3,2,1,0:T(8,128)(2,1)} %refs_0_.7), channel_id=1, source_target_pairs={{0,1},{1,0},{2,3},{3,2},{4,5},{5,4},{6,7},{7,6},{8,9},{9,8},{10,11... | collective-permute-start | bytes 3145736 | tf_op jit(solution)/shard_map/ppermute | solution.py:183
  3.2 25.6 %collective-permute-start = (bf16[8,1,256,256]{3,2,1,0:T(8,128)(2,1)}, bf16[8,1,256,256]{3,2,1,0:T(8,128)(2,1)S(1)}, u32[]{:S(2)}, u32[]{:S(2)}) collective-permute-start(bf16[8,1,256,256]{3,2,1,0:T(8,128)(2,1)} %refs_6_.1), channel_id=1, source_target_pairs={{0,4},{1,5},{2,6},{3,7},{4,0},{5,1},{6,2},{7,3},{8,12},{9,13},{10,... | collective-permute-start | bytes 3145736 | tf_op jit(solution)/shard_map/ppermute | solution.py:183
  4.7 24.0 %collective-permute-start.1 = (bf16[8,1,256,256]{3,2,1,0:T(8,128)(2,1)}, bf16[8,1,256,256]{3,2,1,0:T(8,128)(2,1)S(1)}, u32[]{:S(2)}, u32[]{:S(2)}) collective-permute-start(bf16[8,1,256,256]{3,2,1,0:T(8,128)(2,1)} %refs_6_.1), channel_id=1, source_target_pairs={{4,8},{5,9},{6,10},{7,11},{8,4},{9,5},{10,6},{11,7},{20,24},{21,25... | collective-permute-start | bytes 3145736 | tf_op jit(solution)/shard_map/ppermute | solution.py:183
  6.0 1.6 %copy-start = (bf16[1,16,256,256]{3,2,1,0:T(8,128)(2,1)S(1)}, bf16[1,16,256,256]{3,2,1,0:T(8,128)(2,1)}, u32[]{:S(2)}) copy-start(bf16[1,16,256,256]{3,2,1,0:T(8,128)(2,1)} %refs_2_.7) | copy-start | bytes 6291460
  7.5 1.2 %copy-start.1 = (bf16[8,1,256,256]{3,2,1,0:T(8,128)(2,1)S(1)}, bf16[8,1,256,256]{3,2,1,0:T(8,128)(2,1)}, u32[]{:S(2)}) copy-start(bf16[8,1,256,256]{3,2,1,0:T(8,128)(2,1)} %refs_0_.7) | copy-start | bytes 3145732
  8.8 1.2 %copy-start.2 = (bf16[8,1,256,256]{3,2,1,0:T(8,128)(2,1)S(1)}, bf16[8,1,256,256]{3,2,1,0:T(8,128)(2,1)}, u32[]{:S(2)}) copy-start(bf16[8,1,256,256]{3,2,1,0:T(8,128)(2,1)} %refs_6_.1) | copy-start | bytes 3145732
  10.0 0.7 copy-start.4
  28.7 29.9 %collective-permute-start.4 = (bf16[8,1,256,256]{3,2,1,0:T(8,128)(2,1)S(1)}, bf16[8,1,256,256]{3,2,1,0:T(8,128)(2,1)S(1)}, u32[]{:S(2)}, u32[]{:S(2)}) collective-permute-start(bf16[8,1,256,256]{3,2,1,0:T(8,128)(2,1)S(1)} %collective-permute-done.1.refs_4_.refs_6_), channel_id=1, source_target_pairs={{4,0},{5,1},{6,2},{7,3},{8,12},{9,13},{10,14},{11,15},{20,16},{21,... | collective-permute-start | bytes 3145736 | tf_op jit(solution)/shard_map/ppermute | solution.py:183
  30.0 28.6 %collective-permute-start.5 = (bf16[8,1,256,256]{3,2,1,0:T(8,128)(2,1)S(1)}, bf16[8,1,256,256]{3,2,1,0:T(8,128)(2,1)S(1)}, u32[]{:S(2)}, u32[]{:S(2)}) collective-permute-start(bf16[8,1,256,256]{3,2,1,0:T(8,128)(2,1)S(1)} %collective-permute-done.refs_4_.refs_6_), channel_id=1, source_target_pairs={{4,8},{5,9},{6,10},{7,11},{8,4},{9,5},{10,6},{11,7},{20,24},{21,25... | collective-permute-start | bytes 3145736 | tf_op jit(solution)/shard_map/ppermute | solution.py:183
  49.5 25.0 %collective-permute-start.7 = (bf16[8,1,256,256]{3,2,1,0:T(8,128)(2,1)S(1)}, bf16[8,1,256,256]{3,2,1,0:T(8,128)(2,1)S(1)}, u32[]{:S(2)}, u32[]{:S(2)}) collective-permute-start(bf16[8,1,256,256]{3,2,1,0:T(8,128)(2,1)S(1)} %copy-done.1), channel_id=1, source_target_pairs={{0,2},{1,3},{2,0},{3,1},{4,6},{5,7},{6,4},{7,5},{8,10},{9,11},{10,... | collective-permute-start | bytes 3145736 | tf_op jit(solution)/shard_map/ppermute | solution.py:183
  51.2 11.8 %collective-permute-start.8 = (bf16[2,256,256]{2,1,0:T(8,128)(2,1)S(1)}, bf16[2,256,256]{2,1,0:T(8,128)(2,1)S(1)}, u32[]{:S(2)}, u32[]{:S(2)}) collective-permute-start(bf16[2,256,256]{2,1,0:T(8,128)(2,1)S(1)} %shard_map.47), channel_id=1, source_target_pairs={{0,4},{1,5},{2,6},{3,7},{4,0},{5,1},{6,2},{7,3},{8,12},{9,13},{10,... | collective-permute-start | bytes 786440 | tf_op jit(solution)/shard_map/ppermute | solution.py:183
  52.8 10.2 %collective-permute-start.9 = (bf16[2,256,256]{2,1,0:T(8,128)(2,1)S(1)}, bf16[2,256,256]{2,1,0:T(8,128)(2,1)S(1)}, u32[]{:S(2)}, u32[]{:S(2)}) collective-permute-start(bf16[2,256,256]{2,1,0:T(8,128)(2,1)S(1)} %get-tuple-element.38), channel_id=1, source_target_pairs={{4,8},{5,9},{6,10},{7,11},{8,4},{9,5},{10,6},{11,7},{20,24},{21,25... | collective-permute-start | bytes 786440 | tf_op jit(solution)/shard_map/ppermute | solution.py:183
  58.6 20.3 %collective-permute-start.13 = (bf16[1,9,256,256]{3,2,1,0:T(8,128)(2,1)S(1)}, bf16[1,9,256,256]{3,2,1,0:T(8,128)(2,1)S(1)}, u32[]{:S(2)}, u32[]{:S(2)}) collective-permute-start(bf16[1,9,256,256]{3,2,1,0:T(8,128)(2,1)S(1)} %get-tuple-element.44), channel_id=1, source_target_pairs={{0,1},{1,0},{2,3},{3,2},{4,5},{5,4},{6,7},{7,6},{8,9},{9,8},{10,11... | collective-permute-start | bytes 3538952 | tf_op jit(solution)/shard_map/ppermute | solution.py:183
  58.6 34.1 %collective-permute-start.17 = (bf16[8,1,256,256]{3,2,1,0:T(8,128)(2,1)S(1)}, bf16[8,1,256,256]{3,2,1,0:T(8,128)(2,1)S(1)}, u32[]{:S(2)}, u32[]{:S(2)}) collective-permute-start(bf16[8,1,256,256]{3,2,1,0:T(8,128)(2,1)S(1)} %collective-permute-done.5.refs_5_.refs_7_), channel_id=1, source_target_pairs={{4,0},{5,1},{6,2},{7,3},{8,12},{9,13},{10,14},{11,15},{20,16},{21,... | collective-permute-start | bytes 3145736 | tf_op jit(solution)/shard_map/ppermute | solution.py:183
  63.0 15.3 %collective-permute-start.10 = (bf16[2,256,256]{2,1,0:T(8,128)(2,1)S(1)}, bf16[2,256,256]{2,1,0:T(8,128)(2,1)S(1)}, u32[]{:S(2)}, u32[]{:S(2)}) collective-permute-start(bf16[2,256,256]{2,1,0:T(8,128)(2,1)S(1)} %shard_map.49), channel_id=1, source_target_pairs={{0,8},{1,9},{2,10},{3,11},{4,12},{5,13},{6,14},{7,15},{8,0},{9,1},... | collective-permute-start | bytes 786440 | tf_op jit(solution)/shard_map/ppermute | solution.py:183
  67.6 11.4 %collective-permute-start.14 = (bf16[1,7,256,256]{3,2,1,0:T(8,128)(2,1)S(1)}, bf16[1,7,256,256]{3,2,1,0:T(8,128)(2,1)S(1)}, u32[]{:S(2)}, u32[]{:S(2)}) collective-permute-start(bf16[1,7,256,256]{3,2,1,0:T(8,128)(2,1)S(1)} %get-tuple-element.45), channel_id=1, source_target_pairs={{0,1},{1,0},{2,3},{3,2},{4,5},{5,4},{6,7},{7,6},{8,9},{9,8},{10,11... | collective-permute-start | bytes 2752520 | tf_op jit(solution)/shard_map/ppermute | solution.py:183
  78.4 2.7 %collective-permute-start.11 = (bf16[5,1,256,256]{3,2,1,0:T(8,128)(2,1)S(1)}, bf16[5,1,256,256]{3,2,1,0:T(8,128)(2,1)S(1)}, u32[]{:S(2)}, u32[]{:S(2)}) collective-permute-start(bf16[5,1,256,256]{3,2,1,0:T(8,128)(2,1)S(1)} %get-tuple-element.41), channel_id=1, source_target_pairs={{0,1},{1,0},{2,3},{3,2},{4,5},{5,4},{6,7},{7,6},{8,9},{9,8},{10,11... | collective-permute-start | bytes 1966088 | tf_op jit(solution)/shard_map/ppermute | solution.py:183
  78.5 2.6 %collective-permute-start.12 = (bf16[3,1,256,256]{3,2,1,0:T(8,128)(2,1)S(1)}, bf16[3,1,256,256]{3,2,1,0:T(8,128)(2,1)S(1)}, u32[]{:S(2)}, u32[]{:S(2)}) collective-permute-start(bf16[3,1,256,256]{3,2,1,0:T(8,128)(2,1)S(1)} %get-tuple-element.42), channel_id=1, source_target_pairs={{0,1},{1,0},{2,3},{3,2},{4,5},{5,4},{6,7},{7,6},{8,9},{9,8},{10,11... | collective-permute-start | bytes 1179656 | tf_op jit(solution)/shard_map/ppermute | solution.py:183
  83.0 2.9 %copy-start.3 = (bf16[8,1,256,256]{3,2,1,0:T(8,128)(2,1)S(1)}, bf16[8,1,256,256]{3,2,1,0:T(8,128)(2,1)}, u32[]{:S(2)}) copy-start(bf16[8,1,256,256]{3,2,1,0:T(8,128)(2,1)} %refs_6_.1) | copy-start | bytes 3145732
  83.0 35.0 %collective-permute-start.19 = (bf16[2,256,256]{2,1,0:T(8,128)(2,1)S(1)}, bf16[2,256,256]{2,1,0:T(8,128)(2,1)S(1)}, u32[]{:S(2)}, u32[]{:S(2)}) collective-permute-start(bf16[2,256,256]{2,1,0:T(8,128)(2,1)S(1)} %get-tuple-element.46), channel_id=1, source_target_pairs={{4,8},{5,9},{6,10},{7,11},{8,4},{9,5},{10,6},{11,7},{20,24},{21,25... | collective-permute-start | bytes 786440 | tf_op jit(solution)/shard_map/ppermute | solution.py:183
  87.8 14.0 %collective-permute-start.16 = (bf16[2,256,256]{2,1,0:T(8,128)(2,1)S(1)}, bf16[2,256,256]{2,1,0:T(8,128)(2,1)S(1)}, u32[]{:S(2)}, u32[]{:S(2)}) collective-permute-start(bf16[2,256,256]{2,1,0:T(8,128)(2,1)S(1)} %shard_map.55), channel_id=1, source_target_pairs={{0,4},{1,5},{2,6},{3,7},{4,0},{5,1},{6,2},{7,3},{8,12},{9,13},{10,... | collective-permute-start | bytes 786440 | tf_op jit(solution)/shard_map/ppermute | solution.py:183
  91.1 25.7 %collective-permute-start.15 = (bf16[2,256,256]{2,1,0:T(8,128)(2,1)S(1)}, bf16[2,256,256]{2,1,0:T(8,128)(2,1)S(1)}, u32[]{:S(2)}, u32[]{:S(2)}) collective-permute-start(bf16[2,256,256]{2,1,0:T(8,128)(2,1)S(1)} %shard_map.54), channel_id=1, source_target_pairs={{0,8},{1,9},{2,10},{3,11},{4,12},{5,13},{6,14},{7,15},{8,0},{9,1},... | collective-permute-start | bytes 786440 | tf_op jit(solution)/shard_map/ppermute | solution.py:183
  94.0 24.0 %collective-permute-start.18 = (bf16[4,256,256]{2,1,0:T(8,128)(2,1)S(1)}, bf16[4,256,256]{2,1,0:T(8,128)(2,1)S(1)}, u32[]{:S(2)}, u32[]{:S(2)}) collective-permute-start(bf16[4,256,256]{2,1,0:T(8,128)(2,1)S(1)} %shard_map.57), channel_id=1, source_target_pairs={{0,12},{1,13},{2,14},{3,15},{12,0},{13,1},{14,2},{15,3},{16,28},{1... | collective-permute-start | bytes 1572872 | tf_op jit(solution)/shard_map/ppermute | solution.py:183

commit v21 on v17

--- a/solution.py
+++ b/solution.py
@@ -217,23 +217,23 @@
     x_left, sent_2 = lax.optimization_barrier((x_left, sent_2))
     across_left = [exchange(part, 1, every) for part in split(x_left, 0, 5 * x_left.shape[0] // 8)]
     other = ([(x_left,), across_left], [(x_psi,), across_psi])
+    other_middle, other_mid = products(3, *other, (middle,), keep_mid=True)
+    sent_other_middle = exchange(other_middle, 12, inner)
+    far_out, other_middle = lax.optimization_barrier((far_out, other_middle))
     other_2 = products(2, *other, (far_out, far_in))
     other_sent_2 = exchange(other_2, 8, every)
-    other_middle, other_mid = products(3, *other, (middle,), keep_mid=True)
-    sent_other_middle = exchange(other_middle, 12, inner)
     other_1 = products(1, *other, (near,))
+    other_sent_1 = exchange(other_1, 4, every)
 
     third, other_1, other_2, other_middle = lax.optimization_barrier((third, other_1, other_2, other_middle))
     last_third = second((own_mid, other_mid), third, dtype, 10**10)
-    last_third, other_1 = lax.optimization_barrier((last_third, other_1))
     sent_third = exchange(last_third, 12, outer)
-    other_sent_1 = exchange(other_1, 4, every)
     right_last, last_third = lax.optimization_barrier((right_env, last_third))
     other_0 = products(0, *other, (right_last,))
 
-    out = place(16, [(0, own_0), (2, other_0), (4, sent_1), (8, sent_2), (10, other_sent_2)], flops=10**10)
+    out = place(16, [(0, own_0), (2, other_0), (4, sent_1), (8, sent_2)], flops=10**10)
     last = [(12, sent_third), (12, sent_own_middle), (14, sent_other_middle)]
-    out = place(16, [(6, other_sent_1)] + last, out, 1)[:, None]
+    out = place(16, [(10, other_sent_2), (6, other_sent_1)] + last, out, 2)[:, None]
     if ops > 1:
         out = lax.psum_scatter(out, "op", scatter_dimension=2, tiled=True).astype(jnp.bfloat16)
     return out

time: 121 us -> 116 us (0.959)
  starting transfers between devices: 29.4 us -> 26 us
  waiting for transfers between devices: 67.2 us -> 65.6 us
    ppermute x20, starting transfers between devices: 29.4 us -> 26 us  [exchange(): return lax.ppermute(array, 'sec', [(s, s ^ bits) for s in members])]
    ppermute x20, waiting for transfers between devices: 67.2 us -> 65.6 us  [exchange(): return lax.ppermute(array, 'sec', [(s, s ^ bits) for s in members])]
  transfers between devices with their start and end apart: 20 -> 20, of which waited for: 10 -> 11; matrix products, arithmetic and copies ran while one was open for 0% -> 0% of each run, Pallas kernels for 15% -> 15%
where the time goes in v21:
time: 116 us; the launch traced here: 115 us
  waiting for transfers between devices  65.6 us (57%)
  starting transfers between devices  26 us (22%)
  Pallas kernels  18.8 us (16%)
  local copies, waits for them, and re-layouts  4.73 us (4%)
    ppermute x20, waiting for transfers between devices, exchange(): return lax.ppermute(array, 'sec', [(s, s ^ bits) for s in members])  65.6 us
    ppermute x20, starting transfers between devices, exchange(): return lax.ppermute(array, 'sec', [(s, s ^ bits) for s in members])  26 us
    pallas_call x8, Pallas kernels, slot(): pl.pallas_call(functools.partial(slot_kernel, step, parts, len(rights)),...  15.1 us
    unnamed x10, local copies, waits for them, and re-layouts  4.73 us
  transfers between devices with their start and end apart: 20, of which 11 were waited for; matrix products, arithmetic and copies ran while one was open for 0% of the time, Pallas kernels for 15%

profile of v21, /device:TPU:0, one launch (start us, length us, event | category | flops | bytes accessed | tf_op | source)
XLA Modules:
  0.0 115.3 jit_solution(5225724999780046406)
XLA Ops:
  0.0 0.5 collective-permute-start.3
  0.5 2.5 %collective-permute-start.4 = (bf16[1,16,256,256]{3,2,1,0:T(8,128)(2,1)}, bf16[1,16,256,256]{3,2,1,0:T(8,128)(2,1)S(1)}, u32[]{:S(2)}, u32[]{:S(2)}) collective-permute-start(bf16[1,16,256,256]{3,2,1,0:T(8,128)(2,1)} %refs_2_.7), channel_id=1, source_target_pairs={{0,2},{1,3},{2,0},{3,1},{4,6},{5,7},{6,4},{7,5},{8,10},{9,11},{10,... | collective-permute-start | bytes 6291464 | tf_op jit(solution)/shard_map/ppermute | solution.py:181
  2.9 0.2 collective-permute-start.2
  3.2 1.6 %collective-permute-start = (bf16[8,1,256,256]{3,2,1,0:T(8,128)(2,1)}, bf16[8,1,256,256]{3,2,1,0:T(8,128)(2,1)S(1)}, u32[]{:S(2)}, u32[]{:S(2)}) collective-permute-start(bf16[8,1,256,256]{3,2,1,0:T(8,128)(2,1)} %refs_6_), channel_id=1, source_target_pairs={{0,4},{1,5},{2,6},{3,7},{4,0},{5,1},{6,2},{7,3},{8,12},{9,13},{10,... | collective-permute-start | bytes 3145736 | tf_op jit(solution)/shard_map/ppermute | solution.py:181
  4.7 0.7 collective-permute-start.1
  5.5 0.5 collective-permute-done.2.refs_1_
  6.0 0.0 collective-permute-done.3.refs_3_
  6.0 1.6 %copy-done = bf16[1,16,256,256]{3,2,1,0:T(8,128)(2,1)S(1)} copy-done((bf16[1,16,256,256]{3,2,1,0:T(8,128)(2,1)S(1)}, bf16[1,16,256,256]{3,2,1,0:T(8,128)(2,1)}, u32[]{:S(2)}) %copy-start) | copy-done | bytes 2097176
  7.5 1.2 %copy-done.1 = bf16[8,1,256,256]{3,2,1,0:T(8,128)(2,1)S(1)} copy-done((bf16[8,1,256,256]{3,2,1,0:T(8,128)(2,1)S(1)}, bf16[8,1,256,256]{3,2,1,0:T(8,128)(2,1)}, u32[]{:S(2)}) %copy-start.1) | copy-done | bytes 1048600
  8.8 1.2 %copy-done.2 = bf16[8,1,256,256]{3,2,1,0:T(8,128)(2,1)S(1)} copy-done((bf16[8,1,256,256]{3,2,1,0:T(8,128)(2,1)S(1)}, bf16[8,1,256,256]{3,2,1,0:T(8,128)(2,1)}, u32[]{:S(2)}) %copy-start.2) | copy-done | bytes 1048600
  10.0 0.7 copy-done.4
  10.7 1.9 %shard_map.46.refs_0_ = bf16[2,256,256]{2,1,0:T(8,128)(2,1)S(1)} custom-call(s32[8,16]{1,0:T(8,128)S(1)} %copy-done.4, bf16[8,1,256,256]{3,2,1,0:T(8,128)(2,1)S(1)} %copy-done.1, bf16[8,1,256,256]{3,2,1,0:T(8,128)(2,1)S(1)} %collective-permute-done.2.refs_1_, bf16[1,16,256,256]{3,2,1,0:T(8,128)(2,1)S(1)} %copy-done, ...), custom_call_target="tpu_custom_call" | custom-call | flops 1 | bytes 1 | tf_op jit(solution)/shard_map/pallas_call | solution.py:99
  12.6 16.2 %collective-permute-done.refs_4_.refs_6_ = bf16[8,1,256,256]{3,2,1,0:T(8,128)(2,1)S(1)} collective-permute-done((bf16[8,1,256,256]{3,2,1,0:T(8,128)(2,1)}, bf16[8,1,256,256]{3,2,1,0:T(8,128)(2,1)S(1)}, u32[]{:S(2)}, u32[]{:S(2)}) %collective-permute-start) | collective-permute-done | bytes 1048608 | tf_op jit(solution)/shard_map/ppermute | solution.py:181
  28.7 1.3 %collective-permute-start.6 = (bf16[8,1,256,256]{3,2,1,0:T(8,128)(2,1)S(1)}, bf16[8,1,256,256]{3,2,1,0:T(8,128)(2,1)S(1)}, u32[]{:S(2)}, u32[]{:S(2)}) collective-permute-start(bf16[8,1,256,256]{3,2,1,0:T(8,128)(2,1)S(1)} %collective-permute-done.1.refs_4_.refs_6_), channel_id=1, source_target_pairs={{4,0},{5,1},{6,2},{7,3},{8,12},{9,13},{10,14},{11,15},{20,16},{21,... | collective-permute-start | bytes 3145736 | tf_op jit(solution)/shard_map/ppermute | solution.py:181
  30.0 0.7 collective-permute-start.7
  30.8 1.9 %shard_map.48 = (bf16[2,256,256]{2,1,0:T(8,128)(2,1)S(1)}, bf16[512,2048]{1,0:T(8,128)(2,1)S(1)}) custom-call(s32[8,16]{1,0:T(8,128)S(1)} %copy-done.4, bf16[8,1,256,256]{3,2,1,0:T(8,128)(2,1)S(1)} %copy-done.1, bf16[8,1,256,256]{3,2,1,0:T(8,128)(2,1)S(1)} %collective-permute-done.2.refs_1_, bf16[1,16,256,256]{3,2,1,0:T(8,128)(2,1)S(1)} %copy-done, ...), custom_call_target="tpu_custom_call" | custom-call | flops 1 | bytes 1 | tf_op jit(solution)/shard_map/pallas_call | solution.py:99
  32.6 1.9 %shard_map.47 = bf16[2,256,256]{2,1,0:T(8,128)(2,1)S(1)} custom-call(s32[8,16]{1,0:T(8,128)S(1)} %copy-done.4, bf16[8,1,256,256]{3,2,1,0:T(8,128)(2,1)S(1)} %copy-done.1, bf16[8,1,256,256]{3,2,1,0:T(8,128)(2,1)S(1)} %collective-permute-done.2.refs_1_, bf16[1,16,256,256]{3,2,1,0:T(8,128)(2,1)S(1)} %copy-done, ...), custom_call_target="tpu_custom_call" | custom-call | flops 1 | bytes 1 | tf_op jit(solution)/shard_map/pallas_call | solution.py:99
  34.5 14.9 %collective-permute-done.4.whole.refs_3_ = bf16[1,16,256,256]{3,2,1,0:T(8,128)(2,1)S(1)} collective-permute-done((bf16[1,16,256,256]{3,2,1,0:T(8,128)(2,1)}, bf16[1,16,256,256]{3,2,1,0:T(8,128)(2,1)S(1)}, u32[]{:S(2)}, u32[]{:S(2)}) %collective-permute-start.4) | collective-permute-done | bytes 2097184 | tf_op jit(solution)/shard_map/ppermute | solution.py:181
  49.5 1.7 %collective-permute-start.5 = (bf16[8,1,256,256]{3,2,1,0:T(8,128)(2,1)S(1)}, bf16[8,1,256,256]{3,2,1,0:T(8,128)(2,1)S(1)}, u32[]{:S(2)}, u32[]{:S(2)}) collective-permute-start(bf16[8,1,256,256]{3,2,1,0:T(8,128)(2,1)S(1)} %copy-done.1), channel_id=1, source_target_pairs={{0,2},{1,3},{2,0},{3,1},{4,6},{5,7},{6,4},{7,5},{8,10},{9,11},{10,... | collective-permute-start | bytes 3145736 | tf_op jit(solution)/shard_map/ppermute | solution.py:181
  51.2 1.6 %collective-permute-start.8 = (bf16[2,256,256]{2,1,0:T(8,128)(2,1)S(1)}, bf16[2,256,256]{2,1,0:T(8,128)(2,1)S(1)}, u32[]{:S(2)}, u32[]{:S(2)}) collective-permute-start(bf16[2,256,256]{2,1,0:T(8,128)(2,1)S(1)} %shard_map.47), channel_id=1, source_target_pairs={{0,4},{1,5},{2,6},{3,7},{4,0},{5,1},{6,2},{7,3},{8,12},{9,13},{10,... | collective-permute-start | bytes 786440 | tf_op jit(solution)/shard_map/ppermute | solution.py:181
  52.8 0.7 collective-permute-start.9
  53.4 0.1 shard_map.51
  53.6 5.0 %collective-permute-done.6.refs_4_.refs_6_ = bf16[8,1,256,256]{3,2,1,0:T(8,128)(2,1)S(1)} collective-permute-done((bf16[8,1,256,256]{3,2,1,0:T(8,128)(2,1)S(1)}, bf16[8,1,256,256]{3,2,1,0:T(8,128)(2,1)S(1)}, u32[]{:S(2)}, u32[]{:S(2)}) %collective-permute-start.6) | collective-permute-done | bytes 1048608 | tf_op jit(solution)/shard_map/ppermute | solution.py:181
  58.6 0.0 collective-permute-start.13
  58.6 1.3 %collective-permute-start.15 = (bf16[8,1,256,256]{3,2,1,0:T(8,128)(2,1)S(1)}, bf16[8,1,256,256]{3,2,1,0:T(8,128)(2,1)S(1)}, u32[]{:S(2)}, u32[]{:S(2)}) collective-permute-start(bf16[8,1,256,256]{3,2,1,0:T(8,128)(2,1)S(1)} %collective-permute-done.7.refs_5_.refs_7_), channel_id=1, source_target_pairs={{4,0},{5,1},{6,2},{7,3},{8,12},{9,13},{10,14},{11,15},{20,16},{21,... | collective-permute-start | bytes 3145736 | tf_op jit(solution)/shard_map/ppermute | solution.py:181
  59.9 1.9 %shard_map.49 = bf16[2,256,256]{2,1,0:T(8,128)(2,1)S(1)} custom-call(s32[8,16]{1,0:T(8,128)S(1)} %copy-done.4, bf16[8,1,256,256]{3,2,1,0:T(8,128)(2,1)S(1)} %copy-done.1, bf16[8,1,256,256]{3,2,1,0:T(8,128)(2,1)S(1)} %collective-permute-done.2.refs_1_, bf16[1,16,256,256]{3,2,1,0:T(8,128)(2,1)S(1)} %copy-done, ...), custom_call_target="tpu_custom_call" | custom-call | flops 1 | bytes 1 | tf_op jit(solution)/shard_map/pallas_call | solution.py:99
  61.8 1.2 %collective-permute-done.8.refs_2_ = bf16[2,256,256]{2,1,0:T(8,128)(2,1)S(1)} collective-permute-done((bf16[2,256,256]{2,1,0:T(8,128)(2,1)S(1)}, bf16[2,256,256]{2,1,0:T(8,128)(2,1)S(1)}, u32[]{:S(2)}, u32[]{:S(2)}) %collective-permute-start.8) | collective-permute-done | bytes 262176 | tf_op jit(solution)/shard_map/ppermute | solution.py:181
  63.0 4.6 %collective-permute-start.10 = (bf16[2,256,256]{2,1,0:T(8,128)(2,1)S(1)}, bf16[2,256,256]{2,1,0:T(8,128)(2,1)S(1)}, u32[]{:S(2)}, u32[]{:S(2)}) collective-permute-start(bf16[2,256,256]{2,1,0:T(8,128)(2,1)S(1)} %shard_map.49), channel_id=1, source_target_pairs={{0,8},{1,9},{2,10},{3,11},{4,12},{5,13},{6,14},{7,15},{8,0},{9,1},... | collective-permute-start | bytes 786440 | tf_op jit(solution)/shard_map/ppermute | solution.py:181
  67.6 6.9 %collective-permute-done.5.whole.refs_0_ = bf16[8,1,256,256]{3,2,1,0:T(8,128)(2,1)S(1)} collective-permute-done((bf16[8,1,256,256]{3,2,1,0:T(8,128)(2,1)S(1)}, bf16[8,1,256,256]{3,2,1,0:T(8,128)(2,1)S(1)}, u32[]{:S(2)}, u32[]{:S(2)}) %collective-permute-start.5) | collective-permute-done | bytes 1048608 | tf_op jit(solution)/shard_map/ppermute | solution.py:181
  74.4 3.9 %collective-permute-done.10.refs_3_ = bf16[2,256,256]{2,1,0:T(8,128)(2,1)S(1)} collective-permute-done((bf16[2,256,256]{2,1,0:T(8,128)(2,1)S(1)}, bf16[2,256,256]{2,1,0:T(8,128)(2,1)S(1)}, u32[]{:S(2)}, u32[]{:S(2)}) %collective-permute-start.10) | collective-permute-done | bytes 262176 | tf_op jit(solution)/shard_map/ppermute | solution.py:181
  78.3 0.1 shard_map.50
  78.4 0.1 collective-permute-start.11
  78.5 0.5 collective-permute-start.12
  79.0 2.1 %collective-permute-done.12.refs_2_ = bf16[3,1,256,256]{3,2,1,0:T(8,128)(2,1)S(1)} collective-permute-done((bf16[3,1,256,256]{3,2,1,0:T(8,128)(2,1)S(1)}, bf16[3,1,256,256]{3,2,1,0:T(8,128)(2,1)S(1)}, u32[]{:S(2)}, u32[]{:S(2)}) %collective-permute-start.12) | collective-permute-done | bytes 393248 | tf_op jit(solution)/shard_map/ppermute | solution.py:181
  81.1 1.9 %shard_map.52 = (bf16[2,256,256]{2,1,0:T(8,128)(2,1)S(1)}, bf16[512,2048]{1,0:T(8,128)(2,1)S(1)}) custom-call(s32[8,16]{1,0:T(8,128)S(1)} %copy-done.4, bf16[8,1,256,256]{3,2,1,0:T(8,128)(2,1)S(1)} %collective-permute-done.5.whole.refs_0_, bf16[5,1,256,256]{3,2,1,0:T(8,128)(2,1)S(1)} %collective-permute-done.11.refs_1_, ...), custom_call_target="tpu_custom_call" | custom-call | flops 1 | bytes 1 | tf_op jit(solution)/shard_map/pallas_call | solution.py:99
  83.0 0.7 collective-permute-start.19
  83.7 1.9 %shard_map.54 = bf16[2,256,256]{2,1,0:T(8,128)(2,1)S(1)} custom-call(s32[8,16]{1,0:T(8,128)S(1)} %copy-done.4, bf16[8,1,256,256]{3,2,1,0:T(8,128)(2,1)S(1)} %collective-permute-done.5.whole.refs_0_, bf16[5,1,256,256]{3,2,1,0:T(8,128)(2,1)S(1)} %collective-permute-done.11.refs_1_, bf16[3,1,256,256]{3,2,1,0:T(8,128)(2,1)S(1)} %collective-permute-done.12.refs_2_, ...), custom_call_target="tpu_custom_call" | custom-call | flops 1 | bytes 1 | tf_op jit(solution)/shard_map/pallas_call | solution.py:99
  85.6 1.6 %collective-permute-start.16 = (bf16[2,256,256]{2,1,0:T(8,128)(2,1)S(1)}, bf16[2,256,256]{2,1,0:T(8,128)(2,1)S(1)}, u32[]{:S(2)}, u32[]{:S(2)}) collective-permute-start(bf16[2,256,256]{2,1,0:T(8,128)(2,1)S(1)} %shard_map.54), channel_id=1, source_target_pairs={{0,8},{1,9},{2,10},{3,11},{4,12},{5,13},{6,14},{7,15},{8,0},{9,1},... | collective-permute-start | bytes 786440 | tf_op jit(solution)/shard_map/ppermute | solution.py:181
  87.2 1.9 %shard_map.53 = bf16[2,256,256]{2,1,0:T(8,128)(2,1)S(1)} custom-call(s32[8,16]{1,0:T(8,128)S(1)} %copy-done.4, bf16[8,1,256,256]{3,2,1,0:T(8,128)(2,1)S(1)} %collective-permute-done.5.whole.refs_0_, bf16[5,1,256,256]{3,2,1,0:T(8,128)(2,1)S(1)} %collective-permute-done.11.refs_1_, bf16[3,1,256,256]{3,2,1,0:T(8,128)(2,1)S(1)} %collective-permute-done.12.refs_2_, ...), custom_call_target="tpu_custom_call" | custom-call | flops 1 | bytes 1 | tf_op jit(solution)/shard_map/pallas_call | solution.py:99
  89.0 0.8 collective-permute-start.17
  89.9 2.2 %collective-permute-done.15.refs_2_ = bf16[8,1,256,256]{3,2,1,0:T(8,128)(2,1)S(1)} collective-permute-done((bf16[8,1,256,256]{3,2,1,0:T(8,128)(2,1)S(1)}, bf16[8,1,256,256]{3,2,1,0:T(8,128)(2,1)S(1)}, u32[]{:S(2)}, u32[]{:S(2)}) %collective-permute-start.15) | collective-permute-done | bytes 1048608 | tf_op jit(solution)/shard_map/ppermute | solution.py:181
  92.1 1.3 %shard_map.55 = bf16[4,256,256]{2,1,0:T(8,128)(2,1)S(1)} custom-call(bf16[512,2048]{1,0:T(8,128)(2,1)S(1)} %get-tuple-element.46.refs_0_, bf16[512,2048]{1,0:T(8,128)(2,1)S(1)} %get-tuple-element.47.refs_1_, bf16[8,1,256,256]{3,2,1,0:T(8,128)(2,1)S(1)} %collective-permute-done.15.refs_2_), custom_call_target="tpu_custom_call" | custom-call | flops 10000000000 | bytes 1 | tf_op jit(solution)/shard_map/pallas_call | solution.py:78
  93.3 5.1 %collective-permute-start.18 = (bf16[4,256,256]{2,1,0:T(8,128)(2,1)S(1)}, bf16[4,256,256]{2,1,0:T(8,128)(2,1)S(1)}, u32[]{:S(2)}, u32[]{:S(2)}) collective-permute-start(bf16[4,256,256]{2,1,0:T(8,128)(2,1)S(1)} %shard_map.55), channel_id=1, source_target_pairs={{0,12},{1,13},{2,14},{3,15},{12,0},{13,1},{14,2},{15,3},{16,28},{1... | collective-permute-start | bytes 1572872 | tf_op jit(solution)/shard_map/ppermute | solution.py:181
  98.5 1.9 %shard_map.56.refs_1_ = bf16[2,256,256]{2,1,0:T(8,128)(2,1)S(1)} custom-call(s32[8,16]{1,0:T(8,128)S(1)} %copy-done.4, bf16[8,1,256,256]{3,2,1,0:T(8,128)(2,1)S(1)} %collective-permute-done.5.whole.refs_0_, bf16[5,1,256,256]{3,2,1,0:T(8,128)(2,1)S(1)} %collective-permute-done.11.refs_1_, bf16[3,1,256,256]{3,2,1,0:T(8,128)(2,1)S(1)} %collective-permute-done.12.refs_2_, ...), custom_call_target="tpu_custom_call" | custom-call | flops 1 | bytes 1 | tf_op jit(solution)/shard_map/pallas_call | solution.py:99
  100.4 1.1 shard_map.57.refs_0_
  101.5 12.5 %collective-permute-done.16.refs_1_ = bf16[2,256,256]{2,1,0:T(8,128)(2,1)S(1)} collective-permute-done((bf16[2,256,256]{2,1,0:T(8,128)(2,1)S(1)}, bf16[2,256,256]{2,1,0:T(8,128)(2,1)S(1)}, u32[]{:S(2)}, u32[]{:S(2)}) %collective-permute-start.16) | collective-permute-done | bytes 262176 | tf_op jit(solution)/shard_map/ppermute | solution.py:181
  114.0 0.1 collective-permute-done.17.refs_2_
  114.2 1.1 shard_map.58
  (15 shorter events, 0.0 us)
Async XLA Ops:
  0.0 6.0 %collective-permute-start.3 = (bf16[1,16,256,256]{3,2,1,0:T(8,128)(2,1)}, bf16[1,16,256,256]{3,2,1,0:T(8,128)(2,1)S(1)}, u32[]{:S(2)}, u32[]{:S(2)}) collective-permute-start(bf16[1,16,256,256]{3,2,1,0:T(8,128)(2,1)} %refs_2_.7), channel_id=1, source_target_pairs={{0,1},{1,0},{2,3},{3,2},{4,5},{5,4},{6,7},{7,6},{8,9},{9,8},{10,11... | collective-permute-start | bytes 6291464 | tf_op jit(solution)/shard_map/ppermute | solution.py:181
  0.5 49.0 %collective-permute-start.4 = (bf16[1,16,256,256]{3,2,1,0:T(8,128)(2,1)}, bf16[1,16,256,256]{3,2,1,0:T(8,128)(2,1)S(1)}, u32[]{:S(2)}, u32[]{:S(2)}) collective-permute-start(bf16[1,16,256,256]{3,2,1,0:T(8,128)(2,1)} %refs_2_.7), channel_id=1, source_target_pairs={{0,2},{1,3},{2,0},{3,1},{4,6},{5,7},{6,4},{7,5},{8,10},{9,11},{10,... | collective-permute-start | bytes 6291464 | tf_op jit(solution)/shard_map/ppermute | solution.py:181
  2.9 3.0 %collective-permute-start.2 = (bf16[8,1,256,256]{3,2,1,0:T(8,128)(2,1)}, bf16[8,1,256,256]{3,2,1,0:T(8,128)(2,1)S(1)}, u32[]{:S(2)}, u32[]{:S(2)}) collective-permute-start(bf16[8,1,256,256]{3,2,1,0:T(8,128)(2,1)} %refs_0_.7), channel_id=1, source_target_pairs={{0,1},{1,0},{2,3},{3,2},{4,5},{5,4},{6,7},{7,6},{8,9},{9,8},{10,11... | collective-permute-start | bytes 3145736 | tf_op jit(solution)/shard_map/ppermute | solution.py:181
  3.2 25.6 %collective-permute-start = (bf16[8,1,256,256]{3,2,1,0:T(8,128)(2,1)}, bf16[8,1,256,256]{3,2,1,0:T(8,128)(2,1)S(1)}, u32[]{:S(2)}, u32[]{:S(2)}) collective-permute-start(bf16[8,1,256,256]{3,2,1,0:T(8,128)(2,1)} %refs_6_), channel_id=1, source_target_pairs={{0,4},{1,5},{2,6},{3,7},{4,0},{5,1},{6,2},{7,3},{8,12},{9,13},{10,... | collective-permute-start | bytes 3145736 | tf_op jit(solution)/shard_map/ppermute | solution.py:181
  4.7 24.0 %collective-permute-start.1 = (bf16[8,1,256,256]{3,2,1,0:T(8,128)(2,1)}, bf16[8,1,256,256]{3,2,1,0:T(8,128)(2,1)S(1)}, u32[]{:S(2)}, u32[]{:S(2)}) collective-permute-start(bf16[8,1,256,256]{3,2,1,0:T(8,128)(2,1)} %refs_6_), channel_id=1, source_target_pairs={{4,8},{5,9},{6,10},{7,11},{8,4},{9,5},{10,6},{11,7},{20,24},{21,25... | collective-permute-start | bytes 3145736 | tf_op jit(solution)/shard_map/ppermute | solution.py:181
  6.0 1.6 %copy-start = (bf16[1,16,256,256]{3,2,1,0:T(8,128)(2,1)S(1)}, bf16[1,16,256,256]{3,2,1,0:T(8,128)(2,1)}, u32[]{:S(2)}) copy-start(bf16[1,16,256,256]{3,2,1,0:T(8,128)(2,1)} %refs_2_.7) | copy-start | bytes 6291460
  7.5 1.2 %copy-start.1 = (bf16[8,1,256,256]{3,2,1,0:T(8,128)(2,1)S(1)}, bf16[8,1,256,256]{3,2,1,0:T(8,128)(2,1)}, u32[]{:S(2)}) copy-start(bf16[8,1,256,256]{3,2,1,0:T(8,128)(2,1)} %refs_0_.7) | copy-start | bytes 3145732
  8.8 1.2 %copy-start.2 = (bf16[8,1,256,256]{3,2,1,0:T(8,128)(2,1)S(1)}, bf16[8,1,256,256]{3,2,1,0:T(8,128)(2,1)}, u32[]{:S(2)}) copy-start(bf16[8,1,256,256]{3,2,1,0:T(8,128)(2,1)} %refs_6_) | copy-start | bytes 3145732
  10.0 0.7 copy-start.4
  28.7 29.9 %collective-permute-start.6 = (bf16[8,1,256,256]{3,2,1,0:T(8,128)(2,1)S(1)}, bf16[8,1,256,256]{3,2,1,0:T(8,128)(2,1)S(1)}, u32[]{:S(2)}, u32[]{:S(2)}) collective-permute-start(bf16[8,1,256,256]{3,2,1,0:T(8,128)(2,1)S(1)} %collective-permute-done.1.refs_4_.refs_6_), channel_id=1, source_target_pairs={{4,0},{5,1},{6,2},{7,3},{8,12},{9,13},{10,14},{11,15},{20,16},{21,... | collective-permute-start | bytes 3145736 | tf_op jit(solution)/shard_map/ppermute | solution.py:181
  30.0 28.6 %collective-permute-start.7 = (bf16[8,1,256,256]{3,2,1,0:T(8,128)(2,1)S(1)}, bf16[8,1,256,256]{3,2,1,0:T(8,128)(2,1)S(1)}, u32[]{:S(2)}, u32[]{:S(2)}) collective-permute-start(bf16[8,1,256,256]{3,2,1,0:T(8,128)(2,1)S(1)} %collective-permute-done.refs_4_.refs_6_), channel_id=1, source_target_pairs={{4,8},{5,9},{6,10},{7,11},{8,4},{9,5},{10,6},{11,7},{20,24},{21,25... | collective-permute-start | bytes 3145736 | tf_op jit(solution)/shard_map/ppermute | solution.py:181
  49.5 25.0 %collective-permute-start.5 = (bf16[8,1,256,256]{3,2,1,0:T(8,128)(2,1)S(1)}, bf16[8,1,256,256]{3,2,1,0:T(8,128)(2,1)S(1)}, u32[]{:S(2)}, u32[]{:S(2)}) collective-permute-start(bf16[8,1,256,256]{3,2,1,0:T(8,128)(2,1)S(1)} %copy-done.1), channel_id=1, source_target_pairs={{0,2},{1,3},{2,0},{3,1},{4,6},{5,7},{6,4},{7,5},{8,10},{9,11},{10,... | collective-permute-start | bytes 3145736 | tf_op jit(solution)/shard_map/ppermute | solution.py:181
  51.2 11.8 %collective-permute-start.8 = (bf16[2,256,256]{2,1,0:T(8,128)(2,1)S(1)}, bf16[2,256,256]{2,1,0:T(8,128)(2,1)S(1)}, u32[]{:S(2)}, u32[]{:S(2)}) collective-permute-start(bf16[2,256,256]{2,1,0:T(8,128)(2,1)S(1)} %shard_map.47), channel_id=1, source_target_pairs={{0,4},{1,5},{2,6},{3,7},{4,0},{5,1},{6,2},{7,3},{8,12},{9,13},{10,... | collective-permute-start | bytes 786440 | tf_op jit(solution)/shard_map/ppermute | solution.py:181
  52.8 10.2 %collective-permute-start.9 = (bf16[2,256,256]{2,1,0:T(8,128)(2,1)S(1)}, bf16[2,256,256]{2,1,0:T(8,128)(2,1)S(1)}, u32[]{:S(2)}, u32[]{:S(2)}) collective-permute-start(bf16[2,256,256]{2,1,0:T(8,128)(2,1)S(1)} %get-tuple-element.38), channel_id=1, source_target_pairs={{4,8},{5,9},{6,10},{7,11},{8,4},{9,5},{10,6},{11,7},{20,24},{21,25... | collective-permute-start | bytes 786440 | tf_op jit(solution)/shard_map/ppermute | solution.py:181
  58.6 20.3 %collective-permute-start.13 = (bf16[1,9,256,256]{3,2,1,0:T(8,128)(2,1)S(1)}, bf16[1,9,256,256]{3,2,1,0:T(8,128)(2,1)S(1)}, u32[]{:S(2)}, u32[]{:S(2)}) collective-permute-start(bf16[1,9,256,256]{3,2,1,0:T(8,128)(2,1)S(1)} %get-tuple-element.44), channel_id=1, source_target_pairs={{0,1},{1,0},{2,3},{3,2},{4,5},{5,4},{6,7},{7,6},{8,9},{9,8},{10,11... | collective-permute-start | bytes 3538952 | tf_op jit(solution)/shard_map/ppermute | solution.py:181
  58.6 33.4 %collective-permute-start.15 = (bf16[8,1,256,256]{3,2,1,0:T(8,128)(2,1)S(1)}, bf16[8,1,256,256]{3,2,1,0:T(8,128)(2,1)S(1)}, u32[]{:S(2)}, u32[]{:S(2)}) collective-permute-start(bf16[8,1,256,256]{3,2,1,0:T(8,128)(2,1)S(1)} %collective-permute-done.7.refs_5_.refs_7_), channel_id=1, source_target_pairs={{4,0},{5,1},{6,2},{7,3},{8,12},{9,13},{10,14},{11,15},{20,16},{21,... | collective-permute-start | bytes 3145736 | tf_op jit(solution)/shard_map/ppermute | solution.py:181
  63.0 15.3 %collective-permute-start.10 = (bf16[2,256,256]{2,1,0:T(8,128)(2,1)S(1)}, bf16[2,256,256]{2,1,0:T(8,128)(2,1)S(1)}, u32[]{:S(2)}, u32[]{:S(2)}) collective-permute-start(bf16[2,256,256]{2,1,0:T(8,128)(2,1)S(1)} %shard_map.49), channel_id=1, source_target_pairs={{0,8},{1,9},{2,10},{3,11},{4,12},{5,13},{6,14},{7,15},{8,0},{9,1},... | collective-permute-start | bytes 786440 | tf_op jit(solution)/shard_map/ppermute | solution.py:181
  67.6 11.4 %collective-permute-start.14 = (bf16[1,7,256,256]{3,2,1,0:T(8,128)(2,1)S(1)}, bf16[1,7,256,256]{3,2,1,0:T(8,128)(2,1)S(1)}, u32[]{:S(2)}, u32[]{:S(2)}) collective-permute-start(bf16[1,7,256,256]{3,2,1,0:T(8,128)(2,1)S(1)} %get-tuple-element.45), channel_id=1, source_target_pairs={{0,1},{1,0},{2,3},{3,2},{4,5},{5,4},{6,7},{7,6},{8,9},{9,8},{10,11... | collective-permute-start | bytes 2752520 | tf_op jit(solution)/shard_map/ppermute | solution.py:181
  78.4 2.7 %collective-permute-start.11 = (bf16[5,1,256,256]{3,2,1,0:T(8,128)(2,1)S(1)}, bf16[5,1,256,256]{3,2,1,0:T(8,128)(2,1)S(1)}, u32[]{:S(2)}, u32[]{:S(2)}) collective-permute-start(bf16[5,1,256,256]{3,2,1,0:T(8,128)(2,1)S(1)} %get-tuple-element.41), channel_id=1, source_target_pairs={{0,1},{1,0},{2,3},{3,2},{4,5},{5,4},{6,7},{7,6},{8,9},{9,8},{10,11... | collective-permute-start | bytes 1966088 | tf_op jit(solution)/shard_map/ppermute | solution.py:181
  78.5 2.6 %collective-permute-start.12 = (bf16[3,1,256,256]{3,2,1,0:T(8,128)(2,1)S(1)}, bf16[3,1,256,256]{3,2,1,0:T(8,128)(2,1)S(1)}, u32[]{:S(2)}, u32[]{:S(2)}) collective-permute-start(bf16[3,1,256,256]{3,2,1,0:T(8,128)(2,1)S(1)} %get-tuple-element.42), channel_id=1, source_target_pairs={{0,1},{1,0},{2,3},{3,2},{4,5},{5,4},{6,7},{7,6},{8,9},{9,8},{10,11... | collective-permute-start | bytes 1179656 | tf_op jit(solution)/shard_map/ppermute | solution.py:181
  83.0 31.2 %collective-permute-start.19 = (bf16[2,256,256]{2,1,0:T(8,128)(2,1)S(1)}, bf16[2,256,256]{2,1,0:T(8,128)(2,1)S(1)}, u32[]{:S(2)}, u32[]{:S(2)}) collective-permute-start(bf16[2,256,256]{2,1,0:T(8,128)(2,1)S(1)} %get-tuple-element.48), channel_id=1, source_target_pairs={{4,8},{5,9},{6,10},{7,11},{8,4},{9,5},{10,6},{11,7},{20,24},{21,25... | collective-permute-start | bytes 786440 | tf_op jit(solution)/shard_map/ppermute | solution.py:181
  85.6 28.5 %collective-permute-start.16 = (bf16[2,256,256]{2,1,0:T(8,128)(2,1)S(1)}, bf16[2,256,256]{2,1,0:T(8,128)(2,1)S(1)}, u32[]{:S(2)}, u32[]{:S(2)}) collective-permute-start(bf16[2,256,256]{2,1,0:T(8,128)(2,1)S(1)} %shard_map.54), channel_id=1, source_target_pairs={{0,8},{1,9},{2,10},{3,11},{4,12},{5,13},{6,14},{7,15},{8,0},{9,1},... | collective-permute-start | bytes 786440 | tf_op jit(solution)/shard_map/ppermute | solution.py:181
  89.0 25.1 %collective-permute-start.17 = (bf16[2,256,256]{2,1,0:T(8,128)(2,1)S(1)}, bf16[2,256,256]{2,1,0:T(8,128)(2,1)S(1)}, u32[]{:S(2)}, u32[]{:S(2)}) collective-permute-start(bf16[2,256,256]{2,1,0:T(8,128)(2,1)S(1)} %shard_map.53), channel_id=1, source_target_pairs={{0,4},{1,5},{2,6},{3,7},{4,0},{5,1},{6,2},{7,3},{8,12},{9,13},{10,... | collective-permute-start | bytes 786440 | tf_op jit(solution)/shard_map/ppermute | solution.py:181
  92.1 6.4 %copy-start.3 = (bf16[8,1,256,256]{3,2,1,0:T(8,128)(2,1)S(1)}, bf16[8,1,256,256]{3,2,1,0:T(8,128)(2,1)}, u32[]{:S(2)}) copy-start(bf16[8,1,256,256]{3,2,1,0:T(8,128)(2,1)} %refs_6_) | copy-start | bytes 3145732
  93.3 20.8 %collective-permute-start.18 = (bf16[4,256,256]{2,1,0:T(8,128)(2,1)S(1)}, bf16[4,256,256]{2,1,0:T(8,128)(2,1)S(1)}, u32[]{:S(2)}, u32[]{:S(2)}) collective-permute-start(bf16[4,256,256]{2,1,0:T(8,128)(2,1)S(1)} %shard_map.55), channel_id=1, source_target_pairs={{0,12},{1,13},{2,14},{3,15},{12,0},{13,1},{14,2},{15,3},{16,28},{1... | collective-permute-start | bytes 1572872 | tf_op jit(solution)/shard_map/ppermute | solution.py:181

commit v22 on v21

--- a/solution.py
+++ b/solution.py
@@ -194,7 +194,7 @@
     middle = exchange(right_env, 12, inner)
     x_psi = exchange(psi, 2, every)
     own = ([(left_env,), (exchange(left_env, 1, every),)], [(psi,), (exchange(psi, 1, every),)])
-    own_0 = products(0, *own, (right_env,))
+    own_0 = products(0, *own, (right_env,), flops=2 * 10**10)
 
     near, middle, own_0 = lax.optimization_barrier((near, middle, own_0))
     far_in = exchange(near, 12, inner)

time: 116 us -> 118 us (1.017)
  starting transfers between devices: 26 us -> 29.1 us
    ppermute x20, starting transfers between devices: 26 us -> 29.1 us  [exchange(): return lax.ppermute(array, 'sec', [(s, s ^ bits) for s in members])]
  transfers between devices with their start and end apart: 20 -> 20, of which waited for: 11 -> 8; matrix products, arithmetic and copies ran while one was open for 0% -> 0% of each run, Pallas kernels for 15% -> 15%
where the time goes in v22:
time: 118 us; the launch traced here: 117 us
  waiting for transfers between devices  64.5 us (55%)
  starting transfers between devices  29.1 us (25%)
  Pallas kernels  18.8 us (16%)
  local copies, waits for them, and re-layouts  4.73 us (4%)
    ppermute x20, waiting for transfers between devices, exchange(): return lax.ppermute(array, 'sec', [(s, s ^ bits) for s in members])  64.5 us
    ppermute x20, starting transfers between devices, exchange(): return lax.ppermute(array, 'sec', [(s, s ^ bits) for s in members])  29.1 us
    pallas_call x8, Pallas kernels, slot(): pl.pallas_call(functools.partial(slot_kernel, step, parts, len(rights)),...  15.1 us
    unnamed x10, local copies, waits for them, and re-layouts  4.73 us
  transfers between devices with their start and end apart: 20, of which 8 were waited for; matrix products, arithmetic and copies ran while one was open for 0% of the time, Pallas kernels for 15%

profile of v22, /device:TPU:0, one launch (start us, length us, event | category | flops | bytes accessed | tf_op | source)
XLA Modules:
  0.0 117.4 jit_solution(11625403811995754941)
XLA Ops:
  0.0 0.5 collective-permute-start.3
  0.5 0.1 collective-permute-start.2
  0.5 3.0 %collective-permute-start = (bf16[8,1,256,256]{3,2,1,0:T(8,128)(2,1)}, bf16[8,1,256,256]{3,2,1,0:T(8,128)(2,1)S(1)}, u32[]{:S(2)}, u32[]{:S(2)}) collective-permute-start(bf16[8,1,256,256]{3,2,1,0:T(8,128)(2,1)} %refs_6_), channel_id=1, source_target_pairs={{0,4},{1,5},{2,6},{3,7},{4,0},{5,1},{6,2},{7,3},{8,12},{9,13},{10,... | collective-permute-start | bytes 3145736 | tf_op jit(solution)/shard_map/ppermute | solution.py:181
  3.5 0.7 collective-permute-start.1
  4.3 1.6 %collective-permute-start.4 = (bf16[1,16,256,256]{3,2,1,0:T(8,128)(2,1)}, bf16[1,16,256,256]{3,2,1,0:T(8,128)(2,1)S(1)}, u32[]{:S(2)}, u32[]{:S(2)}) collective-permute-start(bf16[1,16,256,256]{3,2,1,0:T(8,128)(2,1)} %refs_2_.7), channel_id=1, source_target_pairs={{0,2},{1,3},{2,0},{3,1},{4,6},{5,7},{6,4},{7,5},{8,10},{9,11},{10,... | collective-permute-start | bytes 6291464 | tf_op jit(solution)/shard_map/ppermute | solution.py:181
  5.8 0.1 collective-permute-done.2.refs_1_
  6.0 1.6 %copy-done = bf16[1,16,256,256]{3,2,1,0:T(8,128)(2,1)S(1)} copy-done((bf16[1,16,256,256]{3,2,1,0:T(8,128)(2,1)S(1)}, bf16[1,16,256,256]{3,2,1,0:T(8,128)(2,1)}, u32[]{:S(2)}) %copy-start) | copy-done | bytes 2097176
  7.5 1.2 %copy-done.1 = bf16[8,1,256,256]{3,2,1,0:T(8,128)(2,1)S(1)} copy-done((bf16[8,1,256,256]{3,2,1,0:T(8,128)(2,1)S(1)}, bf16[8,1,256,256]{3,2,1,0:T(8,128)(2,1)}, u32[]{:S(2)}) %copy-start.1) | copy-done | bytes 1048600
  8.8 1.2 %copy-done.2 = bf16[8,1,256,256]{3,2,1,0:T(8,128)(2,1)S(1)} copy-done((bf16[8,1,256,256]{3,2,1,0:T(8,128)(2,1)S(1)}, bf16[8,1,256,256]{3,2,1,0:T(8,128)(2,1)}, u32[]{:S(2)}) %copy-start.2) | copy-done | bytes 1048600
  10.0 0.7 copy-done.4
  10.7 1.9 %shard_map.46.refs_0_ = bf16[2,256,256]{2,1,0:T(8,128)(2,1)S(1)} custom-call(s32[8,16]{1,0:T(8,128)S(1)} %copy-done.4, bf16[8,1,256,256]{3,2,1,0:T(8,128)(2,1)S(1)} %copy-done.1, bf16[8,1,256,256]{3,2,1,0:T(8,128)(2,1)S(1)} %collective-permute-done.2.refs_1_, bf16[1,16,256,256]{3,2,1,0:T(8,128)(2,1)S(1)} %copy-done, ...), custom_call_target="tpu_custom_call" | custom-call | flops 20000000000 | bytes 1 | tf_op jit(solution)/shard_map/pallas_call | solution.py:99
  12.6 14.5 %collective-permute-done.refs_4_.refs_6_ = bf16[8,1,256,256]{3,2,1,0:T(8,128)(2,1)S(1)} collective-permute-done((bf16[8,1,256,256]{3,2,1,0:T(8,128)(2,1)}, bf16[8,1,256,256]{3,2,1,0:T(8,128)(2,1)S(1)}, u32[]{:S(2)}, u32[]{:S(2)}) %collective-permute-start) | collective-permute-done | bytes 1048608 | tf_op jit(solution)/shard_map/ppermute | solution.py:181
  27.1 0.0 collective-permute-done.1.refs_4_.refs_6_
  27.1 1.3 %collective-permute-start.6 = (bf16[8,1,256,256]{3,2,1,0:T(8,128)(2,1)S(1)}, bf16[8,1,256,256]{3,2,1,0:T(8,128)(2,1)S(1)}, u32[]{:S(2)}, u32[]{:S(2)}) collective-permute-start(bf16[8,1,256,256]{3,2,1,0:T(8,128)(2,1)S(1)} %collective-permute-done.1.refs_4_.refs_6_), channel_id=1, source_target_pairs={{4,0},{5,1},{6,2},{7,3},{8,12},{9,13},{10,14},{11,15},{20,16},{21,... | collective-permute-start | bytes 3145736 | tf_op jit(solution)/shard_map/ppermute | solution.py:181
  28.4 0.7 collective-permute-start.7
  29.1 1.9 %shard_map.48 = (bf16[2,256,256]{2,1,0:T(8,128)(2,1)S(1)}, bf16[512,2048]{1,0:T(8,128)(2,1)S(1)}) custom-call(s32[8,16]{1,0:T(8,128)S(1)} %copy-done.4, bf16[8,1,256,256]{3,2,1,0:T(8,128)(2,1)S(1)} %copy-done.1, bf16[8,1,256,256]{3,2,1,0:T(8,128)(2,1)S(1)} %collective-permute-done.2.refs_1_, bf16[1,16,256,256]{3,2,1,0:T(8,128)(2,1)S(1)} %copy-done, ...), custom_call_target="tpu_custom_call" | custom-call | flops 1 | bytes 1 | tf_op jit(solution)/shard_map/pallas_call | solution.py:99
  31.0 1.9 %shard_map.47 = bf16[2,256,256]{2,1,0:T(8,128)(2,1)S(1)} custom-call(s32[8,16]{1,0:T(8,128)S(1)} %copy-done.4, bf16[8,1,256,256]{3,2,1,0:T(8,128)(2,1)S(1)} %copy-done.1, bf16[8,1,256,256]{3,2,1,0:T(8,128)(2,1)S(1)} %collective-permute-done.2.refs_1_, bf16[1,16,256,256]{3,2,1,0:T(8,128)(2,1)S(1)} %copy-done, ...), custom_call_target="tpu_custom_call" | custom-call | flops 1 | bytes 1 | tf_op jit(solution)/shard_map/pallas_call | solution.py:99
  32.9 18.9 %collective-permute-done.4.whole.refs_3_ = bf16[1,16,256,256]{3,2,1,0:T(8,128)(2,1)S(1)} collective-permute-done((bf16[1,16,256,256]{3,2,1,0:T(8,128)(2,1)}, bf16[1,16,256,256]{3,2,1,0:T(8,128)(2,1)S(1)}, u32[]{:S(2)}, u32[]{:S(2)}) %collective-permute-start.4) | collective-permute-done | bytes 2097184 | tf_op jit(solution)/shard_map/ppermute | solution.py:181
  51.8 1.5 %collective-permute-start.5 = (bf16[8,1,256,256]{3,2,1,0:T(8,128)(2,1)S(1)}, bf16[8,1,256,256]{3,2,1,0:T(8,128)(2,1)S(1)}, u32[]{:S(2)}, u32[]{:S(2)}) collective-permute-start(bf16[8,1,256,256]{3,2,1,0:T(8,128)(2,1)S(1)} %copy-done.1), channel_id=1, source_target_pairs={{0,2},{1,3},{2,0},{3,1},{4,6},{5,7},{6,4},{7,5},{8,10},{9,11},{10,... | collective-permute-start | bytes 3145736 | tf_op jit(solution)/shard_map/ppermute | solution.py:181
  53.3 4.1 %collective-permute-start.8 = (bf16[2,256,256]{2,1,0:T(8,128)(2,1)S(1)}, bf16[2,256,256]{2,1,0:T(8,128)(2,1)S(1)}, u32[]{:S(2)}, u32[]{:S(2)}) collective-permute-start(bf16[2,256,256]{2,1,0:T(8,128)(2,1)S(1)} %shard_map.47), channel_id=1, source_target_pairs={{0,4},{1,5},{2,6},{3,7},{4,0},{5,1},{6,2},{7,3},{8,12},{9,13},{10,... | collective-permute-start | bytes 786440 | tf_op jit(solution)/shard_map/ppermute | solution.py:181
  57.3 0.7 collective-permute-start.9
  58.0 0.1 shard_map.51
  58.2 0.0 collective-permute-done.6.refs_4_.refs_6_
  58.2 0.1 collective-permute-start.13
  58.2 0.0 collective-permute-done.7.refs_5_.refs_7_
  58.3 1.3 %collective-permute-start.15 = (bf16[8,1,256,256]{3,2,1,0:T(8,128)(2,1)S(1)}, bf16[8,1,256,256]{3,2,1,0:T(8,128)(2,1)S(1)}, u32[]{:S(2)}, u32[]{:S(2)}) collective-permute-start(bf16[8,1,256,256]{3,2,1,0:T(8,128)(2,1)S(1)} %collective-permute-done.7.refs_5_.refs_7_), channel_id=1, source_target_pairs={{4,0},{5,1},{6,2},{7,3},{8,12},{9,13},{10,14},{11,15},{20,16},{21,... | collective-permute-start | bytes 3145736 | tf_op jit(solution)/shard_map/ppermute | solution.py:181
  59.6 1.9 %shard_map.49 = bf16[2,256,256]{2,1,0:T(8,128)(2,1)S(1)} custom-call(s32[8,16]{1,0:T(8,128)S(1)} %copy-done.4, bf16[8,1,256,256]{3,2,1,0:T(8,128)(2,1)S(1)} %copy-done.1, bf16[8,1,256,256]{3,2,1,0:T(8,128)(2,1)S(1)} %collective-permute-done.2.refs_1_, bf16[1,16,256,256]{3,2,1,0:T(8,128)(2,1)S(1)} %copy-done, ...), custom_call_target="tpu_custom_call" | custom-call | flops 1 | bytes 1 | tf_op jit(solution)/shard_map/pallas_call | solution.py:99
  61.5 0.6 collective-permute-done.8.refs_2_
  62.1 3.7 %collective-permute-start.10 = (bf16[2,256,256]{2,1,0:T(8,128)(2,1)S(1)}, bf16[2,256,256]{2,1,0:T(8,128)(2,1)S(1)}, u32[]{:S(2)}, u32[]{:S(2)}) collective-permute-start(bf16[2,256,256]{2,1,0:T(8,128)(2,1)S(1)} %shard_map.49), channel_id=1, source_target_pairs={{0,8},{1,9},{2,10},{3,11},{4,12},{5,13},{6,14},{7,15},{8,0},{9,1},... | collective-permute-start | bytes 786440 | tf_op jit(solution)/shard_map/ppermute | solution.py:181
  65.8 9.9 %collective-permute-done.5.whole.refs_0_ = bf16[8,1,256,256]{3,2,1,0:T(8,128)(2,1)S(1)} collective-permute-done((bf16[8,1,256,256]{3,2,1,0:T(8,128)(2,1)S(1)}, bf16[8,1,256,256]{3,2,1,0:T(8,128)(2,1)S(1)}, u32[]{:S(2)}, u32[]{:S(2)}) %collective-permute-start.5) | collective-permute-done | bytes 1048608 | tf_op jit(solution)/shard_map/ppermute | solution.py:181
  75.7 1.3 %collective-permute-done.10.refs_3_ = bf16[2,256,256]{2,1,0:T(8,128)(2,1)S(1)} collective-permute-done((bf16[2,256,256]{2,1,0:T(8,128)(2,1)S(1)}, bf16[2,256,256]{2,1,0:T(8,128)(2,1)S(1)}, u32[]{:S(2)}, u32[]{:S(2)}) %collective-permute-start.10) | collective-permute-done | bytes 262176 | tf_op jit(solution)/shard_map/ppermute | solution.py:181
  77.0 0.1 shard_map.50
  77.1 0.1 collective-permute-start.11
  77.2 0.5 collective-permute-start.12
  77.7 2.1 %collective-permute-done.12.refs_2_ = bf16[3,1,256,256]{3,2,1,0:T(8,128)(2,1)S(1)} collective-permute-done((bf16[3,1,256,256]{3,2,1,0:T(8,128)(2,1)S(1)}, bf16[3,1,256,256]{3,2,1,0:T(8,128)(2,1)S(1)}, u32[]{:S(2)}, u32[]{:S(2)}) %collective-permute-start.12) | collective-permute-done | bytes 393248 | tf_op jit(solution)/shard_map/ppermute | solution.py:181
  79.8 1.9 %shard_map.52 = (bf16[2,256,256]{2,1,0:T(8,128)(2,1)S(1)}, bf16[512,2048]{1,0:T(8,128)(2,1)S(1)}) custom-call(s32[8,16]{1,0:T(8,128)S(1)} %copy-done.4, bf16[8,1,256,256]{3,2,1,0:T(8,128)(2,1)S(1)} %collective-permute-done.5.whole.refs_0_, bf16[5,1,256,256]{3,2,1,0:T(8,128)(2,1)S(1)} %collective-permute-done.11.refs_1_, ...), custom_call_target="tpu_custom_call" | custom-call | flops 1 | bytes 1 | tf_op jit(solution)/shard_map/pallas_call | solution.py:99
  81.7 0.7 collective-permute-start.19
  82.4 1.9 %shard_map.54 = bf16[2,256,256]{2,1,0:T(8,128)(2,1)S(1)} custom-call(s32[8,16]{1,0:T(8,128)S(1)} %copy-done.4, bf16[8,1,256,256]{3,2,1,0:T(8,128)(2,1)S(1)} %collective-permute-done.5.whole.refs_0_, bf16[5,1,256,256]{3,2,1,0:T(8,128)(2,1)S(1)} %collective-permute-done.11.refs_1_, bf16[3,1,256,256]{3,2,1,0:T(8,128)(2,1)S(1)} %collective-permute-done.12.refs_2_, ...), custom_call_target="tpu_custom_call" | custom-call | flops 1 | bytes 1 | tf_op jit(solution)/shard_map/pallas_call | solution.py:99
  84.3 5.2 %collective-permute-start.16 = (bf16[2,256,256]{2,1,0:T(8,128)(2,1)S(1)}, bf16[2,256,256]{2,1,0:T(8,128)(2,1)S(1)}, u32[]{:S(2)}, u32[]{:S(2)}) collective-permute-start(bf16[2,256,256]{2,1,0:T(8,128)(2,1)S(1)} %shard_map.54), channel_id=1, source_target_pairs={{0,8},{1,9},{2,10},{3,11},{4,12},{5,13},{6,14},{7,15},{8,0},{9,1},... | collective-permute-start | bytes 786440 | tf_op jit(solution)/shard_map/ppermute | solution.py:181
  89.5 1.9 %shard_map.53 = bf16[2,256,256]{2,1,0:T(8,128)(2,1)S(1)} custom-call(s32[8,16]{1,0:T(8,128)S(1)} %copy-done.4, bf16[8,1,256,256]{3,2,1,0:T(8,128)(2,1)S(1)} %collective-permute-done.5.whole.refs_0_, bf16[5,1,256,256]{3,2,1,0:T(8,128)(2,1)S(1)} %collective-permute-done.11.refs_1_, bf16[3,1,256,256]{3,2,1,0:T(8,128)(2,1)S(1)} %collective-permute-done.12.refs_2_, ...), custom_call_target="tpu_custom_call" | custom-call | flops 1 | bytes 1 | tf_op jit(solution)/shard_map/pallas_call | solution.py:99
  91.4 0.1 collective-permute-start.17
  91.5 0.0 copy-start.3
  91.5 1.3 %shard_map.55 = bf16[4,256,256]{2,1,0:T(8,128)(2,1)S(1)} custom-call(bf16[512,2048]{1,0:T(8,128)(2,1)S(1)} %get-tuple-element.46.refs_0_, bf16[512,2048]{1,0:T(8,128)(2,1)S(1)} %get-tuple-element.47.refs_1_, bf16[8,1,256,256]{3,2,1,0:T(8,128)(2,1)S(1)} %collective-permute-done.15.refs_2_), custom_call_target="tpu_custom_call" | custom-call | flops 10000000000 | bytes 1 | tf_op jit(solution)/shard_map/pallas_call | solution.py:78
  92.8 3.5 %collective-permute-start.18 = (bf16[4,256,256]{2,1,0:T(8,128)(2,1)S(1)}, bf16[4,256,256]{2,1,0:T(8,128)(2,1)S(1)}, u32[]{:S(2)}, u32[]{:S(2)}) collective-permute-start(bf16[4,256,256]{2,1,0:T(8,128)(2,1)S(1)} %shard_map.55), channel_id=1, source_target_pairs={{0,12},{1,13},{2,14},{3,15},{12,0},{13,1},{14,2},{15,3},{16,28},{1... | collective-permute-start | bytes 1572872 | tf_op jit(solution)/shard_map/ppermute | solution.py:181
  96.3 1.9 %shard_map.56.refs_1_ = bf16[2,256,256]{2,1,0:T(8,128)(2,1)S(1)} custom-call(s32[8,16]{1,0:T(8,128)S(1)} %copy-done.4, bf16[8,1,256,256]{3,2,1,0:T(8,128)(2,1)S(1)} %collective-permute-done.5.whole.refs_0_, bf16[5,1,256,256]{3,2,1,0:T(8,128)(2,1)S(1)} %collective-permute-done.11.refs_1_, bf16[3,1,256,256]{3,2,1,0:T(8,128)(2,1)S(1)} %collective-permute-done.12.refs_2_, ...), custom_call_target="tpu_custom_call" | custom-call | flops 1 | bytes 1 | tf_op jit(solution)/shard_map/pallas_call | solution.py:99
  98.2 1.1 shard_map.57.refs_0_
  99.3 16.9 %collective-permute-done.16.refs_1_ = bf16[2,256,256]{2,1,0:T(8,128)(2,1)S(1)} collective-permute-done((bf16[2,256,256]{2,1,0:T(8,128)(2,1)S(1)}, bf16[2,256,256]{2,1,0:T(8,128)(2,1)S(1)}, u32[]{:S(2)}, u32[]{:S(2)}) %collective-permute-start.16) | collective-permute-done | bytes 262176 | tf_op jit(solution)/shard_map/ppermute | solution.py:181
  116.3 1.1 shard_map.58
  (15 shorter events, 0.0 us)
Async XLA Ops:
  0.0 6.0 %collective-permute-start.3 = (bf16[1,16,256,256]{3,2,1,0:T(8,128)(2,1)}, bf16[1,16,256,256]{3,2,1,0:T(8,128)(2,1)S(1)}, u32[]{:S(2)}, u32[]{:S(2)}) collective-permute-start(bf16[1,16,256,256]{3,2,1,0:T(8,128)(2,1)} %refs_2_.7), channel_id=1, source_target_pairs={{0,1},{1,0},{2,3},{3,2},{4,5},{5,4},{6,7},{7,6},{8,9},{9,8},{10,11... | collective-permute-start | bytes 6291464 | tf_op jit(solution)/shard_map/ppermute | solution.py:181
  0.5 5.5 %collective-permute-start.2 = (bf16[8,1,256,256]{3,2,1,0:T(8,128)(2,1)}, bf16[8,1,256,256]{3,2,1,0:T(8,128)(2,1)S(1)}, u32[]{:S(2)}, u32[]{:S(2)}) collective-permute-start(bf16[8,1,256,256]{3,2,1,0:T(8,128)(2,1)} %refs_0_.7), channel_id=1, source_target_pairs={{0,1},{1,0},{2,3},{3,2},{4,5},{5,4},{6,7},{7,6},{8,9},{9,8},{10,11... | collective-permute-start | bytes 3145736 | tf_op jit(solution)/shard_map/ppermute | solution.py:181
  0.5 26.6 %collective-permute-start = (bf16[8,1,256,256]{3,2,1,0:T(8,128)(2,1)}, bf16[8,1,256,256]{3,2,1,0:T(8,128)(2,1)S(1)}, u32[]{:S(2)}, u32[]{:S(2)}) collective-permute-start(bf16[8,1,256,256]{3,2,1,0:T(8,128)(2,1)} %refs_6_), channel_id=1, source_target_pairs={{0,4},{1,5},{2,6},{3,7},{4,0},{5,1},{6,2},{7,3},{8,12},{9,13},{10,... | collective-permute-start | bytes 3145736 | tf_op jit(solution)/shard_map/ppermute | solution.py:181
  3.5 23.5 %collective-permute-start.1 = (bf16[8,1,256,256]{3,2,1,0:T(8,128)(2,1)}, bf16[8,1,256,256]{3,2,1,0:T(8,128)(2,1)S(1)}, u32[]{:S(2)}, u32[]{:S(2)}) collective-permute-start(bf16[8,1,256,256]{3,2,1,0:T(8,128)(2,1)} %refs_6_), channel_id=1, source_target_pairs={{4,8},{5,9},{6,10},{7,11},{8,4},{9,5},{10,6},{11,7},{20,24},{21,25... | collective-permute-start | bytes 3145736 | tf_op jit(solution)/shard_map/ppermute | solution.py:181
  4.3 47.5 %collective-permute-start.4 = (bf16[1,16,256,256]{3,2,1,0:T(8,128)(2,1)}, bf16[1,16,256,256]{3,2,1,0:T(8,128)(2,1)S(1)}, u32[]{:S(2)}, u32[]{:S(2)}) collective-permute-start(bf16[1,16,256,256]{3,2,1,0:T(8,128)(2,1)} %refs_2_.7), channel_id=1, source_target_pairs={{0,2},{1,3},{2,0},{3,1},{4,6},{5,7},{6,4},{7,5},{8,10},{9,11},{10,... | collective-permute-start | bytes 6291464 | tf_op jit(solution)/shard_map/ppermute | solution.py:181
  6.0 1.6 %copy-start = (bf16[1,16,256,256]{3,2,1,0:T(8,128)(2,1)S(1)}, bf16[1,16,256,256]{3,2,1,0:T(8,128)(2,1)}, u32[]{:S(2)}) copy-start(bf16[1,16,256,256]{3,2,1,0:T(8,128)(2,1)} %refs_2_.7) | copy-start | bytes 6291460
  7.5 1.2 %copy-start.1 = (bf16[8,1,256,256]{3,2,1,0:T(8,128)(2,1)S(1)}, bf16[8,1,256,256]{3,2,1,0:T(8,128)(2,1)}, u32[]{:S(2)}) copy-start(bf16[8,1,256,256]{3,2,1,0:T(8,128)(2,1)} %refs_0_.7) | copy-start | bytes 3145732
  8.8 1.2 %copy-start.2 = (bf16[8,1,256,256]{3,2,1,0:T(8,128)(2,1)S(1)}, bf16[8,1,256,256]{3,2,1,0:T(8,128)(2,1)}, u32[]{:S(2)}) copy-start(bf16[8,1,256,256]{3,2,1,0:T(8,128)(2,1)} %refs_6_) | copy-start | bytes 3145732
  10.0 0.7 copy-start.4
  27.1 31.1 %collective-permute-start.6 = (bf16[8,1,256,256]{3,2,1,0:T(8,128)(2,1)S(1)}, bf16[8,1,256,256]{3,2,1,0:T(8,128)(2,1)S(1)}, u32[]{:S(2)}, u32[]{:S(2)}) collective-permute-start(bf16[8,1,256,256]{3,2,1,0:T(8,128)(2,1)S(1)} %collective-permute-done.1.refs_4_.refs_6_), channel_id=1, source_target_pairs={{4,0},{5,1},{6,2},{7,3},{8,12},{9,13},{10,14},{11,15},{20,16},{21,... | collective-permute-start | bytes 3145736 | tf_op jit(solution)/shard_map/ppermute | solution.py:181
  28.4 29.9 %collective-permute-start.7 = (bf16[8,1,256,256]{3,2,1,0:T(8,128)(2,1)S(1)}, bf16[8,1,256,256]{3,2,1,0:T(8,128)(2,1)S(1)}, u32[]{:S(2)}, u32[]{:S(2)}) collective-permute-start(bf16[8,1,256,256]{3,2,1,0:T(8,128)(2,1)S(1)} %collective-permute-done.refs_4_.refs_6_), channel_id=1, source_target_pairs={{4,8},{5,9},{6,10},{7,11},{8,4},{9,5},{10,6},{11,7},{20,24},{21,25... | collective-permute-start | bytes 3145736 | tf_op jit(solution)/shard_map/ppermute | solution.py:181
  51.8 23.9 %collective-permute-start.5 = (bf16[8,1,256,256]{3,2,1,0:T(8,128)(2,1)S(1)}, bf16[8,1,256,256]{3,2,1,0:T(8,128)(2,1)S(1)}, u32[]{:S(2)}, u32[]{:S(2)}) collective-permute-start(bf16[8,1,256,256]{3,2,1,0:T(8,128)(2,1)S(1)} %copy-done.1), channel_id=1, source_target_pairs={{0,2},{1,3},{2,0},{3,1},{4,6},{5,7},{6,4},{7,5},{8,10},{9,11},{10,... | collective-permute-start | bytes 3145736 | tf_op jit(solution)/shard_map/ppermute | solution.py:181
  53.3 8.8 %collective-permute-start.8 = (bf16[2,256,256]{2,1,0:T(8,128)(2,1)S(1)}, bf16[2,256,256]{2,1,0:T(8,128)(2,1)S(1)}, u32[]{:S(2)}, u32[]{:S(2)}) collective-permute-start(bf16[2,256,256]{2,1,0:T(8,128)(2,1)S(1)} %shard_map.47), channel_id=1, source_target_pairs={{0,4},{1,5},{2,6},{3,7},{4,0},{5,1},{6,2},{7,3},{8,12},{9,13},{10,... | collective-permute-start | bytes 786440 | tf_op jit(solution)/shard_map/ppermute | solution.py:181
  57.3 4.7 %collective-permute-start.9 = (bf16[2,256,256]{2,1,0:T(8,128)(2,1)S(1)}, bf16[2,256,256]{2,1,0:T(8,128)(2,1)S(1)}, u32[]{:S(2)}, u32[]{:S(2)}) collective-permute-start(bf16[2,256,256]{2,1,0:T(8,128)(2,1)S(1)} %get-tuple-element.38), channel_id=1, source_target_pairs={{4,8},{5,9},{6,10},{7,11},{8,4},{9,5},{10,6},{11,7},{20,24},{21,25... | collective-permute-start | bytes 786440 | tf_op jit(solution)/shard_map/ppermute | solution.py:181
  58.2 19.5 %collective-permute-start.13 = (bf16[1,9,256,256]{3,2,1,0:T(8,128)(2,1)S(1)}, bf16[1,9,256,256]{3,2,1,0:T(8,128)(2,1)S(1)}, u32[]{:S(2)}, u32[]{:S(2)}) collective-permute-start(bf16[1,9,256,256]{3,2,1,0:T(8,128)(2,1)S(1)} %get-tuple-element.44), channel_id=1, source_target_pairs={{0,1},{1,0},{2,3},{3,2},{4,5},{5,4},{6,7},{7,6},{8,9},{9,8},{10,11... | collective-permute-start | bytes 3538952 | tf_op jit(solution)/shard_map/ppermute | solution.py:181
  58.3 33.2 %collective-permute-start.15 = (bf16[8,1,256,256]{3,2,1,0:T(8,128)(2,1)S(1)}, bf16[8,1,256,256]{3,2,1,0:T(8,128)(2,1)S(1)}, u32[]{:S(2)}, u32[]{:S(2)}) collective-permute-start(bf16[8,1,256,256]{3,2,1,0:T(8,128)(2,1)S(1)} %collective-permute-done.7.refs_5_.refs_7_), channel_id=1, source_target_pairs={{4,0},{5,1},{6,2},{7,3},{8,12},{9,13},{10,14},{11,15},{20,16},{21,... | collective-permute-start | bytes 3145736 | tf_op jit(solution)/shard_map/ppermute | solution.py:181
  62.1 15.0 %collective-permute-start.10 = (bf16[2,256,256]{2,1,0:T(8,128)(2,1)S(1)}, bf16[2,256,256]{2,1,0:T(8,128)(2,1)S(1)}, u32[]{:S(2)}, u32[]{:S(2)}) collective-permute-start(bf16[2,256,256]{2,1,0:T(8,128)(2,1)S(1)} %shard_map.49), channel_id=1, source_target_pairs={{0,8},{1,9},{2,10},{3,11},{4,12},{5,13},{6,14},{7,15},{8,0},{9,1},... | collective-permute-start | bytes 786440 | tf_op jit(solution)/shard_map/ppermute | solution.py:181
  65.8 11.9 %collective-permute-start.14 = (bf16[1,7,256,256]{3,2,1,0:T(8,128)(2,1)S(1)}, bf16[1,7,256,256]{3,2,1,0:T(8,128)(2,1)S(1)}, u32[]{:S(2)}, u32[]{:S(2)}) collective-permute-start(bf16[1,7,256,256]{3,2,1,0:T(8,128)(2,1)S(1)} %get-tuple-element.45), channel_id=1, source_target_pairs={{0,1},{1,0},{2,3},{3,2},{4,5},{5,4},{6,7},{7,6},{8,9},{9,8},{10,11... | collective-permute-start | bytes 2752520 | tf_op jit(solution)/shard_map/ppermute | solution.py:181
  77.1 2.7 %collective-permute-start.11 = (bf16[5,1,256,256]{3,2,1,0:T(8,128)(2,1)S(1)}, bf16[5,1,256,256]{3,2,1,0:T(8,128)(2,1)S(1)}, u32[]{:S(2)}, u32[]{:S(2)}) collective-permute-start(bf16[5,1,256,256]{3,2,1,0:T(8,128)(2,1)S(1)} %get-tuple-element.41), channel_id=1, source_target_pairs={{0,1},{1,0},{2,3},{3,2},{4,5},{5,4},{6,7},{7,6},{8,9},{9,8},{10,11... | collective-permute-start | bytes 1966088 | tf_op jit(solution)/shard_map/ppermute | solution.py:181
  77.2 2.6 %collective-permute-start.12 = (bf16[3,1,256,256]{3,2,1,0:T(8,128)(2,1)S(1)}, bf16[3,1,256,256]{3,2,1,0:T(8,128)(2,1)S(1)}, u32[]{:S(2)}, u32[]{:S(2)}) collective-permute-start(bf16[3,1,256,256]{3,2,1,0:T(8,128)(2,1)S(1)} %get-tuple-element.42), channel_id=1, source_target_pairs={{0,1},{1,0},{2,3},{3,2},{4,5},{5,4},{6,7},{7,6},{8,9},{9,8},{10,11... | collective-permute-start | bytes 1179656 | tf_op jit(solution)/shard_map/ppermute | solution.py:181
  81.7 34.6 %collective-permute-start.19 = (bf16[2,256,256]{2,1,0:T(8,128)(2,1)S(1)}, bf16[2,256,256]{2,1,0:T(8,128)(2,1)S(1)}, u32[]{:S(2)}, u32[]{:S(2)}) collective-permute-start(bf16[2,256,256]{2,1,0:T(8,128)(2,1)S(1)} %get-tuple-element.48), channel_id=1, source_target_pairs={{4,8},{5,9},{6,10},{7,11},{8,4},{9,5},{10,6},{11,7},{20,24},{21,25... | collective-permute-start | bytes 786440 | tf_op jit(solution)/shard_map/ppermute | solution.py:181
  84.3 32.0 %collective-permute-start.16 = (bf16[2,256,256]{2,1,0:T(8,128)(2,1)S(1)}, bf16[2,256,256]{2,1,0:T(8,128)(2,1)S(1)}, u32[]{:S(2)}, u32[]{:S(2)}) collective-permute-start(bf16[2,256,256]{2,1,0:T(8,128)(2,1)S(1)} %shard_map.54), channel_id=1, source_target_pairs={{0,8},{1,9},{2,10},{3,11},{4,12},{5,13},{6,14},{7,15},{8,0},{9,1},... | collective-permute-start | bytes 786440 | tf_op jit(solution)/shard_map/ppermute | solution.py:181
  91.4 24.9 %collective-permute-start.17 = (bf16[2,256,256]{2,1,0:T(8,128)(2,1)S(1)}, bf16[2,256,256]{2,1,0:T(8,128)(2,1)S(1)}, u32[]{:S(2)}, u32[]{:S(2)}) collective-permute-start(bf16[2,256,256]{2,1,0:T(8,128)(2,1)S(1)} %shard_map.53), channel_id=1, source_target_pairs={{0,4},{1,5},{2,6},{3,7},{4,0},{5,1},{6,2},{7,3},{8,12},{9,13},{10,... | collective-permute-start | bytes 786440 | tf_op jit(solution)/shard_map/ppermute | solution.py:181
  91.5 4.8 %copy-start.3 = (bf16[8,1,256,256]{3,2,1,0:T(8,128)(2,1)S(1)}, bf16[8,1,256,256]{3,2,1,0:T(8,128)(2,1)}, u32[]{:S(2)}) copy-start(bf16[8,1,256,256]{3,2,1,0:T(8,128)(2,1)} %refs_6_) | copy-start | bytes 3145732
  92.8 23.5 %collective-permute-start.18 = (bf16[4,256,256]{2,1,0:T(8,128)(2,1)S(1)}, bf16[4,256,256]{2,1,0:T(8,128)(2,1)S(1)}, u32[]{:S(2)}, u32[]{:S(2)}) collective-permute-start(bf16[4,256,256]{2,1,0:T(8,128)(2,1)S(1)} %shard_map.55), channel_id=1, source_target_pairs={{0,12},{1,13},{2,14},{3,15},{12,0},{13,1},{14,2},{15,3},{16,28},{1... | collective-permute-start | bytes 1572872 | tf_op jit(solution)/shard_map/ppermute | solution.py:181

commit v23 on v22

--- a/solution.py
+++ b/solution.py
@@ -217,15 +217,14 @@
     x_left, sent_2 = lax.optimization_barrier((x_left, sent_2))
     across_left = [exchange(part, 1, every) for part in split(x_left, 0, 5 * x_left.shape[0] // 8)]
     other = ([(x_left,), across_left], [(x_psi,), across_psi])
+    other_2 = products(2, *other, (far_out, far_in))
+    other_sent_2 = exchange(other_2, 8, every)
     other_middle, other_mid = products(3, *other, (middle,), keep_mid=True)
     sent_other_middle = exchange(other_middle, 12, inner)
-    far_out, other_middle = lax.optimization_barrier((far_out, other_middle))
-    other_2 = products(2, *other, (far_out, far_in))
-    other_sent_2 = exchange(other_2, 8, every)
     other_1 = products(1, *other, (near,))
     other_sent_1 = exchange(other_1, 4, every)
 
-    third, other_1, other_2, other_middle = lax.optimization_barrier((third, other_1, other_2, other_middle))
+    third, other_1, other_middle, other_2 = lax.optimization_barrier((third, other_1, other_middle, other_2))
     last_third = second((own_mid, other_mid), third, dtype, 10**10)
     sent_third = exchange(last_third, 12, outer)
     right_last, last_third = lax.optimization_barrier((right_env, last_third))

time: 118 us -> 115 us (0.975)
  starting transfers between devices: 29.1 us -> 25 us
  waiting for transfers between devices: 64.5 us -> 66.2 us
    ppermute x20, starting transfers between devices: 29.1 us -> 25 us  [exchange(): return lax.ppermute(array, 'sec', [(s, s ^ bits) for s in members])]
    ppermute x20, waiting for transfers between devices: 64.5 us -> 66.2 us  [exchange(): return lax.ppermute(array, 'sec', [(s, s ^ bits) for s in members])]
  transfers between devices with their start and end apart: 20 -> 20, of which waited for: 8 -> 9; matrix products, arithmetic and copies ran while one was open for 0% -> 0% of each run, Pallas kernels for 15% -> 15%
where the time goes in v23:
time: 115 us
  waiting for transfers between devices  66.2 us (58%)
  starting transfers between devices  25 us (22%)
  Pallas kernels  18.8 us (16%)
  local copies, waits for them, and re-layouts  4.73 us (4%)
    ppermute x20, waiting for transfers between devices, exchange(): return lax.ppermute(array, 'sec', [(s, s ^ bits) for s in members])  66.2 us
    ppermute x20, starting transfers between devices, exchange(): return lax.ppermute(array, 'sec', [(s, s ^ bits) for s in members])  25 us
    pallas_call x8, Pallas kernels, slot(): pl.pallas_call(functools.partial(slot_kernel, step, parts, len(rights)),...  15.1 us
    unnamed x10, local copies, waits for them, and re-layouts  4.73 us
  transfers between devices with their start and end apart: 20, of which 9 were waited for; matrix products, arithmetic and copies ran while one was open for 0% of the time, Pallas kernels for 15%

profile of v23, /device:TPU:0, one launch (start us, length us, event | category | flops | bytes accessed | tf_op | source)
XLA Modules:
  0.0 114.9 jit_solution(3826969295958786912)
XLA Ops:
  0.0 0.5 collective-permute-start.3
  0.5 0.1 collective-permute-start.2
  0.5 3.0 %collective-permute-start = (bf16[8,1,256,256]{3,2,1,0:T(8,128)(2,1)}, bf16[8,1,256,256]{3,2,1,0:T(8,128)(2,1)S(1)}, u32[]{:S(2)}, u32[]{:S(2)}) collective-permute-start(bf16[8,1,256,256]{3,2,1,0:T(8,128)(2,1)} %refs_6_), channel_id=1, source_target_pairs={{0,4},{1,5},{2,6},{3,7},{4,0},{5,1},{6,2},{7,3},{8,12},{9,13},{10,... | collective-permute-start | bytes 3145736 | tf_op jit(solution)/shard_map/ppermute | solution.py:181
  3.5 0.7 collective-permute-start.1
  4.3 1.6 %collective-permute-start.4 = (bf16[1,16,256,256]{3,2,1,0:T(8,128)(2,1)}, bf16[1,16,256,256]{3,2,1,0:T(8,128)(2,1)S(1)}, u32[]{:S(2)}, u32[]{:S(2)}) collective-permute-start(bf16[1,16,256,256]{3,2,1,0:T(8,128)(2,1)} %refs_2_.7), channel_id=1, source_target_pairs={{0,2},{1,3},{2,0},{3,1},{4,6},{5,7},{6,4},{7,5},{8,10},{9,11},{10,... | collective-permute-start | bytes 6291464 | tf_op jit(solution)/shard_map/ppermute | solution.py:181
  5.8 0.1 collective-permute-done.2.refs_1_
  6.0 1.6 %copy-done = bf16[1,16,256,256]{3,2,1,0:T(8,128)(2,1)S(1)} copy-done((bf16[1,16,256,256]{3,2,1,0:T(8,128)(2,1)S(1)}, bf16[1,16,256,256]{3,2,1,0:T(8,128)(2,1)}, u32[]{:S(2)}) %copy-start) | copy-done | bytes 2097176
  7.5 1.2 %copy-done.1 = bf16[8,1,256,256]{3,2,1,0:T(8,128)(2,1)S(1)} copy-done((bf16[8,1,256,256]{3,2,1,0:T(8,128)(2,1)S(1)}, bf16[8,1,256,256]{3,2,1,0:T(8,128)(2,1)}, u32[]{:S(2)}) %copy-start.1) | copy-done | bytes 1048600
  8.8 1.2 %copy-done.2 = bf16[8,1,256,256]{3,2,1,0:T(8,128)(2,1)S(1)} copy-done((bf16[8,1,256,256]{3,2,1,0:T(8,128)(2,1)S(1)}, bf16[8,1,256,256]{3,2,1,0:T(8,128)(2,1)}, u32[]{:S(2)}) %copy-start.2) | copy-done | bytes 1048600
  10.0 0.7 copy-done.4
  10.7 1.9 %shard_map.46.refs_0_ = bf16[2,256,256]{2,1,0:T(8,128)(2,1)S(1)} custom-call(s32[8,16]{1,0:T(8,128)S(1)} %copy-done.4, bf16[8,1,256,256]{3,2,1,0:T(8,128)(2,1)S(1)} %copy-done.1, bf16[8,1,256,256]{3,2,1,0:T(8,128)(2,1)S(1)} %collective-permute-done.2.refs_1_, bf16[1,16,256,256]{3,2,1,0:T(8,128)(2,1)S(1)} %copy-done, ...), custom_call_target="tpu_custom_call" | custom-call | flops 20000000000 | bytes 1 | tf_op jit(solution)/shard_map/pallas_call | solution.py:99
  12.6 14.5 %collective-permute-done.refs_4_.refs_6_ = bf16[8,1,256,256]{3,2,1,0:T(8,128)(2,1)S(1)} collective-permute-done((bf16[8,1,256,256]{3,2,1,0:T(8,128)(2,1)}, bf16[8,1,256,256]{3,2,1,0:T(8,128)(2,1)S(1)}, u32[]{:S(2)}, u32[]{:S(2)}) %collective-permute-start) | collective-permute-done | bytes 1048608 | tf_op jit(solution)/shard_map/ppermute | solution.py:181
  27.1 1.3 %collective-permute-start.6 = (bf16[8,1,256,256]{3,2,1,0:T(8,128)(2,1)S(1)}, bf16[8,1,256,256]{3,2,1,0:T(8,128)(2,1)S(1)}, u32[]{:S(2)}, u32[]{:S(2)}) collective-permute-start(bf16[8,1,256,256]{3,2,1,0:T(8,128)(2,1)S(1)} %collective-permute-done.1.refs_4_.refs_6_), channel_id=1, source_target_pairs={{4,0},{5,1},{6,2},{7,3},{8,12},{9,13},{10,14},{11,15},{20,16},{21,... | collective-permute-start | bytes 3145736 | tf_op jit(solution)/shard_map/ppermute | solution.py:181
  28.4 0.7 collective-permute-start.7
  29.1 1.9 %shard_map.48 = (bf16[2,256,256]{2,1,0:T(8,128)(2,1)S(1)}, bf16[512,2048]{1,0:T(8,128)(2,1)S(1)}) custom-call(s32[8,16]{1,0:T(8,128)S(1)} %copy-done.4, bf16[8,1,256,256]{3,2,1,0:T(8,128)(2,1)S(1)} %copy-done.1, bf16[8,1,256,256]{3,2,1,0:T(8,128)(2,1)S(1)} %collective-permute-done.2.refs_1_, bf16[1,16,256,256]{3,2,1,0:T(8,128)(2,1)S(1)} %copy-done, ...), custom_call_target="tpu_custom_call" | custom-call | flops 1 | bytes 1 | tf_op jit(solution)/shard_map/pallas_call | solution.py:99
  31.0 1.9 %shard_map.47 = bf16[2,256,256]{2,1,0:T(8,128)(2,1)S(1)} custom-call(s32[8,16]{1,0:T(8,128)S(1)} %copy-done.4, bf16[8,1,256,256]{3,2,1,0:T(8,128)(2,1)S(1)} %copy-done.1, bf16[8,1,256,256]{3,2,1,0:T(8,128)(2,1)S(1)} %collective-permute-done.2.refs_1_, bf16[1,16,256,256]{3,2,1,0:T(8,128)(2,1)S(1)} %copy-done, ...), custom_call_target="tpu_custom_call" | custom-call | flops 1 | bytes 1 | tf_op jit(solution)/shard_map/pallas_call | solution.py:99
  32.9 18.9 %collective-permute-done.4.whole.refs_3_ = bf16[1,16,256,256]{3,2,1,0:T(8,128)(2,1)S(1)} collective-permute-done((bf16[1,16,256,256]{3,2,1,0:T(8,128)(2,1)}, bf16[1,16,256,256]{3,2,1,0:T(8,128)(2,1)S(1)}, u32[]{:S(2)}, u32[]{:S(2)}) %collective-permute-start.4) | collective-permute-done | bytes 2097184 | tf_op jit(solution)/shard_map/ppermute | solution.py:181
  51.8 1.5 %collective-permute-start.5 = (bf16[8,1,256,256]{3,2,1,0:T(8,128)(2,1)S(1)}, bf16[8,1,256,256]{3,2,1,0:T(8,128)(2,1)S(1)}, u32[]{:S(2)}, u32[]{:S(2)}) collective-permute-start(bf16[8,1,256,256]{3,2,1,0:T(8,128)(2,1)S(1)} %copy-done.1), channel_id=1, source_target_pairs={{0,2},{1,3},{2,0},{3,1},{4,6},{5,7},{6,4},{7,5},{8,10},{9,11},{10,... | collective-permute-start | bytes 3145736 | tf_op jit(solution)/shard_map/ppermute | solution.py:181
  53.3 4.1 %collective-permute-start.8 = (bf16[2,256,256]{2,1,0:T(8,128)(2,1)S(1)}, bf16[2,256,256]{2,1,0:T(8,128)(2,1)S(1)}, u32[]{:S(2)}, u32[]{:S(2)}) collective-permute-start(bf16[2,256,256]{2,1,0:T(8,128)(2,1)S(1)} %shard_map.47), channel_id=1, source_target_pairs={{0,4},{1,5},{2,6},{3,7},{4,0},{5,1},{6,2},{7,3},{8,12},{9,13},{10,... | collective-permute-start | bytes 786440 | tf_op jit(solution)/shard_map/ppermute | solution.py:181
  57.3 0.7 collective-permute-start.9
  58.0 0.1 shard_map.51
  58.2 0.1 collective-permute-start.13
  58.2 0.0 collective-permute-done.7.refs_5_.refs_7_
  58.3 1.3 %collective-permute-start.15 = (bf16[8,1,256,256]{3,2,1,0:T(8,128)(2,1)S(1)}, bf16[8,1,256,256]{3,2,1,0:T(8,128)(2,1)S(1)}, u32[]{:S(2)}, u32[]{:S(2)}) collective-permute-start(bf16[8,1,256,256]{3,2,1,0:T(8,128)(2,1)S(1)} %collective-permute-done.7.refs_5_.refs_7_), channel_id=1, source_target_pairs={{4,0},{5,1},{6,2},{7,3},{8,12},{9,13},{10,14},{11,15},{20,16},{21,... | collective-permute-start | bytes 3145736 | tf_op jit(solution)/shard_map/ppermute | solution.py:181
  59.6 1.9 %shard_map.49 = bf16[2,256,256]{2,1,0:T(8,128)(2,1)S(1)} custom-call(s32[8,16]{1,0:T(8,128)S(1)} %copy-done.4, bf16[8,1,256,256]{3,2,1,0:T(8,128)(2,1)S(1)} %copy-done.1, bf16[8,1,256,256]{3,2,1,0:T(8,128)(2,1)S(1)} %collective-permute-done.2.refs_1_, bf16[1,16,256,256]{3,2,1,0:T(8,128)(2,1)S(1)} %copy-done, ...), custom_call_target="tpu_custom_call" | custom-call | flops 1 | bytes 1 | tf_op jit(solution)/shard_map/pallas_call | solution.py:99
  61.5 0.6 collective-permute-done.8.refs_2_
  62.1 3.7 %collective-permute-start.10 = (bf16[2,256,256]{2,1,0:T(8,128)(2,1)S(1)}, bf16[2,256,256]{2,1,0:T(8,128)(2,1)S(1)}, u32[]{:S(2)}, u32[]{:S(2)}) collective-permute-start(bf16[2,256,256]{2,1,0:T(8,128)(2,1)S(1)} %shard_map.49), channel_id=1, source_target_pairs={{0,8},{1,9},{2,10},{3,11},{4,12},{5,13},{6,14},{7,15},{8,0},{9,1},... | collective-permute-start | bytes 786440 | tf_op jit(solution)/shard_map/ppermute | solution.py:181
  65.8 9.9 %collective-permute-done.5.whole.refs_0_ = bf16[8,1,256,256]{3,2,1,0:T(8,128)(2,1)S(1)} collective-permute-done((bf16[8,1,256,256]{3,2,1,0:T(8,128)(2,1)S(1)}, bf16[8,1,256,256]{3,2,1,0:T(8,128)(2,1)S(1)}, u32[]{:S(2)}, u32[]{:S(2)}) %collective-permute-start.5) | collective-permute-done | bytes 1048608 | tf_op jit(solution)/shard_map/ppermute | solution.py:181
  75.7 1.3 %collective-permute-done.10.refs_3_ = bf16[2,256,256]{2,1,0:T(8,128)(2,1)S(1)} collective-permute-done((bf16[2,256,256]{2,1,0:T(8,128)(2,1)S(1)}, bf16[2,256,256]{2,1,0:T(8,128)(2,1)S(1)}, u32[]{:S(2)}, u32[]{:S(2)}) %collective-permute-start.10) | collective-permute-done | bytes 262176 | tf_op jit(solution)/shard_map/ppermute | solution.py:181
  77.0 0.1 shard_map.50
  77.1 0.1 collective-permute-start.11
  77.2 0.5 collective-permute-start.12
  77.7 0.0 collective-permute-done.14.refs_5_
  77.7 0.0 collective-permute-done.13.refs_4_
  77.7 2.1 %collective-permute-done.12.refs_2_ = bf16[3,1,256,256]{3,2,1,0:T(8,128)(2,1)S(1)} collective-permute-done((bf16[3,1,256,256]{3,2,1,0:T(8,128)(2,1)S(1)}, bf16[3,1,256,256]{3,2,1,0:T(8,128)(2,1)S(1)}, u32[]{:S(2)}, u32[]{:S(2)}) %collective-permute-start.12) | collective-permute-done | bytes 393248 | tf_op jit(solution)/shard_map/ppermute | solution.py:181
  79.8 1.9 %shard_map.54 = bf16[2,256,256]{2,1,0:T(8,128)(2,1)S(1)} custom-call(s32[8,16]{1,0:T(8,128)S(1)} %copy-done.4, bf16[8,1,256,256]{3,2,1,0:T(8,128)(2,1)S(1)} %collective-permute-done.5.whole.refs_0_, bf16[5,1,256,256]{3,2,1,0:T(8,128)(2,1)S(1)} %collective-permute-done.11.refs_1_, bf16[3,1,256,256]{3,2,1,0:T(8,128)(2,1)S(1)} %collective-permute-done.12.refs_2_, ...), custom_call_target="tpu_custom_call" | custom-call | flops 1 | bytes 1 | tf_op jit(solution)/shard_map/pallas_call | solution.py:99
  81.7 2.5 %collective-permute-start.16 = (bf16[2,256,256]{2,1,0:T(8,128)(2,1)S(1)}, bf16[2,256,256]{2,1,0:T(8,128)(2,1)S(1)}, u32[]{:S(2)}, u32[]{:S(2)}) collective-permute-start(bf16[2,256,256]{2,1,0:T(8,128)(2,1)S(1)} %shard_map.54), channel_id=1, source_target_pairs={{0,8},{1,9},{2,10},{3,11},{4,12},{5,13},{6,14},{7,15},{8,0},{9,1},... | collective-permute-start | bytes 786440 | tf_op jit(solution)/shard_map/ppermute | solution.py:181
  84.3 1.9 %shard_map.53 = bf16[2,256,256]{2,1,0:T(8,128)(2,1)S(1)} custom-call(s32[8,16]{1,0:T(8,128)S(1)} %copy-done.4, bf16[8,1,256,256]{3,2,1,0:T(8,128)(2,1)S(1)} %collective-permute-done.5.whole.refs_0_, bf16[5,1,256,256]{3,2,1,0:T(8,128)(2,1)S(1)} %collective-permute-done.11.refs_1_, bf16[3,1,256,256]{3,2,1,0:T(8,128)(2,1)S(1)} %collective-permute-done.12.refs_2_, ...), custom_call_target="tpu_custom_call" | custom-call | flops 1 | bytes 1 | tf_op jit(solution)/shard_map/pallas_call | solution.py:99
  86.2 0.2 collective-permute-start.17
  86.4 1.9 %shard_map.52 = (bf16[2,256,256]{2,1,0:T(8,128)(2,1)S(1)}, bf16[512,2048]{1,0:T(8,128)(2,1)S(1)}) custom-call(s32[8,16]{1,0:T(8,128)S(1)} %copy-done.4, bf16[8,1,256,256]{3,2,1,0:T(8,128)(2,1)S(1)} %collective-permute-done.5.whole.refs_0_, bf16[5,1,256,256]{3,2,1,0:T(8,128)(2,1)S(1)} %collective-permute-done.11.refs_1_, ...), custom_call_target="tpu_custom_call" | custom-call | flops 1 | bytes 1 | tf_op jit(solution)/shard_map/pallas_call | solution.py:99
  88.3 0.7 collective-permute-start.19
  88.9 8.2 %collective-permute-done.15.refs_2_ = bf16[8,1,256,256]{3,2,1,0:T(8,128)(2,1)S(1)} collective-permute-done((bf16[8,1,256,256]{3,2,1,0:T(8,128)(2,1)S(1)}, bf16[8,1,256,256]{3,2,1,0:T(8,128)(2,1)S(1)}, u32[]{:S(2)}, u32[]{:S(2)}) %collective-permute-start.15) | collective-permute-done | bytes 1048608 | tf_op jit(solution)/shard_map/ppermute | solution.py:181
  97.1 1.3 %shard_map.55 = bf16[4,256,256]{2,1,0:T(8,128)(2,1)S(1)} custom-call(bf16[512,2048]{1,0:T(8,128)(2,1)S(1)} %get-tuple-element.45.refs_0_, bf16[512,2048]{1,0:T(8,128)(2,1)S(1)} %get-tuple-element.46.refs_1_, bf16[8,1,256,256]{3,2,1,0:T(8,128)(2,1)S(1)} %collective-permute-done.15.refs_2_), custom_call_target="tpu_custom_call" | custom-call | flops 10000000000 | bytes 1 | tf_op jit(solution)/shard_map/pallas_call | solution.py:78
  98.4 1.9 %collective-permute-start.18 = (bf16[4,256,256]{2,1,0:T(8,128)(2,1)S(1)}, bf16[4,256,256]{2,1,0:T(8,128)(2,1)S(1)}, u32[]{:S(2)}, u32[]{:S(2)}) collective-permute-start(bf16[4,256,256]{2,1,0:T(8,128)(2,1)S(1)} %shard_map.55), channel_id=1, source_target_pairs={{0,12},{1,13},{2,14},{3,15},{12,0},{13,1},{14,2},{15,3},{16,28},{1... | collective-permute-start | bytes 1572872 | tf_op jit(solution)/shard_map/ppermute | solution.py:181
  100.3 1.9 %shard_map.56.refs_1_ = bf16[2,256,256]{2,1,0:T(8,128)(2,1)S(1)} custom-call(s32[8,16]{1,0:T(8,128)S(1)} %copy-done.4, bf16[8,1,256,256]{3,2,1,0:T(8,128)(2,1)S(1)} %collective-permute-done.5.whole.refs_0_, bf16[5,1,256,256]{3,2,1,0:T(8,128)(2,1)S(1)} %collective-permute-done.11.refs_1_, bf16[3,1,256,256]{3,2,1,0:T(8,128)(2,1)S(1)} %collective-permute-done.12.refs_2_, ...), custom_call_target="tpu_custom_call" | custom-call | flops 1 | bytes 1 | tf_op jit(solution)/shard_map/pallas_call | solution.py:99
  102.2 1.1 shard_map.57.refs_0_
  103.4 10.4 %collective-permute-done.17.refs_2_ = bf16[2,256,256]{2,1,0:T(8,128)(2,1)S(1)} collective-permute-done((bf16[2,256,256]{2,1,0:T(8,128)(2,1)S(1)}, bf16[2,256,256]{2,1,0:T(8,128)(2,1)S(1)}, u32[]{:S(2)}, u32[]{:S(2)}) %collective-permute-start.17) | collective-permute-done | bytes 262176 | tf_op jit(solution)/shard_map/ppermute | solution.py:181
  113.8 1.1 shard_map.58
  (15 shorter events, 0.0 us)
Async XLA Ops:
  0.0 6.0 %collective-permute-start.3 = (bf16[1,16,256,256]{3,2,1,0:T(8,128)(2,1)}, bf16[1,16,256,256]{3,2,1,0:T(8,128)(2,1)S(1)}, u32[]{:S(2)}, u32[]{:S(2)}) collective-permute-start(bf16[1,16,256,256]{3,2,1,0:T(8,128)(2,1)} %refs_2_.7), channel_id=1, source_target_pairs={{0,1},{1,0},{2,3},{3,2},{4,5},{5,4},{6,7},{7,6},{8,9},{9,8},{10,11... | collective-permute-start | bytes 6291464 | tf_op jit(solution)/shard_map/ppermute | solution.py:181
  0.5 5.5 %collective-permute-start.2 = (bf16[8,1,256,256]{3,2,1,0:T(8,128)(2,1)}, bf16[8,1,256,256]{3,2,1,0:T(8,128)(2,1)S(1)}, u32[]{:S(2)}, u32[]{:S(2)}) collective-permute-start(bf16[8,1,256,256]{3,2,1,0:T(8,128)(2,1)} %refs_0_.7), channel_id=1, source_target_pairs={{0,1},{1,0},{2,3},{3,2},{4,5},{5,4},{6,7},{7,6},{8,9},{9,8},{10,11... | collective-permute-start | bytes 3145736 | tf_op jit(solution)/shard_map/ppermute | solution.py:181
  0.5 26.6 %collective-permute-start = (bf16[8,1,256,256]{3,2,1,0:T(8,128)(2,1)}, bf16[8,1,256,256]{3,2,1,0:T(8,128)(2,1)S(1)}, u32[]{:S(2)}, u32[]{:S(2)}) collective-permute-start(bf16[8,1,256,256]{3,2,1,0:T(8,128)(2,1)} %refs_6_), channel_id=1, source_target_pairs={{0,4},{1,5},{2,6},{3,7},{4,0},{5,1},{6,2},{7,3},{8,12},{9,13},{10,... | collective-permute-start | bytes 3145736 | tf_op jit(solution)/shard_map/ppermute | solution.py:181
  3.5 23.5 %collective-permute-start.1 = (bf16[8,1,256,256]{3,2,1,0:T(8,128)(2,1)}, bf16[8,1,256,256]{3,2,1,0:T(8,128)(2,1)S(1)}, u32[]{:S(2)}, u32[]{:S(2)}) collective-permute-start(bf16[8,1,256,256]{3,2,1,0:T(8,128)(2,1)} %refs_6_), channel_id=1, source_target_pairs={{4,8},{5,9},{6,10},{7,11},{8,4},{9,5},{10,6},{11,7},{20,24},{21,25... | collective-permute-start | bytes 3145736 | tf_op jit(solution)/shard_map/ppermute | solution.py:181
  4.3 47.5 %collective-permute-start.4 = (bf16[1,16,256,256]{3,2,1,0:T(8,128)(2,1)}, bf16[1,16,256,256]{3,2,1,0:T(8,128)(2,1)S(1)}, u32[]{:S(2)}, u32[]{:S(2)}) collective-permute-start(bf16[1,16,256,256]{3,2,1,0:T(8,128)(2,1)} %refs_2_.7), channel_id=1, source_target_pairs={{0,2},{1,3},{2,0},{3,1},{4,6},{5,7},{6,4},{7,5},{8,10},{9,11},{10,... | collective-permute-start | bytes 6291464 | tf_op jit(solution)/shard_map/ppermute | solution.py:181
  6.0 1.6 %copy-start = (bf16[1,16,256,256]{3,2,1,0:T(8,128)(2,1)S(1)}, bf16[1,16,256,256]{3,2,1,0:T(8,128)(2,1)}, u32[]{:S(2)}) copy-start(bf16[1,16,256,256]{3,2,1,0:T(8,128)(2,1)} %refs_2_.7) | copy-start | bytes 6291460
  7.5 1.2 %copy-start.1 = (bf16[8,1,256,256]{3,2,1,0:T(8,128)(2,1)S(1)}, bf16[8,1,256,256]{3,2,1,0:T(8,128)(2,1)}, u32[]{:S(2)}) copy-start(bf16[8,1,256,256]{3,2,1,0:T(8,128)(2,1)} %refs_0_.7) | copy-start | bytes 3145732
  8.8 1.2 %copy-start.2 = (bf16[8,1,256,256]{3,2,1,0:T(8,128)(2,1)S(1)}, bf16[8,1,256,256]{3,2,1,0:T(8,128)(2,1)}, u32[]{:S(2)}) copy-start(bf16[8,1,256,256]{3,2,1,0:T(8,128)(2,1)} %refs_6_) | copy-start | bytes 3145732
  10.0 0.7 copy-start.4
  27.1 31.1 %collective-permute-start.6 = (bf16[8,1,256,256]{3,2,1,0:T(8,128)(2,1)S(1)}, bf16[8,1,256,256]{3,2,1,0:T(8,128)(2,1)S(1)}, u32[]{:S(2)}, u32[]{:S(2)}) collective-permute-start(bf16[8,1,256,256]{3,2,1,0:T(8,128)(2,1)S(1)} %collective-permute-done.1.refs_4_.refs_6_), channel_id=1, source_target_pairs={{4,0},{5,1},{6,2},{7,3},{8,12},{9,13},{10,14},{11,15},{20,16},{21,... | collective-permute-start | bytes 3145736 | tf_op jit(solution)/shard_map/ppermute | solution.py:181
  28.4 29.9 %collective-permute-start.7 = (bf16[8,1,256,256]{3,2,1,0:T(8,128)(2,1)S(1)}, bf16[8,1,256,256]{3,2,1,0:T(8,128)(2,1)S(1)}, u32[]{:S(2)}, u32[]{:S(2)}) collective-permute-start(bf16[8,1,256,256]{3,2,1,0:T(8,128)(2,1)S(1)} %collective-permute-done.refs_4_.refs_6_), channel_id=1, source_target_pairs={{4,8},{5,9},{6,10},{7,11},{8,4},{9,5},{10,6},{11,7},{20,24},{21,25... | collective-permute-start | bytes 3145736 | tf_op jit(solution)/shard_map/ppermute | solution.py:181
  51.8 23.9 %collective-permute-start.5 = (bf16[8,1,256,256]{3,2,1,0:T(8,128)(2,1)S(1)}, bf16[8,1,256,256]{3,2,1,0:T(8,128)(2,1)S(1)}, u32[]{:S(2)}, u32[]{:S(2)}) collective-permute-start(bf16[8,1,256,256]{3,2,1,0:T(8,128)(2,1)S(1)} %copy-done.1), channel_id=1, source_target_pairs={{0,2},{1,3},{2,0},{3,1},{4,6},{5,7},{6,4},{7,5},{8,10},{9,11},{10,... | collective-permute-start | bytes 3145736 | tf_op jit(solution)/shard_map/ppermute | solution.py:181
  53.3 8.8 %collective-permute-start.8 = (bf16[2,256,256]{2,1,0:T(8,128)(2,1)S(1)}, bf16[2,256,256]{2,1,0:T(8,128)(2,1)S(1)}, u32[]{:S(2)}, u32[]{:S(2)}) collective-permute-start(bf16[2,256,256]{2,1,0:T(8,128)(2,1)S(1)} %shard_map.47), channel_id=1, source_target_pairs={{0,4},{1,5},{2,6},{3,7},{4,0},{5,1},{6,2},{7,3},{8,12},{9,13},{10,... | collective-permute-start | bytes 786440 | tf_op jit(solution)/shard_map/ppermute | solution.py:181
  57.3 4.7 %collective-permute-start.9 = (bf16[2,256,256]{2,1,0:T(8,128)(2,1)S(1)}, bf16[2,256,256]{2,1,0:T(8,128)(2,1)S(1)}, u32[]{:S(2)}, u32[]{:S(2)}) collective-permute-start(bf16[2,256,256]{2,1,0:T(8,128)(2,1)S(1)} %get-tuple-element.37), channel_id=1, source_target_pairs={{4,8},{5,9},{6,10},{7,11},{8,4},{9,5},{10,6},{11,7},{20,24},{21,25... | collective-permute-start | bytes 786440 | tf_op jit(solution)/shard_map/ppermute | solution.py:181
  58.2 19.5 %collective-permute-start.13 = (bf16[1,9,256,256]{3,2,1,0:T(8,128)(2,1)S(1)}, bf16[1,9,256,256]{3,2,1,0:T(8,128)(2,1)S(1)}, u32[]{:S(2)}, u32[]{:S(2)}) collective-permute-start(bf16[1,9,256,256]{3,2,1,0:T(8,128)(2,1)S(1)} %get-tuple-element.43), channel_id=1, source_target_pairs={{0,1},{1,0},{2,3},{3,2},{4,5},{5,4},{6,7},{7,6},{8,9},{9,8},{10,11... | collective-permute-start | bytes 3538952 | tf_op jit(solution)/shard_map/ppermute | solution.py:181
  58.3 38.9 %collective-permute-start.15 = (bf16[8,1,256,256]{3,2,1,0:T(8,128)(2,1)S(1)}, bf16[8,1,256,256]{3,2,1,0:T(8,128)(2,1)S(1)}, u32[]{:S(2)}, u32[]{:S(2)}) collective-permute-start(bf16[8,1,256,256]{3,2,1,0:T(8,128)(2,1)S(1)} %collective-permute-done.7.refs_5_.refs_7_), channel_id=1, source_target_pairs={{4,0},{5,1},{6,2},{7,3},{8,12},{9,13},{10,14},{11,15},{20,16},{21,... | collective-permute-start | bytes 3145736 | tf_op jit(solution)/shard_map/ppermute | solution.py:181
  62.1 15.0 %collective-permute-start.10 = (bf16[2,256,256]{2,1,0:T(8,128)(2,1)S(1)}, bf16[2,256,256]{2,1,0:T(8,128)(2,1)S(1)}, u32[]{:S(2)}, u32[]{:S(2)}) collective-permute-start(bf16[2,256,256]{2,1,0:T(8,128)(2,1)S(1)} %shard_map.49), channel_id=1, source_target_pairs={{0,8},{1,9},{2,10},{3,11},{4,12},{5,13},{6,14},{7,15},{8,0},{9,1},... | collective-permute-start | bytes 786440 | tf_op jit(solution)/shard_map/ppermute | solution.py:181
  65.8 11.9 %collective-permute-start.14 = (bf16[1,7,256,256]{3,2,1,0:T(8,128)(2,1)S(1)}, bf16[1,7,256,256]{3,2,1,0:T(8,128)(2,1)S(1)}, u32[]{:S(2)}, u32[]{:S(2)}) collective-permute-start(bf16[1,7,256,256]{3,2,1,0:T(8,128)(2,1)S(1)} %get-tuple-element.44), channel_id=1, source_target_pairs={{0,1},{1,0},{2,3},{3,2},{4,5},{5,4},{6,7},{7,6},{8,9},{9,8},{10,11... | collective-permute-start | bytes 2752520 | tf_op jit(solution)/shard_map/ppermute | solution.py:181
  77.1 2.7 %collective-permute-start.11 = (bf16[5,1,256,256]{3,2,1,0:T(8,128)(2,1)S(1)}, bf16[5,1,256,256]{3,2,1,0:T(8,128)(2,1)S(1)}, u32[]{:S(2)}, u32[]{:S(2)}) collective-permute-start(bf16[5,1,256,256]{3,2,1,0:T(8,128)(2,1)S(1)} %get-tuple-element.40), channel_id=1, source_target_pairs={{0,1},{1,0},{2,3},{3,2},{4,5},{5,4},{6,7},{7,6},{8,9},{9,8},{10,11... | collective-permute-start | bytes 1966088 | tf_op jit(solution)/shard_map/ppermute | solution.py:181
  77.2 2.6 %collective-permute-start.12 = (bf16[3,1,256,256]{3,2,1,0:T(8,128)(2,1)S(1)}, bf16[3,1,256,256]{3,2,1,0:T(8,128)(2,1)S(1)}, u32[]{:S(2)}, u32[]{:S(2)}) collective-permute-start(bf16[3,1,256,256]{3,2,1,0:T(8,128)(2,1)S(1)} %get-tuple-element.41), channel_id=1, source_target_pairs={{0,1},{1,0},{2,3},{3,2},{4,5},{5,4},{6,7},{7,6},{8,9},{9,8},{10,11... | collective-permute-start | bytes 1179656 | tf_op jit(solution)/shard_map/ppermute | solution.py:181
  81.7 21.6 %collective-permute-start.16 = (bf16[2,256,256]{2,1,0:T(8,128)(2,1)S(1)}, bf16[2,256,256]{2,1,0:T(8,128)(2,1)S(1)}, u32[]{:S(2)}, u32[]{:S(2)}) collective-permute-start(bf16[2,256,256]{2,1,0:T(8,128)(2,1)S(1)} %shard_map.54), channel_id=1, source_target_pairs={{0,8},{1,9},{2,10},{3,11},{4,12},{5,13},{6,14},{7,15},{8,0},{9,1},... | collective-permute-start | bytes 786440 | tf_op jit(solution)/shard_map/ppermute | solution.py:181
  86.2 27.6 %collective-permute-start.17 = (bf16[2,256,256]{2,1,0:T(8,128)(2,1)S(1)}, bf16[2,256,256]{2,1,0:T(8,128)(2,1)S(1)}, u32[]{:S(2)}, u32[]{:S(2)}) collective-permute-start(bf16[2,256,256]{2,1,0:T(8,128)(2,1)S(1)} %shard_map.53), channel_id=1, source_target_pairs={{0,4},{1,5},{2,6},{3,7},{4,0},{5,1},{6,2},{7,3},{8,12},{9,13},{10,... | collective-permute-start | bytes 786440 | tf_op jit(solution)/shard_map/ppermute | solution.py:181
  88.3 25.5 %collective-permute-start.19 = (bf16[2,256,256]{2,1,0:T(8,128)(2,1)S(1)}, bf16[2,256,256]{2,1,0:T(8,128)(2,1)S(1)}, u32[]{:S(2)}, u32[]{:S(2)}) collective-permute-start(bf16[2,256,256]{2,1,0:T(8,128)(2,1)S(1)} %get-tuple-element.47), channel_id=1, source_target_pairs={{4,8},{5,9},{6,10},{7,11},{8,4},{9,5},{10,6},{11,7},{20,24},{21,25... | collective-permute-start | bytes 786440 | tf_op jit(solution)/shard_map/ppermute | solution.py:181
  97.1 3.2 %copy-start.3 = (bf16[8,1,256,256]{3,2,1,0:T(8,128)(2,1)S(1)}, bf16[8,1,256,256]{3,2,1,0:T(8,128)(2,1)}, u32[]{:S(2)}) copy-start(bf16[8,1,256,256]{3,2,1,0:T(8,128)(2,1)} %refs_6_) | copy-start | bytes 3145732
  98.4 15.4 %collective-permute-start.18 = (bf16[4,256,256]{2,1,0:T(8,128)(2,1)S(1)}, bf16[4,256,256]{2,1,0:T(8,128)(2,1)S(1)}, u32[]{:S(2)}, u32[]{:S(2)}) collective-permute-start(bf16[4,256,256]{2,1,0:T(8,128)(2,1)S(1)} %shard_map.55), channel_id=1, source_target_pairs={{0,12},{1,13},{2,14},{3,15},{12,0},{13,1},{14,2},{15,3},{16,28},{1... | collective-permute-start | bytes 1572872 | tf_op jit(solution)/shard_map/ppermute | solution.py:181

commit v24 on v23

--- a/solution.py
+++ b/solution.py
@@ -224,7 +224,7 @@
     other_1 = products(1, *other, (near,))
     other_sent_1 = exchange(other_1, 4, every)
 
-    third, other_1, other_middle, other_2 = lax.optimization_barrier((third, other_1, other_middle, other_2))
+    third, other_2, other_middle, other_1 = lax.optimization_barrier((third, other_2, other_middle, other_1))
     last_third = second((own_mid, other_mid), third, dtype, 10**10)
     sent_third = exchange(last_third, 12, outer)
     right_last, last_third = lax.optimization_barrier((right_env, last_third))

time: 115 us -> 117 us (1.017); the launches traced: 115 us -> 115 us
  waiting for transfers between devices: 66.2 us -> 63.8 us
  starting transfers between devices: 25 us -> 27.4 us
    ppermute x20, starting transfers between devices: 25 us -> 27.4 us  [exchange(): return lax.ppermute(array, 'sec', [(s, s ^ bits) for s in members])]
    ppermute x20, waiting for transfers between devices: 66.2 us -> 63.8 us  [exchange(): return lax.ppermute(array, 'sec', [(s, s ^ bits) for s in members])]
where the time goes in v24:
time: 117 us; the launch traced here: 115 us
  waiting for transfers between devices  63.8 us (55%)
  starting transfers between devices  27.4 us (23%)
  Pallas kernels  18.8 us (16%)
  local copies, waits for them, and re-layouts  4.73 us (4%)
    ppermute x20, waiting for transfers between devices, exchange(): return lax.ppermute(array, 'sec', [(s, s ^ bits) for s in members])  63.8 us
    ppermute x20, starting transfers between devices, exchange(): return lax.ppermute(array, 'sec', [(s, s ^ bits) for s in members])  27.4 us
    pallas_call x8, Pallas kernels, slot(): pl.pallas_call(functools.partial(slot_kernel, step, parts, len(rights)),...  15.1 us
    unnamed x10, local copies, waits for them, and re-layouts  4.73 us
  transfers between devices with their start and end apart: 20, of which 9 were waited for; matrix products, arithmetic and copies ran while one was open for 0% of the time, Pallas kernels for 15%

profile of v24, /device:TPU:0, one launch (start us, length us, event | category | flops | bytes accessed | tf_op | source)
XLA Modules:
  0.0 114.9 jit_solution(472101157605013031)
XLA Ops:
  0.0 0.5 collective-permute-start.3
  0.5 0.1 collective-permute-start.2
  0.5 3.0 %collective-permute-start = (bf16[8,1,256,256]{3,2,1,0:T(8,128)(2,1)}, bf16[8,1,256,256]{3,2,1,0:T(8,128)(2,1)S(1)}, u32[]{:S(2)}, u32[]{:S(2)}) collective-permute-start(bf16[8,1,256,256]{3,2,1,0:T(8,128)(2,1)} %refs_6_), channel_id=1, source_target_pairs={{0,4},{1,5},{2,6},{3,7},{4,0},{5,1},{6,2},{7,3},{8,12},{9,13},{10,... | collective-permute-start | bytes 3145736 | tf_op jit(solution)/shard_map/ppermute | solution.py:181
  3.5 0.7 collective-permute-start.1
  4.3 1.6 %collective-permute-start.4 = (bf16[1,16,256,256]{3,2,1,0:T(8,128)(2,1)}, bf16[1,16,256,256]{3,2,1,0:T(8,128)(2,1)S(1)}, u32[]{:S(2)}, u32[]{:S(2)}) collective-permute-start(bf16[1,16,256,256]{3,2,1,0:T(8,128)(2,1)} %refs_2_.7), channel_id=1, source_target_pairs={{0,2},{1,3},{2,0},{3,1},{4,6},{5,7},{6,4},{7,5},{8,10},{9,11},{10,... | collective-permute-start | bytes 6291464 | tf_op jit(solution)/shard_map/ppermute | solution.py:181
  5.8 0.1 collective-permute-done.2.refs_1_
  6.0 0.0 collective-permute-done.3.refs_3_
  6.0 1.6 %copy-done = bf16[1,16,256,256]{3,2,1,0:T(8,128)(2,1)S(1)} copy-done((bf16[1,16,256,256]{3,2,1,0:T(8,128)(2,1)S(1)}, bf16[1,16,256,256]{3,2,1,0:T(8,128)(2,1)}, u32[]{:S(2)}) %copy-start) | copy-done | bytes 2097176
  7.5 1.2 %copy-done.1 = bf16[8,1,256,256]{3,2,1,0:T(8,128)(2,1)S(1)} copy-done((bf16[8,1,256,256]{3,2,1,0:T(8,128)(2,1)S(1)}, bf16[8,1,256,256]{3,2,1,0:T(8,128)(2,1)}, u32[]{:S(2)}) %copy-start.1) | copy-done | bytes 1048600
  8.8 1.2 %copy-done.2 = bf16[8,1,256,256]{3,2,1,0:T(8,128)(2,1)S(1)} copy-done((bf16[8,1,256,256]{3,2,1,0:T(8,128)(2,1)S(1)}, bf16[8,1,256,256]{3,2,1,0:T(8,128)(2,1)}, u32[]{:S(2)}) %copy-start.2) | copy-done | bytes 1048600
  10.0 0.7 copy-done.4
  10.7 1.9 %shard_map.46.refs_0_ = bf16[2,256,256]{2,1,0:T(8,128)(2,1)S(1)} custom-call(s32[8,16]{1,0:T(8,128)S(1)} %copy-done.4, bf16[8,1,256,256]{3,2,1,0:T(8,128)(2,1)S(1)} %copy-done.1, bf16[8,1,256,256]{3,2,1,0:T(8,128)(2,1)S(1)} %collective-permute-done.2.refs_1_, bf16[1,16,256,256]{3,2,1,0:T(8,128)(2,1)S(1)} %copy-done, ...), custom_call_target="tpu_custom_call" | custom-call | flops 20000000000 | bytes 1 | tf_op jit(solution)/shard_map/pallas_call | solution.py:99
  12.6 14.5 %collective-permute-done.refs_4_.refs_6_ = bf16[8,1,256,256]{3,2,1,0:T(8,128)(2,1)S(1)} collective-permute-done((bf16[8,1,256,256]{3,2,1,0:T(8,128)(2,1)}, bf16[8,1,256,256]{3,2,1,0:T(8,128)(2,1)S(1)}, u32[]{:S(2)}, u32[]{:S(2)}) %collective-permute-start) | collective-permute-done | bytes 1048608 | tf_op jit(solution)/shard_map/ppermute | solution.py:181
  27.1 1.3 %collective-permute-start.6 = (bf16[8,1,256,256]{3,2,1,0:T(8,128)(2,1)S(1)}, bf16[8,1,256,256]{3,2,1,0:T(8,128)(2,1)S(1)}, u32[]{:S(2)}, u32[]{:S(2)}) collective-permute-start(bf16[8,1,256,256]{3,2,1,0:T(8,128)(2,1)S(1)} %collective-permute-done.1.refs_4_.refs_6_), channel_id=1, source_target_pairs={{4,0},{5,1},{6,2},{7,3},{8,12},{9,13},{10,14},{11,15},{20,16},{21,... | collective-permute-start | bytes 3145736 | tf_op jit(solution)/shard_map/ppermute | solution.py:181
  28.4 0.7 collective-permute-start.7
  29.1 1.9 %shard_map.48 = (bf16[2,256,256]{2,1,0:T(8,128)(2,1)S(1)}, bf16[512,2048]{1,0:T(8,128)(2,1)S(1)}) custom-call(s32[8,16]{1,0:T(8,128)S(1)} %copy-done.4, bf16[8,1,256,256]{3,2,1,0:T(8,128)(2,1)S(1)} %copy-done.1, bf16[8,1,256,256]{3,2,1,0:T(8,128)(2,1)S(1)} %collective-permute-done.2.refs_1_, bf16[1,16,256,256]{3,2,1,0:T(8,128)(2,1)S(1)} %copy-done, ...), custom_call_target="tpu_custom_call" | custom-call | flops 1 | bytes 1 | tf_op jit(solution)/shard_map/pallas_call | solution.py:99
  31.0 1.9 %shard_map.47 = bf16[2,256,256]{2,1,0:T(8,128)(2,1)S(1)} custom-call(s32[8,16]{1,0:T(8,128)S(1)} %copy-done.4, bf16[8,1,256,256]{3,2,1,0:T(8,128)(2,1)S(1)} %copy-done.1, bf16[8,1,256,256]{3,2,1,0:T(8,128)(2,1)S(1)} %collective-permute-done.2.refs_1_, bf16[1,16,256,256]{3,2,1,0:T(8,128)(2,1)S(1)} %copy-done, ...), custom_call_target="tpu_custom_call" | custom-call | flops 1 | bytes 1 | tf_op jit(solution)/shard_map/pallas_call | solution.py:99
  32.9 18.9 %collective-permute-done.4.whole.refs_3_ = bf16[1,16,256,256]{3,2,1,0:T(8,128)(2,1)S(1)} collective-permute-done((bf16[1,16,256,256]{3,2,1,0:T(8,128)(2,1)}, bf16[1,16,256,256]{3,2,1,0:T(8,128)(2,1)S(1)}, u32[]{:S(2)}, u32[]{:S(2)}) %collective-permute-start.4) | collective-permute-done | bytes 2097184 | tf_op jit(solution)/shard_map/ppermute | solution.py:181
  51.8 1.5 %collective-permute-start.5 = (bf16[8,1,256,256]{3,2,1,0:T(8,128)(2,1)S(1)}, bf16[8,1,256,256]{3,2,1,0:T(8,128)(2,1)S(1)}, u32[]{:S(2)}, u32[]{:S(2)}) collective-permute-start(bf16[8,1,256,256]{3,2,1,0:T(8,128)(2,1)S(1)} %copy-done.1), channel_id=1, source_target_pairs={{0,2},{1,3},{2,0},{3,1},{4,6},{5,7},{6,4},{7,5},{8,10},{9,11},{10,... | collective-permute-start | bytes 3145736 | tf_op jit(solution)/shard_map/ppermute | solution.py:181
  53.3 4.1 %collective-permute-start.8 = (bf16[2,256,256]{2,1,0:T(8,128)(2,1)S(1)}, bf16[2,256,256]{2,1,0:T(8,128)(2,1)S(1)}, u32[]{:S(2)}, u32[]{:S(2)}) collective-permute-start(bf16[2,256,256]{2,1,0:T(8,128)(2,1)S(1)} %shard_map.47), channel_id=1, source_target_pairs={{0,4},{1,5},{2,6},{3,7},{4,0},{5,1},{6,2},{7,3},{8,12},{9,13},{10,... | collective-permute-start | bytes 786440 | tf_op jit(solution)/shard_map/ppermute | solution.py:181
  57.3 0.7 collective-permute-start.9
  58.0 0.1 shard_map.51
  58.2 0.0 collective-permute-done.6.refs_4_.refs_6_
  58.2 0.1 collective-permute-start.13
  58.3 1.3 %collective-permute-start.15 = (bf16[8,1,256,256]{3,2,1,0:T(8,128)(2,1)S(1)}, bf16[8,1,256,256]{3,2,1,0:T(8,128)(2,1)S(1)}, u32[]{:S(2)}, u32[]{:S(2)}) collective-permute-start(bf16[8,1,256,256]{3,2,1,0:T(8,128)(2,1)S(1)} %collective-permute-done.7.refs_5_.refs_7_), channel_id=1, source_target_pairs={{4,0},{5,1},{6,2},{7,3},{8,12},{9,13},{10,14},{11,15},{20,16},{21,... | collective-permute-start | bytes 3145736 | tf_op jit(solution)/shard_map/ppermute | solution.py:181
  59.6 1.9 %shard_map.49 = bf16[2,256,256]{2,1,0:T(8,128)(2,1)S(1)} custom-call(s32[8,16]{1,0:T(8,128)S(1)} %copy-done.4, bf16[8,1,256,256]{3,2,1,0:T(8,128)(2,1)S(1)} %copy-done.1, bf16[8,1,256,256]{3,2,1,0:T(8,128)(2,1)S(1)} %collective-permute-done.2.refs_1_, bf16[1,16,256,256]{3,2,1,0:T(8,128)(2,1)S(1)} %copy-done, ...), custom_call_target="tpu_custom_call" | custom-call | flops 1 | bytes 1 | tf_op jit(solution)/shard_map/pallas_call | solution.py:99
  61.5 0.6 collective-permute-done.8.refs_2_
  62.0 0.0 collective-permute-done.9.refs_4_
  62.1 3.7 %collective-permute-start.10 = (bf16[2,256,256]{2,1,0:T(8,128)(2,1)S(1)}, bf16[2,256,256]{2,1,0:T(8,128)(2,1)S(1)}, u32[]{:S(2)}, u32[]{:S(2)}) collective-permute-start(bf16[2,256,256]{2,1,0:T(8,128)(2,1)S(1)} %shard_map.49), channel_id=1, source_target_pairs={{0,8},{1,9},{2,10},{3,11},{4,12},{5,13},{6,14},{7,15},{8,0},{9,1},... | collective-permute-start | bytes 786440 | tf_op jit(solution)/shard_map/ppermute | solution.py:181
  65.8 9.9 %collective-permute-done.5.whole.refs_0_ = bf16[8,1,256,256]{3,2,1,0:T(8,128)(2,1)S(1)} collective-permute-done((bf16[8,1,256,256]{3,2,1,0:T(8,128)(2,1)S(1)}, bf16[8,1,256,256]{3,2,1,0:T(8,128)(2,1)S(1)}, u32[]{:S(2)}, u32[]{:S(2)}) %collective-permute-start.5) | collective-permute-done | bytes 1048608 | tf_op jit(solution)/shard_map/ppermute | solution.py:181
  75.7 1.3 %collective-permute-done.10.refs_3_ = bf16[2,256,256]{2,1,0:T(8,128)(2,1)S(1)} collective-permute-done((bf16[2,256,256]{2,1,0:T(8,128)(2,1)S(1)}, bf16[2,256,256]{2,1,0:T(8,128)(2,1)S(1)}, u32[]{:S(2)}, u32[]{:S(2)}) %collective-permute-start.10) | collective-permute-done | bytes 262176 | tf_op jit(solution)/shard_map/ppermute | solution.py:181
  77.0 0.1 shard_map.50
  77.1 0.1 collective-permute-start.11
  77.2 0.5 collective-permute-start.12
  77.7 2.1 %collective-permute-done.12.refs_2_ = bf16[3,1,256,256]{3,2,1,0:T(8,128)(2,1)S(1)} collective-permute-done((bf16[3,1,256,256]{3,2,1,0:T(8,128)(2,1)S(1)}, bf16[3,1,256,256]{3,2,1,0:T(8,128)(2,1)S(1)}, u32[]{:S(2)}, u32[]{:S(2)}) %collective-permute-start.12) | collective-permute-done | bytes 393248 | tf_op jit(solution)/shard_map/ppermute | solution.py:181
  79.8 1.9 %shard_map.54 = bf16[2,256,256]{2,1,0:T(8,128)(2,1)S(1)} custom-call(s32[8,16]{1,0:T(8,128)S(1)} %copy-done.4, bf16[8,1,256,256]{3,2,1,0:T(8,128)(2,1)S(1)} %collective-permute-done.5.whole.refs_0_, bf16[5,1,256,256]{3,2,1,0:T(8,128)(2,1)S(1)} %collective-permute-done.11.refs_1_, bf16[3,1,256,256]{3,2,1,0:T(8,128)(2,1)S(1)} %collective-permute-done.12.refs_2_, ...), custom_call_target="tpu_custom_call" | custom-call | flops 1 | bytes 1 | tf_op jit(solution)/shard_map/pallas_call | solution.py:99
  81.7 2.5 %collective-permute-start.17 = (bf16[2,256,256]{2,1,0:T(8,128)(2,1)S(1)}, bf16[2,256,256]{2,1,0:T(8,128)(2,1)S(1)}, u32[]{:S(2)}, u32[]{:S(2)}) collective-permute-start(bf16[2,256,256]{2,1,0:T(8,128)(2,1)S(1)} %shard_map.54), channel_id=1, source_target_pairs={{0,4},{1,5},{2,6},{3,7},{4,0},{5,1},{6,2},{7,3},{8,12},{9,13},{10,... | collective-permute-start | bytes 786440 | tf_op jit(solution)/shard_map/ppermute | solution.py:181
  84.2 1.9 %shard_map.53 = bf16[2,256,256]{2,1,0:T(8,128)(2,1)S(1)} custom-call(s32[8,16]{1,0:T(8,128)S(1)} %copy-done.4, bf16[8,1,256,256]{3,2,1,0:T(8,128)(2,1)S(1)} %collective-permute-done.5.whole.refs_0_, bf16[5,1,256,256]{3,2,1,0:T(8,128)(2,1)S(1)} %collective-permute-done.11.refs_1_, bf16[3,1,256,256]{3,2,1,0:T(8,128)(2,1)S(1)} %collective-permute-done.12.refs_2_, ...), custom_call_target="tpu_custom_call" | custom-call | flops 1 | bytes 1 | tf_op jit(solution)/shard_map/pallas_call | solution.py:99
  86.1 0.3 collective-permute-start.16
  86.4 1.9 %shard_map.52 = (bf16[2,256,256]{2,1,0:T(8,128)(2,1)S(1)}, bf16[512,2048]{1,0:T(8,128)(2,1)S(1)}) custom-call(s32[8,16]{1,0:T(8,128)S(1)} %copy-done.4, bf16[8,1,256,256]{3,2,1,0:T(8,128)(2,1)S(1)} %collective-permute-done.5.whole.refs_0_, bf16[5,1,256,256]{3,2,1,0:T(8,128)(2,1)S(1)} %collective-permute-done.11.refs_1_, ...), custom_call_target="tpu_custom_call" | custom-call | flops 1 | bytes 1 | tf_op jit(solution)/shard_map/pallas_call | solution.py:99
  88.3 0.7 collective-permute-start.19
  88.9 5.3 %collective-permute-done.15.refs_2_ = bf16[8,1,256,256]{3,2,1,0:T(8,128)(2,1)S(1)} collective-permute-done((bf16[8,1,256,256]{3,2,1,0:T(8,128)(2,1)S(1)}, bf16[8,1,256,256]{3,2,1,0:T(8,128)(2,1)S(1)}, u32[]{:S(2)}, u32[]{:S(2)}) %collective-permute-start.15) | collective-permute-done | bytes 1048608 | tf_op jit(solution)/shard_map/ppermute | solution.py:181
  94.3 1.3 %shard_map.55 = bf16[4,256,256]{2,1,0:T(8,128)(2,1)S(1)} custom-call(bf16[512,2048]{1,0:T(8,128)(2,1)S(1)} %get-tuple-element.45.refs_0_, bf16[512,2048]{1,0:T(8,128)(2,1)S(1)} %get-tuple-element.46.refs_1_, bf16[8,1,256,256]{3,2,1,0:T(8,128)(2,1)S(1)} %collective-permute-done.15.refs_2_), custom_call_target="tpu_custom_call" | custom-call | flops 10000000000 | bytes 1 | tf_op jit(solution)/shard_map/pallas_call | solution.py:78
  95.6 4.3 %collective-permute-start.18 = (bf16[4,256,256]{2,1,0:T(8,128)(2,1)S(1)}, bf16[4,256,256]{2,1,0:T(8,128)(2,1)S(1)}, u32[]{:S(2)}, u32[]{:S(2)}) collective-permute-start(bf16[4,256,256]{2,1,0:T(8,128)(2,1)S(1)} %shard_map.55), channel_id=1, source_target_pairs={{0,12},{1,13},{2,14},{3,15},{12,0},{13,1},{14,2},{15,3},{16,28},{1... | collective-permute-start | bytes 1572872 | tf_op jit(solution)/shard_map/ppermute | solution.py:181
  99.9 1.9 %shard_map.56.refs_1_ = bf16[2,256,256]{2,1,0:T(8,128)(2,1)S(1)} custom-call(s32[8,16]{1,0:T(8,128)S(1)} %copy-done.4, bf16[8,1,256,256]{3,2,1,0:T(8,128)(2,1)S(1)} %collective-permute-done.5.whole.refs_0_, bf16[5,1,256,256]{3,2,1,0:T(8,128)(2,1)S(1)} %collective-permute-done.11.refs_1_, bf16[3,1,256,256]{3,2,1,0:T(8,128)(2,1)S(1)} %collective-permute-done.12.refs_2_, ...), custom_call_target="tpu_custom_call" | custom-call | flops 1 | bytes 1 | tf_op jit(solution)/shard_map/pallas_call | solution.py:99
  101.8 1.1 shard_map.57.refs_0_
  102.9 10.9 %collective-permute-done.17.refs_2_ = bf16[2,256,256]{2,1,0:T(8,128)(2,1)S(1)} collective-permute-done((bf16[2,256,256]{2,1,0:T(8,128)(2,1)S(1)}, bf16[2,256,256]{2,1,0:T(8,128)(2,1)S(1)}, u32[]{:S(2)}, u32[]{:S(2)}) %collective-permute-start.17) | collective-permute-done | bytes 262176 | tf_op jit(solution)/shard_map/ppermute | solution.py:181
  113.8 1.1 shard_map.58
  (15 shorter events, 0.0 us)
Async XLA Ops:
  0.0 6.0 %collective-permute-start.3 = (bf16[1,16,256,256]{3,2,1,0:T(8,128)(2,1)}, bf16[1,16,256,256]{3,2,1,0:T(8,128)(2,1)S(1)}, u32[]{:S(2)}, u32[]{:S(2)}) collective-permute-start(bf16[1,16,256,256]{3,2,1,0:T(8,128)(2,1)} %refs_2_.7), channel_id=1, source_target_pairs={{0,1},{1,0},{2,3},{3,2},{4,5},{5,4},{6,7},{7,6},{8,9},{9,8},{10,11... | collective-permute-start | bytes 6291464 | tf_op jit(solution)/shard_map/ppermute | solution.py:181
  0.5 5.5 %collective-permute-start.2 = (bf16[8,1,256,256]{3,2,1,0:T(8,128)(2,1)}, bf16[8,1,256,256]{3,2,1,0:T(8,128)(2,1)S(1)}, u32[]{:S(2)}, u32[]{:S(2)}) collective-permute-start(bf16[8,1,256,256]{3,2,1,0:T(8,128)(2,1)} %refs_0_.7), channel_id=1, source_target_pairs={{0,1},{1,0},{2,3},{3,2},{4,5},{5,4},{6,7},{7,6},{8,9},{9,8},{10,11... | collective-permute-start | bytes 3145736 | tf_op jit(solution)/shard_map/ppermute | solution.py:181
  0.5 26.6 %collective-permute-start = (bf16[8,1,256,256]{3,2,1,0:T(8,128)(2,1)}, bf16[8,1,256,256]{3,2,1,0:T(8,128)(2,1)S(1)}, u32[]{:S(2)}, u32[]{:S(2)}) collective-permute-start(bf16[8,1,256,256]{3,2,1,0:T(8,128)(2,1)} %refs_6_), channel_id=1, source_target_pairs={{0,4},{1,5},{2,6},{3,7},{4,0},{5,1},{6,2},{7,3},{8,12},{9,13},{10,... | collective-permute-start | bytes 3145736 | tf_op jit(solution)/shard_map/ppermute | solution.py:181
  3.5 23.5 %collective-permute-start.1 = (bf16[8,1,256,256]{3,2,1,0:T(8,128)(2,1)}, bf16[8,1,256,256]{3,2,1,0:T(8,128)(2,1)S(1)}, u32[]{:S(2)}, u32[]{:S(2)}) collective-permute-start(bf16[8,1,256,256]{3,2,1,0:T(8,128)(2,1)} %refs_6_), channel_id=1, source_target_pairs={{4,8},{5,9},{6,10},{7,11},{8,4},{9,5},{10,6},{11,7},{20,24},{21,25... | collective-permute-start | bytes 3145736 | tf_op jit(solution)/shard_map/ppermute | solution.py:181
  4.3 47.5 %collective-permute-start.4 = (bf16[1,16,256,256]{3,2,1,0:T(8,128)(2,1)}, bf16[1,16,256,256]{3,2,1,0:T(8,128)(2,1)S(1)}, u32[]{:S(2)}, u32[]{:S(2)}) collective-permute-start(bf16[1,16,256,256]{3,2,1,0:T(8,128)(2,1)} %refs_2_.7), channel_id=1, source_target_pairs={{0,2},{1,3},{2,0},{3,1},{4,6},{5,7},{6,4},{7,5},{8,10},{9,11},{10,... | collective-permute-start | bytes 6291464 | tf_op jit(solution)/shard_map/ppermute | solution.py:181
  6.0 1.6 %copy-start = (bf16[1,16,256,256]{3,2,1,0:T(8,128)(2,1)S(1)}, bf16[1,16,256,256]{3,2,1,0:T(8,128)(2,1)}, u32[]{:S(2)}) copy-start(bf16[1,16,256,256]{3,2,1,0:T(8,128)(2,1)} %refs_2_.7) | copy-start | bytes 6291460
  7.5 1.2 %copy-start.1 = (bf16[8,1,256,256]{3,2,1,0:T(8,128)(2,1)S(1)}, bf16[8,1,256,256]{3,2,1,0:T(8,128)(2,1)}, u32[]{:S(2)}) copy-start(bf16[8,1,256,256]{3,2,1,0:T(8,128)(2,1)} %refs_0_.7) | copy-start | bytes 3145732
  8.8 1.2 %copy-start.2 = (bf16[8,1,256,256]{3,2,1,0:T(8,128)(2,1)S(1)}, bf16[8,1,256,256]{3,2,1,0:T(8,128)(2,1)}, u32[]{:S(2)}) copy-start(bf16[8,1,256,256]{3,2,1,0:T(8,128)(2,1)} %refs_6_) | copy-start | bytes 3145732
  10.0 0.7 copy-start.4
  27.1 31.1 %collective-permute-start.6 = (bf16[8,1,256,256]{3,2,1,0:T(8,128)(2,1)S(1)}, bf16[8,1,256,256]{3,2,1,0:T(8,128)(2,1)S(1)}, u32[]{:S(2)}, u32[]{:S(2)}) collective-permute-start(bf16[8,1,256,256]{3,2,1,0:T(8,128)(2,1)S(1)} %collective-permute-done.1.refs_4_.refs_6_), channel_id=1, source_target_pairs={{4,0},{5,1},{6,2},{7,3},{8,12},{9,13},{10,14},{11,15},{20,16},{21,... | collective-permute-start | bytes 3145736 | tf_op jit(solution)/shard_map/ppermute | solution.py:181
  28.4 29.9 %collective-permute-start.7 = (bf16[8,1,256,256]{3,2,1,0:T(8,128)(2,1)S(1)}, bf16[8,1,256,256]{3,2,1,0:T(8,128)(2,1)S(1)}, u32[]{:S(2)}, u32[]{:S(2)}) collective-permute-start(bf16[8,1,256,256]{3,2,1,0:T(8,128)(2,1)S(1)} %collective-permute-done.refs_4_.refs_6_), channel_id=1, source_target_pairs={{4,8},{5,9},{6,10},{7,11},{8,4},{9,5},{10,6},{11,7},{20,24},{21,25... | collective-permute-start | bytes 3145736 | tf_op jit(solution)/shard_map/ppermute | solution.py:181
  51.8 23.9 %collective-permute-start.5 = (bf16[8,1,256,256]{3,2,1,0:T(8,128)(2,1)S(1)}, bf16[8,1,256,256]{3,2,1,0:T(8,128)(2,1)S(1)}, u32[]{:S(2)}, u32[]{:S(2)}) collective-permute-start(bf16[8,1,256,256]{3,2,1,0:T(8,128)(2,1)S(1)} %copy-done.1), channel_id=1, source_target_pairs={{0,2},{1,3},{2,0},{3,1},{4,6},{5,7},{6,4},{7,5},{8,10},{9,11},{10,... | collective-permute-start | bytes 3145736 | tf_op jit(solution)/shard_map/ppermute | solution.py:181
  53.3 8.8 %collective-permute-start.8 = (bf16[2,256,256]{2,1,0:T(8,128)(2,1)S(1)}, bf16[2,256,256]{2,1,0:T(8,128)(2,1)S(1)}, u32[]{:S(2)}, u32[]{:S(2)}) collective-permute-start(bf16[2,256,256]{2,1,0:T(8,128)(2,1)S(1)} %shard_map.47), channel_id=1, source_target_pairs={{0,4},{1,5},{2,6},{3,7},{4,0},{5,1},{6,2},{7,3},{8,12},{9,13},{10,... | collective-permute-start | bytes 786440 | tf_op jit(solution)/shard_map/ppermute | solution.py:181
  57.3 4.7 %collective-permute-start.9 = (bf16[2,256,256]{2,1,0:T(8,128)(2,1)S(1)}, bf16[2,256,256]{2,1,0:T(8,128)(2,1)S(1)}, u32[]{:S(2)}, u32[]{:S(2)}) collective-permute-start(bf16[2,256,256]{2,1,0:T(8,128)(2,1)S(1)} %get-tuple-element.37), channel_id=1, source_target_pairs={{4,8},{5,9},{6,10},{7,11},{8,4},{9,5},{10,6},{11,7},{20,24},{21,25... | collective-permute-start | bytes 786440 | tf_op jit(solution)/shard_map/ppermute | solution.py:181
  58.2 19.5 %collective-permute-start.13 = (bf16[1,9,256,256]{3,2,1,0:T(8,128)(2,1)S(1)}, bf16[1,9,256,256]{3,2,1,0:T(8,128)(2,1)S(1)}, u32[]{:S(2)}, u32[]{:S(2)}) collective-permute-start(bf16[1,9,256,256]{3,2,1,0:T(8,128)(2,1)S(1)} %get-tuple-element.43), channel_id=1, source_target_pairs={{0,1},{1,0},{2,3},{3,2},{4,5},{5,4},{6,7},{7,6},{8,9},{9,8},{10,11... | collective-permute-start | bytes 3538952 | tf_op jit(solution)/shard_map/ppermute | solution.py:181
  58.3 36.0 %collective-permute-start.15 = (bf16[8,1,256,256]{3,2,1,0:T(8,128)(2,1)S(1)}, bf16[8,1,256,256]{3,2,1,0:T(8,128)(2,1)S(1)}, u32[]{:S(2)}, u32[]{:S(2)}) collective-permute-start(bf16[8,1,256,256]{3,2,1,0:T(8,128)(2,1)S(1)} %collective-permute-done.7.refs_5_.refs_7_), channel_id=1, source_target_pairs={{4,0},{5,1},{6,2},{7,3},{8,12},{9,13},{10,14},{11,15},{20,16},{21,... | collective-permute-start | bytes 3145736 | tf_op jit(solution)/shard_map/ppermute | solution.py:181
  62.1 15.0 %collective-permute-start.10 = (bf16[2,256,256]{2,1,0:T(8,128)(2,1)S(1)}, bf16[2,256,256]{2,1,0:T(8,128)(2,1)S(1)}, u32[]{:S(2)}, u32[]{:S(2)}) collective-permute-start(bf16[2,256,256]{2,1,0:T(8,128)(2,1)S(1)} %shard_map.49), channel_id=1, source_target_pairs={{0,8},{1,9},{2,10},{3,11},{4,12},{5,13},{6,14},{7,15},{8,0},{9,1},... | collective-permute-start | bytes 786440 | tf_op jit(solution)/shard_map/ppermute | solution.py:181
  65.8 11.9 %collective-permute-start.14 = (bf16[1,7,256,256]{3,2,1,0:T(8,128)(2,1)S(1)}, bf16[1,7,256,256]{3,2,1,0:T(8,128)(2,1)S(1)}, u32[]{:S(2)}, u32[]{:S(2)}) collective-permute-start(bf16[1,7,256,256]{3,2,1,0:T(8,128)(2,1)S(1)} %get-tuple-element.44), channel_id=1, source_target_pairs={{0,1},{1,0},{2,3},{3,2},{4,5},{5,4},{6,7},{7,6},{8,9},{9,8},{10,11... | collective-permute-start | bytes 2752520 | tf_op jit(solution)/shard_map/ppermute | solution.py:181
  77.1 2.7 %collective-permute-start.11 = (bf16[5,1,256,256]{3,2,1,0:T(8,128)(2,1)S(1)}, bf16[5,1,256,256]{3,2,1,0:T(8,128)(2,1)S(1)}, u32[]{:S(2)}, u32[]{:S(2)}) collective-permute-start(bf16[5,1,256,256]{3,2,1,0:T(8,128)(2,1)S(1)} %get-tuple-element.40), channel_id=1, source_target_pairs={{0,1},{1,0},{2,3},{3,2},{4,5},{5,4},{6,7},{7,6},{8,9},{9,8},{10,11... | collective-permute-start | bytes 1966088 | tf_op jit(solution)/shard_map/ppermute | solution.py:181
  77.2 2.6 %collective-permute-start.12 = (bf16[3,1,256,256]{3,2,1,0:T(8,128)(2,1)S(1)}, bf16[3,1,256,256]{3,2,1,0:T(8,128)(2,1)S(1)}, u32[]{:S(2)}, u32[]{:S(2)}) collective-permute-start(bf16[3,1,256,256]{3,2,1,0:T(8,128)(2,1)S(1)} %get-tuple-element.41), channel_id=1, source_target_pairs={{0,1},{1,0},{2,3},{3,2},{4,5},{5,4},{6,7},{7,6},{8,9},{9,8},{10,11... | collective-permute-start | bytes 1179656 | tf_op jit(solution)/shard_map/ppermute | solution.py:181
  81.7 32.1 %collective-permute-start.17 = (bf16[2,256,256]{2,1,0:T(8,128)(2,1)S(1)}, bf16[2,256,256]{2,1,0:T(8,128)(2,1)S(1)}, u32[]{:S(2)}, u32[]{:S(2)}) collective-permute-start(bf16[2,256,256]{2,1,0:T(8,128)(2,1)S(1)} %shard_map.54), channel_id=1, source_target_pairs={{0,4},{1,5},{2,6},{3,7},{4,0},{5,1},{6,2},{7,3},{8,12},{9,13},{10,... | collective-permute-start | bytes 786440 | tf_op jit(solution)/shard_map/ppermute | solution.py:181
  86.1 27.7 %collective-permute-start.16 = (bf16[2,256,256]{2,1,0:T(8,128)(2,1)S(1)}, bf16[2,256,256]{2,1,0:T(8,128)(2,1)S(1)}, u32[]{:S(2)}, u32[]{:S(2)}) collective-permute-start(bf16[2,256,256]{2,1,0:T(8,128)(2,1)S(1)} %shard_map.53), channel_id=1, source_target_pairs={{0,8},{1,9},{2,10},{3,11},{4,12},{5,13},{6,14},{7,15},{8,0},{9,1},... | collective-permute-start | bytes 786440 | tf_op jit(solution)/shard_map/ppermute | solution.py:181
  88.3 25.5 %collective-permute-start.19 = (bf16[2,256,256]{2,1,0:T(8,128)(2,1)S(1)}, bf16[2,256,256]{2,1,0:T(8,128)(2,1)S(1)}, u32[]{:S(2)}, u32[]{:S(2)}) collective-permute-start(bf16[2,256,256]{2,1,0:T(8,128)(2,1)S(1)} %get-tuple-element.47), channel_id=1, source_target_pairs={{4,8},{5,9},{6,10},{7,11},{8,4},{9,5},{10,6},{11,7},{20,24},{21,25... | collective-permute-start | bytes 786440 | tf_op jit(solution)/shard_map/ppermute | solution.py:181
  94.3 5.6 %copy-start.3 = (bf16[8,1,256,256]{3,2,1,0:T(8,128)(2,1)S(1)}, bf16[8,1,256,256]{3,2,1,0:T(8,128)(2,1)}, u32[]{:S(2)}) copy-start(bf16[8,1,256,256]{3,2,1,0:T(8,128)(2,1)} %refs_6_) | copy-start | bytes 3145732
  95.6 18.2 %collective-permute-start.18 = (bf16[4,256,256]{2,1,0:T(8,128)(2,1)S(1)}, bf16[4,256,256]{2,1,0:T(8,128)(2,1)S(1)}, u32[]{:S(2)}, u32[]{:S(2)}) collective-permute-start(bf16[4,256,256]{2,1,0:T(8,128)(2,1)S(1)} %shard_map.55), channel_id=1, source_target_pairs={{0,12},{1,13},{2,14},{3,15},{12,0},{13,1},{14,2},{15,3},{16,28},{1... | collective-permute-start | bytes 1572872 | tf_op jit(solution)/shard_map/ppermute | solution.py:181

commit v25 on v23

--- a/solution.py
+++ b/solution.py
@@ -232,7 +232,8 @@
 
     out = place(16, [(0, own_0), (2, other_0), (4, sent_1), (8, sent_2)], flops=10**10)
     last = [(12, sent_third), (12, sent_own_middle), (14, sent_other_middle)]
-    out = place(16, [(10, other_sent_2), (6, other_sent_1)] + last, out, 2)[:, None]
+    out = place(16, [(10, other_sent_2)] + last, out, 1)
+    out = place(16, [(6, other_sent_1)], out)[:, None]
     if ops > 1:
         out = lax.psum_scatter(out, "op", scatter_dimension=2, tiled=True).astype(jnp.bfloat16)
     return out

time: 115 us -> 115 us (level)
  waiting for transfers between devices: 66.2 us -> 63 us
  starting transfers between devices: 25 us -> 27.1 us
    ppermute x20, waiting for transfers between devices: 66.2 us -> 63 us  [exchange(): return lax.ppermute(array, 'sec', [(s, s ^ bits) for s in members])]
    ppermute x20, starting transfers between devices: 25 us -> 27.1 us  [exchange(): return lax.ppermute(array, 'sec', [(s, s ^ bits) for s in members])]
    pallas_call x2 -> x3, Pallas kernels: 2.2 us -> 2.95 us  [place(): pl.pallas_call(functools.partial(place_kernel, starts, len(held) if share...]
  transfers between devices with their start and end apart: 20 -> 20, of which waited for: 9 -> 10; matrix products, arithmetic and copies ran while one was open for 0% -> 0% of each run, Pallas kernels for 15% -> 16%
where the time goes in v25:
time: 115 us
  waiting for transfers between devices  63 us (55%)
  starting transfers between devices  27.1 us (24%)
  Pallas kernels  19.5 us (17%)
  local copies, waits for them, and re-layouts  4.73 us (4%)
    ppermute x20, waiting for transfers between devices, exchange(): return lax.ppermute(array, 'sec', [(s, s ^ bits) for s in members])  63 us
    ppermute x20, starting transfers between devices, exchange(): return lax.ppermute(array, 'sec', [(s, s ^ bits) for s in members])  27.1 us
    pallas_call x8, Pallas kernels, slot(): pl.pallas_call(functools.partial(slot_kernel, step, parts, len(rights)),...  15.1 us
    unnamed x10, local copies, waits for them, and re-layouts  4.73 us
    pallas_call x3, Pallas kernels, place(): pl.pallas_call(functools.partial(place_kernel, starts, len(held) if share...  2.95 us
  transfers between devices with their start and end apart: 20, of which 10 were waited for; matrix products, arithmetic and copies ran while one was open for 0% of the time, Pallas kernels for 16%

profile of v25, /device:TPU:0, one launch (start us, length us, event | category | flops | bytes accessed | tf_op | source)
XLA Modules:
  0.0 114.6 jit_solution(6809906823116346907)
XLA Ops:
  0.0 0.5 collective-permute-start.3
  0.5 0.1 collective-permute-start.2
  0.5 3.0 %collective-permute-start = (bf16[8,1,256,256]{3,2,1,0:T(8,128)(2,1)}, bf16[8,1,256,256]{3,2,1,0:T(8,128)(2,1)S(1)}, u32[]{:S(2)}, u32[]{:S(2)}) collective-permute-start(bf16[8,1,256,256]{3,2,1,0:T(8,128)(2,1)} %refs_6_), channel_id=1, source_target_pairs={{0,4},{1,5},{2,6},{3,7},{4,0},{5,1},{6,2},{7,3},{8,12},{9,13},{10,... | collective-permute-start | bytes 3145736 | tf_op jit(solution)/shard_map/ppermute | solution.py:181
  3.5 0.7 collective-permute-start.1
  4.3 1.6 %collective-permute-start.4 = (bf16[1,16,256,256]{3,2,1,0:T(8,128)(2,1)}, bf16[1,16,256,256]{3,2,1,0:T(8,128)(2,1)S(1)}, u32[]{:S(2)}, u32[]{:S(2)}) collective-permute-start(bf16[1,16,256,256]{3,2,1,0:T(8,128)(2,1)} %refs_2_.7), channel_id=1, source_target_pairs={{0,2},{1,3},{2,0},{3,1},{4,6},{5,7},{6,4},{7,5},{8,10},{9,11},{10,... | collective-permute-start | bytes 6291464 | tf_op jit(solution)/shard_map/ppermute | solution.py:181
  5.8 0.1 collective-permute-done.2.refs_1_
  6.0 0.0 collective-permute-done.3.refs_3_
  6.0 1.6 %copy-done = bf16[1,16,256,256]{3,2,1,0:T(8,128)(2,1)S(1)} copy-done((bf16[1,16,256,256]{3,2,1,0:T(8,128)(2,1)S(1)}, bf16[1,16,256,256]{3,2,1,0:T(8,128)(2,1)}, u32[]{:S(2)}) %copy-start) | copy-done | bytes 2097176
  7.5 1.2 %copy-done.1 = bf16[8,1,256,256]{3,2,1,0:T(8,128)(2,1)S(1)} copy-done((bf16[8,1,256,256]{3,2,1,0:T(8,128)(2,1)S(1)}, bf16[8,1,256,256]{3,2,1,0:T(8,128)(2,1)}, u32[]{:S(2)}) %copy-start.1) | copy-done | bytes 1048600
  8.8 1.2 %copy-done.2 = bf16[8,1,256,256]{3,2,1,0:T(8,128)(2,1)S(1)} copy-done((bf16[8,1,256,256]{3,2,1,0:T(8,128)(2,1)S(1)}, bf16[8,1,256,256]{3,2,1,0:T(8,128)(2,1)}, u32[]{:S(2)}) %copy-start.2) | copy-done | bytes 1048600
  10.0 0.7 copy-done.4
  10.7 1.9 %shard_map.46.refs_0_ = bf16[2,256,256]{2,1,0:T(8,128)(2,1)S(1)} custom-call(s32[8,16]{1,0:T(8,128)S(1)} %copy-done.4, bf16[8,1,256,256]{3,2,1,0:T(8,128)(2,1)S(1)} %copy-done.1, bf16[8,1,256,256]{3,2,1,0:T(8,128)(2,1)S(1)} %collective-permute-done.2.refs_1_, bf16[1,16,256,256]{3,2,1,0:T(8,128)(2,1)S(1)} %copy-done, ...), custom_call_target="tpu_custom_call" | custom-call | flops 20000000000 | bytes 1 | tf_op jit(solution)/shard_map/pallas_call | solution.py:99
  12.6 14.5 %collective-permute-done.refs_4_.refs_6_ = bf16[8,1,256,256]{3,2,1,0:T(8,128)(2,1)S(1)} collective-permute-done((bf16[8,1,256,256]{3,2,1,0:T(8,128)(2,1)}, bf16[8,1,256,256]{3,2,1,0:T(8,128)(2,1)S(1)}, u32[]{:S(2)}, u32[]{:S(2)}) %collective-permute-start) | collective-permute-done | bytes 1048608 | tf_op jit(solution)/shard_map/ppermute | solution.py:181
  27.1 1.3 %collective-permute-start.6 = (bf16[8,1,256,256]{3,2,1,0:T(8,128)(2,1)S(1)}, bf16[8,1,256,256]{3,2,1,0:T(8,128)(2,1)S(1)}, u32[]{:S(2)}, u32[]{:S(2)}) collective-permute-start(bf16[8,1,256,256]{3,2,1,0:T(8,128)(2,1)S(1)} %collective-permute-done.1.refs_4_.refs_6_), channel_id=1, source_target_pairs={{4,0},{5,1},{6,2},{7,3},{8,12},{9,13},{10,14},{11,15},{20,16},{21,... | collective-permute-start | bytes 3145736 | tf_op jit(solution)/shard_map/ppermute | solution.py:181
  28.4 0.7 collective-permute-start.7
  29.1 1.9 %shard_map.48 = (bf16[2,256,256]{2,1,0:T(8,128)(2,1)S(1)}, bf16[512,2048]{1,0:T(8,128)(2,1)S(1)}) custom-call(s32[8,16]{1,0:T(8,128)S(1)} %copy-done.4, bf16[8,1,256,256]{3,2,1,0:T(8,128)(2,1)S(1)} %copy-done.1, bf16[8,1,256,256]{3,2,1,0:T(8,128)(2,1)S(1)} %collective-permute-done.2.refs_1_, bf16[1,16,256,256]{3,2,1,0:T(8,128)(2,1)S(1)} %copy-done, ...), custom_call_target="tpu_custom_call" | custom-call | flops 1 | bytes 1 | tf_op jit(solution)/shard_map/pallas_call | solution.py:99
  31.0 1.9 %shard_map.47 = bf16[2,256,256]{2,1,0:T(8,128)(2,1)S(1)} custom-call(s32[8,16]{1,0:T(8,128)S(1)} %copy-done.4, bf16[8,1,256,256]{3,2,1,0:T(8,128)(2,1)S(1)} %copy-done.1, bf16[8,1,256,256]{3,2,1,0:T(8,128)(2,1)S(1)} %collective-permute-done.2.refs_1_, bf16[1,16,256,256]{3,2,1,0:T(8,128)(2,1)S(1)} %copy-done, ...), custom_call_target="tpu_custom_call" | custom-call | flops 1 | bytes 1 | tf_op jit(solution)/shard_map/pallas_call | solution.py:99
  32.9 18.9 %collective-permute-done.4.whole.refs_3_ = bf16[1,16,256,256]{3,2,1,0:T(8,128)(2,1)S(1)} collective-permute-done((bf16[1,16,256,256]{3,2,1,0:T(8,128)(2,1)}, bf16[1,16,256,256]{3,2,1,0:T(8,128)(2,1)S(1)}, u32[]{:S(2)}, u32[]{:S(2)}) %collective-permute-start.4) | collective-permute-done | bytes 2097184 | tf_op jit(solution)/shard_map/ppermute | solution.py:181
  51.8 1.5 %collective-permute-start.5 = (bf16[8,1,256,256]{3,2,1,0:T(8,128)(2,1)S(1)}, bf16[8,1,256,256]{3,2,1,0:T(8,128)(2,1)S(1)}, u32[]{:S(2)}, u32[]{:S(2)}) collective-permute-start(bf16[8,1,256,256]{3,2,1,0:T(8,128)(2,1)S(1)} %copy-done.1), channel_id=1, source_target_pairs={{0,2},{1,3},{2,0},{3,1},{4,6},{5,7},{6,4},{7,5},{8,10},{9,11},{10,... | collective-permute-start | bytes 3145736 | tf_op jit(solution)/shard_map/ppermute | solution.py:181
  53.3 4.1 %collective-permute-start.8 = (bf16[2,256,256]{2,1,0:T(8,128)(2,1)S(1)}, bf16[2,256,256]{2,1,0:T(8,128)(2,1)S(1)}, u32[]{:S(2)}, u32[]{:S(2)}) collective-permute-start(bf16[2,256,256]{2,1,0:T(8,128)(2,1)S(1)} %shard_map.47), channel_id=1, source_target_pairs={{0,4},{1,5},{2,6},{3,7},{4,0},{5,1},{6,2},{7,3},{8,12},{9,13},{10,... | collective-permute-start | bytes 786440 | tf_op jit(solution)/shard_map/ppermute | solution.py:181
  57.3 0.7 collective-permute-start.9
  58.0 0.1 shard_map.51
  58.2 0.1 collective-permute-start.13
  58.3 1.3 %collective-permute-start.15 = (bf16[8,1,256,256]{3,2,1,0:T(8,128)(2,1)S(1)}, bf16[8,1,256,256]{3,2,1,0:T(8,128)(2,1)S(1)}, u32[]{:S(2)}, u32[]{:S(2)}) collective-permute-start(bf16[8,1,256,256]{3,2,1,0:T(8,128)(2,1)S(1)} %collective-permute-done.7.refs_5_.refs_7_), channel_id=1, source_target_pairs={{4,0},{5,1},{6,2},{7,3},{8,12},{9,13},{10,14},{11,15},{20,16},{21,... | collective-permute-start | bytes 3145736 | tf_op jit(solution)/shard_map/ppermute | solution.py:181
  59.6 1.9 %shard_map.49 = bf16[2,256,256]{2,1,0:T(8,128)(2,1)S(1)} custom-call(s32[8,16]{1,0:T(8,128)S(1)} %copy-done.4, bf16[8,1,256,256]{3,2,1,0:T(8,128)(2,1)S(1)} %copy-done.1, bf16[8,1,256,256]{3,2,1,0:T(8,128)(2,1)S(1)} %collective-permute-done.2.refs_1_, bf16[1,16,256,256]{3,2,1,0:T(8,128)(2,1)S(1)} %copy-done, ...), custom_call_target="tpu_custom_call" | custom-call | flops 1 | bytes 1 | tf_op jit(solution)/shard_map/pallas_call | solution.py:99
  61.5 0.6 collective-permute-done.8.refs_2_
  62.1 3.7 %collective-permute-start.10 = (bf16[2,256,256]{2,1,0:T(8,128)(2,1)S(1)}, bf16[2,256,256]{2,1,0:T(8,128)(2,1)S(1)}, u32[]{:S(2)}, u32[]{:S(2)}) collective-permute-start(bf16[2,256,256]{2,1,0:T(8,128)(2,1)S(1)} %shard_map.49), channel_id=1, source_target_pairs={{0,8},{1,9},{2,10},{3,11},{4,12},{5,13},{6,14},{7,15},{8,0},{9,1},... | collective-permute-start | bytes 786440 | tf_op jit(solution)/shard_map/ppermute | solution.py:181
  65.8 9.9 %collective-permute-done.5.whole.refs_0_ = bf16[8,1,256,256]{3,2,1,0:T(8,128)(2,1)S(1)} collective-permute-done((bf16[8,1,256,256]{3,2,1,0:T(8,128)(2,1)S(1)}, bf16[8,1,256,256]{3,2,1,0:T(8,128)(2,1)S(1)}, u32[]{:S(2)}, u32[]{:S(2)}) %collective-permute-start.5) | collective-permute-done | bytes 1048608 | tf_op jit(solution)/shard_map/ppermute | solution.py:181
  75.7 1.3 %collective-permute-done.10.refs_3_ = bf16[2,256,256]{2,1,0:T(8,128)(2,1)S(1)} collective-permute-done((bf16[2,256,256]{2,1,0:T(8,128)(2,1)S(1)}, bf16[2,256,256]{2,1,0:T(8,128)(2,1)S(1)}, u32[]{:S(2)}, u32[]{:S(2)}) %collective-permute-start.10) | collective-permute-done | bytes 262176 | tf_op jit(solution)/shard_map/ppermute | solution.py:181
  77.0 0.1 shard_map.50
  77.1 0.1 collective-permute-start.11
  77.2 0.5 collective-permute-start.12
  77.7 2.1 %collective-permute-done.12.refs_2_ = bf16[3,1,256,256]{3,2,1,0:T(8,128)(2,1)S(1)} collective-permute-done((bf16[3,1,256,256]{3,2,1,0:T(8,128)(2,1)S(1)}, bf16[3,1,256,256]{3,2,1,0:T(8,128)(2,1)S(1)}, u32[]{:S(2)}, u32[]{:S(2)}) %collective-permute-start.12) | collective-permute-done | bytes 393248 | tf_op jit(solution)/shard_map/ppermute | solution.py:181
  79.8 1.9 %shard_map.54 = bf16[2,256,256]{2,1,0:T(8,128)(2,1)S(1)} custom-call(s32[8,16]{1,0:T(8,128)S(1)} %copy-done.4, bf16[8,1,256,256]{3,2,1,0:T(8,128)(2,1)S(1)} %collective-permute-done.5.whole.refs_0_, bf16[5,1,256,256]{3,2,1,0:T(8,128)(2,1)S(1)} %collective-permute-done.11.refs_1_, bf16[3,1,256,256]{3,2,1,0:T(8,128)(2,1)S(1)} %collective-permute-done.12.refs_2_, ...), custom_call_target="tpu_custom_call" | custom-call | flops 1 | bytes 1 | tf_op jit(solution)/shard_map/pallas_call | solution.py:99
  81.7 2.5 %collective-permute-start.16 = (bf16[2,256,256]{2,1,0:T(8,128)(2,1)S(1)}, bf16[2,256,256]{2,1,0:T(8,128)(2,1)S(1)}, u32[]{:S(2)}, u32[]{:S(2)}) collective-permute-start(bf16[2,256,256]{2,1,0:T(8,128)(2,1)S(1)} %shard_map.54), channel_id=1, source_target_pairs={{0,8},{1,9},{2,10},{3,11},{4,12},{5,13},{6,14},{7,15},{8,0},{9,1},... | collective-permute-start | bytes 786440 | tf_op jit(solution)/shard_map/ppermute | solution.py:181
  84.3 1.9 %shard_map.52 = (bf16[2,256,256]{2,1,0:T(8,128)(2,1)S(1)}, bf16[512,2048]{1,0:T(8,128)(2,1)S(1)}) custom-call(s32[8,16]{1,0:T(8,128)S(1)} %copy-done.4, bf16[8,1,256,256]{3,2,1,0:T(8,128)(2,1)S(1)} %collective-permute-done.5.whole.refs_0_, bf16[5,1,256,256]{3,2,1,0:T(8,128)(2,1)S(1)} %collective-permute-done.11.refs_1_, ...), custom_call_target="tpu_custom_call" | custom-call | flops 1 | bytes 1 | tf_op jit(solution)/shard_map/pallas_call | solution.py:99
  86.1 0.7 collective-permute-start.18
  86.8 1.9 %shard_map.53 = bf16[2,256,256]{2,1,0:T(8,128)(2,1)S(1)} custom-call(s32[8,16]{1,0:T(8,128)S(1)} %copy-done.4, bf16[8,1,256,256]{3,2,1,0:T(8,128)(2,1)S(1)} %collective-permute-done.5.whole.refs_0_, bf16[5,1,256,256]{3,2,1,0:T(8,128)(2,1)S(1)} %collective-permute-done.11.refs_1_, bf16[3,1,256,256]{3,2,1,0:T(8,128)(2,1)S(1)} %collective-permute-done.12.refs_2_, ...), custom_call_target="tpu_custom_call" | custom-call | flops 1 | bytes 1 | tf_op jit(solution)/shard_map/pallas_call | solution.py:99
  88.7 2.3 %collective-permute-start.19 = (bf16[2,256,256]{2,1,0:T(8,128)(2,1)S(1)}, bf16[2,256,256]{2,1,0:T(8,128)(2,1)S(1)}, u32[]{:S(2)}, u32[]{:S(2)}) collective-permute-start(bf16[2,256,256]{2,1,0:T(8,128)(2,1)S(1)} %shard_map.53), channel_id=1, source_target_pairs={{0,4},{1,5},{2,6},{3,7},{4,0},{5,1},{6,2},{7,3},{8,12},{9,13},{10,... | collective-permute-start | bytes 786440 | tf_op jit(solution)/shard_map/ppermute | solution.py:181
  91.1 6.1 %collective-permute-done.15.refs_2_ = bf16[8,1,256,256]{3,2,1,0:T(8,128)(2,1)S(1)} collective-permute-done((bf16[8,1,256,256]{3,2,1,0:T(8,128)(2,1)S(1)}, bf16[8,1,256,256]{3,2,1,0:T(8,128)(2,1)S(1)}, u32[]{:S(2)}, u32[]{:S(2)}) %collective-permute-start.15) | collective-permute-done | bytes 1048608 | tf_op jit(solution)/shard_map/ppermute | solution.py:181
  97.1 1.3 %shard_map.55 = bf16[4,256,256]{2,1,0:T(8,128)(2,1)S(1)} custom-call(bf16[512,2048]{1,0:T(8,128)(2,1)S(1)} %get-tuple-element.45.refs_0_, bf16[512,2048]{1,0:T(8,128)(2,1)S(1)} %get-tuple-element.46.refs_1_, bf16[8,1,256,256]{3,2,1,0:T(8,128)(2,1)S(1)} %collective-permute-done.15.refs_2_), custom_call_target="tpu_custom_call" | custom-call | flops 10000000000 | bytes 1 | tf_op jit(solution)/shard_map/pallas_call | solution.py:78
  98.4 1.9 %collective-permute-start.17 = (bf16[4,256,256]{2,1,0:T(8,128)(2,1)S(1)}, bf16[4,256,256]{2,1,0:T(8,128)(2,1)S(1)}, u32[]{:S(2)}, u32[]{:S(2)}) collective-permute-start(bf16[4,256,256]{2,1,0:T(8,128)(2,1)S(1)} %shard_map.55), channel_id=1, source_target_pairs={{0,12},{1,13},{2,14},{3,15},{12,0},{13,1},{14,2},{15,3},{16,28},{1... | collective-permute-start | bytes 1572872 | tf_op jit(solution)/shard_map/ppermute | solution.py:181
  100.3 1.9 %shard_map.56.refs_1_ = bf16[2,256,256]{2,1,0:T(8,128)(2,1)S(1)} custom-call(s32[8,16]{1,0:T(8,128)S(1)} %copy-done.4, bf16[8,1,256,256]{3,2,1,0:T(8,128)(2,1)S(1)} %collective-permute-done.5.whole.refs_0_, bf16[5,1,256,256]{3,2,1,0:T(8,128)(2,1)S(1)} %collective-permute-done.11.refs_1_, bf16[3,1,256,256]{3,2,1,0:T(8,128)(2,1)S(1)} %collective-permute-done.12.refs_2_, ...), custom_call_target="tpu_custom_call" | custom-call | flops 1 | bytes 1 | tf_op jit(solution)/shard_map/pallas_call | solution.py:99
  102.2 1.1 shard_map.57.refs_0_
  103.4 8.5 %collective-permute-done.17.refs_2_ = bf16[4,256,256]{2,1,0:T(8,128)(2,1)S(1)} collective-permute-done((bf16[4,256,256]{2,1,0:T(8,128)(2,1)S(1)}, bf16[4,256,256]{2,1,0:T(8,128)(2,1)S(1)}, u32[]{:S(2)}, u32[]{:S(2)}) %collective-permute-start.17) | collective-permute-done | bytes 524320 | tf_op jit(solution)/shard_map/ppermute | solution.py:181
  111.9 1.0 shard_map.58.refs_0_
  112.9 0.9 collective-permute-done.19.refs_1_
  113.8 0.8 shard_map.59
  (16 shorter events, 0.0 us)
Async XLA Ops:
  0.0 6.0 %collective-permute-start.3 = (bf16[1,16,256,256]{3,2,1,0:T(8,128)(2,1)}, bf16[1,16,256,256]{3,2,1,0:T(8,128)(2,1)S(1)}, u32[]{:S(2)}, u32[]{:S(2)}) collective-permute-start(bf16[1,16,256,256]{3,2,1,0:T(8,128)(2,1)} %refs_2_.7), channel_id=1, source_target_pairs={{0,1},{1,0},{2,3},{3,2},{4,5},{5,4},{6,7},{7,6},{8,9},{9,8},{10,11... | collective-permute-start | bytes 6291464 | tf_op jit(solution)/shard_map/ppermute | solution.py:181
  0.5 5.5 %collective-permute-start.2 = (bf16[8,1,256,256]{3,2,1,0:T(8,128)(2,1)}, bf16[8,1,256,256]{3,2,1,0:T(8,128)(2,1)S(1)}, u32[]{:S(2)}, u32[]{:S(2)}) collective-permute-start(bf16[8,1,256,256]{3,2,1,0:T(8,128)(2,1)} %refs_0_.7), channel_id=1, source_target_pairs={{0,1},{1,0},{2,3},{3,2},{4,5},{5,4},{6,7},{7,6},{8,9},{9,8},{10,11... | collective-permute-start | bytes 3145736 | tf_op jit(solution)/shard_map/ppermute | solution.py:181
  0.5 26.6 %collective-permute-start = (bf16[8,1,256,256]{3,2,1,0:T(8,128)(2,1)}, bf16[8,1,256,256]{3,2,1,0:T(8,128)(2,1)S(1)}, u32[]{:S(2)}, u32[]{:S(2)}) collective-permute-start(bf16[8,1,256,256]{3,2,1,0:T(8,128)(2,1)} %refs_6_), channel_id=1, source_target_pairs={{0,4},{1,5},{2,6},{3,7},{4,0},{5,1},{6,2},{7,3},{8,12},{9,13},{10,... | collective-permute-start | bytes 3145736 | tf_op jit(solution)/shard_map/ppermute | solution.py:181
  3.5 23.5 %collective-permute-start.1 = (bf16[8,1,256,256]{3,2,1,0:T(8,128)(2,1)}, bf16[8,1,256,256]{3,2,1,0:T(8,128)(2,1)S(1)}, u32[]{:S(2)}, u32[]{:S(2)}) collective-permute-start(bf16[8,1,256,256]{3,2,1,0:T(8,128)(2,1)} %refs_6_), channel_id=1, source_target_pairs={{4,8},{5,9},{6,10},{7,11},{8,4},{9,5},{10,6},{11,7},{20,24},{21,25... | collective-permute-start | bytes 3145736 | tf_op jit(solution)/shard_map/ppermute | solution.py:181
  4.3 47.5 %collective-permute-start.4 = (bf16[1,16,256,256]{3,2,1,0:T(8,128)(2,1)}, bf16[1,16,256,256]{3,2,1,0:T(8,128)(2,1)S(1)}, u32[]{:S(2)}, u32[]{:S(2)}) collective-permute-start(bf16[1,16,256,256]{3,2,1,0:T(8,128)(2,1)} %refs_2_.7), channel_id=1, source_target_pairs={{0,2},{1,3},{2,0},{3,1},{4,6},{5,7},{6,4},{7,5},{8,10},{9,11},{10,... | collective-permute-start | bytes 6291464 | tf_op jit(solution)/shard_map/ppermute | solution.py:181
  6.0 1.6 %copy-start = (bf16[1,16,256,256]{3,2,1,0:T(8,128)(2,1)S(1)}, bf16[1,16,256,256]{3,2,1,0:T(8,128)(2,1)}, u32[]{:S(2)}) copy-start(bf16[1,16,256,256]{3,2,1,0:T(8,128)(2,1)} %refs_2_.7) | copy-start | bytes 6291460
  7.5 1.2 %copy-start.1 = (bf16[8,1,256,256]{3,2,1,0:T(8,128)(2,1)S(1)}, bf16[8,1,256,256]{3,2,1,0:T(8,128)(2,1)}, u32[]{:S(2)}) copy-start(bf16[8,1,256,256]{3,2,1,0:T(8,128)(2,1)} %refs_0_.7) | copy-start | bytes 3145732
  8.8 1.2 %copy-start.2 = (bf16[8,1,256,256]{3,2,1,0:T(8,128)(2,1)S(1)}, bf16[8,1,256,256]{3,2,1,0:T(8,128)(2,1)}, u32[]{:S(2)}) copy-start(bf16[8,1,256,256]{3,2,1,0:T(8,128)(2,1)} %refs_6_) | copy-start | bytes 3145732
  10.0 0.7 copy-start.4
  27.1 31.1 %collective-permute-start.6 = (bf16[8,1,256,256]{3,2,1,0:T(8,128)(2,1)S(1)}, bf16[8,1,256,256]{3,2,1,0:T(8,128)(2,1)S(1)}, u32[]{:S(2)}, u32[]{:S(2)}) collective-permute-start(bf16[8,1,256,256]{3,2,1,0:T(8,128)(2,1)S(1)} %collective-permute-done.1.refs_4_.refs_6_), channel_id=1, source_target_pairs={{4,0},{5,1},{6,2},{7,3},{8,12},{9,13},{10,14},{11,15},{20,16},{21,... | collective-permute-start | bytes 3145736 | tf_op jit(solution)/shard_map/ppermute | solution.py:181
  28.4 29.9 %collective-permute-start.7 = (bf16[8,1,256,256]{3,2,1,0:T(8,128)(2,1)S(1)}, bf16[8,1,256,256]{3,2,1,0:T(8,128)(2,1)S(1)}, u32[]{:S(2)}, u32[]{:S(2)}) collective-permute-start(bf16[8,1,256,256]{3,2,1,0:T(8,128)(2,1)S(1)} %collective-permute-done.refs_4_.refs_6_), channel_id=1, source_target_pairs={{4,8},{5,9},{6,10},{7,11},{8,4},{9,5},{10,6},{11,7},{20,24},{21,25... | collective-permute-start | bytes 3145736 | tf_op jit(solution)/shard_map/ppermute | solution.py:181
  51.8 23.9 %collective-permute-start.5 = (bf16[8,1,256,256]{3,2,1,0:T(8,128)(2,1)S(1)}, bf16[8,1,256,256]{3,2,1,0:T(8,128)(2,1)S(1)}, u32[]{:S(2)}, u32[]{:S(2)}) collective-permute-start(bf16[8,1,256,256]{3,2,1,0:T(8,128)(2,1)S(1)} %copy-done.1), channel_id=1, source_target_pairs={{0,2},{1,3},{2,0},{3,1},{4,6},{5,7},{6,4},{7,5},{8,10},{9,11},{10,... | collective-permute-start | bytes 3145736 | tf_op jit(solution)/shard_map/ppermute | solution.py:181
  53.3 8.8 %collective-permute-start.8 = (bf16[2,256,256]{2,1,0:T(8,128)(2,1)S(1)}, bf16[2,256,256]{2,1,0:T(8,128)(2,1)S(1)}, u32[]{:S(2)}, u32[]{:S(2)}) collective-permute-start(bf16[2,256,256]{2,1,0:T(8,128)(2,1)S(1)} %shard_map.47), channel_id=1, source_target_pairs={{0,4},{1,5},{2,6},{3,7},{4,0},{5,1},{6,2},{7,3},{8,12},{9,13},{10,... | collective-permute-start | bytes 786440 | tf_op jit(solution)/shard_map/ppermute | solution.py:181
  57.3 4.7 %collective-permute-start.9 = (bf16[2,256,256]{2,1,0:T(8,128)(2,1)S(1)}, bf16[2,256,256]{2,1,0:T(8,128)(2,1)S(1)}, u32[]{:S(2)}, u32[]{:S(2)}) collective-permute-start(bf16[2,256,256]{2,1,0:T(8,128)(2,1)S(1)} %get-tuple-element.37), channel_id=1, source_target_pairs={{4,8},{5,9},{6,10},{7,11},{8,4},{9,5},{10,6},{11,7},{20,24},{21,25... | collective-permute-start | bytes 786440 | tf_op jit(solution)/shard_map/ppermute | solution.py:181
  58.2 19.5 %collective-permute-start.13 = (bf16[1,9,256,256]{3,2,1,0:T(8,128)(2,1)S(1)}, bf16[1,9,256,256]{3,2,1,0:T(8,128)(2,1)S(1)}, u32[]{:S(2)}, u32[]{:S(2)}) collective-permute-start(bf16[1,9,256,256]{3,2,1,0:T(8,128)(2,1)S(1)} %get-tuple-element.43), channel_id=1, source_target_pairs={{0,1},{1,0},{2,3},{3,2},{4,5},{5,4},{6,7},{7,6},{8,9},{9,8},{10,11... | collective-permute-start | bytes 3538952 | tf_op jit(solution)/shard_map/ppermute | solution.py:181
  58.3 38.9 %collective-permute-start.15 = (bf16[8,1,256,256]{3,2,1,0:T(8,128)(2,1)S(1)}, bf16[8,1,256,256]{3,2,1,0:T(8,128)(2,1)S(1)}, u32[]{:S(2)}, u32[]{:S(2)}) collective-permute-start(bf16[8,1,256,256]{3,2,1,0:T(8,128)(2,1)S(1)} %collective-permute-done.7.refs_5_.refs_7_), channel_id=1, source_target_pairs={{4,0},{5,1},{6,2},{7,3},{8,12},{9,13},{10,14},{11,15},{20,16},{21,... | collective-permute-start | bytes 3145736 | tf_op jit(solution)/shard_map/ppermute | solution.py:181
  62.1 15.0 %collective-permute-start.10 = (bf16[2,256,256]{2,1,0:T(8,128)(2,1)S(1)}, bf16[2,256,256]{2,1,0:T(8,128)(2,1)S(1)}, u32[]{:S(2)}, u32[]{:S(2)}) collective-permute-start(bf16[2,256,256]{2,1,0:T(8,128)(2,1)S(1)} %shard_map.49), channel_id=1, source_target_pairs={{0,8},{1,9},{2,10},{3,11},{4,12},{5,13},{6,14},{7,15},{8,0},{9,1},... | collective-permute-start | bytes 786440 | tf_op jit(solution)/shard_map/ppermute | solution.py:181
  65.8 11.9 %collective-permute-start.14 = (bf16[1,7,256,256]{3,2,1,0:T(8,128)(2,1)S(1)}, bf16[1,7,256,256]{3,2,1,0:T(8,128)(2,1)S(1)}, u32[]{:S(2)}, u32[]{:S(2)}) collective-permute-start(bf16[1,7,256,256]{3,2,1,0:T(8,128)(2,1)S(1)} %get-tuple-element.44), channel_id=1, source_target_pairs={{0,1},{1,0},{2,3},{3,2},{4,5},{5,4},{6,7},{7,6},{8,9},{9,8},{10,11... | collective-permute-start | bytes 2752520 | tf_op jit(solution)/shard_map/ppermute | solution.py:181
  77.1 2.7 %collective-permute-start.11 = (bf16[5,1,256,256]{3,2,1,0:T(8,128)(2,1)S(1)}, bf16[5,1,256,256]{3,2,1,0:T(8,128)(2,1)S(1)}, u32[]{:S(2)}, u32[]{:S(2)}) collective-permute-start(bf16[5,1,256,256]{3,2,1,0:T(8,128)(2,1)S(1)} %get-tuple-element.40), channel_id=1, source_target_pairs={{0,1},{1,0},{2,3},{3,2},{4,5},{5,4},{6,7},{7,6},{8,9},{9,8},{10,11... | collective-permute-start | bytes 1966088 | tf_op jit(solution)/shard_map/ppermute | solution.py:181
  77.2 2.6 %collective-permute-start.12 = (bf16[3,1,256,256]{3,2,1,0:T(8,128)(2,1)S(1)}, bf16[3,1,256,256]{3,2,1,0:T(8,128)(2,1)S(1)}, u32[]{:S(2)}, u32[]{:S(2)}) collective-permute-start(bf16[3,1,256,256]{3,2,1,0:T(8,128)(2,1)S(1)} %get-tuple-element.41), channel_id=1, source_target_pairs={{0,1},{1,0},{2,3},{3,2},{4,5},{5,4},{6,7},{7,6},{8,9},{9,8},{10,11... | collective-permute-start | bytes 1179656 | tf_op jit(solution)/shard_map/ppermute | solution.py:181
  81.7 21.6 %collective-permute-start.16 = (bf16[2,256,256]{2,1,0:T(8,128)(2,1)S(1)}, bf16[2,256,256]{2,1,0:T(8,128)(2,1)S(1)}, u32[]{:S(2)}, u32[]{:S(2)}) collective-permute-start(bf16[2,256,256]{2,1,0:T(8,128)(2,1)S(1)} %shard_map.54), channel_id=1, source_target_pairs={{0,8},{1,9},{2,10},{3,11},{4,12},{5,13},{6,14},{7,15},{8,0},{9,1},... | collective-permute-start | bytes 786440 | tf_op jit(solution)/shard_map/ppermute | solution.py:181
  86.1 17.2 %collective-permute-start.18 = (bf16[2,256,256]{2,1,0:T(8,128)(2,1)S(1)}, bf16[2,256,256]{2,1,0:T(8,128)(2,1)S(1)}, u32[]{:S(2)}, u32[]{:S(2)}) collective-permute-start(bf16[2,256,256]{2,1,0:T(8,128)(2,1)S(1)} %get-tuple-element.47), channel_id=1, source_target_pairs={{4,8},{5,9},{6,10},{7,11},{8,4},{9,5},{10,6},{11,7},{20,24},{21,25... | collective-permute-start | bytes 786440 | tf_op jit(solution)/shard_map/ppermute | solution.py:181
  88.7 25.1 %collective-permute-start.19 = (bf16[2,256,256]{2,1,0:T(8,128)(2,1)S(1)}, bf16[2,256,256]{2,1,0:T(8,128)(2,1)S(1)}, u32[]{:S(2)}, u32[]{:S(2)}) collective-permute-start(bf16[2,256,256]{2,1,0:T(8,128)(2,1)S(1)} %shard_map.53), channel_id=1, source_target_pairs={{0,4},{1,5},{2,6},{3,7},{4,0},{5,1},{6,2},{7,3},{8,12},{9,13},{10,... | collective-permute-start | bytes 786440 | tf_op jit(solution)/shard_map/ppermute | solution.py:181
  97.1 3.2 %copy-start.3 = (bf16[8,1,256,256]{3,2,1,0:T(8,128)(2,1)S(1)}, bf16[8,1,256,256]{3,2,1,0:T(8,128)(2,1)}, u32[]{:S(2)}) copy-start(bf16[8,1,256,256]{3,2,1,0:T(8,128)(2,1)} %refs_6_) | copy-start | bytes 3145732
  98.4 13.5 %collective-permute-start.17 = (bf16[4,256,256]{2,1,0:T(8,128)(2,1)S(1)}, bf16[4,256,256]{2,1,0:T(8,128)(2,1)S(1)}, u32[]{:S(2)}, u32[]{:S(2)}) collective-permute-start(bf16[4,256,256]{2,1,0:T(8,128)(2,1)S(1)} %shard_map.55), channel_id=1, source_target_pairs={{0,12},{1,13},{2,14},{3,15},{12,0},{13,1},{14,2},{15,3},{16,28},{1... | collective-permute-start | bytes 1572872 | tf_op jit(solution)/shard_map/ppermute | solution.py:181

commit v26 on v23

--- a/solution.py
+++ b/solution.py
@@ -230,9 +230,9 @@
     right_last, last_third = lax.optimization_barrier((right_env, last_third))
     other_0 = products(0, *other, (right_last,))
 
-    out = place(16, [(0, own_0), (2, other_0), (4, sent_1), (8, sent_2)], flops=10**10)
+    out = place(16, [(0, own_0), (2, other_0), (4, sent_1), (8, sent_2), (10, other_sent_2)], flops=10**10)
     last = [(12, sent_third), (12, sent_own_middle), (14, sent_other_middle)]
-    out = place(16, [(10, other_sent_2), (6, other_sent_1)] + last, out, 2)[:, None]
+    out = place(16, [(6, other_sent_1)] + last, out, 1)[:, None]
     if ops > 1:
         out = lax.psum_scatter(out, "op", scatter_dimension=2, tiled=True).astype(jnp.bfloat16)
     return out

time: 115 us -> 115 us (level)
  no operation moved by 1% of the time
where the time goes in v26:
time: 115 us
  waiting for transfers between devices  66.1 us (57%)
  starting transfers between devices  25 us (22%)
  Pallas kernels  18.8 us (16%)
  local copies, waits for them, and re-layouts  4.73 us (4%)
    ppermute x20, waiting for transfers between devices, exchange(): return lax.ppermute(array, 'sec', [(s, s ^ bits) for s in members])  66.1 us
    ppermute x20, starting transfers between devices, exchange(): return lax.ppermute(array, 'sec', [(s, s ^ bits) for s in members])  25 us
    pallas_call x8, Pallas kernels, slot(): pl.pallas_call(functools.partial(slot_kernel, step, parts, len(rights)),...  15.1 us
    unnamed x10, local copies, waits for them, and re-layouts  4.73 us
  transfers between devices with their start and end apart: 20, of which 9 were waited for; matrix products, arithmetic and copies ran while one was open for 0% of the time, Pallas kernels for 15%

profile of v26, /device:TPU:0, one launch (start us, length us, event | category | flops | bytes accessed | tf_op | source)
XLA Modules:
  0.0 114.8 jit_solution(1721795472244651072)
XLA Ops:
  0.0 0.5 collective-permute-start.3
  0.5 0.1 collective-permute-start.2
  0.5 3.0 %collective-permute-start = (bf16[8,1,256,256]{3,2,1,0:T(8,128)(2,1)}, bf16[8,1,256,256]{3,2,1,0:T(8,128)(2,1)S(1)}, u32[]{:S(2)}, u32[]{:S(2)}) collective-permute-start(bf16[8,1,256,256]{3,2,1,0:T(8,128)(2,1)} %refs_6_), channel_id=1, source_target_pairs={{0,4},{1,5},{2,6},{3,7},{4,0},{5,1},{6,2},{7,3},{8,12},{9,13},{10,... | collective-permute-start | bytes 3145736 | tf_op jit(solution)/shard_map/ppermute | solution.py:181
  3.5 0.7 collective-permute-start.1
  4.3 1.6 %collective-permute-start.4 = (bf16[1,16,256,256]{3,2,1,0:T(8,128)(2,1)}, bf16[1,16,256,256]{3,2,1,0:T(8,128)(2,1)S(1)}, u32[]{:S(2)}, u32[]{:S(2)}) collective-permute-start(bf16[1,16,256,256]{3,2,1,0:T(8,128)(2,1)} %refs_2_.7), channel_id=1, source_target_pairs={{0,2},{1,3},{2,0},{3,1},{4,6},{5,7},{6,4},{7,5},{8,10},{9,11},{10,... | collective-permute-start | bytes 6291464 | tf_op jit(solution)/shard_map/ppermute | solution.py:181
  5.8 0.1 collective-permute-done.2.refs_1_
  6.0 1.6 %copy-done = bf16[1,16,256,256]{3,2,1,0:T(8,128)(2,1)S(1)} copy-done((bf16[1,16,256,256]{3,2,1,0:T(8,128)(2,1)S(1)}, bf16[1,16,256,256]{3,2,1,0:T(8,128)(2,1)}, u32[]{:S(2)}) %copy-start) | copy-done | bytes 2097176
  7.5 1.2 %copy-done.1 = bf16[8,1,256,256]{3,2,1,0:T(8,128)(2,1)S(1)} copy-done((bf16[8,1,256,256]{3,2,1,0:T(8,128)(2,1)S(1)}, bf16[8,1,256,256]{3,2,1,0:T(8,128)(2,1)}, u32[]{:S(2)}) %copy-start.1) | copy-done | bytes 1048600
  8.8 1.2 %copy-done.2 = bf16[8,1,256,256]{3,2,1,0:T(8,128)(2,1)S(1)} copy-done((bf16[8,1,256,256]{3,2,1,0:T(8,128)(2,1)S(1)}, bf16[8,1,256,256]{3,2,1,0:T(8,128)(2,1)}, u32[]{:S(2)}) %copy-start.2) | copy-done | bytes 1048600
  10.0 0.7 copy-done.4
  10.7 1.9 %shard_map.46.refs_0_ = bf16[2,256,256]{2,1,0:T(8,128)(2,1)S(1)} custom-call(s32[8,16]{1,0:T(8,128)S(1)} %copy-done.4, bf16[8,1,256,256]{3,2,1,0:T(8,128)(2,1)S(1)} %copy-done.1, bf16[8,1,256,256]{3,2,1,0:T(8,128)(2,1)S(1)} %collective-permute-done.2.refs_1_, bf16[1,16,256,256]{3,2,1,0:T(8,128)(2,1)S(1)} %copy-done, ...), custom_call_target="tpu_custom_call" | custom-call | flops 20000000000 | bytes 1 | tf_op jit(solution)/shard_map/pallas_call | solution.py:99
  12.6 14.5 %collective-permute-done.refs_4_.refs_6_ = bf16[8,1,256,256]{3,2,1,0:T(8,128)(2,1)S(1)} collective-permute-done((bf16[8,1,256,256]{3,2,1,0:T(8,128)(2,1)}, bf16[8,1,256,256]{3,2,1,0:T(8,128)(2,1)S(1)}, u32[]{:S(2)}, u32[]{:S(2)}) %collective-permute-start) | collective-permute-done | bytes 1048608 | tf_op jit(solution)/shard_map/ppermute | solution.py:181
  27.1 1.3 %collective-permute-start.6 = (bf16[8,1,256,256]{3,2,1,0:T(8,128)(2,1)S(1)}, bf16[8,1,256,256]{3,2,1,0:T(8,128)(2,1)S(1)}, u32[]{:S(2)}, u32[]{:S(2)}) collective-permute-start(bf16[8,1,256,256]{3,2,1,0:T(8,128)(2,1)S(1)} %collective-permute-done.1.refs_4_.refs_6_), channel_id=1, source_target_pairs={{4,0},{5,1},{6,2},{7,3},{8,12},{9,13},{10,14},{11,15},{20,16},{21,... | collective-permute-start | bytes 3145736 | tf_op jit(solution)/shard_map/ppermute | solution.py:181
  28.4 0.7 collective-permute-start.7
  29.1 1.9 %shard_map.48 = (bf16[2,256,256]{2,1,0:T(8,128)(2,1)S(1)}, bf16[512,2048]{1,0:T(8,128)(2,1)S(1)}) custom-call(s32[8,16]{1,0:T(8,128)S(1)} %copy-done.4, bf16[8,1,256,256]{3,2,1,0:T(8,128)(2,1)S(1)} %copy-done.1, bf16[8,1,256,256]{3,2,1,0:T(8,128)(2,1)S(1)} %collective-permute-done.2.refs_1_, bf16[1,16,256,256]{3,2,1,0:T(8,128)(2,1)S(1)} %copy-done, ...), custom_call_target="tpu_custom_call" | custom-call | flops 1 | bytes 1 | tf_op jit(solution)/shard_map/pallas_call | solution.py:99
  31.0 1.9 %shard_map.47 = bf16[2,256,256]{2,1,0:T(8,128)(2,1)S(1)} custom-call(s32[8,16]{1,0:T(8,128)S(1)} %copy-done.4, bf16[8,1,256,256]{3,2,1,0:T(8,128)(2,1)S(1)} %copy-done.1, bf16[8,1,256,256]{3,2,1,0:T(8,128)(2,1)S(1)} %collective-permute-done.2.refs_1_, bf16[1,16,256,256]{3,2,1,0:T(8,128)(2,1)S(1)} %copy-done, ...), custom_call_target="tpu_custom_call" | custom-call | flops 1 | bytes 1 | tf_op jit(solution)/shard_map/pallas_call | solution.py:99
  32.9 18.9 %collective-permute-done.4.whole.refs_3_ = bf16[1,16,256,256]{3,2,1,0:T(8,128)(2,1)S(1)} collective-permute-done((bf16[1,16,256,256]{3,2,1,0:T(8,128)(2,1)}, bf16[1,16,256,256]{3,2,1,0:T(8,128)(2,1)S(1)}, u32[]{:S(2)}, u32[]{:S(2)}) %collective-permute-start.4) | collective-permute-done | bytes 2097184 | tf_op jit(solution)/shard_map/ppermute | solution.py:181
  51.8 1.5 %collective-permute-start.5 = (bf16[8,1,256,256]{3,2,1,0:T(8,128)(2,1)S(1)}, bf16[8,1,256,256]{3,2,1,0:T(8,128)(2,1)S(1)}, u32[]{:S(2)}, u32[]{:S(2)}) collective-permute-start(bf16[8,1,256,256]{3,2,1,0:T(8,128)(2,1)S(1)} %copy-done.1), channel_id=1, source_target_pairs={{0,2},{1,3},{2,0},{3,1},{4,6},{5,7},{6,4},{7,5},{8,10},{9,11},{10,... | collective-permute-start | bytes 3145736 | tf_op jit(solution)/shard_map/ppermute | solution.py:181
  53.3 4.1 %collective-permute-start.8 = (bf16[2,256,256]{2,1,0:T(8,128)(2,1)S(1)}, bf16[2,256,256]{2,1,0:T(8,128)(2,1)S(1)}, u32[]{:S(2)}, u32[]{:S(2)}) collective-permute-start(bf16[2,256,256]{2,1,0:T(8,128)(2,1)S(1)} %shard_map.47), channel_id=1, source_target_pairs={{0,4},{1,5},{2,6},{3,7},{4,0},{5,1},{6,2},{7,3},{8,12},{9,13},{10,... | collective-permute-start | bytes 786440 | tf_op jit(solution)/shard_map/ppermute | solution.py:181
  57.3 0.7 collective-permute-start.9
  58.0 0.1 shard_map.51
  58.2 0.1 collective-permute-start.13
  58.2 0.0 collective-permute-done.7.refs_5_.refs_7_
  58.3 1.3 %collective-permute-start.15 = (bf16[8,1,256,256]{3,2,1,0:T(8,128)(2,1)S(1)}, bf16[8,1,256,256]{3,2,1,0:T(8,128)(2,1)S(1)}, u32[]{:S(2)}, u32[]{:S(2)}) collective-permute-start(bf16[8,1,256,256]{3,2,1,0:T(8,128)(2,1)S(1)} %collective-permute-done.7.refs_5_.refs_7_), channel_id=1, source_target_pairs={{4,0},{5,1},{6,2},{7,3},{8,12},{9,13},{10,14},{11,15},{20,16},{21,... | collective-permute-start | bytes 3145736 | tf_op jit(solution)/shard_map/ppermute | solution.py:181
  59.6 1.9 %shard_map.49 = bf16[2,256,256]{2,1,0:T(8,128)(2,1)S(1)} custom-call(s32[8,16]{1,0:T(8,128)S(1)} %copy-done.4, bf16[8,1,256,256]{3,2,1,0:T(8,128)(2,1)S(1)} %copy-done.1, bf16[8,1,256,256]{3,2,1,0:T(8,128)(2,1)S(1)} %collective-permute-done.2.refs_1_, bf16[1,16,256,256]{3,2,1,0:T(8,128)(2,1)S(1)} %copy-done, ...), custom_call_target="tpu_custom_call" | custom-call | flops 1 | bytes 1 | tf_op jit(solution)/shard_map/pallas_call | solution.py:99
  61.5 0.6 collective-permute-done.8.refs_2_
  62.1 3.7 %collective-permute-start.10 = (bf16[2,256,256]{2,1,0:T(8,128)(2,1)S(1)}, bf16[2,256,256]{2,1,0:T(8,128)(2,1)S(1)}, u32[]{:S(2)}, u32[]{:S(2)}) collective-permute-start(bf16[2,256,256]{2,1,0:T(8,128)(2,1)S(1)} %shard_map.49), channel_id=1, source_target_pairs={{0,8},{1,9},{2,10},{3,11},{4,12},{5,13},{6,14},{7,15},{8,0},{9,1},... | collective-permute-start | bytes 786440 | tf_op jit(solution)/shard_map/ppermute | solution.py:181
  65.8 9.9 %collective-permute-done.5.whole.refs_0_ = bf16[8,1,256,256]{3,2,1,0:T(8,128)(2,1)S(1)} collective-permute-done((bf16[8,1,256,256]{3,2,1,0:T(8,128)(2,1)S(1)}, bf16[8,1,256,256]{3,2,1,0:T(8,128)(2,1)S(1)}, u32[]{:S(2)}, u32[]{:S(2)}) %collective-permute-start.5) | collective-permute-done | bytes 1048608 | tf_op jit(solution)/shard_map/ppermute | solution.py:181
  75.7 1.3 %collective-permute-done.10.refs_3_ = bf16[2,256,256]{2,1,0:T(8,128)(2,1)S(1)} collective-permute-done((bf16[2,256,256]{2,1,0:T(8,128)(2,1)S(1)}, bf16[2,256,256]{2,1,0:T(8,128)(2,1)S(1)}, u32[]{:S(2)}, u32[]{:S(2)}) %collective-permute-start.10) | collective-permute-done | bytes 262176 | tf_op jit(solution)/shard_map/ppermute | solution.py:181
  77.0 0.1 shard_map.50
  77.1 0.1 collective-permute-start.11
  77.2 0.5 collective-permute-start.12
  77.7 0.0 collective-permute-done.14.refs_5_
  77.7 0.0 collective-permute-done.13.refs_4_
  77.7 2.1 %collective-permute-done.12.refs_2_ = bf16[3,1,256,256]{3,2,1,0:T(8,128)(2,1)S(1)} collective-permute-done((bf16[3,1,256,256]{3,2,1,0:T(8,128)(2,1)S(1)}, bf16[3,1,256,256]{3,2,1,0:T(8,128)(2,1)S(1)}, u32[]{:S(2)}, u32[]{:S(2)}) %collective-permute-start.12) | collective-permute-done | bytes 393248 | tf_op jit(solution)/shard_map/ppermute | solution.py:181
  79.8 1.9 %shard_map.54 = bf16[2,256,256]{2,1,0:T(8,128)(2,1)S(1)} custom-call(s32[8,16]{1,0:T(8,128)S(1)} %copy-done.4, bf16[8,1,256,256]{3,2,1,0:T(8,128)(2,1)S(1)} %collective-permute-done.5.whole.refs_0_, bf16[5,1,256,256]{3,2,1,0:T(8,128)(2,1)S(1)} %collective-permute-done.11.refs_1_, bf16[3,1,256,256]{3,2,1,0:T(8,128)(2,1)S(1)} %collective-permute-done.12.refs_2_, ...), custom_call_target="tpu_custom_call" | custom-call | flops 1 | bytes 1 | tf_op jit(solution)/shard_map/pallas_call | solution.py:99
  81.7 2.5 %collective-permute-start.16 = (bf16[2,256,256]{2,1,0:T(8,128)(2,1)S(1)}, bf16[2,256,256]{2,1,0:T(8,128)(2,1)S(1)}, u32[]{:S(2)}, u32[]{:S(2)}) collective-permute-start(bf16[2,256,256]{2,1,0:T(8,128)(2,1)S(1)} %shard_map.54), channel_id=1, source_target_pairs={{0,8},{1,9},{2,10},{3,11},{4,12},{5,13},{6,14},{7,15},{8,0},{9,1},... | collective-permute-start | bytes 786440 | tf_op jit(solution)/shard_map/ppermute | solution.py:181
  84.3 1.9 %shard_map.53 = bf16[2,256,256]{2,1,0:T(8,128)(2,1)S(1)} custom-call(s32[8,16]{1,0:T(8,128)S(1)} %copy-done.4, bf16[8,1,256,256]{3,2,1,0:T(8,128)(2,1)S(1)} %collective-permute-done.5.whole.refs_0_, bf16[5,1,256,256]{3,2,1,0:T(8,128)(2,1)S(1)} %collective-permute-done.11.refs_1_, bf16[3,1,256,256]{3,2,1,0:T(8,128)(2,1)S(1)} %collective-permute-done.12.refs_2_, ...), custom_call_target="tpu_custom_call" | custom-call | flops 1 | bytes 1 | tf_op jit(solution)/shard_map/pallas_call | solution.py:99
  86.2 0.2 collective-permute-start.17
  86.4 1.9 %shard_map.52 = (bf16[2,256,256]{2,1,0:T(8,128)(2,1)S(1)}, bf16[512,2048]{1,0:T(8,128)(2,1)S(1)}) custom-call(s32[8,16]{1,0:T(8,128)S(1)} %copy-done.4, bf16[8,1,256,256]{3,2,1,0:T(8,128)(2,1)S(1)} %collective-permute-done.5.whole.refs_0_, bf16[5,1,256,256]{3,2,1,0:T(8,128)(2,1)S(1)} %collective-permute-done.11.refs_1_, ...), custom_call_target="tpu_custom_call" | custom-call | flops 1 | bytes 1 | tf_op jit(solution)/shard_map/pallas_call | solution.py:99
  88.3 0.7 collective-permute-start.19
  88.9 8.2 %collective-permute-done.15.refs_2_ = bf16[8,1,256,256]{3,2,1,0:T(8,128)(2,1)S(1)} collective-permute-done((bf16[8,1,256,256]{3,2,1,0:T(8,128)(2,1)S(1)}, bf16[8,1,256,256]{3,2,1,0:T(8,128)(2,1)S(1)}, u32[]{:S(2)}, u32[]{:S(2)}) %collective-permute-start.15) | collective-permute-done | bytes 1048608 | tf_op jit(solution)/shard_map/ppermute | solution.py:181
  97.1 1.3 %shard_map.55 = bf16[4,256,256]{2,1,0:T(8,128)(2,1)S(1)} custom-call(bf16[512,2048]{1,0:T(8,128)(2,1)S(1)} %get-tuple-element.45.refs_0_, bf16[512,2048]{1,0:T(8,128)(2,1)S(1)} %get-tuple-element.46.refs_1_, bf16[8,1,256,256]{3,2,1,0:T(8,128)(2,1)S(1)} %collective-permute-done.15.refs_2_), custom_call_target="tpu_custom_call" | custom-call | flops 10000000000 | bytes 1 | tf_op jit(solution)/shard_map/pallas_call | solution.py:78
  98.4 1.9 %collective-permute-start.18 = (bf16[4,256,256]{2,1,0:T(8,128)(2,1)S(1)}, bf16[4,256,256]{2,1,0:T(8,128)(2,1)S(1)}, u32[]{:S(2)}, u32[]{:S(2)}) collective-permute-start(bf16[4,256,256]{2,1,0:T(8,128)(2,1)S(1)} %shard_map.55), channel_id=1, source_target_pairs={{0,12},{1,13},{2,14},{3,15},{12,0},{13,1},{14,2},{15,3},{16,28},{1... | collective-permute-start | bytes 1572872 | tf_op jit(solution)/shard_map/ppermute | solution.py:181
  100.3 1.9 %shard_map.56.refs_1_ = bf16[2,256,256]{2,1,0:T(8,128)(2,1)S(1)} custom-call(s32[8,16]{1,0:T(8,128)S(1)} %copy-done.4, bf16[8,1,256,256]{3,2,1,0:T(8,128)(2,1)S(1)} %collective-permute-done.5.whole.refs_0_, bf16[5,1,256,256]{3,2,1,0:T(8,128)(2,1)S(1)} %collective-permute-done.11.refs_1_, bf16[3,1,256,256]{3,2,1,0:T(8,128)(2,1)S(1)} %collective-permute-done.12.refs_2_, ...), custom_call_target="tpu_custom_call" | custom-call | flops 1 | bytes 1 | tf_op jit(solution)/shard_map/pallas_call | solution.py:99
  102.3 1.2 %shard_map.57.refs_0_ = bf16[16,256,256]{2,1,0:T(8,128)(2,1)} custom-call(bf16[2,256,256]{2,1,0:T(8,128)(2,1)S(1)} %shard_map.46.refs_0_, bf16[2,256,256]{2,1,0:T(8,128)(2,1)S(1)} %shard_map.56.refs_1_, bf16[2,256,256]{2,1,0:T(8,128)(2,1)S(1)} %collective-permute-done.8.refs_2_, bf16[2,256,256]{2,1,0:T(8,128)(2,1)S(1)} %collective-permute-done.10.refs_3_, ...), custom_call_target="tpu_custom_call" | custom-call | flops 10000000000 | bytes 1 | tf_op jit(solution)/shard_map/pallas_call | solution.py:168
  103.5 10.3 %collective-permute-done.17.refs_1_ = bf16[2,256,256]{2,1,0:T(8,128)(2,1)S(1)} collective-permute-done((bf16[2,256,256]{2,1,0:T(8,128)(2,1)S(1)}, bf16[2,256,256]{2,1,0:T(8,128)(2,1)S(1)}, u32[]{:S(2)}, u32[]{:S(2)}) %collective-permute-start.17) | collective-permute-done | bytes 262176 | tf_op jit(solution)/shard_map/ppermute | solution.py:181
  113.8 1.0 shard_map.58
  (15 shorter events, 0.0 us)
Async XLA Ops:
  0.0 6.0 %collective-permute-start.3 = (bf16[1,16,256,256]{3,2,1,0:T(8,128)(2,1)}, bf16[1,16,256,256]{3,2,1,0:T(8,128)(2,1)S(1)}, u32[]{:S(2)}, u32[]{:S(2)}) collective-permute-start(bf16[1,16,256,256]{3,2,1,0:T(8,128)(2,1)} %refs_2_.7), channel_id=1, source_target_pairs={{0,1},{1,0},{2,3},{3,2},{4,5},{5,4},{6,7},{7,6},{8,9},{9,8},{10,11... | collective-permute-start | bytes 6291464 | tf_op jit(solution)/shard_map/ppermute | solution.py:181
  0.5 5.5 %collective-permute-start.2 = (bf16[8,1,256,256]{3,2,1,0:T(8,128)(2,1)}, bf16[8,1,256,256]{3,2,1,0:T(8,128)(2,1)S(1)}, u32[]{:S(2)}, u32[]{:S(2)}) collective-permute-start(bf16[8,1,256,256]{3,2,1,0:T(8,128)(2,1)} %refs_0_.7), channel_id=1, source_target_pairs={{0,1},{1,0},{2,3},{3,2},{4,5},{5,4},{6,7},{7,6},{8,9},{9,8},{10,11... | collective-permute-start | bytes 3145736 | tf_op jit(solution)/shard_map/ppermute | solution.py:181
  0.5 26.6 %collective-permute-start = (bf16[8,1,256,256]{3,2,1,0:T(8,128)(2,1)}, bf16[8,1,256,256]{3,2,1,0:T(8,128)(2,1)S(1)}, u32[]{:S(2)}, u32[]{:S(2)}) collective-permute-start(bf16[8,1,256,256]{3,2,1,0:T(8,128)(2,1)} %refs_6_), channel_id=1, source_target_pairs={{0,4},{1,5},{2,6},{3,7},{4,0},{5,1},{6,2},{7,3},{8,12},{9,13},{10,... | collective-permute-start | bytes 3145736 | tf_op jit(solution)/shard_map/ppermute | solution.py:181
  3.5 23.5 %collective-permute-start.1 = (bf16[8,1,256,256]{3,2,1,0:T(8,128)(2,1)}, bf16[8,1,256,256]{3,2,1,0:T(8,128)(2,1)S(1)}, u32[]{:S(2)}, u32[]{:S(2)}) collective-permute-start(bf16[8,1,256,256]{3,2,1,0:T(8,128)(2,1)} %refs_6_), channel_id=1, source_target_pairs={{4,8},{5,9},{6,10},{7,11},{8,4},{9,5},{10,6},{11,7},{20,24},{21,25... | collective-permute-start | bytes 3145736 | tf_op jit(solution)/shard_map/ppermute | solution.py:181
  4.3 47.5 %collective-permute-start.4 = (bf16[1,16,256,256]{3,2,1,0:T(8,128)(2,1)}, bf16[1,16,256,256]{3,2,1,0:T(8,128)(2,1)S(1)}, u32[]{:S(2)}, u32[]{:S(2)}) collective-permute-start(bf16[1,16,256,256]{3,2,1,0:T(8,128)(2,1)} %refs_2_.7), channel_id=1, source_target_pairs={{0,2},{1,3},{2,0},{3,1},{4,6},{5,7},{6,4},{7,5},{8,10},{9,11},{10,... | collective-permute-start | bytes 6291464 | tf_op jit(solution)/shard_map/ppermute | solution.py:181
  6.0 1.6 %copy-start = (bf16[1,16,256,256]{3,2,1,0:T(8,128)(2,1)S(1)}, bf16[1,16,256,256]{3,2,1,0:T(8,128)(2,1)}, u32[]{:S(2)}) copy-start(bf16[1,16,256,256]{3,2,1,0:T(8,128)(2,1)} %refs_2_.7) | copy-start | bytes 6291460
  7.5 1.2 %copy-start.1 = (bf16[8,1,256,256]{3,2,1,0:T(8,128)(2,1)S(1)}, bf16[8,1,256,256]{3,2,1,0:T(8,128)(2,1)}, u32[]{:S(2)}) copy-start(bf16[8,1,256,256]{3,2,1,0:T(8,128)(2,1)} %refs_0_.7) | copy-start | bytes 3145732
  8.8 1.2 %copy-start.2 = (bf16[8,1,256,256]{3,2,1,0:T(8,128)(2,1)S(1)}, bf16[8,1,256,256]{3,2,1,0:T(8,128)(2,1)}, u32[]{:S(2)}) copy-start(bf16[8,1,256,256]{3,2,1,0:T(8,128)(2,1)} %refs_6_) | copy-start | bytes 3145732
  10.0 0.7 copy-start.4
  27.1 31.1 %collective-permute-start.6 = (bf16[8,1,256,256]{3,2,1,0:T(8,128)(2,1)S(1)}, bf16[8,1,256,256]{3,2,1,0:T(8,128)(2,1)S(1)}, u32[]{:S(2)}, u32[]{:S(2)}) collective-permute-start(bf16[8,1,256,256]{3,2,1,0:T(8,128)(2,1)S(1)} %collective-permute-done.1.refs_4_.refs_6_), channel_id=1, source_target_pairs={{4,0},{5,1},{6,2},{7,3},{8,12},{9,13},{10,14},{11,15},{20,16},{21,... | collective-permute-start | bytes 3145736 | tf_op jit(solution)/shard_map/ppermute | solution.py:181
  28.4 29.9 %collective-permute-start.7 = (bf16[8,1,256,256]{3,2,1,0:T(8,128)(2,1)S(1)}, bf16[8,1,256,256]{3,2,1,0:T(8,128)(2,1)S(1)}, u32[]{:S(2)}, u32[]{:S(2)}) collective-permute-start(bf16[8,1,256,256]{3,2,1,0:T(8,128)(2,1)S(1)} %collective-permute-done.refs_4_.refs_6_), channel_id=1, source_target_pairs={{4,8},{5,9},{6,10},{7,11},{8,4},{9,5},{10,6},{11,7},{20,24},{21,25... | collective-permute-start | bytes 3145736 | tf_op jit(solution)/shard_map/ppermute | solution.py:181
  51.8 23.9 %collective-permute-start.5 = (bf16[8,1,256,256]{3,2,1,0:T(8,128)(2,1)S(1)}, bf16[8,1,256,256]{3,2,1,0:T(8,128)(2,1)S(1)}, u32[]{:S(2)}, u32[]{:S(2)}) collective-permute-start(bf16[8,1,256,256]{3,2,1,0:T(8,128)(2,1)S(1)} %copy-done.1), channel_id=1, source_target_pairs={{0,2},{1,3},{2,0},{3,1},{4,6},{5,7},{6,4},{7,5},{8,10},{9,11},{10,... | collective-permute-start | bytes 3145736 | tf_op jit(solution)/shard_map/ppermute | solution.py:181
  53.3 8.8 %collective-permute-start.8 = (bf16[2,256,256]{2,1,0:T(8,128)(2,1)S(1)}, bf16[2,256,256]{2,1,0:T(8,128)(2,1)S(1)}, u32[]{:S(2)}, u32[]{:S(2)}) collective-permute-start(bf16[2,256,256]{2,1,0:T(8,128)(2,1)S(1)} %shard_map.47), channel_id=1, source_target_pairs={{0,4},{1,5},{2,6},{3,7},{4,0},{5,1},{6,2},{7,3},{8,12},{9,13},{10,... | collective-permute-start | bytes 786440 | tf_op jit(solution)/shard_map/ppermute | solution.py:181
  57.3 4.7 %collective-permute-start.9 = (bf16[2,256,256]{2,1,0:T(8,128)(2,1)S(1)}, bf16[2,256,256]{2,1,0:T(8,128)(2,1)S(1)}, u32[]{:S(2)}, u32[]{:S(2)}) collective-permute-start(bf16[2,256,256]{2,1,0:T(8,128)(2,1)S(1)} %get-tuple-element.37), channel_id=1, source_target_pairs={{4,8},{5,9},{6,10},{7,11},{8,4},{9,5},{10,6},{11,7},{20,24},{21,25... | collective-permute-start | bytes 786440 | tf_op jit(solution)/shard_map/ppermute | solution.py:181
  58.2 19.5 %collective-permute-start.13 = (bf16[1,9,256,256]{3,2,1,0:T(8,128)(2,1)S(1)}, bf16[1,9,256,256]{3,2,1,0:T(8,128)(2,1)S(1)}, u32[]{:S(2)}, u32[]{:S(2)}) collective-permute-start(bf16[1,9,256,256]{3,2,1,0:T(8,128)(2,1)S(1)} %get-tuple-element.43), channel_id=1, source_target_pairs={{0,1},{1,0},{2,3},{3,2},{4,5},{5,4},{6,7},{7,6},{8,9},{9,8},{10,11... | collective-permute-start | bytes 3538952 | tf_op jit(solution)/shard_map/ppermute | solution.py:181
  58.3 38.9 %collective-permute-start.15 = (bf16[8,1,256,256]{3,2,1,0:T(8,128)(2,1)S(1)}, bf16[8,1,256,256]{3,2,1,0:T(8,128)(2,1)S(1)}, u32[]{:S(2)}, u32[]{:S(2)}) collective-permute-start(bf16[8,1,256,256]{3,2,1,0:T(8,128)(2,1)S(1)} %collective-permute-done.7.refs_5_.refs_7_), channel_id=1, source_target_pairs={{4,0},{5,1},{6,2},{7,3},{8,12},{9,13},{10,14},{11,15},{20,16},{21,... | collective-permute-start | bytes 3145736 | tf_op jit(solution)/shard_map/ppermute | solution.py:181
  62.1 15.0 %collective-permute-start.10 = (bf16[2,256,256]{2,1,0:T(8,128)(2,1)S(1)}, bf16[2,256,256]{2,1,0:T(8,128)(2,1)S(1)}, u32[]{:S(2)}, u32[]{:S(2)}) collective-permute-start(bf16[2,256,256]{2,1,0:T(8,128)(2,1)S(1)} %shard_map.49), channel_id=1, source_target_pairs={{0,8},{1,9},{2,10},{3,11},{4,12},{5,13},{6,14},{7,15},{8,0},{9,1},... | collective-permute-start | bytes 786440 | tf_op jit(solution)/shard_map/ppermute | solution.py:181
  65.8 11.9 %collective-permute-start.14 = (bf16[1,7,256,256]{3,2,1,0:T(8,128)(2,1)S(1)}, bf16[1,7,256,256]{3,2,1,0:T(8,128)(2,1)S(1)}, u32[]{:S(2)}, u32[]{:S(2)}) collective-permute-start(bf16[1,7,256,256]{3,2,1,0:T(8,128)(2,1)S(1)} %get-tuple-element.44), channel_id=1, source_target_pairs={{0,1},{1,0},{2,3},{3,2},{4,5},{5,4},{6,7},{7,6},{8,9},{9,8},{10,11... | collective-permute-start | bytes 2752520 | tf_op jit(solution)/shard_map/ppermute | solution.py:181
  77.1 2.7 %collective-permute-start.11 = (bf16[5,1,256,256]{3,2,1,0:T(8,128)(2,1)S(1)}, bf16[5,1,256,256]{3,2,1,0:T(8,128)(2,1)S(1)}, u32[]{:S(2)}, u32[]{:S(2)}) collective-permute-start(bf16[5,1,256,256]{3,2,1,0:T(8,128)(2,1)S(1)} %get-tuple-element.40), channel_id=1, source_target_pairs={{0,1},{1,0},{2,3},{3,2},{4,5},{5,4},{6,7},{7,6},{8,9},{9,8},{10,11... | collective-permute-start | bytes 1966088 | tf_op jit(solution)/shard_map/ppermute | solution.py:181
  77.2 2.6 %collective-permute-start.12 = (bf16[3,1,256,256]{3,2,1,0:T(8,128)(2,1)S(1)}, bf16[3,1,256,256]{3,2,1,0:T(8,128)(2,1)S(1)}, u32[]{:S(2)}, u32[]{:S(2)}) collective-permute-start(bf16[3,1,256,256]{3,2,1,0:T(8,128)(2,1)S(1)} %get-tuple-element.41), channel_id=1, source_target_pairs={{0,1},{1,0},{2,3},{3,2},{4,5},{5,4},{6,7},{7,6},{8,9},{9,8},{10,11... | collective-permute-start | bytes 1179656 | tf_op jit(solution)/shard_map/ppermute | solution.py:181
  81.7 20.5 %collective-permute-start.16 = (bf16[2,256,256]{2,1,0:T(8,128)(2,1)S(1)}, bf16[2,256,256]{2,1,0:T(8,128)(2,1)S(1)}, u32[]{:S(2)}, u32[]{:S(2)}) collective-permute-start(bf16[2,256,256]{2,1,0:T(8,128)(2,1)S(1)} %shard_map.54), channel_id=1, source_target_pairs={{0,8},{1,9},{2,10},{3,11},{4,12},{5,13},{6,14},{7,15},{8,0},{9,1},... | collective-permute-start | bytes 786440 | tf_op jit(solution)/shard_map/ppermute | solution.py:181
  86.2 27.6 %collective-permute-start.17 = (bf16[2,256,256]{2,1,0:T(8,128)(2,1)S(1)}, bf16[2,256,256]{2,1,0:T(8,128)(2,1)S(1)}, u32[]{:S(2)}, u32[]{:S(2)}) collective-permute-start(bf16[2,256,256]{2,1,0:T(8,128)(2,1)S(1)} %shard_map.53), channel_id=1, source_target_pairs={{0,4},{1,5},{2,6},{3,7},{4,0},{5,1},{6,2},{7,3},{8,12},{9,13},{10,... | collective-permute-start | bytes 786440 | tf_op jit(solution)/shard_map/ppermute | solution.py:181
  88.3 25.5 %collective-permute-start.19 = (bf16[2,256,256]{2,1,0:T(8,128)(2,1)S(1)}, bf16[2,256,256]{2,1,0:T(8,128)(2,1)S(1)}, u32[]{:S(2)}, u32[]{:S(2)}) collective-permute-start(bf16[2,256,256]{2,1,0:T(8,128)(2,1)S(1)} %get-tuple-element.47), channel_id=1, source_target_pairs={{4,8},{5,9},{6,10},{7,11},{8,4},{9,5},{10,6},{11,7},{20,24},{21,25... | collective-permute-start | bytes 786440 | tf_op jit(solution)/shard_map/ppermute | solution.py:181
  97.1 3.2 %copy-start.3 = (bf16[8,1,256,256]{3,2,1,0:T(8,128)(2,1)S(1)}, bf16[8,1,256,256]{3,2,1,0:T(8,128)(2,1)}, u32[]{:S(2)}) copy-start(bf16[8,1,256,256]{3,2,1,0:T(8,128)(2,1)} %refs_6_) | copy-start | bytes 3145732
  98.4 15.4 %collective-permute-start.18 = (bf16[4,256,256]{2,1,0:T(8,128)(2,1)S(1)}, bf16[4,256,256]{2,1,0:T(8,128)(2,1)S(1)}, u32[]{:S(2)}, u32[]{:S(2)}) collective-permute-start(bf16[4,256,256]{2,1,0:T(8,128)(2,1)S(1)} %shard_map.55), channel_id=1, source_target_pairs={{0,12},{1,13},{2,14},{3,15},{12,0},{13,1},{14,2},{15,3},{16,28},{1... | collective-permute-start | bytes 1572872 | tf_op jit(solution)/shard_map/ppermute | solution.py:181
